TPU v7x, 128 devices: a whole 4x4x4 slice. The times are simulated.
128 devices in a mesh: grp: 4 (over y_hi, core), tp: 32 (over z, y_lo, x).
Axes of the slice: x: 4, y: 4 (y_hi: 2, y_lo: 2; y = y_hi * 2 + y_lo), z: 4, core: 2. Of those that a mesh axis runs over, the one named last changes fastest.
Arguments:
- main_inputs: bfloat16 [128, 2, 8192], P(('grp', 'tp')), parts along dimension 0, may hold values from -6 to 6
- cont_inputs: bfloat16 [128, 8, 2, 8192], P(('grp', 'tp')), parts along dimension 0, may hold values from -6 to 6
- prefix_cache: bfloat16 [128, 256, 2048], P(('grp', 'tp')), parts along dimension 0, may hold values from -4 to 40.5
- prefix_len: int32 [128], P(('grp', 'tp')), parts along dimension 0, may hold values from 1 to 254, as said below
- boundary: int32 [128], P(('grp', 'tp')), parts along dimension 0, may hold values from 1 to 2
- rms_gain: float32 [8192], replicated, may hold values from 0.1 to 1.9
- qkv_bias: float32 [10240], replicated, may hold values from -2 to 64
- w_qkv: bfloat16 [32, 2048, 1280], P('tp'), may hold values from -0.0625 to 0.0625
- w_out: bfloat16 [32, 2048, 1024], P('tp'), may hold values from -0.0625 to 0.0625
- value_head: float32 [8192], replicated, may hold values from -0.0625 to 0.0625
Outputs:
- main_out: bfloat16 [128, 2, 8192], P(('grp', 'tp')), parts along dimension 0
- values: float32 [128], P(('grp', 'tp')), parts along dimension 0
There are 4 independent parts, one for each index of `grp`. A program takes and returns all parts, laid end to end along the dimension named above; an argument that names none is the same for every part. Nothing has to cross between parts.
Inputs may be any that keep to these rules, and one draw needn't show every extreme that they name: prefix_len + 2 fits in 256; some row reaches the most.
All inputs are finite; a program needn't handle non-finite values.
Results may differ from a plain program's by a relative error of at most 0.0065.
Values may be sent and summed in bfloat16 or wider, within the bound.
No kernel may reach another device: no remote copies, remote signals or barrier semaphores. Data moves between devices by JAX's collectives and lax.ppermute only.
A program may use at most 128 MiB of HBM per device.

v0:
```python
import functools
import math

import jax
import jax.numpy as jnp
from jax import lax
from jax.experimental import pallas as pl
from jax.experimental.pallas import tpu as pltpu
from jax.sharding import PartitionSpec as P

KVH = 8
HD = 128
D = 8192
QKV = 10240
ROW_BLOCKS = 4
COL_BLOCKS = 8
MEMBERS = ROW_BLOCKS * COL_BLOCKS
FEATURES = D // ROW_BLOCKS
CONTS = 8
STEPS = 2
ROWS = 8
TILE = 256

THETA = 1000000.0
EPS = 1e-06
MASKED_SCORE = -1e30

VMEM_LIMIT = 24 * 1024 * 1024
VMEM = pl.BlockSpec(memory_space=pltpu.VMEM)
SMEM = pl.BlockSpec(memory_space=pltpu.SMEM)


def cost(flops, moved):
    return pl.CostEstimate(flops=flops, bytes_accessed=moved, transcendentals=0)


def kernel_params():
    return pltpu.CompilerParams(vmem_limit_bytes=VMEM_LIMIT)


PIECE = FEATURES // 4
QKV_PIECE = 384
OUT_PIECE = D // COL_BLOCKS // 4


def store_copies(out_ref, r, lanes, rows):
    for c in range(COL_BLOCKS):
        out_ref[r * COL_BLOCKS + c, :, lanes] = rows


def norm_kernel(main_ref, cont_ref, gain_ref, first_ref, second_ref, piece_ref):
    def normed(rows):
        wide = rows.astype(jnp.float32)
        inv = lax.rsqrt(jnp.mean(wide * wide, axis=-1, keepdims=True) + EPS)
        return wide * inv * gain_ref[...]

    cont = normed(cont_ref[...])
    main = normed(main_ref[...])
    for r in range(ROW_BLOCKS):
        lanes = slice(r * FEATURES, (r + 1) * FEATURES)
        store_copies(first_ref, r, slice(0, FEATURES), cont[:ROWS, lanes].astype(jnp.bfloat16))
        store_copies(second_ref, r, slice(0, FEATURES), cont[ROWS:, lanes].astype(jnp.bfloat16))
        for j in range(4):
            at = r * FEATURES + j * PIECE
            for s in range(STEPS):
                piece_ref[s * 4 + j : s * 4 + j + 1, :] = main[s : s + 1, at : at + PIECE]
        store_copies(first_ref, r, slice(FEATURES, FEATURES + PIECE), piece_ref[...].astype(jnp.bfloat16))


def norm_rows(main, cont, gain):
    return pl.pallas_call(
        norm_kernel,
        out_shape=(
            jax.ShapeDtypeStruct((MEMBERS, ROWS, FEATURES + PIECE), jnp.bfloat16),
            jax.ShapeDtypeStruct((MEMBERS, ROWS, FEATURES), jnp.bfloat16),
        ),
        in_specs=[VMEM] * 3,
        out_specs=(VMEM, VMEM),
        scratch_shapes=[pltpu.VMEM((8, PIECE), jnp.float32)],
        compiler_params=kernel_params(),
        cost_estimate=cost(10**6, 4 * 10**6),
        name="norm_rows",
    )(main, cont, gain)


def product_kernel(tiles, piece, x_ref, w_ref, out_ref, rows_ref, wide_ref):
    n = pl.program_id(0)
    members = x_ref.shape[0]
    count = members * ROWS

    @pl.when(n == 0)
    def _():
        flat = x_ref[:, :, :FEATURES].astype(jnp.float32).reshape(count, FEATURES)
        rows_ref[:count, :] = flat.astype(jnp.bfloat16)
        if piece:
            packed = x_ref[:, :, FEATURES:].astype(jnp.float32).reshape(count, PIECE)
            for k in range(PIECE // 128):
                wide_ref[k] = packed[:, k * 128 : (k + 1) * 128]
                for j in range(4):
                    rows = wide_ref[k, pl.ds(j, members * STEPS, stride=4), :]
                    lane = j * PIECE + k * 128
                    rows_ref[count:, lane : lane + 128] = rows.astype(jnp.bfloat16)

    weight = w_ref[0, :, pl.ds(pl.multiple_of(n * TILE, TILE), TILE)]
    prod = jnp.dot(rows_ref[...], weight, preferred_element_type=jnp.float32)
    cont = prod[:count].reshape(members, ROWS, TILE).astype(out_ref.dtype)
    out_ref[:, :, pl.ds(pl.multiple_of(n * TILE, TILE), TILE)] = cont
    if piece:
        for tile in range(tiles):

            @pl.when(n == tile)
            def _():
                for h in range(TILE // 128):
                    j, k = divmod(tile * (TILE // 128) + h, piece // 128)
                    wide_ref[k, pl.ds(j, members * STEPS, stride=4), :] = prod[count:, h * 128 : (h + 1) * 128]

        @pl.when(n == tiles - 1)
        def _():
            for k in range(piece // 128):
                lane = tiles * TILE + k * 128
                packed = wide_ref[k].reshape(members, ROWS, 128)
                out_ref[:, :, lane : lane + 128] = packed.astype(out_ref.dtype)


def block_product(rows, blocks, piece, kind):
    tiles = blocks.shape[2] // TILE
    count = MEMBERS * ROWS + (MEMBERS * STEPS if piece else 0)
    return pl.pallas_call(
        functools.partial(product_kernel, tiles, piece),
        out_shape=jax.ShapeDtypeStruct((MEMBERS, ROWS, tiles * TILE + piece), kind),
        grid=(tiles,),
        in_specs=[VMEM, VMEM],
        out_specs=VMEM,
        scratch_shapes=[
            pltpu.VMEM((count, FEATURES), jnp.bfloat16),
            pltpu.VMEM((4, MEMBERS * ROWS, 128), jnp.float32),
        ],
        compiler_params=kernel_params(),
        cost_estimate=cost(2 * count * FEATURES * tiles * TILE, 12 * 10**6),
        name="block_product",
    )(rows, blocks)


def summed_block(parts_ref, c):
    total = parts_ref[c].astype(jnp.float32)
    for r in range(1, ROW_BLOCKS):
        total = total + parts_ref[r * COL_BLOCKS + c].astype(jnp.float32)
    return total


def attend_kernel(first, len_ref, bound_ref, parts_ref, bias_ref, cos_ref, sin_ref, cache_ref, *refs):
    if first:
        out_ref, main_kv_ref, qkv_ref, piece_ref = refs
    else:
        main_kv_ref, out_ref, qkv_ref = refs
    rows = qkv_ref.shape[0]
    prefix_len = len_ref[0]
    boundary = bound_ref[0]
    cols = QKV // COL_BLOCKS
    kv_width = KVH * HD
    if first:
        qkv_ref[ROWS:, :] = jnp.zeros((rows - ROWS, QKV), jnp.float32)
    for c in range(COL_BLOCKS):
        total = summed_block(parts_ref, c)
        qkv_ref[:ROWS, c * cols : (c + 1) * cols] = total[:, :cols]
        if first:
            for m in range(cols // 128):
                j, k = divmod(m, QKV_PIECE // 128)
                lane = cols + k * 128
                at = c * cols + m * 128
                for s in range(STEPS):
                    qkv_ref[ROWS + s : ROWS + s + 1, at : at + 128] = total[s * 4 + j : s * 4 + j + 1, lane : lane + 128]
    cosine = cos_ref[:rows, :]
    sine = sin_ref[:rows, :]

    def plain(start):
        return qkv_ref[:, start : start + HD] + bias_ref[:, start : start + HD]

    def rotated(start):
        head = plain(start)
        return head * cosine + pltpu.roll(head, HD // 2, 1) * sine

    def fresh(values, lane):
        if first:
            main_kv_ref[:, lane : lane + HD] = values[ROWS:]
            parts = [values]
        else:
            parts = [values, main_kv_ref[:, lane : lane + HD]]
        parts.append(jnp.zeros((128 - 2 * ROWS, HD), jnp.float32))
        return jnp.concatenate(parts, axis=0).astype(jnp.bfloat16)

    slots = cache_ref.shape[0]
    group = D // HD // KVH
    seen = lax.broadcasted_iota(jnp.int32, (1, slots), 1) < prefix_len
    row = lax.broadcasted_iota(jnp.int32, (rows, 128), 0)
    col = lax.broadcasted_iota(jnp.int32, (rows, 128), 1)
    own = (row // STEPS == col // STEPS) & (col <= row)
    main = (row < ROWS) & (col >= ROWS) & (col < ROWS + boundary)
    fresh_seen = jnp.concatenate([(own | main).astype(jnp.int32)] * group, axis=0) > 0
    inv_root = 1.0 / math.sqrt(HD)
    contract = (((1,), (1,)), ((), ()))
    for g in range(KVH):
        query = jnp.concatenate([rotated((g * group + h) * HD) for h in range(group)], axis=0).astype(jnp.bfloat16)
        fresh_key = fresh(rotated(D + g * HD), g * HD)
        fresh_value = fresh(plain(D + kv_width + g * HD), kv_width + g * HD)
        key = cache_ref[:, g * HD : (g + 1) * HD]
        value = cache_ref[:, kv_width + g * HD : kv_width + (g + 1) * HD]
        old = lax.dot_general(query, key, contract, preferred_element_type=jnp.float32) * inv_root
        new = lax.dot_general(query, fresh_key, contract, preferred_element_type=jnp.float32) * inv_root
        old = jnp.where(seen, old, MASKED_SCORE)
        new = jnp.where(fresh_seen, new, MASKED_SCORE)
        highest = jnp.maximum(jnp.max(old, axis=-1, keepdims=True), jnp.max(new, axis=-1, keepdims=True))
        old = jnp.exp(old - highest)
        new = jnp.exp(new - highest)
        mass = jnp.sum(old, axis=-1, keepdims=True) + jnp.sum(new, axis=-1, keepdims=True)
        inv_mass = 1.0 / mass
        mixed = jnp.dot((old * inv_mass).astype(jnp.bfloat16), value, preferred_element_type=jnp.float32)
        mixed = mixed + jnp.dot((new * inv_mass).astype(jnp.bfloat16), fresh_value, preferred_element_type=jnp.float32)
        for h in range(group):
            r, place = divmod(g * group + h, FEATURES // HD)
            top = h * rows
            cont = mixed[top : top + ROWS].astype(jnp.bfloat16)
            store_copies(out_ref, r, slice(place * HD, (place + 1) * HD), cont)
            if first:
                j, k = divmod(place, PIECE // HD)
                for s in range(STEPS):
                    at = s * 4 + j
                    line = top + ROWS + s
                    piece_ref[r, at : at + 1, k * HD : (k + 1) * HD] = mixed[line : line + 1]
    if first:
        for r in range(ROW_BLOCKS):
            store_copies(out_ref, r, slice(FEATURES, FEATURES + PIECE), piece_ref[r].astype(jnp.bfloat16))


def attend_first(*args):
    return pl.pallas_call(
        functools.partial(attend_kernel, True),
        out_shape=(
            jax.ShapeDtypeStruct((MEMBERS, ROWS, FEATURES + PIECE), jnp.bfloat16),
            jax.ShapeDtypeStruct((ROWS, 2 * KVH * HD), jnp.float32),
        ),
        in_specs=[SMEM, SMEM] + [VMEM] * 5,
        out_specs=(VMEM, VMEM),
        scratch_shapes=[
            pltpu.VMEM((2 * ROWS, QKV), jnp.float32),
            pltpu.VMEM((ROW_BLOCKS, 8, PIECE), jnp.float32),
        ],
        compiler_params=kernel_params(),
        cost_estimate=cost(2 * 10**8, 8 * 10**6),
        name="attend_first",
    )(*args)


def attend_second(*args):
    return pl.pallas_call(
        functools.partial(attend_kernel, False),
        out_shape=jax.ShapeDtypeStruct((MEMBERS, ROWS, FEATURES), jnp.bfloat16),
        in_specs=[SMEM, SMEM] + [VMEM] * 6,
        out_specs=VMEM,
        scratch_shapes=[pltpu.VMEM((ROWS, QKV), jnp.float32)],
        compiler_params=kernel_params(),
        cost_estimate=cost(2 * 10**8, 8 * 10**6),
        name="attend_second",
    )(*args)


def finish_kernel(first_ref, second_ref, main_ref, cont_ref, head_ref, out_ref, score_ref, wide_ref):
    cols = D // COL_BLOCKS
    total_score = jnp.zeros((ROWS, 128), jnp.float32)
    for c in range(COL_BLOCKS):
        lanes = slice(c * cols, (c + 1) * cols)
        total = summed_block(first_ref, c)
        mixed = jnp.concatenate([total[:, :cols], summed_block(second_ref, c)], axis=0)
        output = (cont_ref[:, lanes].astype(jnp.float32) + mixed).astype(jnp.bfloat16)
        weighted = output.astype(jnp.float32) * head_ref[:, lanes]
        weighted = weighted[:ROWS] + weighted[ROWS:]
        for k in range(cols // 128):
            total_score = total_score + weighted[:, k * 128 : (k + 1) * 128]
        for j in range(4):
            at = slice(c * cols + j * OUT_PIECE, c * cols + (j + 1) * OUT_PIECE)
            for s in range(STEPS):
                wide_ref[s : s + 1, at] = total[s * 4 + j : s * 4 + j + 1, cols:]
    out_ref[...] = (main_ref[...].astype(jnp.float32) + wide_ref[:STEPS, :]).astype(jnp.bfloat16)
    summed = jnp.sum(jnp.sum(total_score, axis=1, keepdims=True), axis=0, keepdims=True)
    score_ref[...] = jnp.broadcast_to(summed / CONTS, (8, 128))


def finish(first, second, main, cont, value_head):
    return pl.pallas_call(
        finish_kernel,
        out_shape=(
            jax.ShapeDtypeStruct((STEPS, D), jnp.bfloat16),
            jax.ShapeDtypeStruct((8, 128), jnp.float32),
        ),
        in_specs=[VMEM] * 5,
        out_specs=(VMEM, VMEM),
        scratch_shapes=[pltpu.VMEM((8, D), jnp.float32)],
        compiler_params=kernel_params(),
        cost_estimate=cost(10**6, 4 * 10**6),
        name="finish",
    )(first, second, main, cont, value_head)


def rope_tables(prefix_len, boundary):
    half = HD // 2
    frequency = THETA ** (-(jnp.arange(half, dtype=jnp.float32) * 2.0) / HD)
    index = jnp.arange(2 * ROWS, dtype=jnp.int32)
    positions = prefix_len + jnp.where(index < ROWS, boundary, 0) + index % STEPS
    angles = positions.astype(jnp.float32)[:, None] * frequency[None, :]
    cosine = jnp.cos(angles)
    sine = jnp.sin(angles)
    return jnp.concatenate([cosine, cosine], axis=1), jnp.concatenate([-sine, sine], axis=1)


def exchange(rows):
    return lax.all_to_all(rows, "tp", split_axis=0, concat_axis=0, tiled=True)


def on_device(
    main_inputs, cont_inputs, prefix_cache, prefix_len, boundary, rms_gain, qkv_bias, w_qkv, w_out, value_head
):
    main = main_inputs.reshape(STEPS, D)
    cont = cont_inputs.reshape(2 * ROWS, D)
    cosine, sine = rope_tables(prefix_len, boundary)
    first, second = norm_rows(main, cont, rms_gain[None, :])
    first = exchange(first)
    second = exchange(second)
    first = exchange(block_product(first, w_qkv, QKV_PIECE, jnp.float32))
    second = exchange(block_product(second, w_qkv, 0, jnp.float32))
    shared = (qkv_bias[None, :], cosine, sine, prefix_cache[0])
    first, main_kv = attend_first(prefix_len, boundary, first, *shared)
    second = attend_second(prefix_len, boundary, second, *shared, main_kv)
    first = exchange(first)
    second = exchange(second)
    first = exchange(block_product(first, w_out, OUT_PIECE, jnp.bfloat16))
    second = exchange(block_product(second, w_out, 0, jnp.bfloat16))
    main_out, score = finish(first, second, main, cont, value_head[None, :])
    return main_out[None], score[0, :1]


def solution(mesh):
    return jax.shard_map(
        on_device,
        mesh=mesh,
        in_specs=(
            P(("grp", "tp"), None, None),
            P(("grp", "tp"), None, None, None),
            P(("grp", "tp"), None, None),
            P(("grp", "tp")),
            P(("grp", "tp")),
            P(),
            P(),
            P("tp", None, None),
            P("tp", None, None),
            P(),
        ),
        out_specs=(P(("grp", "tp"), None, None), P(("grp", "tp"))),
        check_vma=False,
    )
```

profile of v0, /device:TPU:0, one launch (start us, length us, event | category | flops | bytes accessed | tf_op | source)
XLA Modules:
  0.0 188.7 jit_solution(13198232172747132817)
XLA Ops:
  3.6 29.5 %all_to_all.40.x_ref = bf16[32,8,2560]{2,1,0:T(8,128)(2,1)S(1)} all-to-all(bf16[32,8,2560]{2,1,0:T(8,128)(2,1)S(1)} %get-tuple-element.8), channel_id=1, replica_groups=mesh['grp'=4,'tp'=32] {'tp'}, dimensions={0} | all-to-all | bytes 2621440 | tf_op jit(solution)/shard_map/all_to_all | solution.py:316
  33.1 3.9 %all-to-all-start.4 = ((bf16[32,8,2048]{2,1,0:T(8,128)(2,1)}), bf16[32,8,2048]{2,1,0:T(8,128)(2,1)S(1)}, u32[]{:S(2)}, u32[]{:S(2)}) async-start(bf16[32,8,2048]{2,1,0:T(8,128)(2,1)} %copy-done.8), calls=%async_computation.4 | async-start | bytes 2097152 | tf_op jit(solution)/shard_map/all_to_all | solution.py:316
  37.1 2.5 %copy-done = bf16[1,2048,1280]{2,1,0:T(8,128)(2,1)S(1)} copy-done((bf16[1,2048,1280]{2,1,0:T(8,128)(2,1)S(1)}, bf16[1,2048,1280]{2,1,0:T(8,128)(2,1)}, u32[]{:S(2)}) %copy-start) | copy-done | bytes 5242904
  39.5 4.1 %block_product.4 = f32[32,8,1664]{2,1,0:T(8,128)} custom-call(bf16[32,8,2560]{2,1,0:T(8,128)(2,1)S(1)} %all_to_all.40.x_ref, bf16[1,2048,1280]{2,1,0:T(8,128)(2,1)S(1)} %copy-done), custom_call_target="tpu_custom_call" | custom-call | flops 1677721600 | bytes 12000000 | tf_op jit(solution)/shard_map/block_product/pallas_call | solution.py:128
  43.7 9.7 %all-to-all-done.4.x_ref = bf16[32,8,2048]{2,1,0:T(8,128)(2,1)S(1)} async-done(((bf16[32,8,2048]{2,1,0:T(8,128)(2,1)}), bf16[32,8,2048]{2,1,0:T(8,128)(2,1)S(1)}, u32[]{:S(2)}, u32[]{:S(2)}) %all-to-all-start.4) | async-done | bytes 1048608 | tf_op jit(solution)/shard_map/all_to_all | solution.py:316
  53.3 5.0 %all-to-all-start.1 = ((f32[32,8,1664]{2,1,0:T(8,128)}), f32[32,8,1664]{2,1,0:T(8,128)S(1)}, u32[]{:S(2)}, u32[]{:S(2)}) async-start(f32[32,8,1664]{2,1,0:T(8,128)} %block_product.4), calls=%async_computation.1 | async-start | bytes 3407872 | tf_op jit(solution)/shard_map/all_to_all | solution.py:316
  58.4 2.5 %copy-done.1 = bf16[1,2048,1280]{2,1,0:T(8,128)(2,1)S(1)} copy-done((bf16[1,2048,1280]{2,1,0:T(8,128)(2,1)S(1)}, bf16[1,2048,1280]{2,1,0:T(8,128)(2,1)}, u32[]{:S(2)}) %copy-start.1) | copy-done | bytes 5242904
  60.9 2.4 %block_product.6 = f32[32,8,1280]{2,1,0:T(8,128)S(1)} custom-call(bf16[32,8,2048]{2,1,0:T(8,128)(2,1)S(1)} %all-to-all-done.4.x_ref, bf16[1,2048,1280]{2,1,0:T(8,128)(2,1)S(1)} %copy-done.1), custom_call_target="tpu_custom_call" | custom-call | flops 1342177280 | bytes 12000000 | tf_op jit(solution)/shard_map/block_product/pallas_call | solution.py:128
  64.3 17.1 %all-to-all-done.1.parts_ref = f32[32,8,1664]{2,1,0:T(8,128)S(1)} async-done(((f32[32,8,1664]{2,1,0:T(8,128)}), f32[32,8,1664]{2,1,0:T(8,128)S(1)}, u32[]{:S(2)}, u32[]{:S(2)}) %all-to-all-start.1) | async-done | bytes 1703968 | tf_op jit(solution)/shard_map/all_to_all | solution.py:316
  81.4 5.8 %all-to-all-start.5 = ((f32[32,8,1280]{2,1,0:T(8,128)}), f32[32,8,1280]{2,1,0:T(8,128)S(1)}, u32[]{:S(2)}, u32[]{:S(2)}) async-start(f32[32,8,1280]{2,1,0:T(8,128)} %copy-done.4), calls=%async_computation.5 | async-start | bytes 2621440 | tf_op jit(solution)/shard_map/all_to_all | solution.py:316
  88.8 1.2 copy-done.5
  90.0 3.2 %attend_first.1 = (bf16[32,8,2560]{2,1,0:T(8,128)(2,1)S(1)}, f32[8,2048]{1,0:T(8,128)S(1)}) custom-call(s32[1]{0:T(128)} %copy.12.len_ref, s32[1]{0:T(128)} %copy.13.bound_ref, f32[32,8,1664]{2,1,0:T(8,128)S(1)} %all-to-all-done.1.parts_ref, f32[1,10240]{1,0:T(1,128)S(1)} %bitcast.13, f32[16,128]{1,0:T(8,128)S(1)} %get-tuple-element.17.cos_ref, ...), custom_call_target="tpu_custom_call" | custom-call | flops 200000000 | bytes 8000000 | tf_op jit(solution)/shard_map/attend_first/pallas_call | solution.py:236
  94.3 12.5 %all-to-all-done.5.parts_ref = f32[32,8,1280]{2,1,0:T(8,128)S(1)} async-done(((f32[32,8,1280]{2,1,0:T(8,128)}), f32[32,8,1280]{2,1,0:T(8,128)S(1)}, u32[]{:S(2)}, u32[]{:S(2)}) %all-to-all-start.5) | async-done | bytes 1310752 | tf_op jit(solution)/shard_map/all_to_all | solution.py:316
  108.0 3.0 %attend_second.1 = bf16[32,8,2048]{2,1,0:T(8,128)(2,1)S(1)} custom-call(s32[1]{0:T(128)} %copy.12.len_ref, s32[1]{0:T(128)} %copy.13.bound_ref, f32[32,8,1280]{2,1,0:T(8,128)S(1)} %all-to-all-done.5.parts_ref, f32[1,10240]{1,0:T(1,128)S(1)} %bitcast.14, f32[16,128]{1,0:T(8,128)S(1)} %get-tuple-element.17.cos_ref, f32[16,128]{1,0:T(8,128)S(1)} %get-tuple-element.18.sin_ref, ...), custom_call_target="tpu_custom_call" | custom-call | flops 200000000 | bytes 8000000 | tf_op jit(solution)/shard_map/attend_second/pallas_call | solution.py:255
  111.0 21.4 %all_to_all.41.x_ref = bf16[32,8,2048]{2,1,0:T(8,128)(2,1)S(1)} all-to-all(bf16[32,8,2048]{2,1,0:T(8,128)(2,1)S(1)} %attend_second.1), channel_id=1, replica_groups=mesh['grp'=4,'tp'=32] {'tp'}, dimensions={0} | all-to-all | bytes 2097152 | tf_op jit(solution)/shard_map/all_to_all | solution.py:316
  132.5 4.9 %all-to-all-start.2 = ((bf16[32,8,2560]{2,1,0:T(8,128)(2,1)}), bf16[32,8,2560]{2,1,0:T(8,128)(2,1)S(1)}, u32[]{:S(2)}, u32[]{:S(2)}) async-start(bf16[32,8,2560]{2,1,0:T(8,128)(2,1)} %copy-done.7), calls=%async_computation.2 | async-start | bytes 2621440 | tf_op jit(solution)/shard_map/all_to_all | solution.py:316
  137.4 2.2 %copy-done.2 = bf16[1,2048,1024]{2,1,0:T(8,128)(2,1)S(1)} copy-done((bf16[1,2048,1024]{2,1,0:T(8,128)(2,1)S(1)}, bf16[1,2048,1024]{2,1,0:T(8,128)(2,1)}, u32[]{:S(2)}) %copy-start.2) | copy-done | bytes 4194328
  139.5 2.8 %block_product.7 = bf16[32,8,1024]{2,1,0:T(8,128)(2,1)} custom-call(bf16[32,8,2048]{2,1,0:T(8,128)(2,1)S(1)} %all_to_all.41.x_ref, bf16[1,2048,1024]{2,1,0:T(8,128)(2,1)S(1)} %copy-done.2), custom_call_target="tpu_custom_call" | custom-call | flops 1073741824 | bytes 12000000 | tf_op jit(solution)/shard_map/block_product/pallas_call | solution.py:128
  142.3 13.7 %all-to-all-done.2.x_ref = bf16[32,8,2560]{2,1,0:T(8,128)(2,1)S(1)} async-done(((bf16[32,8,2560]{2,1,0:T(8,128)(2,1)}), bf16[32,8,2560]{2,1,0:T(8,128)(2,1)S(1)}, u32[]{:S(2)}, u32[]{:S(2)}) %all-to-all-start.2) | async-done | bytes 1310752 | tf_op jit(solution)/shard_map/all_to_all | solution.py:316
  156.0 5.3 %all-to-all-start.7 = ((bf16[32,8,1024]{2,1,0:T(8,128)(2,1)}), bf16[32,8,1024]{2,1,0:T(8,128)(2,1)S(1)}, u32[]{:S(2)}, u32[]{:S(2)}) async-start(bf16[32,8,1024]{2,1,0:T(8,128)(2,1)} %block_product.7), calls=%async_computation.7 | async-start | bytes 1048576 | tf_op jit(solution)/shard_map/all_to_all | solution.py:316
  161.3 2.2 %copy-done.3 = bf16[1,2048,1024]{2,1,0:T(8,128)(2,1)S(1)} copy-done((bf16[1,2048,1024]{2,1,0:T(8,128)(2,1)S(1)}, bf16[1,2048,1024]{2,1,0:T(8,128)(2,1)}, u32[]{:S(2)}) %copy-start.3) | copy-done | bytes 4194328
  163.5 2.4 %block_product.5 = bf16[32,8,1280]{2,1,0:T(8,128)(2,1)S(1)} custom-call(bf16[32,8,2560]{2,1,0:T(8,128)(2,1)S(1)} %all-to-all-done.2.x_ref, bf16[1,2048,1024]{2,1,0:T(8,128)(2,1)S(1)} %copy-done.3), custom_call_target="tpu_custom_call" | custom-call | flops 1342177280 | bytes 12000000 | tf_op jit(solution)/shard_map/block_product/pallas_call | solution.py:128
  165.9 6.5 %all-to-all-done.7.second_ref = bf16[32,8,1024]{2,1,0:T(8,128)(2,1)S(1)} async-done(((bf16[32,8,1024]{2,1,0:T(8,128)(2,1)}), bf16[32,8,1024]{2,1,0:T(8,128)(2,1)S(1)}, u32[]{:S(2)}, u32[]{:S(2)}) %all-to-all-start.7) | async-done | bytes 524320 | tf_op jit(solution)/shard_map/all_to_all | solution.py:316
  172.4 14.9 %all_to_all.42.first_ref = bf16[32,8,1280]{2,1,0:T(8,128)(2,1)S(1)} all-to-all(bf16[32,8,1280]{2,1,0:T(8,128)(2,1)S(1)} %block_product.5), channel_id=1, replica_groups=mesh['grp'=4,'tp'=32] {'tp'}, dimensions={0} | all-to-all | bytes 1310720 | tf_op jit(solution)/shard_map/all_to_all | solution.py:316
  (31 shorter events, 7.9 us)
Async XLA Ops:
  1.7 0.8 copy-start.10
  2.4 0.8 copy-start.12
  3.6 29.5 %copy-start.8 = (bf16[32,8,2048]{2,1,0:T(8,128)(2,1)}, bf16[32,8,2048]{2,1,0:T(8,128)(2,1)S(1)}, u32[]{:S(2)}) copy-start(bf16[32,8,2048]{2,1,0:T(8,128)(2,1)S(1)} %get-tuple-element.10) | copy-start | bytes 3145732
  33.1 20.2 %all-to-all-start.4 = ((bf16[32,8,2048]{2,1,0:T(8,128)(2,1)}), bf16[32,8,2048]{2,1,0:T(8,128)(2,1)S(1)}, u32[]{:S(2)}, u32[]{:S(2)}) async-start(bf16[32,8,2048]{2,1,0:T(8,128)(2,1)} %copy-done.8), calls=%async_computation.4 | async-start | bytes 2097152 | tf_op jit(solution)/shard_map/all_to_all | solution.py:316
  37.0 2.5 %copy-start = (bf16[1,2048,1280]{2,1,0:T(8,128)(2,1)S(1)}, bf16[1,2048,1280]{2,1,0:T(8,128)(2,1)}, u32[]{:S(2)}) copy-start(bf16[1,2048,1280]{2,1,0:T(8,128)(2,1)} %w_ref.6) | copy-start | bytes 15728644
  53.3 28.1 %all-to-all-start.1 = ((f32[32,8,1664]{2,1,0:T(8,128)}), f32[32,8,1664]{2,1,0:T(8,128)S(1)}, u32[]{:S(2)}, u32[]{:S(2)}) async-start(f32[32,8,1664]{2,1,0:T(8,128)} %block_product.4), calls=%async_computation.1 | async-start | bytes 3407872 | tf_op jit(solution)/shard_map/all_to_all | solution.py:316
  58.4 2.5 %copy-start.1 = (bf16[1,2048,1280]{2,1,0:T(8,128)(2,1)S(1)}, bf16[1,2048,1280]{2,1,0:T(8,128)(2,1)}, u32[]{:S(2)}) copy-start(bf16[1,2048,1280]{2,1,0:T(8,128)(2,1)} %w_ref.6) | copy-start | bytes 15728644
  63.2 1.1 copy-start.4
  64.3 24.5 %copy-start.9 = (f32[10240]{0:T(1024)S(1)}, f32[10240]{0:T(1024)}, u32[]{:S(2)}) copy-start(f32[10240]{0:T(1024)} %param.16) | copy-start | bytes 122884
  81.4 25.4 %all-to-all-start.5 = ((f32[32,8,1280]{2,1,0:T(8,128)}), f32[32,8,1280]{2,1,0:T(8,128)S(1)}, u32[]{:S(2)}, u32[]{:S(2)}) async-start(f32[32,8,1280]{2,1,0:T(8,128)} %copy-done.4), calls=%async_computation.5 | async-start | bytes 2621440 | tf_op jit(solution)/shard_map/all_to_all | solution.py:316
  88.8 1.2 copy-start.5
  93.2 1.1 copy-start.7
  106.8 1.2 copy-start.6
  132.5 23.6 %all-to-all-start.2 = ((bf16[32,8,2560]{2,1,0:T(8,128)(2,1)}), bf16[32,8,2560]{2,1,0:T(8,128)(2,1)S(1)}, u32[]{:S(2)}, u32[]{:S(2)}) async-start(bf16[32,8,2560]{2,1,0:T(8,128)(2,1)} %copy-done.7), calls=%async_computation.2 | async-start | bytes 2621440 | tf_op jit(solution)/shard_map/all_to_all | solution.py:316
  137.4 2.2 %copy-start.2 = (bf16[1,2048,1024]{2,1,0:T(8,128)(2,1)S(1)}, bf16[1,2048,1024]{2,1,0:T(8,128)(2,1)}, u32[]{:S(2)}) copy-start(bf16[1,2048,1024]{2,1,0:T(8,128)(2,1)} %w_ref.7) | copy-start | bytes 12582916
  156.0 16.4 %all-to-all-start.7 = ((bf16[32,8,1024]{2,1,0:T(8,128)(2,1)}), bf16[32,8,1024]{2,1,0:T(8,128)(2,1)S(1)}, u32[]{:S(2)}, u32[]{:S(2)}) async-start(bf16[32,8,1024]{2,1,0:T(8,128)(2,1)} %block_product.7), calls=%async_computation.7 | async-start | bytes 1048576 | tf_op jit(solution)/shard_map/all_to_all | solution.py:316
  161.3 2.2 %copy-start.3 = (bf16[1,2048,1024]{2,1,0:T(8,128)(2,1)S(1)}, bf16[1,2048,1024]{2,1,0:T(8,128)(2,1)}, u32[]{:S(2)}) copy-start(bf16[1,2048,1024]{2,1,0:T(8,128)(2,1)} %w_ref.7) | copy-start | bytes 12582916
  165.9 21.4 %copy-start.11 = (bf16[1,2,8192]{2,1,0:T(2,128)(2,1)S(1)}, bf16[1,2,8192]{2,1,0:T(2,128)(2,1)}, u32[]{:S(2)}) copy-start(bf16[1,2,8192]{2,1,0:T(2,128)(2,1)} %param.10) | copy-start | bytes 98308
  165.9 21.4 %copy-start.13 = (f32[8192]{0:T(1024)S(1)}, f32[8192]{0:T(1024)}, u32[]{:S(2)}) copy-start(f32[8192]{0:T(1024)} %param.19) | copy-start | bytes 98308
where the time goes:
time: 190 us; the launch traced here: 189 us
  blocking collectives  65.8 us (35%)
  waiting for transfers between devices  59.5 us (31%)
  starting transfers between devices  25 us (13%)
  Pallas kernels  19.1 us (10%)
  local copies, waits for them, and re-layouts  17 us (9%)
  between operations  2.11 us (1%)
    all_to_all x3, blocking collectives, exchange(): return lax.all_to_all(rows, 'tp', split_axis=0, concat_axis=0, tiled=True)  65.8 us
    all_to_all x5, waiting for transfers between devices, exchange(): return lax.all_to_all(rows, 'tp', split_axis=0, concat_axis=0, tiled=True)  59.5 us
    all_to_all x5, starting transfers between devices, exchange(): return lax.all_to_all(rows, 'tp', split_axis=0, concat_axis=0, tiled=True)  25 us
    unnamed x28, local copies, waits for them, and re-layouts  15.4 us
    pallas_call x4, Pallas kernels, block_product(): pl.pallas_call(functools.partial(product_kernel, tiles, piece), out_shape...  11.7 us
  transfers between devices with their start and end apart: 5, of which 5 were waited for; matrix products, arithmetic and copies ran while one was open for 0% of the time, Pallas kernels for 8%

commit v1 on v0

v1 whole, which is shorter than its diff:
```python
import functools
import math

import jax
import jax.numpy as jnp
from jax import lax
from jax.experimental import pallas as pl
from jax.experimental.pallas import tpu as pltpu
from jax.sharding import PartitionSpec as P

KVH = 8
HD = 128
D = 8192
QKV = 10240
ROW_BLOCKS = 4
COL_BLOCKS = 8
FEATURES = D // ROW_BLOCKS
CONTS = 8
STEPS = 2
CTOK = CONTS * STEPS
TILE = 256

THETA = 1000000.0
EPS = 1e-06
MASKED_SCORE = -1e30

VMEM_LIMIT = 48 * 1024 * 1024
VMEM = pl.BlockSpec(memory_space=pltpu.VMEM)
SMEM = pl.BlockSpec(memory_space=pltpu.SMEM)


def cost(flops, moved):
    return pl.CostEstimate(flops=flops, bytes_accessed=moved, transcendentals=0)


def kernel_params():
    return pltpu.CompilerParams(vmem_limit_bytes=VMEM_LIMIT)


def norm_kernel(main_ref, cont_ref, gain_ref, out_ref, piece_ref):
    def normed(rows):
        wide = rows.astype(jnp.float32)
        inv = lax.rsqrt(jnp.mean(wide * wide, axis=-1, keepdims=True) + EPS)
        return wide * inv * gain_ref[...]

    cont = normed(cont_ref[...]).astype(jnp.bfloat16)
    main = normed(main_ref[...])
    for r in range(ROW_BLOCKS):
        for j in range(FEATURES // TILE):
            lanes = slice(r * FEATURES + j * TILE, r * FEATURES + (j + 1) * TILE)
            for s in range(STEPS):
                piece_ref[r, s * 8 + j : s * 8 + j + 1, :] = main[s : s + 1, lanes]
    for r in range(ROW_BLOCKS):
        piece = piece_ref[r].astype(jnp.bfloat16)
        for c in range(COL_BLOCKS):
            out_ref[r * COL_BLOCKS + c, :, :FEATURES] = cont[:, r * FEATURES : (r + 1) * FEATURES]
            out_ref[r * COL_BLOCKS + c, :, FEATURES:] = piece


def norm_rows(main, cont, gain):
    return pl.pallas_call(
        norm_kernel,
        out_shape=jax.ShapeDtypeStruct((32, CTOK, FEATURES + TILE), jnp.bfloat16),
        in_specs=[VMEM] * 3,
        out_specs=VMEM,
        scratch_shapes=[pltpu.VMEM((ROW_BLOCKS, 16, TILE), jnp.float32)],
        compiler_params=kernel_params(),
        cost_estimate=cost(10**6, 4 * 10**6),
        name="norm_rows",
    )(main, cont, gain)


REST = 768


def rest_tile(block):
    return jnp.where(block == 6, 2, 0)


def product_kernel(tiles, rest, x_ref, w_ref, out_ref, rows_ref, wide_ref):
    n = pl.program_id(0)
    members = x_ref.shape[0]
    count = members * CTOK
    lines = members * STEPS
    halves = TILE // 128

    @pl.when(n == 0)
    def _():
        rows_ref[:count, :] = x_ref[:, :, :FEATURES].reshape(count, FEATURES)
        packed = x_ref[:, :, FEATURES:].reshape(members * 16, TILE).astype(jnp.float32)
        for k in range(halves):
            wide_ref[k] = packed[:, k * 128 : (k + 1) * 128]
            for j in range(FEATURES // TILE):
                lane = j * TILE + k * 128
                rows_ref[count:, lane : lane + 128] = wide_ref[k, pl.ds(j, lines, stride=8), :].astype(jnp.bfloat16)

    prod = jnp.dot(rows_ref[...], w_ref[0], preferred_element_type=jnp.float32)
    high = prod.astype(jnp.bfloat16)
    out_ref[:, :, pl.ds(pl.multiple_of(n * TILE, TILE), TILE)] = high[:count].reshape(members, CTOK, TILE)
    for k in range(halves):
        wide_ref[k, pl.ds(n, lines, stride=8), :] = prod[count:, k * 128 : (k + 1) * 128]
    width = tiles * TILE
    if rest:
        start = rest_tile(lax.rem(lax.axis_index("tp"), COL_BLOCKS))

        @pl.when((n >= start) & (n < start + rest // TILE))
        def _():
            low = prod - high.astype(jnp.float32)
            place = n - start
            lane = pl.multiple_of(width + place * TILE, TILE)
            out_ref[:, :, pl.ds(lane, TILE)] = low[:count].astype(jnp.bfloat16).reshape(members, CTOK, TILE)
            for k in range(halves):
                wide_ref[k, pl.ds(tiles + place, lines, stride=8), :] = low[count:, k * 128 : (k + 1) * 128]

    @pl.when(n == tiles - 1)
    def _():
        for k in range(halves):
            lane = width + rest + k * 128
            out_ref[:, :, lane : lane + 128] = wide_ref[k].astype(jnp.bfloat16).reshape(members, 16, 128)


def block_product(rows, blocks, rest):
    members = rows.shape[0]
    tiles = blocks.shape[2] // TILE
    return pl.pallas_call(
        functools.partial(product_kernel, tiles, rest),
        out_shape=jax.ShapeDtypeStruct((members, CTOK, (tiles + 1) * TILE + rest), jnp.bfloat16),
        grid=(tiles,),
        in_specs=[
            VMEM,
            pl.BlockSpec((1, FEATURES, TILE), lambda n: (0, 0, n)),
        ],
        out_specs=VMEM,
        scratch_shapes=[
            pltpu.VMEM((members * (CTOK + STEPS), FEATURES), jnp.bfloat16),
            pltpu.VMEM((TILE // 128, members * 16, 128), jnp.float32),
        ],
        compiler_params=kernel_params(),
        cost_estimate=cost(2 * members * (CTOK + STEPS) * FEATURES * tiles * TILE, 12 * 10**6),
        name="block_product",
    )(rows, blocks)


def summed_block(parts_ref, c, lanes):
    total = parts_ref[c, :, lanes].astype(jnp.float32)
    for r in range(1, ROW_BLOCKS):
        total = total + parts_ref[r * COL_BLOCKS + c, :, lanes].astype(jnp.float32)
    return total


def head_attention(query, key, value, fresh_key, fresh_value, seen, fresh_seen):
    inv_root = 1.0 / math.sqrt(HD)
    contract = (((1,), (1,)), ((), ()))
    old = lax.dot_general(query, key, contract, preferred_element_type=jnp.float32) * inv_root
    new = lax.dot_general(query, fresh_key, contract, preferred_element_type=jnp.float32) * inv_root
    old = jnp.where(seen, old, MASKED_SCORE)
    new = jnp.where(fresh_seen, new, MASKED_SCORE)
    highest = jnp.maximum(jnp.max(old, axis=-1, keepdims=True), jnp.max(new, axis=-1, keepdims=True))
    old = jnp.exp(old - highest)
    new = jnp.exp(new - highest)
    mass = jnp.sum(old, axis=-1, keepdims=True) + jnp.sum(new, axis=-1, keepdims=True)
    inv_mass = 1.0 / mass
    mixed = jnp.dot((old * inv_mass).astype(jnp.bfloat16), value, preferred_element_type=jnp.float32)
    return mixed + jnp.dot((new * inv_mass).astype(jnp.bfloat16), fresh_value, preferred_element_type=jnp.float32)


def load_qkv(main, parts_ref, qkv_ref):
    cols = QKV // COL_BLOCKS
    for c in range(COL_BLOCKS):
        first = 2 if c == 6 else 0
        if main:
            total = summed_block(parts_ref, c, slice(cols + REST, cols + REST + TILE))
        else:
            total = summed_block(parts_ref, c, slice(0, cols + REST))
        for j in range(cols // TILE):
            lanes = slice(c * cols + j * TILE, c * cols + (j + 1) * TILE)
            rest = j - first
            has_rest = 0 <= rest < REST // TILE
            if main:
                for s in range(STEPS):
                    line = total[s * 8 + j : s * 8 + j + 1]
                    if has_rest:
                        at = s * 8 + cols // TILE + rest
                        line = line + total[at : at + 1]
                    qkv_ref[s : s + 1, lanes] = line
            else:
                value = total[:, j * TILE : (j + 1) * TILE]
                if has_rest:
                    value = value + total[:, cols + rest * TILE : cols + (rest + 1) * TILE]
                qkv_ref[:, lanes] = value


def head_readers(qkv_ref, bias_ref, cos_ref, sin_ref):
    cosine = cos_ref[...]
    sine = sin_ref[...]

    def plain(start):
        return qkv_ref[:, start : start + HD] + bias_ref[:, start : start + HD]

    def rotated(start):
        head = plain(start)
        return head * cosine + pltpu.roll(head, HD // 2, 1) * sine

    return plain, rotated


def fresh_block(pieces):
    rows = sum(piece.shape[0] for piece in pieces)
    pad = jnp.zeros((128 - rows, HD), jnp.float32)
    return jnp.concatenate(list(pieces) + [pad], axis=0).astype(jnp.bfloat16)


GROUP = D // HD // KVH
KV_WIDTH = KVH * HD


def attend_main_kernel(len_ref, parts_ref, bias_ref, cos_ref, sin_ref, cache_ref, out_ref, kv_ref, qkv_ref, piece_ref):
    rows = qkv_ref.shape[0]
    qkv_ref[...] = jnp.zeros(qkv_ref.shape, jnp.float32)
    load_qkv(True, parts_ref, qkv_ref)
    plain, rotated = head_readers(qkv_ref, bias_ref, cos_ref, sin_ref)
    seen = lax.broadcasted_iota(jnp.int32, (1, cache_ref.shape[0]), 1) < len_ref[0]
    row = lax.broadcasted_iota(jnp.int32, (rows, 128), 0)
    col = lax.broadcasted_iota(jnp.int32, (rows, 128), 1)
    own = ((col <= row) & (col < STEPS)).astype(jnp.int32)
    fresh_seen = jnp.concatenate([own] * GROUP, axis=0) > 0
    for g in range(KVH):
        query = jnp.concatenate([rotated((g * GROUP + h) * HD) for h in range(GROUP)], axis=0).astype(jnp.bfloat16)
        fresh_key = rotated(D + g * HD)
        fresh_value = plain(D + KV_WIDTH + g * HD)
        kv_ref[:, g * HD : (g + 1) * HD] = fresh_key
        kv_ref[:, KV_WIDTH + g * HD : KV_WIDTH + (g + 1) * HD] = fresh_value
        key = cache_ref[:, g * HD : (g + 1) * HD]
        value = cache_ref[:, KV_WIDTH + g * HD : KV_WIDTH + (g + 1) * HD]
        mixed = head_attention(
            query, key, value, fresh_block([fresh_key]), fresh_block([fresh_value]), seen, fresh_seen
        )
        for h in range(GROUP):
            r, place = divmod(g * GROUP + h, FEATURES // HD)
            j, lane = place // 2, (place % 2) * HD
            for s in range(STEPS):
                at = s * 8 + j
                piece_ref[r, at : at + 1, lane : lane + HD] = mixed[h * rows + s : h * rows + s + 1]
    for r in range(ROW_BLOCKS):
        piece = piece_ref[r].astype(jnp.bfloat16)
        for c in range(COL_BLOCKS):
            out_ref[r * COL_BLOCKS + c] = piece


def attend_main(prefix_len, parts, bias, cosine, sine, cache):
    return pl.pallas_call(
        attend_main_kernel,
        out_shape=(
            jax.ShapeDtypeStruct((32, 16, TILE), jnp.bfloat16),
            jax.ShapeDtypeStruct((8, 2 * KV_WIDTH), jnp.float32),
        ),
        in_specs=[SMEM] + [VMEM] * 5,
        out_specs=(VMEM, VMEM),
        scratch_shapes=[
            pltpu.VMEM((8, QKV), jnp.float32),
            pltpu.VMEM((ROW_BLOCKS, 16, TILE), jnp.float32),
        ],
        compiler_params=kernel_params(),
        cost_estimate=cost(2 * 10**8, 6 * 10**6),
        name="attend_main",
    )(prefix_len, parts, bias, cosine, sine, cache)


def attend_cont_kernel(
    len_ref, bound_ref, parts_ref, bias_ref, cos_ref, sin_ref, cache_ref, kv_ref, cont_ref, head_ref, read_ref,
    score_ref, qkv_ref, weight_ref,
):
    rows = qkv_ref.shape[0]
    load_qkv(False, parts_ref, qkv_ref)
    plain, rotated = head_readers(qkv_ref, bias_ref, cos_ref, sin_ref)
    for r in range(ROW_BLOCKS):
        block = read_ref[r * COL_BLOCKS : (r + 1) * COL_BLOCKS, :]
        weight_ref[:, r * FEATURES : (r + 1) * FEATURES] = jnp.sum(block, axis=0, keepdims=True)
    seen = lax.broadcasted_iota(jnp.int32, (1, cache_ref.shape[0]), 1) < len_ref[0]
    row = lax.broadcasted_iota(jnp.int32, (rows, 128), 0)
    col = lax.broadcasted_iota(jnp.int32, (rows, 128), 1)
    own = (row // STEPS == col // STEPS) & (col <= row)
    main = (col >= rows) & (col < rows + bound_ref[0])
    fresh_seen = jnp.concatenate([(own | main).astype(jnp.int32)] * GROUP, axis=0) > 0
    total = jnp.zeros((rows, HD), jnp.float32)
    for k in range(D // HD):
        lanes = slice(k * HD, (k + 1) * HD)
        total = total + cont_ref[:, lanes].astype(jnp.float32) * head_ref[:, lanes]
    for g in range(KVH):
        query = jnp.concatenate([rotated((g * GROUP + h) * HD) for h in range(GROUP)], axis=0).astype(jnp.bfloat16)
        at_key = slice(g * HD, (g + 1) * HD)
        at_value = slice(KV_WIDTH + g * HD, KV_WIDTH + (g + 1) * HD)
        fresh_key = fresh_block([rotated(D + g * HD), kv_ref[:, at_key]])
        fresh_value = fresh_block([plain(D + KV_WIDTH + g * HD), kv_ref[:, at_value]])
        mixed = head_attention(
            query, cache_ref[:, at_key], cache_ref[:, at_value], fresh_key, fresh_value, seen, fresh_seen
        )
        mixed = mixed.astype(jnp.bfloat16).astype(jnp.float32)
        for h in range(GROUP):
            lanes = slice((g * GROUP + h) * HD, (g * GROUP + h + 1) * HD)
            total = total + mixed[h * rows : (h + 1) * rows] * weight_ref[:, lanes]
    summed = jnp.sum(jnp.sum(total, axis=1, keepdims=True), axis=0, keepdims=True)
    score_ref[...] = jnp.broadcast_to(summed / CONTS, (8, 128))


def attend_cont(*args):
    return pl.pallas_call(
        attend_cont_kernel,
        out_shape=jax.ShapeDtypeStruct((8, 128), jnp.float32),
        in_specs=[SMEM, SMEM] + [VMEM] * 9,
        out_specs=VMEM,
        scratch_shapes=[pltpu.VMEM((CTOK, QKV), jnp.float32), pltpu.VMEM((1, D), jnp.float32)],
        compiler_params=kernel_params(),
        cost_estimate=cost(4 * 10**8, 8 * 10**6),
        name="attend_cont",
    )(*args)


def readout_kernel(head_ref, w_ref, out_ref):
    row = head_ref[pl.ds(lax.rem(lax.axis_index("tp"), COL_BLOCKS), 1), :]
    high = row.astype(jnp.bfloat16).astype(jnp.float32)
    middle = (row - high).astype(jnp.bfloat16).astype(jnp.float32)
    low = row - high - middle
    pieces = jnp.concatenate([high, middle, low, jnp.zeros((13, row.shape[1]), jnp.float32)], axis=0)
    prod = lax.dot_general(
        pieces.astype(jnp.bfloat16), w_ref[0], (((1,), (1,)), ((), ())), preferred_element_type=jnp.float32
    )
    out_ref[...] = prod[0:1] + prod[1:2] + prod[2:3]


def readout(value_head, blocks):
    return pl.pallas_call(
        readout_kernel,
        out_shape=jax.ShapeDtypeStruct((1, FEATURES), jnp.float32),
        in_specs=[VMEM, VMEM],
        out_specs=VMEM,
        compiler_params=kernel_params(),
        cost_estimate=cost(2 * 10**8, 5 * 10**6),
        name="readout",
    )(value_head, blocks)


def out_kernel(tiles, x_ref, w_ref, out_ref, rows_ref, wide_ref):
    n = pl.program_id(0)
    members = x_ref.shape[0]
    lines = members * STEPS
    halves = TILE // 128

    @pl.when(n == 0)
    def _():
        packed = x_ref[...].reshape(members * 16, TILE).astype(jnp.float32)
        for k in range(halves):
            wide_ref[k] = packed[:, k * 128 : (k + 1) * 128]
            for j in range(FEATURES // TILE):
                lane = j * TILE + k * 128
                rows_ref[:, lane : lane + 128] = wide_ref[k, pl.ds(j, lines, stride=8), :].astype(jnp.bfloat16)

    prod = jnp.dot(rows_ref[...], w_ref[0], preferred_element_type=jnp.float32)
    for k in range(halves):
        wide_ref[k, pl.ds(n, lines, stride=4), :] = prod[:, k * 128 : (k + 1) * 128]

    @pl.when(n == tiles - 1)
    def _():
        for k in range(halves):
            packed = wide_ref[k, : members * 8, :].reshape(members, 8, 128)
            out_ref[:, :, k * 128 : (k + 1) * 128] = packed


def out_product(rows, blocks):
    members = rows.shape[0]
    tiles = blocks.shape[2] // TILE
    return pl.pallas_call(
        functools.partial(out_kernel, tiles),
        out_shape=jax.ShapeDtypeStruct((members, 8, TILE), jnp.float32),
        grid=(tiles,),
        in_specs=[
            VMEM,
            pl.BlockSpec((1, FEATURES, TILE), lambda n: (0, 0, n)),
        ],
        out_specs=VMEM,
        scratch_shapes=[
            pltpu.VMEM((members * STEPS, FEATURES), jnp.bfloat16),
            pltpu.VMEM((TILE // 128, members * 16, 128), jnp.float32),
        ],
        compiler_params=kernel_params(),
        cost_estimate=cost(3 * 10**8, 5 * 10**6),
        name="out_product",
    )(rows, blocks)


def finish_kernel(parts_ref, main_ref, out_ref, wide_ref):
    cols = D // COL_BLOCKS
    for c in range(COL_BLOCKS):
        total = summed_block(parts_ref, c, slice(0, TILE))
        for j in range(cols // TILE):
            at = slice(c * cols + j * TILE, c * cols + (j + 1) * TILE)
            for s in range(STEPS):
                wide_ref[s : s + 1, at] = total[s * 4 + j : s * 4 + j + 1]
    out_ref[...] = (main_ref[...].astype(jnp.float32) + wide_ref[:STEPS, :]).astype(jnp.bfloat16)


def finish(parts, main):
    return pl.pallas_call(
        finish_kernel,
        out_shape=jax.ShapeDtypeStruct((STEPS, D), jnp.bfloat16),
        in_specs=[VMEM] * 2,
        out_specs=VMEM,
        scratch_shapes=[pltpu.VMEM((8, D), jnp.float32)],
        compiler_params=kernel_params(),
        cost_estimate=cost(10**6, 2 * 10**6),
        name="finish",
    )(parts, main)


def rope_tables(positions):
    half = HD // 2
    frequency = THETA ** (-(jnp.arange(half, dtype=jnp.float32) * 2.0) / HD)
    angles = positions.astype(jnp.float32)[:, None] * frequency[None, :]
    cosine = jnp.cos(angles)
    sine = jnp.sin(angles)
    return jnp.concatenate([cosine, cosine], axis=1), jnp.concatenate([-sine, sine], axis=1)


def exchange(rows):
    return lax.all_to_all(rows, "tp", split_axis=0, concat_axis=0, tiled=True)


def on_device(
    main_inputs, cont_inputs, prefix_cache, prefix_len, boundary, rms_gain, qkv_bias, w_qkv, w_out, value_head
):
    main = main_inputs.reshape(STEPS, D)
    cont = cont_inputs.reshape(CTOK, D)
    bias = qkv_bias[None, :]
    cache = prefix_cache[0]
    head = value_head[None, :]
    step = jnp.arange(CTOK, dtype=jnp.int32) % STEPS
    main_tables = rope_tables(prefix_len + step[:8])
    cont_tables = rope_tables(prefix_len + boundary + step)
    read = lax.all_gather(readout(value_head.reshape(COL_BLOCKS, D // COL_BLOCKS), w_out), "tp", axis=0, tiled=True)
    sent = exchange(norm_rows(main, cont, rms_gain[None, :]))
    parts = exchange(block_product(sent, w_qkv, REST))
    mixed, main_kv = attend_main(prefix_len, parts, bias, *main_tables, cache)
    mixed = exchange(mixed)
    score = attend_cont(prefix_len, boundary, parts, bias, *cont_tables, cache, main_kv, cont, head, read)
    main_out = finish(exchange(out_product(mixed, w_out)), main)
    return main_out[None], score[0, :1]


def solution(mesh):
    return jax.shard_map(
        on_device,
        mesh=mesh,
        in_specs=(
            P(("grp", "tp"), None, None),
            P(("grp", "tp"), None, None, None),
            P(("grp", "tp"), None, None),
            P(("grp", "tp")),
            P(("grp", "tp")),
            P(),
            P(),
            P("tp", None, None),
            P("tp", None, None),
            P(),
        ),
        out_specs=(P(("grp", "tp"), None, None), P(("grp", "tp"))),
        check_vma=False,
    )
```

time: 190 us -> 209 us (1.10)
  blocking collectives: 65.8 us -> 123 us
  waiting for transfers between devices: 59.5 us -> 34.1 us
  starting transfers between devices: 25 us -> 16.4 us
  local copies, waits for them, and re-layouts: 17 us -> 12.8 us
    all_gather x0 -> x1, blocking collectives: none -> 82.6 us  [on_device(): lax.all_gather(readout(value_head.reshape(COL_BLOCKS, D // COL_BLOCKS), w...]
    all_to_all x5 -> x3, waiting for transfers between devices: 59.5 us -> 34.1 us  [exchange(): return lax.all_to_all(rows, 'tp', split_axis=0, concat_axis=0, tiled=True)]
    all_to_all x3 -> x1, blocking collectives: 65.8 us -> 40.7 us  [exchange(): return lax.all_to_all(rows, 'tp', split_axis=0, concat_axis=0, tiled=True)]
    all_to_all x5 -> x3, starting transfers between devices: 25 us -> 16.4 us  [exchange(): return lax.all_to_all(rows, 'tp', split_axis=0, concat_axis=0, tiled=True)]
    unnamed x28 -> x31, local copies, waits for them, and re-layouts: 15.4 us -> 11.3 us
    pallas_call x8 -> x7, Pallas kernels: 19.1 us -> 18.6 us  [the longest x1 6.5 us: block_product(): pl.pallas_call(functools.partial(product_kernel, tiles, rest), out_shape=...]
  transfers between devices with their start and end apart: 5 -> 3, of which waited for: 5 -> 2; matrix products, arithmetic and copies ran while one was open for 0% -> 1% of each run, Pallas kernels for 8% -> 2%
where the time goes in v1:
time: 209 us; the launch traced here: 208 us
  blocking collectives  123 us (59%)
  waiting for transfers between devices  34.1 us (16%)
  Pallas kernels  18.6 us (9%)
  starting transfers between devices  16.4 us (8%)
  local copies, waits for them, and re-layouts  12.8 us (6%)
  between operations  2.11 us (1%)
    all_gather x1, blocking collectives, on_device(): lax.all_gather(readout(value_head.reshape(COL_BLOCKS, D // COL_BLOCKS), w...  82.6 us
    all_to_all x1, blocking collectives, exchange(): return lax.all_to_all(rows, 'tp', split_axis=0, concat_axis=0, tiled=True)  40.7 us
    all_to_all x3, waiting for transfers between devices, exchange(): return lax.all_to_all(rows, 'tp', split_axis=0, concat_axis=0, tiled=True)  34.1 us
    all_to_all x3, starting transfers between devices, exchange(): return lax.all_to_all(rows, 'tp', split_axis=0, concat_axis=0, tiled=True)  16.4 us
    unnamed x31, local copies, waits for them, and re-layouts  11.3 us
    pallas_call x1, Pallas kernels, block_product(): pl.pallas_call(functools.partial(product_kernel, tiles, rest), out_shape=...  6.5 us
  transfers between devices with their start and end apart: 3, of which 2 were waited for; matrix products, arithmetic and copies ran while one was open for 1% of the time, Pallas kernels for 2%

profile of v1, /device:TPU:0, one launch (start us, length us, event | category | flops | bytes accessed | tf_op | source)
XLA Modules:
  0.0 207.8 jit_solution(6161553654880166839)
XLA Ops:
  0.6 1.0 reshape.33.cont_ref
  1.7 0.8 copy-done.9
  2.5 0.8 copy-done.14
  3.6 40.7 %all_to_all.20.x_ref = bf16[32,16,2304]{2,1,0:T(8,128)(2,1)S(1)} all-to-all(bf16[32,16,2304]{2,1,0:T(8,128)(2,1)S(1)} %norm_rows.1), channel_id=1, replica_groups=mesh['grp'=4,'tp'=32] {'tp'}, dimensions={0} | all-to-all | bytes 4718592 | tf_op jit(solution)/shard_map/all_to_all | solution.py:425
  44.4 6.5 %block_product.1 = bf16[32,16,2304]{2,1,0:T(8,128)(2,1)S(1)} custom-call(bf16[32,16,2304]{2,1,0:T(8,128)(2,1)S(1)} %all_to_all.20.x_ref, bf16[1,2048,1280]{2,1,0:T(8,128)(2,1)} %w_ref.3), custom_call_target="tpu_custom_call" | custom-call | flops 3019898880 | bytes 12000000 | tf_op jit(solution)/shard_map/block_product/pallas_call | solution.py:125
  50.9 1.4 copy-done.3
  52.3 4.2 %all-to-all-start.1 = ((bf16[32,16,2304]{2,1,0:T(8,128)(2,1)}), bf16[32,16,2304]{2,1,0:T(8,128)(2,1)S(1)}, u32[]{:S(2)}, u32[]{:S(2)}) async-start(bf16[32,16,2304]{2,1,0:T(8,128)(2,1)} %copy-done.3), calls=%async_computation.1 | async-start | bytes 4718592 | tf_op jit(solution)/shard_map/all_to_all | solution.py:425
  58.1 28.5 %all-to-all-done.1.parts_ref = bf16[32,16,2304]{2,1,0:T(8,128)(2,1)S(1)} async-done(((bf16[32,16,2304]{2,1,0:T(8,128)(2,1)}), bf16[32,16,2304]{2,1,0:T(8,128)(2,1)S(1)}, u32[]{:S(2)}, u32[]{:S(2)}) %all-to-all-start.1) | async-done | bytes 2359328 | tf_op jit(solution)/shard_map/all_to_all | solution.py:425
  86.5 3.0 %attend_main.1 = (bf16[32,16,256]{2,1,0:T(8,128)(2,1)S(1)}, f32[8,2048]{1,0:T(8,128)S(1)}) custom-call(s32[1]{0:T(128)} %copy.15.len_ref, bf16[32,16,2304]{2,1,0:T(8,128)(2,1)S(1)} %all-to-all-done.1.parts_ref, f32[1,10240]{1,0:T(1,128)S(1)} %bitcast.17, f32[8,128]{1,0:T(8,128)S(1)} %get-tuple-element.12.cos_ref, f32[8,128]{1,0:T(8,128)S(1)} %get-tuple-element.13.sin_ref, ...), custom_call_target="tpu_custom_call" | custom-call | flops 200000000 | bytes 6000000 | tf_op jit(solution)/shard_map/attend_main/pallas_call | solution.py:251
  89.5 0.7 copy-done.7
  90.2 0.6 copy-done.12
  90.8 7.6 %all-to-all-start.2 = ((bf16[32,16,256]{2,1,0:T(8,128)(2,1)}), bf16[32,16,256]{2,1,0:T(8,128)(2,1)}, u32[]{:S(2)}, u32[]{:S(2)}) async-start(bf16[32,16,256]{2,1,0:T(8,128)(2,1)} %copy-done.7), calls=%async_computation.2 | async-start | bytes 524288 | tf_op jit(solution)/shard_map/all_to_all | solution.py:425
  98.5 2.2 %copy-done = bf16[1,2048,1024]{2,1,0:T(8,128)(2,1)S(1)} copy-done((bf16[1,2048,1024]{2,1,0:T(8,128)(2,1)S(1)}, bf16[1,2048,1024]{2,1,0:T(8,128)(2,1)}, u32[]{:S(2)}) %copy-start) | copy-done | bytes 4194328
  100.7 1.2 readout.1
  102.0 5.6 %all-to-all-done.2.x_ref = bf16[32,16,256]{2,1,0:T(8,128)(2,1)} async-done(((bf16[32,16,256]{2,1,0:T(8,128)(2,1)}), bf16[32,16,256]{2,1,0:T(8,128)(2,1)}, u32[]{:S(2)}, u32[]{:S(2)}) %all-to-all-start.2) | async-done | bytes 262176 | tf_op jit(solution)/shard_map/all_to_all | solution.py:425
  107.7 2.2 %copy-done.1 = bf16[1,2048,1024]{2,1,0:T(8,128)(2,1)S(1)} copy-done((bf16[1,2048,1024]{2,1,0:T(8,128)(2,1)S(1)}, bf16[1,2048,1024]{2,1,0:T(8,128)(2,1)}, u32[]{:S(2)}) %copy-start.1) | copy-done | bytes 4194328
  109.9 2.8 %out_product.1 = f32[32,8,256]{2,1,0:T(8,128)S(1)} custom-call(bf16[32,16,256]{2,1,0:T(8,128)(2,1)} %all-to-all-done.2.x_ref, bf16[1,2048,1024]{2,1,0:T(8,128)(2,1)S(1)} %copy-done.1), custom_call_target="tpu_custom_call" | custom-call | flops 300000000 | bytes 5000000 | tf_op jit(solution)/shard_map/out_product/pallas_call | solution.py:372
  112.7 0.7 copy-done.6
  113.4 4.6 %all-to-all-start.3 = ((f32[32,8,256]{2,1,0:T(8,128)}), f32[32,8,256]{2,1,0:T(8,128)}, u32[]{:S(2)}, u32[]{:S(2)}) async-start(f32[32,8,256]{2,1,0:T(8,128)} %copy-done.6), calls=%async_computation.3 | async-start | bytes 524288 | tf_op jit(solution)/shard_map/all_to_all | solution.py:425
  118.0 82.6 %all-gather = f32[32,1,2048]{2,1,0:T(1,128)S(1)} all-gather(f32[1,1,2048]{2,1,0:T(1,128)S(1)} %bitcast.23), channel_id=1, replica_groups=mesh['grp'=4,'tp'=32] {'tp'}, dimensions={0}, use_global_device_ids=true | all-gather | bytes 270336 | tf_op jit(solution)/shard_map/all_gather | solution.py:439
  200.8 0.9 copy-done.5
  201.7 0.8 copy-done.13
  202.6 3.1 %attend_cont.1 = f32[8,128]{1,0:T(8,128)S(1)} custom-call(s32[1]{0:T(128)} %copy.15.len_ref, s32[1]{0:T(128)S(6)} %copy.16.bound_ref, bf16[32,16,2304]{2,1,0:T(8,128)(2,1)S(1)} %all-to-all-done.1.parts_ref, f32[1,10240]{1,0:T(1,128)S(1)} %bitcast.18, f32[16,128]{1,0:T(8,128)S(1)} %get-tuple-element.14.cos_ref, f32[16,128]{1,0:T(8,128)S(1)} %get-tuple-element.15.sin_ref, ...), custom_call_target="tpu_custom_call" | custom-call | flops 400000000 | bytes 8000000 | tf_op jit(solution)/shard_map/attend_cont/pallas_call | solution.py:307
  206.2 1.6 finish.1
  (33 shorter events, 1.5 us)
Async XLA Ops:
  1.7 42.7 %copy-start.4 = (bf16[16,8192]{1,0:T(8,128)(2,1)}, bf16[16,8192]{1,0:T(8,128)(2,1)S(1)}, u32[]{:S(2)}) copy-start(bf16[16,8192]{1,0:T(8,128)(2,1)S(1)} %reshape.33.cont_ref) | copy-start | bytes 786436
  1.7 0.8 copy-start.9
  2.5 0.8 copy-start.14
  50.9 1.4 copy-start.3
  52.3 34.2 %copy-start.2 = (bf16[1,256,2048]{2,1,0:T(8,128)(2,1)S(1)}, bf16[1,256,2048]{2,1,0:T(8,128)(2,1)}, u32[]{:S(2)}) copy-start(bf16[1,256,2048]{2,1,0:T(8,128)(2,1)} %param.12) | copy-start | bytes 3145732
  52.3 34.2 %copy-start.8 = (f32[10240]{0:T(1024)S(1)}, f32[10240]{0:T(1024)}, u32[]{:S(2)}) copy-start(f32[10240]{0:T(1024)} %param.16) | copy-start | bytes 122884
  52.3 34.2 %all-to-all-start.1 = ((bf16[32,16,2304]{2,1,0:T(8,128)(2,1)}), bf16[32,16,2304]{2,1,0:T(8,128)(2,1)S(1)}, u32[]{:S(2)}, u32[]{:S(2)}) async-start(bf16[32,16,2304]{2,1,0:T(8,128)(2,1)} %copy-done.3), calls=%async_computation.1 | async-start | bytes 4718592 | tf_op jit(solution)/shard_map/all_to_all | solution.py:425
  56.5 42.0 %copy-start.11 = (f32[8192]{0:T(1024)S(1)}, f32[8192]{0:T(1024)}, u32[]{:S(2)}) copy-start(f32[8192]{0:T(1024)} %param.19) | copy-start | bytes 98308
  89.5 0.7 copy-start.7
  90.2 0.6 copy-start.12
  90.8 16.8 %all-to-all-start.2 = ((bf16[32,16,256]{2,1,0:T(8,128)(2,1)}), bf16[32,16,256]{2,1,0:T(8,128)(2,1)}, u32[]{:S(2)}, u32[]{:S(2)}) async-start(bf16[32,16,256]{2,1,0:T(8,128)(2,1)} %copy-done.7), calls=%async_computation.2 | async-start | bytes 524288 | tf_op jit(solution)/shard_map/all_to_all | solution.py:425
  98.5 2.2 %copy-start = (bf16[1,2048,1024]{2,1,0:T(8,128)(2,1)S(1)}, bf16[1,2048,1024]{2,1,0:T(8,128)(2,1)}, u32[]{:S(2)}) copy-start(bf16[1,2048,1024]{2,1,0:T(8,128)(2,1)} %w_ref.5) | copy-start | bytes 12582916
  107.7 2.2 %copy-start.1 = (bf16[1,2048,1024]{2,1,0:T(8,128)(2,1)S(1)}, bf16[1,2048,1024]{2,1,0:T(8,128)(2,1)}, u32[]{:S(2)}) copy-start(bf16[1,2048,1024]{2,1,0:T(8,128)(2,1)} %w_ref.5) | copy-start | bytes 12582916
  112.7 0.7 copy-start.6
  113.4 92.8 %all-to-all-start.3 = ((f32[32,8,256]{2,1,0:T(8,128)}), f32[32,8,256]{2,1,0:T(8,128)}, u32[]{:S(2)}, u32[]{:S(2)}) async-start(f32[32,8,256]{2,1,0:T(8,128)} %copy-done.6), calls=%async_computation.3 | async-start | bytes 524288 | tf_op jit(solution)/shard_map/all_to_all | solution.py:425
  200.6 5.6 %copy-start.10 = (bf16[1,2,8192]{2,1,0:T(2,128)(2,1)S(1)}, bf16[1,2,8192]{2,1,0:T(2,128)(2,1)}, u32[]{:S(2)}) copy-start(bf16[1,2,8192]{2,1,0:T(2,128)(2,1)} %param.10) | copy-start | bytes 98308
  200.8 1.0 copy-start.5
  201.7 0.8 copy-start.13

commit v2 on v1

--- a/solution.py
+++ b/solution.py
@@ -27,6 +27,11 @@
 VMEM_LIMIT = 48 * 1024 * 1024
 VMEM = pl.BlockSpec(memory_space=pltpu.VMEM)
 SMEM = pl.BlockSpec(memory_space=pltpu.SMEM)
+HBM = pl.BlockSpec(memory_space=pltpu.HBM)
+
+
+def whole(shape):
+    return pl.BlockSpec(shape, lambda *_: (0,) * len(shape))
 
 
 def cost(flops, moved):
@@ -37,14 +42,22 @@
     return pltpu.CompilerParams(vmem_limit_bytes=VMEM_LIMIT)
 
 
-def norm_kernel(main_ref, cont_ref, gain_ref, out_ref, piece_ref):
-    def normed(rows):
-        wide = rows.astype(jnp.float32)
+def norm_kernel(main_hbm, cont_hbm, gain_hbm, out_ref, main_ref, cont_ref, gain_ref, rows_ref, piece_ref, sems):
+    pairs = ((main_hbm, main_ref), (cont_hbm, cont_ref), (gain_hbm, gain_ref))
+    copies = [pltpu.make_async_copy(src, dst, sems.at[i]) for i, (src, dst) in enumerate(pairs)]
+    for copy in copies:
+        copy.start()
+    for copy in copies:
+        copy.wait()
+
+    def normed(wide):
         inv = lax.rsqrt(jnp.mean(wide * wide, axis=-1, keepdims=True) + EPS)
         return wide * inv * gain_ref[...]
 
-    cont = normed(cont_ref[...]).astype(jnp.bfloat16)
-    main = normed(main_ref[...])
+    for c in range(CONTS):
+        rows_ref[c * STEPS : (c + 1) * STEPS, :] = cont_ref[c].astype(jnp.float32)
+    cont = normed(rows_ref[...]).astype(jnp.bfloat16)
+    main = normed(main_ref[...].astype(jnp.float32))
     for r in range(ROW_BLOCKS):
         for j in range(FEATURES // TILE):
             lanes = slice(r * FEATURES + j * TILE, r * FEATURES + (j + 1) * TILE)
@@ -61,15 +74,35 @@
     return pl.pallas_call(
         norm_kernel,
         out_shape=jax.ShapeDtypeStruct((32, CTOK, FEATURES + TILE), jnp.bfloat16),
-        in_specs=[VMEM] * 3,
+        in_specs=[HBM] * 3,
         out_specs=VMEM,
-        scratch_shapes=[pltpu.VMEM((ROW_BLOCKS, 16, TILE), jnp.float32)],
+        scratch_shapes=[
+            pltpu.VMEM((STEPS, D), jnp.bfloat16),
+            pltpu.VMEM((CONTS, STEPS, D), jnp.bfloat16),
+            pltpu.VMEM((1, D), jnp.float32),
+            pltpu.VMEM((CTOK, D), jnp.float32),
+            pltpu.VMEM((ROW_BLOCKS, 16, TILE), jnp.float32),
+            pltpu.SemaphoreType.DMA((3,)),
+        ],
         compiler_params=kernel_params(),
         cost_estimate=cost(10**6, 4 * 10**6),
         name="norm_rows",
     )(main, cont, gain)
 
 
+def weight_tile(n, tiles, w_hbm, w_ref, sems):
+    def copy(i):
+        lanes = pl.ds(pl.multiple_of(i * TILE, TILE), TILE)
+        return pltpu.make_async_copy(w_hbm.at[0, :, lanes], w_ref.at[i], sems.at[i])
+
+    @pl.when(n == 0)
+    def _():
+        for i in range(tiles):
+            copy(i).start()
+
+    return copy(n)
+
+
 REST = 768
 
 
@@ -77,12 +110,13 @@
     return jnp.where(block == 6, 2, 0)
 
 
-def product_kernel(tiles, rest, x_ref, w_ref, out_ref, rows_ref, wide_ref):
+def product_kernel(tiles, rest, x_ref, w_hbm, out_ref, rows_ref, wide_ref, w_ref, sems):
     n = pl.program_id(0)
     members = x_ref.shape[0]
     count = members * CTOK
     lines = members * STEPS
     halves = TILE // 128
+    tile = weight_tile(n, tiles, w_hbm, w_ref, sems)
 
     @pl.when(n == 0)
     def _():
@@ -94,7 +128,8 @@
                 lane = j * TILE + k * 128
                 rows_ref[count:, lane : lane + 128] = wide_ref[k, pl.ds(j, lines, stride=8), :].astype(jnp.bfloat16)
 
-    prod = jnp.dot(rows_ref[...], w_ref[0], preferred_element_type=jnp.float32)
+    tile.wait()
+    prod = jnp.dot(rows_ref[...], w_ref[n], preferred_element_type=jnp.float32)
     high = prod.astype(jnp.bfloat16)
     out_ref[:, :, pl.ds(pl.multiple_of(n * TILE, TILE), TILE)] = high[:count].reshape(members, CTOK, TILE)
     for k in range(halves):
@@ -126,14 +161,13 @@
         functools.partial(product_kernel, tiles, rest),
         out_shape=jax.ShapeDtypeStruct((members, CTOK, (tiles + 1) * TILE + rest), jnp.bfloat16),
         grid=(tiles,),
-        in_specs=[
-            VMEM,
-            pl.BlockSpec((1, FEATURES, TILE), lambda n: (0, 0, n)),
-        ],
-        out_specs=VMEM,
+        in_specs=[VMEM, HBM],
+        out_specs=whole((members, CTOK, (tiles + 1) * TILE + rest)),
         scratch_shapes=[
             pltpu.VMEM((members * (CTOK + STEPS), FEATURES), jnp.bfloat16),
             pltpu.VMEM((TILE // 128, members * 16, 128), jnp.float32),
+            pltpu.VMEM((tiles, FEATURES, TILE), jnp.bfloat16),
+            pltpu.SemaphoreType.DMA((tiles,)),
         ],
         compiler_params=kernel_params(),
         cost_estimate=cost(2 * members * (CTOK + STEPS) * FEATURES * tiles * TILE, 12 * 10**6),
@@ -255,7 +289,7 @@
             jax.ShapeDtypeStruct((8, 2 * KV_WIDTH), jnp.float32),
         ),
         in_specs=[SMEM] + [VMEM] * 5,
-        out_specs=(VMEM, VMEM),
+        out_specs=(whole((32, 16, TILE)), whole((8, 2 * KV_WIDTH))),
         scratch_shapes=[
             pltpu.VMEM((8, QKV), jnp.float32),
             pltpu.VMEM((ROW_BLOCKS, 16, TILE), jnp.float32),
@@ -267,25 +301,17 @@
 
 
 def attend_cont_kernel(
-    len_ref, bound_ref, parts_ref, bias_ref, cos_ref, sin_ref, cache_ref, kv_ref, cont_ref, head_ref, read_ref,
-    score_ref, qkv_ref, weight_ref,
+    len_ref, bound_ref, parts_ref, bias_ref, cos_ref, sin_ref, cache_ref, kv_ref, out_ref, qkv_ref
 ):
     rows = qkv_ref.shape[0]
     load_qkv(False, parts_ref, qkv_ref)
     plain, rotated = head_readers(qkv_ref, bias_ref, cos_ref, sin_ref)
-    for r in range(ROW_BLOCKS):
-        block = read_ref[r * COL_BLOCKS : (r + 1) * COL_BLOCKS, :]
-        weight_ref[:, r * FEATURES : (r + 1) * FEATURES] = jnp.sum(block, axis=0, keepdims=True)
     seen = lax.broadcasted_iota(jnp.int32, (1, cache_ref.shape[0]), 1) < len_ref[0]
     row = lax.broadcasted_iota(jnp.int32, (rows, 128), 0)
     col = lax.broadcasted_iota(jnp.int32, (rows, 128), 1)
     own = (row // STEPS == col // STEPS) & (col <= row)
     main = (col >= rows) & (col < rows + bound_ref[0])
     fresh_seen = jnp.concatenate([(own | main).astype(jnp.int32)] * GROUP, axis=0) > 0
-    total = jnp.zeros((rows, HD), jnp.float32)
-    for k in range(D // HD):
-        lanes = slice(k * HD, (k + 1) * HD)
-        total = total + cont_ref[:, lanes].astype(jnp.float32) * head_ref[:, lanes]
     for g in range(KVH):
         query = jnp.concatenate([rotated((g * GROUP + h) * HD) for h in range(GROUP)], axis=0).astype(jnp.bfloat16)
         at_key = slice(g * HD, (g + 1) * HD)
@@ -295,35 +321,35 @@
         mixed = head_attention(
             query, cache_ref[:, at_key], cache_ref[:, at_value], fresh_key, fresh_value, seen, fresh_seen
         )
-        mixed = mixed.astype(jnp.bfloat16).astype(jnp.float32)
+        mixed = mixed.astype(jnp.bfloat16)
         for h in range(GROUP):
-            lanes = slice((g * GROUP + h) * HD, (g * GROUP + h + 1) * HD)
-            total = total + mixed[h * rows : (h + 1) * rows] * weight_ref[:, lanes]
-    summed = jnp.sum(jnp.sum(total, axis=1, keepdims=True), axis=0, keepdims=True)
-    score_ref[...] = jnp.broadcast_to(summed / CONTS, (8, 128))
+            out_ref[:, (g * GROUP + h) * HD : (g * GROUP + h + 1) * HD] = mixed[h * rows : (h + 1) * rows]
 
 
 def attend_cont(*args):
     return pl.pallas_call(
         attend_cont_kernel,
-        out_shape=jax.ShapeDtypeStruct((8, 128), jnp.float32),
-        in_specs=[SMEM, SMEM] + [VMEM] * 9,
-        out_specs=VMEM,
-        scratch_shapes=[pltpu.VMEM((CTOK, QKV), jnp.float32), pltpu.VMEM((1, D), jnp.float32)],
+        out_shape=jax.ShapeDtypeStruct((CTOK, D), jnp.bfloat16),
+        in_specs=[SMEM, SMEM] + [VMEM] * 5 + [whole((8, 2 * KV_WIDTH))],
+        out_specs=whole((CTOK, D)),
+        scratch_shapes=[pltpu.VMEM((CTOK, QKV), jnp.float32)],
         compiler_params=kernel_params(),
         cost_estimate=cost(4 * 10**8, 8 * 10**6),
         name="attend_cont",
     )(*args)
 
 
-def readout_kernel(head_ref, w_ref, out_ref):
+def readout_kernel(head_ref, w_hbm, out_ref, w_ref, sem):
+    copy = pltpu.make_async_copy(w_hbm.at[0], w_ref, sem)
+    copy.start()
     row = head_ref[pl.ds(lax.rem(lax.axis_index("tp"), COL_BLOCKS), 1), :]
     high = row.astype(jnp.bfloat16).astype(jnp.float32)
     middle = (row - high).astype(jnp.bfloat16).astype(jnp.float32)
     low = row - high - middle
     pieces = jnp.concatenate([high, middle, low, jnp.zeros((13, row.shape[1]), jnp.float32)], axis=0)
+    copy.wait()
     prod = lax.dot_general(
-        pieces.astype(jnp.bfloat16), w_ref[0], (((1,), (1,)), ((), ())), preferred_element_type=jnp.float32
+        pieces.astype(jnp.bfloat16), w_ref[...], (((1,), (1,)), ((), ())), preferred_element_type=jnp.float32
     )
     out_ref[...] = prod[0:1] + prod[1:2] + prod[2:3]
 
@@ -332,22 +358,27 @@
     return pl.pallas_call(
         readout_kernel,
         out_shape=jax.ShapeDtypeStruct((1, FEATURES), jnp.float32),
-        in_specs=[VMEM, VMEM],
-        out_specs=VMEM,
+        in_specs=[whole(value_head.shape), HBM],
+        out_specs=whole((1, FEATURES)),
+        scratch_shapes=[pltpu.VMEM((FEATURES, D // COL_BLOCKS), jnp.bfloat16), pltpu.SemaphoreType.DMA],
         compiler_params=kernel_params(),
         cost_estimate=cost(2 * 10**8, 5 * 10**6),
         name="readout",
     )(value_head, blocks)
 
 
-def out_kernel(tiles, x_ref, w_ref, out_ref, rows_ref, wide_ref):
+def out_kernel(tiles, x_ref, read_ref, w_hbm, out_ref, rows_ref, wide_ref, read8_ref, w_ref, sems):
     n = pl.program_id(0)
     members = x_ref.shape[0]
     lines = members * STEPS
     halves = TILE // 128
+    tile = weight_tile(n, tiles, w_hbm, w_ref, sems)
 
     @pl.when(n == 0)
     def _():
+        for j in range(FEATURES // TILE):
+            read8_ref[j : j + 1, :] = read_ref[:, j * TILE : (j + 1) * TILE]
+        out_ref[:, 8:, :] = jnp.broadcast_to(read8_ref[...][None], (members, 8, TILE))
         packed = x_ref[...].reshape(members * 16, TILE).astype(jnp.float32)
         for k in range(halves):
             wide_ref[k] = packed[:, k * 128 : (k + 1) * 128]
@@ -355,7 +386,8 @@
                 lane = j * TILE + k * 128
                 rows_ref[:, lane : lane + 128] = wide_ref[k, pl.ds(j, lines, stride=8), :].astype(jnp.bfloat16)
 
-    prod = jnp.dot(rows_ref[...], w_ref[0], preferred_element_type=jnp.float32)
+    tile.wait()
+    prod = jnp.dot(rows_ref[...], w_ref[n], preferred_element_type=jnp.float32)
     for k in range(halves):
         wide_ref[k, pl.ds(n, lines, stride=4), :] = prod[:, k * 128 : (k + 1) * 128]
 
@@ -363,32 +395,32 @@
     def _():
         for k in range(halves):
             packed = wide_ref[k, : members * 8, :].reshape(members, 8, 128)
-            out_ref[:, :, k * 128 : (k + 1) * 128] = packed
-
-
-def out_product(rows, blocks):
+            out_ref[:, :8, k * 128 : (k + 1) * 128] = packed
+
+
+def out_product(rows, read, blocks):
     members = rows.shape[0]
     tiles = blocks.shape[2] // TILE
     return pl.pallas_call(
         functools.partial(out_kernel, tiles),
-        out_shape=jax.ShapeDtypeStruct((members, 8, TILE), jnp.float32),
+        out_shape=jax.ShapeDtypeStruct((members, 16, TILE), jnp.float32),
         grid=(tiles,),
-        in_specs=[
-            VMEM,
-            pl.BlockSpec((1, FEATURES, TILE), lambda n: (0, 0, n)),
-        ],
-        out_specs=VMEM,
+        in_specs=[whole(rows.shape), whole(read.shape), HBM],
+        out_specs=whole((members, 16, TILE)),
         scratch_shapes=[
             pltpu.VMEM((members * STEPS, FEATURES), jnp.bfloat16),
             pltpu.VMEM((TILE // 128, members * 16, 128), jnp.float32),
+            pltpu.VMEM((8, TILE), jnp.float32),
+            pltpu.VMEM((tiles, FEATURES, TILE), jnp.bfloat16),
+            pltpu.SemaphoreType.DMA((tiles,)),
         ],
         compiler_params=kernel_params(),
         cost_estimate=cost(3 * 10**8, 5 * 10**6),
         name="out_product",
-    )(rows, blocks)
-
-
-def finish_kernel(parts_ref, main_ref, out_ref, wide_ref):
+    )(rows, read, blocks)
+
+
+def finish_kernel(parts_ref, main_ref, cont_ref, head_ref, mixed_ref, out_ref, score_ref, wide_ref):
     cols = D // COL_BLOCKS
     for c in range(COL_BLOCKS):
         total = summed_block(parts_ref, c, slice(0, TILE))
@@ -397,19 +429,35 @@
             for s in range(STEPS):
                 wide_ref[s : s + 1, at] = total[s * 4 + j : s * 4 + j + 1]
     out_ref[...] = (main_ref[...].astype(jnp.float32) + wide_ref[:STEPS, :]).astype(jnp.bfloat16)
-
-
-def finish(parts, main):
+    score = jnp.zeros((CTOK, TILE), jnp.float32)
+    direct = jnp.zeros((STEPS, TILE), jnp.float32)
+    for r in range(ROW_BLOCKS):
+        read = parts_ref[r * COL_BLOCKS, 8:, :]
+        for c in range(1, COL_BLOCKS):
+            read = read + parts_ref[r * COL_BLOCKS + c, 8:, :]
+        for j in range(FEATURES // TILE):
+            lanes = slice(r * FEATURES + j * TILE, r * FEATURES + (j + 1) * TILE)
+            score = score + mixed_ref[:, lanes].astype(jnp.float32) * read[j : j + 1, :]
+            for c in range(CONTS):
+                direct = direct + cont_ref[c, :, lanes].astype(jnp.float32) * head_ref[:, lanes]
+    total = jnp.sum(score, axis=0, keepdims=True) + jnp.sum(direct, axis=0, keepdims=True)
+    score_ref[...] = jnp.broadcast_to(jnp.sum(total, axis=1, keepdims=True) / CONTS, (8, 128))
+
+
+def finish(parts, main, cont, head, mixed):
     return pl.pallas_call(
         finish_kernel,
-        out_shape=jax.ShapeDtypeStruct((STEPS, D), jnp.bfloat16),
-        in_specs=[VMEM] * 2,
-        out_specs=VMEM,
+        out_shape=(
+            jax.ShapeDtypeStruct((STEPS, D), jnp.bfloat16),
+            jax.ShapeDtypeStruct((8, 128), jnp.float32),
+        ),
+        in_specs=[whole(parts.shape), VMEM, VMEM, VMEM, whole(mixed.shape)],
+        out_specs=(whole((STEPS, D)), whole((8, 128))),
         scratch_shapes=[pltpu.VMEM((8, D), jnp.float32)],
         compiler_params=kernel_params(),
         cost_estimate=cost(10**6, 2 * 10**6),
         name="finish",
-    )(parts, main)
+    )(parts, main, cont, head, mixed)
 
 
 def rope_tables(positions):
@@ -429,20 +477,21 @@
     main_inputs, cont_inputs, prefix_cache, prefix_len, boundary, rms_gain, qkv_bias, w_qkv, w_out, value_head
 ):
     main = main_inputs.reshape(STEPS, D)
-    cont = cont_inputs.reshape(CTOK, D)
+    cont = cont_inputs.reshape(CONTS, STEPS, D)
     bias = qkv_bias[None, :]
     cache = prefix_cache[0]
     head = value_head[None, :]
     step = jnp.arange(CTOK, dtype=jnp.int32) % STEPS
     main_tables = rope_tables(prefix_len + step[:8])
     cont_tables = rope_tables(prefix_len + boundary + step)
-    read = lax.all_gather(readout(value_head.reshape(COL_BLOCKS, D // COL_BLOCKS), w_out), "tp", axis=0, tiled=True)
+    read = readout(value_head.reshape(COL_BLOCKS, D // COL_BLOCKS), w_out)
     sent = exchange(norm_rows(main, cont, rms_gain[None, :]))
     parts = exchange(block_product(sent, w_qkv, REST))
     mixed, main_kv = attend_main(prefix_len, parts, bias, *main_tables, cache)
     mixed = exchange(mixed)
-    score = attend_cont(prefix_len, boundary, parts, bias, *cont_tables, cache, main_kv, cont, head, read)
-    main_out = finish(exchange(out_product(mixed, w_out)), main)
+    cont_mixed = attend_cont(prefix_len, boundary, parts, bias, *cont_tables, cache, main_kv)
+    parts = exchange(out_product(mixed, read, w_out))
+    main_out, score = finish(parts, main, cont, head, cont_mixed)
     return main_out[None], score[0, :1]
 
 

time: 209 us -> 133 us (0.64)
  blocking collectives: 123 us -> 40.7 us
  waiting for transfers between devices: 34.1 us -> 39.6 us
    all_gather x1 -> x0, blocking collectives: 82.6 us -> none  [on_device(): lax.all_gather(readout(value_head.reshape(COL_BLOCKS, D // COL_BLOCKS), w...]
    all_to_all x3, waiting for transfers between devices: 34.1 us -> 39.6 us  [exchange(): return lax.all_to_all(rows, 'tp', split_axis=0, concat_axis=0, tiled=True)]
    unnamed x31 -> x34, local copies, waits for them, and re-layouts: 11.3 us -> 13.9 us
  transfers between devices with their start and end apart: 3 -> 3, of which waited for: 2 -> 3; matrix products, arithmetic and copies ran while one was open for 1% -> 0% of each run, Pallas kernels for 2% -> 3%
where the time goes in v2:
time: 133 us; the launch traced here: 132 us
  blocking collectives  40.7 us (31%)
  waiting for transfers between devices  39.6 us (30%)
  Pallas kernels  18.6 us (14%)
  starting transfers between devices  16.6 us (12%)
  local copies, waits for them, and re-layouts  14.4 us (11%)
  between operations  2.12 us (2%)
    all_to_all x1, blocking collectives, exchange(): return lax.all_to_all(rows, 'tp', split_axis=0, concat_axis=0, tiled=True)  40.7 us
    all_to_all x3, waiting for transfers between devices, exchange(): return lax.all_to_all(rows, 'tp', split_axis=0, concat_axis=0, tiled=True)  39.6 us
    all_to_all x3, starting transfers between devices, exchange(): return lax.all_to_all(rows, 'tp', split_axis=0, concat_axis=0, tiled=True)  16.6 us
    unnamed x34, local copies, waits for them, and re-layouts  13.9 us
    pallas_call x1, Pallas kernels, block_product(): pl.pallas_call(functools.partial(product_kernel, tiles, rest), out_shape=...  5.48 us
    pallas_call x1, Pallas kernels, out_product(): pl.pallas_call(functools.partial(out_kernel, tiles), out_shape=jax.ShapeD...  3 us
    pallas_call x1, Pallas kernels, attend_cont(): pl.pallas_call(attend_cont_kernel, out_shape=jax.ShapeDtypeStruct((CTOK,...  3 us
    pallas_call x1, Pallas kernels, attend_main(): pl.pallas_call(attend_main_kernel, out_shape=(jax.ShapeDtypeStruct((32, 1...  2.99 us
  transfers between devices with their start and end apart: 3, of which 3 were waited for; matrix products, arithmetic and copies ran while one was open for 0% of the time, Pallas kernels for 3%

profile of v2, /device:TPU:0, one launch (start us, length us, event | category | flops | bytes accessed | tf_op | source)
XLA Modules:
  0.0 132.4 jit_solution(15364916369280120998)
XLA Ops:
  0.6 0.9 copy-done.7
  1.6 0.8 copy-done.11
  2.3 0.8 copy-done.16
  3.7 40.7 %all_to_all.20.x_ref = bf16[32,16,2304]{2,1,0:T(8,128)(2,1)S(1)} all-to-all(bf16[32,16,2304]{2,1,0:T(8,128)(2,1)S(1)} %norm_rows.1), channel_id=1, replica_groups=mesh['grp'=4,'tp'=32] {'tp'}, dimensions={0} | all-to-all | bytes 4718592 | tf_op jit(solution)/shard_map/all_to_all | solution.py:473
  44.5 5.5 %block_product.1 = bf16[32,16,2304]{2,1,0:T(8,128)(2,1)S(1)} custom-call(bf16[32,16,2304]{2,1,0:T(8,128)(2,1)S(1)} %all_to_all.20.x_ref, bf16[1,2048,1280]{2,1,0:T(8,128)(2,1)} %w_hbm.3), custom_call_target="tpu_custom_call" | custom-call | flops 3019898880 | bytes 12000000 | tf_op jit(solution)/shard_map/block_product/pallas_call | solution.py:160
  50.0 1.4 %copy-done.3 = bf16[32,16,2304]{2,1,0:T(8,128)(2,1)} copy-done((bf16[32,16,2304]{2,1,0:T(8,128)(2,1)}, bf16[32,16,2304]{2,1,0:T(8,128)(2,1)S(1)}, u32[]{:S(2)}) %copy-start.3) | copy-done | bytes 2359320
  51.4 4.2 %all-to-all-start.1 = ((bf16[32,16,2304]{2,1,0:T(8,128)(2,1)}), bf16[32,16,2304]{2,1,0:T(8,128)(2,1)S(1)}, u32[]{:S(2)}, u32[]{:S(2)}) async-start(bf16[32,16,2304]{2,1,0:T(8,128)(2,1)} %copy-done.3), calls=%async_computation.1 | async-start | bytes 4718592 | tf_op jit(solution)/shard_map/all_to_all | solution.py:473
  56.5 29.1 %all-to-all-done.1.parts_ref = bf16[32,16,2304]{2,1,0:T(8,128)(2,1)S(1)} async-done(((bf16[32,16,2304]{2,1,0:T(8,128)(2,1)}), bf16[32,16,2304]{2,1,0:T(8,128)(2,1)S(1)}, u32[]{:S(2)}, u32[]{:S(2)}) %all-to-all-start.1) | async-done | bytes 2359328 | tf_op jit(solution)/shard_map/all_to_all | solution.py:473
  85.6 3.0 %attend_main.1 = (bf16[32,16,256]{2,1,0:T(8,128)(2,1)S(1)}, f32[8,2048]{1,0:T(8,128)S(1)}) custom-call(s32[1]{0:T(128)} %copy.12.len_ref, bf16[32,16,2304]{2,1,0:T(8,128)(2,1)S(1)} %all-to-all-done.1.parts_ref, f32[1,10240]{1,0:T(1,128)S(1)} %bitcast.15, f32[8,128]{1,0:T(8,128)S(1)} %get-tuple-element.16.cos_ref, f32[8,128]{1,0:T(8,128)S(1)} %get-tuple-element.17.sin_ref, ...), custom_call_target="tpu_custom_call" | custom-call | flops 200000000 | bytes 6000000 | tf_op jit(solution)/shard_map/attend_main/pallas_call | solution.py:285
  88.6 0.7 copy-done.9
  90.0 7.6 %all-to-all-start.2 = ((bf16[32,16,256]{2,1,0:T(8,128)(2,1)}), bf16[32,16,256]{2,1,0:T(8,128)(2,1)}, u32[]{:S(2)}, u32[]{:S(2)}) async-start(bf16[32,16,256]{2,1,0:T(8,128)(2,1)} %copy-done.9), calls=%async_computation.2 | async-start | bytes 524288 | tf_op jit(solution)/shard_map/all_to_all | solution.py:473
  97.6 2.2 %copy-done = bf16[1,2048,1024]{2,1,0:T(8,128)(2,1)S(1)} copy-done((bf16[1,2048,1024]{2,1,0:T(8,128)(2,1)S(1)}, bf16[1,2048,1024]{2,1,0:T(8,128)(2,1)}, u32[]{:S(2)}) %copy-start) | copy-done | bytes 4194328
  99.8 1.5 %readout.1.read_ref = f32[1,2048]{1,0:T(1,128)S(1)} custom-call(f32[8,1024]{1,0:T(8,128)S(1)} %reshape.34.head_ref, bf16[1,2048,1024]{2,1,0:T(8,128)(2,1)S(1)} %copy-done), custom_call_target="tpu_custom_call" | custom-call | flops 200000000 | bytes 5000000 | tf_op jit(solution)/shard_map/readout/pallas_call | solution.py:358
  101.4 5.4 %all-to-all-done.2.x_ref = bf16[32,16,256]{2,1,0:T(8,128)(2,1)} async-done(((bf16[32,16,256]{2,1,0:T(8,128)(2,1)}), bf16[32,16,256]{2,1,0:T(8,128)(2,1)}, u32[]{:S(2)}, u32[]{:S(2)}) %all-to-all-start.2) | async-done | bytes 262176 | tf_op jit(solution)/shard_map/all_to_all | solution.py:473
  106.8 2.2 %copy-done.1 = bf16[1,2048,1024]{2,1,0:T(8,128)(2,1)S(1)} copy-done((bf16[1,2048,1024]{2,1,0:T(8,128)(2,1)S(1)}, bf16[1,2048,1024]{2,1,0:T(8,128)(2,1)}, u32[]{:S(2)}) %copy-start.1) | copy-done | bytes 4194328
  109.0 3.0 %out_product.1 = f32[32,16,256]{2,1,0:T(8,128)S(1)} custom-call(bf16[32,16,256]{2,1,0:T(8,128)(2,1)} %all-to-all-done.2.x_ref, f32[1,2048]{1,0:T(1,128)S(1)} %readout.1.read_ref, bf16[1,2048,1024]{2,1,0:T(8,128)(2,1)S(1)} %copy-done.1), custom_call_target="tpu_custom_call" | custom-call | flops 300000000 | bytes 5000000 | tf_op jit(solution)/shard_map/out_product/pallas_call | solution.py:404
  112.0 0.8 copy-done.4
  112.8 4.7 %all-to-all-start.3 = ((f32[32,16,256]{2,1,0:T(8,128)}), f32[32,16,256]{2,1,0:T(8,128)}, u32[]{:S(2)}, u32[]{:S(2)}) async-start(f32[32,16,256]{2,1,0:T(8,128)} %copy-done.4), calls=%async_computation.3 | async-start | bytes 1048576 | tf_op jit(solution)/shard_map/all_to_all | solution.py:473
  118.4 0.8 copy-done.15
  119.3 3.0 %attend_cont.1.mixed_ref = bf16[16,8192]{1,0:T(8,128)(2,1)S(1)} custom-call(s32[1]{0:T(128)} %copy.12.len_ref, s32[1]{0:T(128)S(6)} %copy.13.bound_ref, bf16[32,16,2304]{2,1,0:T(8,128)(2,1)S(1)} %all-to-all-done.1.parts_ref, f32[1,10240]{1,0:T(1,128)S(1)} %bitcast.16, f32[16,128]{1,0:T(8,128)S(1)} %get-tuple-element.18.cos_ref, ...), custom_call_target="tpu_custom_call" | custom-call | flops 400000000 | bytes 8000000 | tf_op jit(solution)/shard_map/attend_cont/pallas_call | solution.py:330
  123.0 5.0 %all-to-all-done.3.parts_ref = f32[32,16,256]{2,1,0:T(8,128)} async-done(((f32[32,16,256]{2,1,0:T(8,128)}), f32[32,16,256]{2,1,0:T(8,128)}, u32[]{:S(2)}, u32[]{:S(2)}) %all-to-all-start.3) | async-done | bytes 524320 | tf_op jit(solution)/shard_map/all_to_all | solution.py:473
  128.0 0.9 copy-done.6
  129.0 0.9 copy-done.8
  129.9 2.0 %finish.1 = (bf16[2,8192]{1,0:T(2,128)(2,1)}, f32[8,128]{1,0:T(8,128)S(1)}) custom-call(f32[32,16,256]{2,1,0:T(8,128)} %all-to-all-done.3.parts_ref, bf16[2,8192]{1,0:T(2,128)(2,1)S(1)} %bitcast.18, bf16[8,2,8192]{2,1,0:T(2,128)(2,1)S(1)} %bitcast.14, f32[1,8192]{1,0:T(1,128)S(1)} %bitcast.19, bf16[16,8192]{1,0:T(8,128)(2,1)S(1)} %copy-done.6), custom_call_target="tpu_custom_call" | custom-call | flops 1000000 | bytes 2000000 | tf_op jit(solution)/shard_map/finish/pallas_call | solution.py:448
  (34 shorter events, 2.9 us)
Async XLA Ops:
  0.6 1.0 copy-start.7
  1.6 0.8 copy-start.11
  2.3 0.8 copy-start.16
  50.0 1.4 %copy-start.3 = (bf16[32,16,2304]{2,1,0:T(8,128)(2,1)}, bf16[32,16,2304]{2,1,0:T(8,128)(2,1)S(1)}, u32[]{:S(2)}) copy-start(bf16[32,16,2304]{2,1,0:T(8,128)(2,1)S(1)} %block_product.1) | copy-start | bytes 7077892
  51.4 34.2 %copy-start.2 = (bf16[1,256,2048]{2,1,0:T(8,128)(2,1)S(1)}, bf16[1,256,2048]{2,1,0:T(8,128)(2,1)}, u32[]{:S(2)}) copy-start(bf16[1,256,2048]{2,1,0:T(8,128)(2,1)} %param.12) | copy-start | bytes 3145732
  51.4 34.2 %copy-start.10 = (f32[10240]{0:T(1024)S(1)}, f32[10240]{0:T(1024)}, u32[]{:S(2)}) copy-start(f32[10240]{0:T(1024)} %param.16) | copy-start | bytes 122884
  51.4 34.2 %all-to-all-start.1 = ((bf16[32,16,2304]{2,1,0:T(8,128)(2,1)}), bf16[32,16,2304]{2,1,0:T(8,128)(2,1)S(1)}, u32[]{:S(2)}, u32[]{:S(2)}) async-start(bf16[32,16,2304]{2,1,0:T(8,128)(2,1)} %copy-done.3), calls=%async_computation.1 | async-start | bytes 4718592 | tf_op jit(solution)/shard_map/all_to_all | solution.py:473
  55.6 42.0 %copy-start.13 = (f32[8192]{0:T(1024)S(1)}, f32[8192]{0:T(1024)}, u32[]{:S(2)}) copy-start(f32[8192]{0:T(1024)} %param.19) | copy-start | bytes 98308
  88.6 0.7 copy-start.9
  89.3 0.6 copy-start.14
  90.0 16.8 %all-to-all-start.2 = ((bf16[32,16,256]{2,1,0:T(8,128)(2,1)}), bf16[32,16,256]{2,1,0:T(8,128)(2,1)}, u32[]{:S(2)}, u32[]{:S(2)}) async-start(bf16[32,16,256]{2,1,0:T(8,128)(2,1)} %copy-done.9), calls=%async_computation.2 | async-start | bytes 524288 | tf_op jit(solution)/shard_map/all_to_all | solution.py:473
  97.6 2.2 %copy-start = (bf16[1,2048,1024]{2,1,0:T(8,128)(2,1)S(1)}, bf16[1,2048,1024]{2,1,0:T(8,128)(2,1)}, u32[]{:S(2)}) copy-start(bf16[1,2048,1024]{2,1,0:T(8,128)(2,1)} %w_hbm.5) | copy-start | bytes 12582916
  106.8 2.2 %copy-start.1 = (bf16[1,2048,1024]{2,1,0:T(8,128)(2,1)S(1)}, bf16[1,2048,1024]{2,1,0:T(8,128)(2,1)}, u32[]{:S(2)}) copy-start(bf16[1,2048,1024]{2,1,0:T(8,128)(2,1)} %w_hbm.5) | copy-start | bytes 12582916
  112.0 0.8 copy-start.4
  112.8 15.2 %copy-start.12 = (bf16[1,2,8192]{2,1,0:T(2,128)(2,1)S(1)}, bf16[1,2,8192]{2,1,0:T(2,128)(2,1)}, u32[]{:S(2)}) copy-start(bf16[1,2,8192]{2,1,0:T(2,128)(2,1)} %param.10) | copy-start | bytes 98308
  112.8 15.2 %all-to-all-start.3 = ((f32[32,16,256]{2,1,0:T(8,128)}), f32[32,16,256]{2,1,0:T(8,128)}, u32[]{:S(2)}, u32[]{:S(2)}) async-start(f32[32,16,256]{2,1,0:T(8,128)} %copy-done.4), calls=%async_computation.3 | async-start | bytes 1048576 | tf_op jit(solution)/shard_map/all_to_all | solution.py:473
  118.4 0.8 copy-start.15
  122.3 0.7 copy-start.5
  128.0 1.0 copy-start.6
  129.0 0.9 copy-start.8

commit v3 on v2

--- a/solution.py
+++ b/solution.py
@@ -14,6 +14,7 @@
 QKV = 10240
 ROW_BLOCKS = 4
 COL_BLOCKS = 8
+MEMBERS = ROW_BLOCKS * COL_BLOCKS
 FEATURES = D // ROW_BLOCKS
 CONTS = 8
 STEPS = 2
@@ -25,6 +26,8 @@
 MASKED_SCORE = -1e30
 
 VMEM_LIMIT = 48 * 1024 * 1024
+VMEM_MOST = 60 * 1024 * 1024
+VMEM_LESS = 32 * 1024 * 1024
 VMEM = pl.BlockSpec(memory_space=pltpu.VMEM)
 SMEM = pl.BlockSpec(memory_space=pltpu.SMEM)
 HBM = pl.BlockSpec(memory_space=pltpu.HBM)
@@ -38,8 +41,8 @@
     return pl.CostEstimate(flops=flops, bytes_accessed=moved, transcendentals=0)
 
 
-def kernel_params():
-    return pltpu.CompilerParams(vmem_limit_bytes=VMEM_LIMIT)
+def kernel_params(limit=VMEM_LIMIT):
+    return pltpu.CompilerParams(vmem_limit_bytes=limit)
 
 
 def norm_kernel(main_hbm, cont_hbm, gain_hbm, out_ref, main_ref, cont_ref, gain_ref, rows_ref, piece_ref, sems):
@@ -65,15 +68,14 @@
                 piece_ref[r, s * 8 + j : s * 8 + j + 1, :] = main[s : s + 1, lanes]
     for r in range(ROW_BLOCKS):
         piece = piece_ref[r].astype(jnp.bfloat16)
-        for c in range(COL_BLOCKS):
-            out_ref[r * COL_BLOCKS + c, :, :FEATURES] = cont[:, r * FEATURES : (r + 1) * FEATURES]
-            out_ref[r * COL_BLOCKS + c, :, FEATURES:] = piece
+        out_ref[r, :, :FEATURES] = cont[:, r * FEATURES : (r + 1) * FEATURES]
+        out_ref[r, :, FEATURES:] = piece
 
 
 def norm_rows(main, cont, gain):
     return pl.pallas_call(
         norm_kernel,
-        out_shape=jax.ShapeDtypeStruct((32, CTOK, FEATURES + TILE), jnp.bfloat16),
+        out_shape=jax.ShapeDtypeStruct((ROW_BLOCKS, CTOK, FEATURES + TILE), jnp.bfloat16),
         in_specs=[HBM] * 3,
         out_specs=VMEM,
         scratch_shapes=[
@@ -110,20 +112,32 @@
     return jnp.where(block == 6, 2, 0)
 
 
-def product_kernel(tiles, rest, x_ref, w_hbm, out_ref, rows_ref, wide_ref, w_ref, sems):
+def product_kernel(tiles, counts, places, *refs):
+    x_refs = refs[: len(counts)]
+    refs = refs[len(counts) :]
+    if places:
+        earlier_ref, w_hbm, out_ref, rows_ref, wide_ref, w_ref, sems, part_ref = refs
+    else:
+        w_hbm, part_ref, rows_ref, wide_ref, w_ref, sems = refs
     n = pl.program_id(0)
-    members = x_ref.shape[0]
+    members = sum(counts)
     count = members * CTOK
     lines = members * STEPS
     halves = TILE // 128
+    width = tiles * TILE
     tile = weight_tile(n, tiles, w_hbm, w_ref, sems)
 
     @pl.when(n == 0)
     def _():
-        rows_ref[:count, :] = x_ref[:, :, :FEATURES].reshape(count, FEATURES)
-        packed = x_ref[:, :, FEATURES:].reshape(members * 16, TILE).astype(jnp.float32)
+        at = 0
+        for x_ref, size in zip(x_refs, counts):
+            rows = slice(at * CTOK, (at + size) * CTOK)
+            rows_ref[rows, :] = x_ref[:, :, :FEATURES].reshape(size * CTOK, FEATURES)
+            packed = x_ref[:, :, FEATURES:].reshape(size * CTOK, TILE).astype(jnp.float32)
+            for k in range(halves):
+                wide_ref[k, rows, :] = packed[:, k * 128 : (k + 1) * 128]
+            at += size
         for k in range(halves):
-            wide_ref[k] = packed[:, k * 128 : (k + 1) * 128]
             for j in range(FEATURES // TILE):
                 lane = j * TILE + k * 128
                 rows_ref[count:, lane : lane + 128] = wide_ref[k, pl.ds(j, lines, stride=8), :].astype(jnp.bfloat16)
@@ -131,48 +145,68 @@
     tile.wait()
     prod = jnp.dot(rows_ref[...], w_ref[n], preferred_element_type=jnp.float32)
     high = prod.astype(jnp.bfloat16)
-    out_ref[:, :, pl.ds(pl.multiple_of(n * TILE, TILE), TILE)] = high[:count].reshape(members, CTOK, TILE)
+    part_ref[:, :, pl.ds(pl.multiple_of(n * TILE, TILE), TILE)] = high[:count].reshape(members, CTOK, TILE)
     for k in range(halves):
         wide_ref[k, pl.ds(n, lines, stride=8), :] = prod[count:, k * 128 : (k + 1) * 128]
-    width = tiles * TILE
-    if rest:
-        start = rest_tile(lax.rem(lax.axis_index("tp"), COL_BLOCKS))
-
-        @pl.when((n >= start) & (n < start + rest // TILE))
-        def _():
-            low = prod - high.astype(jnp.float32)
-            place = n - start
-            lane = pl.multiple_of(width + place * TILE, TILE)
-            out_ref[:, :, pl.ds(lane, TILE)] = low[:count].astype(jnp.bfloat16).reshape(members, CTOK, TILE)
-            for k in range(halves):
-                wide_ref[k, pl.ds(tiles + place, lines, stride=8), :] = low[count:, k * 128 : (k + 1) * 128]
+    start = rest_tile(lax.rem(lax.axis_index("tp"), COL_BLOCKS))
+
+    @pl.when((n >= start) & (n < start + REST // TILE))
+    def _():
+        low = prod - high.astype(jnp.float32)
+        place = n - start
+        lane = pl.multiple_of(width + place * TILE, TILE)
+        part_ref[:, :, pl.ds(lane, TILE)] = low[:count].astype(jnp.bfloat16).reshape(members, CTOK, TILE)
+        for k in range(halves):
+            wide_ref[k, pl.ds(tiles + place, lines, stride=8), :] = low[count:, k * 128 : (k + 1) * 128]
 
     @pl.when(n == tiles - 1)
     def _():
         for k in range(halves):
-            lane = width + rest + k * 128
-            out_ref[:, :, lane : lane + 128] = wide_ref[k].astype(jnp.bfloat16).reshape(members, 16, 128)
-
-
-def block_product(rows, blocks, rest):
-    members = rows.shape[0]
+            lane = width + REST + k * 128
+            part_ref[:, :, lane : lane + 128] = wide_ref[k].astype(jnp.bfloat16).reshape(members, CTOK, 128)
+        if places:
+            me = lax.rem(lax.axis_index("tp"), COL_BLOCKS)
+            y, x = me // 4, lax.rem(me, 4)
+            done = earlier_ref.shape[0] // ROW_BLOCKS
+            for i, (dy, dx) in enumerate(places):
+                column = lax.rem(y + dy, 2) * 4 + lax.rem(x + dx, 4)
+                for z in range(ROW_BLOCKS):
+                    if i < done:
+                        message = earlier_ref[i * ROW_BLOCKS + z]
+                    else:
+                        message = part_ref[(i - done) * ROW_BLOCKS + z]
+                    out_ref[z * COL_BLOCKS + column] = message
+
+
+def block_product(messages, blocks, earlier=None, places=()):
     tiles = blocks.shape[2] // TILE
-    return pl.pallas_call(
-        functools.partial(product_kernel, tiles, rest),
-        out_shape=jax.ShapeDtypeStruct((members, CTOK, (tiles + 1) * TILE + rest), jnp.bfloat16),
+    lanes = (tiles + 1) * TILE + REST
+    counts = tuple(rows.shape[0] for rows in messages)
+    members = sum(counts)
+    part = (members, CTOK, lanes)
+    scratch = [
+        pltpu.VMEM((members * (CTOK + STEPS), FEATURES), jnp.bfloat16),
+        pltpu.VMEM((TILE // 128, members * CTOK, 128), jnp.float32),
+        pltpu.VMEM((tiles, FEATURES, TILE), jnp.bfloat16),
+        pltpu.SemaphoreType.DMA((tiles,)),
+    ]
+    operands = list(messages)
+    out = part
+    if places:
+        operands.append(earlier)
+        out = (MEMBERS, CTOK, lanes)
+        scratch.append(pltpu.VMEM(part, jnp.bfloat16))
+    return pl.pallas_call(
+        functools.partial(product_kernel, tiles, counts, places),
+        out_shape=jax.ShapeDtypeStruct(out, jnp.bfloat16),
         grid=(tiles,),
-        in_specs=[VMEM, HBM],
-        out_specs=whole((members, CTOK, (tiles + 1) * TILE + rest)),
-        scratch_shapes=[
-            pltpu.VMEM((members * (CTOK + STEPS), FEATURES), jnp.bfloat16),
-            pltpu.VMEM((TILE // 128, members * 16, 128), jnp.float32),
-            pltpu.VMEM((tiles, FEATURES, TILE), jnp.bfloat16),
-            pltpu.SemaphoreType.DMA((tiles,)),
-        ],
-        compiler_params=kernel_params(),
+        in_specs=[VMEM] * len(operands) + [HBM],
+        out_specs=whole(out) if places else VMEM,
+        scratch_shapes=scratch,
+        compiler_params=kernel_params(VMEM_LESS),
         cost_estimate=cost(2 * members * (CTOK + STEPS) * FEATURES * tiles * TILE, 12 * 10**6),
         name="block_product",
-    )(rows, blocks)
+    )(*operands, blocks)
 
 
 def summed_block(parts_ref, c, lanes):
@@ -414,7 +448,7 @@
             pltpu.VMEM((tiles, FEATURES, TILE), jnp.bfloat16),
             pltpu.SemaphoreType.DMA((tiles,)),
         ],
-        compiler_params=kernel_params(),
+        compiler_params=kernel_params(VMEM_MOST),
         cost_estimate=cost(3 * 10**8, 5 * 10**6),
         name="out_product",
     )(rows, read, blocks)
@@ -451,10 +485,10 @@
             jax.ShapeDtypeStruct((STEPS, D), jnp.bfloat16),
             jax.ShapeDtypeStruct((8, 128), jnp.float32),
         ),
-        in_specs=[whole(parts.shape), VMEM, VMEM, VMEM, whole(mixed.shape)],
+        in_specs=[whole(parts.shape), whole(main.shape), whole(cont.shape), whole(head.shape), whole(mixed.shape)],
         out_specs=(whole((STEPS, D)), whole((8, 128))),
         scratch_shapes=[pltpu.VMEM((8, D), jnp.float32)],
-        compiler_params=kernel_params(),
+        compiler_params=kernel_params(VMEM_MOST),
         cost_estimate=cost(10**6, 2 * 10**6),
         name="finish",
     )(parts, main, cont, head, mixed)
@@ -471,6 +505,32 @@
 
 def exchange(rows):
     return lax.all_to_all(rows, "tp", split_axis=0, concat_axis=0, tiled=True)
+
+
+ALONG = [[z * COL_BLOCKS + c for z in range(ROW_BLOCKS)] for c in range(COL_BLOCKS)]
+
+
+def from_side(rows, dy, dx):
+    route = []
+    for to in range(MEMBERS):
+        z, y, x = to // 8, to // 4 % 2, to % 4
+        route.append((z * 8 + (y + dy) % 2 * 4 + (x + dx) % 4, to))
+    return lax.ppermute(rows, "tp", route)
+
+
+def forward_product(rows, blocks):
+    near = lax.all_to_all(rows, "tp", split_axis=0, concat_axis=0, tiled=True, axis_index_groups=ALONG)
+    half = ROW_BLOCKS // 2
+    over = from_side(near, 1, 0)
+    here, far, places = [], [], []
+    for dy, mine in ((0, near), (1, over)):
+        after = from_side(mine, 0, 1)
+        before = from_side(mine, 0, 3)
+        far += [from_side(before[:half], 0, 3), from_side(after[half:], 0, 1)]
+        here += [mine, after, before]
+        places += [(dy, 0), (dy, 1), (dy, 3)]
+    earlier = block_product(here, blocks)
+    return block_product(far, blocks, earlier, tuple(places) + ((0, 2), (1, 2)))
 
 
 def on_device(
@@ -485,11 +545,11 @@
     main_tables = rope_tables(prefix_len + step[:8])
     cont_tables = rope_tables(prefix_len + boundary + step)
     read = readout(value_head.reshape(COL_BLOCKS, D // COL_BLOCKS), w_out)
-    sent = exchange(norm_rows(main, cont, rms_gain[None, :]))
-    parts = exchange(block_product(sent, w_qkv, REST))
+    parts = exchange(forward_product(norm_rows(main, cont, rms_gain[None, :]), w_qkv))
     mixed, main_kv = attend_main(prefix_len, parts, bias, *main_tables, cache)
     mixed = exchange(mixed)
     cont_mixed = attend_cont(prefix_len, boundary, parts, bias, *cont_tables, cache, main_kv)
+    mixed, cont_mixed, read = lax.optimization_barrier((mixed, cont_mixed, read))
     parts = exchange(out_product(mixed, read, w_out))
     main_out, score = finish(parts, main, cont, head, cont_mixed)
     return main_out[None], score[0, :1]

time: 133 us -> 125 us (0.940)
  blocking collectives: 40.7 us -> 31.4 us
  starting transfers between devices: 16.6 us -> 25.8 us
  waiting for transfers between devices: 39.6 us -> 30.7 us
  Pallas kernels: 18.6 us -> 21 us
  local copies, waits for them, and re-layouts: 14.4 us -> 12.4 us
    all_to_all x1, blocking collectives: 40.7 us -> 19.2 us  [exchange(): return lax.all_to_all(rows, 'tp', split_axis=0, concat_axis=0, tiled=True)]
    all_to_all x3 -> x2, waiting for transfers between devices: 39.6 us -> 24.5 us  [exchange(): return lax.all_to_all(rows, 'tp', split_axis=0, concat_axis=0, tiled=True)]
    ppermute x0 -> x9, starting transfers between devices: none -> 14.8 us  [from_side(): return lax.ppermute(rows, 'tp', route)]
    all_to_all x0 -> x1, blocking collectives: none -> 12.2 us  [forward_product(): lax.all_to_all(rows, 'tp', split_axis=0, concat_axis=0, tiled=True, axis_...]
    ppermute x0 -> x9, waiting for transfers between devices: none -> 6.23 us  [from_side(): return lax.ppermute(rows, 'tp', route)]
    all_to_all x3 -> x2, starting transfers between devices: 16.6 us -> 11 us  [exchange(): return lax.all_to_all(rows, 'tp', split_axis=0, concat_axis=0, tiled=True)]
    unnamed x34 -> x28, local copies, waits for them, and re-layouts: 13.9 us -> 10.4 us
    pallas_call x1, Pallas kernels: 3 us -> 4.36 us  [out_product(): pl.pallas_call(functools.partial(out_kernel, tiles), out_shape=jax.ShapeD...]
  transfers between devices with their start and end apart: 3 -> 11, of which waited for: 3 -> 4; matrix products, arithmetic and copies ran while one was open for 0% -> 1% of each run, Pallas kernels for 3% -> 7%
where the time goes in v3:
time: 125 us
  blocking collectives  31.4 us (25%)
  waiting for transfers between devices  30.7 us (25%)
  starting transfers between devices  25.8 us (21%)
  Pallas kernels  21 us (17%)
  local copies, waits for them, and re-layouts  12.4 us (10%)
  between operations  2.16 us (2%)
    all_to_all x2, waiting for transfers between devices, exchange(): return lax.all_to_all(rows, 'tp', split_axis=0, concat_axis=0, tiled=True)  24.5 us
    all_to_all x1, blocking collectives, exchange(): return lax.all_to_all(rows, 'tp', split_axis=0, concat_axis=0, tiled=True)  19.2 us
    ppermute x9, starting transfers between devices, from_side(): return lax.ppermute(rows, 'tp', route)  14.8 us
    all_to_all x1, blocking collectives, forward_product(): lax.all_to_all(rows, 'tp', split_axis=0, concat_axis=0, tiled=True, axis_...  12.2 us
    all_to_all x2, starting transfers between devices, exchange(): return lax.all_to_all(rows, 'tp', split_axis=0, concat_axis=0, tiled=True)  11 us
    unnamed x28, local copies, waits for them, and re-layouts  10.4 us
    pallas_call x2, Pallas kernels, block_product(): pl.pallas_call(functools.partial(product_kernel, tiles, counts, places),...  6.39 us
    ppermute x9, waiting for transfers between devices, from_side(): return lax.ppermute(rows, 'tp', route)  6.23 us
  transfers between devices with their start and end apart: 11, of which 4 were waited for; matrix products, arithmetic and copies ran while one was open for 1% of the time, Pallas kernels for 7%

profile of v3, /device:TPU:0, one launch (start us, length us, event | category | flops | bytes accessed | tf_op | source)
XLA Modules:
  0.0 124.5 jit_solution(15706240697469309090)
XLA Ops:
  3.6 12.2 %all_to_all.20.refs_0_ = bf16[4,16,2304]{2,1,0:T(8,128)(2,1)S(1)} all-to-all(bf16[4,16,2304]{2,1,0:T(8,128)(2,1)S(1)} %norm_rows.1), channel_id=1, replica_groups={{0,8,16,24},{1,9,17,25},{2,10,18,26},{3,11,19,27},{4,12,20,28},{5,13,21..., dimensions={0} | all-to-all | bytes 589824 | tf_op jit(solution)/shard_map/all_to_all | solution.py:522
  15.8 1.6 %collective-permute-start.4 = (bf16[4,16,2304]{2,1,0:T(8,128)(2,1)S(1)}, bf16[4,16,2304]{2,1,0:T(8,128)(2,1)S(1)}, u32[]{:S(2)}, u32[]{:S(2)}) collective-permute-start(bf16[4,16,2304]{2,1,0:T(8,128)(2,1)S(1)} %all_to_all.20.refs_0_), channel_id=1, source_target_pairs={{4,0},{5,1},{6,2},{7,3},{0,4},{1,5},{2,6},{3,7},{12,8},{13,9},{14,... | collective-permute-start | bytes 884744 | tf_op jit(solution)/shard_map/ppermute | solution.py:518
  17.4 1.5 %collective-permute-start = (bf16[4,16,2304]{2,1,0:T(8,128)(2,1)S(1)}, bf16[4,16,2304]{2,1,0:T(8,128)(2,1)S(1)}, u32[]{:S(2)}, u32[]{:S(2)}) collective-permute-start(bf16[4,16,2304]{2,1,0:T(8,128)(2,1)S(1)} %all_to_all.20.refs_0_), channel_id=1, source_target_pairs={{3,0},{0,1},{1,2},{2,3},{7,4},{4,5},{5,6},{6,7},{11,8},{8,9},{9,10... | collective-permute-start | bytes 884744 | tf_op jit(solution)/shard_map/ppermute | solution.py:518
  18.9 1.7 %collective-permute-start.2 = (bf16[4,16,2304]{2,1,0:T(8,128)(2,1)S(1)}, bf16[4,16,2304]{2,1,0:T(8,128)(2,1)S(1)}, u32[]{:S(2)}, u32[]{:S(2)}) collective-permute-start(bf16[4,16,2304]{2,1,0:T(8,128)(2,1)S(1)} %all_to_all.20.refs_0_), channel_id=1, source_target_pairs={{1,0},{2,1},{3,2},{0,3},{5,4},{6,5},{7,6},{4,7},{9,8},{10,9},{11,1... | collective-permute-start | bytes 884744 | tf_op jit(solution)/shard_map/ppermute | solution.py:518
  20.6 2.4 %collective-permute-done.4.refs_3_ = bf16[4,16,2304]{2,1,0:T(8,128)(2,1)S(1)} collective-permute-done((bf16[4,16,2304]{2,1,0:T(8,128)(2,1)S(1)}, bf16[4,16,2304]{2,1,0:T(8,128)(2,1)S(1)}, u32[]{:S(2)}, u32[]{:S(2)}) %collective-permute-start.4) | collective-permute-done | bytes 294944 | tf_op jit(solution)/shard_map/ppermute | solution.py:518
  23.1 1.5 %collective-permute-start.5 = (bf16[4,16,2304]{2,1,0:T(8,128)(2,1)S(1)}, bf16[4,16,2304]{2,1,0:T(8,128)(2,1)S(1)}, u32[]{:S(2)}, u32[]{:S(2)}) collective-permute-start(bf16[4,16,2304]{2,1,0:T(8,128)(2,1)S(1)} %collective-permute-done.4.refs_3_), channel_id=1, source_target_pairs={{3,0},{0,1},{1,2},{2,3},{7,4},{4,5},{5,6},{6,7},{11,8},{8,9},{9,10... | collective-permute-start | bytes 884744 | tf_op jit(solution)/shard_map/ppermute | solution.py:518
  24.6 1.7 %collective-permute-start.7 = (bf16[4,16,2304]{2,1,0:T(8,128)(2,1)S(1)}, bf16[4,16,2304]{2,1,0:T(8,128)(2,1)S(1)}, u32[]{:S(2)}, u32[]{:S(2)}) collective-permute-start(bf16[4,16,2304]{2,1,0:T(8,128)(2,1)S(1)} %collective-permute-done.4.refs_3_), channel_id=1, source_target_pairs={{1,0},{2,1},{3,2},{0,3},{5,4},{6,5},{7,6},{4,7},{9,8},{10,9},{11,1... | collective-permute-start | bytes 884744 | tf_op jit(solution)/shard_map/ppermute | solution.py:518
  27.2 3.0 %collective-permute-start.3 = (bf16[2,16,2304]{2,1,0:T(8,128)(2,1)S(1)}, bf16[2,16,2304]{2,1,0:T(8,128)(2,1)S(1)}, u32[]{:S(2)}, u32[]{:S(2)}) collective-permute-start(bf16[2,16,2304]{2,1,0:T(8,128)(2,1)S(1)} %slice.25), channel_id=1, source_target_pairs={{1,0},{2,1},{3,2},{0,3},{5,4},{6,5},{7,6},{4,7},{9,8},{10,9},{11,1... | collective-permute-start | bytes 442376 | tf_op jit(solution)/shard_map/ppermute | solution.py:518
  30.2 3.3 %collective-permute-done.5.refs_5_ = bf16[4,16,2304]{2,1,0:T(8,128)(2,1)S(1)} collective-permute-done((bf16[4,16,2304]{2,1,0:T(8,128)(2,1)S(1)}, bf16[4,16,2304]{2,1,0:T(8,128)(2,1)S(1)}, u32[]{:S(2)}, u32[]{:S(2)}) %collective-permute-start.5) | collective-permute-done | bytes 294944 | tf_op jit(solution)/shard_map/ppermute | solution.py:518
  34.6 2.3 %collective-permute-start.8 = (bf16[2,16,2304]{2,1,0:T(8,128)(2,1)S(1)}, bf16[2,16,2304]{2,1,0:T(8,128)(2,1)S(1)}, u32[]{:S(2)}, u32[]{:S(2)}) collective-permute-start(bf16[2,16,2304]{2,1,0:T(8,128)(2,1)S(1)} %slice.27), channel_id=1, source_target_pairs={{1,0},{2,1},{3,2},{0,3},{5,4},{6,5},{7,6},{4,7},{9,8},{10,9},{11,1... | collective-permute-start | bytes 442376 | tf_op jit(solution)/shard_map/ppermute | solution.py:518
  36.9 2.5 %copy-done = bf16[1,2048,1280]{2,1,0:T(8,128)(2,1)S(1)} copy-done((bf16[1,2048,1280]{2,1,0:T(8,128)(2,1)S(1)}, bf16[1,2048,1280]{2,1,0:T(8,128)(2,1)}, u32[]{:S(2)}) %copy-start) | copy-done | bytes 5242904
  39.4 4.0 %block_product.2.refs_4_ = bf16[24,16,2304]{2,1,0:T(8,128)(2,1)S(1)} custom-call(bf16[4,16,2304]{2,1,0:T(8,128)(2,1)S(1)} %all_to_all.20.refs_0_, bf16[4,16,2304]{2,1,0:T(8,128)(2,1)S(1)} %collective-permute-done.2.refs_1_, bf16[4,16,2304]{2,1,0:T(8,128)(2,1)S(1)} %collective-permute-done.refs_2_, bf16[4,16,2304]{2,1,0:T(8,128)(2,1)S(1)} %collective-permute-done.4.refs_3_, ...), custom_call_target="tpu_custom_call" | custom-call | flops 2264924160 | bytes 12000000 | tf_op jit(solution)/shard_map/block_product/pallas_call | solution.py:199
  43.4 2.4 %block_product.3 = bf16[32,16,2304]{2,1,0:T(8,128)(2,1)S(1)} custom-call(bf16[2,16,2304]{2,1,0:T(8,128)(2,1)S(1)} %collective-permute-done.1.refs_0_, bf16[2,16,2304]{2,1,0:T(8,128)(2,1)S(1)} %collective-permute-done.3.refs_1_, bf16[2,16,2304]{2,1,0:T(8,128)(2,1)S(1)} %collective-permute-done.6.refs_2_, ...), custom_call_target="tpu_custom_call" | custom-call | flops 754974720 | bytes 12000000 | tf_op jit(solution)/shard_map/block_product/pallas_call | solution.py:199
  45.8 1.4 %copy-done.3 = bf16[32,16,2304]{2,1,0:T(8,128)(2,1)} copy-done((bf16[32,16,2304]{2,1,0:T(8,128)(2,1)}, bf16[32,16,2304]{2,1,0:T(8,128)(2,1)S(1)}, u32[]{:S(2)}) %copy-start.3) | copy-done | bytes 2359320
  47.3 4.6 %all-to-all-start.1 = ((bf16[32,16,2304]{2,1,0:T(8,128)(2,1)}), bf16[32,16,2304]{2,1,0:T(8,128)(2,1)S(1)}, u32[]{:S(2)}, u32[]{:S(2)}) async-start(bf16[32,16,2304]{2,1,0:T(8,128)(2,1)} %copy-done.3), calls=%async_computation.1 | async-start | bytes 4718592 | tf_op jit(solution)/shard_map/all_to_all | solution.py:507
  53.5 24.5 %all-to-all-done.1.parts_ref = bf16[32,16,2304]{2,1,0:T(8,128)(2,1)S(1)} async-done(((bf16[32,16,2304]{2,1,0:T(8,128)(2,1)}), bf16[32,16,2304]{2,1,0:T(8,128)(2,1)S(1)}, u32[]{:S(2)}, u32[]{:S(2)}) %all-to-all-start.1) | async-done | bytes 2359328 | tf_op jit(solution)/shard_map/all_to_all | solution.py:507
  77.9 3.0 %attend_main.1 = (bf16[32,16,256]{2,1,0:T(8,128)(2,1)S(1)}, f32[8,2048]{1,0:T(8,128)S(1)}) custom-call(s32[1]{0:T(128)} %copy.12.len_ref, bf16[32,16,2304]{2,1,0:T(8,128)(2,1)S(1)} %all-to-all-done.1.parts_ref, f32[1,10240]{1,0:T(1,128)S(1)} %bitcast.15, f32[8,128]{1,0:T(8,128)S(1)} %get-tuple-element.22.cos_ref, f32[8,128]{1,0:T(8,128)S(1)} %get-tuple-element.23.sin_ref, ...), custom_call_target="tpu_custom_call" | custom-call | flops 200000000 | bytes 6000000 | tf_op jit(solution)/shard_map/attend_main/pallas_call | solution.py:319
  81.6 6.3 %all-to-all-start.2 = ((bf16[32,16,256]{2,1,0:T(8,128)(2,1)}), bf16[32,16,256]{2,1,0:T(8,128)(2,1)}, u32[]{:S(2)}, u32[]{:S(2)}) async-start(bf16[32,16,256]{2,1,0:T(8,128)(2,1)} %copy-done.7), calls=%async_computation.2 | async-start | bytes 524288 | tf_op jit(solution)/shard_map/all_to_all | solution.py:507
  89.5 2.2 %copy-done.2 = bf16[1,2048,1024]{2,1,0:T(8,128)(2,1)S(1)} copy-done((bf16[1,2048,1024]{2,1,0:T(8,128)(2,1)S(1)}, bf16[1,2048,1024]{2,1,0:T(8,128)(2,1)}, u32[]{:S(2)}) %copy-start.2) | copy-done | bytes 4194328
  91.7 1.5 %readout.1.read_ref = f32[1,2048]{1,0:T(1,128)S(1)} custom-call(f32[8,1024]{1,0:T(8,128)S(1)} %reshape.34.head_ref, bf16[1,2048,1024]{2,1,0:T(8,128)(2,1)S(1)} %copy-done.2), custom_call_target="tpu_custom_call" | custom-call | flops 200000000 | bytes 5000000 | tf_op jit(solution)/shard_map/readout/pallas_call | solution.py:392
  93.8 3.0 %attend_cont.1.mixed_ref = bf16[16,8192]{1,0:T(8,128)(2,1)S(1)} custom-call(s32[1]{0:T(128)} %copy.12.len_ref, s32[1]{0:T(128)S(6)} %copy.13.bound_ref, bf16[32,16,2304]{2,1,0:T(8,128)(2,1)S(1)} %all-to-all-done.1.parts_ref, f32[1,10240]{1,0:T(1,128)S(1)} %bitcast.16, f32[16,128]{1,0:T(8,128)S(1)} %get-tuple-element.24.cos_ref, ...), custom_call_target="tpu_custom_call" | custom-call | flops 400000000 | bytes 8000000 | tf_op jit(solution)/shard_map/attend_cont/pallas_call | solution.py:364
  97.5 4.4 %out_product.1 = f32[32,16,256]{2,1,0:T(8,128)} custom-call(bf16[32,16,256]{2,1,0:T(8,128)(2,1)} %all-to-all-done.2.x_ref, f32[1,2048]{1,0:T(1,128)} %copy-done.10, bf16[1,2048,1024]{2,1,0:T(8,128)(2,1)} %w_hbm.3), custom_call_target="tpu_custom_call" | custom-call | flops 300000000 | bytes 5000000 | tf_op jit(solution)/shard_map/out_product/pallas_call | solution.py:438
  101.9 19.2 %all_to_all.21.parts_ref = f32[32,16,256]{2,1,0:T(8,128)} all-to-all(f32[32,16,256]{2,1,0:T(8,128)} %out_product.1), channel_id=1, replica_groups=mesh['grp'=4,'tp'=32] {'tp'}, dimensions={0} | all-to-all | bytes 1048576 | tf_op jit(solution)/shard_map/all_to_all | solution.py:507
  121.1 2.2 %finish.1 = (bf16[2,8192]{1,0:T(2,128)(2,1)}, f32[8,128]{1,0:T(8,128)}) custom-call(f32[32,16,256]{2,1,0:T(8,128)} %all_to_all.21.parts_ref, bf16[2,8192]{1,0:T(2,128)(2,1)} %bitcast.17, bf16[8,2,8192]{2,1,0:T(2,128)(2,1)} %bitcast.13, f32[1,8192]{1,0:T(1,128)} %bitcast.20, bf16[16,8192]{1,0:T(8,128)(2,1)} %copy-done.5), custom_call_target="tpu_custom_call" | custom-call | flops 1000000 | bytes 2000000 | tf_op jit(solution)/shard_map/finish/pallas_call | solution.py:482
  (50 shorter events, 9.8 us)
Async XLA Ops:
  0.6 1.0 copy-start.6
  1.6 0.8 copy-start.9
  2.3 0.8 copy-start.11
  15.8 7.3 %collective-permute-start.4 = (bf16[4,16,2304]{2,1,0:T(8,128)(2,1)S(1)}, bf16[4,16,2304]{2,1,0:T(8,128)(2,1)S(1)}, u32[]{:S(2)}, u32[]{:S(2)}) collective-permute-start(bf16[4,16,2304]{2,1,0:T(8,128)(2,1)S(1)} %all_to_all.20.refs_0_), channel_id=1, source_target_pairs={{4,0},{5,1},{6,2},{7,3},{0,4},{1,5},{2,6},{3,7},{12,8},{13,9},{14,... | collective-permute-start | bytes 884744 | tf_op jit(solution)/shard_map/ppermute | solution.py:518
  17.4 9.4 %collective-permute-start = (bf16[4,16,2304]{2,1,0:T(8,128)(2,1)S(1)}, bf16[4,16,2304]{2,1,0:T(8,128)(2,1)S(1)}, u32[]{:S(2)}, u32[]{:S(2)}) collective-permute-start(bf16[4,16,2304]{2,1,0:T(8,128)(2,1)S(1)} %all_to_all.20.refs_0_), channel_id=1, source_target_pairs={{3,0},{0,1},{1,2},{2,3},{7,4},{4,5},{5,6},{6,7},{11,8},{8,9},{9,10... | collective-permute-start | bytes 884744 | tf_op jit(solution)/shard_map/ppermute | solution.py:518
  18.9 8.3 %collective-permute-start.2 = (bf16[4,16,2304]{2,1,0:T(8,128)(2,1)S(1)}, bf16[4,16,2304]{2,1,0:T(8,128)(2,1)S(1)}, u32[]{:S(2)}, u32[]{:S(2)}) collective-permute-start(bf16[4,16,2304]{2,1,0:T(8,128)(2,1)S(1)} %all_to_all.20.refs_0_), channel_id=1, source_target_pairs={{1,0},{2,1},{3,2},{0,3},{5,4},{6,5},{7,6},{4,7},{9,8},{10,9},{11,1... | collective-permute-start | bytes 884744 | tf_op jit(solution)/shard_map/ppermute | solution.py:518
  23.1 10.4 %collective-permute-start.5 = (bf16[4,16,2304]{2,1,0:T(8,128)(2,1)S(1)}, bf16[4,16,2304]{2,1,0:T(8,128)(2,1)S(1)}, u32[]{:S(2)}, u32[]{:S(2)}) collective-permute-start(bf16[4,16,2304]{2,1,0:T(8,128)(2,1)S(1)} %collective-permute-done.4.refs_3_), channel_id=1, source_target_pairs={{3,0},{0,1},{1,2},{2,3},{7,4},{4,5},{5,6},{6,7},{11,8},{8,9},{9,10... | collective-permute-start | bytes 884744 | tf_op jit(solution)/shard_map/ppermute | solution.py:518
  24.6 10.0 %collective-permute-start.7 = (bf16[4,16,2304]{2,1,0:T(8,128)(2,1)S(1)}, bf16[4,16,2304]{2,1,0:T(8,128)(2,1)S(1)}, u32[]{:S(2)}, u32[]{:S(2)}) collective-permute-start(bf16[4,16,2304]{2,1,0:T(8,128)(2,1)S(1)} %collective-permute-done.4.refs_3_), channel_id=1, source_target_pairs={{1,0},{2,1},{3,2},{0,3},{5,4},{6,5},{7,6},{4,7},{9,8},{10,9},{11,1... | collective-permute-start | bytes 884744 | tf_op jit(solution)/shard_map/ppermute | solution.py:518
  26.8 16.5 %collective-permute-start.1 = (bf16[2,16,2304]{2,1,0:T(8,128)(2,1)S(1)}, bf16[2,16,2304]{2,1,0:T(8,128)(2,1)S(1)}, u32[]{:S(2)}, u32[]{:S(2)}) collective-permute-start(bf16[2,16,2304]{2,1,0:T(8,128)(2,1)S(1)} %slice.24), channel_id=1, source_target_pairs={{3,0},{0,1},{1,2},{2,3},{7,4},{4,5},{5,6},{6,7},{11,8},{8,9},{9,10... | collective-permute-start | bytes 442376 | tf_op jit(solution)/shard_map/ppermute | solution.py:518
  27.2 16.2 %collective-permute-start.3 = (bf16[2,16,2304]{2,1,0:T(8,128)(2,1)S(1)}, bf16[2,16,2304]{2,1,0:T(8,128)(2,1)S(1)}, u32[]{:S(2)}, u32[]{:S(2)}) collective-permute-start(bf16[2,16,2304]{2,1,0:T(8,128)(2,1)S(1)} %slice.25), channel_id=1, source_target_pairs={{1,0},{2,1},{3,2},{0,3},{5,4},{6,5},{7,6},{4,7},{9,8},{10,9},{11,1... | collective-permute-start | bytes 442376 | tf_op jit(solution)/shard_map/ppermute | solution.py:518
  33.5 9.9 %collective-permute-start.6 = (bf16[2,16,2304]{2,1,0:T(8,128)(2,1)S(1)}, bf16[2,16,2304]{2,1,0:T(8,128)(2,1)S(1)}, u32[]{:S(2)}, u32[]{:S(2)}) collective-permute-start(bf16[2,16,2304]{2,1,0:T(8,128)(2,1)S(1)} %slice.26), channel_id=1, source_target_pairs={{3,0},{0,1},{1,2},{2,3},{7,4},{4,5},{5,6},{6,7},{11,8},{8,9},{9,10... | collective-permute-start | bytes 442376 | tf_op jit(solution)/shard_map/ppermute | solution.py:518
  34.6 8.8 %collective-permute-start.8 = (bf16[2,16,2304]{2,1,0:T(8,128)(2,1)S(1)}, bf16[2,16,2304]{2,1,0:T(8,128)(2,1)S(1)}, u32[]{:S(2)}, u32[]{:S(2)}) collective-permute-start(bf16[2,16,2304]{2,1,0:T(8,128)(2,1)S(1)} %slice.27), channel_id=1, source_target_pairs={{1,0},{2,1},{3,2},{0,3},{5,4},{6,5},{7,6},{4,7},{9,8},{10,9},{11,1... | collective-permute-start | bytes 442376 | tf_op jit(solution)/shard_map/ppermute | solution.py:518
  36.9 2.5 %copy-start = (bf16[1,2048,1280]{2,1,0:T(8,128)(2,1)S(1)}, bf16[1,2048,1280]{2,1,0:T(8,128)(2,1)}, u32[]{:S(2)}) copy-start(bf16[1,2048,1280]{2,1,0:T(8,128)(2,1)} %refs_5_.1) | copy-start | bytes 15728644
  39.4 4.0 %copy-start.1 = (bf16[1,2048,1280]{2,1,0:T(8,128)(2,1)S(1)}, bf16[1,2048,1280]{2,1,0:T(8,128)(2,1)}, u32[]{:S(2)}) copy-start(bf16[1,2048,1280]{2,1,0:T(8,128)(2,1)} %refs_5_.1) | copy-start | bytes 15728644
  45.8 1.4 %copy-start.3 = (bf16[32,16,2304]{2,1,0:T(8,128)(2,1)}, bf16[32,16,2304]{2,1,0:T(8,128)(2,1)S(1)}, u32[]{:S(2)}) copy-start(bf16[32,16,2304]{2,1,0:T(8,128)(2,1)S(1)} %block_product.3) | copy-start | bytes 7077892
  47.3 30.7 %copy-start.4 = (bf16[1,256,2048]{2,1,0:T(8,128)(2,1)S(1)}, bf16[1,256,2048]{2,1,0:T(8,128)(2,1)}, u32[]{:S(2)}) copy-start(bf16[1,256,2048]{2,1,0:T(8,128)(2,1)} %param.12) | copy-start | bytes 3145732
  47.3 30.7 %copy-start.8 = (f32[10240]{0:T(1024)S(1)}, f32[10240]{0:T(1024)}, u32[]{:S(2)}) copy-start(f32[10240]{0:T(1024)} %param.16) | copy-start | bytes 122884
  47.3 30.7 %all-to-all-start.1 = ((bf16[32,16,2304]{2,1,0:T(8,128)(2,1)}), bf16[32,16,2304]{2,1,0:T(8,128)(2,1)S(1)}, u32[]{:S(2)}, u32[]{:S(2)}) async-start(bf16[32,16,2304]{2,1,0:T(8,128)(2,1)} %copy-done.3), calls=%async_computation.1 | async-start | bytes 4718592 | tf_op jit(solution)/shard_map/all_to_all | solution.py:507
  80.9 0.7 copy-start.7
  81.6 15.9 %all-to-all-start.2 = ((bf16[32,16,256]{2,1,0:T(8,128)(2,1)}), bf16[32,16,256]{2,1,0:T(8,128)(2,1)}, u32[]{:S(2)}, u32[]{:S(2)}) async-start(bf16[32,16,256]{2,1,0:T(8,128)(2,1)} %copy-done.7), calls=%async_computation.2 | async-start | bytes 524288 | tf_op jit(solution)/shard_map/all_to_all | solution.py:507
  89.5 2.2 %copy-start.2 = (bf16[1,2048,1024]{2,1,0:T(8,128)(2,1)S(1)}, bf16[1,2048,1024]{2,1,0:T(8,128)(2,1)}, u32[]{:S(2)}) copy-start(bf16[1,2048,1024]{2,1,0:T(8,128)(2,1)} %w_hbm.3) | copy-start | bytes 12582916
  91.7 1.6 %copy-start.12 = (f32[16,64]{1,0:T(8,128)S(1)}, f32[16,64]{1,0:T(8,128)}, u32[]{:S(2)}) copy-start(f32[16,64]{1,0:T(8,128)} %get-tuple-element.17) | copy-start | bytes 12292
  91.7 1.6 %copy-start.13 = (f32[16,64]{1,0:T(8,128)S(1)}, f32[16,64]{1,0:T(8,128)}, u32[]{:S(2)}) copy-start(f32[16,64]{1,0:T(8,128)} %get-tuple-element.18) | copy-start | bytes 12292
  96.8 0.7 copy-start.5
  (1 other events, 0.6 us)

commit v4 on v3

--- a/solution.py
+++ b/solution.py
@@ -25,9 +25,7 @@
 EPS = 1e-06
 MASKED_SCORE = -1e30
 
-VMEM_LIMIT = 48 * 1024 * 1024
-VMEM_MOST = 60 * 1024 * 1024
-VMEM_LESS = 32 * 1024 * 1024
+VMEM_LIMIT = 32 * 1024 * 1024
 VMEM = pl.BlockSpec(memory_space=pltpu.VMEM)
 SMEM = pl.BlockSpec(memory_space=pltpu.SMEM)
 HBM = pl.BlockSpec(memory_space=pltpu.HBM)
@@ -41,8 +39,12 @@
     return pl.CostEstimate(flops=flops, bytes_accessed=moved, transcendentals=0)
 
 
-def kernel_params(limit=VMEM_LIMIT):
-    return pltpu.CompilerParams(vmem_limit_bytes=limit)
+def in_hbm(array):
+    return pltpu.with_memory_space_constraint(array, pltpu.HBM)
+
+
+def kernel_params():
+    return pltpu.CompilerParams(vmem_limit_bytes=VMEM_LIMIT)
 
 
 def norm_kernel(main_hbm, cont_hbm, gain_hbm, out_ref, main_ref, cont_ref, gain_ref, rows_ref, piece_ref, sems):
@@ -89,7 +91,7 @@
         compiler_params=kernel_params(),
         cost_estimate=cost(10**6, 4 * 10**6),
         name="norm_rows",
-    )(main, cont, gain)
+    )(in_hbm(main), in_hbm(cont), in_hbm(gain))
 
 
 def weight_tile(n, tiles, w_hbm, w_ref, sems):
@@ -112,13 +114,15 @@
     return jnp.where(block == 6, 2, 0)
 
 
-def product_kernel(tiles, counts, places, *refs):
+def plane_place():
+    column = lax.rem(lax.axis_index("tp"), COL_BLOCKS)
+    return column // 4, lax.rem(column, 4)
+
+
+def product_kernel(tiles, counts, *refs):
     x_refs = refs[: len(counts)]
-    refs = refs[len(counts) :]
-    if places:
-        earlier_ref, w_hbm, out_ref, rows_ref, wide_ref, w_ref, sems, part_ref = refs
-    else:
-        w_hbm, part_ref, rows_ref, wide_ref, w_ref, sems = refs
+    w_hbm, *out_refs = refs[len(counts) : len(counts) + 1 + ROW_BLOCKS]
+    rows_ref, wide_ref, w_ref, sems, part_ref = refs[len(counts) + 1 + ROW_BLOCKS :]
     n = pl.program_id(0)
     members = sum(counts)
     count = members * CTOK
@@ -164,49 +168,104 @@
         for k in range(halves):
             lane = width + REST + k * 128
             part_ref[:, :, lane : lane + 128] = wide_ref[k].astype(jnp.bfloat16).reshape(members, CTOK, 128)
-        if places:
-            me = lax.rem(lax.axis_index("tp"), COL_BLOCKS)
-            y, x = me // 4, lax.rem(me, 4)
-            done = earlier_ref.shape[0] // ROW_BLOCKS
-            for i, (dy, dx) in enumerate(places):
-                column = lax.rem(y + dy, 2) * 4 + lax.rem(x + dx, 4)
-                for z in range(ROW_BLOCKS):
-                    if i < done:
-                        message = earlier_ref[i * ROW_BLOCKS + z]
-                    else:
-                        message = part_ref[(i - done) * ROW_BLOCKS + z]
-                    out_ref[z * COL_BLOCKS + column] = message
-
-
-def block_product(messages, blocks, earlier=None, places=()):
+        z = lax.axis_index("tp") // COL_BLOCKS
+        for k, out_ref in enumerate(out_refs):
+            to = lax.rem(z + k, ROW_BLOCKS)
+            for g in range(members // ROW_BLOCKS):
+                out_ref[g] = part_ref[g * ROW_BLOCKS + to]
+
+
+def block_product(messages, blocks):
     tiles = blocks.shape[2] // TILE
     lanes = (tiles + 1) * TILE + REST
     counts = tuple(rows.shape[0] for rows in messages)
     members = sum(counts)
-    part = (members, CTOK, lanes)
-    scratch = [
-        pltpu.VMEM((members * (CTOK + STEPS), FEATURES), jnp.bfloat16),
-        pltpu.VMEM((TILE // 128, members * CTOK, 128), jnp.float32),
-        pltpu.VMEM((tiles, FEATURES, TILE), jnp.bfloat16),
-        pltpu.SemaphoreType.DMA((tiles,)),
-    ]
-    operands = list(messages)
-    out = part
-    if places:
-        operands.append(earlier)
-        out = (MEMBERS, CTOK, lanes)
-        scratch.append(pltpu.VMEM(part, jnp.bfloat16))
-    return pl.pallas_call(
-        functools.partial(product_kernel, tiles, counts, places),
-        out_shape=jax.ShapeDtypeStruct(out, jnp.bfloat16),
+    return pl.pallas_call(
+        functools.partial(product_kernel, tiles, counts),
+        out_shape=[jax.ShapeDtypeStruct((members // ROW_BLOCKS, CTOK, lanes), jnp.bfloat16)] * ROW_BLOCKS,
         grid=(tiles,),
-        in_specs=[VMEM] * len(operands) + [HBM],
-        out_specs=whole(out) if places else VMEM,
-        scratch_shapes=scratch,
-        compiler_params=kernel_params(VMEM_LESS),
+        in_specs=[VMEM] * len(counts) + [HBM],
+        out_specs=[VMEM] * ROW_BLOCKS,
+        scratch_shapes=[
+            pltpu.VMEM((members * (CTOK + STEPS), FEATURES), jnp.bfloat16),
+            pltpu.VMEM((TILE // 128, members * CTOK, 128), jnp.float32),
+            pltpu.VMEM((tiles, FEATURES, TILE), jnp.bfloat16),
+            pltpu.SemaphoreType.DMA((tiles,)),
+            pltpu.VMEM((members, CTOK, lanes), jnp.bfloat16),
+        ],
+        compiler_params=kernel_params(),
         cost_estimate=cost(2 * members * (CTOK + STEPS) * FEATURES * tiles * TILE, 12 * 10**6),
         name="block_product",
-    )(*operands, blocks)
+    )(*messages, in_hbm(blocks))
+
+
+def sum_kernel(bias_ref, *refs):
+    part_refs, out_refs = refs[:ROW_BLOCKS], refs[ROW_BLOCKS:]
+    column = lax.rem(lax.axis_index("tp"), COL_BLOCKS)
+    late = column == 6
+    last = (column == COL_BLOCKS - 1).astype(jnp.float32)
+    cols = QKV // COL_BLOCKS
+    tiles = cols // TILE
+    kept = REST // TILE
+    zero = jnp.zeros((CTOK, TILE), jnp.float32)
+
+    def value_bias(j):
+        if j == 0:
+            return jnp.zeros((1, TILE), jnp.float32)
+        at = QKV - cols + j * TILE
+        return bias_ref[:, at : at + TILE] * last
+
+    main_bias = jnp.concatenate([value_bias(j) for j in range(tiles)], axis=0)
+    for g, out_ref in enumerate(out_refs):
+
+        def total(lane):
+            value = part_refs[0][g, :, lane : lane + TILE].astype(jnp.float32)
+            for ref in part_refs[1:]:
+                value = value + ref[g, :, lane : lane + TILE].astype(jnp.float32)
+            return value
+
+        rest = [total(cols + i * TILE) for i in range(kept)] + [zero] * (tiles - kept)
+        lows = []
+        for j in range(tiles):
+            shifted = rest[j - tiles + kept] if j >= tiles - kept else zero
+            value = total(j * TILE) + jnp.where(late, shifted, rest[j]) + value_bias(j)
+            high = value.astype(jnp.bfloat16)
+            out_ref[:, j * TILE : (j + 1) * TILE] = high
+            lows.append(value - high.astype(jnp.float32))
+        for i in range(kept):
+            low = jnp.where(late, lows[i + tiles - kept], lows[i])
+            out_ref[:, cols + i * TILE : cols + (i + 1) * TILE] = low.astype(jnp.bfloat16)
+        main = total(cols + REST)
+        pad = jnp.zeros((tiles - kept, TILE), jnp.float32)
+        pieces = []
+        for s in range(STEPS):
+            low = main[s * 8 + tiles : (s + 1) * 8]
+            both = jnp.where(late, jnp.concatenate([pad, low], axis=0), jnp.concatenate([low, pad], axis=0))
+            value = main[s * 8 : s * 8 + tiles] + both + main_bias
+            high = value.astype(jnp.bfloat16).astype(jnp.float32)
+            low = value - high
+            pieces += [high, jnp.where(late, low[tiles - kept :], low[:kept])]
+        out_ref[:, cols + REST :] = jnp.concatenate(pieces, axis=0).astype(jnp.bfloat16)
+
+
+def sum_parts(bias, parts):
+    groups, rows, lanes = parts[0].shape
+    return pl.pallas_call(
+        sum_kernel,
+        out_shape=[jax.ShapeDtypeStruct((rows, lanes), jnp.bfloat16)] * groups,
+        in_specs=[VMEM] * (1 + len(parts)),
+        out_specs=[VMEM] * groups,
+        compiler_params=kernel_params(),
+        cost_estimate=cost(10**6, 3 * 10**6),
+        name="sum_parts",
+    )(bias, *parts)
+
+
+def load_parts(part_refs, parts_ref):
+    y, x = plane_place()
+    for ref, (dy, dx) in zip(part_refs, HOMES):
+        column = lax.rem(y + dy, 2) * 4 + lax.rem(x + 4 - dx, 4)
+        parts_ref[column] = ref[...]
 
 
 def summed_block(parts_ref, c, lanes):
@@ -237,9 +296,9 @@
     for c in range(COL_BLOCKS):
         first = 2 if c == 6 else 0
         if main:
-            total = summed_block(parts_ref, c, slice(cols + REST, cols + REST + TILE))
+            total = parts_ref[c, :, cols + REST :].astype(jnp.float32)
         else:
-            total = summed_block(parts_ref, c, slice(0, cols + REST))
+            total = parts_ref[c, :, : cols + REST].astype(jnp.float32)
         for j in range(cols // TILE):
             lanes = slice(c * cols + j * TILE, c * cols + (j + 1) * TILE)
             rest = j - first
@@ -263,10 +322,10 @@
     sine = sin_ref[...]
 
     def plain(start):
-        return qkv_ref[:, start : start + HD] + bias_ref[:, start : start + HD]
+        return qkv_ref[:, start : start + HD]
 
     def rotated(start):
-        head = plain(start)
+        head = plain(start) + bias_ref[:, start : start + HD]
         return head * cosine + pltpu.roll(head, HD // 2, 1) * sine
 
     return plain, rotated
@@ -282,8 +341,11 @@
 KV_WIDTH = KVH * HD
 
 
-def attend_main_kernel(len_ref, parts_ref, bias_ref, cos_ref, sin_ref, cache_ref, out_ref, kv_ref, qkv_ref, piece_ref):
+def attend_main_kernel(len_ref, bias_ref, cos_ref, sin_ref, cache_ref, *refs):
+    part_refs = refs[:COL_BLOCKS]
+    out_ref, kv_ref, qkv_ref, piece_ref, parts_ref = refs[COL_BLOCKS:]
     rows = qkv_ref.shape[0]
+    load_parts(part_refs, parts_ref)
     qkv_ref[...] = jnp.zeros(qkv_ref.shape, jnp.float32)
     load_qkv(True, parts_ref, qkv_ref)
     plain, rotated = head_readers(qkv_ref, bias_ref, cos_ref, sin_ref)
@@ -315,28 +377,30 @@
             out_ref[r * COL_BLOCKS + c] = piece
 
 
-def attend_main(prefix_len, parts, bias, cosine, sine, cache):
+def attend_main(prefix_len, bias, cosine, sine, cache, parts):
     return pl.pallas_call(
         attend_main_kernel,
         out_shape=(
             jax.ShapeDtypeStruct((32, 16, TILE), jnp.bfloat16),
             jax.ShapeDtypeStruct((8, 2 * KV_WIDTH), jnp.float32),
         ),
-        in_specs=[SMEM] + [VMEM] * 5,
+        in_specs=[SMEM] + [VMEM] * (4 + COL_BLOCKS),
         out_specs=(whole((32, 16, TILE)), whole((8, 2 * KV_WIDTH))),
         scratch_shapes=[
             pltpu.VMEM((8, QKV), jnp.float32),
             pltpu.VMEM((ROW_BLOCKS, 16, TILE), jnp.float32),
+            pltpu.VMEM((COL_BLOCKS,) + parts[0].shape, jnp.bfloat16),
         ],
         compiler_params=kernel_params(),
         cost_estimate=cost(2 * 10**8, 6 * 10**6),
         name="attend_main",
-    )(prefix_len, parts, bias, cosine, sine, cache)
-
-
-def attend_cont_kernel(
-    len_ref, bound_ref, parts_ref, bias_ref, cos_ref, sin_ref, cache_ref, kv_ref, out_ref, qkv_ref
-):
+    )(prefix_len, bias, cosine, sine, cache, *parts)
+
+
+def attend_cont_kernel(len_ref, bound_ref, bias_ref, cos_ref, sin_ref, cache_ref, kv_ref, *refs):
+    part_refs = refs[:COL_BLOCKS]
+    out_ref, qkv_ref, parts_ref = refs[COL_BLOCKS:]
+    load_parts(part_refs, parts_ref)
     rows = qkv_ref.shape[0]
     load_qkv(False, parts_ref, qkv_ref)
     plain, rotated = head_readers(qkv_ref, bias_ref, cos_ref, sin_ref)
@@ -364,9 +428,12 @@
     return pl.pallas_call(
         attend_cont_kernel,
         out_shape=jax.ShapeDtypeStruct((CTOK, D), jnp.bfloat16),
-        in_specs=[SMEM, SMEM] + [VMEM] * 5 + [whole((8, 2 * KV_WIDTH))],
+        in_specs=[SMEM, SMEM] + [VMEM] * 4 + [whole((8, 2 * KV_WIDTH))] + [VMEM] * COL_BLOCKS,
         out_specs=whole((CTOK, D)),
-        scratch_shapes=[pltpu.VMEM((CTOK, QKV), jnp.float32)],
+        scratch_shapes=[
+            pltpu.VMEM((CTOK, QKV), jnp.float32),
+            pltpu.VMEM((COL_BLOCKS,) + args[-1].shape, jnp.bfloat16),
+        ],
         compiler_params=kernel_params(),
         cost_estimate=cost(4 * 10**8, 8 * 10**6),
         name="attend_cont",
@@ -398,7 +465,7 @@
         compiler_params=kernel_params(),
         cost_estimate=cost(2 * 10**8, 5 * 10**6),
         name="readout",
-    )(value_head, blocks)
+    )(value_head, in_hbm(blocks))
 
 
 def out_kernel(tiles, x_ref, read_ref, w_hbm, out_ref, rows_ref, wide_ref, read8_ref, w_ref, sems):
@@ -448,10 +515,10 @@
             pltpu.VMEM((tiles, FEATURES, TILE), jnp.bfloat16),
             pltpu.SemaphoreType.DMA((tiles,)),
         ],
-        compiler_params=kernel_params(VMEM_MOST),
+        compiler_params=kernel_params(),
         cost_estimate=cost(3 * 10**8, 5 * 10**6),
         name="out_product",
-    )(rows, read, blocks)
+    )(rows, read, in_hbm(blocks))
 
 
 def finish_kernel(parts_ref, main_ref, cont_ref, head_ref, mixed_ref, out_ref, score_ref, wide_ref):
@@ -488,7 +555,7 @@
         in_specs=[whole(parts.shape), whole(main.shape), whole(cont.shape), whole(head.shape), whole(mixed.shape)],
         out_specs=(whole((STEPS, D)), whole((8, 128))),
         scratch_shapes=[pltpu.VMEM((8, D), jnp.float32)],
-        compiler_params=kernel_params(VMEM_MOST),
+        compiler_params=kernel_params(),
         cost_estimate=cost(10**6, 2 * 10**6),
         name="finish",
     )(parts, main, cont, head, mixed)
@@ -518,19 +585,33 @@
     return lax.ppermute(rows, "tp", route)
 
 
-def forward_product(rows, blocks):
+def from_along(rows, dz):
+    route = [((to + dz * COL_BLOCKS) % MEMBERS, to) for to in range(MEMBERS)]
+    return lax.ppermute(rows, "tp", route)
+
+
+FIRST_HOMES = ((0, 0), (1, 0), (0, 1), (0, 3))
+SECOND_HOMES = ((1, 1), (1, 3), (0, 2), (1, 2))
+HOMES = FIRST_HOMES + SECOND_HOMES
+
+
+def project(rows, blocks, bias):
     near = lax.all_to_all(rows, "tp", split_axis=0, concat_axis=0, tiled=True, axis_index_groups=ALONG)
     half = ROW_BLOCKS // 2
     over = from_side(near, 1, 0)
-    here, far, places = [], [], []
-    for dy, mine in ((0, near), (1, over)):
+    sides, far = [], []
+    for mine in (near, over):
         after = from_side(mine, 0, 1)
         before = from_side(mine, 0, 3)
         far += [from_side(before[:half], 0, 3), from_side(after[half:], 0, 1)]
-        here += [mine, after, before]
-        places += [(dy, 0), (dy, 1), (dy, 3)]
-    earlier = block_product(here, blocks)
-    return block_product(far, blocks, earlier, tuple(places) + ((0, 2), (1, 2)))
+        sides.append([after, before])
+    received = []
+    for homes, messages in ((FIRST_HOMES, [near, over] + sides[0]), (SECOND_HOMES, sides[1] + far)):
+        parts = block_product(messages, blocks)
+        parts = [parts[0]] + [from_along(parts[k], -k) for k in range(1, ROW_BLOCKS)]
+        for (dy, dx), summed in zip(homes, sum_parts(bias, parts)):
+            received.append(from_side(summed, -dy, -dx) if dy or dx else summed)
+    return received
 
 
 def on_device(
@@ -545,10 +626,10 @@
     main_tables = rope_tables(prefix_len + step[:8])
     cont_tables = rope_tables(prefix_len + boundary + step)
     read = readout(value_head.reshape(COL_BLOCKS, D // COL_BLOCKS), w_out)
-    parts = exchange(forward_product(norm_rows(main, cont, rms_gain[None, :]), w_qkv))
-    mixed, main_kv = attend_main(prefix_len, parts, bias, *main_tables, cache)
+    parts = project(norm_rows(main, cont, rms_gain[None, :]), w_qkv, bias)
+    mixed, main_kv = attend_main(prefix_len, bias, *main_tables, cache, parts)
     mixed = exchange(mixed)
-    cont_mixed = attend_cont(prefix_len, boundary, parts, bias, *cont_tables, cache, main_kv)
+    cont_mixed = attend_cont(prefix_len, boundary, bias, *cont_tables, cache, main_kv, *parts)
     mixed, cont_mixed, read = lax.optimization_barrier((mixed, cont_mixed, read))
     parts = exchange(out_product(mixed, read, w_out))
     main_out, score = finish(parts, main, cont, head, cont_mixed)

time: 125 us -> 116 us (0.928)
  starting transfers between devices: 25.8 us -> 40.6 us
  local copies, waits for them, and re-layouts: 12.4 us -> 0.6 us
  waiting for transfers between devices: 30.7 us -> 20.6 us
  blocking collectives: 31.4 us -> 28.1 us
  Pallas kernels: 21 us -> 23.6 us
    all_to_all x2 -> x1, waiting for transfers between devices: 24.5 us -> 2.28 us  [exchange(): return lax.all_to_all(rows, 'tp', split_axis=0, concat_axis=0, tiled=True)]
    unnamed x28 -> x10, local copies, waits for them, and re-layouts: 10.4 us -> 0.03 us
    ppermute x9 -> x16, starting transfers between devices: 14.8 us -> 24.2 us  [from_side(): return lax.ppermute(rows, 'tp', route)]
    ppermute x0 -> x6, starting transfers between devices: none -> 9.01 us  [from_along(): return lax.ppermute(rows, 'tp', route)]
    ppermute x0 -> x6, waiting for transfers between devices: none -> 7.79 us  [from_along(): return lax.ppermute(rows, 'tp', route)]
    ppermute x9 -> x16, waiting for transfers between devices: 6.23 us -> 10.5 us  [from_side(): return lax.ppermute(rows, 'tp', route)]
    all_to_all x2 -> x1, starting transfers between devices: 11 us -> 7.3 us  [exchange(): return lax.all_to_all(rows, 'tp', split_axis=0, concat_axis=0, tiled=True)]
    all_to_all x1, blocking collectives: 19.2 us -> 15.9 us  [exchange(): return lax.all_to_all(rows, 'tp', split_axis=0, concat_axis=0, tiled=True)]
  transfers between devices with their start and end apart: 11 -> 23, of which waited for: 4 -> 8; matrix products, arithmetic and copies ran while one was open for 1% -> 0% of each run, Pallas kernels for 7% -> 13%
where the time goes in v4:
time: 116 us
  starting transfers between devices  40.6 us (35%)
  blocking collectives  28.1 us (24%)
  Pallas kernels  23.6 us (20%)
  waiting for transfers between devices  20.6 us (18%)
  between operations  2.17 us (2%)
    ppermute x16, starting transfers between devices, from_side(): return lax.ppermute(rows, 'tp', route)  24.2 us
    all_to_all x1, blocking collectives, exchange(): return lax.all_to_all(rows, 'tp', split_axis=0, concat_axis=0, tiled=True)  15.9 us
    all_to_all x1, blocking collectives, project(): lax.all_to_all(rows, 'tp', split_axis=0, concat_axis=0, tiled=True, axis_...  12.2 us
    ppermute x16, waiting for transfers between devices, from_side(): return lax.ppermute(rows, 'tp', route)  10.5 us
    ppermute x6, starting transfers between devices, from_along(): return lax.ppermute(rows, 'tp', route)  9.01 us
    pallas_call x2, Pallas kernels, block_product(): pl.pallas_call(functools.partial(product_kernel, tiles, counts), out_shap...  7.88 us
    ppermute x6, waiting for transfers between devices, from_along(): return lax.ppermute(rows, 'tp', route)  7.79 us
    all_to_all x1, starting transfers between devices, exchange(): return lax.all_to_all(rows, 'tp', split_axis=0, concat_axis=0, tiled=True)  7.3 us
  transfers between devices with their start and end apart: 23, of which 8 were waited for; matrix products, arithmetic and copies ran while one was open for 0% of the time, Pallas kernels for 13%

profile of v4, /device:TPU:0, one launch (start us, length us, event | category | flops | bytes accessed | tf_op | source)
XLA Modules:
  0.0 115.9 jit_solution(9114706595463573839)
XLA Ops:
  2.0 12.2 %all_to_all.15.refs_0_ = bf16[4,16,2304]{2,1,0:T(8,128)(2,1)S(1)} all-to-all(bf16[4,16,2304]{2,1,0:T(8,128)(2,1)S(1)} %norm_rows.1), channel_id=1, replica_groups={{0,8,16,24},{1,9,17,25},{2,10,18,26},{3,11,19,27},{4,12,20,28},{5,13,21..., dimensions={0} | all-to-all | bytes 589824 | tf_op jit(solution)/shard_map/all_to_all | solution.py:599
  15.8 2.8 %collective-permute-start.1 = (bf16[4,16,2304]{2,1,0:T(8,128)(2,1)S(1)}, bf16[4,16,2304]{2,1,0:T(8,128)(2,1)S(1)}, u32[]{:S(2)}, u32[]{:S(2)}) collective-permute-start(bf16[4,16,2304]{2,1,0:T(8,128)(2,1)S(1)} %all_to_all.15.refs_0_), channel_id=1, source_target_pairs={{1,0},{2,1},{3,2},{0,3},{5,4},{6,5},{7,6},{4,7},{9,8},{10,9},{11,1... | collective-permute-start | bytes 884744 | tf_op jit(solution)/shard_map/ppermute | solution.py:585
  18.6 2.9 %collective-permute-done.refs_1_ = bf16[4,16,2304]{2,1,0:T(8,128)(2,1)S(1)} collective-permute-done((bf16[4,16,2304]{2,1,0:T(8,128)(2,1)S(1)}, bf16[4,16,2304]{2,1,0:T(8,128)(2,1)S(1)}, u32[]{:S(2)}, u32[]{:S(2)}) %collective-permute-start) | collective-permute-done | bytes 294944 | tf_op jit(solution)/shard_map/ppermute | solution.py:585
  23.0 1.7 %collective-permute-start.9 = (bf16[4,16,2304]{2,1,0:T(8,128)(2,1)S(1)}, bf16[4,16,2304]{2,1,0:T(8,128)(2,1)S(1)}, u32[]{:S(2)}, u32[]{:S(2)}) collective-permute-start(bf16[4,16,2304]{2,1,0:T(8,128)(2,1)S(1)} %collective-permute-done.refs_1_), channel_id=1, source_target_pairs={{1,0},{2,1},{3,2},{0,3},{5,4},{6,5},{7,6},{4,7},{9,8},{10,9},{11,1... | collective-permute-start | bytes 884744 | tf_op jit(solution)/shard_map/ppermute | solution.py:585
  25.4 4.2 %collective-permute-done.2.refs_3_ = bf16[4,16,2304]{2,1,0:T(8,128)(2,1)S(1)} collective-permute-done((bf16[4,16,2304]{2,1,0:T(8,128)(2,1)S(1)}, bf16[4,16,2304]{2,1,0:T(8,128)(2,1)S(1)}, u32[]{:S(2)}, u32[]{:S(2)}) %collective-permute-start.2) | collective-permute-done | bytes 294944 | tf_op jit(solution)/shard_map/ppermute | solution.py:585
  29.7 3.9 %block_product.2 = (bf16[4,16,2304]{2,1,0:T(8,128)(2,1)S(1)}, bf16[4,16,2304]{2,1,0:T(8,128)(2,1)S(1)}, bf16[4,16,2304]{2,1,0:T(8,128)(2,1)S(1)}, bf16[4,16,2304]{2,1,0:T(8,128)(2,1)S(1)}) custom-call(bf16[4,16,2304]{2,1,0:T(8,128)(2,1)S(1)} %all_to_all.15.refs_0_, bf16[4,16,2304]{2,1,0:T(8,128)(2,1)S(1)} %collective-permute-done.refs_1_, ...), custom_call_target="tpu_custom_call" | custom-call | flops 1509949440 | bytes 12000000 | tf_op jit(solution)/shard_map/block_product/pallas_call | solution.py:183
  34.4 3.3 %collective-permute-start.12 = (bf16[2,16,2304]{2,1,0:T(8,128)(2,1)S(1)}, bf16[2,16,2304]{2,1,0:T(8,128)(2,1)S(1)}, u32[]{:S(2)}, u32[]{:S(2)}) collective-permute-start(bf16[2,16,2304]{2,1,0:T(8,128)(2,1)S(1)} %slice.25), channel_id=1, source_target_pairs={{1,0},{2,1},{3,2},{0,3},{5,4},{6,5},{7,6},{4,7},{9,8},{10,9},{11,1... | collective-permute-start | bytes 442376 | tf_op jit(solution)/shard_map/ppermute | solution.py:585
  37.8 3.3 %collective-permute-start.14 = (bf16[2,16,2304]{2,1,0:T(8,128)(2,1)S(1)}, bf16[2,16,2304]{2,1,0:T(8,128)(2,1)S(1)}, u32[]{:S(2)}, u32[]{:S(2)}) collective-permute-start(bf16[2,16,2304]{2,1,0:T(8,128)(2,1)S(1)} %slice.27), channel_id=1, source_target_pairs={{1,0},{2,1},{3,2},{0,3},{5,4},{6,5},{7,6},{4,7},{9,8},{10,9},{11,1... | collective-permute-start | bytes 442376 | tf_op jit(solution)/shard_map/ppermute | solution.py:585
  41.8 2.1 %collective-permute-start.4 = (bf16[4,16,2304]{2,1,0:T(8,128)(2,1)S(1)}, bf16[4,16,2304]{2,1,0:T(8,128)(2,1)S(1)}, u32[]{:S(2)}, u32[]{:S(2)}) collective-permute-start(bf16[4,16,2304]{2,1,0:T(8,128)(2,1)S(1)} %get-tuple-element.27), channel_id=1, source_target_pairs={{16,0},{17,1},{18,2},{19,3},{20,4},{21,5},{22,6},{23,7},{24,8},{25... | collective-permute-start | bytes 884744 | tf_op jit(solution)/shard_map/ppermute | solution.py:590
  45.1 3.9 %block_product.3 = (bf16[4,16,2304]{2,1,0:T(8,128)(2,1)S(1)}, bf16[4,16,2304]{2,1,0:T(8,128)(2,1)S(1)}, bf16[4,16,2304]{2,1,0:T(8,128)(2,1)S(1)}, bf16[4,16,2304]{2,1,0:T(8,128)(2,1)S(1)}) custom-call(bf16[4,16,2304]{2,1,0:T(8,128)(2,1)S(1)} %collective-permute-done.9.refs_0_, bf16[4,16,2304]{2,1,0:T(8,128)(2,1)S(1)} %collective-permute-done.10.refs_1_, ...), custom_call_target="tpu_custom_call" | custom-call | flops 1509949440 | bytes 12000000 | tf_op jit(solution)/shard_map/block_product/pallas_call | solution.py:183
  50.0 2.3 %collective-permute-start.16 = (bf16[4,16,2304]{2,1,0:T(8,128)(2,1)S(1)}, bf16[4,16,2304]{2,1,0:T(8,128)(2,1)S(1)}, u32[]{:S(2)}, u32[]{:S(2)}) collective-permute-start(bf16[4,16,2304]{2,1,0:T(8,128)(2,1)S(1)} %get-tuple-element.35), channel_id=1, source_target_pairs={{16,0},{17,1},{18,2},{19,3},{20,4},{21,5},{22,6},{23,7},{24,8},{25... | collective-permute-start | bytes 884744 | tf_op jit(solution)/shard_map/ppermute | solution.py:590
  52.3 1.8 %collective-permute-start.17 = (bf16[4,16,2304]{2,1,0:T(8,128)(2,1)S(1)}, bf16[4,16,2304]{2,1,0:T(8,128)(2,1)S(1)}, u32[]{:S(2)}, u32[]{:S(2)}) collective-permute-start(bf16[4,16,2304]{2,1,0:T(8,128)(2,1)S(1)} %get-tuple-element.36), channel_id=1, source_target_pairs={{8,0},{9,1},{10,2},{11,3},{12,4},{13,5},{14,6},{15,7},{16,8},{17,9... | collective-permute-start | bytes 884744 | tf_op jit(solution)/shard_map/ppermute | solution.py:590
  54.2 4.0 %collective-permute-done.5.refs_3_ = bf16[4,16,2304]{2,1,0:T(8,128)(2,1)S(1)} collective-permute-done((bf16[4,16,2304]{2,1,0:T(8,128)(2,1)S(1)}, bf16[4,16,2304]{2,1,0:T(8,128)(2,1)S(1)}, u32[]{:S(2)}, u32[]{:S(2)}) %collective-permute-start.5) | collective-permute-done | bytes 294944 | tf_op jit(solution)/shard_map/ppermute | solution.py:590
  62.4 2.2 %collective-permute-done.17.refs_3_ = bf16[4,16,2304]{2,1,0:T(8,128)(2,1)S(1)} collective-permute-done((bf16[4,16,2304]{2,1,0:T(8,128)(2,1)S(1)}, bf16[4,16,2304]{2,1,0:T(8,128)(2,1)S(1)}, u32[]{:S(2)}, u32[]{:S(2)}) %collective-permute-start.17) | collective-permute-done | bytes 294944 | tf_op jit(solution)/shard_map/ppermute | solution.py:590
  64.9 4.1 %collective-permute-start.19 = (bf16[16,2304]{1,0:T(8,128)(2,1)S(1)}, bf16[16,2304]{1,0:T(8,128)(2,1)S(1)}, u32[]{:S(2)}, u32[]{:S(2)}) collective-permute-start(bf16[16,2304]{1,0:T(8,128)(2,1)S(1)} %get-tuple-element.38), channel_id=1, source_target_pairs={{5,0},{6,1},{7,2},{4,3},{1,4},{2,5},{3,6},{0,7},{13,8},{14,9},{15,... | collective-permute-start | bytes 221192 | tf_op jit(solution)/shard_map/ppermute | solution.py:585
  69.1 3.5 %collective-permute-start.21 = (bf16[16,2304]{1,0:T(8,128)(2,1)S(1)}, bf16[16,2304]{1,0:T(8,128)(2,1)S(1)}, u32[]{:S(2)}, u32[]{:S(2)}) collective-permute-start(bf16[16,2304]{1,0:T(8,128)(2,1)S(1)} %get-tuple-element.40), channel_id=1, source_target_pairs={{6,0},{7,1},{4,2},{5,3},{2,4},{3,5},{0,6},{1,7},{14,8},{15,9},{12,... | collective-permute-start | bytes 221192 | tf_op jit(solution)/shard_map/ppermute | solution.py:585
  72.6 2.3 %collective-permute-done.20.refs_6_ = bf16[16,2304]{1,0:T(8,128)(2,1)S(1)} collective-permute-done((bf16[16,2304]{1,0:T(8,128)(2,1)S(1)}, bf16[16,2304]{1,0:T(8,128)(2,1)S(1)}, u32[]{:S(2)}, u32[]{:S(2)}) %collective-permute-start.20) | collective-permute-done | bytes 73760 | tf_op jit(solution)/shard_map/ppermute | solution.py:585
  75.9 3.7 %attend_main.1 = (bf16[32,16,256]{2,1,0:T(8,128)(2,1)}, f32[8,2048]{1,0:T(8,128)S(1)}) custom-call(s32[1]{0:T(128)} %copy.12.len_ref, f32[1,10240]{1,0:T(1,128)S(1)} %bitcast.17, f32[8,128]{1,0:T(8,128)S(1)} %get-tuple-element.54.cos_ref, f32[8,128]{1,0:T(8,128)S(1)} %get-tuple-element.55.sin_ref, bf16[256,2048]{1,0:T(8,128)(2,1)S(1)} %bitcast.11, ...), custom_call_target="tpu_custom_call" | custom-call | flops 200000000 | bytes 6000000 | tf_op jit(solution)/shard_map/attend_main/pallas_call | solution.py:381
  79.6 7.3 %all-to-all-start.1 = ((bf16[32,16,256]{2,1,0:T(8,128)(2,1)}), bf16[32,16,256]{2,1,0:T(8,128)(2,1)S(1)}, u32[]{:S(2)}, u32[]{:S(2)}) async-start(bf16[32,16,256]{2,1,0:T(8,128)(2,1)} %get-tuple-element.41), calls=%async_computation.1 | async-start | bytes 524288 | tf_op jit(solution)/shard_map/all_to_all | solution.py:574
  87.1 3.4 %readout.1.read_ref = f32[1,2048]{1,0:T(1,128)S(1)} custom-call(f32[8,1024]{1,0:T(8,128)S(1)} %reshape.34.head_ref, bf16[1,2048,1024]{2,1,0:T(8,128)(2,1)} %w_hbm.3), custom_call_target="tpu_custom_call" | custom-call | flops 200000000 | bytes 5000000 | tf_op jit(solution)/shard_map/readout/pallas_call | solution.py:459
  90.7 3.1 %attend_cont.1.mixed_ref = bf16[16,8192]{1,0:T(8,128)(2,1)S(1)} custom-call(s32[1]{0:T(128)} %copy.12.len_ref, s32[1]{0:T(128)S(6)} %copy.13.bound_ref, f32[1,10240]{1,0:T(1,128)S(1)} %bitcast.18, f32[16,128]{1,0:T(8,128)S(1)} %get-tuple-element.56.cos_ref, f32[16,128]{1,0:T(8,128)S(1)} %get-tuple-element.57.sin_ref, bf16[256,2048]{1,0:T(8,128)(2,1)S(1)} %bitcast.12, ...), custom_call_target="tpu_custom_call" | custom-call | flops 400000000 | bytes 8000000 | tf_op jit(solution)/shard_map/attend_cont/pallas_call | solution.py:428
  93.7 2.3 %all-to-all-done.1.x_ref = bf16[32,16,256]{2,1,0:T(8,128)(2,1)S(1)} async-done(((bf16[32,16,256]{2,1,0:T(8,128)(2,1)}), bf16[32,16,256]{2,1,0:T(8,128)(2,1)S(1)}, u32[]{:S(2)}, u32[]{:S(2)}) %all-to-all-start.1) | async-done | bytes 262176 | tf_op jit(solution)/shard_map/all_to_all | solution.py:574
  96.0 2.6 %out_product.1 = f32[32,16,256]{2,1,0:T(8,128)S(1)} custom-call(bf16[32,16,256]{2,1,0:T(8,128)(2,1)S(1)} %all-to-all-done.1.x_ref, f32[1,2048]{1,0:T(1,128)S(1)} %readout.1.read_ref, bf16[1,2048,1024]{2,1,0:T(8,128)(2,1)} %w_hbm.3), custom_call_target="tpu_custom_call" | custom-call | flops 300000000 | bytes 5000000 | tf_op jit(solution)/shard_map/out_product/pallas_call | solution.py:505
  98.6 15.9 %all_to_all.16.parts_ref = f32[32,16,256]{2,1,0:T(8,128)S(1)} all-to-all(f32[32,16,256]{2,1,0:T(8,128)S(1)} %out_product.1), channel_id=1, replica_groups=mesh['grp'=4,'tp'=32] {'tp'}, dimensions={0} | all-to-all | bytes 1048576 | tf_op jit(solution)/shard_map/all_to_all | solution.py:574
  (58 shorter events, 14.8 us)
Async XLA Ops:
  14.2 7.3 %collective-permute-start = (bf16[4,16,2304]{2,1,0:T(8,128)(2,1)S(1)}, bf16[4,16,2304]{2,1,0:T(8,128)(2,1)S(1)}, u32[]{:S(2)}, u32[]{:S(2)}) collective-permute-start(bf16[4,16,2304]{2,1,0:T(8,128)(2,1)S(1)} %all_to_all.15.refs_0_), channel_id=1, source_target_pairs={{4,0},{5,1},{6,2},{7,3},{0,4},{1,5},{2,6},{3,7},{12,8},{13,9},{14,... | collective-permute-start | bytes 884744 | tf_op jit(solution)/shard_map/ppermute | solution.py:585
  15.8 9.6 %collective-permute-start.1 = (bf16[4,16,2304]{2,1,0:T(8,128)(2,1)S(1)}, bf16[4,16,2304]{2,1,0:T(8,128)(2,1)S(1)}, u32[]{:S(2)}, u32[]{:S(2)}) collective-permute-start(bf16[4,16,2304]{2,1,0:T(8,128)(2,1)S(1)} %all_to_all.15.refs_0_), channel_id=1, source_target_pairs={{1,0},{2,1},{3,2},{0,3},{5,4},{6,5},{7,6},{4,7},{9,8},{10,9},{11,1... | collective-permute-start | bytes 884744 | tf_op jit(solution)/shard_map/ppermute | solution.py:585
  18.6 11.1 %collective-permute-start.2 = (bf16[4,16,2304]{2,1,0:T(8,128)(2,1)S(1)}, bf16[4,16,2304]{2,1,0:T(8,128)(2,1)S(1)}, u32[]{:S(2)}, u32[]{:S(2)}) collective-permute-start(bf16[4,16,2304]{2,1,0:T(8,128)(2,1)S(1)} %all_to_all.15.refs_0_), channel_id=1, source_target_pairs={{3,0},{0,1},{1,2},{2,3},{7,4},{4,5},{5,6},{6,7},{11,8},{8,9},{9,10... | collective-permute-start | bytes 884744 | tf_op jit(solution)/shard_map/ppermute | solution.py:585
  21.5 16.2 %collective-permute-start.10 = (bf16[4,16,2304]{2,1,0:T(8,128)(2,1)S(1)}, bf16[4,16,2304]{2,1,0:T(8,128)(2,1)S(1)}, u32[]{:S(2)}, u32[]{:S(2)}) collective-permute-start(bf16[4,16,2304]{2,1,0:T(8,128)(2,1)S(1)} %collective-permute-done.refs_1_), channel_id=1, source_target_pairs={{3,0},{0,1},{1,2},{2,3},{7,4},{4,5},{5,6},{6,7},{11,8},{8,9},{9,10... | collective-permute-start | bytes 884744 | tf_op jit(solution)/shard_map/ppermute | solution.py:585
  23.0 14.8 %collective-permute-start.9 = (bf16[4,16,2304]{2,1,0:T(8,128)(2,1)S(1)}, bf16[4,16,2304]{2,1,0:T(8,128)(2,1)S(1)}, u32[]{:S(2)}, u32[]{:S(2)}) collective-permute-start(bf16[4,16,2304]{2,1,0:T(8,128)(2,1)S(1)} %collective-permute-done.refs_1_), channel_id=1, source_target_pairs={{1,0},{2,1},{3,2},{0,3},{5,4},{6,5},{7,6},{4,7},{9,8},{10,9},{11,1... | collective-permute-start | bytes 884744 | tf_op jit(solution)/shard_map/ppermute | solution.py:585
  33.6 18.6 %collective-permute-start.3 = (bf16[4,16,2304]{2,1,0:T(8,128)(2,1)S(1)}, bf16[4,16,2304]{2,1,0:T(8,128)(2,1)S(1)}, u32[]{:S(2)}, u32[]{:S(2)}) collective-permute-start(bf16[4,16,2304]{2,1,0:T(8,128)(2,1)S(1)} %get-tuple-element.26), channel_id=1, source_target_pairs={{24,0},{25,1},{26,2},{27,3},{28,4},{29,5},{30,6},{31,7},{0,8},{1,9... | collective-permute-start | bytes 884744 | tf_op jit(solution)/shard_map/ppermute | solution.py:590
  34.3 7.5 %collective-permute-start.11 = (bf16[2,16,2304]{2,1,0:T(8,128)(2,1)S(1)}, bf16[2,16,2304]{2,1,0:T(8,128)(2,1)S(1)}, u32[]{:S(2)}, u32[]{:S(2)}) collective-permute-start(bf16[2,16,2304]{2,1,0:T(8,128)(2,1)S(1)} %slice.24), channel_id=1, source_target_pairs={{3,0},{0,1},{1,2},{2,3},{7,4},{4,5},{5,6},{6,7},{11,8},{8,9},{9,10... | collective-permute-start | bytes 442376 | tf_op jit(solution)/shard_map/ppermute | solution.py:585
  34.4 9.5 %collective-permute-start.12 = (bf16[2,16,2304]{2,1,0:T(8,128)(2,1)S(1)}, bf16[2,16,2304]{2,1,0:T(8,128)(2,1)S(1)}, u32[]{:S(2)}, u32[]{:S(2)}) collective-permute-start(bf16[2,16,2304]{2,1,0:T(8,128)(2,1)S(1)} %slice.25), channel_id=1, source_target_pairs={{1,0},{2,1},{3,2},{0,3},{5,4},{6,5},{7,6},{4,7},{9,8},{10,9},{11,1... | collective-permute-start | bytes 442376 | tf_op jit(solution)/shard_map/ppermute | solution.py:585
  37.7 7.4 %collective-permute-start.13 = (bf16[2,16,2304]{2,1,0:T(8,128)(2,1)S(1)}, bf16[2,16,2304]{2,1,0:T(8,128)(2,1)S(1)}, u32[]{:S(2)}, u32[]{:S(2)}) collective-permute-start(bf16[2,16,2304]{2,1,0:T(8,128)(2,1)S(1)} %slice.26), channel_id=1, source_target_pairs={{3,0},{0,1},{1,2},{2,3},{7,4},{4,5},{5,6},{6,7},{11,8},{8,9},{9,10... | collective-permute-start | bytes 442376 | tf_op jit(solution)/shard_map/ppermute | solution.py:585
  37.8 7.3 %collective-permute-start.14 = (bf16[2,16,2304]{2,1,0:T(8,128)(2,1)S(1)}, bf16[2,16,2304]{2,1,0:T(8,128)(2,1)S(1)}, u32[]{:S(2)}, u32[]{:S(2)}) collective-permute-start(bf16[2,16,2304]{2,1,0:T(8,128)(2,1)S(1)} %slice.27), channel_id=1, source_target_pairs={{1,0},{2,1},{3,2},{0,3},{5,4},{6,5},{7,6},{4,7},{9,8},{10,9},{11,1... | collective-permute-start | bytes 442376 | tf_op jit(solution)/shard_map/ppermute | solution.py:585
  41.8 12.5 %collective-permute-start.4 = (bf16[4,16,2304]{2,1,0:T(8,128)(2,1)S(1)}, bf16[4,16,2304]{2,1,0:T(8,128)(2,1)S(1)}, u32[]{:S(2)}, u32[]{:S(2)}) collective-permute-start(bf16[4,16,2304]{2,1,0:T(8,128)(2,1)S(1)} %get-tuple-element.27), channel_id=1, source_target_pairs={{16,0},{17,1},{18,2},{19,3},{20,4},{21,5},{22,6},{23,7},{24,8},{25... | collective-permute-start | bytes 884744 | tf_op jit(solution)/shard_map/ppermute | solution.py:590
  43.9 43.2 %copy-start.4 = (f32[8192]{0:T(1024)S(1)}, f32[8192]{0:T(1024)}, u32[]{:S(2)}) copy-start(f32[8192]{0:T(1024)} %param.19) | copy-start | bytes 98308
  43.9 14.3 %collective-permute-start.5 = (bf16[4,16,2304]{2,1,0:T(8,128)(2,1)S(1)}, bf16[4,16,2304]{2,1,0:T(8,128)(2,1)S(1)}, u32[]{:S(2)}, u32[]{:S(2)}) collective-permute-start(bf16[4,16,2304]{2,1,0:T(8,128)(2,1)S(1)} %get-tuple-element.28), channel_id=1, source_target_pairs={{8,0},{9,1},{10,2},{11,3},{12,4},{13,5},{14,6},{15,7},{16,8},{17,9... | collective-permute-start | bytes 884744 | tf_op jit(solution)/shard_map/ppermute | solution.py:590
  49.0 11.8 %collective-permute-start.15 = (bf16[4,16,2304]{2,1,0:T(8,128)(2,1)S(1)}, bf16[4,16,2304]{2,1,0:T(8,128)(2,1)S(1)}, u32[]{:S(2)}, u32[]{:S(2)}) collective-permute-start(bf16[4,16,2304]{2,1,0:T(8,128)(2,1)S(1)} %get-tuple-element.34), channel_id=1, source_target_pairs={{24,0},{25,1},{26,2},{27,3},{28,4},{29,5},{30,6},{31,7},{0,8},{1,9... | collective-permute-start | bytes 884744 | tf_op jit(solution)/shard_map/ppermute | solution.py:590
  50.0 12.5 %collective-permute-start.16 = (bf16[4,16,2304]{2,1,0:T(8,128)(2,1)S(1)}, bf16[4,16,2304]{2,1,0:T(8,128)(2,1)S(1)}, u32[]{:S(2)}, u32[]{:S(2)}) collective-permute-start(bf16[4,16,2304]{2,1,0:T(8,128)(2,1)S(1)} %get-tuple-element.35), channel_id=1, source_target_pairs={{16,0},{17,1},{18,2},{19,3},{20,4},{21,5},{22,6},{23,7},{24,8},{25... | collective-permute-start | bytes 884744 | tf_op jit(solution)/shard_map/ppermute | solution.py:590
  52.3 12.3 %collective-permute-start.17 = (bf16[4,16,2304]{2,1,0:T(8,128)(2,1)S(1)}, bf16[4,16,2304]{2,1,0:T(8,128)(2,1)S(1)}, u32[]{:S(2)}, u32[]{:S(2)}) collective-permute-start(bf16[4,16,2304]{2,1,0:T(8,128)(2,1)S(1)} %get-tuple-element.36), channel_id=1, source_target_pairs={{8,0},{9,1},{10,2},{11,3},{12,4},{13,5},{14,6},{15,7},{16,8},{17,9... | collective-permute-start | bytes 884744 | tf_op jit(solution)/shard_map/ppermute | solution.py:590
  58.5 10.6 %collective-permute-start.6 = (bf16[16,2304]{1,0:T(8,128)(2,1)S(1)}, bf16[16,2304]{1,0:T(8,128)(2,1)S(1)}, u32[]{:S(2)}, u32[]{:S(2)}) collective-permute-start(bf16[16,2304]{1,0:T(8,128)(2,1)S(1)} %get-tuple-element.30), channel_id=1, source_target_pairs={{4,0},{5,1},{6,2},{7,3},{0,4},{1,5},{2,6},{3,7},{12,8},{13,9},{14,... | collective-permute-start | bytes 221192 | tf_op jit(solution)/shard_map/ppermute | solution.py:585
  59.1 10.0 %collective-permute-start.7 = (bf16[16,2304]{1,0:T(8,128)(2,1)S(1)}, bf16[16,2304]{1,0:T(8,128)(2,1)S(1)}, u32[]{:S(2)}, u32[]{:S(2)}) collective-permute-start(bf16[16,2304]{1,0:T(8,128)(2,1)S(1)} %get-tuple-element.31), channel_id=1, source_target_pairs={{3,0},{0,1},{1,2},{2,3},{7,4},{4,5},{5,6},{6,7},{11,8},{8,9},{9,10... | collective-permute-start | bytes 221192 | tf_op jit(solution)/shard_map/ppermute | solution.py:585
  60.8 11.8 %collective-permute-start.8 = (bf16[16,2304]{1,0:T(8,128)(2,1)S(1)}, bf16[16,2304]{1,0:T(8,128)(2,1)S(1)}, u32[]{:S(2)}, u32[]{:S(2)}) collective-permute-start(bf16[16,2304]{1,0:T(8,128)(2,1)S(1)} %get-tuple-element.32), channel_id=1, source_target_pairs={{1,0},{2,1},{3,2},{0,3},{5,4},{6,5},{7,6},{4,7},{9,8},{10,9},{11,1... | collective-permute-start | bytes 221192 | tf_op jit(solution)/shard_map/ppermute | solution.py:585
  64.9 7.7 %collective-permute-start.18 = (bf16[16,2304]{1,0:T(8,128)(2,1)S(1)}, bf16[16,2304]{1,0:T(8,128)(2,1)S(1)}, u32[]{:S(2)}, u32[]{:S(2)}) collective-permute-start(bf16[16,2304]{1,0:T(8,128)(2,1)S(1)} %get-tuple-element.37), channel_id=1, source_target_pairs={{7,0},{4,1},{5,2},{6,3},{3,4},{0,5},{1,6},{2,7},{15,8},{12,9},{13,... | collective-permute-start | bytes 221192 | tf_op jit(solution)/shard_map/ppermute | solution.py:585
  64.9 7.6 %collective-permute-start.19 = (bf16[16,2304]{1,0:T(8,128)(2,1)S(1)}, bf16[16,2304]{1,0:T(8,128)(2,1)S(1)}, u32[]{:S(2)}, u32[]{:S(2)}) collective-permute-start(bf16[16,2304]{1,0:T(8,128)(2,1)S(1)} %get-tuple-element.38), channel_id=1, source_target_pairs={{5,0},{6,1},{7,2},{4,3},{1,4},{2,5},{3,6},{0,7},{13,8},{14,9},{15,... | collective-permute-start | bytes 221192 | tf_op jit(solution)/shard_map/ppermute | solution.py:585
  69.1 5.9 %collective-permute-start.20 = (bf16[16,2304]{1,0:T(8,128)(2,1)S(1)}, bf16[16,2304]{1,0:T(8,128)(2,1)S(1)}, u32[]{:S(2)}, u32[]{:S(2)}) collective-permute-start(bf16[16,2304]{1,0:T(8,128)(2,1)S(1)} %get-tuple-element.39), channel_id=1, source_target_pairs={{2,0},{3,1},{0,2},{1,3},{6,4},{7,5},{4,6},{5,7},{10,8},{11,9},{8,1... | collective-permute-start | bytes 221192 | tf_op jit(solution)/shard_map/ppermute | solution.py:585
  69.1 6.8 %collective-permute-start.21 = (bf16[16,2304]{1,0:T(8,128)(2,1)S(1)}, bf16[16,2304]{1,0:T(8,128)(2,1)S(1)}, u32[]{:S(2)}, u32[]{:S(2)}) collective-permute-start(bf16[16,2304]{1,0:T(8,128)(2,1)S(1)} %get-tuple-element.40), channel_id=1, source_target_pairs={{6,0},{7,1},{4,2},{5,3},{2,4},{3,5},{0,6},{1,7},{14,8},{15,9},{12,... | collective-permute-start | bytes 221192 | tf_op jit(solution)/shard_map/ppermute | solution.py:585
  79.6 16.4 %all-to-all-start.1 = ((bf16[32,16,256]{2,1,0:T(8,128)(2,1)}), bf16[32,16,256]{2,1,0:T(8,128)(2,1)S(1)}, u32[]{:S(2)}, u32[]{:S(2)}) async-start(bf16[32,16,256]{2,1,0:T(8,128)(2,1)} %get-tuple-element.41), calls=%async_computation.1 | async-start | bytes 524288 | tf_op jit(solution)/shard_map/all_to_all | solution.py:574
  (4 other events, 121.7 us)

commit v5 on v4

--- a/solution.py
+++ b/solution.py
@@ -590,23 +590,24 @@
     return lax.ppermute(rows, "tp", route)
 
 
-FIRST_HOMES = ((0, 0), (1, 0), (0, 1), (0, 3))
-SECOND_HOMES = ((1, 1), (1, 3), (0, 2), (1, 2))
-HOMES = FIRST_HOMES + SECOND_HOMES
+NEAR_HOMES = ((0, 0), (1, 0))
+SIDE_HOMES = ((0, 1), (0, 3), (1, 1), (1, 3))
+FAR_HOMES = ((0, 2), (1, 2))
+HOMES = NEAR_HOMES + SIDE_HOMES + FAR_HOMES
 
 
 def project(rows, blocks, bias):
     near = lax.all_to_all(rows, "tp", split_axis=0, concat_axis=0, tiled=True, axis_index_groups=ALONG)
     half = ROW_BLOCKS // 2
     over = from_side(near, 1, 0)
-    sides, far = [], []
+    side, far = [], []
     for mine in (near, over):
         after = from_side(mine, 0, 1)
         before = from_side(mine, 0, 3)
         far += [from_side(before[:half], 0, 3), from_side(after[half:], 0, 1)]
-        sides.append([after, before])
+        side += [after, before]
     received = []
-    for homes, messages in ((FIRST_HOMES, [near, over] + sides[0]), (SECOND_HOMES, sides[1] + far)):
+    for homes, messages in ((NEAR_HOMES, [near, over]), (SIDE_HOMES, side), (FAR_HOMES, far)):
         parts = block_product(messages, blocks)
         parts = [parts[0]] + [from_along(parts[k], -k) for k in range(1, ROW_BLOCKS)]
         for (dy, dx), summed in zip(homes, sum_parts(bias, parts)):

time: 116 us -> 124 us (1.069)
  starting transfers between devices: 40.6 us -> 47.2 us
  Pallas kernels: 23.6 us -> 25.8 us
    ppermute x6 -> x9, starting transfers between devices: 9.01 us -> 13.5 us  [from_along(): return lax.ppermute(rows, 'tp', route)]
    ppermute x16, waiting for transfers between devices: 10.5 us -> 8.04 us  [from_side(): return lax.ppermute(rows, 'tp', route)]
    pallas_call x2 -> x3, Pallas kernels: 7.88 us -> 10.2 us  [block_product(): pl.pallas_call(functools.partial(product_kernel, tiles, counts), out_shap...]
    ppermute x6 -> x9, waiting for transfers between devices: 7.79 us -> 8.97 us  [from_along(): return lax.ppermute(rows, 'tp', route)]
  transfers between devices with their start and end apart: 23 -> 26, of which waited for: 8 -> 6; matrix products, arithmetic and copies ran while one was open for 0% -> 0% of each run, Pallas kernels for 13% -> 14%
where the time goes in v5:
time: 124 us
  starting transfers between devices  47.2 us (38%)
  blocking collectives  28.1 us (23%)
  Pallas kernels  25.8 us (21%)
  waiting for transfers between devices  19.5 us (16%)
  between operations  2.15 us (2%)
    ppermute x16, starting transfers between devices, from_side(): return lax.ppermute(rows, 'tp', route)  25.2 us
    all_to_all x1, blocking collectives, exchange(): return lax.all_to_all(rows, 'tp', split_axis=0, concat_axis=0, tiled=True)  15.9 us
    ppermute x9, starting transfers between devices, from_along(): return lax.ppermute(rows, 'tp', route)  13.5 us
    all_to_all x1, blocking collectives, project(): lax.all_to_all(rows, 'tp', split_axis=0, concat_axis=0, tiled=True, axis_...  12.2 us
    pallas_call x3, Pallas kernels, block_product(): pl.pallas_call(functools.partial(product_kernel, tiles, counts), out_shap...  10.2 us
    ppermute x9, waiting for transfers between devices, from_along(): return lax.ppermute(rows, 'tp', route)  8.97 us
    all_to_all x1, starting transfers between devices, exchange(): return lax.all_to_all(rows, 'tp', split_axis=0, concat_axis=0, tiled=True)  8.5 us
    ppermute x16, waiting for transfers between devices, from_side(): return lax.ppermute(rows, 'tp', route)  8.04 us
  transfers between devices with their start and end apart: 26, of which 6 were waited for; matrix products, arithmetic and copies ran while one was open for 0% of the time, Pallas kernels for 14%

profile of v5, /device:TPU:0, one launch (start us, length us, event | category | flops | bytes accessed | tf_op | source)
XLA Modules:
  0.0 123.7 jit_solution(3664021681708898050)
XLA Ops:
  2.0 12.2 %all_to_all.15.refs_0_ = bf16[4,16,2304]{2,1,0:T(8,128)(2,1)S(1)} all-to-all(bf16[4,16,2304]{2,1,0:T(8,128)(2,1)S(1)} %norm_rows.1), channel_id=1, replica_groups={{0,8,16,24},{1,9,17,25},{2,10,18,26},{3,11,19,27},{4,12,20,28},{5,13,21..., dimensions={0} | all-to-all | bytes 589824 | tf_op jit(solution)/shard_map/all_to_all | solution.py:600
  19.1 2.4 %collective-permute-done.refs_1_ = bf16[4,16,2304]{2,1,0:T(8,128)(2,1)S(1)} collective-permute-done((bf16[4,16,2304]{2,1,0:T(8,128)(2,1)S(1)}, bf16[4,16,2304]{2,1,0:T(8,128)(2,1)S(1)}, u32[]{:S(2)}, u32[]{:S(2)}) %collective-permute-start) | collective-permute-done | bytes 294944 | tf_op jit(solution)/shard_map/ppermute | solution.py:585
  25.8 3.0 %collective-permute-start.17 = (bf16[2,16,2304]{2,1,0:T(8,128)(2,1)S(1)}, bf16[2,16,2304]{2,1,0:T(8,128)(2,1)S(1)}, u32[]{:S(2)}, u32[]{:S(2)}) collective-permute-start(bf16[2,16,2304]{2,1,0:T(8,128)(2,1)S(1)} %slice.25), channel_id=1, source_target_pairs={{1,0},{2,1},{3,2},{0,3},{5,4},{6,5},{7,6},{4,7},{9,8},{10,9},{11,1... | collective-permute-start | bytes 442376 | tf_op jit(solution)/shard_map/ppermute | solution.py:585
  28.8 3.1 %collective-permute-done.8.refs_3_ = bf16[4,16,2304]{2,1,0:T(8,128)(2,1)S(1)} collective-permute-done((bf16[4,16,2304]{2,1,0:T(8,128)(2,1)S(1)}, bf16[4,16,2304]{2,1,0:T(8,128)(2,1)S(1)}, u32[]{:S(2)}, u32[]{:S(2)}) %collective-permute-start.8) | collective-permute-done | bytes 294944 | tf_op jit(solution)/shard_map/ppermute | solution.py:585
  33.0 2.3 %collective-permute-start.19 = (bf16[2,16,2304]{2,1,0:T(8,128)(2,1)S(1)}, bf16[2,16,2304]{2,1,0:T(8,128)(2,1)S(1)}, u32[]{:S(2)}, u32[]{:S(2)}) collective-permute-start(bf16[2,16,2304]{2,1,0:T(8,128)(2,1)S(1)} %slice.27), channel_id=1, source_target_pairs={{1,0},{2,1},{3,2},{0,3},{5,4},{6,5},{7,6},{4,7},{9,8},{10,9},{11,1... | collective-permute-start | bytes 442376 | tf_op jit(solution)/shard_map/ppermute | solution.py:585
  35.3 3.1 %block_product.3 = (bf16[2,16,2304]{2,1,0:T(8,128)(2,1)S(1)}, bf16[2,16,2304]{2,1,0:T(8,128)(2,1)S(1)}, bf16[2,16,2304]{2,1,0:T(8,128)(2,1)S(1)}, bf16[2,16,2304]{2,1,0:T(8,128)(2,1)S(1)}) custom-call(bf16[4,16,2304]{2,1,0:T(8,128)(2,1)S(1)} %all_to_all.15.refs_0_, bf16[4,16,2304]{2,1,0:T(8,128)(2,1)S(1)} %collective-permute-done.refs_1_, ...), custom_call_target="tpu_custom_call" | custom-call | flops 754974720 | bytes 12000000 | tf_op jit(solution)/shard_map/block_product/pallas_call | solution.py:183
  39.1 2.1 %collective-permute-start.2 = (bf16[2,16,2304]{2,1,0:T(8,128)(2,1)S(1)}, bf16[2,16,2304]{2,1,0:T(8,128)(2,1)S(1)}, u32[]{:S(2)}, u32[]{:S(2)}) collective-permute-start(bf16[2,16,2304]{2,1,0:T(8,128)(2,1)S(1)} %get-tuple-element.31), channel_id=1, source_target_pairs={{16,0},{17,1},{18,2},{19,3},{20,4},{21,5},{22,6},{23,7},{24,8},{25... | collective-permute-start | bytes 442376 | tf_op jit(solution)/shard_map/ppermute | solution.py:590
  42.5 3.1 %block_product.5 = (bf16[2,16,2304]{2,1,0:T(8,128)(2,1)S(1)}, bf16[2,16,2304]{2,1,0:T(8,128)(2,1)S(1)}, bf16[2,16,2304]{2,1,0:T(8,128)(2,1)S(1)}, bf16[2,16,2304]{2,1,0:T(8,128)(2,1)S(1)}) custom-call(bf16[2,16,2304]{2,1,0:T(8,128)(2,1)S(1)} %collective-permute-done.16.refs_0_, bf16[2,16,2304]{2,1,0:T(8,128)(2,1)S(1)} %collective-permute-done.17.refs_1_, ...), custom_call_target="tpu_custom_call" | custom-call | flops 754974720 | bytes 12000000 | tf_op jit(solution)/shard_map/block_product/pallas_call | solution.py:183
  47.1 4.0 %block_product.4 = (bf16[4,16,2304]{2,1,0:T(8,128)(2,1)S(1)}, bf16[4,16,2304]{2,1,0:T(8,128)(2,1)S(1)}, bf16[4,16,2304]{2,1,0:T(8,128)(2,1)S(1)}, bf16[4,16,2304]{2,1,0:T(8,128)(2,1)S(1)}) custom-call(bf16[4,16,2304]{2,1,0:T(8,128)(2,1)S(1)} %collective-permute-done.5.refs_0_, bf16[4,16,2304]{2,1,0:T(8,128)(2,1)S(1)} %collective-permute-done.6.refs_1_, ...), custom_call_target="tpu_custom_call" | custom-call | flops 1509949440 | bytes 12000000 | tf_op jit(solution)/shard_map/block_product/pallas_call | solution.py:183
  52.6 2.5 %collective-permute-start.10 = (bf16[4,16,2304]{2,1,0:T(8,128)(2,1)S(1)}, bf16[4,16,2304]{2,1,0:T(8,128)(2,1)S(1)}, u32[]{:S(2)}, u32[]{:S(2)}) collective-permute-start(bf16[4,16,2304]{2,1,0:T(8,128)(2,1)S(1)} %get-tuple-element.37), channel_id=1, source_target_pairs={{16,0},{17,1},{18,2},{19,3},{20,4},{21,5},{22,6},{23,7},{24,8},{25... | collective-permute-start | bytes 884744 | tf_op jit(solution)/shard_map/ppermute | solution.py:590
  57.3 2.5 %collective-permute-start.22 = (bf16[2,16,2304]{2,1,0:T(8,128)(2,1)S(1)}, bf16[2,16,2304]{2,1,0:T(8,128)(2,1)S(1)}, u32[]{:S(2)}, u32[]{:S(2)}) collective-permute-start(bf16[2,16,2304]{2,1,0:T(8,128)(2,1)S(1)} %get-tuple-element.46), channel_id=1, source_target_pairs={{8,0},{9,1},{10,2},{11,3},{12,4},{13,5},{14,6},{15,7},{16,8},{17,9... | collective-permute-start | bytes 442376 | tf_op jit(solution)/shard_map/ppermute | solution.py:590
  60.0 6.8 %collective-permute-done.21.refs_2_ = bf16[2,16,2304]{2,1,0:T(8,128)(2,1)S(1)} collective-permute-done((bf16[2,16,2304]{2,1,0:T(8,128)(2,1)S(1)}, bf16[2,16,2304]{2,1,0:T(8,128)(2,1)S(1)}, u32[]{:S(2)}, u32[]{:S(2)}) %collective-permute-start.21) | collective-permute-done | bytes 147488 | tf_op jit(solution)/shard_map/ppermute | solution.py:590
  66.9 2.2 %collective-permute-done.22.refs_3_ = bf16[2,16,2304]{2,1,0:T(8,128)(2,1)S(1)} collective-permute-done((bf16[2,16,2304]{2,1,0:T(8,128)(2,1)S(1)}, bf16[2,16,2304]{2,1,0:T(8,128)(2,1)S(1)}, u32[]{:S(2)}, u32[]{:S(2)}) %collective-permute-start.22) | collective-permute-done | bytes 147488 | tf_op jit(solution)/shard_map/ppermute | solution.py:590
  70.0 2.1 %collective-permute-start.24 = (bf16[16,2304]{1,0:T(8,128)(2,1)S(1)}, bf16[16,2304]{1,0:T(8,128)(2,1)S(1)}, u32[]{:S(2)}, u32[]{:S(2)}) collective-permute-start(bf16[16,2304]{1,0:T(8,128)(2,1)S(1)} %get-tuple-element.48), channel_id=1, source_target_pairs={{6,0},{7,1},{4,2},{5,3},{2,4},{3,5},{0,6},{1,7},{14,8},{15,9},{12,... | collective-permute-start | bytes 221192 | tf_op jit(solution)/shard_map/ppermute | solution.py:585
  72.5 3.2 %collective-permute-start.13 = (bf16[16,2304]{1,0:T(8,128)(2,1)S(1)}, bf16[16,2304]{1,0:T(8,128)(2,1)S(1)}, u32[]{:S(2)}, u32[]{:S(2)}) collective-permute-start(bf16[16,2304]{1,0:T(8,128)(2,1)S(1)} %get-tuple-element.40), channel_id=1, source_target_pairs={{1,0},{2,1},{3,2},{0,3},{5,4},{6,5},{7,6},{4,7},{9,8},{10,9},{11,1... | collective-permute-start | bytes 221192 | tf_op jit(solution)/shard_map/ppermute | solution.py:585
  76.3 3.5 %collective-permute-start.15 = (bf16[16,2304]{1,0:T(8,128)(2,1)S(1)}, bf16[16,2304]{1,0:T(8,128)(2,1)S(1)}, u32[]{:S(2)}, u32[]{:S(2)}) collective-permute-start(bf16[16,2304]{1,0:T(8,128)(2,1)S(1)} %get-tuple-element.42), channel_id=1, source_target_pairs={{5,0},{6,1},{7,2},{4,3},{1,4},{2,5},{3,6},{0,7},{13,8},{14,9},{15,... | collective-permute-start | bytes 221192 | tf_op jit(solution)/shard_map/ppermute | solution.py:585
  79.9 2.5 %collective-permute-done.14.refs_4_ = bf16[16,2304]{1,0:T(8,128)(2,1)S(1)} collective-permute-done((bf16[16,2304]{1,0:T(8,128)(2,1)S(1)}, bf16[16,2304]{1,0:T(8,128)(2,1)S(1)}, u32[]{:S(2)}, u32[]{:S(2)}) %collective-permute-start.14) | collective-permute-done | bytes 73760 | tf_op jit(solution)/shard_map/ppermute | solution.py:585
  82.3 3.7 %attend_main.1 = (bf16[32,16,256]{2,1,0:T(8,128)(2,1)}, f32[8,2048]{1,0:T(8,128)S(1)}) custom-call(s32[1]{0:T(128)} %copy.12.len_ref, f32[1,10240]{1,0:T(1,128)S(1)} %bitcast.18, f32[8,128]{1,0:T(8,128)S(1)} %get-tuple-element.62.cos_ref, f32[8,128]{1,0:T(8,128)S(1)} %get-tuple-element.63.sin_ref, bf16[256,2048]{1,0:T(8,128)(2,1)S(1)} %bitcast.11, ...), custom_call_target="tpu_custom_call" | custom-call | flops 200000000 | bytes 6000000 | tf_op jit(solution)/shard_map/attend_main/pallas_call | solution.py:381
  86.1 8.5 %all-to-all-start.1 = ((bf16[32,16,256]{2,1,0:T(8,128)(2,1)}), bf16[32,16,256]{2,1,0:T(8,128)(2,1)S(1)}, u32[]{:S(2)}, u32[]{:S(2)}) async-start(bf16[32,16,256]{2,1,0:T(8,128)(2,1)} %get-tuple-element.49), calls=%async_computation.1 | async-start | bytes 524288 | tf_op jit(solution)/shard_map/all_to_all | solution.py:574
  94.7 3.4 %readout.1.read_ref = f32[1,2048]{1,0:T(1,128)S(1)} custom-call(f32[8,1024]{1,0:T(8,128)S(1)} %reshape.34.head_ref, bf16[1,2048,1024]{2,1,0:T(8,128)(2,1)} %w_hbm.3), custom_call_target="tpu_custom_call" | custom-call | flops 200000000 | bytes 5000000 | tf_op jit(solution)/shard_map/readout/pallas_call | solution.py:459
  98.3 3.1 %attend_cont.1.mixed_ref = bf16[16,8192]{1,0:T(8,128)(2,1)S(1)} custom-call(s32[1]{0:T(128)} %copy.12.len_ref, s32[1]{0:T(128)S(6)} %copy.13.bound_ref, f32[1,10240]{1,0:T(1,128)S(1)} %bitcast.19, f32[16,128]{1,0:T(8,128)S(1)} %get-tuple-element.64.cos_ref, f32[16,128]{1,0:T(8,128)S(1)} %get-tuple-element.65.sin_ref, bf16[256,2048]{1,0:T(8,128)(2,1)S(1)} %bitcast.12, ...), custom_call_target="tpu_custom_call" | custom-call | flops 400000000 | bytes 8000000 | tf_op jit(solution)/shard_map/attend_cont/pallas_call | solution.py:428
  101.3 2.5 %all-to-all-done.1.x_ref = bf16[32,16,256]{2,1,0:T(8,128)(2,1)S(1)} async-done(((bf16[32,16,256]{2,1,0:T(8,128)(2,1)}), bf16[32,16,256]{2,1,0:T(8,128)(2,1)S(1)}, u32[]{:S(2)}, u32[]{:S(2)}) %all-to-all-start.1) | async-done | bytes 262176 | tf_op jit(solution)/shard_map/all_to_all | solution.py:574
  103.8 2.6 %out_product.1 = f32[32,16,256]{2,1,0:T(8,128)S(1)} custom-call(bf16[32,16,256]{2,1,0:T(8,128)(2,1)S(1)} %all-to-all-done.1.x_ref, f32[1,2048]{1,0:T(1,128)S(1)} %readout.1.read_ref, bf16[1,2048,1024]{2,1,0:T(8,128)(2,1)} %w_hbm.3), custom_call_target="tpu_custom_call" | custom-call | flops 300000000 | bytes 5000000 | tf_op jit(solution)/shard_map/out_product/pallas_call | solution.py:505
  106.4 15.9 %all_to_all.16.parts_ref = f32[32,16,256]{2,1,0:T(8,128)S(1)} all-to-all(f32[32,16,256]{2,1,0:T(8,128)S(1)} %out_product.1), channel_id=1, replica_groups=mesh['grp'=4,'tp'=32] {'tp'}, dimensions={0} | all-to-all | bytes 1048576 | tf_op jit(solution)/shard_map/all_to_all | solution.py:574
  (66 shorter events, 21.3 us)
Async XLA Ops:
  14.2 7.3 %collective-permute-start = (bf16[4,16,2304]{2,1,0:T(8,128)(2,1)S(1)}, bf16[4,16,2304]{2,1,0:T(8,128)(2,1)S(1)}, u32[]{:S(2)}, u32[]{:S(2)}) collective-permute-start(bf16[4,16,2304]{2,1,0:T(8,128)(2,1)S(1)} %all_to_all.15.refs_0_), channel_id=1, source_target_pairs={{4,0},{5,1},{6,2},{7,3},{0,4},{1,5},{2,6},{3,7},{12,8},{13,9},{14,... | collective-permute-start | bytes 884744 | tf_op jit(solution)/shard_map/ppermute | solution.py:585
  15.8 9.6 %collective-permute-start.6 = (bf16[4,16,2304]{2,1,0:T(8,128)(2,1)S(1)}, bf16[4,16,2304]{2,1,0:T(8,128)(2,1)S(1)}, u32[]{:S(2)}, u32[]{:S(2)}) collective-permute-start(bf16[4,16,2304]{2,1,0:T(8,128)(2,1)S(1)} %all_to_all.15.refs_0_), channel_id=1, source_target_pairs={{3,0},{0,1},{1,2},{2,3},{7,4},{4,5},{5,6},{6,7},{11,8},{8,9},{9,10... | collective-permute-start | bytes 884744 | tf_op jit(solution)/shard_map/ppermute | solution.py:585
  17.3 8.5 %collective-permute-start.5 = (bf16[4,16,2304]{2,1,0:T(8,128)(2,1)S(1)}, bf16[4,16,2304]{2,1,0:T(8,128)(2,1)S(1)}, u32[]{:S(2)}, u32[]{:S(2)}) collective-permute-start(bf16[4,16,2304]{2,1,0:T(8,128)(2,1)S(1)} %all_to_all.15.refs_0_), channel_id=1, source_target_pairs={{1,0},{2,1},{3,2},{0,3},{5,4},{6,5},{7,6},{4,7},{9,8},{10,9},{11,1... | collective-permute-start | bytes 884744 | tf_op jit(solution)/shard_map/ppermute | solution.py:585
  21.5 10.4 %collective-permute-start.8 = (bf16[4,16,2304]{2,1,0:T(8,128)(2,1)S(1)}, bf16[4,16,2304]{2,1,0:T(8,128)(2,1)S(1)}, u32[]{:S(2)}, u32[]{:S(2)}) collective-permute-start(bf16[4,16,2304]{2,1,0:T(8,128)(2,1)S(1)} %collective-permute-done.refs_1_), channel_id=1, source_target_pairs={{3,0},{0,1},{1,2},{2,3},{7,4},{4,5},{5,6},{6,7},{11,8},{8,9},{9,10... | collective-permute-start | bytes 884744 | tf_op jit(solution)/shard_map/ppermute | solution.py:585
  23.0 10.0 %collective-permute-start.7 = (bf16[4,16,2304]{2,1,0:T(8,128)(2,1)S(1)}, bf16[4,16,2304]{2,1,0:T(8,128)(2,1)S(1)}, u32[]{:S(2)}, u32[]{:S(2)}) collective-permute-start(bf16[4,16,2304]{2,1,0:T(8,128)(2,1)S(1)} %collective-permute-done.refs_1_), channel_id=1, source_target_pairs={{1,0},{2,1},{3,2},{0,3},{5,4},{6,5},{7,6},{4,7},{9,8},{10,9},{11,1... | collective-permute-start | bytes 884744 | tf_op jit(solution)/shard_map/ppermute | solution.py:585
  25.4 13.6 %collective-permute-start.16 = (bf16[2,16,2304]{2,1,0:T(8,128)(2,1)S(1)}, bf16[2,16,2304]{2,1,0:T(8,128)(2,1)S(1)}, u32[]{:S(2)}, u32[]{:S(2)}) collective-permute-start(bf16[2,16,2304]{2,1,0:T(8,128)(2,1)S(1)} %slice.24), channel_id=1, source_target_pairs={{3,0},{0,1},{1,2},{2,3},{7,4},{4,5},{5,6},{6,7},{11,8},{8,9},{9,10... | collective-permute-start | bytes 442376 | tf_op jit(solution)/shard_map/ppermute | solution.py:585
  25.8 15.3 %collective-permute-start.17 = (bf16[2,16,2304]{2,1,0:T(8,128)(2,1)S(1)}, bf16[2,16,2304]{2,1,0:T(8,128)(2,1)S(1)}, u32[]{:S(2)}, u32[]{:S(2)}) collective-permute-start(bf16[2,16,2304]{2,1,0:T(8,128)(2,1)S(1)} %slice.25), channel_id=1, source_target_pairs={{1,0},{2,1},{3,2},{0,3},{5,4},{6,5},{7,6},{4,7},{9,8},{10,9},{11,1... | collective-permute-start | bytes 442376 | tf_op jit(solution)/shard_map/ppermute | solution.py:585
  31.9 10.5 %collective-permute-start.18 = (bf16[2,16,2304]{2,1,0:T(8,128)(2,1)S(1)}, bf16[2,16,2304]{2,1,0:T(8,128)(2,1)S(1)}, u32[]{:S(2)}, u32[]{:S(2)}) collective-permute-start(bf16[2,16,2304]{2,1,0:T(8,128)(2,1)S(1)} %slice.26), channel_id=1, source_target_pairs={{3,0},{0,1},{1,2},{2,3},{7,4},{4,5},{5,6},{6,7},{11,8},{8,9},{9,10... | collective-permute-start | bytes 442376 | tf_op jit(solution)/shard_map/ppermute | solution.py:585
  33.0 9.4 %collective-permute-start.19 = (bf16[2,16,2304]{2,1,0:T(8,128)(2,1)S(1)}, bf16[2,16,2304]{2,1,0:T(8,128)(2,1)S(1)}, u32[]{:S(2)}, u32[]{:S(2)}) collective-permute-start(bf16[2,16,2304]{2,1,0:T(8,128)(2,1)S(1)} %slice.27), channel_id=1, source_target_pairs={{1,0},{2,1},{3,2},{0,3},{5,4},{6,5},{7,6},{4,7},{9,8},{10,9},{11,1... | collective-permute-start | bytes 442376 | tf_op jit(solution)/shard_map/ppermute | solution.py:585
  38.4 14.1 %collective-permute-start.1 = (bf16[2,16,2304]{2,1,0:T(8,128)(2,1)S(1)}, bf16[2,16,2304]{2,1,0:T(8,128)(2,1)S(1)}, u32[]{:S(2)}, u32[]{:S(2)}) collective-permute-start(bf16[2,16,2304]{2,1,0:T(8,128)(2,1)S(1)} %get-tuple-element.30), channel_id=1, source_target_pairs={{24,0},{25,1},{26,2},{27,3},{28,4},{29,5},{30,6},{31,7},{0,8},{1,9... | collective-permute-start | bytes 442376 | tf_op jit(solution)/shard_map/ppermute | solution.py:590
  39.1 16.0 %collective-permute-start.2 = (bf16[2,16,2304]{2,1,0:T(8,128)(2,1)S(1)}, bf16[2,16,2304]{2,1,0:T(8,128)(2,1)S(1)}, u32[]{:S(2)}, u32[]{:S(2)}) collective-permute-start(bf16[2,16,2304]{2,1,0:T(8,128)(2,1)S(1)} %get-tuple-element.31), channel_id=1, source_target_pairs={{16,0},{17,1},{18,2},{19,3},{20,4},{21,5},{22,6},{23,7},{24,8},{25... | collective-permute-start | bytes 442376 | tf_op jit(solution)/shard_map/ppermute | solution.py:590
  41.2 14.2 %collective-permute-start.3 = (bf16[2,16,2304]{2,1,0:T(8,128)(2,1)S(1)}, bf16[2,16,2304]{2,1,0:T(8,128)(2,1)S(1)}, u32[]{:S(2)}, u32[]{:S(2)}) collective-permute-start(bf16[2,16,2304]{2,1,0:T(8,128)(2,1)S(1)} %get-tuple-element.32), channel_id=1, source_target_pairs={{8,0},{9,1},{10,2},{11,3},{12,4},{13,5},{14,6},{15,7},{16,8},{17,9... | collective-permute-start | bytes 442376 | tf_op jit(solution)/shard_map/ppermute | solution.py:590
  45.6 11.7 %collective-permute-start.20 = (bf16[2,16,2304]{2,1,0:T(8,128)(2,1)S(1)}, bf16[2,16,2304]{2,1,0:T(8,128)(2,1)S(1)}, u32[]{:S(2)}, u32[]{:S(2)}) collective-permute-start(bf16[2,16,2304]{2,1,0:T(8,128)(2,1)S(1)} %get-tuple-element.44), channel_id=1, source_target_pairs={{24,0},{25,1},{26,2},{27,3},{28,4},{29,5},{30,6},{31,7},{0,8},{1,9... | collective-permute-start | bytes 442376 | tf_op jit(solution)/shard_map/ppermute | solution.py:590
  51.0 19.0 %collective-permute-start.9 = (bf16[4,16,2304]{2,1,0:T(8,128)(2,1)S(1)}, bf16[4,16,2304]{2,1,0:T(8,128)(2,1)S(1)}, u32[]{:S(2)}, u32[]{:S(2)}) collective-permute-start(bf16[4,16,2304]{2,1,0:T(8,128)(2,1)S(1)} %get-tuple-element.36), channel_id=1, source_target_pairs={{24,0},{25,1},{26,2},{27,3},{28,4},{29,5},{30,6},{31,7},{0,8},{1,9... | collective-permute-start | bytes 884744 | tf_op jit(solution)/shard_map/ppermute | solution.py:590
  52.6 19.6 %collective-permute-start.10 = (bf16[4,16,2304]{2,1,0:T(8,128)(2,1)S(1)}, bf16[4,16,2304]{2,1,0:T(8,128)(2,1)S(1)}, u32[]{:S(2)}, u32[]{:S(2)}) collective-permute-start(bf16[4,16,2304]{2,1,0:T(8,128)(2,1)S(1)} %get-tuple-element.37), channel_id=1, source_target_pairs={{16,0},{17,1},{18,2},{19,3},{20,4},{21,5},{22,6},{23,7},{24,8},{25... | collective-permute-start | bytes 884744 | tf_op jit(solution)/shard_map/ppermute | solution.py:590
  55.1 17.1 %collective-permute-start.11 = (bf16[4,16,2304]{2,1,0:T(8,128)(2,1)S(1)}, bf16[4,16,2304]{2,1,0:T(8,128)(2,1)S(1)}, u32[]{:S(2)}, u32[]{:S(2)}) collective-permute-start(bf16[4,16,2304]{2,1,0:T(8,128)(2,1)S(1)} %get-tuple-element.38), channel_id=1, source_target_pairs={{8,0},{9,1},{10,2},{11,3},{12,4},{13,5},{14,6},{15,7},{16,8},{17,9... | collective-permute-start | bytes 884744 | tf_op jit(solution)/shard_map/ppermute | solution.py:590
  55.3 11.5 %collective-permute-start.21 = (bf16[2,16,2304]{2,1,0:T(8,128)(2,1)S(1)}, bf16[2,16,2304]{2,1,0:T(8,128)(2,1)S(1)}, u32[]{:S(2)}, u32[]{:S(2)}) collective-permute-start(bf16[2,16,2304]{2,1,0:T(8,128)(2,1)S(1)} %get-tuple-element.45), channel_id=1, source_target_pairs={{16,0},{17,1},{18,2},{19,3},{20,4},{21,5},{22,6},{23,7},{24,8},{25... | collective-permute-start | bytes 442376 | tf_op jit(solution)/shard_map/ppermute | solution.py:590
  57.3 11.8 %collective-permute-start.22 = (bf16[2,16,2304]{2,1,0:T(8,128)(2,1)S(1)}, bf16[2,16,2304]{2,1,0:T(8,128)(2,1)S(1)}, u32[]{:S(2)}, u32[]{:S(2)}) collective-permute-start(bf16[2,16,2304]{2,1,0:T(8,128)(2,1)S(1)} %get-tuple-element.46), channel_id=1, source_target_pairs={{8,0},{9,1},{10,2},{11,3},{12,4},{13,5},{14,6},{15,7},{16,8},{17,9... | collective-permute-start | bytes 442376 | tf_op jit(solution)/shard_map/ppermute | solution.py:590
  66.8 8.9 %collective-permute-start.4 = (bf16[16,2304]{1,0:T(8,128)(2,1)S(1)}, bf16[16,2304]{1,0:T(8,128)(2,1)S(1)}, u32[]{:S(2)}, u32[]{:S(2)}) collective-permute-start(bf16[16,2304]{1,0:T(8,128)(2,1)S(1)} %get-tuple-element.34), channel_id=1, source_target_pairs={{4,0},{5,1},{6,2},{7,3},{0,4},{1,5},{2,6},{3,7},{12,8},{13,9},{14,... | collective-permute-start | bytes 221192 | tf_op jit(solution)/shard_map/ppermute | solution.py:585
  69.2 7.1 %collective-permute-start.23 = (bf16[16,2304]{1,0:T(8,128)(2,1)S(1)}, bf16[16,2304]{1,0:T(8,128)(2,1)S(1)}, u32[]{:S(2)}, u32[]{:S(2)}) collective-permute-start(bf16[16,2304]{1,0:T(8,128)(2,1)S(1)} %get-tuple-element.47), channel_id=1, source_target_pairs={{2,0},{3,1},{0,2},{1,3},{6,4},{7,5},{4,6},{5,7},{10,8},{11,9},{8,1... | collective-permute-start | bytes 221192 | tf_op jit(solution)/shard_map/ppermute | solution.py:585
  70.0 9.9 %collective-permute-start.24 = (bf16[16,2304]{1,0:T(8,128)(2,1)S(1)}, bf16[16,2304]{1,0:T(8,128)(2,1)S(1)}, u32[]{:S(2)}, u32[]{:S(2)}) collective-permute-start(bf16[16,2304]{1,0:T(8,128)(2,1)S(1)} %get-tuple-element.48), channel_id=1, source_target_pairs={{6,0},{7,1},{4,2},{5,3},{2,4},{3,5},{0,6},{1,7},{14,8},{15,9},{12,... | collective-permute-start | bytes 221192 | tf_op jit(solution)/shard_map/ppermute | solution.py:585
  72.4 7.5 %collective-permute-start.12 = (bf16[16,2304]{1,0:T(8,128)(2,1)S(1)}, bf16[16,2304]{1,0:T(8,128)(2,1)S(1)}, u32[]{:S(2)}, u32[]{:S(2)}) collective-permute-start(bf16[16,2304]{1,0:T(8,128)(2,1)S(1)} %get-tuple-element.39), channel_id=1, source_target_pairs={{3,0},{0,1},{1,2},{2,3},{7,4},{4,5},{5,6},{6,7},{11,8},{8,9},{9,10... | collective-permute-start | bytes 221192 | tf_op jit(solution)/shard_map/ppermute | solution.py:585
  72.5 7.4 %collective-permute-start.13 = (bf16[16,2304]{1,0:T(8,128)(2,1)S(1)}, bf16[16,2304]{1,0:T(8,128)(2,1)S(1)}, u32[]{:S(2)}, u32[]{:S(2)}) collective-permute-start(bf16[16,2304]{1,0:T(8,128)(2,1)S(1)} %get-tuple-element.40), channel_id=1, source_target_pairs={{1,0},{2,1},{3,2},{0,3},{5,4},{6,5},{7,6},{4,7},{9,8},{10,9},{11,1... | collective-permute-start | bytes 221192 | tf_op jit(solution)/shard_map/ppermute | solution.py:585
  86.1 17.7 %all-to-all-start.1 = ((bf16[32,16,256]{2,1,0:T(8,128)(2,1)}), bf16[32,16,256]{2,1,0:T(8,128)(2,1)S(1)}, u32[]{:S(2)}, u32[]{:S(2)}) async-start(bf16[32,16,256]{2,1,0:T(8,128)(2,1)} %get-tuple-element.49), calls=%async_computation.1 | async-start | bytes 524288 | tf_op jit(solution)/shard_map/all_to_all | solution.py:574
  (7 other events, 170.9 us)

commit v6 on v4

--- a/solution.py
+++ b/solution.py
@@ -119,10 +119,12 @@
     return column // 4, lax.rem(column, 4)
 
 
-def product_kernel(tiles, counts, *refs):
-    x_refs = refs[: len(counts)]
-    w_hbm, *out_refs = refs[len(counts) : len(counts) + 1 + ROW_BLOCKS]
-    rows_ref, wide_ref, w_ref, sems, part_ref = refs[len(counts) + 1 + ROW_BLOCKS :]
+def product_kernel(tiles, counts, places, *refs):
+    x_refs, refs = refs[: len(counts)], refs[len(counts) :]
+    if places:
+        earlier_ref, refs = refs[0], refs[1:]
+    w_hbm, *out_refs = refs[: 1 + ROW_BLOCKS]
+    main_ref, rows_ref, wide_ref, w_ref, sems, part_ref = refs[1 + ROW_BLOCKS :]
     n = pl.program_id(0)
     members = sum(counts)
     count = members * CTOK
@@ -165,27 +167,40 @@
 
     @pl.when(n == tiles - 1)
     def _():
+        z = lax.axis_index("tp") // COL_BLOCKS
+        done = earlier_ref.shape[0] // ROW_BLOCKS if places else 0
         for k in range(halves):
-            lane = width + REST + k * 128
-            part_ref[:, :, lane : lane + 128] = wide_ref[k].astype(jnp.bfloat16).reshape(members, CTOK, 128)
-        z = lax.axis_index("tp") // COL_BLOCKS
+            lanes = slice(k * 128, (k + 1) * 128)
+            packed = wide_ref[k].astype(jnp.bfloat16).reshape(members, CTOK, 128)
+            if not places:
+                main_ref[:, :, lanes] = packed
+            for i, (dy, dx) in enumerate(places):
+                y, x = plane_place()
+                column = lax.rem(y + dy, 2) * 4 + lax.rem(x + dx, 4)
+                for r in range(ROW_BLOCKS):
+                    if i < done:
+                        message = earlier_ref[i * ROW_BLOCKS + r, :, lanes]
+                    else:
+                        message = packed[(i - done) * ROW_BLOCKS + r]
+                    main_ref[r * COL_BLOCKS + column, :, lanes] = message
         for k, out_ref in enumerate(out_refs):
             to = lax.rem(z + k, ROW_BLOCKS)
             for g in range(members // ROW_BLOCKS):
                 out_ref[g] = part_ref[g * ROW_BLOCKS + to]
 
 
-def block_product(messages, blocks):
+def block_product(messages, blocks, earlier=(), places=()):
     tiles = blocks.shape[2] // TILE
-    lanes = (tiles + 1) * TILE + REST
+    lanes = tiles * TILE + REST
     counts = tuple(rows.shape[0] for rows in messages)
     members = sum(counts)
     return pl.pallas_call(
-        functools.partial(product_kernel, tiles, counts),
-        out_shape=[jax.ShapeDtypeStruct((members // ROW_BLOCKS, CTOK, lanes), jnp.bfloat16)] * ROW_BLOCKS,
+        functools.partial(product_kernel, tiles, counts, places),
+        out_shape=[jax.ShapeDtypeStruct((members // ROW_BLOCKS, CTOK, lanes), jnp.bfloat16)] * ROW_BLOCKS
+        + [jax.ShapeDtypeStruct((MEMBERS if places else members, CTOK, TILE), jnp.bfloat16)],
         grid=(tiles,),
-        in_specs=[VMEM] * len(counts) + [HBM],
-        out_specs=[VMEM] * ROW_BLOCKS,
+        in_specs=[VMEM] * (len(counts) + len(earlier)) + [HBM],
+        out_specs=[VMEM] * (1 + ROW_BLOCKS),
         scratch_shapes=[
             pltpu.VMEM((members * (CTOK + STEPS), FEATURES), jnp.bfloat16),
             pltpu.VMEM((TILE // 128, members * CTOK, 128), jnp.float32),
@@ -196,7 +211,7 @@
         compiler_params=kernel_params(),
         cost_estimate=cost(2 * members * (CTOK + STEPS) * FEATURES * tiles * TILE, 12 * 10**6),
         name="block_product",
-    )(*messages, in_hbm(blocks))
+    )(*messages, *earlier, in_hbm(blocks))
 
 
 def sum_kernel(bias_ref, *refs):
@@ -215,7 +230,6 @@
         at = QKV - cols + j * TILE
         return bias_ref[:, at : at + TILE] * last
 
-    main_bias = jnp.concatenate([value_bias(j) for j in range(tiles)], axis=0)
     for g, out_ref in enumerate(out_refs):
 
         def total(lane):
@@ -235,17 +249,6 @@
         for i in range(kept):
             low = jnp.where(late, lows[i + tiles - kept], lows[i])
             out_ref[:, cols + i * TILE : cols + (i + 1) * TILE] = low.astype(jnp.bfloat16)
-        main = total(cols + REST)
-        pad = jnp.zeros((tiles - kept, TILE), jnp.float32)
-        pieces = []
-        for s in range(STEPS):
-            low = main[s * 8 + tiles : (s + 1) * 8]
-            both = jnp.where(late, jnp.concatenate([pad, low], axis=0), jnp.concatenate([low, pad], axis=0))
-            value = main[s * 8 : s * 8 + tiles] + both + main_bias
-            high = value.astype(jnp.bfloat16).astype(jnp.float32)
-            low = value - high
-            pieces += [high, jnp.where(late, low[tiles - kept :], low[:kept])]
-        out_ref[:, cols + REST :] = jnp.concatenate(pieces, axis=0).astype(jnp.bfloat16)
 
 
 def sum_parts(bias, parts):
@@ -295,10 +298,7 @@
     cols = QKV // COL_BLOCKS
     for c in range(COL_BLOCKS):
         first = 2 if c == 6 else 0
-        if main:
-            total = parts_ref[c, :, cols + REST :].astype(jnp.float32)
-        else:
-            total = parts_ref[c, :, : cols + REST].astype(jnp.float32)
+        total = summed_block(parts_ref, c, slice(0, TILE)) if main else parts_ref[c].astype(jnp.float32)
         for j in range(cols // TILE):
             lanes = slice(c * cols + j * TILE, c * cols + (j + 1) * TILE)
             rest = j - first
@@ -341,13 +341,13 @@
 KV_WIDTH = KVH * HD
 
 
-def attend_main_kernel(len_ref, bias_ref, cos_ref, sin_ref, cache_ref, *refs):
-    part_refs = refs[:COL_BLOCKS]
-    out_ref, kv_ref, qkv_ref, piece_ref, parts_ref = refs[COL_BLOCKS:]
+def attend_main_kernel(
+    len_ref, bias_ref, cos_ref, sin_ref, cache_ref, parts_ref, out_ref, kv_ref, qkv_ref, piece_ref
+):
     rows = qkv_ref.shape[0]
-    load_parts(part_refs, parts_ref)
     qkv_ref[...] = jnp.zeros(qkv_ref.shape, jnp.float32)
     load_qkv(True, parts_ref, qkv_ref)
+    qkv_ref[:, D + KV_WIDTH :] = qkv_ref[:, D + KV_WIDTH :] + bias_ref[:, D + KV_WIDTH :]
     plain, rotated = head_readers(qkv_ref, bias_ref, cos_ref, sin_ref)
     seen = lax.broadcasted_iota(jnp.int32, (1, cache_ref.shape[0]), 1) < len_ref[0]
     row = lax.broadcasted_iota(jnp.int32, (rows, 128), 0)
@@ -384,17 +384,16 @@
             jax.ShapeDtypeStruct((32, 16, TILE), jnp.bfloat16),
             jax.ShapeDtypeStruct((8, 2 * KV_WIDTH), jnp.float32),
         ),
-        in_specs=[SMEM] + [VMEM] * (4 + COL_BLOCKS),
+        in_specs=[SMEM] + [VMEM] * 5,
         out_specs=(whole((32, 16, TILE)), whole((8, 2 * KV_WIDTH))),
         scratch_shapes=[
             pltpu.VMEM((8, QKV), jnp.float32),
             pltpu.VMEM((ROW_BLOCKS, 16, TILE), jnp.float32),
-            pltpu.VMEM((COL_BLOCKS,) + parts[0].shape, jnp.bfloat16),
         ],
         compiler_params=kernel_params(),
         cost_estimate=cost(2 * 10**8, 6 * 10**6),
         name="attend_main",
-    )(prefix_len, bias, cosine, sine, cache, *parts)
+    )(prefix_len, bias, cosine, sine, cache, parts)
 
 
 def attend_cont_kernel(len_ref, bound_ref, bias_ref, cos_ref, sin_ref, cache_ref, kv_ref, *refs):
@@ -605,13 +604,14 @@
         before = from_side(mine, 0, 3)
         far += [from_side(before[:half], 0, 3), from_side(after[half:], 0, 1)]
         sides.append([after, before])
+    *first, main = block_product([near, over] + sides[0], blocks)
+    *second, main = block_product(sides[1] + far, blocks, (main,), HOMES)
     received = []
-    for homes, messages in ((FIRST_HOMES, [near, over] + sides[0]), (SECOND_HOMES, sides[1] + far)):
-        parts = block_product(messages, blocks)
+    for homes, parts in ((FIRST_HOMES, first), (SECOND_HOMES, second)):
         parts = [parts[0]] + [from_along(parts[k], -k) for k in range(1, ROW_BLOCKS)]
         for (dy, dx), summed in zip(homes, sum_parts(bias, parts)):
             received.append(from_side(summed, -dy, -dx) if dy or dx else summed)
-    return received
+    return received, exchange(main)
 
 
 def on_device(
@@ -626,11 +626,10 @@
     main_tables = rope_tables(prefix_len + step[:8])
     cont_tables = rope_tables(prefix_len + boundary + step)
     read = readout(value_head.reshape(COL_BLOCKS, D // COL_BLOCKS), w_out)
-    parts = project(norm_rows(main, cont, rms_gain[None, :]), w_qkv, bias)
-    mixed, main_kv = attend_main(prefix_len, bias, *main_tables, cache, parts)
+    parts, main_parts = project(norm_rows(main, cont, rms_gain[None, :]), w_qkv, bias)
+    mixed, main_kv = attend_main(prefix_len, bias, *main_tables, cache, main_parts)
     mixed = exchange(mixed)
     cont_mixed = attend_cont(prefix_len, boundary, bias, *cont_tables, cache, main_kv, *parts)
-    mixed, cont_mixed, read = lax.optimization_barrier((mixed, cont_mixed, read))
     parts = exchange(out_product(mixed, read, w_out))
     main_out, score = finish(parts, main, cont, head, cont_mixed)
     return main_out[None], score[0, :1]

time: 116 us -> 122 us (1.052)
  blocking collectives: 28.1 us -> 12.2 us
  starting transfers between devices: 40.6 us -> 54.1 us
  waiting for transfers between devices: 20.6 us -> 24 us
  Pallas kernels: 23.6 us -> 25.9 us
  local copies, waits for them, and re-layouts: 0.6 us -> 2.73 us
    all_to_all x1 -> x0, blocking collectives: 15.9 us -> none  [exchange(): return lax.all_to_all(rows, 'tp', split_axis=0, concat_axis=0, tiled=True)]
    all_to_all x1 -> x3, waiting for transfers between devices: 2.28 us -> 9.04 us  [exchange(): return lax.all_to_all(rows, 'tp', split_axis=0, concat_axis=0, tiled=True)]
    all_to_all x1 -> x3, starting transfers between devices: 7.3 us -> 13.4 us  [exchange(): return lax.all_to_all(rows, 'tp', split_axis=0, concat_axis=0, tiled=True)]
    ppermute x6, waiting for transfers between devices: 7.79 us -> 2.12 us  [from_along(): return lax.ppermute(rows, 'tp', route)]
    ppermute x16, starting transfers between devices: 24.2 us -> 28.7 us  [from_side(): return lax.ppermute(rows, 'tp', route)]
    ppermute x6, starting transfers between devices: 9.01 us -> 12 us  [from_along(): return lax.ppermute(rows, 'tp', route)]
    ppermute x16, waiting for transfers between devices: 10.5 us -> 12.9 us  [from_side(): return lax.ppermute(rows, 'tp', route)]
    unnamed x10 -> x18, local copies, waits for them, and re-layouts: 0.03 us -> 2.16 us
  transfers between devices with their start and end apart: 23 -> 25, of which waited for: 8 -> 9; matrix products, arithmetic and copies ran while one was open for 0% -> 0% of each run, Pallas kernels for 13% -> 12%
where the time goes in v6:
time: 122 us
  starting transfers between devices  54.1 us (44%)
  Pallas kernels  25.9 us (21%)
  waiting for transfers between devices  24 us (20%)
  blocking collectives  12.2 us (10%)
  local copies, waits for them, and re-layouts  2.73 us (2%)
  between operations  2.21 us (2%)
    ppermute x16, starting transfers between devices, from_side(): return lax.ppermute(rows, 'tp', route)  28.7 us
    all_to_all x3, starting transfers between devices, exchange(): return lax.all_to_all(rows, 'tp', split_axis=0, concat_axis=0, tiled=True)  13.4 us
    ppermute x16, waiting for transfers between devices, from_side(): return lax.ppermute(rows, 'tp', route)  12.9 us
    all_to_all x1, blocking collectives, project(): lax.all_to_all(rows, 'tp', split_axis=0, concat_axis=0, tiled=True, axis_...  12.2 us
    ppermute x6, starting transfers between devices, from_along(): return lax.ppermute(rows, 'tp', route)  12 us
    pallas_call x2, Pallas kernels, block_product(): pl.pallas_call(functools.partial(product_kernel, tiles, counts, places),...  9.59 us
    all_to_all x3, waiting for transfers between devices, exchange(): return lax.all_to_all(rows, 'tp', split_axis=0, concat_axis=0, tiled=True)  9.04 us
    pallas_call x1, Pallas kernels, attend_main(): pl.pallas_call(attend_main_kernel, out_shape=(jax.ShapeDtypeStruct((32, 1...  3.71 us
  transfers between devices with their start and end apart: 25, of which 9 were waited for; matrix products, arithmetic and copies ran while one was open for 0% of the time, Pallas kernels for 12%

profile of v6, /device:TPU:0, one launch (start us, length us, event | category | flops | bytes accessed | tf_op | source)
XLA Modules:
  0.0 121.6 jit_solution(15788572370467376139)
XLA Ops:
  2.0 12.2 %all_to_all.20.refs_0_ = bf16[4,16,2304]{2,1,0:T(8,128)(2,1)S(1)} all-to-all(bf16[4,16,2304]{2,1,0:T(8,128)(2,1)S(1)} %norm_rows.1), channel_id=1, replica_groups={{0,8,16,24},{1,9,17,25},{2,10,18,26},{3,11,19,27},{4,12,20,28},{5,13,21..., dimensions={0} | all-to-all | bytes 589824 | tf_op jit(solution)/shard_map/all_to_all | solution.py:598
  16.5 2.8 %collective-permute-start.5 = (bf16[4,16,2304]{2,1,0:T(8,128)(2,1)S(1)}, bf16[4,16,2304]{2,1,0:T(8,128)(2,1)S(1)}, u32[]{:S(2)}, u32[]{:S(2)}) collective-permute-start(bf16[4,16,2304]{2,1,0:T(8,128)(2,1)S(1)} %all_to_all.20.refs_0_), channel_id=1, source_target_pairs={{1,0},{2,1},{3,2},{0,3},{5,4},{6,5},{7,6},{4,7},{9,8},{10,9},{11,1... | collective-permute-start | bytes 884744 | tf_op jit(solution)/shard_map/ppermute | solution.py:584
  19.3 2.2 %collective-permute-done.refs_1_ = bf16[4,16,2304]{2,1,0:T(8,128)(2,1)S(1)} collective-permute-done((bf16[4,16,2304]{2,1,0:T(8,128)(2,1)S(1)}, bf16[4,16,2304]{2,1,0:T(8,128)(2,1)S(1)}, u32[]{:S(2)}, u32[]{:S(2)}) %collective-permute-start) | collective-permute-done | bytes 294944 | tf_op jit(solution)/shard_map/ppermute | solution.py:584
  25.5 3.8 %collective-permute-start.6 = (bf16[2,16,2304]{2,1,0:T(8,128)(2,1)S(1)}, bf16[2,16,2304]{2,1,0:T(8,128)(2,1)S(1)}, u32[]{:S(2)}, u32[]{:S(2)}) collective-permute-start(bf16[2,16,2304]{2,1,0:T(8,128)(2,1)S(1)} %slice.25), channel_id=1, source_target_pairs={{1,0},{2,1},{3,2},{0,3},{5,4},{6,5},{7,6},{4,7},{9,8},{10,9},{11,1... | collective-permute-start | bytes 442376 | tf_op jit(solution)/shard_map/ppermute | solution.py:584
  30.6 5.3 %collective-permute-done.2.refs_1_ = bf16[4,16,2304]{2,1,0:T(8,128)(2,1)S(1)} collective-permute-done((bf16[4,16,2304]{2,1,0:T(8,128)(2,1)S(1)}, bf16[4,16,2304]{2,1,0:T(8,128)(2,1)S(1)}, u32[]{:S(2)}, u32[]{:S(2)}) %collective-permute-start.2) | collective-permute-done | bytes 294944 | tf_op jit(solution)/shard_map/ppermute | solution.py:584
  36.0 3.3 %collective-permute-start.8 = (bf16[2,16,2304]{2,1,0:T(8,128)(2,1)S(1)}, bf16[2,16,2304]{2,1,0:T(8,128)(2,1)S(1)}, u32[]{:S(2)}, u32[]{:S(2)}) collective-permute-start(bf16[2,16,2304]{2,1,0:T(8,128)(2,1)S(1)} %slice.27), channel_id=1, source_target_pairs={{1,0},{2,1},{3,2},{0,3},{5,4},{6,5},{7,6},{4,7},{9,8},{10,9},{11,1... | collective-permute-start | bytes 442376 | tf_op jit(solution)/shard_map/ppermute | solution.py:584
  39.3 4.9 %block_product.2 = (bf16[4,16,2048]{2,1,0:T(8,128)(2,1)S(1)}, bf16[4,16,2048]{2,1,0:T(8,128)(2,1)}, bf16[4,16,2048]{2,1,0:T(8,128)(2,1)}, bf16[4,16,2048]{2,1,0:T(8,128)(2,1)S(1)}, bf16[16,16,256]{2,1,0:T(8,128)(2,1)S(1)}) custom-call(bf16[4,16,2304]{2,1,0:T(8,128)(2,1)S(1)} %all_to_all.20.refs_0_, bf16[4,16,2304]{2,1,0:T(8,128)(2,1)S(1)} %collective-permute-done.refs_1_, ...), custom_call_target="tpu_custom_call" | custom-call | flops 1509949440 | bytes 12000000 | tf_op jit(solution)/shard_map/block_product/pallas_call | solution.py:197
  44.2 4.7 %block_product.3 = (bf16[4,16,2048]{2,1,0:T(8,128)(2,1)S(1)}, bf16[4,16,2048]{2,1,0:T(8,128)(2,1)S(1)}, bf16[4,16,2048]{2,1,0:T(8,128)(2,1)S(1)}, bf16[4,16,2048]{2,1,0:T(8,128)(2,1)S(1)}, bf16[32,16,256]{2,1,0:T(8,128)(2,1)}) custom-call(bf16[4,16,2304]{2,1,0:T(8,128)(2,1)S(1)} %collective-permute-done.1.refs_0_, ...), custom_call_target="tpu_custom_call" | custom-call | flops 1509949440 | bytes 12000000 | tf_op jit(solution)/shard_map/block_product/pallas_call | solution.py:197
  51.1 3.9 %all-to-all-start.1 = ((bf16[32,16,256]{2,1,0:T(8,128)(2,1)}), bf16[32,16,256]{2,1,0:T(8,128)(2,1)S(1)}, u32[]{:S(2)}, u32[]{:S(2)}) async-start(bf16[32,16,256]{2,1,0:T(8,128)(2,1)} %get-tuple-element.25), calls=%async_computation.1 | async-start | bytes 524288 | tf_op jit(solution)/shard_map/all_to_all | solution.py:573
  55.2 9.0 %all-to-all-done.1.parts_ref = bf16[32,16,256]{2,1,0:T(8,128)(2,1)S(1)} async-done(((bf16[32,16,256]{2,1,0:T(8,128)(2,1)}), bf16[32,16,256]{2,1,0:T(8,128)(2,1)S(1)}, u32[]{:S(2)}, u32[]{:S(2)}) %all-to-all-start.1) | async-done | bytes 262176 | tf_op jit(solution)/shard_map/all_to_all | solution.py:573
  64.2 3.7 %attend_main.1 = (bf16[32,16,256]{2,1,0:T(8,128)(2,1)}, f32[8,2048]{1,0:T(8,128)S(1)}) custom-call(s32[1]{0:T(128)} %copy.12.len_ref, f32[1,10240]{1,0:T(1,128)S(1)} %bitcast.15, f32[8,128]{1,0:T(8,128)S(1)} %get-tuple-element.52.cos_ref, f32[8,128]{1,0:T(8,128)S(1)} %get-tuple-element.53.sin_ref, bf16[256,2048]{1,0:T(8,128)(2,1)S(1)} %bitcast.11, ...), custom_call_target="tpu_custom_call" | custom-call | flops 200000000 | bytes 6000000 | tf_op jit(solution)/shard_map/attend_main/pallas_call | solution.py:381
  67.9 3.9 %all-to-all-start.2 = ((bf16[32,16,256]{2,1,0:T(8,128)(2,1)}), bf16[32,16,256]{2,1,0:T(8,128)(2,1)S(1)}, u32[]{:S(2)}, u32[]{:S(2)}) async-start(bf16[32,16,256]{2,1,0:T(8,128)(2,1)} %get-tuple-element.26), calls=%async_computation.2 | async-start | bytes 524288 | tf_op jit(solution)/shard_map/all_to_all | solution.py:573
  71.8 1.8 %collective-permute-start.9 = (bf16[4,16,2048]{2,1,0:T(8,128)(2,1)}, bf16[4,16,2048]{2,1,0:T(8,128)(2,1)S(1)}, u32[]{:S(2)}, u32[]{:S(2)}) collective-permute-start(bf16[4,16,2048]{2,1,0:T(8,128)(2,1)} %get-tuple-element.29), channel_id=1, source_target_pairs={{24,0},{25,1},{26,2},{27,3},{28,4},{29,5},{30,6},{31,7},{0,8},{1,9... | collective-permute-start | bytes 786440 | tf_op jit(solution)/shard_map/ppermute | solution.py:589
  73.6 2.7 %collective-permute-start.10 = (bf16[4,16,2048]{2,1,0:T(8,128)(2,1)}, bf16[4,16,2048]{2,1,0:T(8,128)(2,1)S(1)}, u32[]{:S(2)}, u32[]{:S(2)}) collective-permute-start(bf16[4,16,2048]{2,1,0:T(8,128)(2,1)} %get-tuple-element.30), channel_id=1, source_target_pairs={{16,0},{17,1},{18,2},{19,3},{20,4},{21,5},{22,6},{23,7},{24,8},{25... | collective-permute-start | bytes 786440 | tf_op jit(solution)/shard_map/ppermute | solution.py:589
  77.8 3.4 %readout.1.read_ref = f32[1,2048]{1,0:T(1,128)S(1)} custom-call(f32[8,1024]{1,0:T(8,128)S(1)} %reshape.34.head_ref, bf16[1,2048,1024]{2,1,0:T(8,128)(2,1)} %w_hbm.3), custom_call_target="tpu_custom_call" | custom-call | flops 200000000 | bytes 5000000 | tf_op jit(solution)/shard_map/readout/pallas_call | solution.py:458
  81.3 3.5 %out_product.1 = f32[32,16,256]{2,1,0:T(8,128)} custom-call(bf16[32,16,256]{2,1,0:T(8,128)(2,1)S(1)} %all-to-all-done.2.x_ref, f32[1,2048]{1,0:T(1,128)S(1)} %readout.1.read_ref, bf16[1,2048,1024]{2,1,0:T(8,128)(2,1)} %w_hbm.3), custom_call_target="tpu_custom_call" | custom-call | flops 300000000 | bytes 5000000 | tf_op jit(solution)/shard_map/out_product/pallas_call | solution.py:504
  84.7 5.6 %all-to-all-start.3 = ((f32[32,16,256]{2,1,0:T(8,128)}), f32[32,16,256]{2,1,0:T(8,128)S(1)}, u32[]{:S(2)}, u32[]{:S(2)}) async-start(f32[32,16,256]{2,1,0:T(8,128)} %out_product.1), calls=%async_computation.3 | async-start | bytes 1048576 | tf_op jit(solution)/shard_map/all_to_all | solution.py:573
  91.0 1.9 %collective-permute-start.15 = (bf16[4,16,2048]{2,1,0:T(8,128)(2,1)}, bf16[4,16,2048]{2,1,0:T(8,128)(2,1)S(1)}, u32[]{:S(2)}, u32[]{:S(2)}) collective-permute-start(bf16[4,16,2048]{2,1,0:T(8,128)(2,1)} %copy-done.7), channel_id=1, source_target_pairs={{24,0},{25,1},{26,2},{27,3},{28,4},{29,5},{30,6},{31,7},{0,8},{1,9... | collective-permute-start | bytes 786440 | tf_op jit(solution)/shard_map/ppermute | solution.py:589
  92.9 2.7 %collective-permute-start.16 = (bf16[4,16,2048]{2,1,0:T(8,128)(2,1)}, bf16[4,16,2048]{2,1,0:T(8,128)(2,1)S(1)}, u32[]{:S(2)}, u32[]{:S(2)}) collective-permute-start(bf16[4,16,2048]{2,1,0:T(8,128)(2,1)} %copy-done.6), channel_id=1, source_target_pairs={{16,0},{17,1},{18,2},{19,3},{20,4},{21,5},{22,6},{23,7},{24,8},{25... | collective-permute-start | bytes 786440 | tf_op jit(solution)/shard_map/ppermute | solution.py:589
  101.2 2.4 %collective-permute-start.14 = (bf16[16,2048]{1,0:T(8,128)(2,1)S(1)}, bf16[16,2048]{1,0:T(8,128)(2,1)S(1)}, u32[]{:S(2)}, u32[]{:S(2)}) collective-permute-start(bf16[16,2048]{1,0:T(8,128)(2,1)S(1)} %get-tuple-element.35), channel_id=1, source_target_pairs={{1,0},{2,1},{3,2},{0,3},{5,4},{6,5},{7,6},{4,7},{9,8},{10,9},{11,1... | collective-permute-start | bytes 196616 | tf_op jit(solution)/shard_map/ppermute | solution.py:584
  106.5 2.8 %collective-permute-start.19 = (bf16[16,2048]{1,0:T(8,128)(2,1)S(1)}, bf16[16,2048]{1,0:T(8,128)(2,1)S(1)}, u32[]{:S(2)}, u32[]{:S(2)}) collective-permute-start(bf16[16,2048]{1,0:T(8,128)(2,1)S(1)} %get-tuple-element.41), channel_id=1, source_target_pairs={{5,0},{6,1},{7,2},{4,3},{1,4},{2,5},{3,6},{0,7},{13,8},{14,9},{15,... | collective-permute-start | bytes 196616 | tf_op jit(solution)/shard_map/ppermute | solution.py:584
  110.4 3.2 %collective-permute-start.21 = (bf16[16,2048]{1,0:T(8,128)(2,1)S(1)}, bf16[16,2048]{1,0:T(8,128)(2,1)S(1)}, u32[]{:S(2)}, u32[]{:S(2)}) collective-permute-start(bf16[16,2048]{1,0:T(8,128)(2,1)S(1)} %get-tuple-element.43), channel_id=1, source_target_pairs={{6,0},{7,1},{4,2},{5,3},{2,4},{3,5},{0,6},{1,7},{14,8},{15,9},{12,... | collective-permute-start | bytes 196616 | tf_op jit(solution)/shard_map/ppermute | solution.py:584
  115.1 2.0 %collective-permute-done.21.refs_7_ = bf16[16,2048]{1,0:T(8,128)(2,1)S(1)} collective-permute-done((bf16[16,2048]{1,0:T(8,128)(2,1)S(1)}, bf16[16,2048]{1,0:T(8,128)(2,1)S(1)}, u32[]{:S(2)}, u32[]{:S(2)}) %collective-permute-start.21) | collective-permute-done | bytes 65568 | tf_op jit(solution)/shard_map/ppermute | solution.py:584
  117.1 3.0 %attend_cont.1.mixed_ref = bf16[16,8192]{1,0:T(8,128)(2,1)S(1)} custom-call(s32[1]{0:T(128)} %copy.12.len_ref, s32[1]{0:T(128)S(6)} %copy.13.bound_ref, f32[1,10240]{1,0:T(1,128)S(1)} %bitcast.18, f32[16,128]{1,0:T(8,128)S(1)} %get-tuple-element.54.cos_ref, f32[16,128]{1,0:T(8,128)S(1)} %get-tuple-element.55.sin_ref, bf16[256,2048]{1,0:T(8,128)(2,1)S(1)} %bitcast.12, ...), custom_call_target="tpu_custom_call" | custom-call | flops 400000000 | bytes 8000000 | tf_op jit(solution)/shard_map/attend_cont/pallas_call | solution.py:427
  (69 shorter events, 24.7 us)
Async XLA Ops:
  14.2 7.3 %collective-permute-start = (bf16[4,16,2304]{2,1,0:T(8,128)(2,1)S(1)}, bf16[4,16,2304]{2,1,0:T(8,128)(2,1)S(1)}, u32[]{:S(2)}, u32[]{:S(2)}) collective-permute-start(bf16[4,16,2304]{2,1,0:T(8,128)(2,1)S(1)} %all_to_all.20.refs_0_), channel_id=1, source_target_pairs={{4,0},{5,1},{6,2},{7,3},{0,4},{1,5},{2,6},{3,7},{12,8},{13,9},{14,... | collective-permute-start | bytes 884744 | tf_op jit(solution)/shard_map/ppermute | solution.py:584
  16.5 9.1 %collective-permute-start.5 = (bf16[4,16,2304]{2,1,0:T(8,128)(2,1)S(1)}, bf16[4,16,2304]{2,1,0:T(8,128)(2,1)S(1)}, u32[]{:S(2)}, u32[]{:S(2)}) collective-permute-start(bf16[4,16,2304]{2,1,0:T(8,128)(2,1)S(1)} %all_to_all.20.refs_0_), channel_id=1, source_target_pairs={{1,0},{2,1},{3,2},{0,3},{5,4},{6,5},{7,6},{4,7},{9,8},{10,9},{11,1... | collective-permute-start | bytes 884744 | tf_op jit(solution)/shard_map/ppermute | solution.py:584
  19.3 11.2 %collective-permute-start.3 = (bf16[4,16,2304]{2,1,0:T(8,128)(2,1)S(1)}, bf16[4,16,2304]{2,1,0:T(8,128)(2,1)S(1)}, u32[]{:S(2)}, u32[]{:S(2)}) collective-permute-start(bf16[4,16,2304]{2,1,0:T(8,128)(2,1)S(1)} %all_to_all.20.refs_0_), channel_id=1, source_target_pairs={{3,0},{0,1},{1,2},{2,3},{7,4},{4,5},{5,6},{6,7},{11,8},{8,9},{9,10... | collective-permute-start | bytes 884744 | tf_op jit(solution)/shard_map/ppermute | solution.py:584
  21.5 14.4 %collective-permute-start.2 = (bf16[4,16,2304]{2,1,0:T(8,128)(2,1)S(1)}, bf16[4,16,2304]{2,1,0:T(8,128)(2,1)S(1)}, u32[]{:S(2)}, u32[]{:S(2)}) collective-permute-start(bf16[4,16,2304]{2,1,0:T(8,128)(2,1)S(1)} %collective-permute-done.refs_1_), channel_id=1, source_target_pairs={{3,0},{0,1},{1,2},{2,3},{7,4},{4,5},{5,6},{6,7},{11,8},{8,9},{9,10... | collective-permute-start | bytes 884744 | tf_op jit(solution)/shard_map/ppermute | solution.py:584
  23.0 13.0 %collective-permute-start.1 = (bf16[4,16,2304]{2,1,0:T(8,128)(2,1)S(1)}, bf16[4,16,2304]{2,1,0:T(8,128)(2,1)S(1)}, u32[]{:S(2)}, u32[]{:S(2)}) collective-permute-start(bf16[4,16,2304]{2,1,0:T(8,128)(2,1)S(1)} %collective-permute-done.refs_1_), channel_id=1, source_target_pairs={{1,0},{2,1},{3,2},{0,3},{5,4},{6,5},{7,6},{4,7},{9,8},{10,9},{11,1... | collective-permute-start | bytes 884744 | tf_op jit(solution)/shard_map/ppermute | solution.py:584
  25.5 18.7 %collective-permute-start.6 = (bf16[2,16,2304]{2,1,0:T(8,128)(2,1)S(1)}, bf16[2,16,2304]{2,1,0:T(8,128)(2,1)S(1)}, u32[]{:S(2)}, u32[]{:S(2)}) collective-permute-start(bf16[2,16,2304]{2,1,0:T(8,128)(2,1)S(1)} %slice.25), channel_id=1, source_target_pairs={{1,0},{2,1},{3,2},{0,3},{5,4},{6,5},{7,6},{4,7},{9,8},{10,9},{11,1... | collective-permute-start | bytes 442376 | tf_op jit(solution)/shard_map/ppermute | solution.py:584
  30.5 13.7 %collective-permute-start.4 = (bf16[2,16,2304]{2,1,0:T(8,128)(2,1)S(1)}, bf16[2,16,2304]{2,1,0:T(8,128)(2,1)S(1)}, u32[]{:S(2)}, u32[]{:S(2)}) collective-permute-start(bf16[2,16,2304]{2,1,0:T(8,128)(2,1)S(1)} %slice.24), channel_id=1, source_target_pairs={{3,0},{0,1},{1,2},{2,3},{7,4},{4,5},{5,6},{6,7},{11,8},{8,9},{9,10... | collective-permute-start | bytes 442376 | tf_op jit(solution)/shard_map/ppermute | solution.py:584
  35.9 8.3 %collective-permute-start.7 = (bf16[2,16,2304]{2,1,0:T(8,128)(2,1)S(1)}, bf16[2,16,2304]{2,1,0:T(8,128)(2,1)S(1)}, u32[]{:S(2)}, u32[]{:S(2)}) collective-permute-start(bf16[2,16,2304]{2,1,0:T(8,128)(2,1)S(1)} %slice.26), channel_id=1, source_target_pairs={{3,0},{0,1},{1,2},{2,3},{7,4},{4,5},{5,6},{6,7},{11,8},{8,9},{9,10... | collective-permute-start | bytes 442376 | tf_op jit(solution)/shard_map/ppermute | solution.py:584
  36.0 8.2 %collective-permute-start.8 = (bf16[2,16,2304]{2,1,0:T(8,128)(2,1)S(1)}, bf16[2,16,2304]{2,1,0:T(8,128)(2,1)S(1)}, u32[]{:S(2)}, u32[]{:S(2)}) collective-permute-start(bf16[2,16,2304]{2,1,0:T(8,128)(2,1)S(1)} %slice.27), channel_id=1, source_target_pairs={{1,0},{2,1},{3,2},{0,3},{5,4},{6,5},{7,6},{4,7},{9,8},{10,9},{11,1... | collective-permute-start | bytes 442376 | tf_op jit(solution)/shard_map/ppermute | solution.py:584
  51.1 13.1 %all-to-all-start.1 = ((bf16[32,16,256]{2,1,0:T(8,128)(2,1)}), bf16[32,16,256]{2,1,0:T(8,128)(2,1)S(1)}, u32[]{:S(2)}, u32[]{:S(2)}) async-start(bf16[32,16,256]{2,1,0:T(8,128)(2,1)} %get-tuple-element.25), calls=%async_computation.1 | async-start | bytes 524288 | tf_op jit(solution)/shard_map/all_to_all | solution.py:573
  67.9 13.3 %all-to-all-start.2 = ((bf16[32,16,256]{2,1,0:T(8,128)(2,1)}), bf16[32,16,256]{2,1,0:T(8,128)(2,1)S(1)}, u32[]{:S(2)}, u32[]{:S(2)}) async-start(bf16[32,16,256]{2,1,0:T(8,128)(2,1)} %get-tuple-element.26), calls=%async_computation.2 | async-start | bytes 524288 | tf_op jit(solution)/shard_map/all_to_all | solution.py:573
  71.8 23.8 %collective-permute-start.9 = (bf16[4,16,2048]{2,1,0:T(8,128)(2,1)}, bf16[4,16,2048]{2,1,0:T(8,128)(2,1)S(1)}, u32[]{:S(2)}, u32[]{:S(2)}) collective-permute-start(bf16[4,16,2048]{2,1,0:T(8,128)(2,1)} %get-tuple-element.29), channel_id=1, source_target_pairs={{24,0},{25,1},{26,2},{27,3},{28,4},{29,5},{30,6},{31,7},{0,8},{1,9... | collective-permute-start | bytes 786440 | tf_op jit(solution)/shard_map/ppermute | solution.py:589
  73.6 23.4 %collective-permute-start.10 = (bf16[4,16,2048]{2,1,0:T(8,128)(2,1)}, bf16[4,16,2048]{2,1,0:T(8,128)(2,1)S(1)}, u32[]{:S(2)}, u32[]{:S(2)}) collective-permute-start(bf16[4,16,2048]{2,1,0:T(8,128)(2,1)} %get-tuple-element.30), channel_id=1, source_target_pairs={{16,0},{17,1},{18,2},{19,3},{20,4},{21,5},{22,6},{23,7},{24,8},{25... | collective-permute-start | bytes 786440 | tf_op jit(solution)/shard_map/ppermute | solution.py:589
  76.4 20.7 %collective-permute-start.11 = (bf16[4,16,2048]{2,1,0:T(8,128)(2,1)}, bf16[4,16,2048]{2,1,0:T(8,128)(2,1)S(1)}, u32[]{:S(2)}, u32[]{:S(2)}) collective-permute-start(bf16[4,16,2048]{2,1,0:T(8,128)(2,1)} %copy-done.8), channel_id=1, source_target_pairs={{8,0},{9,1},{10,2},{11,3},{12,4},{13,5},{14,6},{15,7},{16,8},{17,9... | collective-permute-start | bytes 786440 | tf_op jit(solution)/shard_map/ppermute | solution.py:589
  84.7 35.4 %all-to-all-start.3 = ((f32[32,16,256]{2,1,0:T(8,128)}), f32[32,16,256]{2,1,0:T(8,128)S(1)}, u32[]{:S(2)}, u32[]{:S(2)}) async-start(f32[32,16,256]{2,1,0:T(8,128)} %out_product.1), calls=%async_computation.3 | async-start | bytes 1048576 | tf_op jit(solution)/shard_map/all_to_all | solution.py:573
  91.0 10.2 %collective-permute-start.15 = (bf16[4,16,2048]{2,1,0:T(8,128)(2,1)}, bf16[4,16,2048]{2,1,0:T(8,128)(2,1)S(1)}, u32[]{:S(2)}, u32[]{:S(2)}) collective-permute-start(bf16[4,16,2048]{2,1,0:T(8,128)(2,1)} %copy-done.7), channel_id=1, source_target_pairs={{24,0},{25,1},{26,2},{27,3},{28,4},{29,5},{30,6},{31,7},{0,8},{1,9... | collective-permute-start | bytes 786440 | tf_op jit(solution)/shard_map/ppermute | solution.py:589
  92.9 12.0 %collective-permute-start.16 = (bf16[4,16,2048]{2,1,0:T(8,128)(2,1)}, bf16[4,16,2048]{2,1,0:T(8,128)(2,1)S(1)}, u32[]{:S(2)}, u32[]{:S(2)}) collective-permute-start(bf16[4,16,2048]{2,1,0:T(8,128)(2,1)} %copy-done.6), channel_id=1, source_target_pairs={{16,0},{17,1},{18,2},{19,3},{20,4},{21,5},{22,6},{23,7},{24,8},{25... | collective-permute-start | bytes 786440 | tf_op jit(solution)/shard_map/ppermute | solution.py:589
  95.6 9.3 %collective-permute-start.17 = (bf16[4,16,2048]{2,1,0:T(8,128)(2,1)}, bf16[4,16,2048]{2,1,0:T(8,128)(2,1)S(1)}, u32[]{:S(2)}, u32[]{:S(2)}) collective-permute-start(bf16[4,16,2048]{2,1,0:T(8,128)(2,1)} %copy-done.5), channel_id=1, source_target_pairs={{8,0},{9,1},{10,2},{11,3},{12,4},{13,5},{14,6},{15,7},{16,8},{17,9... | collective-permute-start | bytes 786440 | tf_op jit(solution)/shard_map/ppermute | solution.py:589
  97.2 12.1 %collective-permute-start.12 = (bf16[16,2048]{1,0:T(8,128)(2,1)S(1)}, bf16[16,2048]{1,0:T(8,128)(2,1)S(1)}, u32[]{:S(2)}, u32[]{:S(2)}) collective-permute-start(bf16[16,2048]{1,0:T(8,128)(2,1)S(1)} %get-tuple-element.33), channel_id=1, source_target_pairs={{4,0},{5,1},{6,2},{7,3},{0,4},{1,5},{2,6},{3,7},{12,8},{13,9},{14,... | collective-permute-start | bytes 196616 | tf_op jit(solution)/shard_map/ppermute | solution.py:584
  98.8 11.6 %collective-permute-start.13 = (bf16[16,2048]{1,0:T(8,128)(2,1)S(1)}, bf16[16,2048]{1,0:T(8,128)(2,1)S(1)}, u32[]{:S(2)}, u32[]{:S(2)}) collective-permute-start(bf16[16,2048]{1,0:T(8,128)(2,1)S(1)} %get-tuple-element.34), channel_id=1, source_target_pairs={{3,0},{0,1},{1,2},{2,3},{7,4},{4,5},{5,6},{6,7},{11,8},{8,9},{9,10... | collective-permute-start | bytes 196616 | tf_op jit(solution)/shard_map/ppermute | solution.py:584
  101.2 12.4 %collective-permute-start.14 = (bf16[16,2048]{1,0:T(8,128)(2,1)S(1)}, bf16[16,2048]{1,0:T(8,128)(2,1)S(1)}, u32[]{:S(2)}, u32[]{:S(2)}) collective-permute-start(bf16[16,2048]{1,0:T(8,128)(2,1)S(1)} %get-tuple-element.35), channel_id=1, source_target_pairs={{1,0},{2,1},{3,2},{0,3},{5,4},{6,5},{7,6},{4,7},{9,8},{10,9},{11,1... | collective-permute-start | bytes 196616 | tf_op jit(solution)/shard_map/ppermute | solution.py:584
  105.1 8.6 %collective-permute-start.18 = (bf16[16,2048]{1,0:T(8,128)(2,1)S(1)}, bf16[16,2048]{1,0:T(8,128)(2,1)S(1)}, u32[]{:S(2)}, u32[]{:S(2)}) collective-permute-start(bf16[16,2048]{1,0:T(8,128)(2,1)S(1)} %get-tuple-element.40), channel_id=1, source_target_pairs={{7,0},{4,1},{5,2},{6,3},{3,4},{0,5},{1,6},{2,7},{15,8},{12,9},{13,... | collective-permute-start | bytes 196616 | tf_op jit(solution)/shard_map/ppermute | solution.py:584
  106.5 7.2 %collective-permute-start.19 = (bf16[16,2048]{1,0:T(8,128)(2,1)S(1)}, bf16[16,2048]{1,0:T(8,128)(2,1)S(1)}, u32[]{:S(2)}, u32[]{:S(2)}) collective-permute-start(bf16[16,2048]{1,0:T(8,128)(2,1)S(1)} %get-tuple-element.41), channel_id=1, source_target_pairs={{5,0},{6,1},{7,2},{4,3},{1,4},{2,5},{3,6},{0,7},{13,8},{14,9},{15,... | collective-permute-start | bytes 196616 | tf_op jit(solution)/shard_map/ppermute | solution.py:584
  110.4 6.7 %collective-permute-start.21 = (bf16[16,2048]{1,0:T(8,128)(2,1)S(1)}, bf16[16,2048]{1,0:T(8,128)(2,1)S(1)}, u32[]{:S(2)}, u32[]{:S(2)}) collective-permute-start(bf16[16,2048]{1,0:T(8,128)(2,1)S(1)} %get-tuple-element.43), channel_id=1, source_target_pairs={{6,0},{7,1},{4,2},{5,3},{2,4},{3,5},{0,6},{1,7},{14,8},{15,9},{12,... | collective-permute-start | bytes 196616 | tf_op jit(solution)/shard_map/ppermute | solution.py:584
  (10 other events, 174.1 us)

commit v7 on v2

--- a/solution.py
+++ b/solution.py
@@ -14,6 +14,7 @@
 QKV = 10240
 ROW_BLOCKS = 4
 COL_BLOCKS = 8
+MEMBERS = ROW_BLOCKS * COL_BLOCKS
 FEATURES = D // ROW_BLOCKS
 CONTS = 8
 STEPS = 2
@@ -24,7 +25,7 @@
 EPS = 1e-06
 MASKED_SCORE = -1e30
 
-VMEM_LIMIT = 48 * 1024 * 1024
+VMEM_LIMIT = 32 * 1024 * 1024
 VMEM = pl.BlockSpec(memory_space=pltpu.VMEM)
 SMEM = pl.BlockSpec(memory_space=pltpu.SMEM)
 HBM = pl.BlockSpec(memory_space=pltpu.HBM)
@@ -38,11 +39,15 @@
     return pl.CostEstimate(flops=flops, bytes_accessed=moved, transcendentals=0)
 
 
+def in_hbm(array):
+    return pltpu.with_memory_space_constraint(array, pltpu.HBM)
+
+
 def kernel_params():
     return pltpu.CompilerParams(vmem_limit_bytes=VMEM_LIMIT)
 
 
-def norm_kernel(main_hbm, cont_hbm, gain_hbm, out_ref, main_ref, cont_ref, gain_ref, rows_ref, piece_ref, sems):
+def norm_kernel(main_hbm, cont_hbm, gain_hbm, z0_ref, z1_ref, z2_ref, z3_ref, out_ref, main_ref, cont_ref, gain_ref, rows_ref, piece_ref, sems):
     pairs = ((main_hbm, main_ref), (cont_hbm, cont_ref), (gain_hbm, gain_ref))
     copies = [pltpu.make_async_copy(src, dst, sems.at[i]) for i, (src, dst) in enumerate(pairs)]
     for copy in copies:
@@ -66,16 +71,22 @@
     for r in range(ROW_BLOCKS):
         piece = piece_ref[r].astype(jnp.bfloat16)
         for c in range(COL_BLOCKS):
-            out_ref[r * COL_BLOCKS + c, :, :FEATURES] = cont[:, r * FEATURES : (r + 1) * FEATURES]
-            out_ref[r * COL_BLOCKS + c, :, FEATURES:] = piece
+            out_ref[r * COL_BLOCKS + c] = piece
+        ahead = lax.rem(r + ROW_BLOCKS - lax.axis_index("tp") // COL_BLOCKS, ROW_BLOCKS)
+        for k, z_ref in enumerate((z0_ref, z1_ref, z2_ref, z3_ref)):
+
+            @pl.when(ahead == k)
+            def _():
+                z_ref[...] = cont[:, r * FEATURES : (r + 1) * FEATURES]
 
 
 def norm_rows(main, cont, gain):
     return pl.pallas_call(
         norm_kernel,
-        out_shape=jax.ShapeDtypeStruct((32, CTOK, FEATURES + TILE), jnp.bfloat16),
+        out_shape=[jax.ShapeDtypeStruct((CTOK, FEATURES), jnp.bfloat16)] * ROW_BLOCKS
+        + [jax.ShapeDtypeStruct((MEMBERS, CTOK, TILE), jnp.bfloat16)],
         in_specs=[HBM] * 3,
-        out_specs=VMEM,
+        out_specs=[VMEM] * (1 + ROW_BLOCKS),
         scratch_shapes=[
             pltpu.VMEM((STEPS, D), jnp.bfloat16),
             pltpu.VMEM((CONTS, STEPS, D), jnp.bfloat16),
@@ -87,7 +98,7 @@
         compiler_params=kernel_params(),
         cost_estimate=cost(10**6, 4 * 10**6),
         name="norm_rows",
-    )(main, cont, gain)
+    )(in_hbm(main), in_hbm(cont), in_hbm(gain))
 
 
 def weight_tile(n, tiles, w_hbm, w_ref, sems):
@@ -110,69 +121,152 @@
     return jnp.where(block == 6, 2, 0)
 
 
-def product_kernel(tiles, rest, x_ref, w_hbm, out_ref, rows_ref, wide_ref, w_ref, sems):
+def plane_place():
+    column = lax.rem(lax.axis_index("tp"), COL_BLOCKS)
+    return column // 4, lax.rem(column, 4)
+
+
+def product_kernel(tiles, counts, places, *refs):
+    x_refs, refs = refs[: len(counts)], refs[len(counts) :]
+    if places:
+        earlier_ref, w_hbm, out_ref, rows_ref, w_ref, sems, part_ref = refs
+    else:
+        w_hbm, part_ref, rows_ref, w_ref, sems = refs
+    n = pl.program_id(0)
+    members = sum(counts)
+    tile = weight_tile(n, tiles, w_hbm, w_ref, sems)
+
+    @pl.when(n == 0)
+    def _():
+        at = 0
+        for x_ref, size in zip(x_refs, counts):
+            rows_ref[at * CTOK : (at + size) * CTOK, :] = x_ref[...].reshape(size * CTOK, FEATURES)
+            at += size
+
+    tile.wait()
+    prod = jnp.dot(rows_ref[...], w_ref[n], preferred_element_type=jnp.float32)
+    high = prod.astype(jnp.bfloat16)
+    part_ref[:, :, pl.ds(pl.multiple_of(n * TILE, TILE), TILE)] = high.reshape(members, CTOK, TILE)
+    start = rest_tile(lax.rem(lax.axis_index("tp"), COL_BLOCKS))
+
+    @pl.when((n >= start) & (n < start + REST // TILE))
+    def _():
+        low = (prod - high.astype(jnp.float32)).astype(jnp.bfloat16)
+        lane = pl.multiple_of((tiles + n - start) * TILE, TILE)
+        part_ref[:, :, pl.ds(lane, TILE)] = low.reshape(members, CTOK, TILE)
+
+    if places:
+
+        @pl.when(n == tiles - 1)
+        def _():
+            column = lax.rem(lax.axis_index("tp"), COL_BLOCKS)
+            y, x = column // 4, lax.rem(column, 4)
+            done = earlier_ref.shape[0] // ROW_BLOCKS
+            for i, (dy, dx) in enumerate(places):
+                home = lax.rem(y + dy, 2) * 4 + lax.rem(x + dx, 4)
+                for r in range(ROW_BLOCKS):
+                    if i < done:
+                        message = earlier_ref[i * ROW_BLOCKS + r]
+                    else:
+                        message = part_ref[(i - done) * ROW_BLOCKS + r]
+                    out_ref[r * COL_BLOCKS + home] = message
+
+
+def block_product(messages, blocks, earlier=(), places=()):
+    tiles = blocks.shape[2] // TILE
+    counts = tuple(rows.shape[0] for rows in messages)
+    members = sum(counts)
+    part = (members, CTOK, tiles * TILE + REST)
+    out = (MEMBERS,) + part[1:] if places else part
+    return pl.pallas_call(
+        functools.partial(product_kernel, tiles, counts, places),
+        out_shape=jax.ShapeDtypeStruct(out, jnp.bfloat16),
+        grid=(tiles,),
+        in_specs=[VMEM] * (len(counts) + len(earlier)) + [HBM],
+        out_specs=VMEM,
+        scratch_shapes=[
+            pltpu.VMEM((members * CTOK, FEATURES), jnp.bfloat16),
+            pltpu.VMEM((tiles, FEATURES, TILE), jnp.bfloat16),
+            pltpu.SemaphoreType.DMA((tiles,)),
+        ]
+        + ([pltpu.VMEM(part, jnp.bfloat16)] if places else []),
+        compiler_params=kernel_params(),
+        cost_estimate=cost(2 * members * CTOK * FEATURES * tiles * TILE, 12 * 10**6),
+        name="block_product",
+    )(*messages, *earlier, in_hbm(blocks))
+
+
+def main_kernel(tiles, x_ref, w_hbm, out_ref, rows_ref, wide_ref, w_ref, sems):
     n = pl.program_id(0)
     members = x_ref.shape[0]
-    count = members * CTOK
     lines = members * STEPS
     halves = TILE // 128
     tile = weight_tile(n, tiles, w_hbm, w_ref, sems)
 
     @pl.when(n == 0)
     def _():
-        rows_ref[:count, :] = x_ref[:, :, :FEATURES].reshape(count, FEATURES)
-        packed = x_ref[:, :, FEATURES:].reshape(members * 16, TILE).astype(jnp.float32)
+        packed = x_ref[...].reshape(members * CTOK, TILE).astype(jnp.float32)
         for k in range(halves):
             wide_ref[k] = packed[:, k * 128 : (k + 1) * 128]
             for j in range(FEATURES // TILE):
                 lane = j * TILE + k * 128
-                rows_ref[count:, lane : lane + 128] = wide_ref[k, pl.ds(j, lines, stride=8), :].astype(jnp.bfloat16)
+                rows_ref[:, lane : lane + 128] = wide_ref[k, pl.ds(j, lines, stride=8), :].astype(jnp.bfloat16)
 
     tile.wait()
     prod = jnp.dot(rows_ref[...], w_ref[n], preferred_element_type=jnp.float32)
-    high = prod.astype(jnp.bfloat16)
-    out_ref[:, :, pl.ds(pl.multiple_of(n * TILE, TILE), TILE)] = high[:count].reshape(members, CTOK, TILE)
     for k in range(halves):
-        wide_ref[k, pl.ds(n, lines, stride=8), :] = prod[count:, k * 128 : (k + 1) * 128]
-    width = tiles * TILE
-    if rest:
-        start = rest_tile(lax.rem(lax.axis_index("tp"), COL_BLOCKS))
-
-        @pl.when((n >= start) & (n < start + rest // TILE))
-        def _():
-            low = prod - high.astype(jnp.float32)
-            place = n - start
-            lane = pl.multiple_of(width + place * TILE, TILE)
-            out_ref[:, :, pl.ds(lane, TILE)] = low[:count].astype(jnp.bfloat16).reshape(members, CTOK, TILE)
-            for k in range(halves):
-                wide_ref[k, pl.ds(tiles + place, lines, stride=8), :] = low[count:, k * 128 : (k + 1) * 128]
+        wide_ref[k, pl.ds(n, lines, stride=8), :] = prod[:, k * 128 : (k + 1) * 128]
+    start = rest_tile(lax.rem(lax.axis_index("tp"), COL_BLOCKS))
+
+    @pl.when((n >= start) & (n < start + REST // TILE))
+    def _():
+        low = prod - prod.astype(jnp.bfloat16).astype(jnp.float32)
+        for k in range(halves):
+            wide_ref[k, pl.ds(tiles + n - start, lines, stride=8), :] = low[:, k * 128 : (k + 1) * 128]
 
     @pl.when(n == tiles - 1)
     def _():
         for k in range(halves):
-            lane = width + rest + k * 128
-            out_ref[:, :, lane : lane + 128] = wide_ref[k].astype(jnp.bfloat16).reshape(members, 16, 128)
-
-
-def block_product(rows, blocks, rest):
-    members = rows.shape[0]
+            packed = wide_ref[k].astype(jnp.bfloat16).reshape(members, CTOK, 128)
+            out_ref[:, :, k * 128 : (k + 1) * 128] = packed
+
+
+def main_product(rows, blocks):
     tiles = blocks.shape[2] // TILE
     return pl.pallas_call(
-        functools.partial(product_kernel, tiles, rest),
-        out_shape=jax.ShapeDtypeStruct((members, CTOK, (tiles + 1) * TILE + rest), jnp.bfloat16),
+        functools.partial(main_kernel, tiles),
+        out_shape=jax.ShapeDtypeStruct(rows.shape, jnp.bfloat16),
         grid=(tiles,),
         in_specs=[VMEM, HBM],
-        out_specs=whole((members, CTOK, (tiles + 1) * TILE + rest)),
+        out_specs=VMEM,
         scratch_shapes=[
-            pltpu.VMEM((members * (CTOK + STEPS), FEATURES), jnp.bfloat16),
-            pltpu.VMEM((TILE // 128, members * 16, 128), jnp.float32),
+            pltpu.VMEM((MEMBERS * STEPS, FEATURES), jnp.bfloat16),
+            pltpu.VMEM((TILE // 128, MEMBERS * CTOK, 128), jnp.float32),
             pltpu.VMEM((tiles, FEATURES, TILE), jnp.bfloat16),
             pltpu.SemaphoreType.DMA((tiles,)),
         ],
         compiler_params=kernel_params(),
-        cost_estimate=cost(2 * members * (CTOK + STEPS) * FEATURES * tiles * TILE, 12 * 10**6),
-        name="block_product",
-    )(rows, blocks)
+        cost_estimate=cost(3 * 10**8, 6 * 10**6),
+        name="main_product",
+    )(rows, in_hbm(blocks))
+
+
+def gather_kernel(own_ref, ahead1_ref, ahead2_ref, ahead3_ref, out_ref):
+    z = lax.axis_index("tp") // COL_BLOCKS
+    for k, ref in enumerate((own_ref, ahead1_ref, ahead2_ref, ahead3_ref)):
+        out_ref[lax.rem(z + k, ROW_BLOCKS)] = ref[...]
+
+
+def gather_along(parts):
+    return pl.pallas_call(
+        gather_kernel,
+        out_shape=jax.ShapeDtypeStruct((ROW_BLOCKS,) + parts[0].shape, jnp.bfloat16),
+        in_specs=[VMEM] * ROW_BLOCKS,
+        out_specs=VMEM,
+        compiler_params=kernel_params(),
+        cost_estimate=cost(10**5, 10**6),
+        name="gather_along",
+    )(*parts)
 
 
 def summed_block(parts_ref, c, lanes):
@@ -202,10 +296,7 @@
     cols = QKV // COL_BLOCKS
     for c in range(COL_BLOCKS):
         first = 2 if c == 6 else 0
-        if main:
-            total = summed_block(parts_ref, c, slice(cols + REST, cols + REST + TILE))
-        else:
-            total = summed_block(parts_ref, c, slice(0, cols + REST))
+        total = summed_block(parts_ref, c, slice(0, TILE if main else cols + REST))
         for j in range(cols // TILE):
             lanes = slice(c * cols + j * TILE, c * cols + (j + 1) * TILE)
             rest = j - first
@@ -248,7 +339,9 @@
 KV_WIDTH = KVH * HD
 
 
-def attend_main_kernel(len_ref, parts_ref, bias_ref, cos_ref, sin_ref, cache_ref, out_ref, kv_ref, qkv_ref, piece_ref):
+def attend_main_kernel(
+    len_ref, bias_ref, cos_ref, sin_ref, cache_ref, parts_ref, out_ref, kv_ref, qkv_ref, piece_ref
+):
     rows = qkv_ref.shape[0]
     qkv_ref[...] = jnp.zeros(qkv_ref.shape, jnp.float32)
     load_qkv(True, parts_ref, qkv_ref)
@@ -281,7 +374,7 @@
             out_ref[r * COL_BLOCKS + c] = piece
 
 
-def attend_main(prefix_len, parts, bias, cosine, sine, cache):
+def attend_main(prefix_len, bias, cosine, sine, cache, parts):
     return pl.pallas_call(
         attend_main_kernel,
         out_shape=(
@@ -297,11 +390,11 @@
         compiler_params=kernel_params(),
         cost_estimate=cost(2 * 10**8, 6 * 10**6),
         name="attend_main",
-    )(prefix_len, parts, bias, cosine, sine, cache)
+    )(prefix_len, bias, cosine, sine, cache, parts)
 
 
 def attend_cont_kernel(
-    len_ref, bound_ref, parts_ref, bias_ref, cos_ref, sin_ref, cache_ref, kv_ref, out_ref, qkv_ref
+    len_ref, bound_ref, bias_ref, cos_ref, sin_ref, cache_ref, kv_ref, parts_ref, out_ref, qkv_ref
 ):
     rows = qkv_ref.shape[0]
     load_qkv(False, parts_ref, qkv_ref)
@@ -330,7 +423,7 @@
     return pl.pallas_call(
         attend_cont_kernel,
         out_shape=jax.ShapeDtypeStruct((CTOK, D), jnp.bfloat16),
-        in_specs=[SMEM, SMEM] + [VMEM] * 5 + [whole((8, 2 * KV_WIDTH))],
+        in_specs=[SMEM, SMEM] + [VMEM] * 6,
         out_specs=whole((CTOK, D)),
         scratch_shapes=[pltpu.VMEM((CTOK, QKV), jnp.float32)],
         compiler_params=kernel_params(),
@@ -364,7 +457,7 @@
         compiler_params=kernel_params(),
         cost_estimate=cost(2 * 10**8, 5 * 10**6),
         name="readout",
-    )(value_head, blocks)
+    )(value_head, in_hbm(blocks))
 
 
 def out_kernel(tiles, x_ref, read_ref, w_hbm, out_ref, rows_ref, wide_ref, read8_ref, w_ref, sems):
@@ -417,7 +510,7 @@
         compiler_params=kernel_params(),
         cost_estimate=cost(3 * 10**8, 5 * 10**6),
         name="out_product",
-    )(rows, read, blocks)
+    )(rows, read, in_hbm(blocks))
 
 
 def finish_kernel(parts_ref, main_ref, cont_ref, head_ref, mixed_ref, out_ref, score_ref, wide_ref):
@@ -451,7 +544,7 @@
             jax.ShapeDtypeStruct((STEPS, D), jnp.bfloat16),
             jax.ShapeDtypeStruct((8, 128), jnp.float32),
         ),
-        in_specs=[whole(parts.shape), VMEM, VMEM, VMEM, whole(mixed.shape)],
+        in_specs=[whole(parts.shape), whole(main.shape), whole(cont.shape), whole(head.shape), whole(mixed.shape)],
         out_specs=(whole((STEPS, D)), whole((8, 128))),
         scratch_shapes=[pltpu.VMEM((8, D), jnp.float32)],
         compiler_params=kernel_params(),
@@ -471,6 +564,34 @@
 
 def exchange(rows):
     return lax.all_to_all(rows, "tp", split_axis=0, concat_axis=0, tiled=True)
+
+
+def from_side(rows, dy, dx):
+    route = []
+    for to in range(MEMBERS):
+        z, y, x = to // 8, to // 4 % 2, to % 4
+        route.append((z * 8 + (y + dy) % 2 * 4 + (x + dx) % 4, to))
+    return lax.ppermute(rows, "tp", route)
+
+
+def from_along(rows, dz):
+    route = [((to + dz * COL_BLOCKS) % MEMBERS, to) for to in range(MEMBERS)]
+    return lax.ppermute(rows, "tp", route)
+
+
+def project(rows, blocks):
+    near = gather_along([rows[0]] + [from_along(rows[ROW_BLOCKS - k], k) for k in range(1, ROW_BLOCKS)])
+    half = ROW_BLOCKS // 2
+    over = from_side(near, 1, 0)
+    here, far, places = [], [], []
+    for dy, mine in ((0, near), (1, over)):
+        after = from_side(mine, 0, 1)
+        before = from_side(mine, 0, 3)
+        far += [from_side(before[:half], 0, 3), from_side(after[half:], 0, 1)]
+        here += [mine, after, before]
+        places += [(dy, 0), (dy, 1), (dy, 3)]
+    earlier = block_product(here, blocks)
+    return exchange(block_product(far, blocks, (earlier,), tuple(places) + ((0, 2), (1, 2))))
 
 
 def on_device(
@@ -485,11 +606,12 @@
     main_tables = rope_tables(prefix_len + step[:8])
     cont_tables = rope_tables(prefix_len + boundary + step)
     read = readout(value_head.reshape(COL_BLOCKS, D // COL_BLOCKS), w_out)
-    sent = exchange(norm_rows(main, cont, rms_gain[None, :]))
-    parts = exchange(block_product(sent, w_qkv, REST))
-    mixed, main_kv = attend_main(prefix_len, parts, bias, *main_tables, cache)
+    *rows, main_rows = norm_rows(main, cont, rms_gain[None, :])
+    main_parts = exchange(main_product(exchange(main_rows), w_qkv))
+    parts = project(rows, w_qkv)
+    mixed, main_kv = attend_main(prefix_len, bias, *main_tables, cache, main_parts)
     mixed = exchange(mixed)
-    cont_mixed = attend_cont(prefix_len, boundary, parts, bias, *cont_tables, cache, main_kv)
+    cont_mixed = attend_cont(prefix_len, boundary, bias, *cont_tables, cache, main_kv, parts)
     parts = exchange(out_product(mixed, read, w_out))
     main_out, score = finish(parts, main, cont, head, cont_mixed)
     return main_out[None], score[0, :1]

time: 133 us -> 117 us (0.88)
  blocking collectives: 40.7 us -> 0 us
  starting transfers between devices: 16.6 us -> 47.6 us
  Pallas kernels: 18.6 us -> 27.9 us
  local copies, waits for them, and re-layouts: 14.4 us -> 5.85 us
  waiting for transfers between devices: 39.6 us -> 31.8 us
    all_to_all x1 -> x0, blocking collectives: 40.7 us -> none  [exchange(): return lax.all_to_all(rows, 'tp', split_axis=0, concat_axis=0, tiled=True)]
    ppermute x0 -> x12, starting transfers between devices: none -> 19.1 us  [the longest x9 13.7 us: from_side(): return lax.ppermute(rows, 'tp', route)]
    all_to_all x3 -> x5, starting transfers between devices: 16.6 us -> 28.4 us  [exchange(): return lax.all_to_all(rows, 'tp', split_axis=0, concat_axis=0, tiled=True)]
    all_to_all x3 -> x5, waiting for transfers between devices: 39.6 us -> 30.2 us  [exchange(): return lax.all_to_all(rows, 'tp', split_axis=0, concat_axis=0, tiled=True)]
    unnamed x34 -> x22, local copies, waits for them, and re-layouts: 13.9 us -> 5.28 us
    pallas_call x2 -> x5, Pallas kernels: 6.09 us -> 13.2 us  [the longest x2 7.41 us: block_product(): pl.pallas_call(functools.partial(product_kernel, tiles, counts, places),...]
    pallas_call x1, Pallas kernels: 1.53 us -> 3.41 us  [readout(): pl.pallas_call(readout_kernel, out_shape=jax.ShapeDtypeStruct((1, FEATURE...]
    ppermute x0 -> x12, waiting for transfers between devices: none -> 1.61 us  [the longest x9 1.61 us: from_side(): return lax.ppermute(rows, 'tp', route)]
  transfers between devices with their start and end apart: 3 -> 17, of which waited for: 3 -> 5; matrix products, arithmetic and copies ran while one was open for 0% -> 0% of each run, Pallas kernels for 3% -> 21%
where the time goes in v7:
time: 117 us; the launch traced here: 116 us
  starting transfers between devices  47.6 us (41%)
  waiting for transfers between devices  31.8 us (27%)
  Pallas kernels  27.9 us (24%)
  local copies, waits for them, and re-layouts  5.85 us (5%)
  between operations  2.22 us (2%)
    all_to_all x5, waiting for transfers between devices, exchange(): return lax.all_to_all(rows, 'tp', split_axis=0, concat_axis=0, tiled=True)  30.2 us
    all_to_all x5, starting transfers between devices, exchange(): return lax.all_to_all(rows, 'tp', split_axis=0, concat_axis=0, tiled=True)  28.4 us
    ppermute x9, starting transfers between devices, from_side(): return lax.ppermute(rows, 'tp', route)  13.7 us
    pallas_call x2, Pallas kernels, block_product(): pl.pallas_call(functools.partial(product_kernel, tiles, counts, places),...  7.41 us
    ppermute x3, starting transfers between devices, from_along(): return lax.ppermute(rows, 'tp', route)  5.45 us
    unnamed x22, local copies, waits for them, and re-layouts  5.28 us
    pallas_call x1, Pallas kernels, attend_main(): pl.pallas_call(attend_main_kernel, out_shape=(jax.ShapeDtypeStruct((32, 1...  3.69 us
    pallas_call x1, Pallas kernels, main_product(): pl.pallas_call(functools.partial(main_kernel, tiles), out_shape=jax.Shape...  3.63 us
  transfers between devices with their start and end apart: 17, of which 5 were waited for; matrix products, arithmetic and copies ran while one was open for 0% of the time, Pallas kernels for 21%

profile of v7, /device:TPU:0, one launch (start us, length us, event | category | flops | bytes accessed | tf_op | source)
XLA Modules:
  0.0 115.8 jit_solution(1598531873146799428)
XLA Ops:
  0.6 2.2 %norm_rows.1 = (bf16[16,2048]{1,0:T(8,128)(2,1)S(1)}, bf16[16,2048]{1,0:T(8,128)(2,1)S(1)}, bf16[16,2048]{1,0:T(8,128)(2,1)S(1)}, bf16[16,2048]{1,0:T(8,128)(2,1)S(1)}, bf16[32,16,256]{2,1,0:T(8,128)(2,1)}) custom-call(bf16[2,8192]{1,0:T(2,128)(2,1)} %bitcast.17, bf16[8,2,8192]{2,1,0:T(2,128)(2,1)} %bitcast.13, f32[1,8192]{1,0:T(1,128)} %bitcast.20), custom_call_target="tpu_custom_call" | custom-call | flops 1000000 | bytes 4000000 | tf_op jit(solution)/shard_map/norm_rows/pallas_call | solution.py:84
  2.8 4.2 %collective-permute-start = (bf16[16,2048]{1,0:T(8,128)(2,1)S(1)}, bf16[16,2048]{1,0:T(8,128)(2,1)S(1)}, u32[]{:S(2)}, u32[]{:S(2)}) collective-permute-start(bf16[16,2048]{1,0:T(8,128)(2,1)S(1)} %get-tuple-element.15), channel_id=1, source_target_pairs={{8,0},{9,1},{10,2},{11,3},{12,4},{13,5},{14,6},{15,7},{16,8},{17,9... | collective-permute-start | bytes 196616 | tf_op jit(solution)/shard_map/ppermute | solution.py:579
  8.2 7.4 %all-to-all-start = ((bf16[32,16,256]{2,1,0:T(8,128)(2,1)}), bf16[32,16,256]{2,1,0:T(8,128)(2,1)S(1)}, u32[]{:S(2)}, u32[]{:S(2)}) async-start(bf16[32,16,256]{2,1,0:T(8,128)(2,1)} %get-tuple-element.11), calls=%async_computation | async-start | bytes 524288 | tf_op jit(solution)/shard_map/all_to_all | solution.py:566
  15.7 1.9 %collective-permute-start.7 = (bf16[4,16,2048]{2,1,0:T(8,128)(2,1)S(1)}, bf16[4,16,2048]{2,1,0:T(8,128)(2,1)S(1)}, u32[]{:S(2)}, u32[]{:S(2)}) collective-permute-start(bf16[4,16,2048]{2,1,0:T(8,128)(2,1)S(1)} %gather_along.1.refs_0_), channel_id=1, source_target_pairs={{4,0},{5,1},{6,2},{7,3},{0,4},{1,5},{2,6},{3,7},{12,8},{13,9},{14,... | collective-permute-start | bytes 786440 | tf_op jit(solution)/shard_map/ppermute | solution.py:574
  19.9 1.8 %collective-permute-start.5 = (bf16[4,16,2048]{2,1,0:T(8,128)(2,1)S(1)}, bf16[4,16,2048]{2,1,0:T(8,128)(2,1)S(1)}, u32[]{:S(2)}, u32[]{:S(2)}) collective-permute-start(bf16[4,16,2048]{2,1,0:T(8,128)(2,1)S(1)} %gather_along.1.refs_0_), channel_id=1, source_target_pairs={{1,0},{2,1},{3,2},{0,3},{5,4},{6,5},{7,6},{4,7},{9,8},{10,9},{11,1... | collective-permute-start | bytes 786440 | tf_op jit(solution)/shard_map/ppermute | solution.py:574
  21.6 4.2 %all-to-all-done.x_ref = bf16[32,16,256]{2,1,0:T(8,128)(2,1)S(1)} async-done(((bf16[32,16,256]{2,1,0:T(8,128)(2,1)}), bf16[32,16,256]{2,1,0:T(8,128)(2,1)S(1)}, u32[]{:S(2)}, u32[]{:S(2)}) %all-to-all-start) | async-done | bytes 262176 | tf_op jit(solution)/shard_map/all_to_all | solution.py:566
  25.8 3.6 %main_product.1 = bf16[32,16,256]{2,1,0:T(8,128)(2,1)} custom-call(bf16[32,16,256]{2,1,0:T(8,128)(2,1)S(1)} %all-to-all-done.x_ref, bf16[1,2048,1280]{2,1,0:T(8,128)(2,1)} %refs_5_.1), custom_call_target="tpu_custom_call" | custom-call | flops 300000000 | bytes 6000000 | tf_op jit(solution)/shard_map/main_product/pallas_call | solution.py:236
  29.5 3.9 %all-to-all-start.1 = ((bf16[32,16,256]{2,1,0:T(8,128)(2,1)}), bf16[32,16,256]{2,1,0:T(8,128)(2,1)S(1)}, u32[]{:S(2)}, u32[]{:S(2)}) async-start(bf16[32,16,256]{2,1,0:T(8,128)(2,1)} %main_product.1), calls=%async_computation.1 | async-start | bytes 524288 | tf_op jit(solution)/shard_map/all_to_all | solution.py:566
  33.4 3.0 %collective-permute-start.10 = (bf16[4,16,2048]{2,1,0:T(8,128)(2,1)S(1)}, bf16[4,16,2048]{2,1,0:T(8,128)(2,1)S(1)}, u32[]{:S(2)}, u32[]{:S(2)}) collective-permute-start(bf16[4,16,2048]{2,1,0:T(8,128)(2,1)S(1)} %collective-permute-done.7.refs_3_), channel_id=1, source_target_pairs={{1,0},{2,1},{3,2},{0,3},{5,4},{6,5},{7,6},{4,7},{9,8},{10,9},{11,1... | collective-permute-start | bytes 786440 | tf_op jit(solution)/shard_map/ppermute | solution.py:574
  36.5 6.4 %all-to-all-done.1.parts_ref = bf16[32,16,256]{2,1,0:T(8,128)(2,1)S(1)} async-done(((bf16[32,16,256]{2,1,0:T(8,128)(2,1)}), bf16[32,16,256]{2,1,0:T(8,128)(2,1)S(1)}, u32[]{:S(2)}, u32[]{:S(2)}) %all-to-all-start.1) | async-done | bytes 262176 | tf_op jit(solution)/shard_map/all_to_all | solution.py:566
  42.9 3.7 %attend_main.1 = (bf16[32,16,256]{2,1,0:T(8,128)(2,1)}, f32[8,2048]{1,0:T(8,128)S(1)}) custom-call(s32[1]{0:T(128)} %copy.12.len_ref, f32[1,10240]{1,0:T(1,128)S(1)} %bitcast.15, f32[8,128]{1,0:T(8,128)S(1)} %get-tuple-element.26.cos_ref, f32[8,128]{1,0:T(8,128)S(1)} %get-tuple-element.27.sin_ref, bf16[256,2048]{1,0:T(8,128)(2,1)S(1)} %bitcast.11, ...), custom_call_target="tpu_custom_call" | custom-call | flops 200000000 | bytes 6000000 | tf_op jit(solution)/shard_map/attend_main/pallas_call | solution.py:378
  47.2 4.3 %all-to-all-start.2 = ((bf16[32,16,256]{2,1,0:T(8,128)(2,1)}), bf16[32,16,256]{2,1,0:T(8,128)(2,1)S(1)}, u32[]{:S(2)}, u32[]{:S(2)}) async-start(bf16[32,16,256]{2,1,0:T(8,128)(2,1)} %get-tuple-element.12), calls=%async_computation.2 | async-start | bytes 524288 | tf_op jit(solution)/shard_map/all_to_all | solution.py:566
  51.5 1.9 %collective-permute-start.4 = (bf16[2,16,2048]{2,1,0:T(8,128)(2,1)S(1)}, bf16[2,16,2048]{2,1,0:T(8,128)(2,1)S(1)}, u32[]{:S(2)}, u32[]{:S(2)}) collective-permute-start(bf16[2,16,2048]{2,1,0:T(8,128)(2,1)S(1)} %slice.24), channel_id=1, source_target_pairs={{3,0},{0,1},{1,2},{2,3},{7,4},{4,5},{5,6},{6,7},{11,8},{8,9},{9,10... | collective-permute-start | bytes 393224 | tf_op jit(solution)/shard_map/ppermute | solution.py:574
  54.9 1.9 %collective-permute-start.11 = (bf16[2,16,2048]{2,1,0:T(8,128)(2,1)S(1)}, bf16[2,16,2048]{2,1,0:T(8,128)(2,1)S(1)}, u32[]{:S(2)}, u32[]{:S(2)}) collective-permute-start(bf16[2,16,2048]{2,1,0:T(8,128)(2,1)S(1)} %slice.27), channel_id=1, source_target_pairs={{1,0},{2,1},{3,2},{0,3},{5,4},{6,5},{7,6},{4,7},{9,8},{10,9},{11,1... | collective-permute-start | bytes 393224 | tf_op jit(solution)/shard_map/ppermute | solution.py:574
  57.1 4.3 %block_product.2.refs_4_ = bf16[24,16,2048]{2,1,0:T(8,128)(2,1)S(1)} custom-call(bf16[4,16,2048]{2,1,0:T(8,128)(2,1)S(1)} %gather_along.1.refs_0_, bf16[4,16,2048]{2,1,0:T(8,128)(2,1)S(1)} %collective-permute-done.5.refs_1_, bf16[4,16,2048]{2,1,0:T(8,128)(2,1)S(1)} %collective-permute-done.3.refs_2_, ...), custom_call_target="tpu_custom_call" | custom-call | flops 2013265920 | bytes 12000000 | tf_op jit(solution)/shard_map/block_product/pallas_call | solution.py:181
  63.1 3.1 %block_product.3 = bf16[32,16,2048]{2,1,0:T(8,128)(2,1)S(1)} custom-call(bf16[2,16,2048]{2,1,0:T(8,128)(2,1)S(1)} %collective-permute-done.4.refs_0_, bf16[2,16,2048]{2,1,0:T(8,128)(2,1)S(1)} %collective-permute-done.6.refs_1_, bf16[2,16,2048]{2,1,0:T(8,128)(2,1)S(1)} %collective-permute-done.9.refs_2_, ...), custom_call_target="tpu_custom_call" | custom-call | flops 671088640 | bytes 12000000 | tf_op jit(solution)/shard_map/block_product/pallas_call | solution.py:181
  67.5 6.6 %all-to-all-start.4 = ((bf16[32,16,2048]{2,1,0:T(8,128)(2,1)}), bf16[32,16,2048]{2,1,0:T(8,128)(2,1)S(1)}, u32[]{:S(2)}, u32[]{:S(2)}) async-start(bf16[32,16,2048]{2,1,0:T(8,128)(2,1)} %copy-done), calls=%async_computation.4 | async-start | bytes 4194304 | tf_op jit(solution)/shard_map/all_to_all | solution.py:566
  74.2 3.4 %readout.1.read_ref = f32[1,2048]{1,0:T(1,128)S(1)} custom-call(f32[8,1024]{1,0:T(8,128)S(1)} %reshape.34.head_ref, bf16[1,2048,1024]{2,1,0:T(8,128)(2,1)} %w_hbm.5), custom_call_target="tpu_custom_call" | custom-call | flops 200000000 | bytes 5000000 | tf_op jit(solution)/shard_map/readout/pallas_call | solution.py:451
  77.6 2.6 %out_product.1 = f32[32,16,256]{2,1,0:T(8,128)S(1)} custom-call(bf16[32,16,256]{2,1,0:T(8,128)(2,1)S(1)} %all-to-all-done.2.x_ref, f32[1,2048]{1,0:T(1,128)S(1)} %readout.1.read_ref, bf16[1,2048,1024]{2,1,0:T(8,128)(2,1)} %w_hbm.5), custom_call_target="tpu_custom_call" | custom-call | flops 300000000 | bytes 5000000 | tf_op jit(solution)/shard_map/out_product/pallas_call | solution.py:497
  81.0 14.9 %all-to-all-done.4.parts_ref = bf16[32,16,2048]{2,1,0:T(8,128)(2,1)S(1)} async-done(((bf16[32,16,2048]{2,1,0:T(8,128)(2,1)}), bf16[32,16,2048]{2,1,0:T(8,128)(2,1)S(1)}, u32[]{:S(2)}, u32[]{:S(2)}) %all-to-all-start.4) | async-done | bytes 2097184 | tf_op jit(solution)/shard_map/all_to_all | solution.py:566
  95.9 6.3 %all-to-all-start.3 = ((f32[32,16,256]{2,1,0:T(8,128)}), f32[32,16,256]{2,1,0:T(8,128)}, u32[]{:S(2)}, u32[]{:S(2)}) async-start(f32[32,16,256]{2,1,0:T(8,128)} %copy-done.2), calls=%async_computation.3 | async-start | bytes 1048576 | tf_op jit(solution)/shard_map/all_to_all | solution.py:566
  103.9 3.0 %attend_cont.1.mixed_ref = bf16[16,8192]{1,0:T(8,128)(2,1)S(1)} custom-call(s32[1]{0:T(128)} %copy.12.len_ref, s32[1]{0:T(128)S(6)} %copy.13.bound_ref, f32[1,10240]{1,0:T(1,128)S(1)} %bitcast.16, f32[16,128]{1,0:T(8,128)S(1)} %get-tuple-element.28.cos_ref, f32[16,128]{1,0:T(8,128)S(1)} %get-tuple-element.29.sin_ref, bf16[256,2048]{1,0:T(8,128)(2,1)S(1)} %bitcast.12, ...), custom_call_target="tpu_custom_call" | custom-call | flops 400000000 | bytes 8000000 | tf_op jit(solution)/shard_map/attend_cont/pallas_call | solution.py:423
  107.6 4.8 %all-to-all-done.3.parts_ref = f32[32,16,256]{2,1,0:T(8,128)} async-done(((f32[32,16,256]{2,1,0:T(8,128)}), f32[32,16,256]{2,1,0:T(8,128)}, u32[]{:S(2)}, u32[]{:S(2)}) %all-to-all-start.3) | async-done | bytes 524320 | tf_op jit(solution)/shard_map/all_to_all | solution.py:566
  113.3 2.0 %finish.1 = (bf16[2,8192]{1,0:T(2,128)(2,1)}, f32[8,128]{1,0:T(8,128)S(1)}) custom-call(f32[32,16,256]{2,1,0:T(8,128)} %all-to-all-done.3.parts_ref, bf16[2,8192]{1,0:T(2,128)(2,1)S(1)} %bitcast.18, bf16[8,2,8192]{2,1,0:T(2,128)(2,1)S(1)} %bitcast.14, f32[1,8192]{1,0:T(1,128)S(1)} %bitcast.19, bf16[16,8192]{1,0:T(8,128)(2,1)S(1)} %copy-done.5), custom_call_target="tpu_custom_call" | custom-call | flops 1000000 | bytes 2000000 | tf_op jit(solution)/shard_map/finish/pallas_call | solution.py:541
  (56 shorter events, 12.5 us)
Async XLA Ops:
  2.8 12.9 %collective-permute-start = (bf16[16,2048]{1,0:T(8,128)(2,1)S(1)}, bf16[16,2048]{1,0:T(8,128)(2,1)S(1)}, u32[]{:S(2)}, u32[]{:S(2)}) collective-permute-start(bf16[16,2048]{1,0:T(8,128)(2,1)S(1)} %get-tuple-element.15), channel_id=1, source_target_pairs={{8,0},{9,1},{10,2},{11,3},{12,4},{13,5},{14,6},{15,7},{16,8},{17,9... | collective-permute-start | bytes 196616 | tf_op jit(solution)/shard_map/ppermute | solution.py:579
  7.0 8.7 %collective-permute-start.1 = (bf16[16,2048]{1,0:T(8,128)(2,1)S(1)}, bf16[16,2048]{1,0:T(8,128)(2,1)S(1)}, u32[]{:S(2)}, u32[]{:S(2)}) collective-permute-start(bf16[16,2048]{1,0:T(8,128)(2,1)S(1)} %get-tuple-element.16), channel_id=1, source_target_pairs={{16,0},{17,1},{18,2},{19,3},{20,4},{21,5},{22,6},{23,7},{24,8},{25... | collective-permute-start | bytes 196616 | tf_op jit(solution)/shard_map/ppermute | solution.py:579
  7.0 8.7 %collective-permute-start.2 = (bf16[16,2048]{1,0:T(8,128)(2,1)S(1)}, bf16[16,2048]{1,0:T(8,128)(2,1)S(1)}, u32[]{:S(2)}, u32[]{:S(2)}) collective-permute-start(bf16[16,2048]{1,0:T(8,128)(2,1)S(1)} %get-tuple-element.17), channel_id=1, source_target_pairs={{24,0},{25,1},{26,2},{27,3},{28,4},{29,5},{30,6},{31,7},{0,8},{1,9... | collective-permute-start | bytes 196616 | tf_op jit(solution)/shard_map/ppermute | solution.py:579
  8.2 17.6 %all-to-all-start = ((bf16[32,16,256]{2,1,0:T(8,128)(2,1)}), bf16[32,16,256]{2,1,0:T(8,128)(2,1)S(1)}, u32[]{:S(2)}, u32[]{:S(2)}) async-start(bf16[32,16,256]{2,1,0:T(8,128)(2,1)} %get-tuple-element.11), calls=%async_computation | async-start | bytes 524288 | tf_op jit(solution)/shard_map/all_to_all | solution.py:566
  15.7 17.6 %collective-permute-start.7 = (bf16[4,16,2048]{2,1,0:T(8,128)(2,1)S(1)}, bf16[4,16,2048]{2,1,0:T(8,128)(2,1)S(1)}, u32[]{:S(2)}, u32[]{:S(2)}) collective-permute-start(bf16[4,16,2048]{2,1,0:T(8,128)(2,1)S(1)} %gather_along.1.refs_0_), channel_id=1, source_target_pairs={{4,0},{5,1},{6,2},{7,3},{0,4},{1,5},{2,6},{3,7},{12,8},{13,9},{14,... | collective-permute-start | bytes 786440 | tf_op jit(solution)/shard_map/ppermute | solution.py:574
  18.3 24.6 %copy-start.1 = (bf16[1,256,2048]{2,1,0:T(8,128)(2,1)S(1)}, bf16[1,256,2048]{2,1,0:T(8,128)(2,1)}, u32[]{:S(2)}) copy-start(bf16[1,256,2048]{2,1,0:T(8,128)(2,1)} %param.12) | copy-start | bytes 3145732
  18.3 24.6 %copy-start.6 = (f32[10240]{0:T(1024)S(1)}, f32[10240]{0:T(1024)}, u32[]{:S(2)}) copy-start(f32[10240]{0:T(1024)} %param.16) | copy-start | bytes 122884
  18.3 33.2 %collective-permute-start.3 = (bf16[4,16,2048]{2,1,0:T(8,128)(2,1)S(1)}, bf16[4,16,2048]{2,1,0:T(8,128)(2,1)S(1)}, u32[]{:S(2)}, u32[]{:S(2)}) collective-permute-start(bf16[4,16,2048]{2,1,0:T(8,128)(2,1)S(1)} %gather_along.1.refs_0_), channel_id=1, source_target_pairs={{3,0},{0,1},{1,2},{2,3},{7,4},{4,5},{5,6},{6,7},{11,8},{8,9},{9,10... | collective-permute-start | bytes 786440 | tf_op jit(solution)/shard_map/ppermute | solution.py:574
  19.9 33.5 %collective-permute-start.5 = (bf16[4,16,2048]{2,1,0:T(8,128)(2,1)S(1)}, bf16[4,16,2048]{2,1,0:T(8,128)(2,1)S(1)}, u32[]{:S(2)}, u32[]{:S(2)}) collective-permute-start(bf16[4,16,2048]{2,1,0:T(8,128)(2,1)S(1)} %gather_along.1.refs_0_), channel_id=1, source_target_pairs={{1,0},{2,1},{3,2},{0,3},{5,4},{6,5},{7,6},{4,7},{9,8},{10,9},{11,1... | collective-permute-start | bytes 786440 | tf_op jit(solution)/shard_map/ppermute | solution.py:574
  29.5 13.4 %all-to-all-start.1 = ((bf16[32,16,256]{2,1,0:T(8,128)(2,1)}), bf16[32,16,256]{2,1,0:T(8,128)(2,1)S(1)}, u32[]{:S(2)}, u32[]{:S(2)}) async-start(bf16[32,16,256]{2,1,0:T(8,128)(2,1)} %main_product.1), calls=%async_computation.1 | async-start | bytes 524288 | tf_op jit(solution)/shard_map/all_to_all | solution.py:566
  33.4 21.5 %collective-permute-start.10 = (bf16[4,16,2048]{2,1,0:T(8,128)(2,1)S(1)}, bf16[4,16,2048]{2,1,0:T(8,128)(2,1)S(1)}, u32[]{:S(2)}, u32[]{:S(2)}) collective-permute-start(bf16[4,16,2048]{2,1,0:T(8,128)(2,1)S(1)} %collective-permute-done.7.refs_3_), channel_id=1, source_target_pairs={{1,0},{2,1},{3,2},{0,3},{5,4},{6,5},{7,6},{4,7},{9,8},{10,9},{11,1... | collective-permute-start | bytes 786440 | tf_op jit(solution)/shard_map/ppermute | solution.py:574
  36.4 20.4 %collective-permute-start.8 = (bf16[4,16,2048]{2,1,0:T(8,128)(2,1)S(1)}, bf16[4,16,2048]{2,1,0:T(8,128)(2,1)S(1)}, u32[]{:S(2)}, u32[]{:S(2)}) collective-permute-start(bf16[4,16,2048]{2,1,0:T(8,128)(2,1)S(1)} %collective-permute-done.7.refs_3_), channel_id=1, source_target_pairs={{3,0},{0,1},{1,2},{2,3},{7,4},{4,5},{5,6},{6,7},{11,8},{8,9},{9,10... | collective-permute-start | bytes 786440 | tf_op jit(solution)/shard_map/ppermute | solution.py:574
  47.2 20.3 %all-to-all-start.2 = ((bf16[32,16,256]{2,1,0:T(8,128)(2,1)}), bf16[32,16,256]{2,1,0:T(8,128)(2,1)S(1)}, u32[]{:S(2)}, u32[]{:S(2)}) async-start(bf16[32,16,256]{2,1,0:T(8,128)(2,1)} %get-tuple-element.12), calls=%async_computation.2 | async-start | bytes 524288 | tf_op jit(solution)/shard_map/all_to_all | solution.py:566
  51.5 9.9 %collective-permute-start.4 = (bf16[2,16,2048]{2,1,0:T(8,128)(2,1)S(1)}, bf16[2,16,2048]{2,1,0:T(8,128)(2,1)S(1)}, u32[]{:S(2)}, u32[]{:S(2)}) collective-permute-start(bf16[2,16,2048]{2,1,0:T(8,128)(2,1)S(1)} %slice.24), channel_id=1, source_target_pairs={{3,0},{0,1},{1,2},{2,3},{7,4},{4,5},{5,6},{6,7},{11,8},{8,9},{9,10... | collective-permute-start | bytes 393224 | tf_op jit(solution)/shard_map/ppermute | solution.py:574
  53.4 8.1 %collective-permute-start.6 = (bf16[2,16,2048]{2,1,0:T(8,128)(2,1)S(1)}, bf16[2,16,2048]{2,1,0:T(8,128)(2,1)S(1)}, u32[]{:S(2)}, u32[]{:S(2)}) collective-permute-start(bf16[2,16,2048]{2,1,0:T(8,128)(2,1)S(1)} %slice.25), channel_id=1, source_target_pairs={{1,0},{2,1},{3,2},{0,3},{5,4},{6,5},{7,6},{4,7},{9,8},{10,9},{11,1... | collective-permute-start | bytes 393224 | tf_op jit(solution)/shard_map/ppermute | solution.py:574
  54.9 6.5 %collective-permute-start.11 = (bf16[2,16,2048]{2,1,0:T(8,128)(2,1)S(1)}, bf16[2,16,2048]{2,1,0:T(8,128)(2,1)S(1)}, u32[]{:S(2)}, u32[]{:S(2)}) collective-permute-start(bf16[2,16,2048]{2,1,0:T(8,128)(2,1)S(1)} %slice.27), channel_id=1, source_target_pairs={{1,0},{2,1},{3,2},{0,3},{5,4},{6,5},{7,6},{4,7},{9,8},{10,9},{11,1... | collective-permute-start | bytes 393224 | tf_op jit(solution)/shard_map/ppermute | solution.py:574
  56.8 6.2 %collective-permute-start.9 = (bf16[2,16,2048]{2,1,0:T(8,128)(2,1)S(1)}, bf16[2,16,2048]{2,1,0:T(8,128)(2,1)S(1)}, u32[]{:S(2)}, u32[]{:S(2)}) collective-permute-start(bf16[2,16,2048]{2,1,0:T(8,128)(2,1)S(1)} %slice.26), channel_id=1, source_target_pairs={{3,0},{0,1},{1,2},{2,3},{7,4},{4,5},{5,6},{6,7},{11,8},{8,9},{9,10... | collective-permute-start | bytes 393224 | tf_op jit(solution)/shard_map/ppermute | solution.py:574
  66.2 1.4 %copy-start = (bf16[32,16,2048]{2,1,0:T(8,128)(2,1)}, bf16[32,16,2048]{2,1,0:T(8,128)(2,1)S(1)}, u32[]{:S(2)}) copy-start(bf16[32,16,2048]{2,1,0:T(8,128)(2,1)S(1)} %block_product.3) | copy-start | bytes 6291460
  67.5 6.6 %copy-start.8 = (f32[8192]{0:T(1024)S(1)}, f32[8192]{0:T(1024)}, u32[]{:S(2)}) copy-start(f32[8192]{0:T(1024)} %param.19) | copy-start | bytes 98308
  67.5 28.3 %all-to-all-start.4 = ((bf16[32,16,2048]{2,1,0:T(8,128)(2,1)}), bf16[32,16,2048]{2,1,0:T(8,128)(2,1)S(1)}, u32[]{:S(2)}, u32[]{:S(2)}) async-start(bf16[32,16,2048]{2,1,0:T(8,128)(2,1)} %copy-done), calls=%async_computation.4 | async-start | bytes 4194304 | tf_op jit(solution)/shard_map/all_to_all | solution.py:566
  81.0 31.3 %copy-start.3 = (bf16[1,8,2,8192]{3,2,1,0:T(2,128)(2,1)S(1)}, bf16[1,8,2,8192]{3,2,1,0:T(2,128)(2,1)}, u32[]{:S(2)}) copy-start(bf16[1,8,2,8192]{3,2,1,0:T(2,128)(2,1)} %param.11) | copy-start | bytes 786436
  81.0 31.3 %copy-start.7 = (bf16[1,2,8192]{2,1,0:T(2,128)(2,1)S(1)}, bf16[1,2,8192]{2,1,0:T(2,128)(2,1)}, u32[]{:S(2)}) copy-start(bf16[1,2,8192]{2,1,0:T(2,128)(2,1)} %param.10) | copy-start | bytes 98308
  95.9 16.5 %all-to-all-start.3 = ((f32[32,16,256]{2,1,0:T(8,128)}), f32[32,16,256]{2,1,0:T(8,128)}, u32[]{:S(2)}, u32[]{:S(2)}) async-start(f32[32,16,256]{2,1,0:T(8,128)} %copy-done.2), calls=%async_computation.3 | async-start | bytes 1048576 | tf_op jit(solution)/shard_map/all_to_all | solution.py:566
  112.3 1.0 copy-start.5
  (4 other events, 3.0 us)

commit v8 on v7

--- a/solution.py
+++ b/solution.py
@@ -29,6 +29,7 @@
 VMEM = pl.BlockSpec(memory_space=pltpu.VMEM)
 SMEM = pl.BlockSpec(memory_space=pltpu.SMEM)
 HBM = pl.BlockSpec(memory_space=pltpu.HBM)
+UNREAD = pl.BlockSpec(memory_space=pl.ANY)
 
 
 def whole(shape):
@@ -47,22 +48,22 @@
     return pltpu.CompilerParams(vmem_limit_bytes=VMEM_LIMIT)
 
 
-def norm_kernel(main_hbm, cont_hbm, gain_hbm, z0_ref, z1_ref, z2_ref, z3_ref, out_ref, main_ref, cont_ref, gain_ref, rows_ref, piece_ref, sems):
-    pairs = ((main_hbm, main_ref), (cont_hbm, cont_ref), (gain_hbm, gain_ref))
+def fetch(pairs, sems):
     copies = [pltpu.make_async_copy(src, dst, sems.at[i]) for i, (src, dst) in enumerate(pairs)]
     for copy in copies:
         copy.start()
     for copy in copies:
         copy.wait()
 
-    def normed(wide):
-        inv = lax.rsqrt(jnp.mean(wide * wide, axis=-1, keepdims=True) + EPS)
-        return wide * inv * gain_ref[...]
-
-    for c in range(CONTS):
-        rows_ref[c * STEPS : (c + 1) * STEPS, :] = cont_ref[c].astype(jnp.float32)
-    cont = normed(rows_ref[...]).astype(jnp.bfloat16)
-    main = normed(main_ref[...].astype(jnp.float32))
+
+def normed(wide, gain):
+    inv = lax.rsqrt(jnp.mean(wide * wide, axis=-1, keepdims=True) + EPS)
+    return wide * inv * gain
+
+
+def norm_main_kernel(main_hbm, gain_hbm, out_ref, main_ref, gain_ref, piece_ref, sems):
+    fetch(((main_hbm, main_ref), (gain_hbm, gain_ref)), sems)
+    main = normed(main_ref[...].astype(jnp.float32), gain_ref[...])
     for r in range(ROW_BLOCKS):
         for j in range(FEATURES // TILE):
             lanes = slice(r * FEATURES + j * TILE, r * FEATURES + (j + 1) * TILE)
@@ -72,6 +73,32 @@
         piece = piece_ref[r].astype(jnp.bfloat16)
         for c in range(COL_BLOCKS):
             out_ref[r * COL_BLOCKS + c] = piece
+
+
+def norm_main(main, gain):
+    return pl.pallas_call(
+        norm_main_kernel,
+        out_shape=jax.ShapeDtypeStruct((MEMBERS, CTOK, TILE), jnp.bfloat16),
+        in_specs=[HBM] * 2,
+        out_specs=VMEM,
+        scratch_shapes=[
+            pltpu.VMEM((STEPS, D), jnp.bfloat16),
+            pltpu.VMEM((1, D), jnp.float32),
+            pltpu.VMEM((ROW_BLOCKS, 16, TILE), jnp.float32),
+            pltpu.SemaphoreType.DMA((2,)),
+        ],
+        compiler_params=kernel_params(),
+        cost_estimate=cost(10**6, 4 * 10**6),
+        name="norm_main",
+    )(in_hbm(main), in_hbm(gain))
+
+
+def norm_cont_kernel(cont_hbm, gain_hbm, after_ref, z0_ref, z1_ref, z2_ref, z3_ref, cont_ref, gain_ref, rows_ref, sems):
+    fetch(((cont_hbm, cont_ref), (gain_hbm, gain_ref)), sems)
+    for c in range(CONTS):
+        rows_ref[c * STEPS : (c + 1) * STEPS, :] = cont_ref[c].astype(jnp.float32)
+    cont = normed(rows_ref[...], gain_ref[...]).astype(jnp.bfloat16)
+    for r in range(ROW_BLOCKS):
         ahead = lax.rem(r + ROW_BLOCKS - lax.axis_index("tp") // COL_BLOCKS, ROW_BLOCKS)
         for k, z_ref in enumerate((z0_ref, z1_ref, z2_ref, z3_ref)):
 
@@ -80,25 +107,22 @@
                 z_ref[...] = cont[:, r * FEATURES : (r + 1) * FEATURES]
 
 
-def norm_rows(main, cont, gain):
-    return pl.pallas_call(
-        norm_kernel,
-        out_shape=[jax.ShapeDtypeStruct((CTOK, FEATURES), jnp.bfloat16)] * ROW_BLOCKS
-        + [jax.ShapeDtypeStruct((MEMBERS, CTOK, TILE), jnp.bfloat16)],
-        in_specs=[HBM] * 3,
-        out_specs=[VMEM] * (1 + ROW_BLOCKS),
+def norm_cont(cont, gain, after):
+    return pl.pallas_call(
+        norm_cont_kernel,
+        out_shape=[jax.ShapeDtypeStruct((CTOK, FEATURES), jnp.bfloat16)] * ROW_BLOCKS,
+        in_specs=[HBM] * 2 + [UNREAD],
+        out_specs=[VMEM] * ROW_BLOCKS,
         scratch_shapes=[
-            pltpu.VMEM((STEPS, D), jnp.bfloat16),
             pltpu.VMEM((CONTS, STEPS, D), jnp.bfloat16),
             pltpu.VMEM((1, D), jnp.float32),
             pltpu.VMEM((CTOK, D), jnp.float32),
-            pltpu.VMEM((ROW_BLOCKS, 16, TILE), jnp.float32),
-            pltpu.SemaphoreType.DMA((3,)),
+            pltpu.SemaphoreType.DMA((2,)),
         ],
         compiler_params=kernel_params(),
-        cost_estimate=cost(10**6, 4 * 10**6),
-        name="norm_rows",
-    )(in_hbm(main), in_hbm(cont), in_hbm(gain))
+        cost_estimate=cost(10**6, 5 * 10**6),
+        name="norm_cont",
+    )(in_hbm(cont), in_hbm(gain), after)
 
 
 def weight_tile(n, tiles, w_hbm, w_ref, sems):
@@ -115,15 +139,11 @@
 
 
 REST = 768
+CONT_LANES = QKV // COL_BLOCKS + REST
 
 
 def rest_tile(block):
     return jnp.where(block == 6, 2, 0)
-
-
-def plane_place():
-    column = lax.rem(lax.axis_index("tp"), COL_BLOCKS)
-    return column // 4, lax.rem(column, 4)
 
 
 def product_kernel(tiles, counts, places, *refs):
@@ -191,12 +211,12 @@
         ]
         + ([pltpu.VMEM(part, jnp.bfloat16)] if places else []),
         compiler_params=kernel_params(),
-        cost_estimate=cost(2 * members * CTOK * FEATURES * tiles * TILE, 12 * 10**6),
+        cost_estimate=cost(2 * members * CTOK * FEATURES * tiles * TILE, 14 * 10**6),
         name="block_product",
     )(*messages, *earlier, in_hbm(blocks))
 
 
-def main_kernel(tiles, x_ref, w_hbm, out_ref, rows_ref, wide_ref, w_ref, sems):
+def main_kernel(tiles, x_ref, w_hbm, after_ref, out_ref, rows_ref, wide_ref, w_ref, sems):
     n = pl.program_id(0)
     members = x_ref.shape[0]
     lines = members * STEPS
@@ -231,13 +251,13 @@
             out_ref[:, :, k * 128 : (k + 1) * 128] = packed
 
 
-def main_product(rows, blocks):
+def main_product(rows, blocks, after):
     tiles = blocks.shape[2] // TILE
     return pl.pallas_call(
         functools.partial(main_kernel, tiles),
         out_shape=jax.ShapeDtypeStruct(rows.shape, jnp.bfloat16),
         grid=(tiles,),
-        in_specs=[VMEM, HBM],
+        in_specs=[VMEM, HBM, UNREAD],
         out_specs=VMEM,
         scratch_shapes=[
             pltpu.VMEM((MEMBERS * STEPS, FEATURES), jnp.bfloat16),
@@ -246,9 +266,9 @@
             pltpu.SemaphoreType.DMA((tiles,)),
         ],
         compiler_params=kernel_params(),
-        cost_estimate=cost(3 * 10**8, 6 * 10**6),
+        cost_estimate=cost(3 * 10**8, 13 * 10**6),
         name="main_product",
-    )(rows, in_hbm(blocks))
+    )(rows, in_hbm(blocks), after)
 
 
 def gather_kernel(own_ref, ahead1_ref, ahead2_ref, ahead3_ref, out_ref):
@@ -340,8 +360,9 @@
 
 
 def attend_main_kernel(
-    len_ref, bias_ref, cos_ref, sin_ref, cache_ref, parts_ref, out_ref, kv_ref, qkv_ref, piece_ref
+    len_ref, bias_ref, cos_ref, sin_ref, cache_ref, parts_ref, *refs
 ):
+    out_ref, kv_ref, qkv_ref, piece_ref = refs[-4:]
     rows = qkv_ref.shape[0]
     qkv_ref[...] = jnp.zeros(qkv_ref.shape, jnp.float32)
     load_qkv(True, parts_ref, qkv_ref)
@@ -374,28 +395,43 @@
             out_ref[r * COL_BLOCKS + c] = piece
 
 
-def attend_main(prefix_len, bias, cosine, sine, cache, parts):
+def attend_main(prefix_len, bias, cosine, sine, cache, parts, after):
     return pl.pallas_call(
         attend_main_kernel,
         out_shape=(
             jax.ShapeDtypeStruct((32, 16, TILE), jnp.bfloat16),
             jax.ShapeDtypeStruct((8, 2 * KV_WIDTH), jnp.float32),
         ),
-        in_specs=[SMEM] + [VMEM] * 5,
+        in_specs=[SMEM] + [VMEM] * 5 + [UNREAD] * len(after),
         out_specs=(whole((32, 16, TILE)), whole((8, 2 * KV_WIDTH))),
         scratch_shapes=[
             pltpu.VMEM((8, QKV), jnp.float32),
             pltpu.VMEM((ROW_BLOCKS, 16, TILE), jnp.float32),
         ],
         compiler_params=kernel_params(),
-        cost_estimate=cost(2 * 10**8, 6 * 10**6),
+        cost_estimate=cost(2 * 10**8, 13 * 10**6),
         name="attend_main",
-    )(prefix_len, bias, cosine, sine, cache, parts)
-
-
-def attend_cont_kernel(
-    len_ref, bound_ref, bias_ref, cos_ref, sin_ref, cache_ref, kv_ref, parts_ref, out_ref, qkv_ref
+    )(prefix_len, bias, cosine, sine, cache, parts, *after)
+
+
+def last_kernel(
+    len_ref, bound_ref, bias_ref, cos_ref, sin_ref, cache_ref, kv_ref, parts_ref, main_ref, cont_ref, head_ref,
+    out_ref, score_ref, qkv_ref, wide_ref, read_ref,
 ):
+    out_cols = D // COL_BLOCKS
+    for c in range(COL_BLOCKS):
+        total = summed_block(parts_ref, c, slice(CONT_LANES, CONT_LANES + TILE))
+        total = total[:8] + total[8:]
+        for j in range(out_cols // TILE):
+            at = slice(c * out_cols + j * TILE, c * out_cols + (j + 1) * TILE)
+            for s in range(STEPS):
+                wide_ref[s : s + 1, at] = total[s * 4 + j : s * 4 + j + 1]
+    out_ref[...] = (main_ref[...].astype(jnp.float32) + wide_ref[:STEPS, :]).astype(jnp.bfloat16)
+    for r in range(ROW_BLOCKS):
+        read = parts_ref[r * COL_BLOCKS, :, CONT_LANES + TILE :].astype(jnp.float32)
+        for c in range(1, COL_BLOCKS):
+            read = read + parts_ref[r * COL_BLOCKS + c, :, CONT_LANES + TILE :].astype(jnp.float32)
+        read_ref[r] = read[:8] + read[8:]
     rows = qkv_ref.shape[0]
     load_qkv(False, parts_ref, qkv_ref)
     plain, rotated = head_readers(qkv_ref, bias_ref, cos_ref, sin_ref)
@@ -405,6 +441,8 @@
     own = (row // STEPS == col // STEPS) & (col <= row)
     main = (col >= rows) & (col < rows + bound_ref[0])
     fresh_seen = jnp.concatenate([(own | main).astype(jnp.int32)] * GROUP, axis=0) > 0
+    score = jnp.zeros((rows, HD), jnp.float32)
+    direct = jnp.zeros((STEPS, HD), jnp.float32)
     for g in range(KVH):
         query = jnp.concatenate([rotated((g * GROUP + h) * HD) for h in range(GROUP)], axis=0).astype(jnp.bfloat16)
         at_key = slice(g * HD, (g + 1) * HD)
@@ -414,20 +452,35 @@
         mixed = head_attention(
             query, cache_ref[:, at_key], cache_ref[:, at_value], fresh_key, fresh_value, seen, fresh_seen
         )
-        mixed = mixed.astype(jnp.bfloat16)
+        mixed = mixed.astype(jnp.bfloat16).astype(jnp.float32)
         for h in range(GROUP):
-            out_ref[:, (g * GROUP + h) * HD : (g * GROUP + h + 1) * HD] = mixed[h * rows : (h + 1) * rows]
-
-
-def attend_cont(*args):
-    return pl.pallas_call(
-        attend_cont_kernel,
-        out_shape=jax.ShapeDtypeStruct((CTOK, D), jnp.bfloat16),
-        in_specs=[SMEM, SMEM] + [VMEM] * 6,
-        out_specs=whole((CTOK, D)),
-        scratch_shapes=[pltpu.VMEM((CTOK, QKV), jnp.float32)],
-        compiler_params=kernel_params(),
-        cost_estimate=cost(4 * 10**8, 8 * 10**6),
+            head = g * GROUP + h
+            r, place = divmod(head, FEATURES // HD)
+            j, lane = place // 2, (place % 2) * HD
+            score = score + mixed[h * rows : (h + 1) * rows] * read_ref[r, j : j + 1, lane : lane + HD]
+            lanes = slice(head * HD, (head + 1) * HD)
+            for c in range(CONTS):
+                direct = direct + cont_ref[c, :, lanes].astype(jnp.float32) * head_ref[:, lanes]
+    total = jnp.sum(score, axis=0, keepdims=True) + jnp.sum(direct, axis=0, keepdims=True)
+    score_ref[...] = jnp.broadcast_to(jnp.sum(total, axis=1, keepdims=True) / CONTS, (8, 128))
+
+
+def last(*args):
+    return pl.pallas_call(
+        last_kernel,
+        out_shape=(
+            jax.ShapeDtypeStruct((STEPS, D), jnp.bfloat16),
+            jax.ShapeDtypeStruct((8, 128), jnp.float32),
+        ),
+        in_specs=[SMEM, SMEM] + [VMEM] * 9,
+        out_specs=(VMEM, VMEM),
+        scratch_shapes=[
+            pltpu.VMEM((CTOK, QKV), jnp.float32),
+            pltpu.VMEM((8, D), jnp.float32),
+            pltpu.VMEM((ROW_BLOCKS, 8, TILE), jnp.float32),
+        ],
+        compiler_params=kernel_params(),
+        cost_estimate=cost(4 * 10**8, 18 * 10**6),
         name="attend_cont",
     )(*args)
 
@@ -455,12 +508,17 @@
         out_specs=whole((1, FEATURES)),
         scratch_shapes=[pltpu.VMEM((FEATURES, D // COL_BLOCKS), jnp.bfloat16), pltpu.SemaphoreType.DMA],
         compiler_params=kernel_params(),
-        cost_estimate=cost(2 * 10**8, 5 * 10**6),
+        cost_estimate=cost(2 * 10**8, 12 * 10**6),
         name="readout",
     )(value_head, in_hbm(blocks))
 
 
-def out_kernel(tiles, x_ref, read_ref, w_hbm, out_ref, rows_ref, wide_ref, read8_ref, w_ref, sems):
+def split(wide):
+    high = wide.astype(jnp.bfloat16).astype(jnp.float32)
+    return jnp.concatenate([high, wide - high], axis=-2).astype(jnp.bfloat16)
+
+
+def out_kernel(tiles, x_ref, read_ref, cont_ref, w_hbm, out_ref, rows_ref, wide_ref, read8_ref, w_ref, sems):
     n = pl.program_id(0)
     members = x_ref.shape[0]
     lines = members * STEPS
@@ -469,9 +527,10 @@
 
     @pl.when(n == 0)
     def _():
+        out_ref[:, :, :CONT_LANES] = cont_ref[...]
         for j in range(FEATURES // TILE):
             read8_ref[j : j + 1, :] = read_ref[:, j * TILE : (j + 1) * TILE]
-        out_ref[:, 8:, :] = jnp.broadcast_to(read8_ref[...][None], (members, 8, TILE))
+        out_ref[:, :, CONT_LANES + TILE :] = jnp.broadcast_to(split(read8_ref[...])[None], (members, 16, TILE))
         packed = x_ref[...].reshape(members * 16, TILE).astype(jnp.float32)
         for k in range(halves):
             wide_ref[k] = packed[:, k * 128 : (k + 1) * 128]
@@ -487,19 +546,19 @@
     @pl.when(n == tiles - 1)
     def _():
         for k in range(halves):
-            packed = wide_ref[k, : members * 8, :].reshape(members, 8, 128)
-            out_ref[:, :8, k * 128 : (k + 1) * 128] = packed
-
-
-def out_product(rows, read, blocks):
+            lane = CONT_LANES + k * 128
+            out_ref[:, :, lane : lane + 128] = split(wide_ref[k, : members * 8, :].reshape(members, 8, 128))
+
+
+def out_product(rows, read, cont_parts, blocks):
     members = rows.shape[0]
     tiles = blocks.shape[2] // TILE
     return pl.pallas_call(
         functools.partial(out_kernel, tiles),
-        out_shape=jax.ShapeDtypeStruct((members, 16, TILE), jnp.float32),
+        out_shape=jax.ShapeDtypeStruct((members, CTOK, CONT_LANES + 2 * TILE), jnp.bfloat16),
         grid=(tiles,),
-        in_specs=[whole(rows.shape), whole(read.shape), HBM],
-        out_specs=whole((members, 16, TILE)),
+        in_specs=[VMEM, VMEM, VMEM, HBM],
+        out_specs=VMEM,
         scratch_shapes=[
             pltpu.VMEM((members * STEPS, FEATURES), jnp.bfloat16),
             pltpu.VMEM((TILE // 128, members * 16, 128), jnp.float32),
@@ -508,49 +567,9 @@
             pltpu.SemaphoreType.DMA((tiles,)),
         ],
         compiler_params=kernel_params(),
-        cost_estimate=cost(3 * 10**8, 5 * 10**6),
+        cost_estimate=cost(3 * 10**8, 8 * 10**6),
         name="out_product",
-    )(rows, read, in_hbm(blocks))
-
-
-def finish_kernel(parts_ref, main_ref, cont_ref, head_ref, mixed_ref, out_ref, score_ref, wide_ref):
-    cols = D // COL_BLOCKS
-    for c in range(COL_BLOCKS):
-        total = summed_block(parts_ref, c, slice(0, TILE))
-        for j in range(cols // TILE):
-            at = slice(c * cols + j * TILE, c * cols + (j + 1) * TILE)
-            for s in range(STEPS):
-                wide_ref[s : s + 1, at] = total[s * 4 + j : s * 4 + j + 1]
-    out_ref[...] = (main_ref[...].astype(jnp.float32) + wide_ref[:STEPS, :]).astype(jnp.bfloat16)
-    score = jnp.zeros((CTOK, TILE), jnp.float32)
-    direct = jnp.zeros((STEPS, TILE), jnp.float32)
-    for r in range(ROW_BLOCKS):
-        read = parts_ref[r * COL_BLOCKS, 8:, :]
-        for c in range(1, COL_BLOCKS):
-            read = read + parts_ref[r * COL_BLOCKS + c, 8:, :]
-        for j in range(FEATURES // TILE):
-            lanes = slice(r * FEATURES + j * TILE, r * FEATURES + (j + 1) * TILE)
-            score = score + mixed_ref[:, lanes].astype(jnp.float32) * read[j : j + 1, :]
-            for c in range(CONTS):
-                direct = direct + cont_ref[c, :, lanes].astype(jnp.float32) * head_ref[:, lanes]
-    total = jnp.sum(score, axis=0, keepdims=True) + jnp.sum(direct, axis=0, keepdims=True)
-    score_ref[...] = jnp.broadcast_to(jnp.sum(total, axis=1, keepdims=True) / CONTS, (8, 128))
-
-
-def finish(parts, main, cont, head, mixed):
-    return pl.pallas_call(
-        finish_kernel,
-        out_shape=(
-            jax.ShapeDtypeStruct((STEPS, D), jnp.bfloat16),
-            jax.ShapeDtypeStruct((8, 128), jnp.float32),
-        ),
-        in_specs=[whole(parts.shape), whole(main.shape), whole(cont.shape), whole(head.shape), whole(mixed.shape)],
-        out_specs=(whole((STEPS, D)), whole((8, 128))),
-        scratch_shapes=[pltpu.VMEM((8, D), jnp.float32)],
-        compiler_params=kernel_params(),
-        cost_estimate=cost(10**6, 2 * 10**6),
-        name="finish",
-    )(parts, main, cont, head, mixed)
+    )(rows, read, cont_parts, in_hbm(blocks))
 
 
 def rope_tables(positions):
@@ -579,19 +598,21 @@
     return lax.ppermute(rows, "tp", route)
 
 
-def project(rows, blocks):
+def ring(rows):
     near = gather_along([rows[0]] + [from_along(rows[ROW_BLOCKS - k], k) for k in range(1, ROW_BLOCKS)])
     half = ROW_BLOCKS // 2
     over = from_side(near, 1, 0)
-    here, far, places = [], [], []
-    for dy, mine in ((0, near), (1, over)):
+    here, far = [], []
+    for mine in (near, over):
         after = from_side(mine, 0, 1)
         before = from_side(mine, 0, 3)
         far += [from_side(before[:half], 0, 3), from_side(after[half:], 0, 1)]
         here += [mine, after, before]
-        places += [(dy, 0), (dy, 1), (dy, 3)]
-    earlier = block_product(here, blocks)
-    return exchange(block_product(far, blocks, (earlier,), tuple(places) + ((0, 2), (1, 2))))
+    return here, far
+
+
+HERE = ((0, 0), (0, 1), (0, 3), (1, 0), (1, 1), (1, 3))
+FAR = ((0, 2), (1, 2))
 
 
 def on_device(
@@ -606,14 +627,18 @@
     main_tables = rope_tables(prefix_len + step[:8])
     cont_tables = rope_tables(prefix_len + boundary + step)
     read = readout(value_head.reshape(COL_BLOCKS, D // COL_BLOCKS), w_out)
-    *rows, main_rows = norm_rows(main, cont, rms_gain[None, :])
-    main_parts = exchange(main_product(exchange(main_rows), w_qkv))
-    parts = project(rows, w_qkv)
-    mixed, main_kv = attend_main(prefix_len, bias, *main_tables, cache, main_parts)
+    gain = rms_gain[None, :]
+    main_rows = norm_main(main, gain)
+    here, far = ring(norm_cont(cont, gain, main_rows))
+    main_parts = exchange(main_product(exchange(main_rows), w_qkv, here[0]))
+    mixed, main_kv = attend_main(prefix_len, bias, *main_tables, cache, main_parts, here)
+    mixed, far = lax.optimization_barrier((mixed, far))
     mixed = exchange(mixed)
-    cont_mixed = attend_cont(prefix_len, boundary, bias, *cont_tables, cache, main_kv, parts)
-    parts = exchange(out_product(mixed, read, w_out))
-    main_out, score = finish(parts, main, cont, head, cont_mixed)
+    cont_parts = block_product(far, w_qkv, (block_product(here, w_qkv),), HERE + FAR)
+    parts = exchange(out_product(mixed, read, cont_parts, w_out))
+    main_out, score = last(
+        prefix_len, boundary, bias, *cont_tables, cache, main_kv, parts, main, cont, head
+    )
     return main_out[None], score[0, :1]
 
 

time: 117 us -> 122 us (1.043)
  waiting for transfers between devices: 31.8 us -> 34.2 us
  starting transfers between devices: 47.6 us -> 49.8 us
    ppermute x9, waiting for transfers between devices: 1.61 us -> 4.54 us  [from_side(): return lax.ppermute(rows, 'tp', route)]
    slice x4, local copies, waits for them, and re-layouts: 0.04 us -> 2.62 us  [ring(): far += [from_side(before[:half], 0, 3), from_side(after[half:], 0, 1)]]
    unnamed x22 -> x18, local copies, waits for them, and re-layouts: 5.28 us -> 2.74 us
    all_to_all x5 -> x4, starting transfers between devices: 28.4 us -> 30.6 us  [exchange(): return lax.all_to_all(rows, 'tp', split_axis=0, concat_axis=0, tiled=True)]
    all_to_all x5 -> x4, waiting for transfers between devices: 30.2 us -> 29.7 us  [exchange(): return lax.all_to_all(rows, 'tp', split_axis=0, concat_axis=0, tiled=True)]
  transfers between devices with their start and end apart: 17 -> 16, of which waited for: 5 -> 3; matrix products, arithmetic and copies ran while one was open for 0% -> 3% of each run, Pallas kernels for 21% -> 15%
where the time goes in v8:
time: 122 us; the launch traced here: 121 us
  starting transfers between devices  49.8 us (41%)
  waiting for transfers between devices  34.2 us (28%)
  Pallas kernels  27.7 us (23%)
  local copies, waits for them, and re-layouts  6.64 us (5%)
  between operations  2.18 us (2%)
    all_to_all x4, starting transfers between devices, exchange(): return lax.all_to_all(rows, 'tp', split_axis=0, concat_axis=0, tiled=True)  30.6 us
    all_to_all x4, waiting for transfers between devices, exchange(): return lax.all_to_all(rows, 'tp', split_axis=0, concat_axis=0, tiled=True)  29.7 us
    ppermute x9, starting transfers between devices, from_side(): return lax.ppermute(rows, 'tp', route)  13.8 us
    pallas_call x2, Pallas kernels, block_product(): pl.pallas_call(functools.partial(product_kernel, tiles, counts, places),...  7.45 us
    ppermute x3, starting transfers between devices, from_along(): return lax.ppermute(rows, 'tp', route)  5.45 us
    ppermute x9, waiting for transfers between devices, from_side(): return lax.ppermute(rows, 'tp', route)  4.54 us
    pallas_call x1, Pallas kernels, main_product(): pl.pallas_call(functools.partial(main_kernel, tiles), out_shape=jax.Shape...  3.72 us
    pallas_call x1, Pallas kernels, last(): pl.pallas_call(last_kernel, out_shape=(jax.ShapeDtypeStruct((STEPS, D), j...  3.72 us
  transfers between devices with their start and end apart: 16, of which 3 were waited for; matrix products, arithmetic and copies ran while one was open for 3% of the time, Pallas kernels for 15%

profile of v8, /device:TPU:0, one launch (start us, length us, event | category | flops | bytes accessed | tf_op | source)
XLA Modules:
  0.0 121.0 jit_solution(12750125119212956759)
XLA Ops:
  0.6 1.7 %norm_main.1.after_ref = bf16[32,16,256]{2,1,0:T(8,128)(2,1)} custom-call(bf16[2,8192]{1,0:T(2,128)(2,1)} %bitcast.17, f32[1,8192]{1,0:T(1,128)} %bitcast.20), custom_call_target="tpu_custom_call" | custom-call | flops 1000000 | bytes 4000000 | tf_op jit(solution)/shard_map/norm_main/pallas_call | solution.py:79
  2.3 1.4 %norm_cont.1 = (bf16[16,2048]{1,0:T(8,128)(2,1)S(1)}, bf16[16,2048]{1,0:T(8,128)(2,1)S(1)}, bf16[16,2048]{1,0:T(8,128)(2,1)S(1)}, bf16[16,2048]{1,0:T(8,128)(2,1)S(1)}) custom-call(bf16[8,2,8192]{2,1,0:T(2,128)(2,1)} %bitcast.13, f32[1,8192]{1,0:T(1,128)} %bitcast.21, bf16[32,16,256]{2,1,0:T(8,128)(2,1)} %norm_main.1.after_ref), custom_call_target="tpu_custom_call" | custom-call | flops 1000000 | bytes 5000000 | tf_op jit(solution)/shard_map/norm_cont/pallas_call | solution.py:111
  3.7 4.2 %collective-permute-start = (bf16[16,2048]{1,0:T(8,128)(2,1)S(1)}, bf16[16,2048]{1,0:T(8,128)(2,1)S(1)}, u32[]{:S(2)}, u32[]{:S(2)}) collective-permute-start(bf16[16,2048]{1,0:T(8,128)(2,1)S(1)} %get-tuple-element.16), channel_id=1, source_target_pairs={{8,0},{9,1},{10,2},{11,3},{12,4},{13,5},{14,6},{15,7},{16,8},{17,9... | collective-permute-start | bytes 196616 | tf_op jit(solution)/shard_map/ppermute | solution.py:598
  7.9 1.3 %collective-permute-start.2 = (bf16[16,2048]{1,0:T(8,128)(2,1)S(1)}, bf16[16,2048]{1,0:T(8,128)(2,1)S(1)}, u32[]{:S(2)}, u32[]{:S(2)}) collective-permute-start(bf16[16,2048]{1,0:T(8,128)(2,1)S(1)} %get-tuple-element.18), channel_id=1, source_target_pairs={{24,0},{25,1},{26,2},{27,3},{28,4},{29,5},{30,6},{31,7},{0,8},{1,9... | collective-permute-start | bytes 196616 | tf_op jit(solution)/shard_map/ppermute | solution.py:598
  9.2 7.4 %all-to-all-start = ((bf16[32,16,256]{2,1,0:T(8,128)(2,1)}), bf16[32,16,256]{2,1,0:T(8,128)(2,1)S(1)}, u32[]{:S(2)}, u32[]{:S(2)}) async-start(bf16[32,16,256]{2,1,0:T(8,128)(2,1)} %norm_main.1.after_ref), calls=%async_computation | async-start | bytes 524288 | tf_op jit(solution)/shard_map/all_to_all | solution.py:585
  16.7 1.9 %collective-permute-start.5 = (bf16[4,16,2048]{2,1,0:T(8,128)(2,1)S(1)}, bf16[4,16,2048]{2,1,0:T(8,128)(2,1)S(1)}, u32[]{:S(2)}, u32[]{:S(2)}) collective-permute-start(bf16[4,16,2048]{2,1,0:T(8,128)(2,1)S(1)} %gather_along.1.after_ref.refs_0_), channel_id=1, source_target_pairs={{4,0},{5,1},{6,2},{7,3},{0,4},{1,5},{2,6},{3,7},{12,8},{13,9},{14,... | collective-permute-start | bytes 786440 | tf_op jit(solution)/shard_map/ppermute | solution.py:593
  19.2 2.7 %collective-permute-start.3 = (bf16[4,16,2048]{2,1,0:T(8,128)(2,1)S(1)}, bf16[4,16,2048]{2,1,0:T(8,128)(2,1)S(1)}, u32[]{:S(2)}, u32[]{:S(2)}) collective-permute-start(bf16[4,16,2048]{2,1,0:T(8,128)(2,1)S(1)} %gather_along.1.after_ref.refs_0_), channel_id=1, source_target_pairs={{1,0},{2,1},{3,2},{0,3},{5,4},{6,5},{7,6},{4,7},{9,8},{10,9},{11,1... | collective-permute-start | bytes 786440 | tf_op jit(solution)/shard_map/ppermute | solution.py:593
  22.0 4.5 %collective-permute-done.5.refs_3_ = bf16[4,16,2048]{2,1,0:T(8,128)(2,1)S(1)} collective-permute-done((bf16[4,16,2048]{2,1,0:T(8,128)(2,1)S(1)}, bf16[4,16,2048]{2,1,0:T(8,128)(2,1)S(1)}, u32[]{:S(2)}, u32[]{:S(2)}) %collective-permute-start.5) | collective-permute-done | bytes 262176 | tf_op jit(solution)/shard_map/ppermute | solution.py:593
  26.5 2.7 %collective-permute-start.6 = (bf16[4,16,2048]{2,1,0:T(8,128)(2,1)S(1)}, bf16[4,16,2048]{2,1,0:T(8,128)(2,1)S(1)}, u32[]{:S(2)}, u32[]{:S(2)}) collective-permute-start(bf16[4,16,2048]{2,1,0:T(8,128)(2,1)S(1)} %collective-permute-done.5.refs_3_), channel_id=1, source_target_pairs={{1,0},{2,1},{3,2},{0,3},{5,4},{6,5},{7,6},{4,7},{9,8},{10,9},{11,1... | collective-permute-start | bytes 786440 | tf_op jit(solution)/shard_map/ppermute | solution.py:593
  30.0 3.7 %main_product.1 = bf16[32,16,256]{2,1,0:T(8,128)(2,1)} custom-call(bf16[32,16,256]{2,1,0:T(8,128)(2,1)S(1)} %all-to-all-done.x_ref, bf16[1,2048,1280]{2,1,0:T(8,128)(2,1)} %refs_5_.1, bf16[4,16,2048]{2,1,0:T(8,128)(2,1)S(1)} %gather_along.1.after_ref.refs_0_), custom_call_target="tpu_custom_call" | custom-call | flops 300000000 | bytes 13000000 | tf_op jit(solution)/shard_map/main_product/pallas_call | solution.py:256
  33.7 7.6 %all-to-all-start.1 = ((bf16[32,16,256]{2,1,0:T(8,128)(2,1)}), bf16[32,16,256]{2,1,0:T(8,128)(2,1)S(1)}, u32[]{:S(2)}, u32[]{:S(2)}) async-start(bf16[32,16,256]{2,1,0:T(8,128)(2,1)} %main_product.1), calls=%async_computation.1 | async-start | bytes 524288 | tf_op jit(solution)/shard_map/all_to_all | solution.py:585
  42.1 1.8 %collective-permute-start.8 = (bf16[2,16,2048]{2,1,0:T(8,128)(2,1)}, bf16[2,16,2048]{2,1,0:T(8,128)(2,1)S(1)}, u32[]{:S(2)}, u32[]{:S(2)}) collective-permute-start(bf16[2,16,2048]{2,1,0:T(8,128)(2,1)} %slice.24), channel_id=1, source_target_pairs={{3,0},{0,1},{1,2},{2,3},{7,4},{4,5},{5,6},{6,7},{11,8},{8,9},{9,10... | collective-permute-start | bytes 393224 | tf_op jit(solution)/shard_map/ppermute | solution.py:593
  44.6 1.4 %collective-permute-start.9 = (bf16[2,16,2048]{2,1,0:T(8,128)(2,1)}, bf16[2,16,2048]{2,1,0:T(8,128)(2,1)S(1)}, u32[]{:S(2)}, u32[]{:S(2)}) collective-permute-start(bf16[2,16,2048]{2,1,0:T(8,128)(2,1)} %slice.25), channel_id=1, source_target_pairs={{1,0},{2,1},{3,2},{0,3},{5,4},{6,5},{7,6},{4,7},{9,8},{10,9},{11,1... | collective-permute-start | bytes 393224 | tf_op jit(solution)/shard_map/ppermute | solution.py:593
  47.9 2.7 %collective-permute-start.11 = (bf16[2,16,2048]{2,1,0:T(8,128)(2,1)}, bf16[2,16,2048]{2,1,0:T(8,128)(2,1)S(1)}, u32[]{:S(2)}, u32[]{:S(2)}) collective-permute-start(bf16[2,16,2048]{2,1,0:T(8,128)(2,1)} %slice.27), channel_id=1, source_target_pairs={{1,0},{2,1},{3,2},{0,3},{5,4},{6,5},{7,6},{4,7},{9,8},{10,9},{11,1... | collective-permute-start | bytes 393224 | tf_op jit(solution)/shard_map/ppermute | solution.py:593
  51.4 3.7 %attend_main.1 = (bf16[32,16,256]{2,1,0:T(8,128)(2,1)}, f32[8,2048]{1,0:T(8,128)S(1)}) custom-call(s32[1]{0:T(128)} %copy.12.len_ref, f32[1,10240]{1,0:T(1,128)S(1)} %bitcast.15, f32[8,128]{1,0:T(8,128)S(1)} %get-tuple-element.36.cos_ref, f32[8,128]{1,0:T(8,128)S(1)} %get-tuple-element.37.sin_ref, bf16[256,2048]{1,0:T(8,128)(2,1)S(1)} %bitcast.11, ...), custom_call_target="tpu_custom_call" | custom-call | flops 200000000 | bytes 13000000 | tf_op jit(solution)/shard_map/attend_main/pallas_call | solution.py:399
  55.1 7.1 %all-to-all-start.2 = ((bf16[32,16,256]{2,1,0:T(8,128)(2,1)}), bf16[32,16,256]{2,1,0:T(8,128)(2,1)S(1)}, u32[]{:S(2)}, u32[]{:S(2)}) async-start(bf16[32,16,256]{2,1,0:T(8,128)(2,1)} %get-tuple-element.21), calls=%async_computation.2 | async-start | bytes 524288 | tf_op jit(solution)/shard_map/all_to_all | solution.py:585
  62.3 3.4 %readout.1.read_ref = f32[1,2048]{1,0:T(1,128)S(1)} custom-call(f32[8,1024]{1,0:T(8,128)S(1)} %reshape.34.head_ref, bf16[1,2048,1024]{2,1,0:T(8,128)(2,1)} %w_hbm.5), custom_call_target="tpu_custom_call" | custom-call | flops 200000000 | bytes 12000000 | tf_op jit(solution)/shard_map/readout/pallas_call | solution.py:504
  65.7 4.3 %block_product.2.refs_4_ = bf16[24,16,2048]{2,1,0:T(8,128)(2,1)S(1)} custom-call(bf16[4,16,2048]{2,1,0:T(8,128)(2,1)S(1)} %gather_along.1.after_ref.refs_0_, bf16[4,16,2048]{2,1,0:T(8,128)(2,1)S(1)} %collective-permute-done.3.refs_1_, bf16[4,16,2048]{2,1,0:T(8,128)(2,1)S(1)} %collective-permute-done.4.refs_2_, ...), custom_call_target="tpu_custom_call" | custom-call | flops 2013265920 | bytes 14000000 | tf_op jit(solution)/shard_map/block_product/pallas_call | solution.py:201
  70.0 3.1 %block_product.3.cont_ref = bf16[32,16,2048]{2,1,0:T(8,128)(2,1)S(1)} custom-call(bf16[2,16,2048]{2,1,0:T(8,128)(2,1)S(1)} %collective-permute-done.8.refs_0_, bf16[2,16,2048]{2,1,0:T(8,128)(2,1)S(1)} %collective-permute-done.9.refs_1_, bf16[2,16,2048]{2,1,0:T(8,128)(2,1)S(1)} %collective-permute-done.10.refs_2_, ...), custom_call_target="tpu_custom_call" | custom-call | flops 671088640 | bytes 14000000 | tf_op jit(solution)/shard_map/block_product/pallas_call | solution.py:201
  73.2 2.6 %out_product.1 = bf16[32,16,2560]{2,1,0:T(8,128)(2,1)S(1)} custom-call(bf16[32,16,256]{2,1,0:T(8,128)(2,1)S(1)} %all-to-all-done.2.x_ref, f32[1,2048]{1,0:T(1,128)S(1)} %readout.1.read_ref, bf16[32,16,2048]{2,1,0:T(8,128)(2,1)S(1)} %block_product.3.cont_ref, bf16[1,2048,1024]{2,1,0:T(8,128)(2,1)} %w_hbm.5), custom_call_target="tpu_custom_call" | custom-call | flops 300000000 | bytes 8000000 | tf_op jit(solution)/shard_map/out_product/pallas_call | solution.py:556
  75.8 1.5 %copy-done = bf16[32,16,2560]{2,1,0:T(8,128)(2,1)} copy-done((bf16[32,16,2560]{2,1,0:T(8,128)(2,1)}, bf16[32,16,2560]{2,1,0:T(8,128)(2,1)S(1)}, u32[]{:S(2)}) %copy-start) | copy-done | bytes 2621464
  77.3 8.4 %all-to-all-start.3 = ((bf16[32,16,2560]{2,1,0:T(8,128)(2,1)}), bf16[32,16,2560]{2,1,0:T(8,128)(2,1)S(1)}, u32[]{:S(2)}, u32[]{:S(2)}) async-start(bf16[32,16,2560]{2,1,0:T(8,128)(2,1)} %copy-done), calls=%async_computation.3 | async-start | bytes 5242880 | tf_op jit(solution)/shard_map/all_to_all | solution.py:585
  86.6 28.9 %all-to-all-done.3.parts_ref = bf16[32,16,2560]{2,1,0:T(8,128)(2,1)S(1)} async-done(((bf16[32,16,2560]{2,1,0:T(8,128)(2,1)}), bf16[32,16,2560]{2,1,0:T(8,128)(2,1)S(1)}, u32[]{:S(2)}, u32[]{:S(2)}) %all-to-all-start.3) | async-done | bytes 2621472 | tf_op jit(solution)/shard_map/all_to_all | solution.py:585
  116.8 3.7 %attend_cont.1 = (bf16[2,8192]{1,0:T(2,128)(2,1)}, f32[8,128]{1,0:T(8,128)S(1)}) custom-call(s32[1]{0:T(128)} %copy.12.len_ref, s32[1]{0:T(128)S(6)} %copy.13.bound_ref, f32[1,10240]{1,0:T(1,128)S(1)} %bitcast.16, f32[16,128]{1,0:T(8,128)S(1)} %get-tuple-element.34.cos_ref, f32[16,128]{1,0:T(8,128)S(1)} %get-tuple-element.35.sin_ref, ...), custom_call_target="tpu_custom_call" | custom-call | flops 400000000 | bytes 18000000 | tf_op jit(solution)/shard_map/attend_cont/pallas_call | solution.py:469
  (50 shorter events, 7.0 us)
Async XLA Ops:
  3.7 12.9 %collective-permute-start = (bf16[16,2048]{1,0:T(8,128)(2,1)S(1)}, bf16[16,2048]{1,0:T(8,128)(2,1)S(1)}, u32[]{:S(2)}, u32[]{:S(2)}) collective-permute-start(bf16[16,2048]{1,0:T(8,128)(2,1)S(1)} %get-tuple-element.16), channel_id=1, source_target_pairs={{8,0},{9,1},{10,2},{11,3},{12,4},{13,5},{14,6},{15,7},{16,8},{17,9... | collective-permute-start | bytes 196616 | tf_op jit(solution)/shard_map/ppermute | solution.py:598
  7.9 8.7 %collective-permute-start.1 = (bf16[16,2048]{1,0:T(8,128)(2,1)S(1)}, bf16[16,2048]{1,0:T(8,128)(2,1)S(1)}, u32[]{:S(2)}, u32[]{:S(2)}) collective-permute-start(bf16[16,2048]{1,0:T(8,128)(2,1)S(1)} %get-tuple-element.17), channel_id=1, source_target_pairs={{16,0},{17,1},{18,2},{19,3},{20,4},{21,5},{22,6},{23,7},{24,8},{25... | collective-permute-start | bytes 196616 | tf_op jit(solution)/shard_map/ppermute | solution.py:598
  7.9 8.7 %collective-permute-start.2 = (bf16[16,2048]{1,0:T(8,128)(2,1)S(1)}, bf16[16,2048]{1,0:T(8,128)(2,1)S(1)}, u32[]{:S(2)}, u32[]{:S(2)}) collective-permute-start(bf16[16,2048]{1,0:T(8,128)(2,1)S(1)} %get-tuple-element.18), channel_id=1, source_target_pairs={{24,0},{25,1},{26,2},{27,3},{28,4},{29,5},{30,6},{31,7},{0,8},{1,9... | collective-permute-start | bytes 196616 | tf_op jit(solution)/shard_map/ppermute | solution.py:598
  9.2 20.8 %all-to-all-start = ((bf16[32,16,256]{2,1,0:T(8,128)(2,1)}), bf16[32,16,256]{2,1,0:T(8,128)(2,1)S(1)}, u32[]{:S(2)}, u32[]{:S(2)}) async-start(bf16[32,16,256]{2,1,0:T(8,128)(2,1)} %norm_main.1.after_ref), calls=%async_computation | async-start | bytes 524288 | tf_op jit(solution)/shard_map/all_to_all | solution.py:585
  16.7 9.8 %collective-permute-start.5 = (bf16[4,16,2048]{2,1,0:T(8,128)(2,1)S(1)}, bf16[4,16,2048]{2,1,0:T(8,128)(2,1)S(1)}, u32[]{:S(2)}, u32[]{:S(2)}) collective-permute-start(bf16[4,16,2048]{2,1,0:T(8,128)(2,1)S(1)} %gather_along.1.after_ref.refs_0_), channel_id=1, source_target_pairs={{4,0},{5,1},{6,2},{7,3},{0,4},{1,5},{2,6},{3,7},{12,8},{13,9},{14,... | collective-permute-start | bytes 786440 | tf_op jit(solution)/shard_map/ppermute | solution.py:593
  19.2 24.7 %collective-permute-start.3 = (bf16[4,16,2048]{2,1,0:T(8,128)(2,1)S(1)}, bf16[4,16,2048]{2,1,0:T(8,128)(2,1)S(1)}, u32[]{:S(2)}, u32[]{:S(2)}) collective-permute-start(bf16[4,16,2048]{2,1,0:T(8,128)(2,1)S(1)} %gather_along.1.after_ref.refs_0_), channel_id=1, source_target_pairs={{1,0},{2,1},{3,2},{0,3},{5,4},{6,5},{7,6},{4,7},{9,8},{10,9},{11,1... | collective-permute-start | bytes 786440 | tf_op jit(solution)/shard_map/ppermute | solution.py:593
  22.0 19.5 %collective-permute-start.4 = (bf16[4,16,2048]{2,1,0:T(8,128)(2,1)S(1)}, bf16[4,16,2048]{2,1,0:T(8,128)(2,1)S(1)}, u32[]{:S(2)}, u32[]{:S(2)}) collective-permute-start(bf16[4,16,2048]{2,1,0:T(8,128)(2,1)S(1)} %gather_along.1.after_ref.refs_0_), channel_id=1, source_target_pairs={{3,0},{0,1},{1,2},{2,3},{7,4},{4,5},{5,6},{6,7},{11,8},{8,9},{9,10... | collective-permute-start | bytes 786440 | tf_op jit(solution)/shard_map/ppermute | solution.py:593
  26.5 20.8 %collective-permute-start.6 = (bf16[4,16,2048]{2,1,0:T(8,128)(2,1)S(1)}, bf16[4,16,2048]{2,1,0:T(8,128)(2,1)S(1)}, u32[]{:S(2)}, u32[]{:S(2)}) collective-permute-start(bf16[4,16,2048]{2,1,0:T(8,128)(2,1)S(1)} %collective-permute-done.5.refs_3_), channel_id=1, source_target_pairs={{1,0},{2,1},{3,2},{0,3},{5,4},{6,5},{7,6},{4,7},{9,8},{10,9},{11,1... | collective-permute-start | bytes 786440 | tf_op jit(solution)/shard_map/ppermute | solution.py:593
  29.2 16.9 %collective-permute-start.7 = (bf16[4,16,2048]{2,1,0:T(8,128)(2,1)S(1)}, bf16[4,16,2048]{2,1,0:T(8,128)(2,1)S(1)}, u32[]{:S(2)}, u32[]{:S(2)}) collective-permute-start(bf16[4,16,2048]{2,1,0:T(8,128)(2,1)S(1)} %collective-permute-done.5.refs_3_), channel_id=1, source_target_pairs={{3,0},{0,1},{1,2},{2,3},{7,4},{4,5},{5,6},{6,7},{11,8},{8,9},{9,10... | collective-permute-start | bytes 786440 | tf_op jit(solution)/shard_map/ppermute | solution.py:593
  29.2 12.2 %copy-start.7 = (f32[64]{0:T(128)}, f32[64]{0:T(128)S(1)}, u32[]{:S(2)}) copy-start(f32[64]{0:T(128)S(1)} %multiply_power_fusion) | copy-start | bytes 772
  30.0 21.5 %copy-start.1 = (bf16[1,256,2048]{2,1,0:T(8,128)(2,1)S(1)}, bf16[1,256,2048]{2,1,0:T(8,128)(2,1)}, u32[]{:S(2)}) copy-start(bf16[1,256,2048]{2,1,0:T(8,128)(2,1)} %param.12) | copy-start | bytes 3145732
  30.0 21.5 %copy-start.4 = (f32[10240]{0:T(1024)S(1)}, f32[10240]{0:T(1024)}, u32[]{:S(2)}) copy-start(f32[10240]{0:T(1024)} %param.16) | copy-start | bytes 122884
  33.7 17.7 %all-to-all-start.1 = ((bf16[32,16,256]{2,1,0:T(8,128)(2,1)}), bf16[32,16,256]{2,1,0:T(8,128)(2,1)S(1)}, u32[]{:S(2)}, u32[]{:S(2)}) async-start(bf16[32,16,256]{2,1,0:T(8,128)(2,1)} %main_product.1), calls=%async_computation.1 | async-start | bytes 524288 | tf_op jit(solution)/shard_map/all_to_all | solution.py:585
  42.1 13.0 %collective-permute-start.8 = (bf16[2,16,2048]{2,1,0:T(8,128)(2,1)}, bf16[2,16,2048]{2,1,0:T(8,128)(2,1)S(1)}, u32[]{:S(2)}, u32[]{:S(2)}) collective-permute-start(bf16[2,16,2048]{2,1,0:T(8,128)(2,1)} %slice.24), channel_id=1, source_target_pairs={{3,0},{0,1},{1,2},{2,3},{7,4},{4,5},{5,6},{6,7},{11,8},{8,9},{9,10... | collective-permute-start | bytes 393224 | tf_op jit(solution)/shard_map/ppermute | solution.py:593
  44.6 10.5 %collective-permute-start.9 = (bf16[2,16,2048]{2,1,0:T(8,128)(2,1)}, bf16[2,16,2048]{2,1,0:T(8,128)(2,1)S(1)}, u32[]{:S(2)}, u32[]{:S(2)}) collective-permute-start(bf16[2,16,2048]{2,1,0:T(8,128)(2,1)} %slice.25), channel_id=1, source_target_pairs={{1,0},{2,1},{3,2},{0,3},{5,4},{6,5},{7,6},{4,7},{9,8},{10,9},{11,1... | collective-permute-start | bytes 393224 | tf_op jit(solution)/shard_map/ppermute | solution.py:593
  46.7 8.4 %collective-permute-start.10 = (bf16[2,16,2048]{2,1,0:T(8,128)(2,1)}, bf16[2,16,2048]{2,1,0:T(8,128)(2,1)S(1)}, u32[]{:S(2)}, u32[]{:S(2)}) collective-permute-start(bf16[2,16,2048]{2,1,0:T(8,128)(2,1)} %slice.26), channel_id=1, source_target_pairs={{3,0},{0,1},{1,2},{2,3},{7,4},{4,5},{5,6},{6,7},{11,8},{8,9},{9,10... | collective-permute-start | bytes 393224 | tf_op jit(solution)/shard_map/ppermute | solution.py:593
  47.9 7.2 %collective-permute-start.11 = (bf16[2,16,2048]{2,1,0:T(8,128)(2,1)}, bf16[2,16,2048]{2,1,0:T(8,128)(2,1)S(1)}, u32[]{:S(2)}, u32[]{:S(2)}) collective-permute-start(bf16[2,16,2048]{2,1,0:T(8,128)(2,1)} %slice.27), channel_id=1, source_target_pairs={{1,0},{2,1},{3,2},{0,3},{5,4},{6,5},{7,6},{4,7},{9,8},{10,9},{11,1... | collective-permute-start | bytes 393224 | tf_op jit(solution)/shard_map/ppermute | solution.py:593
  55.1 18.0 %all-to-all-start.2 = ((bf16[32,16,256]{2,1,0:T(8,128)(2,1)}), bf16[32,16,256]{2,1,0:T(8,128)(2,1)S(1)}, u32[]{:S(2)}, u32[]{:S(2)}) async-start(bf16[32,16,256]{2,1,0:T(8,128)(2,1)} %get-tuple-element.21), calls=%async_computation.2 | async-start | bytes 524288 | tf_op jit(solution)/shard_map/all_to_all | solution.py:585
  75.8 1.5 %copy-start = (bf16[32,16,2560]{2,1,0:T(8,128)(2,1)}, bf16[32,16,2560]{2,1,0:T(8,128)(2,1)S(1)}, u32[]{:S(2)}) copy-start(bf16[32,16,2560]{2,1,0:T(8,128)(2,1)S(1)} %out_product.1) | copy-start | bytes 7864324
  77.3 9.1 %copy-start.8 = (f32[64]{0:T(128)S(1)}, f32[64]{0:T(128)}, u32[]{:S(2)}) copy-start(f32[64]{0:T(128)} %copy-done.7) | copy-start | bytes 772
  77.3 38.2 %copy-start.3 = (bf16[1,8,2,8192]{3,2,1,0:T(2,128)(2,1)S(1)}, bf16[1,8,2,8192]{3,2,1,0:T(2,128)(2,1)}, u32[]{:S(2)}) copy-start(bf16[1,8,2,8192]{3,2,1,0:T(2,128)(2,1)} %param.11) | copy-start | bytes 786436
  77.3 38.2 %copy-start.5 = (bf16[1,2,8192]{2,1,0:T(2,128)(2,1)S(1)}, bf16[1,2,8192]{2,1,0:T(2,128)(2,1)}, u32[]{:S(2)}) copy-start(bf16[1,2,8192]{2,1,0:T(2,128)(2,1)} %param.10) | copy-start | bytes 98308
  77.3 38.2 %copy-start.6 = (f32[8192]{0:T(1024)S(1)}, f32[8192]{0:T(1024)}, u32[]{:S(2)}) copy-start(f32[8192]{0:T(1024)} %param.19) | copy-start | bytes 98308
  77.3 38.2 %all-to-all-start.3 = ((bf16[32,16,2560]{2,1,0:T(8,128)(2,1)}), bf16[32,16,2560]{2,1,0:T(8,128)(2,1)S(1)}, u32[]{:S(2)}, u32[]{:S(2)}) async-start(bf16[32,16,2560]{2,1,0:T(8,128)(2,1)} %copy-done), calls=%async_computation.3 | async-start | bytes 5242880 | tf_op jit(solution)/shard_map/all_to_all | solution.py:585
  (1 other events, 1.2 us)

commit v9 on v8

--- a/solution.py
+++ b/solution.py
@@ -146,10 +146,15 @@
     return jnp.where(block == 6, 2, 0)
 
 
+def split(wide):
+    high = wide.astype(jnp.bfloat16).astype(jnp.float32)
+    return jnp.concatenate([high, wide - high], axis=-2).astype(jnp.bfloat16)
+
+
 def product_kernel(tiles, counts, places, *refs):
     x_refs, refs = refs[: len(counts)], refs[len(counts) :]
     if places:
-        earlier_ref, w_hbm, out_ref, rows_ref, w_ref, sems, part_ref = refs
+        earlier_ref, read_ref, w_hbm, out_ref, rows_ref, w_ref, sems, part_ref = refs
     else:
         w_hbm, part_ref, rows_ref, w_ref, sems = refs
     n = pl.program_id(0)
@@ -182,6 +187,7 @@
             column = lax.rem(lax.axis_index("tp"), COL_BLOCKS)
             y, x = column // 4, lax.rem(column, 4)
             done = earlier_ref.shape[0] // ROW_BLOCKS
+            out_ref[:, :, CONT_LANES:] = jnp.broadcast_to(split(read_ref[...])[None], (MEMBERS, CTOK, TILE))
             for i, (dy, dx) in enumerate(places):
                 home = lax.rem(y + dy, 2) * 4 + lax.rem(x + dx, 4)
                 for r in range(ROW_BLOCKS):
@@ -189,7 +195,7 @@
                         message = earlier_ref[i * ROW_BLOCKS + r]
                     else:
                         message = part_ref[(i - done) * ROW_BLOCKS + r]
-                    out_ref[r * COL_BLOCKS + home] = message
+                    out_ref[r * COL_BLOCKS + home, :, :CONT_LANES] = message
 
 
 def block_product(messages, blocks, earlier=(), places=()):
@@ -197,7 +203,7 @@
     counts = tuple(rows.shape[0] for rows in messages)
     members = sum(counts)
     part = (members, CTOK, tiles * TILE + REST)
-    out = (MEMBERS,) + part[1:] if places else part
+    out = (MEMBERS, CTOK, CONT_LANES + TILE) if places else part
     return pl.pallas_call(
         functools.partial(product_kernel, tiles, counts, places),
         out_shape=jax.ShapeDtypeStruct(out, jnp.bfloat16),
@@ -415,22 +421,24 @@
 
 
 def last_kernel(
-    len_ref, bound_ref, bias_ref, cos_ref, sin_ref, cache_ref, kv_ref, parts_ref, main_ref, cont_ref, head_ref,
-    out_ref, score_ref, qkv_ref, wide_ref, read_ref,
+    len_ref, bound_ref, bias_ref, cos_ref, sin_ref, cache_ref, kv_ref, parts_ref, main_ref, cont_ref, head_ref, *refs
 ):
+    sum_refs = refs[:COL_BLOCKS]
+    out_ref, score_ref, qkv_ref, wide_ref, read_ref, sums_ref = refs[COL_BLOCKS:]
     out_cols = D // COL_BLOCKS
+    for (dy, dx), ref in zip(HERE + FAR, sum_refs):
+        sums_ref[column_at(-dy, -dx)] = ref[...]
     for c in range(COL_BLOCKS):
-        total = summed_block(parts_ref, c, slice(CONT_LANES, CONT_LANES + TILE))
-        total = total[:8] + total[8:]
+        total = sums_ref[c]
         for j in range(out_cols // TILE):
             at = slice(c * out_cols + j * TILE, c * out_cols + (j + 1) * TILE)
             for s in range(STEPS):
                 wide_ref[s : s + 1, at] = total[s * 4 + j : s * 4 + j + 1]
     out_ref[...] = (main_ref[...].astype(jnp.float32) + wide_ref[:STEPS, :]).astype(jnp.bfloat16)
     for r in range(ROW_BLOCKS):
-        read = parts_ref[r * COL_BLOCKS, :, CONT_LANES + TILE :].astype(jnp.float32)
+        read = parts_ref[r * COL_BLOCKS, :, CONT_LANES:].astype(jnp.float32)
         for c in range(1, COL_BLOCKS):
-            read = read + parts_ref[r * COL_BLOCKS + c, :, CONT_LANES + TILE :].astype(jnp.float32)
+            read = read + parts_ref[r * COL_BLOCKS + c, :, CONT_LANES:].astype(jnp.float32)
         read_ref[r] = read[:8] + read[8:]
     rows = qkv_ref.shape[0]
     load_qkv(False, parts_ref, qkv_ref)
@@ -472,12 +480,13 @@
             jax.ShapeDtypeStruct((STEPS, D), jnp.bfloat16),
             jax.ShapeDtypeStruct((8, 128), jnp.float32),
         ),
-        in_specs=[SMEM, SMEM] + [VMEM] * 9,
+        in_specs=[SMEM, SMEM] + [VMEM] * (9 + COL_BLOCKS),
         out_specs=(VMEM, VMEM),
         scratch_shapes=[
             pltpu.VMEM((CTOK, QKV), jnp.float32),
             pltpu.VMEM((8, D), jnp.float32),
             pltpu.VMEM((ROW_BLOCKS, 8, TILE), jnp.float32),
+            pltpu.VMEM((COL_BLOCKS, 8, TILE), jnp.float32),
         ],
         compiler_params=kernel_params(),
         cost_estimate=cost(4 * 10**8, 18 * 10**6),
@@ -485,7 +494,7 @@
     )(*args)
 
 
-def readout_kernel(head_ref, w_hbm, out_ref, w_ref, sem):
+def readout_kernel(head_ref, w_hbm, after_ref, out_ref, w_ref, sem):
     copy = pltpu.make_async_copy(w_hbm.at[0], w_ref, sem)
     copy.start()
     row = head_ref[pl.ds(lax.rem(lax.axis_index("tp"), COL_BLOCKS), 1), :]
@@ -497,20 +506,22 @@
     prod = lax.dot_general(
         pieces.astype(jnp.bfloat16), w_ref[...], (((1,), (1,)), ((), ())), preferred_element_type=jnp.float32
     )
-    out_ref[...] = prod[0:1] + prod[1:2] + prod[2:3]
-
-
-def readout(value_head, blocks):
+    total = prod[0:1] + prod[1:2] + prod[2:3]
+    for j in range(FEATURES // TILE):
+        out_ref[j : j + 1, :] = total[:, j * TILE : (j + 1) * TILE]
+
+
+def readout(value_head, blocks, after):
     return pl.pallas_call(
         readout_kernel,
-        out_shape=jax.ShapeDtypeStruct((1, FEATURES), jnp.float32),
-        in_specs=[whole(value_head.shape), HBM],
-        out_specs=whole((1, FEATURES)),
+        out_shape=jax.ShapeDtypeStruct((8, TILE), jnp.float32),
+        in_specs=[VMEM, HBM, UNREAD],
+        out_specs=VMEM,
         scratch_shapes=[pltpu.VMEM((FEATURES, D // COL_BLOCKS), jnp.bfloat16), pltpu.SemaphoreType.DMA],
         compiler_params=kernel_params(),
         cost_estimate=cost(2 * 10**8, 12 * 10**6),
         name="readout",
-    )(value_head, in_hbm(blocks))
+    )(value_head, in_hbm(blocks), after)
 
 
 def split(wide):
@@ -518,7 +529,7 @@
     return jnp.concatenate([high, wide - high], axis=-2).astype(jnp.bfloat16)
 
 
-def out_kernel(tiles, x_ref, read_ref, cont_ref, w_hbm, out_ref, rows_ref, wide_ref, read8_ref, w_ref, sems):
+def out_kernel(tiles, x_ref, w_hbm, after_ref, z0_ref, z1_ref, z2_ref, z3_ref, rows_ref, wide_ref, w_ref, sems):
     n = pl.program_id(0)
     members = x_ref.shape[0]
     lines = members * STEPS
@@ -527,10 +538,6 @@
 
     @pl.when(n == 0)
     def _():
-        out_ref[:, :, :CONT_LANES] = cont_ref[...]
-        for j in range(FEATURES // TILE):
-            read8_ref[j : j + 1, :] = read_ref[:, j * TILE : (j + 1) * TILE]
-        out_ref[:, :, CONT_LANES + TILE :] = jnp.broadcast_to(split(read8_ref[...])[None], (members, 16, TILE))
         packed = x_ref[...].reshape(members * 16, TILE).astype(jnp.float32)
         for k in range(halves):
             wide_ref[k] = packed[:, k * 128 : (k + 1) * 128]
@@ -545,31 +552,60 @@
 
     @pl.when(n == tiles - 1)
     def _():
-        for k in range(halves):
-            lane = CONT_LANES + k * 128
-            out_ref[:, :, lane : lane + 128] = split(wide_ref[k, : members * 8, :].reshape(members, 8, 128))
-
-
-def out_product(rows, read, cont_parts, blocks):
+        z = lax.axis_index("tp") // COL_BLOCKS
+        size = COL_BLOCKS * 8
+        for ahead, z_ref in enumerate((z0_ref, z1_ref, z2_ref, z3_ref)):
+            start = pl.multiple_of(lax.rem(z + ahead, ROW_BLOCKS) * size, size)
+            for k in range(halves):
+                packed = wide_ref[k, pl.ds(start, size), :].reshape(COL_BLOCKS, 8, 128)
+                z_ref[:, :, k * 128 : (k + 1) * 128] = packed
+
+
+def out_product(rows, blocks, after):
     members = rows.shape[0]
     tiles = blocks.shape[2] // TILE
     return pl.pallas_call(
         functools.partial(out_kernel, tiles),
-        out_shape=jax.ShapeDtypeStruct((members, CTOK, CONT_LANES + 2 * TILE), jnp.bfloat16),
+        out_shape=[jax.ShapeDtypeStruct((COL_BLOCKS, 8, TILE), jnp.float32)] * ROW_BLOCKS,
         grid=(tiles,),
-        in_specs=[VMEM, VMEM, VMEM, HBM],
-        out_specs=VMEM,
+        in_specs=[VMEM, HBM, UNREAD],
+        out_specs=[VMEM] * ROW_BLOCKS,
         scratch_shapes=[
             pltpu.VMEM((members * STEPS, FEATURES), jnp.bfloat16),
             pltpu.VMEM((TILE // 128, members * 16, 128), jnp.float32),
-            pltpu.VMEM((8, TILE), jnp.float32),
             pltpu.VMEM((tiles, FEATURES, TILE), jnp.bfloat16),
             pltpu.SemaphoreType.DMA((tiles,)),
         ],
         compiler_params=kernel_params(),
-        cost_estimate=cost(3 * 10**8, 8 * 10**6),
+        cost_estimate=cost(3 * 10**8, 9 * 10**6),
         name="out_product",
-    )(rows, read, cont_parts, in_hbm(blocks))
+    )(rows, in_hbm(blocks), after)
+
+
+def column_at(dy, dx):
+    column = lax.rem(lax.axis_index("tp"), COL_BLOCKS)
+    return lax.rem(column // 4 + dy + 2, 2) * 4 + lax.rem(column + dx + 4, 4)
+
+
+def sum_kernel(*refs):
+    for (dy, dx), out_ref in zip(HERE + FAR, refs[ROW_BLOCKS:]):
+        home = column_at(dy, dx)
+        total = refs[0][home]
+        for ref in refs[1:ROW_BLOCKS]:
+            total = total + ref[home]
+        out_ref[...] = total
+
+
+def sum_along(parts):
+    return pl.pallas_call(
+        sum_kernel,
+        out_shape=[jax.ShapeDtypeStruct(parts[0].shape[1:], jnp.float32)] * COL_BLOCKS,
+        in_specs=[VMEM] * ROW_BLOCKS,
+        out_specs=[VMEM] * COL_BLOCKS,
+        compiler_params=kernel_params(),
+        cost_estimate=cost(10**5, 10**6),
+        name="sum_along",
+    )(*parts)
 
 
 def rope_tables(positions):
@@ -600,15 +636,11 @@
 
 def ring(rows):
     near = gather_along([rows[0]] + [from_along(rows[ROW_BLOCKS - k], k) for k in range(1, ROW_BLOCKS)])
-    half = ROW_BLOCKS // 2
     over = from_side(near, 1, 0)
-    here, far = [], []
+    here = []
     for mine in (near, over):
-        after = from_side(mine, 0, 1)
-        before = from_side(mine, 0, 3)
-        far += [from_side(before[:half], 0, 3), from_side(after[half:], 0, 1)]
-        here += [mine, after, before]
-    return here, far
+        here += [mine, from_side(mine, 0, 1), from_side(mine, 0, 3)]
+    return here, [from_side(here[2], 0, 3), from_side(here[4], 0, 1)]
 
 
 HERE = ((0, 0), (0, 1), (0, 3), (1, 0), (1, 1), (1, 3))
@@ -626,18 +658,21 @@
     step = jnp.arange(CTOK, dtype=jnp.int32) % STEPS
     main_tables = rope_tables(prefix_len + step[:8])
     cont_tables = rope_tables(prefix_len + boundary + step)
-    read = readout(value_head.reshape(COL_BLOCKS, D // COL_BLOCKS), w_out)
     gain = rms_gain[None, :]
     main_rows = norm_main(main, gain)
     here, far = ring(norm_cont(cont, gain, main_rows))
-    main_parts = exchange(main_product(exchange(main_rows), w_qkv, here[0]))
+    read = readout(value_head.reshape(COL_BLOCKS, D // COL_BLOCKS), w_out, here[0])
+    main_parts = exchange(main_product(exchange(main_rows), w_qkv, read))
     mixed, main_kv = attend_main(prefix_len, bias, *main_tables, cache, main_parts, here)
     mixed, far = lax.optimization_barrier((mixed, far))
     mixed = exchange(mixed)
-    cont_parts = block_product(far, w_qkv, (block_product(here, w_qkv),), HERE + FAR)
-    parts = exchange(out_product(mixed, read, cont_parts, w_out))
+    cont_parts = block_product(far, w_qkv, (block_product(here, w_qkv), read), HERE + FAR)
+    sums = out_product(mixed, w_out, cont_parts)
+    cont_parts = exchange(cont_parts)
+    sums = sum_along([sums[0]] + [from_along(sums[k], -k) for k in range(1, ROW_BLOCKS)])
+    sums = [from_side(rows, -dy, -dx) if dy or dx else rows for rows, (dy, dx) in zip(sums, HERE + FAR)]
     main_out, score = last(
-        prefix_len, boundary, bias, *cont_tables, cache, main_kv, parts, main, cont, head
+        prefix_len, boundary, bias, *cont_tables, cache, main_kv, cont_parts, main, cont, head, *sums
     )
     return main_out[None], score[0, :1]
 

time: 122 us -> 134 us (1.098)
  starting transfers between devices: 49.8 us -> 61.3 us
  local copies, waits for them, and re-layouts: 6.64 us -> 12.5 us
  waiting for transfers between devices: 34.2 us -> 28.4 us
    all_to_all x4, waiting for transfers between devices: 29.7 us -> 5.43 us  [exchange(): return lax.all_to_all(rows, 'tp', split_axis=0, concat_axis=0, tiled=True)]
    ppermute x3 -> x6, waiting for transfers between devices: 0.01 us -> 21 us  [from_along(): return lax.ppermute(rows, 'tp', route)]
    ppermute x9 -> x14, starting transfers between devices: 13.8 us -> 24.5 us  [from_side(): return lax.ppermute(rows, 'tp', route)]
    unnamed x18 -> x44, local copies, waits for them, and re-layouts: 2.74 us -> 11.2 us
    ppermute x3 -> x6, starting transfers between devices: 5.45 us -> 11.4 us  [from_along(): return lax.ppermute(rows, 'tp', route)]
    all_to_all x4, starting transfers between devices: 30.6 us -> 25.3 us  [exchange(): return lax.all_to_all(rows, 'tp', split_axis=0, concat_axis=0, tiled=True)]
    slice x4 -> x0, local copies, waits for them, and re-layouts: 2.62 us -> none  [ring(): far += [from_side(before[:half], 0, 3), from_side(after[half:], 0, 1)]]
    ppermute x9 -> x14, waiting for transfers between devices: 4.54 us -> 2 us  [from_side(): return lax.ppermute(rows, 'tp', route)]
  transfers between devices with their start and end apart: 16 -> 24, of which waited for: 3 -> 10; matrix products, arithmetic and copies ran while one was open for 3% -> 1% of each run, Pallas kernels for 15% -> 16%
where the time goes in v9:
time: 134 us; the launch traced here: 133 us
  starting transfers between devices  61.3 us (46%)
  Pallas kernels  28.4 us (21%)
  waiting for transfers between devices  28.4 us (21%)
  local copies, waits for them, and re-layouts  12.5 us (9%)
  between operations  2.14 us (2%)
    all_to_all x4, starting transfers between devices, exchange(): return lax.all_to_all(rows, 'tp', split_axis=0, concat_axis=0, tiled=True)  25.3 us
    ppermute x14, starting transfers between devices, from_side(): return lax.ppermute(rows, 'tp', route)  24.5 us
    ppermute x6, waiting for transfers between devices, from_along(): return lax.ppermute(rows, 'tp', route)  21 us
    ppermute x6, starting transfers between devices, from_along(): return lax.ppermute(rows, 'tp', route)  11.4 us
    unnamed x44, local copies, waits for them, and re-layouts  11.2 us
    pallas_call x2, Pallas kernels, block_product(): pl.pallas_call(functools.partial(product_kernel, tiles, counts, places),...  8.86 us
    all_to_all x4, waiting for transfers between devices, exchange(): return lax.all_to_all(rows, 'tp', split_axis=0, concat_axis=0, tiled=True)  5.43 us
    pallas_call x1, Pallas kernels, main_product(): pl.pallas_call(functools.partial(main_kernel, tiles), out_shape=jax.Shape...  3.7 us
  transfers between devices with their start and end apart: 24, of which 10 were waited for; matrix products, arithmetic and copies ran while one was open for 1% of the time, Pallas kernels for 16%

profile of v9, /device:TPU:0, one launch (start us, length us, event | category | flops | bytes accessed | tf_op | source)
XLA Modules:
  0.0 133.2 jit_solution(17631188431820653792)
XLA Ops:
  3.7 4.2 %collective-permute-start = (bf16[16,2048]{1,0:T(8,128)(2,1)S(1)}, bf16[16,2048]{1,0:T(8,128)(2,1)S(1)}, u32[]{:S(2)}, u32[]{:S(2)}) collective-permute-start(bf16[16,2048]{1,0:T(8,128)(2,1)S(1)} %get-tuple-element.26), channel_id=1, source_target_pairs={{8,0},{9,1},{10,2},{11,3},{12,4},{13,5},{14,6},{15,7},{16,8},{17,9... | collective-permute-start | bytes 196616 | tf_op jit(solution)/shard_map/ppermute | solution.py:634
  10.7 3.0 %collective-permute-done.1.ahead2_ref = bf16[16,2048]{1,0:T(8,128)(2,1)S(1)} collective-permute-done((bf16[16,2048]{1,0:T(8,128)(2,1)S(1)}, bf16[16,2048]{1,0:T(8,128)(2,1)S(1)}, u32[]{:S(2)}, u32[]{:S(2)}) %collective-permute-start.1) | collective-permute-done | bytes 65568 | tf_op jit(solution)/shard_map/ppermute | solution.py:634
  15.8 5.7 %all-to-all-start = ((bf16[32,16,256]{2,1,0:T(8,128)(2,1)}), bf16[32,16,256]{2,1,0:T(8,128)(2,1)S(1)}, u32[]{:S(2)}, u32[]{:S(2)}) async-start(bf16[32,16,256]{2,1,0:T(8,128)(2,1)} %norm_main.1.after_ref), calls=%async_computation | async-start | bytes 524288 | tf_op jit(solution)/shard_map/all_to_all | solution.py:621
  23.0 1.9 %collective-permute-start.4 = (bf16[4,16,2048]{2,1,0:T(8,128)(2,1)S(1)}, bf16[4,16,2048]{2,1,0:T(8,128)(2,1)S(1)}, u32[]{:S(2)}, u32[]{:S(2)}) collective-permute-start(bf16[4,16,2048]{2,1,0:T(8,128)(2,1)S(1)} %gather_along.1.after_ref.refs_0_), channel_id=1, source_target_pairs={{3,0},{0,1},{1,2},{2,3},{7,4},{4,5},{5,6},{6,7},{11,8},{8,9},{9,10... | collective-permute-start | bytes 786440 | tf_op jit(solution)/shard_map/ppermute | solution.py:629
  26.3 1.8 %collective-permute-start.3 = (bf16[4,16,2048]{2,1,0:T(8,128)(2,1)S(1)}, bf16[4,16,2048]{2,1,0:T(8,128)(2,1)S(1)}, u32[]{:S(2)}, u32[]{:S(2)}) collective-permute-start(bf16[4,16,2048]{2,1,0:T(8,128)(2,1)S(1)} %gather_along.1.after_ref.refs_0_), channel_id=1, source_target_pairs={{1,0},{2,1},{3,2},{0,3},{5,4},{6,5},{7,6},{4,7},{9,8},{10,9},{11,1... | collective-permute-start | bytes 786440 | tf_op jit(solution)/shard_map/ppermute | solution.py:629
  28.1 3.4 %readout.1.after_ref.refs_3_ = f32[8,256]{1,0:T(8,128)S(1)} custom-call(f32[8,1024]{1,0:T(8,128)S(1)} %reshape.33.head_ref, bf16[1,2048,1024]{2,1,0:T(8,128)(2,1)} %w_hbm.5, bf16[4,16,2048]{2,1,0:T(8,128)(2,1)S(1)} %gather_along.1.after_ref.refs_0_), custom_call_target="tpu_custom_call" | custom-call | flops 200000000 | bytes 12000000 | tf_op jit(solution)/shard_map/readout/pallas_call | solution.py:515
  31.7 3.7 %main_product.1 = bf16[32,16,256]{2,1,0:T(8,128)(2,1)} custom-call(bf16[32,16,256]{2,1,0:T(8,128)(2,1)S(1)} %all-to-all-done.x_ref, bf16[1,2048,1280]{2,1,0:T(8,128)(2,1)} %refs_4_.1, f32[8,256]{1,0:T(8,128)S(1)} %readout.1.after_ref.refs_3_), custom_call_target="tpu_custom_call" | custom-call | flops 300000000 | bytes 13000000 | tf_op jit(solution)/shard_map/main_product/pallas_call | solution.py:262
  35.4 5.8 %all-to-all-start.1 = ((bf16[32,16,256]{2,1,0:T(8,128)(2,1)}), bf16[32,16,256]{2,1,0:T(8,128)(2,1)S(1)}, u32[]{:S(2)}, u32[]{:S(2)}) async-start(bf16[32,16,256]{2,1,0:T(8,128)(2,1)} %main_product.1), calls=%async_computation.1 | async-start | bytes 524288 | tf_op jit(solution)/shard_map/all_to_all | solution.py:621
  41.2 1.9 %collective-permute-start.7 = (bf16[4,16,2048]{2,1,0:T(8,128)(2,1)S(1)}, bf16[4,16,2048]{2,1,0:T(8,128)(2,1)S(1)}, u32[]{:S(2)}, u32[]{:S(2)}) collective-permute-start(bf16[4,16,2048]{2,1,0:T(8,128)(2,1)S(1)} %collective-permute-done.5.refs_3_), channel_id=1, source_target_pairs={{3,0},{0,1},{1,2},{2,3},{7,4},{4,5},{5,6},{6,7},{11,8},{8,9},{9,10... | collective-permute-start | bytes 786440 | tf_op jit(solution)/shard_map/ppermute | solution.py:629
  44.5 1.8 %collective-permute-start.9 = (bf16[4,16,2048]{2,1,0:T(8,128)(2,1)S(1)}, bf16[4,16,2048]{2,1,0:T(8,128)(2,1)S(1)}, u32[]{:S(2)}, u32[]{:S(2)}) collective-permute-start(bf16[4,16,2048]{2,1,0:T(8,128)(2,1)S(1)} %collective-permute-done.6.refs_4_), channel_id=1, source_target_pairs={{1,0},{2,1},{3,2},{0,3},{5,4},{6,5},{7,6},{4,7},{9,8},{10,9},{11,1... | collective-permute-start | bytes 786440 | tf_op jit(solution)/shard_map/ppermute | solution.py:629
  46.5 5.0 %all-to-all-done.1.parts_ref = bf16[32,16,256]{2,1,0:T(8,128)(2,1)S(1)} async-done(((bf16[32,16,256]{2,1,0:T(8,128)(2,1)}), bf16[32,16,256]{2,1,0:T(8,128)(2,1)S(1)}, u32[]{:S(2)}, u32[]{:S(2)}) %all-to-all-start.1) | async-done | bytes 262176 | tf_op jit(solution)/shard_map/all_to_all | solution.py:621
  52.8 3.0 %attend_main.1 = (bf16[32,16,256]{2,1,0:T(8,128)(2,1)S(1)}, f32[8,2048]{1,0:T(8,128)S(1)}) custom-call(s32[1]{0:T(128)} %copy.12.len_ref, f32[1,10240]{1,0:T(1,128)S(1)} %bitcast.15, f32[8,128]{1,0:T(8,128)S(1)} %get-tuple-element.56.cos_ref, f32[8,128]{1,0:T(8,128)S(1)} %get-tuple-element.57.sin_ref, bf16[256,2048]{1,0:T(8,128)(2,1)S(1)} %bitcast.11, ...), custom_call_target="tpu_custom_call" | custom-call | flops 200000000 | bytes 13000000 | tf_op jit(solution)/shard_map/attend_main/pallas_call | solution.py:405
  57.1 5.9 %all-to-all-start.3 = ((bf16[32,16,256]{2,1,0:T(8,128)(2,1)}), bf16[32,16,256]{2,1,0:T(8,128)(2,1)S(1)}, u32[]{:S(2)}, u32[]{:S(2)}) async-start(bf16[32,16,256]{2,1,0:T(8,128)(2,1)} %copy-done.4), calls=%async_computation.3 | async-start | bytes 524288 | tf_op jit(solution)/shard_map/all_to_all | solution.py:621
  63.0 4.3 %block_product.2.refs_2_ = bf16[24,16,2048]{2,1,0:T(8,128)(2,1)S(1)} custom-call(bf16[4,16,2048]{2,1,0:T(8,128)(2,1)S(1)} %gather_along.1.after_ref.refs_0_, bf16[4,16,2048]{2,1,0:T(8,128)(2,1)S(1)} %collective-permute-done.3.refs_1_, bf16[4,16,2048]{2,1,0:T(8,128)(2,1)S(1)} %collective-permute-done.4.refs_2_, ...), custom_call_target="tpu_custom_call" | custom-call | flops 2013265920 | bytes 14000000 | tf_op jit(solution)/shard_map/block_product/pallas_call | solution.py:207
  67.3 4.5 %block_product.3.after_ref = bf16[32,16,2304]{2,1,0:T(8,128)(2,1)} custom-call(bf16[4,16,2048]{2,1,0:T(8,128)(2,1)S(1)} %collective-permute-done.8.refs_0_, bf16[4,16,2048]{2,1,0:T(8,128)(2,1)S(1)} %collective-permute-done.9.refs_1_, bf16[24,16,2048]{2,1,0:T(8,128)(2,1)S(1)} %block_product.2.refs_2_, f32[8,256]{1,0:T(8,128)S(1)} %readout.1.after_ref.refs_3_, ...), custom_call_target="tpu_custom_call" | custom-call | flops 671088640 | bytes 14000000 | tf_op jit(solution)/shard_map/block_product/pallas_call | solution.py:207
  72.9 8.0 %all-to-all-start.2 = ((bf16[32,16,2304]{2,1,0:T(8,128)(2,1)}), bf16[32,16,2304]{2,1,0:T(8,128)(2,1)S(1)}, u32[]{:S(2)}, u32[]{:S(2)}) async-start(bf16[32,16,2304]{2,1,0:T(8,128)(2,1)} %block_product.3.after_ref), calls=%async_computation.2 | async-start | bytes 4718592 | tf_op jit(solution)/shard_map/all_to_all | solution.py:621
  82.5 2.6 %out_product.1 = (f32[8,8,256]{2,1,0:T(8,128)S(1)}, f32[8,8,256]{2,1,0:T(8,128)S(1)}, f32[8,8,256]{2,1,0:T(8,128)S(1)}, f32[8,8,256]{2,1,0:T(8,128)S(1)}) custom-call(bf16[32,16,256]{2,1,0:T(8,128)(2,1)S(1)} %copy-done.3, bf16[1,2048,1024]{2,1,0:T(8,128)(2,1)} %w_hbm.5, bf16[32,16,2304]{2,1,0:T(8,128)(2,1)} %block_product.3.after_ref), custom_call_target="tpu_custom_call" | custom-call | flops 300000000 | bytes 9000000 | tf_op jit(solution)/shard_map/out_product/pallas_call | solution.py:567
  85.1 1.9 %collective-permute-start.10 = (f32[8,8,256]{2,1,0:T(8,128)S(1)}, f32[8,8,256]{2,1,0:T(8,128)S(1)}, u32[]{:S(2)}, u32[]{:S(2)}) collective-permute-start(f32[8,8,256]{2,1,0:T(8,128)S(1)} %get-tuple-element.35), channel_id=1, source_target_pairs={{24,0},{25,1},{26,2},{27,3},{28,4},{29,5},{30,6},{31,7},{0,8},{1,9... | collective-permute-start | bytes 196616 | tf_op jit(solution)/shard_map/ppermute | solution.py:634
  86.9 2.7 %collective-permute-start.11 = (f32[8,8,256]{2,1,0:T(8,128)S(1)}, f32[8,8,256]{2,1,0:T(8,128)S(1)}, u32[]{:S(2)}, u32[]{:S(2)}) collective-permute-start(f32[8,8,256]{2,1,0:T(8,128)S(1)} %get-tuple-element.36), channel_id=1, source_target_pairs={{16,0},{17,1},{18,2},{19,3},{20,4},{21,5},{22,6},{23,7},{24,8},{25... | collective-permute-start | bytes 196616 | tf_op jit(solution)/shard_map/ppermute | solution.py:634
  91.1 15.3 %collective-permute-done.10.refs_1_ = f32[8,8,256]{2,1,0:T(8,128)S(1)} collective-permute-done((f32[8,8,256]{2,1,0:T(8,128)S(1)}, f32[8,8,256]{2,1,0:T(8,128)S(1)}, u32[]{:S(2)}, u32[]{:S(2)}) %collective-permute-start.10) | collective-permute-done | bytes 65568 | tf_op jit(solution)/shard_map/ppermute | solution.py:634
  107.2 2.0 %collective-permute-start.13 = (f32[8,256]{1,0:T(8,128)S(1)}, f32[8,256]{1,0:T(8,128)S(1)}, u32[]{:S(2)}, u32[]{:S(2)}) collective-permute-start(f32[8,256]{1,0:T(8,128)S(1)} %get-tuple-element.39), channel_id=1, source_target_pairs={{3,0},{0,1},{1,2},{2,3},{7,4},{4,5},{5,6},{6,7},{11,8},{8,9},{9,10... | collective-permute-start | bytes 24584 | tf_op jit(solution)/shard_map/ppermute | solution.py:629
  113.1 3.4 %collective-permute-start.17 = (f32[8,256]{1,0:T(8,128)S(1)}, f32[8,256]{1,0:T(8,128)S(1)}, u32[]{:S(2)}, u32[]{:S(2)}) collective-permute-start(f32[8,256]{1,0:T(8,128)S(1)} %get-tuple-element.43), channel_id=1, source_target_pairs={{5,0},{6,1},{7,2},{4,3},{1,4},{2,5},{3,6},{0,7},{13,8},{14,9},{15,... | collective-permute-start | bytes 24584 | tf_op jit(solution)/shard_map/ppermute | solution.py:629
  117.0 3.0 %collective-permute-start.19 = (f32[8,256]{1,0:T(8,128)S(1)}, f32[8,256]{1,0:T(8,128)S(1)}, u32[]{:S(2)}, u32[]{:S(2)}) collective-permute-start(f32[8,256]{1,0:T(8,128)S(1)} %get-tuple-element.45), channel_id=1, source_target_pairs={{6,0},{7,1},{4,2},{5,3},{2,4},{3,5},{0,6},{1,7},{14,8},{15,9},{12,... | collective-permute-start | bytes 24584 | tf_op jit(solution)/shard_map/ppermute | solution.py:629
  129.0 3.7 %attend_cont.1 = (bf16[2,8192]{1,0:T(2,128)(2,1)}, f32[8,128]{1,0:T(8,128)S(1)}) custom-call(s32[1]{0:T(128)} %copy.12.len_ref, s32[1]{0:T(128)S(6)} %copy.13.bound_ref, f32[1,10240]{1,0:T(1,128)S(1)} %bitcast.16, f32[16,128]{1,0:T(8,128)S(1)} %get-tuple-element.54.cos_ref, f32[16,128]{1,0:T(8,128)S(1)} %get-tuple-element.55.sin_ref, ...), custom_call_target="tpu_custom_call" | custom-call | flops 400000000 | bytes 18000000 | tf_op jit(solution)/shard_map/attend_cont/pallas_call | solution.py:477
  (89 shorter events, 32.7 us)
Async XLA Ops:
  3.7 7.0 %collective-permute-start = (bf16[16,2048]{1,0:T(8,128)(2,1)S(1)}, bf16[16,2048]{1,0:T(8,128)(2,1)S(1)}, u32[]{:S(2)}, u32[]{:S(2)}) collective-permute-start(bf16[16,2048]{1,0:T(8,128)(2,1)S(1)} %get-tuple-element.26), channel_id=1, source_target_pairs={{8,0},{9,1},{10,2},{11,3},{12,4},{13,5},{14,6},{15,7},{16,8},{17,9... | collective-permute-start | bytes 196616 | tf_op jit(solution)/shard_map/ppermute | solution.py:634
  7.9 5.8 %collective-permute-start.1 = (bf16[16,2048]{1,0:T(8,128)(2,1)S(1)}, bf16[16,2048]{1,0:T(8,128)(2,1)S(1)}, u32[]{:S(2)}, u32[]{:S(2)}) collective-permute-start(bf16[16,2048]{1,0:T(8,128)(2,1)S(1)} %get-tuple-element.27), channel_id=1, source_target_pairs={{16,0},{17,1},{18,2},{19,3},{20,4},{21,5},{22,6},{23,7},{24,8},{25... | collective-permute-start | bytes 196616 | tf_op jit(solution)/shard_map/ppermute | solution.py:634
  7.9 6.2 %collective-permute-start.2 = (bf16[16,2048]{1,0:T(8,128)(2,1)S(1)}, bf16[16,2048]{1,0:T(8,128)(2,1)S(1)}, u32[]{:S(2)}, u32[]{:S(2)}) collective-permute-start(bf16[16,2048]{1,0:T(8,128)(2,1)S(1)} %get-tuple-element.28), channel_id=1, source_target_pairs={{24,0},{25,1},{26,2},{27,3},{28,4},{29,5},{30,6},{31,7},{0,8},{1,9... | collective-permute-start | bytes 196616 | tf_op jit(solution)/shard_map/ppermute | solution.py:634
  14.1 10.7 %collective-permute-start.5 = (bf16[4,16,2048]{2,1,0:T(8,128)(2,1)S(1)}, bf16[4,16,2048]{2,1,0:T(8,128)(2,1)S(1)}, u32[]{:S(2)}, u32[]{:S(2)}) collective-permute-start(bf16[4,16,2048]{2,1,0:T(8,128)(2,1)S(1)} %gather_along.1.after_ref.refs_0_), channel_id=1, source_target_pairs={{4,0},{5,1},{6,2},{7,3},{0,4},{1,5},{2,6},{3,7},{12,8},{13,9},{14,... | collective-permute-start | bytes 786440 | tf_op jit(solution)/shard_map/ppermute | solution.py:629
  15.8 15.9 %all-to-all-start = ((bf16[32,16,256]{2,1,0:T(8,128)(2,1)}), bf16[32,16,256]{2,1,0:T(8,128)(2,1)S(1)}, u32[]{:S(2)}, u32[]{:S(2)}) async-start(bf16[32,16,256]{2,1,0:T(8,128)(2,1)} %norm_main.1.after_ref), calls=%async_computation | async-start | bytes 524288 | tf_op jit(solution)/shard_map/all_to_all | solution.py:621
  23.0 20.0 %collective-permute-start.4 = (bf16[4,16,2048]{2,1,0:T(8,128)(2,1)S(1)}, bf16[4,16,2048]{2,1,0:T(8,128)(2,1)S(1)}, u32[]{:S(2)}, u32[]{:S(2)}) collective-permute-start(bf16[4,16,2048]{2,1,0:T(8,128)(2,1)S(1)} %gather_along.1.after_ref.refs_0_), channel_id=1, source_target_pairs={{3,0},{0,1},{1,2},{2,3},{7,4},{4,5},{5,6},{6,7},{11,8},{8,9},{9,10... | collective-permute-start | bytes 786440 | tf_op jit(solution)/shard_map/ppermute | solution.py:629
  24.9 19.6 %collective-permute-start.6 = (bf16[4,16,2048]{2,1,0:T(8,128)(2,1)S(1)}, bf16[4,16,2048]{2,1,0:T(8,128)(2,1)S(1)}, u32[]{:S(2)}, u32[]{:S(2)}) collective-permute-start(bf16[4,16,2048]{2,1,0:T(8,128)(2,1)S(1)} %collective-permute-done.5.refs_3_), channel_id=1, source_target_pairs={{1,0},{2,1},{3,2},{0,3},{5,4},{6,5},{7,6},{4,7},{9,8},{10,9},{11,1... | collective-permute-start | bytes 786440 | tf_op jit(solution)/shard_map/ppermute | solution.py:629
  26.3 20.2 %collective-permute-start.3 = (bf16[4,16,2048]{2,1,0:T(8,128)(2,1)S(1)}, bf16[4,16,2048]{2,1,0:T(8,128)(2,1)S(1)}, u32[]{:S(2)}, u32[]{:S(2)}) collective-permute-start(bf16[4,16,2048]{2,1,0:T(8,128)(2,1)S(1)} %gather_along.1.after_ref.refs_0_), channel_id=1, source_target_pairs={{1,0},{2,1},{3,2},{0,3},{5,4},{6,5},{7,6},{4,7},{9,8},{10,9},{11,1... | collective-permute-start | bytes 786440 | tf_op jit(solution)/shard_map/ppermute | solution.py:629
  35.4 16.1 %all-to-all-start.1 = ((bf16[32,16,256]{2,1,0:T(8,128)(2,1)}), bf16[32,16,256]{2,1,0:T(8,128)(2,1)S(1)}, u32[]{:S(2)}, u32[]{:S(2)}) async-start(bf16[32,16,256]{2,1,0:T(8,128)(2,1)} %main_product.1), calls=%async_computation.1 | async-start | bytes 524288 | tf_op jit(solution)/shard_map/all_to_all | solution.py:621
  41.2 11.6 %collective-permute-start.7 = (bf16[4,16,2048]{2,1,0:T(8,128)(2,1)S(1)}, bf16[4,16,2048]{2,1,0:T(8,128)(2,1)S(1)}, u32[]{:S(2)}, u32[]{:S(2)}) collective-permute-start(bf16[4,16,2048]{2,1,0:T(8,128)(2,1)S(1)} %collective-permute-done.5.refs_3_), channel_id=1, source_target_pairs={{3,0},{0,1},{1,2},{2,3},{7,4},{4,5},{5,6},{6,7},{11,8},{8,9},{9,10... | collective-permute-start | bytes 786440 | tf_op jit(solution)/shard_map/ppermute | solution.py:629
  43.0 14.1 %collective-permute-start.8 = (bf16[4,16,2048]{2,1,0:T(8,128)(2,1)S(1)}, bf16[4,16,2048]{2,1,0:T(8,128)(2,1)S(1)}, u32[]{:S(2)}, u32[]{:S(2)}) collective-permute-start(bf16[4,16,2048]{2,1,0:T(8,128)(2,1)S(1)} %collective-permute-done.4.refs_2_), channel_id=1, source_target_pairs={{3,0},{0,1},{1,2},{2,3},{7,4},{4,5},{5,6},{6,7},{11,8},{8,9},{9,10... | collective-permute-start | bytes 786440 | tf_op jit(solution)/shard_map/ppermute | solution.py:629
  44.5 12.6 %collective-permute-start.9 = (bf16[4,16,2048]{2,1,0:T(8,128)(2,1)S(1)}, bf16[4,16,2048]{2,1,0:T(8,128)(2,1)S(1)}, u32[]{:S(2)}, u32[]{:S(2)}) collective-permute-start(bf16[4,16,2048]{2,1,0:T(8,128)(2,1)S(1)} %collective-permute-done.6.refs_4_), channel_id=1, source_target_pairs={{1,0},{2,1},{3,2},{0,3},{5,4},{6,5},{7,6},{4,7},{9,8},{10,9},{11,1... | collective-permute-start | bytes 786440 | tf_op jit(solution)/shard_map/ppermute | solution.py:629
  57.1 15.1 %all-to-all-start.3 = ((bf16[32,16,256]{2,1,0:T(8,128)(2,1)}), bf16[32,16,256]{2,1,0:T(8,128)(2,1)S(1)}, u32[]{:S(2)}, u32[]{:S(2)}) async-start(bf16[32,16,256]{2,1,0:T(8,128)(2,1)} %copy-done.4), calls=%async_computation.3 | async-start | bytes 524288 | tf_op jit(solution)/shard_map/all_to_all | solution.py:621
  72.9 50.8 %all-to-all-start.2 = ((bf16[32,16,2304]{2,1,0:T(8,128)(2,1)}), bf16[32,16,2304]{2,1,0:T(8,128)(2,1)S(1)}, u32[]{:S(2)}, u32[]{:S(2)}) async-start(bf16[32,16,2304]{2,1,0:T(8,128)(2,1)} %block_product.3.after_ref), calls=%async_computation.2 | async-start | bytes 4718592 | tf_op jit(solution)/shard_map/all_to_all | solution.py:621
  85.1 21.3 %collective-permute-start.10 = (f32[8,8,256]{2,1,0:T(8,128)S(1)}, f32[8,8,256]{2,1,0:T(8,128)S(1)}, u32[]{:S(2)}, u32[]{:S(2)}) collective-permute-start(f32[8,8,256]{2,1,0:T(8,128)S(1)} %get-tuple-element.35), channel_id=1, source_target_pairs={{24,0},{25,1},{26,2},{27,3},{28,4},{29,5},{30,6},{31,7},{0,8},{1,9... | collective-permute-start | bytes 196616 | tf_op jit(solution)/shard_map/ppermute | solution.py:634
  86.9 20.2 %collective-permute-start.11 = (f32[8,8,256]{2,1,0:T(8,128)S(1)}, f32[8,8,256]{2,1,0:T(8,128)S(1)}, u32[]{:S(2)}, u32[]{:S(2)}) collective-permute-start(f32[8,8,256]{2,1,0:T(8,128)S(1)} %get-tuple-element.36), channel_id=1, source_target_pairs={{16,0},{17,1},{18,2},{19,3},{20,4},{21,5},{22,6},{23,7},{24,8},{25... | collective-permute-start | bytes 196616 | tf_op jit(solution)/shard_map/ppermute | solution.py:634
  89.7 17.5 %collective-permute-start.12 = (f32[8,8,256]{2,1,0:T(8,128)S(1)}, f32[8,8,256]{2,1,0:T(8,128)S(1)}, u32[]{:S(2)}, u32[]{:S(2)}) collective-permute-start(f32[8,8,256]{2,1,0:T(8,128)S(1)} %get-tuple-element.37), channel_id=1, source_target_pairs={{8,0},{9,1},{10,2},{11,3},{12,4},{13,5},{14,6},{15,7},{16,8},{17,9... | collective-permute-start | bytes 196616 | tf_op jit(solution)/shard_map/ppermute | solution.py:634
  107.2 9.3 %collective-permute-start.13 = (f32[8,256]{1,0:T(8,128)S(1)}, f32[8,256]{1,0:T(8,128)S(1)}, u32[]{:S(2)}, u32[]{:S(2)}) collective-permute-start(f32[8,256]{1,0:T(8,128)S(1)} %get-tuple-element.39), channel_id=1, source_target_pairs={{3,0},{0,1},{1,2},{2,3},{7,4},{4,5},{5,6},{6,7},{11,8},{8,9},{9,10... | collective-permute-start | bytes 24584 | tf_op jit(solution)/shard_map/ppermute | solution.py:629
  109.2 7.8 %collective-permute-start.14 = (f32[8,256]{1,0:T(8,128)S(1)}, f32[8,256]{1,0:T(8,128)S(1)}, u32[]{:S(2)}, u32[]{:S(2)}) collective-permute-start(f32[8,256]{1,0:T(8,128)S(1)} %get-tuple-element.40), channel_id=1, source_target_pairs={{1,0},{2,1},{3,2},{0,3},{5,4},{6,5},{7,6},{4,7},{9,8},{10,9},{11,1... | collective-permute-start | bytes 24584 | tf_op jit(solution)/shard_map/ppermute | solution.py:629
  110.6 9.5 %collective-permute-start.15 = (f32[8,256]{1,0:T(8,128)S(1)}, f32[8,256]{1,0:T(8,128)S(1)}, u32[]{:S(2)}, u32[]{:S(2)}) collective-permute-start(f32[8,256]{1,0:T(8,128)S(1)} %get-tuple-element.41), channel_id=1, source_target_pairs={{4,0},{5,1},{6,2},{7,3},{0,4},{1,5},{2,6},{3,7},{12,8},{13,9},{14,... | collective-permute-start | bytes 24584 | tf_op jit(solution)/shard_map/ppermute | solution.py:629
  112.3 8.3 %collective-permute-start.16 = (f32[8,256]{1,0:T(8,128)S(1)}, f32[8,256]{1,0:T(8,128)S(1)}, u32[]{:S(2)}, u32[]{:S(2)}) collective-permute-start(f32[8,256]{1,0:T(8,128)S(1)} %get-tuple-element.42), channel_id=1, source_target_pairs={{7,0},{4,1},{5,2},{6,3},{3,4},{0,5},{1,6},{2,7},{15,8},{12,9},{13,... | collective-permute-start | bytes 24584 | tf_op jit(solution)/shard_map/ppermute | solution.py:629
  113.1 8.2 %collective-permute-start.17 = (f32[8,256]{1,0:T(8,128)S(1)}, f32[8,256]{1,0:T(8,128)S(1)}, u32[]{:S(2)}, u32[]{:S(2)}) collective-permute-start(f32[8,256]{1,0:T(8,128)S(1)} %get-tuple-element.43), channel_id=1, source_target_pairs={{5,0},{6,1},{7,2},{4,3},{1,4},{2,5},{3,6},{0,7},{13,8},{14,9},{15,... | collective-permute-start | bytes 24584 | tf_op jit(solution)/shard_map/ppermute | solution.py:629
  116.5 5.4 %collective-permute-start.18 = (f32[8,256]{1,0:T(8,128)S(1)}, f32[8,256]{1,0:T(8,128)S(1)}, u32[]{:S(2)}, u32[]{:S(2)}) collective-permute-start(f32[8,256]{1,0:T(8,128)S(1)} %get-tuple-element.44), channel_id=1, source_target_pairs={{2,0},{3,1},{0,2},{1,3},{6,4},{7,5},{4,6},{5,7},{10,8},{11,9},{8,1... | collective-permute-start | bytes 24584 | tf_op jit(solution)/shard_map/ppermute | solution.py:629
  117.0 6.1 %collective-permute-start.19 = (f32[8,256]{1,0:T(8,128)S(1)}, f32[8,256]{1,0:T(8,128)S(1)}, u32[]{:S(2)}, u32[]{:S(2)}) collective-permute-start(f32[8,256]{1,0:T(8,128)S(1)} %get-tuple-element.45), channel_id=1, source_target_pairs={{6,0},{7,1},{4,2},{5,3},{2,4},{3,5},{0,6},{1,7},{14,8},{15,9},{12,... | collective-permute-start | bytes 24584 | tf_op jit(solution)/shard_map/ppermute | solution.py:629
  (22 other events, 188.9 us)

commit v10 on v3

--- a/solution.py
+++ b/solution.py
@@ -25,12 +25,11 @@
 EPS = 1e-06
 MASKED_SCORE = -1e30
 
-VMEM_LIMIT = 48 * 1024 * 1024
-VMEM_MOST = 60 * 1024 * 1024
-VMEM_LESS = 32 * 1024 * 1024
+VMEM_LIMIT = 32 * 1024 * 1024
 VMEM = pl.BlockSpec(memory_space=pltpu.VMEM)
 SMEM = pl.BlockSpec(memory_space=pltpu.SMEM)
 HBM = pl.BlockSpec(memory_space=pltpu.HBM)
+UNREAD = pl.BlockSpec(memory_space=pl.ANY)
 
 
 def whole(shape):
@@ -41,8 +40,12 @@
     return pl.CostEstimate(flops=flops, bytes_accessed=moved, transcendentals=0)
 
 
-def kernel_params(limit=VMEM_LIMIT):
-    return pltpu.CompilerParams(vmem_limit_bytes=limit)
+def in_hbm(array):
+    return pltpu.with_memory_space_constraint(array, pltpu.HBM)
+
+
+def kernel_params():
+    return pltpu.CompilerParams(vmem_limit_bytes=VMEM_LIMIT)
 
 
 def norm_kernel(main_hbm, cont_hbm, gain_hbm, out_ref, main_ref, cont_ref, gain_ref, rows_ref, piece_ref, sems):
@@ -89,7 +92,7 @@
         compiler_params=kernel_params(),
         cost_estimate=cost(10**6, 4 * 10**6),
         name="norm_rows",
-    )(main, cont, gain)
+    )(in_hbm(main), in_hbm(cont), in_hbm(gain))
 
 
 def weight_tile(n, tiles, w_hbm, w_ref, sems):
@@ -201,12 +204,12 @@
         out_shape=jax.ShapeDtypeStruct(out, jnp.bfloat16),
         grid=(tiles,),
         in_specs=[VMEM] * len(operands) + [HBM],
-        out_specs=whole(out) if places else VMEM,
+        out_specs=VMEM,
         scratch_shapes=scratch,
-        compiler_params=kernel_params(VMEM_LESS),
+        compiler_params=kernel_params(),
         cost_estimate=cost(2 * members * (CTOK + STEPS) * FEATURES * tiles * TILE, 12 * 10**6),
         name="block_product",
-    )(*operands, blocks)
+    )(*operands, in_hbm(blocks))
 
 
 def summed_block(parts_ref, c, lanes):
@@ -323,7 +326,7 @@
             jax.ShapeDtypeStruct((8, 2 * KV_WIDTH), jnp.float32),
         ),
         in_specs=[SMEM] + [VMEM] * 5,
-        out_specs=(whole((32, 16, TILE)), whole((8, 2 * KV_WIDTH))),
+        out_specs=(VMEM, VMEM),
         scratch_shapes=[
             pltpu.VMEM((8, QKV), jnp.float32),
             pltpu.VMEM((ROW_BLOCKS, 16, TILE), jnp.float32),
@@ -364,8 +367,8 @@
     return pl.pallas_call(
         attend_cont_kernel,
         out_shape=jax.ShapeDtypeStruct((CTOK, D), jnp.bfloat16),
-        in_specs=[SMEM, SMEM] + [VMEM] * 5 + [whole((8, 2 * KV_WIDTH))],
-        out_specs=whole((CTOK, D)),
+        in_specs=[SMEM, SMEM] + [VMEM] * 6,
+        out_specs=VMEM,
         scratch_shapes=[pltpu.VMEM((CTOK, QKV), jnp.float32)],
         compiler_params=kernel_params(),
         cost_estimate=cost(4 * 10**8, 8 * 10**6),
@@ -373,7 +376,7 @@
     )(*args)
 
 
-def readout_kernel(head_ref, w_hbm, out_ref, w_ref, sem):
+def readout_kernel(head_ref, w_hbm, after_ref, out_ref, w_ref, sem):
     copy = pltpu.make_async_copy(w_hbm.at[0], w_ref, sem)
     copy.start()
     row = head_ref[pl.ds(lax.rem(lax.axis_index("tp"), COL_BLOCKS), 1), :]
@@ -388,17 +391,17 @@
     out_ref[...] = prod[0:1] + prod[1:2] + prod[2:3]
 
 
-def readout(value_head, blocks):
+def readout(value_head, blocks, after):
     return pl.pallas_call(
         readout_kernel,
         out_shape=jax.ShapeDtypeStruct((1, FEATURES), jnp.float32),
-        in_specs=[whole(value_head.shape), HBM],
-        out_specs=whole((1, FEATURES)),
+        in_specs=[VMEM, HBM, UNREAD],
+        out_specs=VMEM,
         scratch_shapes=[pltpu.VMEM((FEATURES, D // COL_BLOCKS), jnp.bfloat16), pltpu.SemaphoreType.DMA],
         compiler_params=kernel_params(),
         cost_estimate=cost(2 * 10**8, 5 * 10**6),
         name="readout",
-    )(value_head, blocks)
+    )(value_head, in_hbm(blocks), after)
 
 
 def out_kernel(tiles, x_ref, read_ref, w_hbm, out_ref, rows_ref, wide_ref, read8_ref, w_ref, sems):
@@ -439,8 +442,8 @@
         functools.partial(out_kernel, tiles),
         out_shape=jax.ShapeDtypeStruct((members, 16, TILE), jnp.float32),
         grid=(tiles,),
-        in_specs=[whole(rows.shape), whole(read.shape), HBM],
-        out_specs=whole((members, 16, TILE)),
+        in_specs=[VMEM, VMEM, HBM],
+        out_specs=VMEM,
         scratch_shapes=[
             pltpu.VMEM((members * STEPS, FEATURES), jnp.bfloat16),
             pltpu.VMEM((TILE // 128, members * 16, 128), jnp.float32),
@@ -448,10 +451,10 @@
             pltpu.VMEM((tiles, FEATURES, TILE), jnp.bfloat16),
             pltpu.SemaphoreType.DMA((tiles,)),
         ],
-        compiler_params=kernel_params(VMEM_MOST),
+        compiler_params=kernel_params(),
         cost_estimate=cost(3 * 10**8, 5 * 10**6),
         name="out_product",
-    )(rows, read, blocks)
+    )(rows, read, in_hbm(blocks))
 
 
 def finish_kernel(parts_ref, main_ref, cont_ref, head_ref, mixed_ref, out_ref, score_ref, wide_ref):
@@ -485,10 +488,10 @@
             jax.ShapeDtypeStruct((STEPS, D), jnp.bfloat16),
             jax.ShapeDtypeStruct((8, 128), jnp.float32),
         ),
-        in_specs=[whole(parts.shape), whole(main.shape), whole(cont.shape), whole(head.shape), whole(mixed.shape)],
+        in_specs=[VMEM] * 5,
         out_specs=(whole((STEPS, D)), whole((8, 128))),
         scratch_shapes=[pltpu.VMEM((8, D), jnp.float32)],
-        compiler_params=kernel_params(VMEM_MOST),
+        compiler_params=kernel_params(),
         cost_estimate=cost(10**6, 2 * 10**6),
         name="finish",
     )(parts, main, cont, head, mixed)
@@ -520,17 +523,14 @@
 
 def forward_product(rows, blocks):
     near = lax.all_to_all(rows, "tp", split_axis=0, concat_axis=0, tiled=True, axis_index_groups=ALONG)
-    half = ROW_BLOCKS // 2
     over = from_side(near, 1, 0)
-    here, far, places = [], [], []
+    here, places = [], []
     for dy, mine in ((0, near), (1, over)):
-        after = from_side(mine, 0, 1)
-        before = from_side(mine, 0, 3)
-        far += [from_side(before[:half], 0, 3), from_side(after[half:], 0, 1)]
-        here += [mine, after, before]
+        here += [mine, from_side(mine, 0, 1), from_side(mine, 0, 3)]
         places += [(dy, 0), (dy, 1), (dy, 3)]
+    far = [from_side(here[2], 0, 3), from_side(here[4], 0, 1)]
     earlier = block_product(here, blocks)
-    return block_product(far, blocks, earlier, tuple(places) + ((0, 2), (1, 2)))
+    return block_product(far, blocks, earlier, tuple(places) + ((0, 2), (1, 2))), near
 
 
 def on_device(
@@ -544,12 +544,12 @@
     step = jnp.arange(CTOK, dtype=jnp.int32) % STEPS
     main_tables = rope_tables(prefix_len + step[:8])
     cont_tables = rope_tables(prefix_len + boundary + step)
-    read = readout(value_head.reshape(COL_BLOCKS, D // COL_BLOCKS), w_out)
-    parts = exchange(forward_product(norm_rows(main, cont, rms_gain[None, :]), w_qkv))
+    parts, near = forward_product(norm_rows(main, cont, rms_gain[None, :]), w_qkv)
+    parts = exchange(parts)
+    read = readout(value_head.reshape(COL_BLOCKS, D // COL_BLOCKS), w_out, near)
     mixed, main_kv = attend_main(prefix_len, parts, bias, *main_tables, cache)
     mixed = exchange(mixed)
     cont_mixed = attend_cont(prefix_len, boundary, parts, bias, *cont_tables, cache, main_kv)
-    mixed, cont_mixed, read = lax.optimization_barrier((mixed, cont_mixed, read))
     parts = exchange(out_product(mixed, read, w_out))
     main_out, score = finish(parts, main, cont, head, cont_mixed)
     return main_out[None], score[0, :1]

time: 125 us -> 125 us (level)
  blocking collectives: 31.4 us -> 12.2 us
  waiting for transfers between devices: 30.7 us -> 46.5 us
  starting transfers between devices: 25.8 us -> 30 us
  local copies, waits for them, and re-layouts: 12.4 us -> 8.47 us
  Pallas kernels: 21 us -> 24.2 us
    all_to_all x1 -> x0, blocking collectives: 19.2 us -> none  [exchange(): return lax.all_to_all(rows, 'tp', split_axis=0, concat_axis=0, tiled=True)]
    all_to_all x2 -> x3, waiting for transfers between devices: 24.5 us -> 34.7 us  [exchange(): return lax.all_to_all(rows, 'tp', split_axis=0, concat_axis=0, tiled=True)]
    all_to_all x2 -> x3, starting transfers between devices: 11 us -> 18.4 us  [exchange(): return lax.all_to_all(rows, 'tp', split_axis=0, concat_axis=0, tiled=True)]
    ppermute x9 -> x7, waiting for transfers between devices: 6.23 us -> 11.8 us  [from_side(): return lax.ppermute(rows, 'tp', route)]
    ppermute x9 -> x7, starting transfers between devices: 14.8 us -> 11.6 us  [from_side(): return lax.ppermute(rows, 'tp', route)]
    unnamed x28, local copies, waits for them, and re-layouts: 10.4 us -> 7.94 us
    pallas_call x1, Pallas kernels: 1.53 us -> 3.4 us  [readout(): pl.pallas_call(readout_kernel, out_shape=jax.ShapeDtypeStruct((1, FEATURE...]
    pallas_call x2, Pallas kernels: 6.39 us -> 7.89 us  [block_product(): pl.pallas_call(functools.partial(product_kernel, tiles, counts, places),...]
  transfers between devices with their start and end apart: 11 -> 10, of which waited for: 4 -> 6; matrix products, arithmetic and copies ran while one was open for 1% -> 0% of each run, Pallas kernels for 7% -> 9%
where the time goes in v10:
time: 125 us; the launch traced here: 124 us
  waiting for transfers between devices  46.5 us (37%)
  starting transfers between devices  30 us (24%)
  Pallas kernels  24.2 us (19%)
  blocking collectives  12.2 us (10%)
  local copies, waits for them, and re-layouts  8.47 us (7%)
  between operations  2.15 us (2%)
    all_to_all x3, waiting for transfers between devices, exchange(): return lax.all_to_all(rows, 'tp', split_axis=0, concat_axis=0, tiled=True)  34.7 us
    all_to_all x3, starting transfers between devices, exchange(): return lax.all_to_all(rows, 'tp', split_axis=0, concat_axis=0, tiled=True)  18.4 us
    all_to_all x1, blocking collectives, forward_product(): lax.all_to_all(rows, 'tp', split_axis=0, concat_axis=0, tiled=True, axis_...  12.2 us
    ppermute x7, waiting for transfers between devices, from_side(): return lax.ppermute(rows, 'tp', route)  11.8 us
    ppermute x7, starting transfers between devices, from_side(): return lax.ppermute(rows, 'tp', route)  11.6 us
    unnamed x28, local copies, waits for them, and re-layouts  7.94 us
    pallas_call x2, Pallas kernels, block_product(): pl.pallas_call(functools.partial(product_kernel, tiles, counts, places),...  7.89 us
    pallas_call x1, Pallas kernels, out_product(): pl.pallas_call(functools.partial(out_kernel, tiles), out_shape=jax.ShapeD...  3.55 us
  transfers between devices with their start and end apart: 10, of which 6 were waited for; matrix products, arithmetic and copies ran while one was open for 0% of the time, Pallas kernels for 9%

profile of v10, /device:TPU:0, one launch (start us, length us, event | category | flops | bytes accessed | tf_op | source)
XLA Modules:
  0.0 123.9 jit_solution(12996841571918873667)
XLA Ops:
  0.6 1.4 %norm_rows.1 = bf16[4,16,2304]{2,1,0:T(8,128)(2,1)S(1)} custom-call(bf16[2,8192]{1,0:T(2,128)(2,1)} %bitcast.17, bf16[8,2,8192]{2,1,0:T(2,128)(2,1)} %bitcast.13, f32[1,8192]{1,0:T(1,128)} %bitcast.20), custom_call_target="tpu_custom_call" | custom-call | flops 1000000 | bytes 4000000 | tf_op jit(solution)/shard_map/norm_rows/pallas_call | solution.py:79
  2.0 12.2 %all_to_all.20.refs_0_.after_ref = bf16[4,16,2304]{2,1,0:T(8,128)(2,1)S(1)} all-to-all(bf16[4,16,2304]{2,1,0:T(8,128)(2,1)S(1)} %norm_rows.1), channel_id=1, replica_groups={{0,8,16,24},{1,9,17,25},{2,10,18,26},{3,11,19,27},{4,12,20,28},{5,13,21..., dimensions={0} | all-to-all | bytes 589824 | tf_op jit(solution)/shard_map/all_to_all | solution.py:525
  14.2 1.6 %collective-permute-start.2 = (bf16[4,16,2304]{2,1,0:T(8,128)(2,1)S(1)}, bf16[4,16,2304]{2,1,0:T(8,128)(2,1)S(1)}, u32[]{:S(2)}, u32[]{:S(2)}) collective-permute-start(bf16[4,16,2304]{2,1,0:T(8,128)(2,1)S(1)} %all_to_all.20.refs_0_.after_ref), channel_id=1, source_target_pairs={{4,0},{5,1},{6,2},{7,3},{0,4},{1,5},{2,6},{3,7},{12,8},{13,9},{14,... | collective-permute-start | bytes 884744 | tf_op jit(solution)/shard_map/ppermute | solution.py:521
  15.8 1.5 %collective-permute-start = (bf16[4,16,2304]{2,1,0:T(8,128)(2,1)S(1)}, bf16[4,16,2304]{2,1,0:T(8,128)(2,1)S(1)}, u32[]{:S(2)}, u32[]{:S(2)}) collective-permute-start(bf16[4,16,2304]{2,1,0:T(8,128)(2,1)S(1)} %all_to_all.20.refs_0_.after_ref), channel_id=1, source_target_pairs={{3,0},{0,1},{1,2},{2,3},{7,4},{4,5},{5,6},{6,7},{11,8},{8,9},{9,10... | collective-permute-start | bytes 884744 | tf_op jit(solution)/shard_map/ppermute | solution.py:521
  17.3 4.2 %collective-permute-done.2.refs_3_ = bf16[4,16,2304]{2,1,0:T(8,128)(2,1)S(1)} collective-permute-done((bf16[4,16,2304]{2,1,0:T(8,128)(2,1)S(1)}, bf16[4,16,2304]{2,1,0:T(8,128)(2,1)S(1)}, u32[]{:S(2)}, u32[]{:S(2)}) %collective-permute-start.2) | collective-permute-done | bytes 294944 | tf_op jit(solution)/shard_map/ppermute | solution.py:521
  21.5 2.8 %collective-permute-start.3 = (bf16[4,16,2304]{2,1,0:T(8,128)(2,1)S(1)}, bf16[4,16,2304]{2,1,0:T(8,128)(2,1)S(1)}, u32[]{:S(2)}, u32[]{:S(2)}) collective-permute-start(bf16[4,16,2304]{2,1,0:T(8,128)(2,1)S(1)} %collective-permute-done.2.refs_3_), channel_id=1, source_target_pairs={{1,0},{2,1},{3,2},{0,3},{5,4},{6,5},{7,6},{4,7},{9,8},{10,9},{11,1... | collective-permute-start | bytes 884744 | tf_op jit(solution)/shard_map/ppermute | solution.py:521
  25.1 1.2 collective-permute-start.6
  26.3 5.4 %collective-permute-done.3.refs_4_ = bf16[4,16,2304]{2,1,0:T(8,128)(2,1)S(1)} collective-permute-done((bf16[4,16,2304]{2,1,0:T(8,128)(2,1)S(1)}, bf16[4,16,2304]{2,1,0:T(8,128)(2,1)S(1)}, u32[]{:S(2)}, u32[]{:S(2)}) %collective-permute-start.3) | collective-permute-done | bytes 294944 | tf_op jit(solution)/shard_map/ppermute | solution.py:521
  31.7 3.7 %collective-permute-start.4 = (bf16[4,16,2304]{2,1,0:T(8,128)(2,1)S(1)}, bf16[4,16,2304]{2,1,0:T(8,128)(2,1)S(1)}, u32[]{:S(2)}, u32[]{:S(2)}) collective-permute-start(bf16[4,16,2304]{2,1,0:T(8,128)(2,1)S(1)} %collective-permute-done.3.refs_4_), channel_id=1, source_target_pairs={{1,0},{2,1},{3,2},{0,3},{5,4},{6,5},{7,6},{4,7},{9,8},{10,9},{11,1... | collective-permute-start | bytes 884744 | tf_op jit(solution)/shard_map/ppermute | solution.py:521
  35.4 2.2 %collective-permute-done.5.refs_1_ = bf16[4,16,2304]{2,1,0:T(8,128)(2,1)S(1)} collective-permute-done((bf16[4,16,2304]{2,1,0:T(8,128)(2,1)S(1)}, bf16[4,16,2304]{2,1,0:T(8,128)(2,1)S(1)}, u32[]{:S(2)}, u32[]{:S(2)}) %collective-permute-start.5) | collective-permute-done | bytes 294944 | tf_op jit(solution)/shard_map/ppermute | solution.py:521
  37.6 4.7 %block_product.2.refs_2_ = bf16[24,16,2304]{2,1,0:T(8,128)(2,1)S(1)} custom-call(bf16[4,16,2304]{2,1,0:T(8,128)(2,1)S(1)} %all_to_all.20.refs_0_.after_ref, bf16[4,16,2304]{2,1,0:T(8,128)(2,1)S(1)} %collective-permute-done.5.refs_1_, bf16[4,16,2304]{2,1,0:T(8,128)(2,1)S(1)} %collective-permute-done.refs_2_, ...), custom_call_target="tpu_custom_call" | custom-call | flops 2264924160 | bytes 12000000 | tf_op jit(solution)/shard_map/block_product/pallas_call | solution.py:202
  42.3 3.2 %block_product.3 = bf16[32,16,2304]{2,1,0:T(8,128)(2,1)S(1)} custom-call(bf16[4,16,2304]{2,1,0:T(8,128)(2,1)S(1)} %collective-permute-done.1.refs_0_, bf16[4,16,2304]{2,1,0:T(8,128)(2,1)S(1)} %collective-permute-done.4.refs_1_, bf16[24,16,2304]{2,1,0:T(8,128)(2,1)S(1)} %block_product.2.refs_2_, bf16[1,2048,1280]{2,1,0:T(8,128)(2,1)} %refs_3_.1), custom_call_target="tpu_custom_call" | custom-call | flops 754974720 | bytes 12000000 | tf_op jit(solution)/shard_map/block_product/pallas_call | solution.py:202
  45.6 1.4 %copy-done = bf16[32,16,2304]{2,1,0:T(8,128)(2,1)} copy-done((bf16[32,16,2304]{2,1,0:T(8,128)(2,1)}, bf16[32,16,2304]{2,1,0:T(8,128)(2,1)S(1)}, u32[]{:S(2)}) %copy-start) | copy-done | bytes 2359320
  47.0 7.4 %all-to-all-start.1 = ((bf16[32,16,2304]{2,1,0:T(8,128)(2,1)}), bf16[32,16,2304]{2,1,0:T(8,128)(2,1)S(1)}, u32[]{:S(2)}, u32[]{:S(2)}) async-start(bf16[32,16,2304]{2,1,0:T(8,128)(2,1)} %copy-done), calls=%async_computation.1 | async-start | bytes 4718592 | tf_op jit(solution)/shard_map/all_to_all | solution.py:510
  55.3 24.9 %all-to-all-done.1.parts_ref = bf16[32,16,2304]{2,1,0:T(8,128)(2,1)S(1)} async-done(((bf16[32,16,2304]{2,1,0:T(8,128)(2,1)}), bf16[32,16,2304]{2,1,0:T(8,128)(2,1)S(1)}, u32[]{:S(2)}, u32[]{:S(2)}) %all-to-all-start.1) | async-done | bytes 2359328 | tf_op jit(solution)/shard_map/all_to_all | solution.py:510
  80.3 3.0 %attend_main.1 = (bf16[32,16,256]{2,1,0:T(8,128)(2,1)S(1)}, f32[8,2048]{1,0:T(8,128)S(1)}) custom-call(s32[1]{0:T(128)} %copy.12.len_ref, bf16[32,16,2304]{2,1,0:T(8,128)(2,1)S(1)} %all-to-all-done.1.parts_ref, f32[1,10240]{1,0:T(1,128)S(1)} %bitcast.15, f32[8,128]{1,0:T(8,128)S(1)} %get-tuple-element.16.cos_ref, f32[8,128]{1,0:T(8,128)S(1)} %get-tuple-element.17.sin_ref, ...), custom_call_target="tpu_custom_call" | custom-call | flops 200000000 | bytes 6000000 | tf_op jit(solution)/shard_map/attend_main/pallas_call | solution.py:322
  84.6 6.2 %all-to-all-start.2 = ((bf16[32,16,256]{2,1,0:T(8,128)(2,1)}), bf16[32,16,256]{2,1,0:T(8,128)(2,1)}, u32[]{:S(2)}, u32[]{:S(2)}) async-start(bf16[32,16,256]{2,1,0:T(8,128)(2,1)} %copy-done.8), calls=%async_computation.2 | async-start | bytes 524288 | tf_op jit(solution)/shard_map/all_to_all | solution.py:510
  91.8 3.4 %readout.1.read_ref = f32[1,2048]{1,0:T(1,128)S(1)} custom-call(f32[8,1024]{1,0:T(8,128)S(1)} %reshape.34.head_ref, bf16[1,2048,1024]{2,1,0:T(8,128)(2,1)} %w_hbm.3, bf16[4,16,2304]{2,1,0:T(8,128)(2,1)S(1)} %copy-done.3), custom_call_target="tpu_custom_call" | custom-call | flops 200000000 | bytes 5000000 | tf_op jit(solution)/shard_map/readout/pallas_call | solution.py:395
  95.2 4.8 %all-to-all-done.2.x_ref = bf16[32,16,256]{2,1,0:T(8,128)(2,1)} async-done(((bf16[32,16,256]{2,1,0:T(8,128)(2,1)}), bf16[32,16,256]{2,1,0:T(8,128)(2,1)}, u32[]{:S(2)}, u32[]{:S(2)}) %all-to-all-start.2) | async-done | bytes 262176 | tf_op jit(solution)/shard_map/all_to_all | solution.py:510
  100.0 3.5 %out_product.1 = f32[32,16,256]{2,1,0:T(8,128)S(1)} custom-call(bf16[32,16,256]{2,1,0:T(8,128)(2,1)} %all-to-all-done.2.x_ref, f32[1,2048]{1,0:T(1,128)S(1)} %readout.1.read_ref, bf16[1,2048,1024]{2,1,0:T(8,128)(2,1)} %w_hbm.3), custom_call_target="tpu_custom_call" | custom-call | flops 300000000 | bytes 5000000 | tf_op jit(solution)/shard_map/out_product/pallas_call | solution.py:441
  104.3 4.8 %all-to-all-start.3 = ((f32[32,16,256]{2,1,0:T(8,128)}), f32[32,16,256]{2,1,0:T(8,128)}, u32[]{:S(2)}, u32[]{:S(2)}) async-start(f32[32,16,256]{2,1,0:T(8,128)} %copy-done.4), calls=%async_computation.3 | async-start | bytes 1048576 | tf_op jit(solution)/shard_map/all_to_all | solution.py:510
  110.8 3.0 %attend_cont.1.mixed_ref = bf16[16,8192]{1,0:T(8,128)(2,1)S(1)} custom-call(s32[1]{0:T(128)} %copy.12.len_ref, s32[1]{0:T(128)S(6)} %copy.13.bound_ref, bf16[32,16,2304]{2,1,0:T(8,128)(2,1)S(1)} %all-to-all-done.1.parts_ref, f32[1,10240]{1,0:T(1,128)S(1)} %bitcast.16, f32[16,128]{1,0:T(8,128)S(1)} %get-tuple-element.18.cos_ref, ...), custom_call_target="tpu_custom_call" | custom-call | flops 400000000 | bytes 8000000 | tf_op jit(solution)/shard_map/attend_cont/pallas_call | solution.py:367
  114.5 4.9 %all-to-all-done.3.parts_ref = f32[32,16,256]{2,1,0:T(8,128)} async-done(((f32[32,16,256]{2,1,0:T(8,128)}), f32[32,16,256]{2,1,0:T(8,128)}, u32[]{:S(2)}, u32[]{:S(2)}) %all-to-all-start.3) | async-done | bytes 524320 | tf_op jit(solution)/shard_map/all_to_all | solution.py:510
  121.4 2.0 %finish.1 = (bf16[2,8192]{1,0:T(2,128)(2,1)}, f32[8,128]{1,0:T(8,128)S(1)}) custom-call(f32[32,16,256]{2,1,0:T(8,128)} %all-to-all-done.3.parts_ref, bf16[2,8192]{1,0:T(2,128)(2,1)S(1)} %bitcast.18, bf16[8,2,8192]{2,1,0:T(2,128)(2,1)S(1)} %bitcast.14, f32[1,8192]{1,0:T(1,128)S(1)} %bitcast.19, bf16[16,8192]{1,0:T(8,128)(2,1)S(1)} %copy-done.6), custom_call_target="tpu_custom_call" | custom-call | flops 1000000 | bytes 2000000 | tf_op jit(solution)/shard_map/finish/pallas_call | solution.py:485
  (43 shorter events, 8.3 us)
Async XLA Ops:
  14.2 28.0 %copy-start.2 = (bf16[4,16,2304]{2,1,0:T(8,128)(2,1)}, bf16[4,16,2304]{2,1,0:T(8,128)(2,1)S(1)}, u32[]{:S(2)}) copy-start(bf16[4,16,2304]{2,1,0:T(8,128)(2,1)S(1)} %all_to_all.20.refs_0_.after_ref) | copy-start | bytes 884740
  14.2 7.3 %collective-permute-start.2 = (bf16[4,16,2304]{2,1,0:T(8,128)(2,1)S(1)}, bf16[4,16,2304]{2,1,0:T(8,128)(2,1)S(1)}, u32[]{:S(2)}, u32[]{:S(2)}) collective-permute-start(bf16[4,16,2304]{2,1,0:T(8,128)(2,1)S(1)} %all_to_all.20.refs_0_.after_ref), channel_id=1, source_target_pairs={{4,0},{5,1},{6,2},{7,3},{0,4},{1,5},{2,6},{3,7},{12,8},{13,9},{14,... | collective-permute-start | bytes 884744 | tf_op jit(solution)/shard_map/ppermute | solution.py:521
  15.8 10.5 %collective-permute-start = (bf16[4,16,2304]{2,1,0:T(8,128)(2,1)S(1)}, bf16[4,16,2304]{2,1,0:T(8,128)(2,1)S(1)}, u32[]{:S(2)}, u32[]{:S(2)}) collective-permute-start(bf16[4,16,2304]{2,1,0:T(8,128)(2,1)S(1)} %all_to_all.20.refs_0_.after_ref), channel_id=1, source_target_pairs={{3,0},{0,1},{1,2},{2,3},{7,4},{4,5},{5,6},{6,7},{11,8},{8,9},{9,10... | collective-permute-start | bytes 884744 | tf_op jit(solution)/shard_map/ppermute | solution.py:521
  21.5 10.2 %collective-permute-start.3 = (bf16[4,16,2304]{2,1,0:T(8,128)(2,1)S(1)}, bf16[4,16,2304]{2,1,0:T(8,128)(2,1)S(1)}, u32[]{:S(2)}, u32[]{:S(2)}) collective-permute-start(bf16[4,16,2304]{2,1,0:T(8,128)(2,1)S(1)} %collective-permute-done.2.refs_3_), channel_id=1, source_target_pairs={{1,0},{2,1},{3,2},{0,3},{5,4},{6,5},{7,6},{4,7},{9,8},{10,9},{11,1... | collective-permute-start | bytes 884744 | tf_op jit(solution)/shard_map/ppermute | solution.py:521
  24.3 13.3 %collective-permute-start.5 = (bf16[4,16,2304]{2,1,0:T(8,128)(2,1)S(1)}, bf16[4,16,2304]{2,1,0:T(8,128)(2,1)S(1)}, u32[]{:S(2)}, u32[]{:S(2)}) collective-permute-start(bf16[4,16,2304]{2,1,0:T(8,128)(2,1)S(1)} %all_to_all.20.refs_0_.after_ref), channel_id=1, source_target_pairs={{1,0},{2,1},{3,2},{0,3},{5,4},{6,5},{7,6},{4,7},{9,8},{10,9},{11,1... | collective-permute-start | bytes 884744 | tf_op jit(solution)/shard_map/ppermute | solution.py:521
  25.1 12.5 %collective-permute-start.6 = (bf16[4,16,2304]{2,1,0:T(8,128)(2,1)S(1)}, bf16[4,16,2304]{2,1,0:T(8,128)(2,1)S(1)}, u32[]{:S(2)}, u32[]{:S(2)}) collective-permute-start(bf16[4,16,2304]{2,1,0:T(8,128)(2,1)S(1)} %collective-permute-done.2.refs_3_), channel_id=1, source_target_pairs={{3,0},{0,1},{1,2},{2,3},{7,4},{4,5},{5,6},{6,7},{11,8},{8,9},{9,10... | collective-permute-start | bytes 884744 | tf_op jit(solution)/shard_map/ppermute | solution.py:521
  26.3 16.0 %collective-permute-start.1 = (bf16[4,16,2304]{2,1,0:T(8,128)(2,1)S(1)}, bf16[4,16,2304]{2,1,0:T(8,128)(2,1)S(1)}, u32[]{:S(2)}, u32[]{:S(2)}) collective-permute-start(bf16[4,16,2304]{2,1,0:T(8,128)(2,1)S(1)} %collective-permute-done.refs_2_), channel_id=1, source_target_pairs={{3,0},{0,1},{1,2},{2,3},{7,4},{4,5},{5,6},{6,7},{11,8},{8,9},{9,10... | collective-permute-start | bytes 884744 | tf_op jit(solution)/shard_map/ppermute | solution.py:521
  31.7 10.6 %collective-permute-start.4 = (bf16[4,16,2304]{2,1,0:T(8,128)(2,1)S(1)}, bf16[4,16,2304]{2,1,0:T(8,128)(2,1)S(1)}, u32[]{:S(2)}, u32[]{:S(2)}) collective-permute-start(bf16[4,16,2304]{2,1,0:T(8,128)(2,1)S(1)} %collective-permute-done.3.refs_4_), channel_id=1, source_target_pairs={{1,0},{2,1},{3,2},{0,3},{5,4},{6,5},{7,6},{4,7},{9,8},{10,9},{11,1... | collective-permute-start | bytes 884744 | tf_op jit(solution)/shard_map/ppermute | solution.py:521
  45.6 1.4 %copy-start = (bf16[32,16,2304]{2,1,0:T(8,128)(2,1)}, bf16[32,16,2304]{2,1,0:T(8,128)(2,1)S(1)}, u32[]{:S(2)}) copy-start(bf16[32,16,2304]{2,1,0:T(8,128)(2,1)S(1)} %block_product.3) | copy-start | bytes 7077892
  47.0 33.3 %copy-start.1 = (bf16[1,256,2048]{2,1,0:T(8,128)(2,1)S(1)}, bf16[1,256,2048]{2,1,0:T(8,128)(2,1)}, u32[]{:S(2)}) copy-start(bf16[1,256,2048]{2,1,0:T(8,128)(2,1)} %param.12) | copy-start | bytes 3145732
  47.0 33.3 %copy-start.9 = (f32[10240]{0:T(1024)S(1)}, f32[10240]{0:T(1024)}, u32[]{:S(2)}) copy-start(f32[10240]{0:T(1024)} %param.16) | copy-start | bytes 122884
  47.0 33.3 %all-to-all-start.1 = ((bf16[32,16,2304]{2,1,0:T(8,128)(2,1)}), bf16[32,16,2304]{2,1,0:T(8,128)(2,1)S(1)}, u32[]{:S(2)}, u32[]{:S(2)}) async-start(bf16[32,16,2304]{2,1,0:T(8,128)(2,1)} %copy-done), calls=%async_computation.1 | async-start | bytes 4718592 | tf_op jit(solution)/shard_map/all_to_all | solution.py:510
  54.4 36.4 %copy-start.11 = (f32[8192]{0:T(1024)S(1)}, f32[8192]{0:T(1024)}, u32[]{:S(2)}) copy-start(f32[8192]{0:T(1024)} %param.19) | copy-start | bytes 98308
  83.2 0.7 copy-start.8
  83.9 0.6 copy-start.12
  84.6 15.4 %all-to-all-start.2 = ((bf16[32,16,256]{2,1,0:T(8,128)(2,1)}), bf16[32,16,256]{2,1,0:T(8,128)(2,1)}, u32[]{:S(2)}, u32[]{:S(2)}) async-start(bf16[32,16,256]{2,1,0:T(8,128)(2,1)} %copy-done.8), calls=%async_computation.2 | async-start | bytes 524288 | tf_op jit(solution)/shard_map/all_to_all | solution.py:510
  90.8 1.0 copy-start.3
  103.5 0.8 copy-start.4
  104.3 15.1 %copy-start.10 = (bf16[1,2,8192]{2,1,0:T(2,128)(2,1)S(1)}, bf16[1,2,8192]{2,1,0:T(2,128)(2,1)}, u32[]{:S(2)}) copy-start(bf16[1,2,8192]{2,1,0:T(2,128)(2,1)} %param.10) | copy-start | bytes 98308
  104.3 15.1 %all-to-all-start.3 = ((f32[32,16,256]{2,1,0:T(8,128)}), f32[32,16,256]{2,1,0:T(8,128)}, u32[]{:S(2)}, u32[]{:S(2)}) async-start(f32[32,16,256]{2,1,0:T(8,128)} %copy-done.4), calls=%async_computation.3 | async-start | bytes 1048576 | tf_op jit(solution)/shard_map/all_to_all | solution.py:510
  110.0 0.8 copy-start.13
  113.8 0.7 copy-start.5
  119.5 1.0 copy-start.6
  120.4 0.9 copy-start.7

commit v11 on v6

--- a/solution.py
+++ b/solution.py
@@ -596,19 +596,17 @@
 
 def project(rows, blocks, bias):
     near = lax.all_to_all(rows, "tp", split_axis=0, concat_axis=0, tiled=True, axis_index_groups=ALONG)
-    half = ROW_BLOCKS // 2
     over = from_side(near, 1, 0)
-    sides, far = [], []
-    for mine in (near, over):
-        after = from_side(mine, 0, 1)
-        before = from_side(mine, 0, 3)
-        far += [from_side(before[:half], 0, 3), from_side(after[half:], 0, 1)]
-        sides.append([after, before])
-    *first, main = block_product([near, over] + sides[0], blocks)
-    *second, main = block_product(sides[1] + far, blocks, (main,), HOMES)
+    after, before = from_side(near, 0, 1), from_side(near, 0, 3)
+    over_after, over_before = from_side(over, 0, 1), from_side(over, 0, 3)
+    far = [from_side(before, 0, 3), from_side(over_after, 0, 1)]
+    *first, main = block_product([near, over, after, before], blocks)
+    first = [first[0]] + [from_along(first[k], -k) for k in range(1, ROW_BLOCKS)]
+    *second, main = block_product([over_after, over_before] + far, blocks, (main,), HOMES)
+    main, first = lax.optimization_barrier((main, first))
+    second = [second[0]] + [from_along(second[k], -k) for k in range(1, ROW_BLOCKS)]
     received = []
     for homes, parts in ((FIRST_HOMES, first), (SECOND_HOMES, second)):
-        parts = [parts[0]] + [from_along(parts[k], -k) for k in range(1, ROW_BLOCKS)]
         for (dy, dx), summed in zip(homes, sum_parts(bias, parts)):
             received.append(from_side(summed, -dy, -dx) if dy or dx else summed)
     return received, exchange(main)

time: 122 us -> 122 us (level)
  waiting for transfers between devices: 24 us -> 29.7 us
  starting transfers between devices: 54.1 us -> 48.7 us
    all_to_all x3, waiting for transfers between devices: 9.04 us -> 14.8 us  [exchange(): return lax.all_to_all(rows, 'tp', split_axis=0, concat_axis=0, tiled=True)]
    ppermute x16 -> x14, starting transfers between devices: 28.7 us -> 24.6 us  [from_side(): return lax.ppermute(rows, 'tp', route)]
    ppermute x6, starting transfers between devices: 12 us -> 9.68 us  [from_along(): return lax.ppermute(rows, 'tp', route)]
    ppermute x16 -> x14, waiting for transfers between devices: 12.9 us -> 12.5 us  [from_side(): return lax.ppermute(rows, 'tp', route)]
  transfers between devices with their start and end apart: 25 -> 23, of which waited for: 9 -> 10; matrix products, arithmetic and copies ran while one was open for 0% -> 0% of each run, Pallas kernels for 12% -> 13%
where the time goes in v11:
time: 122 us
  starting transfers between devices  48.7 us (40%)
  waiting for transfers between devices  29.7 us (24%)
  Pallas kernels  25 us (20%)
  blocking collectives  12.2 us (10%)
  local copies, waits for them, and re-layouts  3.43 us (3%)
  between operations  2.15 us (2%)
    ppermute x14, starting transfers between devices, from_side(): return lax.ppermute(rows, 'tp', route)  24.6 us
    all_to_all x3, waiting for transfers between devices, exchange(): return lax.all_to_all(rows, 'tp', split_axis=0, concat_axis=0, tiled=True)  14.8 us
    all_to_all x3, starting transfers between devices, exchange(): return lax.all_to_all(rows, 'tp', split_axis=0, concat_axis=0, tiled=True)  14.4 us
    ppermute x14, waiting for transfers between devices, from_side(): return lax.ppermute(rows, 'tp', route)  12.5 us
    all_to_all x1, blocking collectives, project(): lax.all_to_all(rows, 'tp', split_axis=0, concat_axis=0, tiled=True, axis_...  12.2 us
    ppermute x6, starting transfers between devices, from_along(): return lax.ppermute(rows, 'tp', route)  9.68 us
    pallas_call x2, Pallas kernels, block_product(): pl.pallas_call(functools.partial(product_kernel, tiles, counts, places),...  8.74 us
    pallas_call x1, Pallas kernels, attend_main(): pl.pallas_call(attend_main_kernel, out_shape=(jax.ShapeDtypeStruct((32, 1...  3.69 us
  transfers between devices with their start and end apart: 23, of which 10 were waited for; matrix products, arithmetic and copies ran while one was open for 0% of the time, Pallas kernels for 13%

profile of v11, /device:TPU:0, one launch (start us, length us, event | category | flops | bytes accessed | tf_op | source)
XLA Modules:
  0.0 121.5 jit_solution(9703099348212420609)
XLA Ops:
  2.0 12.2 %all_to_all.20.refs_0_ = bf16[4,16,2304]{2,1,0:T(8,128)(2,1)S(1)} all-to-all(bf16[4,16,2304]{2,1,0:T(8,128)(2,1)S(1)} %norm_rows.1), channel_id=1, replica_groups={{0,8,16,24},{1,9,17,25},{2,10,18,26},{3,11,19,27},{4,12,20,28},{5,13,21..., dimensions={0} | all-to-all | bytes 589824 | tf_op jit(solution)/shard_map/all_to_all | solution.py:598
  17.3 1.7 %collective-permute-start.6 = (bf16[4,16,2304]{2,1,0:T(8,128)(2,1)S(1)}, bf16[4,16,2304]{2,1,0:T(8,128)(2,1)S(1)}, u32[]{:S(2)}, u32[]{:S(2)}) collective-permute-start(bf16[4,16,2304]{2,1,0:T(8,128)(2,1)S(1)} %all_to_all.20.refs_0_), channel_id=1, source_target_pairs={{1,0},{2,1},{3,2},{0,3},{5,4},{6,5},{7,6},{4,7},{9,8},{10,9},{11,1... | collective-permute-start | bytes 884744 | tf_op jit(solution)/shard_map/ppermute | solution.py:584
  19.1 2.4 %collective-permute-done.refs_1_ = bf16[4,16,2304]{2,1,0:T(8,128)(2,1)S(1)} collective-permute-done((bf16[4,16,2304]{2,1,0:T(8,128)(2,1)S(1)}, bf16[4,16,2304]{2,1,0:T(8,128)(2,1)S(1)}, u32[]{:S(2)}, u32[]{:S(2)}) %collective-permute-start) | collective-permute-done | bytes 294944 | tf_op jit(solution)/shard_map/ppermute | solution.py:584
  21.5 2.8 %collective-permute-start.1 = (bf16[4,16,2304]{2,1,0:T(8,128)(2,1)S(1)}, bf16[4,16,2304]{2,1,0:T(8,128)(2,1)S(1)}, u32[]{:S(2)}, u32[]{:S(2)}) collective-permute-start(bf16[4,16,2304]{2,1,0:T(8,128)(2,1)S(1)} %collective-permute-done.refs_1_), channel_id=1, source_target_pairs={{1,0},{2,1},{3,2},{0,3},{5,4},{6,5},{7,6},{4,7},{9,8},{10,9},{11,1... | collective-permute-start | bytes 884744 | tf_op jit(solution)/shard_map/ppermute | solution.py:584
  26.6 4.0 %block_product.2 = (bf16[4,16,2048]{2,1,0:T(8,128)(2,1)S(1)}, bf16[4,16,2048]{2,1,0:T(8,128)(2,1)S(1)}, bf16[4,16,2048]{2,1,0:T(8,128)(2,1)S(1)}, bf16[4,16,2048...) custom-call(bf16[4,16,2304]{2,1,0:T(8,128)(2,1)S(1)} %all_to_all.20.refs_0_, ...), custom_call_target="tpu_custom_call" | custom-call | flops 1509949440 | bytes 12000000 | tf_op jit(solution)/shard_map/block_product/pallas_call | solution.py:197
  31.2 2.1 %collective-permute-start.8 = (bf16[4,16,2048]{2,1,0:T(8,128)(2,1)S(1)}, bf16[4,16,2048]{2,1,0:T(8,128)(2,1)S(1)}, u32[]{:S(2)}, u32[]{:S(2)}) collective-permute-start(bf16[4,16,2048]{2,1,0:T(8,128)(2,1)S(1)} %get-tuple-element.33), channel_id=1, source_target_pairs={{16,0},{17,1},{18,2},{19,3},{20,4},{21,5},{22,6},{23,7},{24,8},{25... | collective-permute-start | bytes 786440 | tf_op jit(solution)/shard_map/ppermute | solution.py:589
  35.8 1.7 %collective-permute-start.5 = (bf16[4,16,2304]{2,1,0:T(8,128)(2,1)S(1)}, bf16[4,16,2304]{2,1,0:T(8,128)(2,1)S(1)}, u32[]{:S(2)}, u32[]{:S(2)}) collective-permute-start(bf16[4,16,2304]{2,1,0:T(8,128)(2,1)S(1)} %collective-permute-done.1.refs_0_), channel_id=1, source_target_pairs={{1,0},{2,1},{3,2},{0,3},{5,4},{6,5},{7,6},{4,7},{9,8},{10,9},{11,1... | collective-permute-start | bytes 884744 | tf_op jit(solution)/shard_map/ppermute | solution.py:584
  37.6 4.7 %collective-permute-done.4.refs_2_ = bf16[4,16,2304]{2,1,0:T(8,128)(2,1)S(1)} collective-permute-done((bf16[4,16,2304]{2,1,0:T(8,128)(2,1)S(1)}, bf16[4,16,2304]{2,1,0:T(8,128)(2,1)S(1)}, u32[]{:S(2)}, u32[]{:S(2)}) %collective-permute-start.4) | collective-permute-done | bytes 294944 | tf_op jit(solution)/shard_map/ppermute | solution.py:584
  42.5 4.7 %block_product.3 = (bf16[4,16,2048]{2,1,0:T(8,128)(2,1)S(1)}, bf16[4,16,2048]{2,1,0:T(8,128)(2,1)S(1)}, bf16[4,16,2048]{2,1,0:T(8,128)(2,1)S(1)}, bf16[4,16,2048]{2,1,0:T(8,128)(2,1)S(1)}, bf16[32,16,256]{2,1,0:T(8,128)(2,1)}) custom-call(bf16[4,16,2304]{2,1,0:T(8,128)(2,1)S(1)} %collective-permute-done.1.refs_0_, ...), custom_call_target="tpu_custom_call" | custom-call | flops 1509949440 | bytes 12000000 | tf_op jit(solution)/shard_map/block_product/pallas_call | solution.py:197
  48.7 6.6 %all-to-all-start.1 = ((bf16[32,16,256]{2,1,0:T(8,128)(2,1)}), bf16[32,16,256]{2,1,0:T(8,128)(2,1)S(1)}, u32[]{:S(2)}, u32[]{:S(2)}) async-start(bf16[32,16,256]{2,1,0:T(8,128)(2,1)} %get-tuple-element.35), calls=%async_computation.1 | async-start | bytes 524288 | tf_op jit(solution)/shard_map/all_to_all | solution.py:573
  55.5 9.0 %all-to-all-done.1.parts_ref = bf16[32,16,256]{2,1,0:T(8,128)(2,1)S(1)} async-done(((bf16[32,16,256]{2,1,0:T(8,128)(2,1)}), bf16[32,16,256]{2,1,0:T(8,128)(2,1)S(1)}, u32[]{:S(2)}, u32[]{:S(2)}) %all-to-all-start.1) | async-done | bytes 262176 | tf_op jit(solution)/shard_map/all_to_all | solution.py:573
  64.6 3.7 %attend_main.1 = (bf16[32,16,256]{2,1,0:T(8,128)(2,1)}, f32[8,2048]{1,0:T(8,128)S(1)}) custom-call(s32[1]{0:T(128)} %copy.12.len_ref, f32[1,10240]{1,0:T(1,128)S(1)} %bitcast.15, f32[8,128]{1,0:T(8,128)S(1)} %get-tuple-element.62.cos_ref, f32[8,128]{1,0:T(8,128)S(1)} %get-tuple-element.63.sin_ref, bf16[256,2048]{1,0:T(8,128)(2,1)S(1)} %bitcast.11, ...), custom_call_target="tpu_custom_call" | custom-call | flops 200000000 | bytes 6000000 | tf_op jit(solution)/shard_map/attend_main/pallas_call | solution.py:381
  68.9 3.9 %all-to-all-start.2 = ((bf16[32,16,256]{2,1,0:T(8,128)(2,1)}), bf16[32,16,256]{2,1,0:T(8,128)(2,1)S(1)}, u32[]{:S(2)}, u32[]{:S(2)}) async-start(bf16[32,16,256]{2,1,0:T(8,128)(2,1)} %get-tuple-element.36), calls=%async_computation.2 | async-start | bytes 524288 | tf_op jit(solution)/shard_map/all_to_all | solution.py:573
  72.8 3.4 %readout.1.read_ref = f32[1,2048]{1,0:T(1,128)S(1)} custom-call(f32[8,1024]{1,0:T(8,128)S(1)} %reshape.34.head_ref, bf16[1,2048,1024]{2,1,0:T(8,128)(2,1)} %w_hbm.3), custom_call_target="tpu_custom_call" | custom-call | flops 200000000 | bytes 5000000 | tf_op jit(solution)/shard_map/readout/pallas_call | solution.py:458
  76.2 5.8 %all-to-all-done.2.x_ref = bf16[32,16,256]{2,1,0:T(8,128)(2,1)S(1)} async-done(((bf16[32,16,256]{2,1,0:T(8,128)(2,1)}), bf16[32,16,256]{2,1,0:T(8,128)(2,1)S(1)}, u32[]{:S(2)}, u32[]{:S(2)}) %all-to-all-start.2) | async-done | bytes 262176 | tf_op jit(solution)/shard_map/all_to_all | solution.py:573
  82.0 3.4 %out_product.1 = f32[32,16,256]{2,1,0:T(8,128)} custom-call(bf16[32,16,256]{2,1,0:T(8,128)(2,1)S(1)} %all-to-all-done.2.x_ref, f32[1,2048]{1,0:T(1,128)S(1)} %readout.1.read_ref, bf16[1,2048,1024]{2,1,0:T(8,128)(2,1)} %w_hbm.3), custom_call_target="tpu_custom_call" | custom-call | flops 300000000 | bytes 5000000 | tf_op jit(solution)/shard_map/out_product/pallas_call | solution.py:504
  85.4 3.9 %all-to-all-start.3 = ((f32[32,16,256]{2,1,0:T(8,128)}), f32[32,16,256]{2,1,0:T(8,128)S(1)}, u32[]{:S(2)}, u32[]{:S(2)}) async-start(f32[32,16,256]{2,1,0:T(8,128)} %out_product.1), calls=%async_computation.3 | async-start | bytes 1048576 | tf_op jit(solution)/shard_map/all_to_all | solution.py:573
  89.9 1.8 %collective-permute-start.13 = (bf16[4,16,2048]{2,1,0:T(8,128)(2,1)}, bf16[4,16,2048]{2,1,0:T(8,128)(2,1)S(1)}, u32[]{:S(2)}, u32[]{:S(2)}) collective-permute-start(bf16[4,16,2048]{2,1,0:T(8,128)(2,1)} %copy-done.8), channel_id=1, source_target_pairs={{24,0},{25,1},{26,2},{27,3},{28,4},{29,5},{30,6},{31,7},{0,8},{1,9... | collective-permute-start | bytes 786440 | tf_op jit(solution)/shard_map/ppermute | solution.py:589
  91.7 2.8 %collective-permute-start.14 = (bf16[4,16,2048]{2,1,0:T(8,128)(2,1)}, bf16[4,16,2048]{2,1,0:T(8,128)(2,1)S(1)}, u32[]{:S(2)}, u32[]{:S(2)}) collective-permute-start(bf16[4,16,2048]{2,1,0:T(8,128)(2,1)} %copy-done.7), channel_id=1, source_target_pairs={{16,0},{17,1},{18,2},{19,3},{20,4},{21,5},{22,6},{23,7},{24,8},{25... | collective-permute-start | bytes 786440 | tf_op jit(solution)/shard_map/ppermute | solution.py:589
  100.4 2.1 %collective-permute-start.12 = (bf16[16,2048]{1,0:T(8,128)(2,1)S(1)}, bf16[16,2048]{1,0:T(8,128)(2,1)S(1)}, u32[]{:S(2)}, u32[]{:S(2)}) collective-permute-start(bf16[16,2048]{1,0:T(8,128)(2,1)S(1)} %get-tuple-element.45), channel_id=1, source_target_pairs={{1,0},{2,1},{3,2},{0,3},{5,4},{6,5},{7,6},{4,7},{9,8},{10,9},{11,1... | collective-permute-start | bytes 196616 | tf_op jit(solution)/shard_map/ppermute | solution.py:584
  105.6 2.8 %collective-permute-start.17 = (bf16[16,2048]{1,0:T(8,128)(2,1)S(1)}, bf16[16,2048]{1,0:T(8,128)(2,1)S(1)}, u32[]{:S(2)}, u32[]{:S(2)}) collective-permute-start(bf16[16,2048]{1,0:T(8,128)(2,1)S(1)} %get-tuple-element.51), channel_id=1, source_target_pairs={{5,0},{6,1},{7,2},{4,3},{1,4},{2,5},{3,6},{0,7},{13,8},{14,9},{15,... | collective-permute-start | bytes 196616 | tf_op jit(solution)/shard_map/ppermute | solution.py:584
  109.5 3.2 %collective-permute-start.19 = (bf16[16,2048]{1,0:T(8,128)(2,1)S(1)}, bf16[16,2048]{1,0:T(8,128)(2,1)S(1)}, u32[]{:S(2)}, u32[]{:S(2)}) collective-permute-start(bf16[16,2048]{1,0:T(8,128)(2,1)S(1)} %get-tuple-element.53), channel_id=1, source_target_pairs={{6,0},{7,1},{4,2},{5,3},{2,4},{3,5},{0,6},{1,7},{14,8},{15,9},{12,... | collective-permute-start | bytes 196616 | tf_op jit(solution)/shard_map/ppermute | solution.py:584
  114.2 2.0 %collective-permute-done.19.refs_7_ = bf16[16,2048]{1,0:T(8,128)(2,1)S(1)} collective-permute-done((bf16[16,2048]{1,0:T(8,128)(2,1)S(1)}, bf16[16,2048]{1,0:T(8,128)(2,1)S(1)}, u32[]{:S(2)}, u32[]{:S(2)}) %collective-permute-start.19) | collective-permute-done | bytes 65568 | tf_op jit(solution)/shard_map/ppermute | solution.py:584
  117.0 3.0 %attend_cont.1.mixed_ref = bf16[16,8192]{1,0:T(8,128)(2,1)S(1)} custom-call(s32[1]{0:T(128)} %copy.12.len_ref, s32[1]{0:T(128)S(6)} %copy.13.bound_ref, f32[1,10240]{1,0:T(1,128)S(1)} %bitcast.18, f32[16,128]{1,0:T(8,128)S(1)} %get-tuple-element.64.cos_ref, f32[16,128]{1,0:T(8,128)S(1)} %get-tuple-element.65.sin_ref, bf16[256,2048]{1,0:T(8,128)(2,1)S(1)} %bitcast.12, ...), custom_call_target="tpu_custom_call" | custom-call | flops 400000000 | bytes 8000000 | tf_op jit(solution)/shard_map/attend_cont/pallas_call | solution.py:427
  (61 shorter events, 25.6 us)
Async XLA Ops:
  14.2 7.3 %collective-permute-start = (bf16[4,16,2304]{2,1,0:T(8,128)(2,1)S(1)}, bf16[4,16,2304]{2,1,0:T(8,128)(2,1)S(1)}, u32[]{:S(2)}, u32[]{:S(2)}) collective-permute-start(bf16[4,16,2304]{2,1,0:T(8,128)(2,1)S(1)} %all_to_all.20.refs_0_), channel_id=1, source_target_pairs={{4,0},{5,1},{6,2},{7,3},{0,4},{1,5},{2,6},{3,7},{12,8},{13,9},{14,... | collective-permute-start | bytes 884744 | tf_op jit(solution)/shard_map/ppermute | solution.py:584
  15.8 9.1 %collective-permute-start.3 = (bf16[4,16,2304]{2,1,0:T(8,128)(2,1)S(1)}, bf16[4,16,2304]{2,1,0:T(8,128)(2,1)S(1)}, u32[]{:S(2)}, u32[]{:S(2)}) collective-permute-start(bf16[4,16,2304]{2,1,0:T(8,128)(2,1)S(1)} %all_to_all.20.refs_0_), channel_id=1, source_target_pairs={{3,0},{0,1},{1,2},{2,3},{7,4},{4,5},{5,6},{6,7},{11,8},{8,9},{9,10... | collective-permute-start | bytes 884744 | tf_op jit(solution)/shard_map/ppermute | solution.py:584
  17.3 9.3 %collective-permute-start.6 = (bf16[4,16,2304]{2,1,0:T(8,128)(2,1)S(1)}, bf16[4,16,2304]{2,1,0:T(8,128)(2,1)S(1)}, u32[]{:S(2)}, u32[]{:S(2)}) collective-permute-start(bf16[4,16,2304]{2,1,0:T(8,128)(2,1)S(1)} %all_to_all.20.refs_0_), channel_id=1, source_target_pairs={{1,0},{2,1},{3,2},{0,3},{5,4},{6,5},{7,6},{4,7},{9,8},{10,9},{11,1... | collective-permute-start | bytes 884744 | tf_op jit(solution)/shard_map/ppermute | solution.py:584
  21.5 12.8 %collective-permute-start.1 = (bf16[4,16,2304]{2,1,0:T(8,128)(2,1)S(1)}, bf16[4,16,2304]{2,1,0:T(8,128)(2,1)S(1)}, u32[]{:S(2)}, u32[]{:S(2)}) collective-permute-start(bf16[4,16,2304]{2,1,0:T(8,128)(2,1)S(1)} %collective-permute-done.refs_1_), channel_id=1, source_target_pairs={{1,0},{2,1},{3,2},{0,3},{5,4},{6,5},{7,6},{4,7},{9,8},{10,9},{11,1... | collective-permute-start | bytes 884744 | tf_op jit(solution)/shard_map/ppermute | solution.py:584
  24.3 11.5 %collective-permute-start.2 = (bf16[4,16,2304]{2,1,0:T(8,128)(2,1)S(1)}, bf16[4,16,2304]{2,1,0:T(8,128)(2,1)S(1)}, u32[]{:S(2)}, u32[]{:S(2)}) collective-permute-start(bf16[4,16,2304]{2,1,0:T(8,128)(2,1)S(1)} %collective-permute-done.refs_1_), channel_id=1, source_target_pairs={{3,0},{0,1},{1,2},{2,3},{7,4},{4,5},{5,6},{6,7},{11,8},{8,9},{9,10... | collective-permute-start | bytes 884744 | tf_op jit(solution)/shard_map/ppermute | solution.py:584
  30.6 18.1 %collective-permute-start.7 = (bf16[4,16,2048]{2,1,0:T(8,128)(2,1)S(1)}, bf16[4,16,2048]{2,1,0:T(8,128)(2,1)S(1)}, u32[]{:S(2)}, u32[]{:S(2)}) collective-permute-start(bf16[4,16,2048]{2,1,0:T(8,128)(2,1)S(1)} %get-tuple-element.32), channel_id=1, source_target_pairs={{24,0},{25,1},{26,2},{27,3},{28,4},{29,5},{30,6},{31,7},{0,8},{1,9... | collective-permute-start | bytes 786440 | tf_op jit(solution)/shard_map/ppermute | solution.py:589
  31.2 17.5 %collective-permute-start.8 = (bf16[4,16,2048]{2,1,0:T(8,128)(2,1)S(1)}, bf16[4,16,2048]{2,1,0:T(8,128)(2,1)S(1)}, u32[]{:S(2)}, u32[]{:S(2)}) collective-permute-start(bf16[4,16,2048]{2,1,0:T(8,128)(2,1)S(1)} %get-tuple-element.33), channel_id=1, source_target_pairs={{16,0},{17,1},{18,2},{19,3},{20,4},{21,5},{22,6},{23,7},{24,8},{25... | collective-permute-start | bytes 786440 | tf_op jit(solution)/shard_map/ppermute | solution.py:589
  33.3 15.4 %collective-permute-start.9 = (bf16[4,16,2048]{2,1,0:T(8,128)(2,1)S(1)}, bf16[4,16,2048]{2,1,0:T(8,128)(2,1)S(1)}, u32[]{:S(2)}, u32[]{:S(2)}) collective-permute-start(bf16[4,16,2048]{2,1,0:T(8,128)(2,1)S(1)} %get-tuple-element.34), channel_id=1, source_target_pairs={{8,0},{9,1},{10,2},{11,3},{12,4},{13,5},{14,6},{15,7},{16,8},{17,9... | collective-permute-start | bytes 786440 | tf_op jit(solution)/shard_map/ppermute | solution.py:589
  34.3 7.9 %collective-permute-start.4 = (bf16[4,16,2304]{2,1,0:T(8,128)(2,1)S(1)}, bf16[4,16,2304]{2,1,0:T(8,128)(2,1)S(1)}, u32[]{:S(2)}, u32[]{:S(2)}) collective-permute-start(bf16[4,16,2304]{2,1,0:T(8,128)(2,1)S(1)} %collective-permute-done.3.refs_3_), channel_id=1, source_target_pairs={{3,0},{0,1},{1,2},{2,3},{7,4},{4,5},{5,6},{6,7},{11,8},{8,9},{9,10... | collective-permute-start | bytes 884744 | tf_op jit(solution)/shard_map/ppermute | solution.py:584
  35.8 6.7 %collective-permute-start.5 = (bf16[4,16,2304]{2,1,0:T(8,128)(2,1)S(1)}, bf16[4,16,2304]{2,1,0:T(8,128)(2,1)S(1)}, u32[]{:S(2)}, u32[]{:S(2)}) collective-permute-start(bf16[4,16,2304]{2,1,0:T(8,128)(2,1)S(1)} %collective-permute-done.1.refs_0_), channel_id=1, source_target_pairs={{1,0},{2,1},{3,2},{0,3},{5,4},{6,5},{7,6},{4,7},{9,8},{10,9},{11,1... | collective-permute-start | bytes 884744 | tf_op jit(solution)/shard_map/ppermute | solution.py:584
  48.7 15.8 %all-to-all-start.1 = ((bf16[32,16,256]{2,1,0:T(8,128)(2,1)}), bf16[32,16,256]{2,1,0:T(8,128)(2,1)S(1)}, u32[]{:S(2)}, u32[]{:S(2)}) async-start(bf16[32,16,256]{2,1,0:T(8,128)(2,1)} %get-tuple-element.35), calls=%async_computation.1 | async-start | bytes 524288 | tf_op jit(solution)/shard_map/all_to_all | solution.py:573
  68.9 13.1 %all-to-all-start.2 = ((bf16[32,16,256]{2,1,0:T(8,128)(2,1)}), bf16[32,16,256]{2,1,0:T(8,128)(2,1)S(1)}, u32[]{:S(2)}, u32[]{:S(2)}) async-start(bf16[32,16,256]{2,1,0:T(8,128)(2,1)} %get-tuple-element.36), calls=%async_computation.2 | async-start | bytes 524288 | tf_op jit(solution)/shard_map/all_to_all | solution.py:573
  76.2 43.9 %copy-start.1 = (bf16[1,8,2,8192]{3,2,1,0:T(2,128)(2,1)S(1)}, bf16[1,8,2,8192]{3,2,1,0:T(2,128)(2,1)}, u32[]{:S(2)}) copy-start(bf16[1,8,2,8192]{3,2,1,0:T(2,128)(2,1)} %param.11) | copy-start | bytes 786436
  85.4 34.7 %all-to-all-start.3 = ((f32[32,16,256]{2,1,0:T(8,128)}), f32[32,16,256]{2,1,0:T(8,128)S(1)}, u32[]{:S(2)}, u32[]{:S(2)}) async-start(f32[32,16,256]{2,1,0:T(8,128)} %out_product.1), calls=%async_computation.3 | async-start | bytes 1048576 | tf_op jit(solution)/shard_map/all_to_all | solution.py:573
  89.9 10.5 %collective-permute-start.13 = (bf16[4,16,2048]{2,1,0:T(8,128)(2,1)}, bf16[4,16,2048]{2,1,0:T(8,128)(2,1)S(1)}, u32[]{:S(2)}, u32[]{:S(2)}) collective-permute-start(bf16[4,16,2048]{2,1,0:T(8,128)(2,1)} %copy-done.8), channel_id=1, source_target_pairs={{24,0},{25,1},{26,2},{27,3},{28,4},{29,5},{30,6},{31,7},{0,8},{1,9... | collective-permute-start | bytes 786440 | tf_op jit(solution)/shard_map/ppermute | solution.py:589
  91.7 12.1 %collective-permute-start.14 = (bf16[4,16,2048]{2,1,0:T(8,128)(2,1)}, bf16[4,16,2048]{2,1,0:T(8,128)(2,1)S(1)}, u32[]{:S(2)}, u32[]{:S(2)}) collective-permute-start(bf16[4,16,2048]{2,1,0:T(8,128)(2,1)} %copy-done.7), channel_id=1, source_target_pairs={{16,0},{17,1},{18,2},{19,3},{20,4},{21,5},{22,6},{23,7},{24,8},{25... | collective-permute-start | bytes 786440 | tf_op jit(solution)/shard_map/ppermute | solution.py:589
  94.5 9.3 %collective-permute-start.15 = (bf16[4,16,2048]{2,1,0:T(8,128)(2,1)S(1)}, bf16[4,16,2048]{2,1,0:T(8,128)(2,1)S(1)}, u32[]{:S(2)}, u32[]{:S(2)}) collective-permute-start(bf16[4,16,2048]{2,1,0:T(8,128)(2,1)S(1)} %get-tuple-element.49), channel_id=1, source_target_pairs={{8,0},{9,1},{10,2},{11,3},{12,4},{13,5},{14,6},{15,7},{16,8},{17,9... | collective-permute-start | bytes 786440 | tf_op jit(solution)/shard_map/ppermute | solution.py:589
  96.1 12.3 %collective-permute-start.10 = (bf16[16,2048]{1,0:T(8,128)(2,1)S(1)}, bf16[16,2048]{1,0:T(8,128)(2,1)S(1)}, u32[]{:S(2)}, u32[]{:S(2)}) collective-permute-start(bf16[16,2048]{1,0:T(8,128)(2,1)S(1)} %get-tuple-element.43), channel_id=1, source_target_pairs={{4,0},{5,1},{6,2},{7,3},{0,4},{1,5},{2,6},{3,7},{12,8},{13,9},{14,... | collective-permute-start | bytes 196616 | tf_op jit(solution)/shard_map/ppermute | solution.py:584
  97.7 11.8 %collective-permute-start.11 = (bf16[16,2048]{1,0:T(8,128)(2,1)S(1)}, bf16[16,2048]{1,0:T(8,128)(2,1)S(1)}, u32[]{:S(2)}, u32[]{:S(2)}) collective-permute-start(bf16[16,2048]{1,0:T(8,128)(2,1)S(1)} %get-tuple-element.44), channel_id=1, source_target_pairs={{3,0},{0,1},{1,2},{2,3},{7,4},{4,5},{5,6},{6,7},{11,8},{8,9},{9,10... | collective-permute-start | bytes 196616 | tf_op jit(solution)/shard_map/ppermute | solution.py:584
  100.4 12.4 %collective-permute-start.12 = (bf16[16,2048]{1,0:T(8,128)(2,1)S(1)}, bf16[16,2048]{1,0:T(8,128)(2,1)S(1)}, u32[]{:S(2)}, u32[]{:S(2)}) collective-permute-start(bf16[16,2048]{1,0:T(8,128)(2,1)S(1)} %get-tuple-element.45), channel_id=1, source_target_pairs={{1,0},{2,1},{3,2},{0,3},{5,4},{6,5},{7,6},{4,7},{9,8},{10,9},{11,1... | collective-permute-start | bytes 196616 | tf_op jit(solution)/shard_map/ppermute | solution.py:584
  104.0 8.8 %collective-permute-start.16 = (bf16[16,2048]{1,0:T(8,128)(2,1)S(1)}, bf16[16,2048]{1,0:T(8,128)(2,1)S(1)}, u32[]{:S(2)}, u32[]{:S(2)}) collective-permute-start(bf16[16,2048]{1,0:T(8,128)(2,1)S(1)} %get-tuple-element.50), channel_id=1, source_target_pairs={{7,0},{4,1},{5,2},{6,3},{3,4},{0,5},{1,6},{2,7},{15,8},{12,9},{13,... | collective-permute-start | bytes 196616 | tf_op jit(solution)/shard_map/ppermute | solution.py:584
  105.6 7.2 %collective-permute-start.17 = (bf16[16,2048]{1,0:T(8,128)(2,1)S(1)}, bf16[16,2048]{1,0:T(8,128)(2,1)S(1)}, u32[]{:S(2)}, u32[]{:S(2)}) collective-permute-start(bf16[16,2048]{1,0:T(8,128)(2,1)S(1)} %get-tuple-element.51), channel_id=1, source_target_pairs={{5,0},{6,1},{7,2},{4,3},{1,4},{2,5},{3,6},{0,7},{13,8},{14,9},{15,... | collective-permute-start | bytes 196616 | tf_op jit(solution)/shard_map/ppermute | solution.py:584
  108.4 5.8 %collective-permute-start.18 = (bf16[16,2048]{1,0:T(8,128)(2,1)S(1)}, bf16[16,2048]{1,0:T(8,128)(2,1)S(1)}, u32[]{:S(2)}, u32[]{:S(2)}) collective-permute-start(bf16[16,2048]{1,0:T(8,128)(2,1)S(1)} %get-tuple-element.52), channel_id=1, source_target_pairs={{2,0},{3,1},{0,2},{1,3},{6,4},{7,5},{4,6},{5,7},{10,8},{11,9},{8,1... | collective-permute-start | bytes 196616 | tf_op jit(solution)/shard_map/ppermute | solution.py:584
  109.5 6.7 %collective-permute-start.19 = (bf16[16,2048]{1,0:T(8,128)(2,1)S(1)}, bf16[16,2048]{1,0:T(8,128)(2,1)S(1)}, u32[]{:S(2)}, u32[]{:S(2)}) collective-permute-start(bf16[16,2048]{1,0:T(8,128)(2,1)S(1)} %get-tuple-element.53), channel_id=1, source_target_pairs={{6,0},{7,1},{4,2},{5,3},{2,4},{3,5},{0,6},{1,7},{14,8},{15,9},{12,... | collective-permute-start | bytes 196616 | tf_op jit(solution)/shard_map/ppermute | solution.py:584
  (8 other events, 168.1 us)

commit v12 on v11

--- a/solution.py
+++ b/solution.py
@@ -29,6 +29,7 @@
 VMEM = pl.BlockSpec(memory_space=pltpu.VMEM)
 SMEM = pl.BlockSpec(memory_space=pltpu.SMEM)
 HBM = pl.BlockSpec(memory_space=pltpu.HBM)
+UNREAD = pl.BlockSpec(memory_space=pl.ANY)
 
 
 def whole(shape):
@@ -342,8 +343,9 @@
 
 
 def attend_main_kernel(
-    len_ref, bias_ref, cos_ref, sin_ref, cache_ref, parts_ref, out_ref, kv_ref, qkv_ref, piece_ref
+    len_ref, bias_ref, cos_ref, sin_ref, cache_ref, parts_ref, *refs
 ):
+    out_ref, kv_ref, qkv_ref, piece_ref = refs[-4:]
     rows = qkv_ref.shape[0]
     qkv_ref[...] = jnp.zeros(qkv_ref.shape, jnp.float32)
     load_qkv(True, parts_ref, qkv_ref)
@@ -377,14 +379,14 @@
             out_ref[r * COL_BLOCKS + c] = piece
 
 
-def attend_main(prefix_len, bias, cosine, sine, cache, parts):
+def attend_main(prefix_len, bias, cosine, sine, cache, parts, after):
     return pl.pallas_call(
         attend_main_kernel,
         out_shape=(
             jax.ShapeDtypeStruct((32, 16, TILE), jnp.bfloat16),
             jax.ShapeDtypeStruct((8, 2 * KV_WIDTH), jnp.float32),
         ),
-        in_specs=[SMEM] + [VMEM] * 5,
+        in_specs=[SMEM] + [VMEM] * 5 + [UNREAD] * len(after),
         out_specs=(whole((32, 16, TILE)), whole((8, 2 * KV_WIDTH))),
         scratch_shapes=[
             pltpu.VMEM((8, QKV), jnp.float32),
@@ -393,7 +395,7 @@
         compiler_params=kernel_params(),
         cost_estimate=cost(2 * 10**8, 6 * 10**6),
         name="attend_main",
-    )(prefix_len, bias, cosine, sine, cache, parts)
+    )(prefix_len, bias, cosine, sine, cache, parts, *after)
 
 
 def attend_cont_kernel(len_ref, bound_ref, bias_ref, cos_ref, sin_ref, cache_ref, kv_ref, *refs):
@@ -467,7 +469,8 @@
     )(value_head, in_hbm(blocks))
 
 
-def out_kernel(tiles, x_ref, read_ref, w_hbm, out_ref, rows_ref, wide_ref, read8_ref, w_ref, sems):
+def out_kernel(tiles, x_ref, read_ref, w_hbm, *refs):
+    out_ref, rows_ref, wide_ref, read8_ref, w_ref, sems = refs[-6:]
     n = pl.program_id(0)
     members = x_ref.shape[0]
     lines = members * STEPS
@@ -498,14 +501,14 @@
             out_ref[:, :8, k * 128 : (k + 1) * 128] = packed
 
 
-def out_product(rows, read, blocks):
+def out_product(rows, read, blocks, after):
     members = rows.shape[0]
     tiles = blocks.shape[2] // TILE
     return pl.pallas_call(
         functools.partial(out_kernel, tiles),
         out_shape=jax.ShapeDtypeStruct((members, 16, TILE), jnp.float32),
         grid=(tiles,),
-        in_specs=[whole(rows.shape), whole(read.shape), HBM],
+        in_specs=[whole(rows.shape), whole(read.shape), HBM] + [UNREAD] * len(after),
         out_specs=whole((members, 16, TILE)),
         scratch_shapes=[
             pltpu.VMEM((members * STEPS, FEATURES), jnp.bfloat16),
@@ -517,7 +520,7 @@
         compiler_params=kernel_params(),
         cost_estimate=cost(3 * 10**8, 5 * 10**6),
         name="out_product",
-    )(rows, read, in_hbm(blocks))
+    )(rows, read, in_hbm(blocks), *after)
 
 
 def finish_kernel(parts_ref, main_ref, cont_ref, head_ref, mixed_ref, out_ref, score_ref, wide_ref):
@@ -609,7 +612,7 @@
     for homes, parts in ((FIRST_HOMES, first), (SECOND_HOMES, second)):
         for (dy, dx), summed in zip(homes, sum_parts(bias, parts)):
             received.append(from_side(summed, -dy, -dx) if dy or dx else summed)
-    return received, exchange(main)
+    return received, exchange(main), second[1:] + received[1:4]
 
 
 def on_device(
@@ -624,11 +627,11 @@
     main_tables = rope_tables(prefix_len + step[:8])
     cont_tables = rope_tables(prefix_len + boundary + step)
     read = readout(value_head.reshape(COL_BLOCKS, D // COL_BLOCKS), w_out)
-    parts, main_parts = project(norm_rows(main, cont, rms_gain[None, :]), w_qkv, bias)
-    mixed, main_kv = attend_main(prefix_len, bias, *main_tables, cache, main_parts)
+    parts, main_parts, before = project(norm_rows(main, cont, rms_gain[None, :]), w_qkv, bias)
+    mixed, main_kv = attend_main(prefix_len, bias, *main_tables, cache, main_parts, before)
     mixed = exchange(mixed)
     cont_mixed = attend_cont(prefix_len, boundary, bias, *cont_tables, cache, main_kv, *parts)
-    parts = exchange(out_product(mixed, read, w_out))
+    parts = exchange(out_product(mixed, read, w_out, parts[4:]))
     main_out, score = finish(parts, main, cont, head, cont_mixed)
     return main_out[None], score[0, :1]
 

time: 122 us -> 114 us (0.934)
  waiting for transfers between devices: 29.7 us -> 21.5 us
  local copies, waits for them, and re-layouts: 3.43 us -> 1.19 us
  starting transfers between devices: 48.7 us -> 50.5 us
    all_to_all x3, waiting for transfers between devices: 14.8 us -> 8.77 us  [exchange(): return lax.all_to_all(rows, 'tp', split_axis=0, concat_axis=0, tiled=True)]
    all_to_all x3, starting transfers between devices: 14.4 us -> 18.5 us  [exchange(): return lax.all_to_all(rows, 'tp', split_axis=0, concat_axis=0, tiled=True)]
    ppermute x6, waiting for transfers between devices: 2.44 us -> 0.02 us  [from_along(): return lax.ppermute(rows, 'tp', route)]
    unnamed x18 -> x16, local copies, waits for them, and re-layouts: 2.91 us -> 0.67 us
    ppermute x14, starting transfers between devices: 24.6 us -> 23.1 us  [from_side(): return lax.ppermute(rows, 'tp', route)]
  transfers between devices with their start and end apart: 23 -> 23, of which waited for: 10 -> 8; matrix products, arithmetic and copies ran while one was open for 0% -> 0% of each run, Pallas kernels for 13% -> 14%
where the time goes in v12:
time: 114 us; the launch traced here: 113 us
  starting transfers between devices  50.5 us (44%)
  Pallas kernels  25.1 us (22%)
  waiting for transfers between devices  21.5 us (19%)
  blocking collectives  12.2 us (11%)
  between operations  2.18 us (2%)
  local copies, waits for them, and re-layouts  1.19 us (1%)
    ppermute x14, starting transfers between devices, from_side(): return lax.ppermute(rows, 'tp', route)  23.1 us
    all_to_all x3, starting transfers between devices, exchange(): return lax.all_to_all(rows, 'tp', split_axis=0, concat_axis=0, tiled=True)  18.5 us
    ppermute x14, waiting for transfers between devices, from_side(): return lax.ppermute(rows, 'tp', route)  12.7 us
    all_to_all x1, blocking collectives, project(): lax.all_to_all(rows, 'tp', split_axis=0, concat_axis=0, tiled=True, axis_...  12.2 us
    ppermute x6, starting transfers between devices, from_along(): return lax.ppermute(rows, 'tp', route)  8.93 us
    all_to_all x3, waiting for transfers between devices, exchange(): return lax.all_to_all(rows, 'tp', split_axis=0, concat_axis=0, tiled=True)  8.77 us
    pallas_call x2, Pallas kernels, block_product(): pl.pallas_call(functools.partial(product_kernel, tiles, counts, places),...  8.76 us
    pallas_call x1, Pallas kernels, attend_main(): pl.pallas_call(attend_main_kernel, out_shape=(jax.ShapeDtypeStruct((32, 1...  3.7 us
  transfers between devices with their start and end apart: 23, of which 8 were waited for; matrix products, arithmetic and copies ran while one was open for 0% of the time, Pallas kernels for 14%

profile of v12, /device:TPU:0, one launch (start us, length us, event | category | flops | bytes accessed | tf_op | source)
XLA Modules:
  0.0 113.0 jit_solution(12879995253371216955)
XLA Ops:
  2.0 12.2 %all_to_all.20.refs_0_ = bf16[4,16,2304]{2,1,0:T(8,128)(2,1)S(1)} all-to-all(bf16[4,16,2304]{2,1,0:T(8,128)(2,1)S(1)} %norm_rows.1), channel_id=1, replica_groups={{0,8,16,24},{1,9,17,25},{2,10,18,26},{3,11,19,27},{4,12,20,28},{5,13,21..., dimensions={0} | all-to-all | bytes 589824 | tf_op jit(solution)/shard_map/all_to_all | solution.py:601
  17.3 1.7 %collective-permute-start.6 = (bf16[4,16,2304]{2,1,0:T(8,128)(2,1)S(1)}, bf16[4,16,2304]{2,1,0:T(8,128)(2,1)S(1)}, u32[]{:S(2)}, u32[]{:S(2)}) collective-permute-start(bf16[4,16,2304]{2,1,0:T(8,128)(2,1)S(1)} %all_to_all.20.refs_0_), channel_id=1, source_target_pairs={{1,0},{2,1},{3,2},{0,3},{5,4},{6,5},{7,6},{4,7},{9,8},{10,9},{11,1... | collective-permute-start | bytes 884744 | tf_op jit(solution)/shard_map/ppermute | solution.py:587
  19.1 2.4 %collective-permute-done.refs_1_ = bf16[4,16,2304]{2,1,0:T(8,128)(2,1)S(1)} collective-permute-done((bf16[4,16,2304]{2,1,0:T(8,128)(2,1)S(1)}, bf16[4,16,2304]{2,1,0:T(8,128)(2,1)S(1)}, u32[]{:S(2)}, u32[]{:S(2)}) %collective-permute-start) | collective-permute-done | bytes 294944 | tf_op jit(solution)/shard_map/ppermute | solution.py:587
  21.5 2.8 %collective-permute-start.1 = (bf16[4,16,2304]{2,1,0:T(8,128)(2,1)S(1)}, bf16[4,16,2304]{2,1,0:T(8,128)(2,1)S(1)}, u32[]{:S(2)}, u32[]{:S(2)}) collective-permute-start(bf16[4,16,2304]{2,1,0:T(8,128)(2,1)S(1)} %collective-permute-done.refs_1_), channel_id=1, source_target_pairs={{1,0},{2,1},{3,2},{0,3},{5,4},{6,5},{7,6},{4,7},{9,8},{10,9},{11,1... | collective-permute-start | bytes 884744 | tf_op jit(solution)/shard_map/ppermute | solution.py:587
  26.6 4.0 %block_product.2 = (bf16[4,16,2048]{2,1,0:T(8,128)(2,1)S(1)}, bf16[4,16,2048]{2,1,0:T(8,128)(2,1)S(1)}, bf16[4,16,2048]{2,1,0:T(8,128)(2,1)S(1)}, bf16[4,16,2048...) custom-call(bf16[4,16,2304]{2,1,0:T(8,128)(2,1)S(1)} %all_to_all.20.refs_0_, ...), custom_call_target="tpu_custom_call" | custom-call | flops 1509949440 | bytes 12000000 | tf_op jit(solution)/shard_map/block_product/pallas_call | solution.py:198
  31.2 2.1 %collective-permute-start.8 = (bf16[4,16,2048]{2,1,0:T(8,128)(2,1)S(1)}, bf16[4,16,2048]{2,1,0:T(8,128)(2,1)S(1)}, u32[]{:S(2)}, u32[]{:S(2)}) collective-permute-start(bf16[4,16,2048]{2,1,0:T(8,128)(2,1)S(1)} %get-tuple-element.33), channel_id=1, source_target_pairs={{16,0},{17,1},{18,2},{19,3},{20,4},{21,5},{22,6},{23,7},{24,8},{25... | collective-permute-start | bytes 786440 | tf_op jit(solution)/shard_map/ppermute | solution.py:592
  35.8 1.7 %collective-permute-start.5 = (bf16[4,16,2304]{2,1,0:T(8,128)(2,1)S(1)}, bf16[4,16,2304]{2,1,0:T(8,128)(2,1)S(1)}, u32[]{:S(2)}, u32[]{:S(2)}) collective-permute-start(bf16[4,16,2304]{2,1,0:T(8,128)(2,1)S(1)} %collective-permute-done.1.refs_0_), channel_id=1, source_target_pairs={{1,0},{2,1},{3,2},{0,3},{5,4},{6,5},{7,6},{4,7},{9,8},{10,9},{11,1... | collective-permute-start | bytes 884744 | tf_op jit(solution)/shard_map/ppermute | solution.py:587
  37.6 4.7 %collective-permute-done.4.refs_2_ = bf16[4,16,2304]{2,1,0:T(8,128)(2,1)S(1)} collective-permute-done((bf16[4,16,2304]{2,1,0:T(8,128)(2,1)S(1)}, bf16[4,16,2304]{2,1,0:T(8,128)(2,1)S(1)}, u32[]{:S(2)}, u32[]{:S(2)}) %collective-permute-start.4) | collective-permute-done | bytes 294944 | tf_op jit(solution)/shard_map/ppermute | solution.py:587
  42.5 4.8 %block_product.3 = (bf16[4,16,2048]{2,1,0:T(8,128)(2,1)S(1)}, bf16[4,16,2048]{2,1,0:T(8,128)(2,1)S(1)}, bf16[4,16,2048]{2,1,0:T(8,128)(2,1)S(1)}, bf16[4,16,2048]{2,1,0:T(8,128)(2,1)S(1)}, bf16[32,16,256]{2,1,0:T(8,128)(2,1)}) custom-call(bf16[4,16,2304]{2,1,0:T(8,128)(2,1)S(1)} %collective-permute-done.1.refs_0_, ...), custom_call_target="tpu_custom_call" | custom-call | flops 1509949440 | bytes 12000000 | tf_op jit(solution)/shard_map/block_product/pallas_call | solution.py:198
  50.0 2.5 %collective-permute-start.12 = (bf16[4,16,2048]{2,1,0:T(8,128)(2,1)S(1)}, bf16[4,16,2048]{2,1,0:T(8,128)(2,1)S(1)}, u32[]{:S(2)}, u32[]{:S(2)}) collective-permute-start(bf16[4,16,2048]{2,1,0:T(8,128)(2,1)S(1)} %get-tuple-element.38), channel_id=1, source_target_pairs={{8,0},{9,1},{10,2},{11,3},{12,4},{13,5},{14,6},{15,7},{16,8},{17,9... | collective-permute-start | bytes 786440 | tf_op jit(solution)/shard_map/ppermute | solution.py:592
  53.4 6.5 %all-to-all-start.1 = ((bf16[32,16,256]{2,1,0:T(8,128)(2,1)}), bf16[32,16,256]{2,1,0:T(8,128)(2,1)S(1)}, u32[]{:S(2)}, u32[]{:S(2)}) async-start(bf16[32,16,256]{2,1,0:T(8,128)(2,1)} %get-tuple-element.35), calls=%async_computation.1 | async-start | bytes 524288 | tf_op jit(solution)/shard_map/all_to_all | solution.py:576
  60.0 1.9 %collective-permute-start.14 = (bf16[16,2048]{1,0:T(8,128)(2,1)S(1)}, bf16[16,2048]{1,0:T(8,128)(2,1)S(1)}, u32[]{:S(2)}, u32[]{:S(2)}) collective-permute-start(bf16[16,2048]{1,0:T(8,128)(2,1)S(1)} %get-tuple-element.44), channel_id=1, source_target_pairs={{3,0},{0,1},{1,2},{2,3},{7,4},{4,5},{5,6},{6,7},{11,8},{8,9},{9,10... | collective-permute-start | bytes 196616 | tf_op jit(solution)/shard_map/ppermute | solution.py:587
  63.4 3.2 %collective-permute-done.14.refs_4_.refs_2_ = bf16[16,2048]{1,0:T(8,128)(2,1)S(1)} collective-permute-done((bf16[16,2048]{1,0:T(8,128)(2,1)S(1)}, bf16[16,2048]{1,0:T(8,128)(2,1)S(1)}, u32[]{:S(2)}, u32[]{:S(2)}) %collective-permute-start.14) | collective-permute-done | bytes 65568 | tf_op jit(solution)/shard_map/ppermute | solution.py:587
  66.6 2.5 %all-to-all-done.1.parts_ref = bf16[32,16,256]{2,1,0:T(8,128)(2,1)S(1)} async-done(((bf16[32,16,256]{2,1,0:T(8,128)(2,1)}), bf16[32,16,256]{2,1,0:T(8,128)(2,1)S(1)}, u32[]{:S(2)}, u32[]{:S(2)}) %all-to-all-start.1) | async-done | bytes 262176 | tf_op jit(solution)/shard_map/all_to_all | solution.py:576
  69.2 3.7 %attend_main.1 = (bf16[32,16,256]{2,1,0:T(8,128)(2,1)}, f32[8,2048]{1,0:T(8,128)S(1)}) custom-call(s32[1]{0:T(128)} %copy.12.len_ref, f32[1,10240]{1,0:T(1,128)S(1)} %bitcast.16, f32[8,128]{1,0:T(8,128)S(1)} %get-tuple-element.62.cos_ref, f32[8,128]{1,0:T(8,128)S(1)} %get-tuple-element.63.sin_ref, bf16[256,2048]{1,0:T(8,128)(2,1)S(1)} %bitcast.11, ...), custom_call_target="tpu_custom_call" | custom-call | flops 200000000 | bytes 6000000 | tf_op jit(solution)/shard_map/attend_main/pallas_call | solution.py:383
  72.9 5.2 %all-to-all-start.2 = ((bf16[32,16,256]{2,1,0:T(8,128)(2,1)}), bf16[32,16,256]{2,1,0:T(8,128)(2,1)S(1)}, u32[]{:S(2)}, u32[]{:S(2)}) async-start(bf16[32,16,256]{2,1,0:T(8,128)(2,1)} %get-tuple-element.46), calls=%async_computation.2 | async-start | bytes 524288 | tf_op jit(solution)/shard_map/all_to_all | solution.py:576
  78.3 2.8 %collective-permute-start.16 = (bf16[16,2048]{1,0:T(8,128)(2,1)S(1)}, bf16[16,2048]{1,0:T(8,128)(2,1)S(1)}, u32[]{:S(2)}, u32[]{:S(2)}) collective-permute-start(bf16[16,2048]{1,0:T(8,128)(2,1)S(1)} %get-tuple-element.48), channel_id=1, source_target_pairs={{7,0},{4,1},{5,2},{6,3},{3,4},{0,5},{1,6},{2,7},{15,8},{12,9},{13,... | collective-permute-start | bytes 196616 | tf_op jit(solution)/shard_map/ppermute | solution.py:587
  82.5 2.1 %collective-permute-start.18 = (bf16[16,2048]{1,0:T(8,128)(2,1)S(1)}, bf16[16,2048]{1,0:T(8,128)(2,1)S(1)}, u32[]{:S(2)}, u32[]{:S(2)}) collective-permute-start(bf16[16,2048]{1,0:T(8,128)(2,1)S(1)} %get-tuple-element.50), channel_id=1, source_target_pairs={{2,0},{3,1},{0,2},{1,3},{6,4},{7,5},{4,6},{5,7},{10,8},{11,9},{8,1... | collective-permute-start | bytes 196616 | tf_op jit(solution)/shard_map/ppermute | solution.py:587
  84.6 2.7 %collective-permute-start.19 = (bf16[16,2048]{1,0:T(8,128)(2,1)S(1)}, bf16[16,2048]{1,0:T(8,128)(2,1)S(1)}, u32[]{:S(2)}, u32[]{:S(2)}) collective-permute-start(bf16[16,2048]{1,0:T(8,128)(2,1)S(1)} %get-tuple-element.51), channel_id=1, source_target_pairs={{6,0},{7,1},{4,2},{5,3},{2,4},{3,5},{0,6},{1,7},{14,8},{15,9},{12,... | collective-permute-start | bytes 196616 | tf_op jit(solution)/shard_map/ppermute | solution.py:587
  87.3 3.4 %readout.1.read_ref = f32[1,2048]{1,0:T(1,128)S(1)} custom-call(f32[8,1024]{1,0:T(8,128)S(1)} %reshape.34.head_ref, bf16[1,2048,1024]{2,1,0:T(8,128)(2,1)} %w_hbm.3), custom_call_target="tpu_custom_call" | custom-call | flops 200000000 | bytes 5000000 | tf_op jit(solution)/shard_map/readout/pallas_call | solution.py:460
  91.2 3.4 %out_product.1 = f32[32,16,256]{2,1,0:T(8,128)} custom-call(bf16[32,16,256]{2,1,0:T(8,128)(2,1)S(1)} %all-to-all-done.2.x_ref, f32[1,2048]{1,0:T(1,128)S(1)} %readout.1.read_ref, bf16[1,2048,1024]{2,1,0:T(8,128)(2,1)} %w_hbm.3, bf16[16,2048]{1,0:T(8,128)(2,1)S(1)} %collective-permute-done.16.refs_0_.refs_4_, ...), custom_call_target="tpu_custom_call" | custom-call | flops 300000000 | bytes 5000000 | tf_op jit(solution)/shard_map/out_product/pallas_call | solution.py:507
  94.6 6.8 %all-to-all-start.3 = ((f32[32,16,256]{2,1,0:T(8,128)}), f32[32,16,256]{2,1,0:T(8,128)S(1)}, u32[]{:S(2)}, u32[]{:S(2)}) async-start(f32[32,16,256]{2,1,0:T(8,128)} %out_product.1), calls=%async_computation.3 | async-start | bytes 1048576 | tf_op jit(solution)/shard_map/all_to_all | solution.py:576
  102.3 3.1 %attend_cont.1.mixed_ref = bf16[16,8192]{1,0:T(8,128)(2,1)S(1)} custom-call(s32[1]{0:T(128)} %copy.12.len_ref, s32[1]{0:T(128)S(6)} %copy.13.bound_ref, f32[1,10240]{1,0:T(1,128)S(1)} %bitcast.18, f32[16,128]{1,0:T(8,128)S(1)} %get-tuple-element.64.cos_ref, f32[16,128]{1,0:T(8,128)S(1)} %get-tuple-element.65.sin_ref, bf16[256,2048]{1,0:T(8,128)(2,1)S(1)} %bitcast.12, ...), custom_call_target="tpu_custom_call" | custom-call | flops 400000000 | bytes 8000000 | tf_op jit(solution)/shard_map/attend_cont/pallas_call | solution.py:429
  105.3 6.3 %all-to-all-done.3.parts_ref = f32[32,16,256]{2,1,0:T(8,128)S(1)} async-done(((f32[32,16,256]{2,1,0:T(8,128)}), f32[32,16,256]{2,1,0:T(8,128)S(1)}, u32[]{:S(2)}, u32[]{:S(2)}) %all-to-all-start.3) | async-done | bytes 524320 | tf_op jit(solution)/shard_map/all_to_all | solution.py:576
  (59 shorter events, 18.5 us)
Async XLA Ops:
  14.2 7.3 %collective-permute-start = (bf16[4,16,2304]{2,1,0:T(8,128)(2,1)S(1)}, bf16[4,16,2304]{2,1,0:T(8,128)(2,1)S(1)}, u32[]{:S(2)}, u32[]{:S(2)}) collective-permute-start(bf16[4,16,2304]{2,1,0:T(8,128)(2,1)S(1)} %all_to_all.20.refs_0_), channel_id=1, source_target_pairs={{4,0},{5,1},{6,2},{7,3},{0,4},{1,5},{2,6},{3,7},{12,8},{13,9},{14,... | collective-permute-start | bytes 884744 | tf_op jit(solution)/shard_map/ppermute | solution.py:587
  15.8 9.1 %collective-permute-start.3 = (bf16[4,16,2304]{2,1,0:T(8,128)(2,1)S(1)}, bf16[4,16,2304]{2,1,0:T(8,128)(2,1)S(1)}, u32[]{:S(2)}, u32[]{:S(2)}) collective-permute-start(bf16[4,16,2304]{2,1,0:T(8,128)(2,1)S(1)} %all_to_all.20.refs_0_), channel_id=1, source_target_pairs={{3,0},{0,1},{1,2},{2,3},{7,4},{4,5},{5,6},{6,7},{11,8},{8,9},{9,10... | collective-permute-start | bytes 884744 | tf_op jit(solution)/shard_map/ppermute | solution.py:587
  17.3 9.3 %collective-permute-start.6 = (bf16[4,16,2304]{2,1,0:T(8,128)(2,1)S(1)}, bf16[4,16,2304]{2,1,0:T(8,128)(2,1)S(1)}, u32[]{:S(2)}, u32[]{:S(2)}) collective-permute-start(bf16[4,16,2304]{2,1,0:T(8,128)(2,1)S(1)} %all_to_all.20.refs_0_), channel_id=1, source_target_pairs={{1,0},{2,1},{3,2},{0,3},{5,4},{6,5},{7,6},{4,7},{9,8},{10,9},{11,1... | collective-permute-start | bytes 884744 | tf_op jit(solution)/shard_map/ppermute | solution.py:587
  21.5 12.8 %collective-permute-start.1 = (bf16[4,16,2304]{2,1,0:T(8,128)(2,1)S(1)}, bf16[4,16,2304]{2,1,0:T(8,128)(2,1)S(1)}, u32[]{:S(2)}, u32[]{:S(2)}) collective-permute-start(bf16[4,16,2304]{2,1,0:T(8,128)(2,1)S(1)} %collective-permute-done.refs_1_), channel_id=1, source_target_pairs={{1,0},{2,1},{3,2},{0,3},{5,4},{6,5},{7,6},{4,7},{9,8},{10,9},{11,1... | collective-permute-start | bytes 884744 | tf_op jit(solution)/shard_map/ppermute | solution.py:587
  24.3 11.5 %collective-permute-start.2 = (bf16[4,16,2304]{2,1,0:T(8,128)(2,1)S(1)}, bf16[4,16,2304]{2,1,0:T(8,128)(2,1)S(1)}, u32[]{:S(2)}, u32[]{:S(2)}) collective-permute-start(bf16[4,16,2304]{2,1,0:T(8,128)(2,1)S(1)} %collective-permute-done.refs_1_), channel_id=1, source_target_pairs={{3,0},{0,1},{1,2},{2,3},{7,4},{4,5},{5,6},{6,7},{11,8},{8,9},{9,10... | collective-permute-start | bytes 884744 | tf_op jit(solution)/shard_map/ppermute | solution.py:587
  30.6 19.4 %collective-permute-start.7 = (bf16[4,16,2048]{2,1,0:T(8,128)(2,1)S(1)}, bf16[4,16,2048]{2,1,0:T(8,128)(2,1)S(1)}, u32[]{:S(2)}, u32[]{:S(2)}) collective-permute-start(bf16[4,16,2048]{2,1,0:T(8,128)(2,1)S(1)} %get-tuple-element.32), channel_id=1, source_target_pairs={{24,0},{25,1},{26,2},{27,3},{28,4},{29,5},{30,6},{31,7},{0,8},{1,9... | collective-permute-start | bytes 786440 | tf_op jit(solution)/shard_map/ppermute | solution.py:592
  31.2 21.3 %collective-permute-start.8 = (bf16[4,16,2048]{2,1,0:T(8,128)(2,1)S(1)}, bf16[4,16,2048]{2,1,0:T(8,128)(2,1)S(1)}, u32[]{:S(2)}, u32[]{:S(2)}) collective-permute-start(bf16[4,16,2048]{2,1,0:T(8,128)(2,1)S(1)} %get-tuple-element.33), channel_id=1, source_target_pairs={{16,0},{17,1},{18,2},{19,3},{20,4},{21,5},{22,6},{23,7},{24,8},{25... | collective-permute-start | bytes 786440 | tf_op jit(solution)/shard_map/ppermute | solution.py:592
  33.3 19.2 %collective-permute-start.9 = (bf16[4,16,2048]{2,1,0:T(8,128)(2,1)S(1)}, bf16[4,16,2048]{2,1,0:T(8,128)(2,1)S(1)}, u32[]{:S(2)}, u32[]{:S(2)}) collective-permute-start(bf16[4,16,2048]{2,1,0:T(8,128)(2,1)S(1)} %get-tuple-element.34), channel_id=1, source_target_pairs={{8,0},{9,1},{10,2},{11,3},{12,4},{13,5},{14,6},{15,7},{16,8},{17,9... | collective-permute-start | bytes 786440 | tf_op jit(solution)/shard_map/ppermute | solution.py:592
  34.3 7.9 %collective-permute-start.4 = (bf16[4,16,2304]{2,1,0:T(8,128)(2,1)S(1)}, bf16[4,16,2304]{2,1,0:T(8,128)(2,1)S(1)}, u32[]{:S(2)}, u32[]{:S(2)}) collective-permute-start(bf16[4,16,2304]{2,1,0:T(8,128)(2,1)S(1)} %collective-permute-done.3.refs_3_), channel_id=1, source_target_pairs={{3,0},{0,1},{1,2},{2,3},{7,4},{4,5},{5,6},{6,7},{11,8},{8,9},{9,10... | collective-permute-start | bytes 884744 | tf_op jit(solution)/shard_map/ppermute | solution.py:587
  35.8 6.7 %collective-permute-start.5 = (bf16[4,16,2304]{2,1,0:T(8,128)(2,1)S(1)}, bf16[4,16,2304]{2,1,0:T(8,128)(2,1)S(1)}, u32[]{:S(2)}, u32[]{:S(2)}) collective-permute-start(bf16[4,16,2304]{2,1,0:T(8,128)(2,1)S(1)} %collective-permute-done.1.refs_0_), channel_id=1, source_target_pairs={{1,0},{2,1},{3,2},{0,3},{5,4},{6,5},{7,6},{4,7},{9,8},{10,9},{11,1... | collective-permute-start | bytes 884744 | tf_op jit(solution)/shard_map/ppermute | solution.py:587
  42.5 44.7 %copy-start.4 = (f32[8192]{0:T(1024)S(1)}, f32[8192]{0:T(1024)}, u32[]{:S(2)}) copy-start(f32[8192]{0:T(1024)} %param.19) | copy-start | bytes 98308
  47.3 21.9 %collective-permute-start.10 = (bf16[4,16,2048]{2,1,0:T(8,128)(2,1)S(1)}, bf16[4,16,2048]{2,1,0:T(8,128)(2,1)S(1)}, u32[]{:S(2)}, u32[]{:S(2)}) collective-permute-start(bf16[4,16,2048]{2,1,0:T(8,128)(2,1)S(1)} %get-tuple-element.36), channel_id=1, source_target_pairs={{24,0},{25,1},{26,2},{27,3},{28,4},{29,5},{30,6},{31,7},{0,8},{1,9... | collective-permute-start | bytes 786440 | tf_op jit(solution)/shard_map/ppermute | solution.py:592
  48.4 20.8 %collective-permute-start.11 = (bf16[4,16,2048]{2,1,0:T(8,128)(2,1)S(1)}, bf16[4,16,2048]{2,1,0:T(8,128)(2,1)S(1)}, u32[]{:S(2)}, u32[]{:S(2)}) collective-permute-start(bf16[4,16,2048]{2,1,0:T(8,128)(2,1)S(1)} %get-tuple-element.37), channel_id=1, source_target_pairs={{16,0},{17,1},{18,2},{19,3},{20,4},{21,5},{22,6},{23,7},{24,8},{25... | collective-permute-start | bytes 786440 | tf_op jit(solution)/shard_map/ppermute | solution.py:592
  50.0 19.2 %collective-permute-start.12 = (bf16[4,16,2048]{2,1,0:T(8,128)(2,1)S(1)}, bf16[4,16,2048]{2,1,0:T(8,128)(2,1)S(1)}, u32[]{:S(2)}, u32[]{:S(2)}) collective-permute-start(bf16[4,16,2048]{2,1,0:T(8,128)(2,1)S(1)} %get-tuple-element.38), channel_id=1, source_target_pairs={{8,0},{9,1},{10,2},{11,3},{12,4},{13,5},{14,6},{15,7},{16,8},{17,9... | collective-permute-start | bytes 786440 | tf_op jit(solution)/shard_map/ppermute | solution.py:592
  53.4 8.5 %collective-permute-start.13 = (bf16[16,2048]{1,0:T(8,128)(2,1)S(1)}, bf16[16,2048]{1,0:T(8,128)(2,1)S(1)}, u32[]{:S(2)}, u32[]{:S(2)}) collective-permute-start(bf16[16,2048]{1,0:T(8,128)(2,1)S(1)} %get-tuple-element.43), channel_id=1, source_target_pairs={{4,0},{5,1},{6,2},{7,3},{0,4},{1,5},{2,6},{3,7},{12,8},{13,9},{14,... | collective-permute-start | bytes 196616 | tf_op jit(solution)/shard_map/ppermute | solution.py:587
  53.4 15.8 %all-to-all-start.1 = ((bf16[32,16,256]{2,1,0:T(8,128)(2,1)}), bf16[32,16,256]{2,1,0:T(8,128)(2,1)S(1)}, u32[]{:S(2)}, u32[]{:S(2)}) async-start(bf16[32,16,256]{2,1,0:T(8,128)(2,1)} %get-tuple-element.35), calls=%async_computation.1 | async-start | bytes 524288 | tf_op jit(solution)/shard_map/all_to_all | solution.py:576
  60.0 6.6 %collective-permute-start.14 = (bf16[16,2048]{1,0:T(8,128)(2,1)S(1)}, bf16[16,2048]{1,0:T(8,128)(2,1)S(1)}, u32[]{:S(2)}, u32[]{:S(2)}) collective-permute-start(bf16[16,2048]{1,0:T(8,128)(2,1)S(1)} %get-tuple-element.44), channel_id=1, source_target_pairs={{3,0},{0,1},{1,2},{2,3},{7,4},{4,5},{5,6},{6,7},{11,8},{8,9},{9,10... | collective-permute-start | bytes 196616 | tf_op jit(solution)/shard_map/ppermute | solution.py:587
  61.9 4.8 %collective-permute-start.15 = (bf16[16,2048]{1,0:T(8,128)(2,1)}, bf16[16,2048]{1,0:T(8,128)(2,1)S(1)}, u32[]{:S(2)}, u32[]{:S(2)}) collective-permute-start(bf16[16,2048]{1,0:T(8,128)(2,1)} %copy-done.5), channel_id=1, source_target_pairs={{1,0},{2,1},{3,2},{0,3},{5,4},{6,5},{7,6},{4,7},{9,8},{10,9},{11,1... | collective-permute-start | bytes 196616 | tf_op jit(solution)/shard_map/ppermute | solution.py:587
  72.9 18.4 %all-to-all-start.2 = ((bf16[32,16,256]{2,1,0:T(8,128)(2,1)}), bf16[32,16,256]{2,1,0:T(8,128)(2,1)S(1)}, u32[]{:S(2)}, u32[]{:S(2)}) async-start(bf16[32,16,256]{2,1,0:T(8,128)(2,1)} %get-tuple-element.46), calls=%async_computation.2 | async-start | bytes 524288 | tf_op jit(solution)/shard_map/all_to_all | solution.py:576
  78.3 12.5 %collective-permute-start.16 = (bf16[16,2048]{1,0:T(8,128)(2,1)S(1)}, bf16[16,2048]{1,0:T(8,128)(2,1)S(1)}, u32[]{:S(2)}, u32[]{:S(2)}) collective-permute-start(bf16[16,2048]{1,0:T(8,128)(2,1)S(1)} %get-tuple-element.48), channel_id=1, source_target_pairs={{7,0},{4,1},{5,2},{6,3},{3,4},{0,5},{1,6},{2,7},{15,8},{12,9},{13,... | collective-permute-start | bytes 196616 | tf_op jit(solution)/shard_map/ppermute | solution.py:587
  81.0 9.7 %collective-permute-start.17 = (bf16[16,2048]{1,0:T(8,128)(2,1)S(1)}, bf16[16,2048]{1,0:T(8,128)(2,1)S(1)}, u32[]{:S(2)}, u32[]{:S(2)}) collective-permute-start(bf16[16,2048]{1,0:T(8,128)(2,1)S(1)} %get-tuple-element.49), channel_id=1, source_target_pairs={{5,0},{6,1},{7,2},{4,3},{1,4},{2,5},{3,6},{0,7},{13,8},{14,9},{15,... | collective-permute-start | bytes 196616 | tf_op jit(solution)/shard_map/ppermute | solution.py:587
  82.5 8.3 %collective-permute-start.18 = (bf16[16,2048]{1,0:T(8,128)(2,1)S(1)}, bf16[16,2048]{1,0:T(8,128)(2,1)S(1)}, u32[]{:S(2)}, u32[]{:S(2)}) collective-permute-start(bf16[16,2048]{1,0:T(8,128)(2,1)S(1)} %get-tuple-element.50), channel_id=1, source_target_pairs={{2,0},{3,1},{0,2},{1,3},{6,4},{7,5},{4,6},{5,7},{10,8},{11,9},{8,1... | collective-permute-start | bytes 196616 | tf_op jit(solution)/shard_map/ppermute | solution.py:587
  84.6 6.7 %collective-permute-start.19 = (bf16[16,2048]{1,0:T(8,128)(2,1)S(1)}, bf16[16,2048]{1,0:T(8,128)(2,1)S(1)}, u32[]{:S(2)}, u32[]{:S(2)}) collective-permute-start(bf16[16,2048]{1,0:T(8,128)(2,1)S(1)} %get-tuple-element.51), channel_id=1, source_target_pairs={{6,0},{7,1},{4,2},{5,3},{2,4},{3,5},{0,6},{1,7},{14,8},{15,9},{12,... | collective-permute-start | bytes 196616 | tf_op jit(solution)/shard_map/ppermute | solution.py:587
  94.6 17.0 %all-to-all-start.3 = ((f32[32,16,256]{2,1,0:T(8,128)}), f32[32,16,256]{2,1,0:T(8,128)S(1)}, u32[]{:S(2)}, u32[]{:S(2)}) async-start(f32[32,16,256]{2,1,0:T(8,128)} %out_product.1), calls=%async_computation.3 | async-start | bytes 1048576 | tf_op jit(solution)/shard_map/all_to_all | solution.py:576
  (7 other events, 152.7 us)

commit v13 on v12

--- a/solution.py
+++ b/solution.py
@@ -120,12 +120,13 @@
     return column // 4, lax.rem(column, 4)
 
 
-def product_kernel(tiles, counts, places, *refs):
+def product_kernel(tiles, counts, places, unread, *refs):
     x_refs, refs = refs[: len(counts)], refs[len(counts) :]
     if places:
         earlier_ref, refs = refs[0], refs[1:]
-    w_hbm, *out_refs = refs[: 1 + ROW_BLOCKS]
-    main_ref, rows_ref, wide_ref, w_ref, sems, part_ref = refs[1 + ROW_BLOCKS :]
+    w_hbm, refs = refs[0], refs[1 + unread :]
+    out_refs = refs[:ROW_BLOCKS]
+    main_ref, rows_ref, wide_ref, w_ref, sems, part_ref = refs[ROW_BLOCKS:]
     n = pl.program_id(0)
     members = sum(counts)
     count = members * CTOK
@@ -190,17 +191,17 @@
                 out_ref[g] = part_ref[g * ROW_BLOCKS + to]
 
 
-def block_product(messages, blocks, earlier=(), places=()):
+def block_product(messages, blocks, earlier=(), places=(), after=()):
     tiles = blocks.shape[2] // TILE
     lanes = tiles * TILE + REST
     counts = tuple(rows.shape[0] for rows in messages)
     members = sum(counts)
     return pl.pallas_call(
-        functools.partial(product_kernel, tiles, counts, places),
+        functools.partial(product_kernel, tiles, counts, places, len(after)),
         out_shape=[jax.ShapeDtypeStruct((members // ROW_BLOCKS, CTOK, lanes), jnp.bfloat16)] * ROW_BLOCKS
         + [jax.ShapeDtypeStruct((MEMBERS if places else members, CTOK, TILE), jnp.bfloat16)],
         grid=(tiles,),
-        in_specs=[VMEM] * (len(counts) + len(earlier)) + [HBM],
+        in_specs=[VMEM] * (len(counts) + len(earlier)) + [HBM] + [UNREAD] * len(after),
         out_specs=[VMEM] * (1 + ROW_BLOCKS),
         scratch_shapes=[
             pltpu.VMEM((members * (CTOK + STEPS), FEATURES), jnp.bfloat16),
@@ -212,7 +213,7 @@
         compiler_params=kernel_params(),
         cost_estimate=cost(2 * members * (CTOK + STEPS) * FEATURES * tiles * TILE, 12 * 10**6),
         name="block_product",
-    )(*messages, *earlier, in_hbm(blocks))
+    )(*messages, *earlier, in_hbm(blocks), *after)
 
 
 def sum_kernel(bias_ref, *refs):
@@ -597,7 +598,7 @@
 HOMES = FIRST_HOMES + SECOND_HOMES
 
 
-def project(rows, blocks, bias):
+def project(rows, blocks, bias, read):
     near = lax.all_to_all(rows, "tp", split_axis=0, concat_axis=0, tiled=True, axis_index_groups=ALONG)
     over = from_side(near, 1, 0)
     after, before = from_side(near, 0, 1), from_side(near, 0, 3)
@@ -605,7 +606,7 @@
     far = [from_side(before, 0, 3), from_side(over_after, 0, 1)]
     *first, main = block_product([near, over, after, before], blocks)
     first = [first[0]] + [from_along(first[k], -k) for k in range(1, ROW_BLOCKS)]
-    *second, main = block_product([over_after, over_before] + far, blocks, (main,), HOMES)
+    *second, main = block_product([over_after, over_before] + far, blocks, (main,), HOMES, (read,))
     main, first = lax.optimization_barrier((main, first))
     second = [second[0]] + [from_along(second[k], -k) for k in range(1, ROW_BLOCKS)]
     received = []
@@ -627,7 +628,7 @@
     main_tables = rope_tables(prefix_len + step[:8])
     cont_tables = rope_tables(prefix_len + boundary + step)
     read = readout(value_head.reshape(COL_BLOCKS, D // COL_BLOCKS), w_out)
-    parts, main_parts, before = project(norm_rows(main, cont, rms_gain[None, :]), w_qkv, bias)
+    parts, main_parts, before = project(norm_rows(main, cont, rms_gain[None, :]), w_qkv, bias, read)
     mixed, main_kv = attend_main(prefix_len, bias, *main_tables, cache, main_parts, before)
     mixed = exchange(mixed)
     cont_mixed = attend_cont(prefix_len, boundary, bias, *cont_tables, cache, main_kv, *parts)

time: 114 us -> 122 us (1.070)
  waiting for transfers between devices: 21.5 us -> 25 us
  starting transfers between devices: 50.5 us -> 53.8 us
  other arithmetic: 0.4 us -> 2.18 us
    ppermute x14, waiting for transfers between devices: 12.7 us -> 16.5 us  [from_side(): return lax.ppermute(rows, 'tp', route)]
    ppermute x14, starting transfers between devices: 23.1 us -> 25.6 us  [from_side(): return lax.ppermute(rows, 'tp', route)]
  transfers between devices with their start and end apart: 23 -> 23, of which waited for: 8 -> 9; matrix products, arithmetic and copies ran while one was open for 0% -> 2% of each run, Pallas kernels for 14% -> 13%
where the time goes in v13:
time: 122 us
  starting transfers between devices  53.8 us (44%)
  waiting for transfers between devices  25 us (20%)
  Pallas kernels  24.9 us (20%)
  blocking collectives  12.2 us (10%)
  other arithmetic  2.18 us (2%)
  between operations  2.09 us (2%)
  local copies, waits for them, and re-layouts  1.31 us (1%)
    ppermute x14, starting transfers between devices, from_side(): return lax.ppermute(rows, 'tp', route)  25.6 us
    all_to_all x3, starting transfers between devices, exchange(): return lax.all_to_all(rows, 'tp', split_axis=0, concat_axis=0, tiled=True)  19.2 us
    ppermute x14, waiting for transfers between devices, from_side(): return lax.ppermute(rows, 'tp', route)  16.5 us
    all_to_all x1, blocking collectives, project(): lax.all_to_all(rows, 'tp', split_axis=0, concat_axis=0, tiled=True, axis_...  12.2 us
    ppermute x6, starting transfers between devices, from_along(): return lax.ppermute(rows, 'tp', route)  8.93 us
    pallas_call x2, Pallas kernels, block_product(): pl.pallas_call(functools.partial(product_kernel, tiles, counts, places, l...  8.68 us
    all_to_all x3, waiting for transfers between devices, exchange(): return lax.all_to_all(rows, 'tp', split_axis=0, concat_axis=0, tiled=True)  8.52 us
    pallas_call x1, Pallas kernels, attend_main(): pl.pallas_call(attend_main_kernel, out_shape=(jax.ShapeDtypeStruct((32, 1...  3.7 us
  transfers between devices with their start and end apart: 23, of which 9 were waited for; matrix products, arithmetic and copies ran while one was open for 2% of the time, Pallas kernels for 13%

profile of v13, /device:TPU:0, one launch (start us, length us, event | category | flops | bytes accessed | tf_op | source)
XLA Modules:
  0.0 121.5 jit_solution(2601811496502863611)
XLA Ops:
  2.0 12.2 %all_to_all.20.refs_0_ = bf16[4,16,2304]{2,1,0:T(8,128)(2,1)S(1)} all-to-all(bf16[4,16,2304]{2,1,0:T(8,128)(2,1)S(1)} %norm_rows.1), channel_id=1, replica_groups={{0,8,16,24},{1,9,17,25},{2,10,18,26},{3,11,19,27},{4,12,20,28},{5,13,21..., dimensions={0} | all-to-all | bytes 589824 | tf_op jit(solution)/shard_map/all_to_all | solution.py:602
  17.3 4.2 %collective-permute-done.refs_1_ = bf16[4,16,2304]{2,1,0:T(8,128)(2,1)S(1)} collective-permute-done((bf16[4,16,2304]{2,1,0:T(8,128)(2,1)S(1)}, bf16[4,16,2304]{2,1,0:T(8,128)(2,1)S(1)}, u32[]{:S(2)}, u32[]{:S(2)}) %collective-permute-start) | collective-permute-done | bytes 294944 | tf_op jit(solution)/shard_map/ppermute | solution.py:588
  21.5 2.8 %collective-permute-start.1 = (bf16[4,16,2304]{2,1,0:T(8,128)(2,1)S(1)}, bf16[4,16,2304]{2,1,0:T(8,128)(2,1)S(1)}, u32[]{:S(2)}, u32[]{:S(2)}) collective-permute-start(bf16[4,16,2304]{2,1,0:T(8,128)(2,1)S(1)} %collective-permute-done.refs_1_), channel_id=1, source_target_pairs={{1,0},{2,1},{3,2},{0,3},{5,4},{6,5},{7,6},{4,7},{9,8},{10,9},{11,1... | collective-permute-start | bytes 884744 | tf_op jit(solution)/shard_map/ppermute | solution.py:588
  27.1 4.6 %collective-permute-done.1.refs_0_ = bf16[4,16,2304]{2,1,0:T(8,128)(2,1)S(1)} collective-permute-done((bf16[4,16,2304]{2,1,0:T(8,128)(2,1)S(1)}, bf16[4,16,2304]{2,1,0:T(8,128)(2,1)S(1)}, u32[]{:S(2)}, u32[]{:S(2)}) %collective-permute-start.1) | collective-permute-done | bytes 294944 | tf_op jit(solution)/shard_map/ppermute | solution.py:588
  31.7 3.7 %collective-permute-start.5 = (bf16[4,16,2304]{2,1,0:T(8,128)(2,1)S(1)}, bf16[4,16,2304]{2,1,0:T(8,128)(2,1)S(1)}, u32[]{:S(2)}, u32[]{:S(2)}) collective-permute-start(bf16[4,16,2304]{2,1,0:T(8,128)(2,1)S(1)} %collective-permute-done.1.refs_0_), channel_id=1, source_target_pairs={{1,0},{2,1},{3,2},{0,3},{5,4},{6,5},{7,6},{4,7},{9,8},{10,9},{11,1... | collective-permute-start | bytes 884744 | tf_op jit(solution)/shard_map/ppermute | solution.py:588
  37.6 3.9 %block_product.2 = (bf16[4,16,2048]{2,1,0:T(8,128)(2,1)S(1)}, bf16[4,16,2048]{2,1,0:T(8,128)(2,1)S(1)}, bf16[4,16,2048]{2,1,0:T(8,128)(2,1)S(1)}, bf16[4,16,2048...) custom-call(bf16[4,16,2304]{2,1,0:T(8,128)(2,1)S(1)} %all_to_all.20.refs_0_, ...), custom_call_target="tpu_custom_call" | custom-call | flops 1509949440 | bytes 12000000 | tf_op jit(solution)/shard_map/block_product/pallas_call | solution.py:199
  42.2 2.1 %collective-permute-start.8 = (bf16[4,16,2048]{2,1,0:T(8,128)(2,1)S(1)}, bf16[4,16,2048]{2,1,0:T(8,128)(2,1)S(1)}, u32[]{:S(2)}, u32[]{:S(2)}) collective-permute-start(bf16[4,16,2048]{2,1,0:T(8,128)(2,1)S(1)} %get-tuple-element.33), channel_id=1, source_target_pairs={{16,0},{17,1},{18,2},{19,3},{20,4},{21,5},{22,6},{23,7},{24,8},{25... | collective-permute-start | bytes 786440 | tf_op jit(solution)/shard_map/ppermute | solution.py:593
  45.7 3.4 %readout.1.refs_6_.read_ref = f32[1,2048]{1,0:T(1,128)S(1)} custom-call(f32[8,1024]{1,0:T(8,128)S(1)} %reshape.34.head_ref, bf16[1,2048,1024]{2,1,0:T(8,128)(2,1)} %w_hbm.3), custom_call_target="tpu_custom_call" | custom-call | flops 200000000 | bytes 5000000 | tf_op jit(solution)/shard_map/readout/pallas_call | solution.py:461
  49.7 4.8 %block_product.3 = (bf16[4,16,2048]{2,1,0:T(8,128)(2,1)S(1)}, bf16[4,16,2048]{2,1,0:T(8,128)(2,1)}, bf16[4,16,2048]{2,1,0:T(8,128)(2,1)S(1)}, bf16[4,16,2048]{2,1,0:T(8,128)(2,1)S(1)}, bf16[32,16,256]{2,1,0:T(8,128)(2,1)}) custom-call(bf16[4,16,2304]{2,1,0:T(8,128)(2,1)S(1)} %collective-permute-done.1.refs_0_, ...), custom_call_target="tpu_custom_call" | custom-call | flops 1509949440 | bytes 12000000 | tf_op jit(solution)/shard_map/block_product/pallas_call | solution.py:199
  56.6 2.5 %collective-permute-start.12 = (bf16[4,16,2048]{2,1,0:T(8,128)(2,1)S(1)}, bf16[4,16,2048]{2,1,0:T(8,128)(2,1)S(1)}, u32[]{:S(2)}, u32[]{:S(2)}) collective-permute-start(bf16[4,16,2048]{2,1,0:T(8,128)(2,1)S(1)} %get-tuple-element.38), channel_id=1, source_target_pairs={{8,0},{9,1},{10,2},{11,3},{12,4},{13,5},{14,6},{15,7},{16,8},{17,9... | collective-permute-start | bytes 786440 | tf_op jit(solution)/shard_map/ppermute | solution.py:593
  61.1 6.3 %all-to-all-start.1 = ((bf16[32,16,256]{2,1,0:T(8,128)(2,1)}), bf16[32,16,256]{2,1,0:T(8,128)(2,1)S(1)}, u32[]{:S(2)}, u32[]{:S(2)}) async-start(bf16[32,16,256]{2,1,0:T(8,128)(2,1)} %get-tuple-element.35), calls=%async_computation.1 | async-start | bytes 524288 | tf_op jit(solution)/shard_map/all_to_all | solution.py:577
  68.2 1.9 %collective-permute-start.14 = (bf16[16,2048]{1,0:T(8,128)(2,1)S(1)}, bf16[16,2048]{1,0:T(8,128)(2,1)S(1)}, u32[]{:S(2)}, u32[]{:S(2)}) collective-permute-start(bf16[16,2048]{1,0:T(8,128)(2,1)S(1)} %get-tuple-element.44), channel_id=1, source_target_pairs={{3,0},{0,1},{1,2},{2,3},{7,4},{4,5},{5,6},{6,7},{11,8},{8,9},{9,10... | collective-permute-start | bytes 196616 | tf_op jit(solution)/shard_map/ppermute | solution.py:588
  71.6 2.5 %collective-permute-done.14.refs_4_.refs_2_ = bf16[16,2048]{1,0:T(8,128)(2,1)S(1)} collective-permute-done((bf16[16,2048]{1,0:T(8,128)(2,1)S(1)}, bf16[16,2048]{1,0:T(8,128)(2,1)S(1)}, u32[]{:S(2)}, u32[]{:S(2)}) %collective-permute-start.14) | collective-permute-done | bytes 65568 | tf_op jit(solution)/shard_map/ppermute | solution.py:588
  74.3 2.3 %all-to-all-done.1.parts_ref = bf16[32,16,256]{2,1,0:T(8,128)(2,1)S(1)} async-done(((bf16[32,16,256]{2,1,0:T(8,128)(2,1)}), bf16[32,16,256]{2,1,0:T(8,128)(2,1)S(1)}, u32[]{:S(2)}, u32[]{:S(2)}) %all-to-all-start.1) | async-done | bytes 262176 | tf_op jit(solution)/shard_map/all_to_all | solution.py:577
  76.6 3.7 %attend_main.1 = (bf16[32,16,256]{2,1,0:T(8,128)(2,1)}, f32[8,2048]{1,0:T(8,128)S(1)}) custom-call(s32[1]{0:T(128)} %copy.12.len_ref, f32[1,10240]{1,0:T(1,128)S(1)} %bitcast.16, f32[8,128]{1,0:T(8,128)S(1)} %get-tuple-element.62.cos_ref, f32[8,128]{1,0:T(8,128)S(1)} %get-tuple-element.63.sin_ref, bf16[256,2048]{1,0:T(8,128)(2,1)S(1)} %bitcast.11, ...), custom_call_target="tpu_custom_call" | custom-call | flops 200000000 | bytes 6000000 | tf_op jit(solution)/shard_map/attend_main/pallas_call | solution.py:384
  80.3 5.9 %all-to-all-start.2 = ((bf16[32,16,256]{2,1,0:T(8,128)(2,1)}), bf16[32,16,256]{2,1,0:T(8,128)(2,1)S(1)}, u32[]{:S(2)}, u32[]{:S(2)}) async-start(bf16[32,16,256]{2,1,0:T(8,128)(2,1)} %get-tuple-element.46), calls=%async_computation.2 | async-start | bytes 524288 | tf_op jit(solution)/shard_map/all_to_all | solution.py:577
  86.4 2.8 %collective-permute-start.16 = (bf16[16,2048]{1,0:T(8,128)(2,1)S(1)}, bf16[16,2048]{1,0:T(8,128)(2,1)S(1)}, u32[]{:S(2)}, u32[]{:S(2)}) collective-permute-start(bf16[16,2048]{1,0:T(8,128)(2,1)S(1)} %get-tuple-element.48), channel_id=1, source_target_pairs={{7,0},{4,1},{5,2},{6,3},{3,4},{0,5},{1,6},{2,7},{15,8},{12,9},{13,... | collective-permute-start | bytes 196616 | tf_op jit(solution)/shard_map/ppermute | solution.py:588
  90.6 2.1 %collective-permute-start.18 = (bf16[16,2048]{1,0:T(8,128)(2,1)S(1)}, bf16[16,2048]{1,0:T(8,128)(2,1)S(1)}, u32[]{:S(2)}, u32[]{:S(2)}) collective-permute-start(bf16[16,2048]{1,0:T(8,128)(2,1)S(1)} %get-tuple-element.50), channel_id=1, source_target_pairs={{2,0},{3,1},{0,2},{1,3},{6,4},{7,5},{4,6},{5,7},{10,8},{11,9},{8,1... | collective-permute-start | bytes 196616 | tf_op jit(solution)/shard_map/ppermute | solution.py:588
  92.7 2.7 %collective-permute-start.19 = (bf16[16,2048]{1,0:T(8,128)(2,1)S(1)}, bf16[16,2048]{1,0:T(8,128)(2,1)S(1)}, u32[]{:S(2)}, u32[]{:S(2)}) collective-permute-start(bf16[16,2048]{1,0:T(8,128)(2,1)S(1)} %get-tuple-element.51), channel_id=1, source_target_pairs={{6,0},{7,1},{4,2},{5,3},{2,4},{3,5},{0,6},{1,7},{14,8},{15,9},{12,... | collective-permute-start | bytes 196616 | tf_op jit(solution)/shard_map/ppermute | solution.py:588
  96.4 3.0 %collective-permute-done.19.refs_3_.refs_7_ = bf16[16,2048]{1,0:T(8,128)(2,1)S(1)} collective-permute-done((bf16[16,2048]{1,0:T(8,128)(2,1)S(1)}, bf16[16,2048]{1,0:T(8,128)(2,1)S(1)}, u32[]{:S(2)}, u32[]{:S(2)}) %collective-permute-start.19) | collective-permute-done | bytes 65568 | tf_op jit(solution)/shard_map/ppermute | solution.py:588
  99.4 3.4 %out_product.1 = f32[32,16,256]{2,1,0:T(8,128)} custom-call(bf16[32,16,256]{2,1,0:T(8,128)(2,1)S(1)} %all-to-all-done.2.x_ref, f32[1,2048]{1,0:T(1,128)S(1)} %readout.1.refs_6_.read_ref, bf16[1,2048,1024]{2,1,0:T(8,128)(2,1)} %w_hbm.3, bf16[16,2048]{1,0:T(8,128)(2,1)S(1)} %collective-permute-done.16.refs_0_.refs_4_, ...), custom_call_target="tpu_custom_call" | custom-call | flops 300000000 | bytes 5000000 | tf_op jit(solution)/shard_map/out_product/pallas_call | solution.py:508
  102.8 7.1 %all-to-all-start.3 = ((f32[32,16,256]{2,1,0:T(8,128)}), f32[32,16,256]{2,1,0:T(8,128)S(1)}, u32[]{:S(2)}, u32[]{:S(2)}) async-start(f32[32,16,256]{2,1,0:T(8,128)} %out_product.1), calls=%async_computation.3 | async-start | bytes 1048576 | tf_op jit(solution)/shard_map/all_to_all | solution.py:577
  110.7 3.0 %attend_cont.1.mixed_ref = bf16[16,8192]{1,0:T(8,128)(2,1)S(1)} custom-call(s32[1]{0:T(128)} %copy.12.len_ref, s32[1]{0:T(128)S(6)} %copy.13.bound_ref, f32[1,10240]{1,0:T(1,128)S(1)} %bitcast.18, f32[16,128]{1,0:T(8,128)S(1)} %get-tuple-element.64.cos_ref, f32[16,128]{1,0:T(8,128)S(1)} %get-tuple-element.65.sin_ref, bf16[256,2048]{1,0:T(8,128)(2,1)S(1)} %bitcast.12, ...), custom_call_target="tpu_custom_call" | custom-call | flops 400000000 | bytes 8000000 | tf_op jit(solution)/shard_map/attend_cont/pallas_call | solution.py:430
  113.8 6.3 %all-to-all-done.3.parts_ref = f32[32,16,256]{2,1,0:T(8,128)S(1)} async-done(((f32[32,16,256]{2,1,0:T(8,128)}), f32[32,16,256]{2,1,0:T(8,128)S(1)}, u32[]{:S(2)}, u32[]{:S(2)}) %all-to-all-start.3) | async-done | bytes 524320 | tf_op jit(solution)/shard_map/all_to_all | solution.py:577
  (55 shorter events, 22.5 us)
Async XLA Ops:
  14.2 7.3 %collective-permute-start = (bf16[4,16,2304]{2,1,0:T(8,128)(2,1)S(1)}, bf16[4,16,2304]{2,1,0:T(8,128)(2,1)S(1)}, u32[]{:S(2)}, u32[]{:S(2)}) collective-permute-start(bf16[4,16,2304]{2,1,0:T(8,128)(2,1)S(1)} %all_to_all.20.refs_0_), channel_id=1, source_target_pairs={{4,0},{5,1},{6,2},{7,3},{0,4},{1,5},{2,6},{3,7},{12,8},{13,9},{14,... | collective-permute-start | bytes 884744 | tf_op jit(solution)/shard_map/ppermute | solution.py:588
  15.8 11.2 %collective-permute-start.3 = (bf16[4,16,2304]{2,1,0:T(8,128)(2,1)S(1)}, bf16[4,16,2304]{2,1,0:T(8,128)(2,1)S(1)}, u32[]{:S(2)}, u32[]{:S(2)}) collective-permute-start(bf16[4,16,2304]{2,1,0:T(8,128)(2,1)S(1)} %all_to_all.20.refs_0_), channel_id=1, source_target_pairs={{3,0},{0,1},{1,2},{2,3},{7,4},{4,5},{5,6},{6,7},{11,8},{8,9},{9,10... | collective-permute-start | bytes 884744 | tf_op jit(solution)/shard_map/ppermute | solution.py:588
  21.5 10.2 %collective-permute-start.1 = (bf16[4,16,2304]{2,1,0:T(8,128)(2,1)S(1)}, bf16[4,16,2304]{2,1,0:T(8,128)(2,1)S(1)}, u32[]{:S(2)}, u32[]{:S(2)}) collective-permute-start(bf16[4,16,2304]{2,1,0:T(8,128)(2,1)S(1)} %collective-permute-done.refs_1_), channel_id=1, source_target_pairs={{1,0},{2,1},{3,2},{0,3},{5,4},{6,5},{7,6},{4,7},{9,8},{10,9},{11,1... | collective-permute-start | bytes 884744 | tf_op jit(solution)/shard_map/ppermute | solution.py:588
  24.9 12.7 %collective-permute-start.6 = (bf16[4,16,2304]{2,1,0:T(8,128)(2,1)S(1)}, bf16[4,16,2304]{2,1,0:T(8,128)(2,1)S(1)}, u32[]{:S(2)}, u32[]{:S(2)}) collective-permute-start(bf16[4,16,2304]{2,1,0:T(8,128)(2,1)S(1)} %all_to_all.20.refs_0_), channel_id=1, source_target_pairs={{1,0},{2,1},{3,2},{0,3},{5,4},{6,5},{7,6},{4,7},{9,8},{10,9},{11,1... | collective-permute-start | bytes 884744 | tf_op jit(solution)/shard_map/ppermute | solution.py:588
  25.8 18.4 %collective-permute-start.2 = (bf16[4,16,2304]{2,1,0:T(8,128)(2,1)S(1)}, bf16[4,16,2304]{2,1,0:T(8,128)(2,1)S(1)}, u32[]{:S(2)}, u32[]{:S(2)}) collective-permute-start(bf16[4,16,2304]{2,1,0:T(8,128)(2,1)S(1)} %collective-permute-done.refs_1_), channel_id=1, source_target_pairs={{3,0},{0,1},{1,2},{2,3},{7,4},{4,5},{5,6},{6,7},{11,8},{8,9},{9,10... | collective-permute-start | bytes 884744 | tf_op jit(solution)/shard_map/ppermute | solution.py:588
  27.0 22.7 %collective-permute-start.4 = (bf16[4,16,2304]{2,1,0:T(8,128)(2,1)S(1)}, bf16[4,16,2304]{2,1,0:T(8,128)(2,1)S(1)}, u32[]{:S(2)}, u32[]{:S(2)}) collective-permute-start(bf16[4,16,2304]{2,1,0:T(8,128)(2,1)S(1)} %collective-permute-done.3.refs_3_), channel_id=1, source_target_pairs={{3,0},{0,1},{1,2},{2,3},{7,4},{4,5},{5,6},{6,7},{11,8},{8,9},{9,10... | collective-permute-start | bytes 884744 | tf_op jit(solution)/shard_map/ppermute | solution.py:588
  31.7 18.0 %collective-permute-start.5 = (bf16[4,16,2304]{2,1,0:T(8,128)(2,1)S(1)}, bf16[4,16,2304]{2,1,0:T(8,128)(2,1)S(1)}, u32[]{:S(2)}, u32[]{:S(2)}) collective-permute-start(bf16[4,16,2304]{2,1,0:T(8,128)(2,1)S(1)} %collective-permute-done.1.refs_0_), channel_id=1, source_target_pairs={{1,0},{2,1},{3,2},{0,3},{5,4},{6,5},{7,6},{4,7},{9,8},{10,9},{11,1... | collective-permute-start | bytes 884744 | tf_op jit(solution)/shard_map/ppermute | solution.py:588
  41.5 15.1 %collective-permute-start.7 = (bf16[4,16,2048]{2,1,0:T(8,128)(2,1)S(1)}, bf16[4,16,2048]{2,1,0:T(8,128)(2,1)S(1)}, u32[]{:S(2)}, u32[]{:S(2)}) collective-permute-start(bf16[4,16,2048]{2,1,0:T(8,128)(2,1)S(1)} %get-tuple-element.32), channel_id=1, source_target_pairs={{24,0},{25,1},{26,2},{27,3},{28,4},{29,5},{30,6},{31,7},{0,8},{1,9... | collective-permute-start | bytes 786440 | tf_op jit(solution)/shard_map/ppermute | solution.py:593
  42.2 17.0 %collective-permute-start.8 = (bf16[4,16,2048]{2,1,0:T(8,128)(2,1)S(1)}, bf16[4,16,2048]{2,1,0:T(8,128)(2,1)S(1)}, u32[]{:S(2)}, u32[]{:S(2)}) collective-permute-start(bf16[4,16,2048]{2,1,0:T(8,128)(2,1)S(1)} %get-tuple-element.33), channel_id=1, source_target_pairs={{16,0},{17,1},{18,2},{19,3},{20,4},{21,5},{22,6},{23,7},{24,8},{25... | collective-permute-start | bytes 786440 | tf_op jit(solution)/shard_map/ppermute | solution.py:593
  44.2 15.0 %collective-permute-start.9 = (bf16[4,16,2048]{2,1,0:T(8,128)(2,1)S(1)}, bf16[4,16,2048]{2,1,0:T(8,128)(2,1)S(1)}, u32[]{:S(2)}, u32[]{:S(2)}) collective-permute-start(bf16[4,16,2048]{2,1,0:T(8,128)(2,1)S(1)} %get-tuple-element.34), channel_id=1, source_target_pairs={{8,0},{9,1},{10,2},{11,3},{12,4},{13,5},{14,6},{15,7},{16,8},{17,9... | collective-permute-start | bytes 786440 | tf_op jit(solution)/shard_map/ppermute | solution.py:593
  54.4 22.1 %collective-permute-start.10 = (bf16[4,16,2048]{2,1,0:T(8,128)(2,1)}, bf16[4,16,2048]{2,1,0:T(8,128)(2,1)S(1)}, u32[]{:S(2)}, u32[]{:S(2)}) collective-permute-start(bf16[4,16,2048]{2,1,0:T(8,128)(2,1)} %get-tuple-element.36), channel_id=1, source_target_pairs={{24,0},{25,1},{26,2},{27,3},{28,4},{29,5},{30,6},{31,7},{0,8},{1,9... | collective-permute-start | bytes 786440 | tf_op jit(solution)/shard_map/ppermute | solution.py:593
  55.0 21.5 %collective-permute-start.11 = (bf16[4,16,2048]{2,1,0:T(8,128)(2,1)S(1)}, bf16[4,16,2048]{2,1,0:T(8,128)(2,1)S(1)}, u32[]{:S(2)}, u32[]{:S(2)}) collective-permute-start(bf16[4,16,2048]{2,1,0:T(8,128)(2,1)S(1)} %get-tuple-element.37), channel_id=1, source_target_pairs={{16,0},{17,1},{18,2},{19,3},{20,4},{21,5},{22,6},{23,7},{24,8},{25... | collective-permute-start | bytes 786440 | tf_op jit(solution)/shard_map/ppermute | solution.py:593
  56.6 19.9 %collective-permute-start.12 = (bf16[4,16,2048]{2,1,0:T(8,128)(2,1)S(1)}, bf16[4,16,2048]{2,1,0:T(8,128)(2,1)S(1)}, u32[]{:S(2)}, u32[]{:S(2)}) collective-permute-start(bf16[4,16,2048]{2,1,0:T(8,128)(2,1)S(1)} %get-tuple-element.38), channel_id=1, source_target_pairs={{8,0},{9,1},{10,2},{11,3},{12,4},{13,5},{14,6},{15,7},{16,8},{17,9... | collective-permute-start | bytes 786440 | tf_op jit(solution)/shard_map/ppermute | solution.py:593
  59.4 10.7 %collective-permute-start.13 = (bf16[16,2048]{1,0:T(8,128)(2,1)S(1)}, bf16[16,2048]{1,0:T(8,128)(2,1)S(1)}, u32[]{:S(2)}, u32[]{:S(2)}) collective-permute-start(bf16[16,2048]{1,0:T(8,128)(2,1)S(1)} %get-tuple-element.43), channel_id=1, source_target_pairs={{4,0},{5,1},{6,2},{7,3},{0,4},{1,5},{2,6},{3,7},{12,8},{13,9},{14,... | collective-permute-start | bytes 196616 | tf_op jit(solution)/shard_map/ppermute | solution.py:588
  61.1 15.5 %all-to-all-start.1 = ((bf16[32,16,256]{2,1,0:T(8,128)(2,1)}), bf16[32,16,256]{2,1,0:T(8,128)(2,1)S(1)}, u32[]{:S(2)}, u32[]{:S(2)}) async-start(bf16[32,16,256]{2,1,0:T(8,128)(2,1)} %get-tuple-element.35), calls=%async_computation.1 | async-start | bytes 524288 | tf_op jit(solution)/shard_map/all_to_all | solution.py:577
  67.4 43.2 %copy-start.5 = (f32[64]{0:T(128)S(1)}, f32[64]{0:T(128)}, u32[]{:S(2)}) copy-start(f32[64]{0:T(128)} %multiply_power_fusion) | copy-start | bytes 772
  68.2 5.9 %collective-permute-start.14 = (bf16[16,2048]{1,0:T(8,128)(2,1)S(1)}, bf16[16,2048]{1,0:T(8,128)(2,1)S(1)}, u32[]{:S(2)}, u32[]{:S(2)}) collective-permute-start(bf16[16,2048]{1,0:T(8,128)(2,1)S(1)} %get-tuple-element.44), channel_id=1, source_target_pairs={{3,0},{0,1},{1,2},{2,3},{7,4},{4,5},{5,6},{6,7},{11,8},{8,9},{9,10... | collective-permute-start | bytes 196616 | tf_op jit(solution)/shard_map/ppermute | solution.py:588
  70.1 4.3 %collective-permute-start.15 = (bf16[16,2048]{1,0:T(8,128)(2,1)S(1)}, bf16[16,2048]{1,0:T(8,128)(2,1)S(1)}, u32[]{:S(2)}, u32[]{:S(2)}) collective-permute-start(bf16[16,2048]{1,0:T(8,128)(2,1)S(1)} %get-tuple-element.45), channel_id=1, source_target_pairs={{1,0},{2,1},{3,2},{0,3},{5,4},{6,5},{7,6},{4,7},{9,8},{10,9},{11,1... | collective-permute-start | bytes 196616 | tf_op jit(solution)/shard_map/ppermute | solution.py:588
  80.3 19.1 %all-to-all-start.2 = ((bf16[32,16,256]{2,1,0:T(8,128)(2,1)}), bf16[32,16,256]{2,1,0:T(8,128)(2,1)S(1)}, u32[]{:S(2)}, u32[]{:S(2)}) async-start(bf16[32,16,256]{2,1,0:T(8,128)(2,1)} %get-tuple-element.46), calls=%async_computation.2 | async-start | bytes 524288 | tf_op jit(solution)/shard_map/all_to_all | solution.py:577
  86.4 9.0 %collective-permute-start.16 = (bf16[16,2048]{1,0:T(8,128)(2,1)S(1)}, bf16[16,2048]{1,0:T(8,128)(2,1)S(1)}, u32[]{:S(2)}, u32[]{:S(2)}) collective-permute-start(bf16[16,2048]{1,0:T(8,128)(2,1)S(1)} %get-tuple-element.48), channel_id=1, source_target_pairs={{7,0},{4,1},{5,2},{6,3},{3,4},{0,5},{1,6},{2,7},{15,8},{12,9},{13,... | collective-permute-start | bytes 196616 | tf_op jit(solution)/shard_map/ppermute | solution.py:588
  89.1 6.2 %collective-permute-start.17 = (bf16[16,2048]{1,0:T(8,128)(2,1)S(1)}, bf16[16,2048]{1,0:T(8,128)(2,1)S(1)}, u32[]{:S(2)}, u32[]{:S(2)}) collective-permute-start(bf16[16,2048]{1,0:T(8,128)(2,1)S(1)} %get-tuple-element.49), channel_id=1, source_target_pairs={{5,0},{6,1},{7,2},{4,3},{1,4},{2,5},{3,6},{0,7},{13,8},{14,9},{15,... | collective-permute-start | bytes 196616 | tf_op jit(solution)/shard_map/ppermute | solution.py:588
  90.6 5.8 %collective-permute-start.18 = (bf16[16,2048]{1,0:T(8,128)(2,1)S(1)}, bf16[16,2048]{1,0:T(8,128)(2,1)S(1)}, u32[]{:S(2)}, u32[]{:S(2)}) collective-permute-start(bf16[16,2048]{1,0:T(8,128)(2,1)S(1)} %get-tuple-element.50), channel_id=1, source_target_pairs={{2,0},{3,1},{0,2},{1,3},{6,4},{7,5},{4,6},{5,7},{10,8},{11,9},{8,1... | collective-permute-start | bytes 196616 | tf_op jit(solution)/shard_map/ppermute | solution.py:588
  92.7 6.7 %collective-permute-start.19 = (bf16[16,2048]{1,0:T(8,128)(2,1)S(1)}, bf16[16,2048]{1,0:T(8,128)(2,1)S(1)}, u32[]{:S(2)}, u32[]{:S(2)}) collective-permute-start(bf16[16,2048]{1,0:T(8,128)(2,1)S(1)} %get-tuple-element.51), channel_id=1, source_target_pairs={{6,0},{7,1},{4,2},{5,3},{2,4},{3,5},{0,6},{1,7},{14,8},{15,9},{12,... | collective-permute-start | bytes 196616 | tf_op jit(solution)/shard_map/ppermute | solution.py:588
  102.8 17.3 %all-to-all-start.3 = ((f32[32,16,256]{2,1,0:T(8,128)}), f32[32,16,256]{2,1,0:T(8,128)S(1)}, u32[]{:S(2)}, u32[]{:S(2)}) async-start(f32[32,16,256]{2,1,0:T(8,128)} %out_product.1), calls=%async_computation.3 | async-start | bytes 1048576 | tf_op jit(solution)/shard_map/all_to_all | solution.py:577
  (5 other events, 166.6 us)

commit v14 on v12

--- a/solution.py
+++ b/solution.py
@@ -628,7 +628,7 @@
     cont_tables = rope_tables(prefix_len + boundary + step)
     read = readout(value_head.reshape(COL_BLOCKS, D // COL_BLOCKS), w_out)
     parts, main_parts, before = project(norm_rows(main, cont, rms_gain[None, :]), w_qkv, bias)
-    mixed, main_kv = attend_main(prefix_len, bias, *main_tables, cache, main_parts, before)
+    mixed, main_kv = attend_main(prefix_len, bias, *main_tables, cache, main_parts, before + [read])
     mixed = exchange(mixed)
     cont_mixed = attend_cont(prefix_len, boundary, bias, *cont_tables, cache, main_kv, *parts)
     parts = exchange(out_product(mixed, read, w_out, parts[4:]))

time: 114 us -> 114 us (level)
  no operation moved by 1% of the time
where the time goes in v14:
time: 114 us
  starting transfers between devices  50.6 us (44%)
  Pallas kernels  25.5 us (22%)
  waiting for transfers between devices  21.6 us (19%)
  blocking collectives  12.2 us (11%)
  between operations  2.11 us (2%)
  local copies, waits for them, and re-layouts  1.18 us (1%)
    ppermute x14, starting transfers between devices, from_side(): return lax.ppermute(rows, 'tp', route)  23.1 us
    all_to_all x3, starting transfers between devices, exchange(): return lax.all_to_all(rows, 'tp', split_axis=0, concat_axis=0, tiled=True)  18.6 us
    ppermute x14, waiting for transfers between devices, from_side(): return lax.ppermute(rows, 'tp', route)  13 us
    all_to_all x1, blocking collectives, project(): lax.all_to_all(rows, 'tp', split_axis=0, concat_axis=0, tiled=True, axis_...  12.2 us
    ppermute x6, starting transfers between devices, from_along(): return lax.ppermute(rows, 'tp', route)  8.93 us
    pallas_call x2, Pallas kernels, block_product(): pl.pallas_call(functools.partial(product_kernel, tiles, counts, places),...  8.76 us
    all_to_all x3, waiting for transfers between devices, exchange(): return lax.all_to_all(rows, 'tp', split_axis=0, concat_axis=0, tiled=True)  8.58 us
    pallas_call x1, Pallas kernels, attend_main(): pl.pallas_call(attend_main_kernel, out_shape=(jax.ShapeDtypeStruct((32, 1...  3.69 us
  transfers between devices with their start and end apart: 23, of which 8 were waited for; matrix products, arithmetic and copies ran while one was open for 0% of the time, Pallas kernels for 14%

profile of v14, /device:TPU:0, one launch (start us, length us, event | category | flops | bytes accessed | tf_op | source)
XLA Modules:
  0.0 113.7 jit_solution(278787757866725159)
XLA Ops:
  2.0 12.2 %all_to_all.20.refs_0_ = bf16[4,16,2304]{2,1,0:T(8,128)(2,1)S(1)} all-to-all(bf16[4,16,2304]{2,1,0:T(8,128)(2,1)S(1)} %norm_rows.1), channel_id=1, replica_groups={{0,8,16,24},{1,9,17,25},{2,10,18,26},{3,11,19,27},{4,12,20,28},{5,13,21..., dimensions={0} | all-to-all | bytes 589824 | tf_op jit(solution)/shard_map/all_to_all | solution.py:601
  17.3 1.7 %collective-permute-start.6 = (bf16[4,16,2304]{2,1,0:T(8,128)(2,1)S(1)}, bf16[4,16,2304]{2,1,0:T(8,128)(2,1)S(1)}, u32[]{:S(2)}, u32[]{:S(2)}) collective-permute-start(bf16[4,16,2304]{2,1,0:T(8,128)(2,1)S(1)} %all_to_all.20.refs_0_), channel_id=1, source_target_pairs={{1,0},{2,1},{3,2},{0,3},{5,4},{6,5},{7,6},{4,7},{9,8},{10,9},{11,1... | collective-permute-start | bytes 884744 | tf_op jit(solution)/shard_map/ppermute | solution.py:587
  19.1 2.4 %collective-permute-done.refs_1_ = bf16[4,16,2304]{2,1,0:T(8,128)(2,1)S(1)} collective-permute-done((bf16[4,16,2304]{2,1,0:T(8,128)(2,1)S(1)}, bf16[4,16,2304]{2,1,0:T(8,128)(2,1)S(1)}, u32[]{:S(2)}, u32[]{:S(2)}) %collective-permute-start) | collective-permute-done | bytes 294944 | tf_op jit(solution)/shard_map/ppermute | solution.py:587
  21.5 2.8 %collective-permute-start.1 = (bf16[4,16,2304]{2,1,0:T(8,128)(2,1)S(1)}, bf16[4,16,2304]{2,1,0:T(8,128)(2,1)S(1)}, u32[]{:S(2)}, u32[]{:S(2)}) collective-permute-start(bf16[4,16,2304]{2,1,0:T(8,128)(2,1)S(1)} %collective-permute-done.refs_1_), channel_id=1, source_target_pairs={{1,0},{2,1},{3,2},{0,3},{5,4},{6,5},{7,6},{4,7},{9,8},{10,9},{11,1... | collective-permute-start | bytes 884744 | tf_op jit(solution)/shard_map/ppermute | solution.py:587
  26.6 3.9 %block_product.2 = (bf16[4,16,2048]{2,1,0:T(8,128)(2,1)S(1)}, bf16[4,16,2048]{2,1,0:T(8,128)(2,1)S(1)}, bf16[4,16,2048]{2,1,0:T(8,128)(2,1)S(1)}, bf16[4,16,2048...) custom-call(bf16[4,16,2304]{2,1,0:T(8,128)(2,1)S(1)} %all_to_all.20.refs_0_, ...), custom_call_target="tpu_custom_call" | custom-call | flops 1509949440 | bytes 12000000 | tf_op jit(solution)/shard_map/block_product/pallas_call | solution.py:198
  31.2 2.1 %collective-permute-start.8 = (bf16[4,16,2048]{2,1,0:T(8,128)(2,1)S(1)}, bf16[4,16,2048]{2,1,0:T(8,128)(2,1)S(1)}, u32[]{:S(2)}, u32[]{:S(2)}) collective-permute-start(bf16[4,16,2048]{2,1,0:T(8,128)(2,1)S(1)} %get-tuple-element.33), channel_id=1, source_target_pairs={{16,0},{17,1},{18,2},{19,3},{20,4},{21,5},{22,6},{23,7},{24,8},{25... | collective-permute-start | bytes 786440 | tf_op jit(solution)/shard_map/ppermute | solution.py:592
  35.7 1.7 %collective-permute-start.5 = (bf16[4,16,2304]{2,1,0:T(8,128)(2,1)S(1)}, bf16[4,16,2304]{2,1,0:T(8,128)(2,1)S(1)}, u32[]{:S(2)}, u32[]{:S(2)}) collective-permute-start(bf16[4,16,2304]{2,1,0:T(8,128)(2,1)S(1)} %collective-permute-done.1.refs_0_), channel_id=1, source_target_pairs={{1,0},{2,1},{3,2},{0,3},{5,4},{6,5},{7,6},{4,7},{9,8},{10,9},{11,1... | collective-permute-start | bytes 884744 | tf_op jit(solution)/shard_map/ppermute | solution.py:587
  37.5 4.7 %collective-permute-done.4.refs_2_ = bf16[4,16,2304]{2,1,0:T(8,128)(2,1)S(1)} collective-permute-done((bf16[4,16,2304]{2,1,0:T(8,128)(2,1)S(1)}, bf16[4,16,2304]{2,1,0:T(8,128)(2,1)S(1)}, u32[]{:S(2)}, u32[]{:S(2)}) %collective-permute-start.4) | collective-permute-done | bytes 294944 | tf_op jit(solution)/shard_map/ppermute | solution.py:587
  42.4 4.8 %block_product.3 = (bf16[4,16,2048]{2,1,0:T(8,128)(2,1)S(1)}, bf16[4,16,2048]{2,1,0:T(8,128)(2,1)}, bf16[4,16,2048]{2,1,0:T(8,128)(2,1)S(1)}, bf16[4,16,2048]{2,1,0:T(8,128)(2,1)S(1)}, bf16[32,16,256]{2,1,0:T(8,128)(2,1)}) custom-call(bf16[4,16,2304]{2,1,0:T(8,128)(2,1)S(1)} %collective-permute-done.1.refs_0_, ...), custom_call_target="tpu_custom_call" | custom-call | flops 1509949440 | bytes 12000000 | tf_op jit(solution)/shard_map/block_product/pallas_call | solution.py:198
  50.0 2.5 %collective-permute-start.12 = (bf16[4,16,2048]{2,1,0:T(8,128)(2,1)S(1)}, bf16[4,16,2048]{2,1,0:T(8,128)(2,1)S(1)}, u32[]{:S(2)}, u32[]{:S(2)}) collective-permute-start(bf16[4,16,2048]{2,1,0:T(8,128)(2,1)S(1)} %get-tuple-element.38), channel_id=1, source_target_pairs={{8,0},{9,1},{10,2},{11,3},{12,4},{13,5},{14,6},{15,7},{16,8},{17,9... | collective-permute-start | bytes 786440 | tf_op jit(solution)/shard_map/ppermute | solution.py:592
  53.9 6.5 %all-to-all-start.1 = ((bf16[32,16,256]{2,1,0:T(8,128)(2,1)}), bf16[32,16,256]{2,1,0:T(8,128)(2,1)S(1)}, u32[]{:S(2)}, u32[]{:S(2)}) async-start(bf16[32,16,256]{2,1,0:T(8,128)(2,1)} %get-tuple-element.35), calls=%async_computation.1 | async-start | bytes 524288 | tf_op jit(solution)/shard_map/all_to_all | solution.py:576
  60.5 1.9 %collective-permute-start.14 = (bf16[16,2048]{1,0:T(8,128)(2,1)}, bf16[16,2048]{1,0:T(8,128)(2,1)S(1)}, u32[]{:S(2)}, u32[]{:S(2)}) collective-permute-start(bf16[16,2048]{1,0:T(8,128)(2,1)} %get-tuple-element.44), channel_id=1, source_target_pairs={{3,0},{0,1},{1,2},{2,3},{7,4},{4,5},{5,6},{6,7},{11,8},{8,9},{9,10... | collective-permute-start | bytes 196616 | tf_op jit(solution)/shard_map/ppermute | solution.py:587
  63.9 3.4 %readout.1.refs_6_.read_ref = f32[1,2048]{1,0:T(1,128)S(1)} custom-call(f32[8,1024]{1,0:T(8,128)S(1)} %reshape.34.head_ref, bf16[1,2048,1024]{2,1,0:T(8,128)(2,1)} %w_hbm.3), custom_call_target="tpu_custom_call" | custom-call | flops 200000000 | bytes 5000000 | tf_op jit(solution)/shard_map/readout/pallas_call | solution.py:460
  67.3 2.3 %all-to-all-done.1.parts_ref = bf16[32,16,256]{2,1,0:T(8,128)(2,1)S(1)} async-done(((bf16[32,16,256]{2,1,0:T(8,128)(2,1)}), bf16[32,16,256]{2,1,0:T(8,128)(2,1)S(1)}, u32[]{:S(2)}, u32[]{:S(2)}) %all-to-all-start.1) | async-done | bytes 262176 | tf_op jit(solution)/shard_map/all_to_all | solution.py:576
  69.6 3.7 %attend_main.1 = (bf16[32,16,256]{2,1,0:T(8,128)(2,1)}, f32[8,2048]{1,0:T(8,128)S(1)}) custom-call(s32[1]{0:T(128)} %copy.12.len_ref, f32[1,10240]{1,0:T(1,128)S(1)} %bitcast.16, f32[8,128]{1,0:T(8,128)S(1)} %get-tuple-element.62.cos_ref, f32[8,128]{1,0:T(8,128)S(1)} %get-tuple-element.63.sin_ref, bf16[256,2048]{1,0:T(8,128)(2,1)S(1)} %bitcast.11, ...), custom_call_target="tpu_custom_call" | custom-call | flops 200000000 | bytes 6000000 | tf_op jit(solution)/shard_map/attend_main/pallas_call | solution.py:383
  73.3 5.3 %all-to-all-start.2 = ((bf16[32,16,256]{2,1,0:T(8,128)(2,1)}), bf16[32,16,256]{2,1,0:T(8,128)(2,1)S(1)}, u32[]{:S(2)}, u32[]{:S(2)}) async-start(bf16[32,16,256]{2,1,0:T(8,128)(2,1)} %get-tuple-element.46), calls=%async_computation.2 | async-start | bytes 524288 | tf_op jit(solution)/shard_map/all_to_all | solution.py:576
  78.9 2.8 %collective-permute-start.16 = (bf16[16,2048]{1,0:T(8,128)(2,1)S(1)}, bf16[16,2048]{1,0:T(8,128)(2,1)S(1)}, u32[]{:S(2)}, u32[]{:S(2)}) collective-permute-start(bf16[16,2048]{1,0:T(8,128)(2,1)S(1)} %get-tuple-element.48), channel_id=1, source_target_pairs={{7,0},{4,1},{5,2},{6,3},{3,4},{0,5},{1,6},{2,7},{15,8},{12,9},{13,... | collective-permute-start | bytes 196616 | tf_op jit(solution)/shard_map/ppermute | solution.py:587
  83.1 2.1 %collective-permute-start.18 = (bf16[16,2048]{1,0:T(8,128)(2,1)S(1)}, bf16[16,2048]{1,0:T(8,128)(2,1)S(1)}, u32[]{:S(2)}, u32[]{:S(2)}) collective-permute-start(bf16[16,2048]{1,0:T(8,128)(2,1)S(1)} %get-tuple-element.50), channel_id=1, source_target_pairs={{2,0},{3,1},{0,2},{1,3},{6,4},{7,5},{4,6},{5,7},{10,8},{11,9},{8,1... | collective-permute-start | bytes 196616 | tf_op jit(solution)/shard_map/ppermute | solution.py:587
  85.2 2.7 %collective-permute-start.19 = (bf16[16,2048]{1,0:T(8,128)(2,1)S(1)}, bf16[16,2048]{1,0:T(8,128)(2,1)S(1)}, u32[]{:S(2)}, u32[]{:S(2)}) collective-permute-start(bf16[16,2048]{1,0:T(8,128)(2,1)S(1)} %get-tuple-element.51), channel_id=1, source_target_pairs={{6,0},{7,1},{4,2},{5,3},{2,4},{3,5},{0,6},{1,7},{14,8},{15,9},{12,... | collective-permute-start | bytes 196616 | tf_op jit(solution)/shard_map/ppermute | solution.py:587
  88.9 3.0 %collective-permute-done.19.refs_3_.refs_7_ = bf16[16,2048]{1,0:T(8,128)(2,1)S(1)} collective-permute-done((bf16[16,2048]{1,0:T(8,128)(2,1)S(1)}, bf16[16,2048]{1,0:T(8,128)(2,1)S(1)}, u32[]{:S(2)}, u32[]{:S(2)}) %collective-permute-start.19) | collective-permute-done | bytes 65568 | tf_op jit(solution)/shard_map/ppermute | solution.py:587
  91.8 3.4 %out_product.1 = f32[32,16,256]{2,1,0:T(8,128)} custom-call(bf16[32,16,256]{2,1,0:T(8,128)(2,1)S(1)} %all-to-all-done.2.x_ref, f32[1,2048]{1,0:T(1,128)S(1)} %readout.1.refs_6_.read_ref, bf16[1,2048,1024]{2,1,0:T(8,128)(2,1)} %w_hbm.3, bf16[16,2048]{1,0:T(8,128)(2,1)S(1)} %collective-permute-done.16.refs_0_.refs_4_, ...), custom_call_target="tpu_custom_call" | custom-call | flops 300000000 | bytes 5000000 | tf_op jit(solution)/shard_map/out_product/pallas_call | solution.py:507
  95.2 6.8 %all-to-all-start.3 = ((f32[32,16,256]{2,1,0:T(8,128)}), f32[32,16,256]{2,1,0:T(8,128)S(1)}, u32[]{:S(2)}, u32[]{:S(2)}) async-start(f32[32,16,256]{2,1,0:T(8,128)} %out_product.1), calls=%async_computation.3 | async-start | bytes 1048576 | tf_op jit(solution)/shard_map/all_to_all | solution.py:576
  102.9 3.0 %attend_cont.1.mixed_ref = bf16[16,8192]{1,0:T(8,128)(2,1)S(1)} custom-call(s32[1]{0:T(128)} %copy.12.len_ref, s32[1]{0:T(128)S(6)} %copy.13.bound_ref, f32[1,10240]{1,0:T(1,128)S(1)} %bitcast.18, f32[16,128]{1,0:T(8,128)S(1)} %get-tuple-element.64.cos_ref, f32[16,128]{1,0:T(8,128)S(1)} %get-tuple-element.65.sin_ref, bf16[256,2048]{1,0:T(8,128)(2,1)S(1)} %bitcast.12, ...), custom_call_target="tpu_custom_call" | custom-call | flops 400000000 | bytes 8000000 | tf_op jit(solution)/shard_map/attend_cont/pallas_call | solution.py:429
  105.9 6.3 %all-to-all-done.3.parts_ref = f32[32,16,256]{2,1,0:T(8,128)S(1)} async-done(((f32[32,16,256]{2,1,0:T(8,128)}), f32[32,16,256]{2,1,0:T(8,128)S(1)}, u32[]{:S(2)}, u32[]{:S(2)}) %all-to-all-start.3) | async-done | bytes 524320 | tf_op jit(solution)/shard_map/all_to_all | solution.py:576
  (55 shorter events, 19.5 us)
Async XLA Ops:
  14.2 7.3 %collective-permute-start = (bf16[4,16,2304]{2,1,0:T(8,128)(2,1)S(1)}, bf16[4,16,2304]{2,1,0:T(8,128)(2,1)S(1)}, u32[]{:S(2)}, u32[]{:S(2)}) collective-permute-start(bf16[4,16,2304]{2,1,0:T(8,128)(2,1)S(1)} %all_to_all.20.refs_0_), channel_id=1, source_target_pairs={{4,0},{5,1},{6,2},{7,3},{0,4},{1,5},{2,6},{3,7},{12,8},{13,9},{14,... | collective-permute-start | bytes 884744 | tf_op jit(solution)/shard_map/ppermute | solution.py:587
  15.8 9.1 %collective-permute-start.3 = (bf16[4,16,2304]{2,1,0:T(8,128)(2,1)S(1)}, bf16[4,16,2304]{2,1,0:T(8,128)(2,1)S(1)}, u32[]{:S(2)}, u32[]{:S(2)}) collective-permute-start(bf16[4,16,2304]{2,1,0:T(8,128)(2,1)S(1)} %all_to_all.20.refs_0_), channel_id=1, source_target_pairs={{3,0},{0,1},{1,2},{2,3},{7,4},{4,5},{5,6},{6,7},{11,8},{8,9},{9,10... | collective-permute-start | bytes 884744 | tf_op jit(solution)/shard_map/ppermute | solution.py:587
  17.3 9.3 %collective-permute-start.6 = (bf16[4,16,2304]{2,1,0:T(8,128)(2,1)S(1)}, bf16[4,16,2304]{2,1,0:T(8,128)(2,1)S(1)}, u32[]{:S(2)}, u32[]{:S(2)}) collective-permute-start(bf16[4,16,2304]{2,1,0:T(8,128)(2,1)S(1)} %all_to_all.20.refs_0_), channel_id=1, source_target_pairs={{1,0},{2,1},{3,2},{0,3},{5,4},{6,5},{7,6},{4,7},{9,8},{10,9},{11,1... | collective-permute-start | bytes 884744 | tf_op jit(solution)/shard_map/ppermute | solution.py:587
  21.5 12.7 %collective-permute-start.1 = (bf16[4,16,2304]{2,1,0:T(8,128)(2,1)S(1)}, bf16[4,16,2304]{2,1,0:T(8,128)(2,1)S(1)}, u32[]{:S(2)}, u32[]{:S(2)}) collective-permute-start(bf16[4,16,2304]{2,1,0:T(8,128)(2,1)S(1)} %collective-permute-done.refs_1_), channel_id=1, source_target_pairs={{1,0},{2,1},{3,2},{0,3},{5,4},{6,5},{7,6},{4,7},{9,8},{10,9},{11,1... | collective-permute-start | bytes 884744 | tf_op jit(solution)/shard_map/ppermute | solution.py:587
  24.3 11.5 %collective-permute-start.2 = (bf16[4,16,2304]{2,1,0:T(8,128)(2,1)S(1)}, bf16[4,16,2304]{2,1,0:T(8,128)(2,1)S(1)}, u32[]{:S(2)}, u32[]{:S(2)}) collective-permute-start(bf16[4,16,2304]{2,1,0:T(8,128)(2,1)S(1)} %collective-permute-done.refs_1_), channel_id=1, source_target_pairs={{3,0},{0,1},{1,2},{2,3},{7,4},{4,5},{5,6},{6,7},{11,8},{8,9},{9,10... | collective-permute-start | bytes 884744 | tf_op jit(solution)/shard_map/ppermute | solution.py:587
  30.5 19.5 %collective-permute-start.7 = (bf16[4,16,2048]{2,1,0:T(8,128)(2,1)S(1)}, bf16[4,16,2048]{2,1,0:T(8,128)(2,1)S(1)}, u32[]{:S(2)}, u32[]{:S(2)}) collective-permute-start(bf16[4,16,2048]{2,1,0:T(8,128)(2,1)S(1)} %get-tuple-element.32), channel_id=1, source_target_pairs={{24,0},{25,1},{26,2},{27,3},{28,4},{29,5},{30,6},{31,7},{0,8},{1,9... | collective-permute-start | bytes 786440 | tf_op jit(solution)/shard_map/ppermute | solution.py:592
  31.2 21.4 %collective-permute-start.8 = (bf16[4,16,2048]{2,1,0:T(8,128)(2,1)S(1)}, bf16[4,16,2048]{2,1,0:T(8,128)(2,1)S(1)}, u32[]{:S(2)}, u32[]{:S(2)}) collective-permute-start(bf16[4,16,2048]{2,1,0:T(8,128)(2,1)S(1)} %get-tuple-element.33), channel_id=1, source_target_pairs={{16,0},{17,1},{18,2},{19,3},{20,4},{21,5},{22,6},{23,7},{24,8},{25... | collective-permute-start | bytes 786440 | tf_op jit(solution)/shard_map/ppermute | solution.py:592
  33.2 19.3 %collective-permute-start.9 = (bf16[4,16,2048]{2,1,0:T(8,128)(2,1)S(1)}, bf16[4,16,2048]{2,1,0:T(8,128)(2,1)S(1)}, u32[]{:S(2)}, u32[]{:S(2)}) collective-permute-start(bf16[4,16,2048]{2,1,0:T(8,128)(2,1)S(1)} %get-tuple-element.34), channel_id=1, source_target_pairs={{8,0},{9,1},{10,2},{11,3},{12,4},{13,5},{14,6},{15,7},{16,8},{17,9... | collective-permute-start | bytes 786440 | tf_op jit(solution)/shard_map/ppermute | solution.py:592
  34.2 7.9 %collective-permute-start.4 = (bf16[4,16,2304]{2,1,0:T(8,128)(2,1)S(1)}, bf16[4,16,2304]{2,1,0:T(8,128)(2,1)S(1)}, u32[]{:S(2)}, u32[]{:S(2)}) collective-permute-start(bf16[4,16,2304]{2,1,0:T(8,128)(2,1)S(1)} %collective-permute-done.3.refs_3_), channel_id=1, source_target_pairs={{3,0},{0,1},{1,2},{2,3},{7,4},{4,5},{5,6},{6,7},{11,8},{8,9},{9,10... | collective-permute-start | bytes 884744 | tf_op jit(solution)/shard_map/ppermute | solution.py:587
  35.7 6.7 %collective-permute-start.5 = (bf16[4,16,2304]{2,1,0:T(8,128)(2,1)S(1)}, bf16[4,16,2304]{2,1,0:T(8,128)(2,1)S(1)}, u32[]{:S(2)}, u32[]{:S(2)}) collective-permute-start(bf16[4,16,2304]{2,1,0:T(8,128)(2,1)S(1)} %collective-permute-done.1.refs_0_), channel_id=1, source_target_pairs={{1,0},{2,1},{3,2},{0,3},{5,4},{6,5},{7,6},{4,7},{9,8},{10,9},{11,1... | collective-permute-start | bytes 884744 | tf_op jit(solution)/shard_map/ppermute | solution.py:587
  47.3 22.3 %collective-permute-start.10 = (bf16[4,16,2048]{2,1,0:T(8,128)(2,1)}, bf16[4,16,2048]{2,1,0:T(8,128)(2,1)S(1)}, u32[]{:S(2)}, u32[]{:S(2)}) collective-permute-start(bf16[4,16,2048]{2,1,0:T(8,128)(2,1)} %get-tuple-element.36), channel_id=1, source_target_pairs={{24,0},{25,1},{26,2},{27,3},{28,4},{29,5},{30,6},{31,7},{0,8},{1,9... | collective-permute-start | bytes 786440 | tf_op jit(solution)/shard_map/ppermute | solution.py:592
  48.4 21.2 %collective-permute-start.11 = (bf16[4,16,2048]{2,1,0:T(8,128)(2,1)S(1)}, bf16[4,16,2048]{2,1,0:T(8,128)(2,1)S(1)}, u32[]{:S(2)}, u32[]{:S(2)}) collective-permute-start(bf16[4,16,2048]{2,1,0:T(8,128)(2,1)S(1)} %get-tuple-element.37), channel_id=1, source_target_pairs={{16,0},{17,1},{18,2},{19,3},{20,4},{21,5},{22,6},{23,7},{24,8},{25... | collective-permute-start | bytes 786440 | tf_op jit(solution)/shard_map/ppermute | solution.py:592
  50.0 19.6 %collective-permute-start.12 = (bf16[4,16,2048]{2,1,0:T(8,128)(2,1)S(1)}, bf16[4,16,2048]{2,1,0:T(8,128)(2,1)S(1)}, u32[]{:S(2)}, u32[]{:S(2)}) collective-permute-start(bf16[4,16,2048]{2,1,0:T(8,128)(2,1)S(1)} %get-tuple-element.38), channel_id=1, source_target_pairs={{8,0},{9,1},{10,2},{11,3},{12,4},{13,5},{14,6},{15,7},{16,8},{17,9... | collective-permute-start | bytes 786440 | tf_op jit(solution)/shard_map/ppermute | solution.py:592
  53.9 8.5 %collective-permute-start.13 = (bf16[16,2048]{1,0:T(8,128)(2,1)S(1)}, bf16[16,2048]{1,0:T(8,128)(2,1)S(1)}, u32[]{:S(2)}, u32[]{:S(2)}) collective-permute-start(bf16[16,2048]{1,0:T(8,128)(2,1)S(1)} %get-tuple-element.43), channel_id=1, source_target_pairs={{4,0},{5,1},{6,2},{7,3},{0,4},{1,5},{2,6},{3,7},{12,8},{13,9},{14,... | collective-permute-start | bytes 196616 | tf_op jit(solution)/shard_map/ppermute | solution.py:587
  53.9 15.8 %all-to-all-start.1 = ((bf16[32,16,256]{2,1,0:T(8,128)(2,1)}), bf16[32,16,256]{2,1,0:T(8,128)(2,1)S(1)}, u32[]{:S(2)}, u32[]{:S(2)}) async-start(bf16[32,16,256]{2,1,0:T(8,128)(2,1)} %get-tuple-element.35), calls=%async_computation.1 | async-start | bytes 524288 | tf_op jit(solution)/shard_map/all_to_all | solution.py:576
  60.5 6.8 %collective-permute-start.14 = (bf16[16,2048]{1,0:T(8,128)(2,1)}, bf16[16,2048]{1,0:T(8,128)(2,1)S(1)}, u32[]{:S(2)}, u32[]{:S(2)}) collective-permute-start(bf16[16,2048]{1,0:T(8,128)(2,1)} %get-tuple-element.44), channel_id=1, source_target_pairs={{3,0},{0,1},{1,2},{2,3},{7,4},{4,5},{5,6},{6,7},{11,8},{8,9},{9,10... | collective-permute-start | bytes 196616 | tf_op jit(solution)/shard_map/ppermute | solution.py:587
  62.3 5.0 %collective-permute-start.15 = (bf16[16,2048]{1,0:T(8,128)(2,1)}, bf16[16,2048]{1,0:T(8,128)(2,1)S(1)}, u32[]{:S(2)}, u32[]{:S(2)}) collective-permute-start(bf16[16,2048]{1,0:T(8,128)(2,1)} %copy-done.5), channel_id=1, source_target_pairs={{1,0},{2,1},{3,2},{0,3},{5,4},{6,5},{7,6},{4,7},{9,8},{10,9},{11,1... | collective-permute-start | bytes 196616 | tf_op jit(solution)/shard_map/ppermute | solution.py:587
  73.3 38.9 %copy-start.3 = (bf16[1,2,8192]{2,1,0:T(2,128)(2,1)S(1)}, bf16[1,2,8192]{2,1,0:T(2,128)(2,1)}, u32[]{:S(2)}) copy-start(bf16[1,2,8192]{2,1,0:T(2,128)(2,1)} %param.10) | copy-start | bytes 98308
  73.3 18.5 %all-to-all-start.2 = ((bf16[32,16,256]{2,1,0:T(8,128)(2,1)}), bf16[32,16,256]{2,1,0:T(8,128)(2,1)S(1)}, u32[]{:S(2)}, u32[]{:S(2)}) async-start(bf16[32,16,256]{2,1,0:T(8,128)(2,1)} %get-tuple-element.46), calls=%async_computation.2 | async-start | bytes 524288 | tf_op jit(solution)/shard_map/all_to_all | solution.py:576
  78.9 9.0 %collective-permute-start.16 = (bf16[16,2048]{1,0:T(8,128)(2,1)S(1)}, bf16[16,2048]{1,0:T(8,128)(2,1)S(1)}, u32[]{:S(2)}, u32[]{:S(2)}) collective-permute-start(bf16[16,2048]{1,0:T(8,128)(2,1)S(1)} %get-tuple-element.48), channel_id=1, source_target_pairs={{7,0},{4,1},{5,2},{6,3},{3,4},{0,5},{1,6},{2,7},{15,8},{12,9},{13,... | collective-permute-start | bytes 196616 | tf_op jit(solution)/shard_map/ppermute | solution.py:587
  81.6 6.2 %collective-permute-start.17 = (bf16[16,2048]{1,0:T(8,128)(2,1)S(1)}, bf16[16,2048]{1,0:T(8,128)(2,1)S(1)}, u32[]{:S(2)}, u32[]{:S(2)}) collective-permute-start(bf16[16,2048]{1,0:T(8,128)(2,1)S(1)} %get-tuple-element.49), channel_id=1, source_target_pairs={{5,0},{6,1},{7,2},{4,3},{1,4},{2,5},{3,6},{0,7},{13,8},{14,9},{15,... | collective-permute-start | bytes 196616 | tf_op jit(solution)/shard_map/ppermute | solution.py:587
  83.1 5.8 %collective-permute-start.18 = (bf16[16,2048]{1,0:T(8,128)(2,1)S(1)}, bf16[16,2048]{1,0:T(8,128)(2,1)S(1)}, u32[]{:S(2)}, u32[]{:S(2)}) collective-permute-start(bf16[16,2048]{1,0:T(8,128)(2,1)S(1)} %get-tuple-element.50), channel_id=1, source_target_pairs={{2,0},{3,1},{0,2},{1,3},{6,4},{7,5},{4,6},{5,7},{10,8},{11,9},{8,1... | collective-permute-start | bytes 196616 | tf_op jit(solution)/shard_map/ppermute | solution.py:587
  85.2 6.7 %collective-permute-start.19 = (bf16[16,2048]{1,0:T(8,128)(2,1)S(1)}, bf16[16,2048]{1,0:T(8,128)(2,1)S(1)}, u32[]{:S(2)}, u32[]{:S(2)}) collective-permute-start(bf16[16,2048]{1,0:T(8,128)(2,1)S(1)} %get-tuple-element.51), channel_id=1, source_target_pairs={{6,0},{7,1},{4,2},{5,3},{2,4},{3,5},{0,6},{1,7},{14,8},{15,9},{12,... | collective-permute-start | bytes 196616 | tf_op jit(solution)/shard_map/ppermute | solution.py:587
  95.2 17.0 %all-to-all-start.3 = ((f32[32,16,256]{2,1,0:T(8,128)}), f32[32,16,256]{2,1,0:T(8,128)S(1)}, u32[]{:S(2)}, u32[]{:S(2)}) async-start(f32[32,16,256]{2,1,0:T(8,128)} %out_product.1), calls=%async_computation.3 | async-start | bytes 1048576 | tf_op jit(solution)/shard_map/all_to_all | solution.py:576
  (5 other events, 127.7 us)

commit v15 on v14

--- a/solution.py
+++ b/solution.py
@@ -631,7 +631,7 @@
     mixed, main_kv = attend_main(prefix_len, bias, *main_tables, cache, main_parts, before + [read])
     mixed = exchange(mixed)
     cont_mixed = attend_cont(prefix_len, boundary, bias, *cont_tables, cache, main_kv, *parts)
-    parts = exchange(out_product(mixed, read, w_out, parts[4:]))
+    parts = exchange(out_product(mixed, read, w_out, parts[4:6]))
     main_out, score = finish(parts, main, cont, head, cont_mixed)
     return main_out[None], score[0, :1]
 

time: 114 us -> 113 us (level)
    all_to_all x3, waiting for transfers between devices: 8.58 us -> 3.18 us  [exchange(): return lax.all_to_all(rows, 'tp', split_axis=0, concat_axis=0, tiled=True)]
    ppermute x14, waiting for transfers between devices: 13 us -> 18.1 us  [from_side(): return lax.ppermute(rows, 'tp', route)]
  transfers between devices with their start and end apart: 23 -> 23, of which waited for: 8 -> 10; matrix products, arithmetic and copies ran while one was open for 0% -> 0% of each run, Pallas kernels for 14% -> 14%
where the time goes in v15:
time: 113 us
  starting transfers between devices  49.9 us (44%)
  Pallas kernels  25.5 us (23%)
  waiting for transfers between devices  21.3 us (19%)
  blocking collectives  12.2 us (11%)
  between operations  2.13 us (2%)
  local copies, waits for them, and re-layouts  1.18 us (1%)
    ppermute x14, starting transfers between devices, from_side(): return lax.ppermute(rows, 'tp', route)  23.2 us
    ppermute x14, waiting for transfers between devices, from_side(): return lax.ppermute(rows, 'tp', route)  18.1 us
    all_to_all x3, starting transfers between devices, exchange(): return lax.all_to_all(rows, 'tp', split_axis=0, concat_axis=0, tiled=True)  17.8 us
    all_to_all x1, blocking collectives, project(): lax.all_to_all(rows, 'tp', split_axis=0, concat_axis=0, tiled=True, axis_...  12.2 us
    ppermute x6, starting transfers between devices, from_along(): return lax.ppermute(rows, 'tp', route)  8.93 us
    pallas_call x2, Pallas kernels, block_product(): pl.pallas_call(functools.partial(product_kernel, tiles, counts, places),...  8.76 us
    pallas_call x1, Pallas kernels, attend_main(): pl.pallas_call(attend_main_kernel, out_shape=(jax.ShapeDtypeStruct((32, 1...  3.69 us
    pallas_call x1, Pallas kernels, readout(): pl.pallas_call(readout_kernel, out_shape=jax.ShapeDtypeStruct((1, FEATURE...  3.41 us
  transfers between devices with their start and end apart: 23, of which 10 were waited for; matrix products, arithmetic and copies ran while one was open for 0% of the time, Pallas kernels for 14%

profile of v15, /device:TPU:0, one launch (start us, length us, event | category | flops | bytes accessed | tf_op | source)
XLA Modules:
  0.0 112.7 jit_solution(8438148425416657409)
XLA Ops:
  2.0 12.2 %all_to_all.20.refs_0_ = bf16[4,16,2304]{2,1,0:T(8,128)(2,1)S(1)} all-to-all(bf16[4,16,2304]{2,1,0:T(8,128)(2,1)S(1)} %norm_rows.1), channel_id=1, replica_groups={{0,8,16,24},{1,9,17,25},{2,10,18,26},{3,11,19,27},{4,12,20,28},{5,13,21..., dimensions={0} | all-to-all | bytes 589824 | tf_op jit(solution)/shard_map/all_to_all | solution.py:601
  17.3 1.7 %collective-permute-start.6 = (bf16[4,16,2304]{2,1,0:T(8,128)(2,1)S(1)}, bf16[4,16,2304]{2,1,0:T(8,128)(2,1)S(1)}, u32[]{:S(2)}, u32[]{:S(2)}) collective-permute-start(bf16[4,16,2304]{2,1,0:T(8,128)(2,1)S(1)} %all_to_all.20.refs_0_), channel_id=1, source_target_pairs={{1,0},{2,1},{3,2},{0,3},{5,4},{6,5},{7,6},{4,7},{9,8},{10,9},{11,1... | collective-permute-start | bytes 884744 | tf_op jit(solution)/shard_map/ppermute | solution.py:587
  19.1 2.4 %collective-permute-done.refs_1_ = bf16[4,16,2304]{2,1,0:T(8,128)(2,1)S(1)} collective-permute-done((bf16[4,16,2304]{2,1,0:T(8,128)(2,1)S(1)}, bf16[4,16,2304]{2,1,0:T(8,128)(2,1)S(1)}, u32[]{:S(2)}, u32[]{:S(2)}) %collective-permute-start) | collective-permute-done | bytes 294944 | tf_op jit(solution)/shard_map/ppermute | solution.py:587
  21.5 2.8 %collective-permute-start.1 = (bf16[4,16,2304]{2,1,0:T(8,128)(2,1)S(1)}, bf16[4,16,2304]{2,1,0:T(8,128)(2,1)S(1)}, u32[]{:S(2)}, u32[]{:S(2)}) collective-permute-start(bf16[4,16,2304]{2,1,0:T(8,128)(2,1)S(1)} %collective-permute-done.refs_1_), channel_id=1, source_target_pairs={{1,0},{2,1},{3,2},{0,3},{5,4},{6,5},{7,6},{4,7},{9,8},{10,9},{11,1... | collective-permute-start | bytes 884744 | tf_op jit(solution)/shard_map/ppermute | solution.py:587
  26.6 3.9 %block_product.2 = (bf16[4,16,2048]{2,1,0:T(8,128)(2,1)S(1)}, bf16[4,16,2048]{2,1,0:T(8,128)(2,1)S(1)}, bf16[4,16,2048]{2,1,0:T(8,128)(2,1)S(1)}, bf16[4,16,2048...) custom-call(bf16[4,16,2304]{2,1,0:T(8,128)(2,1)S(1)} %all_to_all.20.refs_0_, ...), custom_call_target="tpu_custom_call" | custom-call | flops 1509949440 | bytes 12000000 | tf_op jit(solution)/shard_map/block_product/pallas_call | solution.py:198
  31.2 2.1 %collective-permute-start.8 = (bf16[4,16,2048]{2,1,0:T(8,128)(2,1)S(1)}, bf16[4,16,2048]{2,1,0:T(8,128)(2,1)S(1)}, u32[]{:S(2)}, u32[]{:S(2)}) collective-permute-start(bf16[4,16,2048]{2,1,0:T(8,128)(2,1)S(1)} %get-tuple-element.33), channel_id=1, source_target_pairs={{16,0},{17,1},{18,2},{19,3},{20,4},{21,5},{22,6},{23,7},{24,8},{25... | collective-permute-start | bytes 786440 | tf_op jit(solution)/shard_map/ppermute | solution.py:592
  35.7 1.7 %collective-permute-start.5 = (bf16[4,16,2304]{2,1,0:T(8,128)(2,1)S(1)}, bf16[4,16,2304]{2,1,0:T(8,128)(2,1)S(1)}, u32[]{:S(2)}, u32[]{:S(2)}) collective-permute-start(bf16[4,16,2304]{2,1,0:T(8,128)(2,1)S(1)} %collective-permute-done.1.refs_0_), channel_id=1, source_target_pairs={{1,0},{2,1},{3,2},{0,3},{5,4},{6,5},{7,6},{4,7},{9,8},{10,9},{11,1... | collective-permute-start | bytes 884744 | tf_op jit(solution)/shard_map/ppermute | solution.py:587
  37.5 4.7 %collective-permute-done.4.refs_2_ = bf16[4,16,2304]{2,1,0:T(8,128)(2,1)S(1)} collective-permute-done((bf16[4,16,2304]{2,1,0:T(8,128)(2,1)S(1)}, bf16[4,16,2304]{2,1,0:T(8,128)(2,1)S(1)}, u32[]{:S(2)}, u32[]{:S(2)}) %collective-permute-start.4) | collective-permute-done | bytes 294944 | tf_op jit(solution)/shard_map/ppermute | solution.py:587
  42.4 4.8 %block_product.3 = (bf16[4,16,2048]{2,1,0:T(8,128)(2,1)S(1)}, bf16[4,16,2048]{2,1,0:T(8,128)(2,1)}, bf16[4,16,2048]{2,1,0:T(8,128)(2,1)S(1)}, bf16[4,16,2048]{2,1,0:T(8,128)(2,1)S(1)}, bf16[32,16,256]{2,1,0:T(8,128)(2,1)}) custom-call(bf16[4,16,2304]{2,1,0:T(8,128)(2,1)S(1)} %collective-permute-done.1.refs_0_, ...), custom_call_target="tpu_custom_call" | custom-call | flops 1509949440 | bytes 12000000 | tf_op jit(solution)/shard_map/block_product/pallas_call | solution.py:198
  50.0 2.5 %collective-permute-start.12 = (bf16[4,16,2048]{2,1,0:T(8,128)(2,1)S(1)}, bf16[4,16,2048]{2,1,0:T(8,128)(2,1)S(1)}, u32[]{:S(2)}, u32[]{:S(2)}) collective-permute-start(bf16[4,16,2048]{2,1,0:T(8,128)(2,1)S(1)} %get-tuple-element.38), channel_id=1, source_target_pairs={{8,0},{9,1},{10,2},{11,3},{12,4},{13,5},{14,6},{15,7},{16,8},{17,9... | collective-permute-start | bytes 786440 | tf_op jit(solution)/shard_map/ppermute | solution.py:592
  53.9 6.5 %all-to-all-start.1 = ((bf16[32,16,256]{2,1,0:T(8,128)(2,1)}), bf16[32,16,256]{2,1,0:T(8,128)(2,1)S(1)}, u32[]{:S(2)}, u32[]{:S(2)}) async-start(bf16[32,16,256]{2,1,0:T(8,128)(2,1)} %get-tuple-element.35), calls=%async_computation.1 | async-start | bytes 524288 | tf_op jit(solution)/shard_map/all_to_all | solution.py:576
  60.5 1.9 %collective-permute-start.14 = (bf16[16,2048]{1,0:T(8,128)(2,1)}, bf16[16,2048]{1,0:T(8,128)(2,1)S(1)}, u32[]{:S(2)}, u32[]{:S(2)}) collective-permute-start(bf16[16,2048]{1,0:T(8,128)(2,1)} %get-tuple-element.44), channel_id=1, source_target_pairs={{3,0},{0,1},{1,2},{2,3},{7,4},{4,5},{5,6},{6,7},{11,8},{8,9},{9,10... | collective-permute-start | bytes 196616 | tf_op jit(solution)/shard_map/ppermute | solution.py:587
  63.9 3.4 %readout.1.refs_6_.read_ref = f32[1,2048]{1,0:T(1,128)S(1)} custom-call(f32[8,1024]{1,0:T(8,128)S(1)} %reshape.34.head_ref, bf16[1,2048,1024]{2,1,0:T(8,128)(2,1)} %w_hbm.3), custom_call_target="tpu_custom_call" | custom-call | flops 200000000 | bytes 5000000 | tf_op jit(solution)/shard_map/readout/pallas_call | solution.py:460
  67.3 2.3 %all-to-all-done.1.parts_ref = bf16[32,16,256]{2,1,0:T(8,128)(2,1)S(1)} async-done(((bf16[32,16,256]{2,1,0:T(8,128)(2,1)}), bf16[32,16,256]{2,1,0:T(8,128)(2,1)S(1)}, u32[]{:S(2)}, u32[]{:S(2)}) %all-to-all-start.1) | async-done | bytes 262176 | tf_op jit(solution)/shard_map/all_to_all | solution.py:576
  69.6 3.7 %attend_main.1 = (bf16[32,16,256]{2,1,0:T(8,128)(2,1)}, f32[8,2048]{1,0:T(8,128)S(1)}) custom-call(s32[1]{0:T(128)} %copy.12.len_ref, f32[1,10240]{1,0:T(1,128)S(1)} %bitcast.16, f32[8,128]{1,0:T(8,128)S(1)} %get-tuple-element.62.cos_ref, f32[8,128]{1,0:T(8,128)S(1)} %get-tuple-element.63.sin_ref, bf16[256,2048]{1,0:T(8,128)(2,1)S(1)} %bitcast.11, ...), custom_call_target="tpu_custom_call" | custom-call | flops 200000000 | bytes 6000000 | tf_op jit(solution)/shard_map/attend_main/pallas_call | solution.py:383
  73.3 5.3 %all-to-all-start.2 = ((bf16[32,16,256]{2,1,0:T(8,128)(2,1)}), bf16[32,16,256]{2,1,0:T(8,128)(2,1)S(1)}, u32[]{:S(2)}, u32[]{:S(2)}) async-start(bf16[32,16,256]{2,1,0:T(8,128)(2,1)} %get-tuple-element.46), calls=%async_computation.2 | async-start | bytes 524288 | tf_op jit(solution)/shard_map/all_to_all | solution.py:576
  78.9 2.8 %collective-permute-start.16 = (bf16[16,2048]{1,0:T(8,128)(2,1)S(1)}, bf16[16,2048]{1,0:T(8,128)(2,1)S(1)}, u32[]{:S(2)}, u32[]{:S(2)}) collective-permute-start(bf16[16,2048]{1,0:T(8,128)(2,1)S(1)} %get-tuple-element.48), channel_id=1, source_target_pairs={{7,0},{4,1},{5,2},{6,3},{3,4},{0,5},{1,6},{2,7},{15,8},{12,9},{13,... | collective-permute-start | bytes 196616 | tf_op jit(solution)/shard_map/ppermute | solution.py:587
  83.1 3.4 %collective-permute-done.16.refs_0_.refs_4_ = bf16[16,2048]{1,0:T(8,128)(2,1)S(1)} collective-permute-done((bf16[16,2048]{1,0:T(8,128)(2,1)S(1)}, bf16[16,2048]{1,0:T(8,128)(2,1)S(1)}, u32[]{:S(2)}, u32[]{:S(2)}) %collective-permute-start.16) | collective-permute-done | bytes 65568 | tf_op jit(solution)/shard_map/ppermute | solution.py:587
  87.9 3.4 %out_product.1 = f32[32,16,256]{2,1,0:T(8,128)} custom-call(bf16[32,16,256]{2,1,0:T(8,128)(2,1)S(1)} %all-to-all-done.2.x_ref, f32[1,2048]{1,0:T(1,128)S(1)} %readout.1.refs_6_.read_ref, bf16[1,2048,1024]{2,1,0:T(8,128)(2,1)} %w_hbm.3, bf16[16,2048]{1,0:T(8,128)(2,1)S(1)} %collective-permute-done.16.refs_0_.refs_4_, ...), custom_call_target="tpu_custom_call" | custom-call | flops 300000000 | bytes 5000000 | tf_op jit(solution)/shard_map/out_product/pallas_call | solution.py:507
  91.3 6.0 %all-to-all-start.3 = ((f32[32,16,256]{2,1,0:T(8,128)}), f32[32,16,256]{2,1,0:T(8,128)S(1)}, u32[]{:S(2)}, u32[]{:S(2)}) async-start(f32[32,16,256]{2,1,0:T(8,128)} %out_product.1), calls=%async_computation.3 | async-start | bytes 1048576 | tf_op jit(solution)/shard_map/all_to_all | solution.py:576
  98.1 3.4 %collective-permute-start.18 = (bf16[16,2048]{1,0:T(8,128)(2,1)S(1)}, bf16[16,2048]{1,0:T(8,128)(2,1)S(1)}, u32[]{:S(2)}, u32[]{:S(2)}) collective-permute-start(bf16[16,2048]{1,0:T(8,128)(2,1)S(1)} %get-tuple-element.52), channel_id=1, source_target_pairs={{2,0},{3,1},{0,2},{1,3},{6,4},{7,5},{4,6},{5,7},{10,8},{11,9},{8,1... | collective-permute-start | bytes 196616 | tf_op jit(solution)/shard_map/ppermute | solution.py:587
  103.0 2.7 %collective-permute-done.18.refs_6_ = bf16[16,2048]{1,0:T(8,128)(2,1)S(1)} collective-permute-done((bf16[16,2048]{1,0:T(8,128)(2,1)S(1)}, bf16[16,2048]{1,0:T(8,128)(2,1)S(1)}, u32[]{:S(2)}, u32[]{:S(2)}) %collective-permute-start.18) | collective-permute-done | bytes 65568 | tf_op jit(solution)/shard_map/ppermute | solution.py:587
  105.7 2.4 %collective-permute-done.19.refs_7_ = bf16[16,2048]{1,0:T(8,128)(2,1)S(1)} collective-permute-done((bf16[16,2048]{1,0:T(8,128)(2,1)S(1)}, bf16[16,2048]{1,0:T(8,128)(2,1)S(1)}, u32[]{:S(2)}, u32[]{:S(2)}) %collective-permute-start.19) | collective-permute-done | bytes 65568 | tf_op jit(solution)/shard_map/ppermute | solution.py:587
  108.1 3.0 %attend_cont.1.mixed_ref = bf16[16,8192]{1,0:T(8,128)(2,1)S(1)} custom-call(s32[1]{0:T(128)} %copy.12.len_ref, s32[1]{0:T(128)S(6)} %copy.13.bound_ref, f32[1,10240]{1,0:T(1,128)S(1)} %bitcast.18, f32[16,128]{1,0:T(8,128)S(1)} %get-tuple-element.64.cos_ref, f32[16,128]{1,0:T(8,128)S(1)} %get-tuple-element.65.sin_ref, bf16[256,2048]{1,0:T(8,128)(2,1)S(1)} %bitcast.12, ...), custom_call_target="tpu_custom_call" | custom-call | flops 400000000 | bytes 8000000 | tf_op jit(solution)/shard_map/attend_cont/pallas_call | solution.py:429
  (55 shorter events, 21.4 us)
Async XLA Ops:
  14.2 7.3 %collective-permute-start = (bf16[4,16,2304]{2,1,0:T(8,128)(2,1)S(1)}, bf16[4,16,2304]{2,1,0:T(8,128)(2,1)S(1)}, u32[]{:S(2)}, u32[]{:S(2)}) collective-permute-start(bf16[4,16,2304]{2,1,0:T(8,128)(2,1)S(1)} %all_to_all.20.refs_0_), channel_id=1, source_target_pairs={{4,0},{5,1},{6,2},{7,3},{0,4},{1,5},{2,6},{3,7},{12,8},{13,9},{14,... | collective-permute-start | bytes 884744 | tf_op jit(solution)/shard_map/ppermute | solution.py:587
  15.8 9.1 %collective-permute-start.3 = (bf16[4,16,2304]{2,1,0:T(8,128)(2,1)S(1)}, bf16[4,16,2304]{2,1,0:T(8,128)(2,1)S(1)}, u32[]{:S(2)}, u32[]{:S(2)}) collective-permute-start(bf16[4,16,2304]{2,1,0:T(8,128)(2,1)S(1)} %all_to_all.20.refs_0_), channel_id=1, source_target_pairs={{3,0},{0,1},{1,2},{2,3},{7,4},{4,5},{5,6},{6,7},{11,8},{8,9},{9,10... | collective-permute-start | bytes 884744 | tf_op jit(solution)/shard_map/ppermute | solution.py:587
  17.3 9.3 %collective-permute-start.6 = (bf16[4,16,2304]{2,1,0:T(8,128)(2,1)S(1)}, bf16[4,16,2304]{2,1,0:T(8,128)(2,1)S(1)}, u32[]{:S(2)}, u32[]{:S(2)}) collective-permute-start(bf16[4,16,2304]{2,1,0:T(8,128)(2,1)S(1)} %all_to_all.20.refs_0_), channel_id=1, source_target_pairs={{1,0},{2,1},{3,2},{0,3},{5,4},{6,5},{7,6},{4,7},{9,8},{10,9},{11,1... | collective-permute-start | bytes 884744 | tf_op jit(solution)/shard_map/ppermute | solution.py:587
  21.5 12.7 %collective-permute-start.1 = (bf16[4,16,2304]{2,1,0:T(8,128)(2,1)S(1)}, bf16[4,16,2304]{2,1,0:T(8,128)(2,1)S(1)}, u32[]{:S(2)}, u32[]{:S(2)}) collective-permute-start(bf16[4,16,2304]{2,1,0:T(8,128)(2,1)S(1)} %collective-permute-done.refs_1_), channel_id=1, source_target_pairs={{1,0},{2,1},{3,2},{0,3},{5,4},{6,5},{7,6},{4,7},{9,8},{10,9},{11,1... | collective-permute-start | bytes 884744 | tf_op jit(solution)/shard_map/ppermute | solution.py:587
  24.3 11.5 %collective-permute-start.2 = (bf16[4,16,2304]{2,1,0:T(8,128)(2,1)S(1)}, bf16[4,16,2304]{2,1,0:T(8,128)(2,1)S(1)}, u32[]{:S(2)}, u32[]{:S(2)}) collective-permute-start(bf16[4,16,2304]{2,1,0:T(8,128)(2,1)S(1)} %collective-permute-done.refs_1_), channel_id=1, source_target_pairs={{3,0},{0,1},{1,2},{2,3},{7,4},{4,5},{5,6},{6,7},{11,8},{8,9},{9,10... | collective-permute-start | bytes 884744 | tf_op jit(solution)/shard_map/ppermute | solution.py:587
  30.5 19.5 %collective-permute-start.7 = (bf16[4,16,2048]{2,1,0:T(8,128)(2,1)S(1)}, bf16[4,16,2048]{2,1,0:T(8,128)(2,1)S(1)}, u32[]{:S(2)}, u32[]{:S(2)}) collective-permute-start(bf16[4,16,2048]{2,1,0:T(8,128)(2,1)S(1)} %get-tuple-element.32), channel_id=1, source_target_pairs={{24,0},{25,1},{26,2},{27,3},{28,4},{29,5},{30,6},{31,7},{0,8},{1,9... | collective-permute-start | bytes 786440 | tf_op jit(solution)/shard_map/ppermute | solution.py:592
  31.2 21.4 %collective-permute-start.8 = (bf16[4,16,2048]{2,1,0:T(8,128)(2,1)S(1)}, bf16[4,16,2048]{2,1,0:T(8,128)(2,1)S(1)}, u32[]{:S(2)}, u32[]{:S(2)}) collective-permute-start(bf16[4,16,2048]{2,1,0:T(8,128)(2,1)S(1)} %get-tuple-element.33), channel_id=1, source_target_pairs={{16,0},{17,1},{18,2},{19,3},{20,4},{21,5},{22,6},{23,7},{24,8},{25... | collective-permute-start | bytes 786440 | tf_op jit(solution)/shard_map/ppermute | solution.py:592
  33.2 19.3 %collective-permute-start.9 = (bf16[4,16,2048]{2,1,0:T(8,128)(2,1)S(1)}, bf16[4,16,2048]{2,1,0:T(8,128)(2,1)S(1)}, u32[]{:S(2)}, u32[]{:S(2)}) collective-permute-start(bf16[4,16,2048]{2,1,0:T(8,128)(2,1)S(1)} %get-tuple-element.34), channel_id=1, source_target_pairs={{8,0},{9,1},{10,2},{11,3},{12,4},{13,5},{14,6},{15,7},{16,8},{17,9... | collective-permute-start | bytes 786440 | tf_op jit(solution)/shard_map/ppermute | solution.py:592
  34.2 7.9 %collective-permute-start.4 = (bf16[4,16,2304]{2,1,0:T(8,128)(2,1)S(1)}, bf16[4,16,2304]{2,1,0:T(8,128)(2,1)S(1)}, u32[]{:S(2)}, u32[]{:S(2)}) collective-permute-start(bf16[4,16,2304]{2,1,0:T(8,128)(2,1)S(1)} %collective-permute-done.3.refs_3_), channel_id=1, source_target_pairs={{3,0},{0,1},{1,2},{2,3},{7,4},{4,5},{5,6},{6,7},{11,8},{8,9},{9,10... | collective-permute-start | bytes 884744 | tf_op jit(solution)/shard_map/ppermute | solution.py:587
  35.7 6.7 %collective-permute-start.5 = (bf16[4,16,2304]{2,1,0:T(8,128)(2,1)S(1)}, bf16[4,16,2304]{2,1,0:T(8,128)(2,1)S(1)}, u32[]{:S(2)}, u32[]{:S(2)}) collective-permute-start(bf16[4,16,2304]{2,1,0:T(8,128)(2,1)S(1)} %collective-permute-done.1.refs_0_), channel_id=1, source_target_pairs={{1,0},{2,1},{3,2},{0,3},{5,4},{6,5},{7,6},{4,7},{9,8},{10,9},{11,1... | collective-permute-start | bytes 884744 | tf_op jit(solution)/shard_map/ppermute | solution.py:587
  47.3 22.3 %collective-permute-start.10 = (bf16[4,16,2048]{2,1,0:T(8,128)(2,1)}, bf16[4,16,2048]{2,1,0:T(8,128)(2,1)S(1)}, u32[]{:S(2)}, u32[]{:S(2)}) collective-permute-start(bf16[4,16,2048]{2,1,0:T(8,128)(2,1)} %get-tuple-element.36), channel_id=1, source_target_pairs={{24,0},{25,1},{26,2},{27,3},{28,4},{29,5},{30,6},{31,7},{0,8},{1,9... | collective-permute-start | bytes 786440 | tf_op jit(solution)/shard_map/ppermute | solution.py:592
  48.4 21.2 %collective-permute-start.11 = (bf16[4,16,2048]{2,1,0:T(8,128)(2,1)S(1)}, bf16[4,16,2048]{2,1,0:T(8,128)(2,1)S(1)}, u32[]{:S(2)}, u32[]{:S(2)}) collective-permute-start(bf16[4,16,2048]{2,1,0:T(8,128)(2,1)S(1)} %get-tuple-element.37), channel_id=1, source_target_pairs={{16,0},{17,1},{18,2},{19,3},{20,4},{21,5},{22,6},{23,7},{24,8},{25... | collective-permute-start | bytes 786440 | tf_op jit(solution)/shard_map/ppermute | solution.py:592
  50.0 19.6 %collective-permute-start.12 = (bf16[4,16,2048]{2,1,0:T(8,128)(2,1)S(1)}, bf16[4,16,2048]{2,1,0:T(8,128)(2,1)S(1)}, u32[]{:S(2)}, u32[]{:S(2)}) collective-permute-start(bf16[4,16,2048]{2,1,0:T(8,128)(2,1)S(1)} %get-tuple-element.38), channel_id=1, source_target_pairs={{8,0},{9,1},{10,2},{11,3},{12,4},{13,5},{14,6},{15,7},{16,8},{17,9... | collective-permute-start | bytes 786440 | tf_op jit(solution)/shard_map/ppermute | solution.py:592
  53.9 8.5 %collective-permute-start.13 = (bf16[16,2048]{1,0:T(8,128)(2,1)S(1)}, bf16[16,2048]{1,0:T(8,128)(2,1)S(1)}, u32[]{:S(2)}, u32[]{:S(2)}) collective-permute-start(bf16[16,2048]{1,0:T(8,128)(2,1)S(1)} %get-tuple-element.43), channel_id=1, source_target_pairs={{4,0},{5,1},{6,2},{7,3},{0,4},{1,5},{2,6},{3,7},{12,8},{13,9},{14,... | collective-permute-start | bytes 196616 | tf_op jit(solution)/shard_map/ppermute | solution.py:587
  53.9 15.8 %all-to-all-start.1 = ((bf16[32,16,256]{2,1,0:T(8,128)(2,1)}), bf16[32,16,256]{2,1,0:T(8,128)(2,1)S(1)}, u32[]{:S(2)}, u32[]{:S(2)}) async-start(bf16[32,16,256]{2,1,0:T(8,128)(2,1)} %get-tuple-element.35), calls=%async_computation.1 | async-start | bytes 524288 | tf_op jit(solution)/shard_map/all_to_all | solution.py:576
  60.5 6.8 %collective-permute-start.14 = (bf16[16,2048]{1,0:T(8,128)(2,1)}, bf16[16,2048]{1,0:T(8,128)(2,1)S(1)}, u32[]{:S(2)}, u32[]{:S(2)}) collective-permute-start(bf16[16,2048]{1,0:T(8,128)(2,1)} %get-tuple-element.44), channel_id=1, source_target_pairs={{3,0},{0,1},{1,2},{2,3},{7,4},{4,5},{5,6},{6,7},{11,8},{8,9},{9,10... | collective-permute-start | bytes 196616 | tf_op jit(solution)/shard_map/ppermute | solution.py:587
  62.3 5.0 %collective-permute-start.15 = (bf16[16,2048]{1,0:T(8,128)(2,1)}, bf16[16,2048]{1,0:T(8,128)(2,1)S(1)}, u32[]{:S(2)}, u32[]{:S(2)}) collective-permute-start(bf16[16,2048]{1,0:T(8,128)(2,1)} %copy-done.5), channel_id=1, source_target_pairs={{1,0},{2,1},{3,2},{0,3},{5,4},{6,5},{7,6},{4,7},{9,8},{10,9},{11,1... | collective-permute-start | bytes 196616 | tf_op jit(solution)/shard_map/ppermute | solution.py:587
  73.3 37.8 %copy-start.3 = (bf16[1,2,8192]{2,1,0:T(2,128)(2,1)S(1)}, bf16[1,2,8192]{2,1,0:T(2,128)(2,1)}, u32[]{:S(2)}) copy-start(bf16[1,2,8192]{2,1,0:T(2,128)(2,1)} %param.10) | copy-start | bytes 98308
  73.3 14.6 %all-to-all-start.2 = ((bf16[32,16,256]{2,1,0:T(8,128)(2,1)}), bf16[32,16,256]{2,1,0:T(8,128)(2,1)S(1)}, u32[]{:S(2)}, u32[]{:S(2)}) async-start(bf16[32,16,256]{2,1,0:T(8,128)(2,1)} %get-tuple-element.46), calls=%async_computation.2 | async-start | bytes 524288 | tf_op jit(solution)/shard_map/all_to_all | solution.py:576
  78.9 7.7 %collective-permute-start.16 = (bf16[16,2048]{1,0:T(8,128)(2,1)S(1)}, bf16[16,2048]{1,0:T(8,128)(2,1)S(1)}, u32[]{:S(2)}, u32[]{:S(2)}) collective-permute-start(bf16[16,2048]{1,0:T(8,128)(2,1)S(1)} %get-tuple-element.48), channel_id=1, source_target_pairs={{7,0},{4,1},{5,2},{6,3},{3,4},{0,5},{1,6},{2,7},{15,8},{12,9},{13,... | collective-permute-start | bytes 196616 | tf_op jit(solution)/shard_map/ppermute | solution.py:587
  81.6 5.4 %collective-permute-start.17 = (bf16[16,2048]{1,0:T(8,128)(2,1)S(1)}, bf16[16,2048]{1,0:T(8,128)(2,1)S(1)}, u32[]{:S(2)}, u32[]{:S(2)}) collective-permute-start(bf16[16,2048]{1,0:T(8,128)(2,1)S(1)} %get-tuple-element.49), channel_id=1, source_target_pairs={{5,0},{6,1},{7,2},{4,3},{1,4},{2,5},{3,6},{0,7},{13,8},{14,9},{15,... | collective-permute-start | bytes 196616 | tf_op jit(solution)/shard_map/ppermute | solution.py:587
  91.3 19.9 %all-to-all-start.3 = ((f32[32,16,256]{2,1,0:T(8,128)}), f32[32,16,256]{2,1,0:T(8,128)S(1)}, u32[]{:S(2)}, u32[]{:S(2)}) async-start(f32[32,16,256]{2,1,0:T(8,128)} %out_product.1), calls=%async_computation.3 | async-start | bytes 1048576 | tf_op jit(solution)/shard_map/all_to_all | solution.py:576
  98.1 7.7 %collective-permute-start.18 = (bf16[16,2048]{1,0:T(8,128)(2,1)S(1)}, bf16[16,2048]{1,0:T(8,128)(2,1)S(1)}, u32[]{:S(2)}, u32[]{:S(2)}) collective-permute-start(bf16[16,2048]{1,0:T(8,128)(2,1)S(1)} %get-tuple-element.52), channel_id=1, source_target_pairs={{2,0},{3,1},{0,2},{1,3},{6,4},{7,5},{4,6},{5,7},{10,8},{11,9},{8,1... | collective-permute-start | bytes 196616 | tf_op jit(solution)/shard_map/ppermute | solution.py:587
  101.4 6.7 %collective-permute-start.19 = (bf16[16,2048]{1,0:T(8,128)(2,1)S(1)}, bf16[16,2048]{1,0:T(8,128)(2,1)S(1)}, u32[]{:S(2)}, u32[]{:S(2)}) collective-permute-start(bf16[16,2048]{1,0:T(8,128)(2,1)S(1)} %get-tuple-element.53), channel_id=1, source_target_pairs={{6,0},{7,1},{4,2},{5,3},{2,4},{3,5},{0,6},{1,7},{14,8},{15,9},{12,... | collective-permute-start | bytes 196616 | tf_op jit(solution)/shard_map/ppermute | solution.py:587
  (5 other events, 126.6 us)

commit v16 on v15

--- a/solution.py
+++ b/solution.py
@@ -95,17 +95,17 @@
     )(in_hbm(main), in_hbm(cont), in_hbm(gain))
 
 
-def weight_tile(n, tiles, w_hbm, w_ref, sems):
-    def copy(i):
-        lanes = pl.ds(pl.multiple_of(i * TILE, TILE), TILE)
-        return pltpu.make_async_copy(w_hbm.at[0, :, lanes], w_ref.at[i], sems.at[i])
-
-    @pl.when(n == 0)
-    def _():
-        for i in range(tiles):
-            copy(i).start()
-
-    return copy(n)
+def weight_copies(pieces, w_hbm, w_ref, sems):
+    copies = []
+    for i, (start, width) in enumerate(pieces):
+        lanes = slice(start, start + width)
+        copies.append(pltpu.make_async_copy(w_hbm.at[0, :, lanes], w_ref.at[:, lanes], sems.at[i]))
+        copies[-1].start()
+    return copies
+
+
+QKV_PIECES = ((0, 512), (512, 768))
+OUT_PIECES = ((0, 512), (512, 512))
 
 
 REST = 768
@@ -126,68 +126,69 @@
         earlier_ref, refs = refs[0], refs[1:]
     w_hbm, *out_refs = refs[: 1 + ROW_BLOCKS]
     main_ref, rows_ref, wide_ref, w_ref, sems, part_ref = refs[1 + ROW_BLOCKS :]
-    n = pl.program_id(0)
+    copies = weight_copies(QKV_PIECES, w_hbm, w_ref, sems)
     members = sum(counts)
     count = members * CTOK
     lines = members * STEPS
     halves = TILE // 128
     width = tiles * TILE
-    tile = weight_tile(n, tiles, w_hbm, w_ref, sems)
-
-    @pl.when(n == 0)
-    def _():
-        at = 0
-        for x_ref, size in zip(x_refs, counts):
-            rows = slice(at * CTOK, (at + size) * CTOK)
-            rows_ref[rows, :] = x_ref[:, :, :FEATURES].reshape(size * CTOK, FEATURES)
-            packed = x_ref[:, :, FEATURES:].reshape(size * CTOK, TILE).astype(jnp.float32)
-            for k in range(halves):
-                wide_ref[k, rows, :] = packed[:, k * 128 : (k + 1) * 128]
-            at += size
+    at = 0
+    for x_ref, size in zip(x_refs, counts):
+        rows = slice(at * CTOK, (at + size) * CTOK)
+        rows_ref[rows, :] = x_ref[:, :, :FEATURES].reshape(size * CTOK, FEATURES)
+        packed = x_ref[:, :, FEATURES:].reshape(size * CTOK, TILE).astype(jnp.float32)
         for k in range(halves):
-            for j in range(FEATURES // TILE):
-                lane = j * TILE + k * 128
-                rows_ref[count:, lane : lane + 128] = wide_ref[k, pl.ds(j, lines, stride=8), :].astype(jnp.bfloat16)
-
-    tile.wait()
-    prod = jnp.dot(rows_ref[...], w_ref[n], preferred_element_type=jnp.float32)
-    high = prod.astype(jnp.bfloat16)
-    part_ref[:, :, pl.ds(pl.multiple_of(n * TILE, TILE), TILE)] = high[:count].reshape(members, CTOK, TILE)
+            wide_ref[k, rows, :] = packed[:, k * 128 : (k + 1) * 128]
+        at += size
     for k in range(halves):
-        wide_ref[k, pl.ds(n, lines, stride=8), :] = prod[count:, k * 128 : (k + 1) * 128]
-    start = rest_tile(lax.rem(lax.axis_index("tp"), COL_BLOCKS))
-
-    @pl.when((n >= start) & (n < start + REST // TILE))
-    def _():
+        for j in range(FEATURES // TILE):
+            lane = j * TILE + k * 128
+            rows_ref[count:, lane : lane + 128] = wide_ref[k, pl.ds(j, lines, stride=8), :].astype(jnp.bfloat16)
+
+    late = lax.rem(lax.axis_index("tp"), COL_BLOCKS) == 6
+    for (first, size), copy in zip(QKV_PIECES, copies):
+        copy.wait()
+        prod = jnp.dot(rows_ref[...], w_ref[:, first : first + size], preferred_element_type=jnp.float32)
+        high = prod.astype(jnp.bfloat16)
+        part_ref[:, :, first : first + size] = high[:count].reshape(members, CTOK, size)
         low = prod - high.astype(jnp.float32)
-        place = n - start
-        lane = pl.multiple_of(width + place * TILE, TILE)
-        part_ref[:, :, pl.ds(lane, TILE)] = low[:count].astype(jnp.bfloat16).reshape(members, CTOK, TILE)
-        for k in range(halves):
-            wide_ref[k, pl.ds(tiles + place, lines, stride=8), :] = low[count:, k * 128 : (k + 1) * 128]
-
-    @pl.when(n == tiles - 1)
-    def _():
-        z = lax.axis_index("tp") // COL_BLOCKS
-        done = earlier_ref.shape[0] // ROW_BLOCKS if places else 0
-        for k in range(halves):
-            lanes = slice(k * 128, (k + 1) * 128)
-            packed = wide_ref[k].astype(jnp.bfloat16).reshape(members, CTOK, 128)
-            if not places:
-                main_ref[:, :, lanes] = packed
-            for i, (dy, dx) in enumerate(places):
-                y, x = plane_place()
-                column = lax.rem(y + dy, 2) * 4 + lax.rem(x + dx, 4)
-                for r in range(ROW_BLOCKS):
-                    if i < done:
-                        message = earlier_ref[i * ROW_BLOCKS + r, :, lanes]
-                    else:
-                        message = packed[(i - done) * ROW_BLOCKS + r]
-                    main_ref[r * COL_BLOCKS + column, :, lanes] = message
-        for k, out_ref in enumerate(out_refs):
-            to = lax.rem(z + k, ROW_BLOCKS)
-            for g in range(members // ROW_BLOCKS):
-                out_ref[g] = part_ref[g * ROW_BLOCKS + to]
+        for start in range(0, size, 128):
+            n, k = divmod((first + start) // 128, halves)
+            wide_ref[k, pl.ds(n, lines, stride=8), :] = prod[count:, start : start + 128]
+        for begin, here in ((width - REST, late), (0, jnp.logical_not(late))):
+            start, end = max(begin, first), min(begin + REST, first + size)
+            if start >= end:
+                continue
+
+            @pl.when(here)
+            def _():
+                kept = low[:, start - first : end - first]
+                lanes = slice(width + start - begin, width + end - begin)
+                part_ref[:, :, lanes] = kept[:count].astype(jnp.bfloat16).reshape(members, CTOK, end - start)
+                for lane in range(0, end - start, 128):
+                    n, k = divmod((start - begin + lane) // 128, halves)
+                    wide_ref[k, pl.ds(tiles + n, lines, stride=8), :] = kept[count:, lane : lane + 128]
+
+    z = lax.axis_index("tp") // COL_BLOCKS
+    done = earlier_ref.shape[0] // ROW_BLOCKS if places else 0
+    for k in range(halves):
+        lanes = slice(k * 128, (k + 1) * 128)
+        packed = wide_ref[k].astype(jnp.bfloat16).reshape(members, CTOK, 128)
+        if not places:
+            main_ref[:, :, lanes] = packed
+        for i, (dy, dx) in enumerate(places):
+            y, x = plane_place()
+            column = lax.rem(y + dy, 2) * 4 + lax.rem(x + dx, 4)
+            for r in range(ROW_BLOCKS):
+                if i < done:
+                    message = earlier_ref[i * ROW_BLOCKS + r, :, lanes]
+                else:
+                    message = packed[(i - done) * ROW_BLOCKS + r]
+                main_ref[r * COL_BLOCKS + column, :, lanes] = message
+    for k, out_ref in enumerate(out_refs):
+        to = lax.rem(z + k, ROW_BLOCKS)
+        for g in range(members // ROW_BLOCKS):
+            out_ref[g] = part_ref[g * ROW_BLOCKS + to]
 
 
 def block_product(messages, blocks, earlier=(), places=()):
@@ -199,14 +200,13 @@
         functools.partial(product_kernel, tiles, counts, places),
         out_shape=[jax.ShapeDtypeStruct((members // ROW_BLOCKS, CTOK, lanes), jnp.bfloat16)] * ROW_BLOCKS
         + [jax.ShapeDtypeStruct((MEMBERS if places else members, CTOK, TILE), jnp.bfloat16)],
-        grid=(tiles,),
         in_specs=[VMEM] * (len(counts) + len(earlier)) + [HBM],
         out_specs=[VMEM] * (1 + ROW_BLOCKS),
         scratch_shapes=[
             pltpu.VMEM((members * (CTOK + STEPS), FEATURES), jnp.bfloat16),
             pltpu.VMEM((TILE // 128, members * CTOK, 128), jnp.float32),
-            pltpu.VMEM((tiles, FEATURES, TILE), jnp.bfloat16),
-            pltpu.SemaphoreType.DMA((tiles,)),
+            pltpu.VMEM((FEATURES, tiles * TILE), jnp.bfloat16),
+            pltpu.SemaphoreType.DMA((len(QKV_PIECES),)),
             pltpu.VMEM((members, CTOK, lanes), jnp.bfloat16),
         ],
         compiler_params=kernel_params(),
@@ -469,53 +469,45 @@
     )(value_head, in_hbm(blocks))
 
 
-def out_kernel(tiles, x_ref, read_ref, w_hbm, *refs):
+def out_kernel(x_ref, read_ref, w_hbm, *refs):
     out_ref, rows_ref, wide_ref, read8_ref, w_ref, sems = refs[-6:]
-    n = pl.program_id(0)
+    copies = weight_copies(OUT_PIECES, w_hbm, w_ref, sems)
     members = x_ref.shape[0]
     lines = members * STEPS
     halves = TILE // 128
-    tile = weight_tile(n, tiles, w_hbm, w_ref, sems)
-
-    @pl.when(n == 0)
-    def _():
+    for j in range(FEATURES // TILE):
+        read8_ref[j : j + 1, :] = read_ref[:, j * TILE : (j + 1) * TILE]
+    out_ref[:, 8:, :] = jnp.broadcast_to(read8_ref[...][None], (members, 8, TILE))
+    packed = x_ref[...].reshape(members * 16, TILE).astype(jnp.float32)
+    for k in range(halves):
+        wide_ref[k] = packed[:, k * 128 : (k + 1) * 128]
         for j in range(FEATURES // TILE):
-            read8_ref[j : j + 1, :] = read_ref[:, j * TILE : (j + 1) * TILE]
-        out_ref[:, 8:, :] = jnp.broadcast_to(read8_ref[...][None], (members, 8, TILE))
-        packed = x_ref[...].reshape(members * 16, TILE).astype(jnp.float32)
-        for k in range(halves):
-            wide_ref[k] = packed[:, k * 128 : (k + 1) * 128]
-            for j in range(FEATURES // TILE):
-                lane = j * TILE + k * 128
-                rows_ref[:, lane : lane + 128] = wide_ref[k, pl.ds(j, lines, stride=8), :].astype(jnp.bfloat16)
-
-    tile.wait()
-    prod = jnp.dot(rows_ref[...], w_ref[n], preferred_element_type=jnp.float32)
+            lane = j * TILE + k * 128
+            rows_ref[:, lane : lane + 128] = wide_ref[k, pl.ds(j, lines, stride=8), :].astype(jnp.bfloat16)
+
+    for (first, size), copy in zip(OUT_PIECES, copies):
+        copy.wait()
+        prod = jnp.dot(rows_ref[...], w_ref[:, first : first + size], preferred_element_type=jnp.float32)
+        for start in range(0, size, 128):
+            n, k = divmod((first + start) // 128, halves)
+            wide_ref[k, pl.ds(n, lines, stride=4), :] = prod[:, start : start + 128]
     for k in range(halves):
-        wide_ref[k, pl.ds(n, lines, stride=4), :] = prod[:, k * 128 : (k + 1) * 128]
-
-    @pl.when(n == tiles - 1)
-    def _():
-        for k in range(halves):
-            packed = wide_ref[k, : members * 8, :].reshape(members, 8, 128)
-            out_ref[:, :8, k * 128 : (k + 1) * 128] = packed
+        out_ref[:, :8, k * 128 : (k + 1) * 128] = wide_ref[k, : members * 8, :].reshape(members, 8, 128)
 
 
 def out_product(rows, read, blocks, after):
     members = rows.shape[0]
-    tiles = blocks.shape[2] // TILE
-    return pl.pallas_call(
-        functools.partial(out_kernel, tiles),
+    return pl.pallas_call(
+        out_kernel,
         out_shape=jax.ShapeDtypeStruct((members, 16, TILE), jnp.float32),
-        grid=(tiles,),
-        in_specs=[whole(rows.shape), whole(read.shape), HBM] + [UNREAD] * len(after),
-        out_specs=whole((members, 16, TILE)),
+        in_specs=[VMEM, VMEM, HBM] + [UNREAD] * len(after),
+        out_specs=VMEM,
         scratch_shapes=[
             pltpu.VMEM((members * STEPS, FEATURES), jnp.bfloat16),
             pltpu.VMEM((TILE // 128, members * 16, 128), jnp.float32),
             pltpu.VMEM((8, TILE), jnp.float32),
-            pltpu.VMEM((tiles, FEATURES, TILE), jnp.bfloat16),
-            pltpu.SemaphoreType.DMA((tiles,)),
+            pltpu.VMEM(blocks.shape[1:], jnp.bfloat16),
+            pltpu.SemaphoreType.DMA((len(OUT_PIECES),)),
         ],
         compiler_params=kernel_params(),
         cost_estimate=cost(3 * 10**8, 5 * 10**6),

time: 113 us -> 114 us (level)
  transfers between devices with their start and end apart: 23 -> 23, of which waited for: 10 -> 10; matrix products, arithmetic and copies ran while one was open for 0% -> 0% of each run, Pallas kernels for 14% -> 15%
where the time goes in v16:
time: 114 us; the launch traced here: 113 us
  starting transfers between devices  49.9 us (44%)
  Pallas kernels  26.3 us (23%)
  waiting for transfers between devices  21.3 us (19%)
  blocking collectives  12.2 us (11%)
  between operations  2.13 us (2%)
  local copies, waits for them, and re-layouts  1.18 us (1%)
    ppermute x14, starting transfers between devices, from_side(): return lax.ppermute(rows, 'tp', route)  23.2 us
    ppermute x14, waiting for transfers between devices, from_side(): return lax.ppermute(rows, 'tp', route)  18.1 us
    all_to_all x3, starting transfers between devices, exchange(): return lax.all_to_all(rows, 'tp', split_axis=0, concat_axis=0, tiled=True)  17.8 us
    all_to_all x1, blocking collectives, project(): lax.all_to_all(rows, 'tp', split_axis=0, concat_axis=0, tiled=True, axis_...  12.2 us
    pallas_call x2, Pallas kernels, block_product(): pl.pallas_call(functools.partial(product_kernel, tiles, counts, places),...  9.36 us
    ppermute x6, starting transfers between devices, from_along(): return lax.ppermute(rows, 'tp', route)  8.93 us
    pallas_call x1, Pallas kernels, attend_main(): pl.pallas_call(attend_main_kernel, out_shape=(jax.ShapeDtypeStruct((32, 1...  3.7 us
    pallas_call x1, Pallas kernels, out_product(): pl.pallas_call(out_kernel, out_shape=jax.ShapeDtypeStruct((members, 16, T...  3.53 us
  transfers between devices with their start and end apart: 23, of which 10 were waited for; matrix products, arithmetic and copies ran while one was open for 0% of the time, Pallas kernels for 15%

profile of v16, /device:TPU:0, one launch (start us, length us, event | category | flops | bytes accessed | tf_op | source)
XLA Modules:
  0.0 113.4 jit_solution(2924953846055242645)
XLA Ops:
  2.0 12.2 %all_to_all.20.refs_0_ = bf16[4,16,2304]{2,1,0:T(8,128)(2,1)S(1)} all-to-all(bf16[4,16,2304]{2,1,0:T(8,128)(2,1)S(1)} %norm_rows.1), channel_id=1, replica_groups={{0,8,16,24},{1,9,17,25},{2,10,18,26},{3,11,19,27},{4,12,20,28},{5,13,21..., dimensions={0} | all-to-all | bytes 589824 | tf_op jit(solution)/shard_map/all_to_all | solution.py:593
  17.3 1.7 %collective-permute-start.6 = (bf16[4,16,2304]{2,1,0:T(8,128)(2,1)S(1)}, bf16[4,16,2304]{2,1,0:T(8,128)(2,1)S(1)}, u32[]{:S(2)}, u32[]{:S(2)}) collective-permute-start(bf16[4,16,2304]{2,1,0:T(8,128)(2,1)S(1)} %all_to_all.20.refs_0_), channel_id=1, source_target_pairs={{1,0},{2,1},{3,2},{0,3},{5,4},{6,5},{7,6},{4,7},{9,8},{10,9},{11,1... | collective-permute-start | bytes 884744 | tf_op jit(solution)/shard_map/ppermute | solution.py:579
  19.1 2.4 %collective-permute-done.refs_1_ = bf16[4,16,2304]{2,1,0:T(8,128)(2,1)S(1)} collective-permute-done((bf16[4,16,2304]{2,1,0:T(8,128)(2,1)S(1)}, bf16[4,16,2304]{2,1,0:T(8,128)(2,1)S(1)}, u32[]{:S(2)}, u32[]{:S(2)}) %collective-permute-start) | collective-permute-done | bytes 294944 | tf_op jit(solution)/shard_map/ppermute | solution.py:579
  21.5 2.8 %collective-permute-start.1 = (bf16[4,16,2304]{2,1,0:T(8,128)(2,1)S(1)}, bf16[4,16,2304]{2,1,0:T(8,128)(2,1)S(1)}, u32[]{:S(2)}, u32[]{:S(2)}) collective-permute-start(bf16[4,16,2304]{2,1,0:T(8,128)(2,1)S(1)} %collective-permute-done.refs_1_), channel_id=1, source_target_pairs={{1,0},{2,1},{3,2},{0,3},{5,4},{6,5},{7,6},{4,7},{9,8},{10,9},{11,1... | collective-permute-start | bytes 884744 | tf_op jit(solution)/shard_map/ppermute | solution.py:579
  26.6 4.2 %block_product.2 = (bf16[4,16,2048]{2,1,0:T(8,128)(2,1)S(1)}, bf16[4,16,2048]{2,1,0:T(8,128)(2,1)S(1)}, bf16[4,16,2048]{2,1,0:T(8,128)(2,1)S(1)}, bf16[4,16,2048...) custom-call(bf16[4,16,2304]{2,1,0:T(8,128)(2,1)S(1)} %all_to_all.20.refs_0_, ...), custom_call_target="tpu_custom_call" | custom-call | flops 1509949440 | bytes 12000000 | tf_op jit(solution)/shard_map/block_product/pallas_call | solution.py:199
  31.5 2.1 %collective-permute-start.8 = (bf16[4,16,2048]{2,1,0:T(8,128)(2,1)S(1)}, bf16[4,16,2048]{2,1,0:T(8,128)(2,1)S(1)}, u32[]{:S(2)}, u32[]{:S(2)}) collective-permute-start(bf16[4,16,2048]{2,1,0:T(8,128)(2,1)S(1)} %get-tuple-element.33), channel_id=1, source_target_pairs={{16,0},{17,1},{18,2},{19,3},{20,4},{21,5},{22,6},{23,7},{24,8},{25... | collective-permute-start | bytes 786440 | tf_op jit(solution)/shard_map/ppermute | solution.py:584
  36.0 1.7 %collective-permute-start.5 = (bf16[4,16,2304]{2,1,0:T(8,128)(2,1)S(1)}, bf16[4,16,2304]{2,1,0:T(8,128)(2,1)S(1)}, u32[]{:S(2)}, u32[]{:S(2)}) collective-permute-start(bf16[4,16,2304]{2,1,0:T(8,128)(2,1)S(1)} %collective-permute-done.1.refs_0_), channel_id=1, source_target_pairs={{1,0},{2,1},{3,2},{0,3},{5,4},{6,5},{7,6},{4,7},{9,8},{10,9},{11,1... | collective-permute-start | bytes 884744 | tf_op jit(solution)/shard_map/ppermute | solution.py:579
  37.8 4.7 %collective-permute-done.4.refs_2_ = bf16[4,16,2304]{2,1,0:T(8,128)(2,1)S(1)} collective-permute-done((bf16[4,16,2304]{2,1,0:T(8,128)(2,1)S(1)}, bf16[4,16,2304]{2,1,0:T(8,128)(2,1)S(1)}, u32[]{:S(2)}, u32[]{:S(2)}) %collective-permute-start.4) | collective-permute-done | bytes 294944 | tf_op jit(solution)/shard_map/ppermute | solution.py:579
  42.8 5.1 %block_product.3 = (bf16[4,16,2048]{2,1,0:T(8,128)(2,1)S(1)}, bf16[4,16,2048]{2,1,0:T(8,128)(2,1)}, bf16[4,16,2048]{2,1,0:T(8,128)(2,1)S(1)}, bf16[4,16,2048]{2,1,0:T(8,128)(2,1)S(1)}, bf16[32,16,256]{2,1,0:T(8,128)(2,1)}) custom-call(bf16[4,16,2304]{2,1,0:T(8,128)(2,1)S(1)} %collective-permute-done.1.refs_0_, ...), custom_call_target="tpu_custom_call" | custom-call | flops 1509949440 | bytes 12000000 | tf_op jit(solution)/shard_map/block_product/pallas_call | solution.py:199
  50.6 2.5 %collective-permute-start.12 = (bf16[4,16,2048]{2,1,0:T(8,128)(2,1)S(1)}, bf16[4,16,2048]{2,1,0:T(8,128)(2,1)S(1)}, u32[]{:S(2)}, u32[]{:S(2)}) collective-permute-start(bf16[4,16,2048]{2,1,0:T(8,128)(2,1)S(1)} %get-tuple-element.38), channel_id=1, source_target_pairs={{8,0},{9,1},{10,2},{11,3},{12,4},{13,5},{14,6},{15,7},{16,8},{17,9... | collective-permute-start | bytes 786440 | tf_op jit(solution)/shard_map/ppermute | solution.py:584
  54.5 6.5 %all-to-all-start.1 = ((bf16[32,16,256]{2,1,0:T(8,128)(2,1)}), bf16[32,16,256]{2,1,0:T(8,128)(2,1)S(1)}, u32[]{:S(2)}, u32[]{:S(2)}) async-start(bf16[32,16,256]{2,1,0:T(8,128)(2,1)} %get-tuple-element.35), calls=%async_computation.1 | async-start | bytes 524288 | tf_op jit(solution)/shard_map/all_to_all | solution.py:568
  61.1 1.9 %collective-permute-start.14 = (bf16[16,2048]{1,0:T(8,128)(2,1)}, bf16[16,2048]{1,0:T(8,128)(2,1)S(1)}, u32[]{:S(2)}, u32[]{:S(2)}) collective-permute-start(bf16[16,2048]{1,0:T(8,128)(2,1)} %get-tuple-element.44), channel_id=1, source_target_pairs={{3,0},{0,1},{1,2},{2,3},{7,4},{4,5},{5,6},{6,7},{11,8},{8,9},{9,10... | collective-permute-start | bytes 196616 | tf_op jit(solution)/shard_map/ppermute | solution.py:579
  64.5 3.4 %readout.1.refs_6_.read_ref = f32[1,2048]{1,0:T(1,128)S(1)} custom-call(f32[8,1024]{1,0:T(8,128)S(1)} %reshape.34.head_ref, bf16[1,2048,1024]{2,1,0:T(8,128)(2,1)} %w_hbm.3), custom_call_target="tpu_custom_call" | custom-call | flops 200000000 | bytes 5000000 | tf_op jit(solution)/shard_map/readout/pallas_call | solution.py:460
  68.0 2.3 %all-to-all-done.1.parts_ref = bf16[32,16,256]{2,1,0:T(8,128)(2,1)S(1)} async-done(((bf16[32,16,256]{2,1,0:T(8,128)(2,1)}), bf16[32,16,256]{2,1,0:T(8,128)(2,1)S(1)}, u32[]{:S(2)}, u32[]{:S(2)}) %all-to-all-start.1) | async-done | bytes 262176 | tf_op jit(solution)/shard_map/all_to_all | solution.py:568
  70.2 3.7 %attend_main.1 = (bf16[32,16,256]{2,1,0:T(8,128)(2,1)}, f32[8,2048]{1,0:T(8,128)S(1)}) custom-call(s32[1]{0:T(128)} %copy.12.len_ref, f32[1,10240]{1,0:T(1,128)S(1)} %bitcast.16, f32[8,128]{1,0:T(8,128)S(1)} %get-tuple-element.62.cos_ref, f32[8,128]{1,0:T(8,128)S(1)} %get-tuple-element.63.sin_ref, bf16[256,2048]{1,0:T(8,128)(2,1)S(1)} %bitcast.11, ...), custom_call_target="tpu_custom_call" | custom-call | flops 200000000 | bytes 6000000 | tf_op jit(solution)/shard_map/attend_main/pallas_call | solution.py:383
  73.9 5.3 %all-to-all-start.2 = ((bf16[32,16,256]{2,1,0:T(8,128)(2,1)}), bf16[32,16,256]{2,1,0:T(8,128)(2,1)S(1)}, u32[]{:S(2)}, u32[]{:S(2)}) async-start(bf16[32,16,256]{2,1,0:T(8,128)(2,1)} %get-tuple-element.46), calls=%async_computation.2 | async-start | bytes 524288 | tf_op jit(solution)/shard_map/all_to_all | solution.py:568
  79.5 2.8 %collective-permute-start.16 = (bf16[16,2048]{1,0:T(8,128)(2,1)S(1)}, bf16[16,2048]{1,0:T(8,128)(2,1)S(1)}, u32[]{:S(2)}, u32[]{:S(2)}) collective-permute-start(bf16[16,2048]{1,0:T(8,128)(2,1)S(1)} %get-tuple-element.48), channel_id=1, source_target_pairs={{7,0},{4,1},{5,2},{6,3},{3,4},{0,5},{1,6},{2,7},{15,8},{12,9},{13,... | collective-permute-start | bytes 196616 | tf_op jit(solution)/shard_map/ppermute | solution.py:579
  83.7 3.4 %collective-permute-done.16.refs_0_.refs_4_ = bf16[16,2048]{1,0:T(8,128)(2,1)S(1)} collective-permute-done((bf16[16,2048]{1,0:T(8,128)(2,1)S(1)}, bf16[16,2048]{1,0:T(8,128)(2,1)S(1)}, u32[]{:S(2)}, u32[]{:S(2)}) %collective-permute-start.16) | collective-permute-done | bytes 65568 | tf_op jit(solution)/shard_map/ppermute | solution.py:579
  88.5 3.5 %out_product.1 = f32[32,16,256]{2,1,0:T(8,128)} custom-call(bf16[32,16,256]{2,1,0:T(8,128)(2,1)S(1)} %all-to-all-done.2.x_ref, f32[1,2048]{1,0:T(1,128)S(1)} %readout.1.refs_6_.read_ref, bf16[1,2048,1024]{2,1,0:T(8,128)(2,1)} %w_hbm.3, bf16[16,2048]{1,0:T(8,128)(2,1)S(1)} %collective-permute-done.16.refs_0_.refs_4_, ...), custom_call_target="tpu_custom_call" | custom-call | flops 300000000 | bytes 5000000 | tf_op jit(solution)/shard_map/out_product/pallas_call | solution.py:500
  92.0 6.0 %all-to-all-start.3 = ((f32[32,16,256]{2,1,0:T(8,128)}), f32[32,16,256]{2,1,0:T(8,128)S(1)}, u32[]{:S(2)}, u32[]{:S(2)}) async-start(f32[32,16,256]{2,1,0:T(8,128)} %out_product.1), calls=%async_computation.3 | async-start | bytes 1048576 | tf_op jit(solution)/shard_map/all_to_all | solution.py:568
  98.8 3.4 %collective-permute-start.18 = (bf16[16,2048]{1,0:T(8,128)(2,1)S(1)}, bf16[16,2048]{1,0:T(8,128)(2,1)S(1)}, u32[]{:S(2)}, u32[]{:S(2)}) collective-permute-start(bf16[16,2048]{1,0:T(8,128)(2,1)S(1)} %get-tuple-element.52), channel_id=1, source_target_pairs={{2,0},{3,1},{0,2},{1,3},{6,4},{7,5},{4,6},{5,7},{10,8},{11,9},{8,1... | collective-permute-start | bytes 196616 | tf_op jit(solution)/shard_map/ppermute | solution.py:579
  103.7 2.7 %collective-permute-done.18.refs_6_ = bf16[16,2048]{1,0:T(8,128)(2,1)S(1)} collective-permute-done((bf16[16,2048]{1,0:T(8,128)(2,1)S(1)}, bf16[16,2048]{1,0:T(8,128)(2,1)S(1)}, u32[]{:S(2)}, u32[]{:S(2)}) %collective-permute-start.18) | collective-permute-done | bytes 65568 | tf_op jit(solution)/shard_map/ppermute | solution.py:579
  106.5 2.4 %collective-permute-done.19.refs_7_ = bf16[16,2048]{1,0:T(8,128)(2,1)S(1)} collective-permute-done((bf16[16,2048]{1,0:T(8,128)(2,1)S(1)}, bf16[16,2048]{1,0:T(8,128)(2,1)S(1)}, u32[]{:S(2)}, u32[]{:S(2)}) %collective-permute-start.19) | collective-permute-done | bytes 65568 | tf_op jit(solution)/shard_map/ppermute | solution.py:579
  108.9 3.0 %attend_cont.1.mixed_ref = bf16[16,8192]{1,0:T(8,128)(2,1)S(1)} custom-call(s32[1]{0:T(128)} %copy.12.len_ref, s32[1]{0:T(128)S(6)} %copy.13.bound_ref, f32[1,10240]{1,0:T(1,128)S(1)} %bitcast.18, f32[16,128]{1,0:T(8,128)S(1)} %get-tuple-element.64.cos_ref, f32[16,128]{1,0:T(8,128)S(1)} %get-tuple-element.65.sin_ref, bf16[256,2048]{1,0:T(8,128)(2,1)S(1)} %bitcast.12, ...), custom_call_target="tpu_custom_call" | custom-call | flops 400000000 | bytes 8000000 | tf_op jit(solution)/shard_map/attend_cont/pallas_call | solution.py:429
  (55 shorter events, 21.4 us)
Async XLA Ops:
  14.2 7.3 %collective-permute-start = (bf16[4,16,2304]{2,1,0:T(8,128)(2,1)S(1)}, bf16[4,16,2304]{2,1,0:T(8,128)(2,1)S(1)}, u32[]{:S(2)}, u32[]{:S(2)}) collective-permute-start(bf16[4,16,2304]{2,1,0:T(8,128)(2,1)S(1)} %all_to_all.20.refs_0_), channel_id=1, source_target_pairs={{4,0},{5,1},{6,2},{7,3},{0,4},{1,5},{2,6},{3,7},{12,8},{13,9},{14,... | collective-permute-start | bytes 884744 | tf_op jit(solution)/shard_map/ppermute | solution.py:579
  15.8 9.1 %collective-permute-start.3 = (bf16[4,16,2304]{2,1,0:T(8,128)(2,1)S(1)}, bf16[4,16,2304]{2,1,0:T(8,128)(2,1)S(1)}, u32[]{:S(2)}, u32[]{:S(2)}) collective-permute-start(bf16[4,16,2304]{2,1,0:T(8,128)(2,1)S(1)} %all_to_all.20.refs_0_), channel_id=1, source_target_pairs={{3,0},{0,1},{1,2},{2,3},{7,4},{4,5},{5,6},{6,7},{11,8},{8,9},{9,10... | collective-permute-start | bytes 884744 | tf_op jit(solution)/shard_map/ppermute | solution.py:579
  17.3 9.3 %collective-permute-start.6 = (bf16[4,16,2304]{2,1,0:T(8,128)(2,1)S(1)}, bf16[4,16,2304]{2,1,0:T(8,128)(2,1)S(1)}, u32[]{:S(2)}, u32[]{:S(2)}) collective-permute-start(bf16[4,16,2304]{2,1,0:T(8,128)(2,1)S(1)} %all_to_all.20.refs_0_), channel_id=1, source_target_pairs={{1,0},{2,1},{3,2},{0,3},{5,4},{6,5},{7,6},{4,7},{9,8},{10,9},{11,1... | collective-permute-start | bytes 884744 | tf_op jit(solution)/shard_map/ppermute | solution.py:579
  21.5 13.0 %collective-permute-start.1 = (bf16[4,16,2304]{2,1,0:T(8,128)(2,1)S(1)}, bf16[4,16,2304]{2,1,0:T(8,128)(2,1)S(1)}, u32[]{:S(2)}, u32[]{:S(2)}) collective-permute-start(bf16[4,16,2304]{2,1,0:T(8,128)(2,1)S(1)} %collective-permute-done.refs_1_), channel_id=1, source_target_pairs={{1,0},{2,1},{3,2},{0,3},{5,4},{6,5},{7,6},{4,7},{9,8},{10,9},{11,1... | collective-permute-start | bytes 884744 | tf_op jit(solution)/shard_map/ppermute | solution.py:579
  24.3 11.8 %collective-permute-start.2 = (bf16[4,16,2304]{2,1,0:T(8,128)(2,1)S(1)}, bf16[4,16,2304]{2,1,0:T(8,128)(2,1)S(1)}, u32[]{:S(2)}, u32[]{:S(2)}) collective-permute-start(bf16[4,16,2304]{2,1,0:T(8,128)(2,1)S(1)} %collective-permute-done.refs_1_), channel_id=1, source_target_pairs={{3,0},{0,1},{1,2},{2,3},{7,4},{4,5},{5,6},{6,7},{11,8},{8,9},{9,10... | collective-permute-start | bytes 884744 | tf_op jit(solution)/shard_map/ppermute | solution.py:579
  30.8 19.8 %collective-permute-start.7 = (bf16[4,16,2048]{2,1,0:T(8,128)(2,1)S(1)}, bf16[4,16,2048]{2,1,0:T(8,128)(2,1)S(1)}, u32[]{:S(2)}, u32[]{:S(2)}) collective-permute-start(bf16[4,16,2048]{2,1,0:T(8,128)(2,1)S(1)} %get-tuple-element.32), channel_id=1, source_target_pairs={{24,0},{25,1},{26,2},{27,3},{28,4},{29,5},{30,6},{31,7},{0,8},{1,9... | collective-permute-start | bytes 786440 | tf_op jit(solution)/shard_map/ppermute | solution.py:584
  31.5 21.7 %collective-permute-start.8 = (bf16[4,16,2048]{2,1,0:T(8,128)(2,1)S(1)}, bf16[4,16,2048]{2,1,0:T(8,128)(2,1)S(1)}, u32[]{:S(2)}, u32[]{:S(2)}) collective-permute-start(bf16[4,16,2048]{2,1,0:T(8,128)(2,1)S(1)} %get-tuple-element.33), channel_id=1, source_target_pairs={{16,0},{17,1},{18,2},{19,3},{20,4},{21,5},{22,6},{23,7},{24,8},{25... | collective-permute-start | bytes 786440 | tf_op jit(solution)/shard_map/ppermute | solution.py:584
  33.5 19.6 %collective-permute-start.9 = (bf16[4,16,2048]{2,1,0:T(8,128)(2,1)S(1)}, bf16[4,16,2048]{2,1,0:T(8,128)(2,1)S(1)}, u32[]{:S(2)}, u32[]{:S(2)}) collective-permute-start(bf16[4,16,2048]{2,1,0:T(8,128)(2,1)S(1)} %get-tuple-element.34), channel_id=1, source_target_pairs={{8,0},{9,1},{10,2},{11,3},{12,4},{13,5},{14,6},{15,7},{16,8},{17,9... | collective-permute-start | bytes 786440 | tf_op jit(solution)/shard_map/ppermute | solution.py:584
  34.5 7.9 %collective-permute-start.4 = (bf16[4,16,2304]{2,1,0:T(8,128)(2,1)S(1)}, bf16[4,16,2304]{2,1,0:T(8,128)(2,1)S(1)}, u32[]{:S(2)}, u32[]{:S(2)}) collective-permute-start(bf16[4,16,2304]{2,1,0:T(8,128)(2,1)S(1)} %collective-permute-done.3.refs_3_), channel_id=1, source_target_pairs={{3,0},{0,1},{1,2},{2,3},{7,4},{4,5},{5,6},{6,7},{11,8},{8,9},{9,10... | collective-permute-start | bytes 884744 | tf_op jit(solution)/shard_map/ppermute | solution.py:579
  36.0 6.7 %collective-permute-start.5 = (bf16[4,16,2304]{2,1,0:T(8,128)(2,1)S(1)}, bf16[4,16,2304]{2,1,0:T(8,128)(2,1)S(1)}, u32[]{:S(2)}, u32[]{:S(2)}) collective-permute-start(bf16[4,16,2304]{2,1,0:T(8,128)(2,1)S(1)} %collective-permute-done.1.refs_0_), channel_id=1, source_target_pairs={{1,0},{2,1},{3,2},{0,3},{5,4},{6,5},{7,6},{4,7},{9,8},{10,9},{11,1... | collective-permute-start | bytes 884744 | tf_op jit(solution)/shard_map/ppermute | solution.py:579
  47.9 22.3 %collective-permute-start.10 = (bf16[4,16,2048]{2,1,0:T(8,128)(2,1)}, bf16[4,16,2048]{2,1,0:T(8,128)(2,1)S(1)}, u32[]{:S(2)}, u32[]{:S(2)}) collective-permute-start(bf16[4,16,2048]{2,1,0:T(8,128)(2,1)} %get-tuple-element.36), channel_id=1, source_target_pairs={{24,0},{25,1},{26,2},{27,3},{28,4},{29,5},{30,6},{31,7},{0,8},{1,9... | collective-permute-start | bytes 786440 | tf_op jit(solution)/shard_map/ppermute | solution.py:584
  49.0 21.2 %collective-permute-start.11 = (bf16[4,16,2048]{2,1,0:T(8,128)(2,1)S(1)}, bf16[4,16,2048]{2,1,0:T(8,128)(2,1)S(1)}, u32[]{:S(2)}, u32[]{:S(2)}) collective-permute-start(bf16[4,16,2048]{2,1,0:T(8,128)(2,1)S(1)} %get-tuple-element.37), channel_id=1, source_target_pairs={{16,0},{17,1},{18,2},{19,3},{20,4},{21,5},{22,6},{23,7},{24,8},{25... | collective-permute-start | bytes 786440 | tf_op jit(solution)/shard_map/ppermute | solution.py:584
  50.6 19.6 %collective-permute-start.12 = (bf16[4,16,2048]{2,1,0:T(8,128)(2,1)S(1)}, bf16[4,16,2048]{2,1,0:T(8,128)(2,1)S(1)}, u32[]{:S(2)}, u32[]{:S(2)}) collective-permute-start(bf16[4,16,2048]{2,1,0:T(8,128)(2,1)S(1)} %get-tuple-element.38), channel_id=1, source_target_pairs={{8,0},{9,1},{10,2},{11,3},{12,4},{13,5},{14,6},{15,7},{16,8},{17,9... | collective-permute-start | bytes 786440 | tf_op jit(solution)/shard_map/ppermute | solution.py:584
  54.5 8.5 %collective-permute-start.13 = (bf16[16,2048]{1,0:T(8,128)(2,1)S(1)}, bf16[16,2048]{1,0:T(8,128)(2,1)S(1)}, u32[]{:S(2)}, u32[]{:S(2)}) collective-permute-start(bf16[16,2048]{1,0:T(8,128)(2,1)S(1)} %get-tuple-element.43), channel_id=1, source_target_pairs={{4,0},{5,1},{6,2},{7,3},{0,4},{1,5},{2,6},{3,7},{12,8},{13,9},{14,... | collective-permute-start | bytes 196616 | tf_op jit(solution)/shard_map/ppermute | solution.py:579
  54.5 15.8 %all-to-all-start.1 = ((bf16[32,16,256]{2,1,0:T(8,128)(2,1)}), bf16[32,16,256]{2,1,0:T(8,128)(2,1)S(1)}, u32[]{:S(2)}, u32[]{:S(2)}) async-start(bf16[32,16,256]{2,1,0:T(8,128)(2,1)} %get-tuple-element.35), calls=%async_computation.1 | async-start | bytes 524288 | tf_op jit(solution)/shard_map/all_to_all | solution.py:568
  61.1 6.9 %collective-permute-start.14 = (bf16[16,2048]{1,0:T(8,128)(2,1)}, bf16[16,2048]{1,0:T(8,128)(2,1)S(1)}, u32[]{:S(2)}, u32[]{:S(2)}) collective-permute-start(bf16[16,2048]{1,0:T(8,128)(2,1)} %get-tuple-element.44), channel_id=1, source_target_pairs={{3,0},{0,1},{1,2},{2,3},{7,4},{4,5},{5,6},{6,7},{11,8},{8,9},{9,10... | collective-permute-start | bytes 196616 | tf_op jit(solution)/shard_map/ppermute | solution.py:579
  62.9 5.0 %collective-permute-start.15 = (bf16[16,2048]{1,0:T(8,128)(2,1)}, bf16[16,2048]{1,0:T(8,128)(2,1)S(1)}, u32[]{:S(2)}, u32[]{:S(2)}) collective-permute-start(bf16[16,2048]{1,0:T(8,128)(2,1)} %copy-done.5), channel_id=1, source_target_pairs={{1,0},{2,1},{3,2},{0,3},{5,4},{6,5},{7,6},{4,7},{9,8},{10,9},{11,1... | collective-permute-start | bytes 196616 | tf_op jit(solution)/shard_map/ppermute | solution.py:579
  73.9 38.0 %copy-start.3 = (bf16[1,2,8192]{2,1,0:T(2,128)(2,1)S(1)}, bf16[1,2,8192]{2,1,0:T(2,128)(2,1)}, u32[]{:S(2)}) copy-start(bf16[1,2,8192]{2,1,0:T(2,128)(2,1)} %param.10) | copy-start | bytes 98308
  73.9 14.6 %all-to-all-start.2 = ((bf16[32,16,256]{2,1,0:T(8,128)(2,1)}), bf16[32,16,256]{2,1,0:T(8,128)(2,1)S(1)}, u32[]{:S(2)}, u32[]{:S(2)}) async-start(bf16[32,16,256]{2,1,0:T(8,128)(2,1)} %get-tuple-element.46), calls=%async_computation.2 | async-start | bytes 524288 | tf_op jit(solution)/shard_map/all_to_all | solution.py:568
  79.5 7.7 %collective-permute-start.16 = (bf16[16,2048]{1,0:T(8,128)(2,1)S(1)}, bf16[16,2048]{1,0:T(8,128)(2,1)S(1)}, u32[]{:S(2)}, u32[]{:S(2)}) collective-permute-start(bf16[16,2048]{1,0:T(8,128)(2,1)S(1)} %get-tuple-element.48), channel_id=1, source_target_pairs={{7,0},{4,1},{5,2},{6,3},{3,4},{0,5},{1,6},{2,7},{15,8},{12,9},{13,... | collective-permute-start | bytes 196616 | tf_op jit(solution)/shard_map/ppermute | solution.py:579
  82.2 5.4 %collective-permute-start.17 = (bf16[16,2048]{1,0:T(8,128)(2,1)S(1)}, bf16[16,2048]{1,0:T(8,128)(2,1)S(1)}, u32[]{:S(2)}, u32[]{:S(2)}) collective-permute-start(bf16[16,2048]{1,0:T(8,128)(2,1)S(1)} %get-tuple-element.49), channel_id=1, source_target_pairs={{5,0},{6,1},{7,2},{4,3},{1,4},{2,5},{3,6},{0,7},{13,8},{14,9},{15,... | collective-permute-start | bytes 196616 | tf_op jit(solution)/shard_map/ppermute | solution.py:579
  92.0 19.9 %all-to-all-start.3 = ((f32[32,16,256]{2,1,0:T(8,128)}), f32[32,16,256]{2,1,0:T(8,128)S(1)}, u32[]{:S(2)}, u32[]{:S(2)}) async-start(f32[32,16,256]{2,1,0:T(8,128)} %out_product.1), calls=%async_computation.3 | async-start | bytes 1048576 | tf_op jit(solution)/shard_map/all_to_all | solution.py:568
  98.8 7.7 %collective-permute-start.18 = (bf16[16,2048]{1,0:T(8,128)(2,1)S(1)}, bf16[16,2048]{1,0:T(8,128)(2,1)S(1)}, u32[]{:S(2)}, u32[]{:S(2)}) collective-permute-start(bf16[16,2048]{1,0:T(8,128)(2,1)S(1)} %get-tuple-element.52), channel_id=1, source_target_pairs={{2,0},{3,1},{0,2},{1,3},{6,4},{7,5},{4,6},{5,7},{10,8},{11,9},{8,1... | collective-permute-start | bytes 196616 | tf_op jit(solution)/shard_map/ppermute | solution.py:579
  102.2 6.7 %collective-permute-start.19 = (bf16[16,2048]{1,0:T(8,128)(2,1)S(1)}, bf16[16,2048]{1,0:T(8,128)(2,1)S(1)}, u32[]{:S(2)}, u32[]{:S(2)}) collective-permute-start(bf16[16,2048]{1,0:T(8,128)(2,1)S(1)} %get-tuple-element.53), channel_id=1, source_target_pairs={{6,0},{7,1},{4,2},{5,3},{2,4},{3,5},{0,6},{1,7},{14,8},{15,9},{12,... | collective-permute-start | bytes 196616 | tf_op jit(solution)/shard_map/ppermute | solution.py:579
  (5 other events, 128.0 us)

commit v17 on v15

--- a/solution.py
+++ b/solution.py
@@ -25,7 +25,7 @@
 EPS = 1e-06
 MASKED_SCORE = -1e30
 
-VMEM_LIMIT = 32 * 1024 * 1024
+VMEM_LIMIT = 28 * 1024 * 1024
 VMEM = pl.BlockSpec(memory_space=pltpu.VMEM)
 SMEM = pl.BlockSpec(memory_space=pltpu.SMEM)
 HBM = pl.BlockSpec(memory_space=pltpu.HBM)
@@ -123,16 +123,19 @@
 def product_kernel(tiles, counts, places, *refs):
     x_refs, refs = refs[: len(counts)], refs[len(counts) :]
     if places:
-        earlier_ref, refs = refs[0], refs[1:]
-    w_hbm, *out_refs = refs[: 1 + ROW_BLOCKS]
-    main_ref, rows_ref, wide_ref, w_ref, sems, part_ref = refs[1 + ROW_BLOCKS :]
+        earlier_ref, w_ref, *out_refs = refs[: 2 + ROW_BLOCKS]
+        main_ref, rows_ref, wide_ref, part_ref = refs[2 + ROW_BLOCKS :]
+    else:
+        w_hbm, *out_refs = refs[: 1 + ROW_BLOCKS]
+        main_ref, w_ref, rows_ref, wide_ref, part_ref, sems = refs[1 + ROW_BLOCKS :]
     n = pl.program_id(0)
     members = sum(counts)
     count = members * CTOK
     lines = members * STEPS
     halves = TILE // 128
     width = tiles * TILE
-    tile = weight_tile(n, tiles, w_hbm, w_ref, sems)
+    if not places:
+        tile = weight_tile(n, tiles, w_hbm, w_ref, sems)
 
     @pl.when(n == 0)
     def _():
@@ -149,7 +152,8 @@
                 lane = j * TILE + k * 128
                 rows_ref[count:, lane : lane + 128] = wide_ref[k, pl.ds(j, lines, stride=8), :].astype(jnp.bfloat16)
 
-    tile.wait()
+    if not places:
+        tile.wait()
     prod = jnp.dot(rows_ref[...], w_ref[n], preferred_element_type=jnp.float32)
     high = prod.astype(jnp.bfloat16)
     part_ref[:, :, pl.ds(pl.multiple_of(n * TILE, TILE), TILE)] = high[:count].reshape(members, CTOK, TILE)
@@ -190,29 +194,37 @@
                 out_ref[g] = part_ref[g * ROW_BLOCKS + to]
 
 
-def block_product(messages, blocks, earlier=(), places=()):
-    tiles = blocks.shape[2] // TILE
+def block_product(messages, weight, earlier=None, places=()):
+    tiles = QKV // COL_BLOCKS // TILE
     lanes = tiles * TILE + REST
     counts = tuple(rows.shape[0] for rows in messages)
     members = sum(counts)
+    out = [jax.ShapeDtypeStruct((members // ROW_BLOCKS, CTOK, lanes), jnp.bfloat16)] * ROW_BLOCKS
+    out.append(jax.ShapeDtypeStruct((MEMBERS if places else members, CTOK, TILE), jnp.bfloat16))
+    scratch = [
+        pltpu.VMEM((members * (CTOK + STEPS), FEATURES), jnp.bfloat16),
+        pltpu.VMEM((TILE // 128, members * CTOK, 128), jnp.float32),
+        pltpu.VMEM((members, CTOK, lanes), jnp.bfloat16),
+    ]
+    if places:
+        operands = list(messages) + [earlier, weight]
+        in_specs = [VMEM] * len(operands)
+    else:
+        operands = list(messages) + [in_hbm(weight)]
+        in_specs = [VMEM] * len(messages) + [HBM]
+        out.append(jax.ShapeDtypeStruct((tiles, FEATURES, TILE), jnp.bfloat16))
+        scratch.append(pltpu.SemaphoreType.DMA((tiles,)))
     return pl.pallas_call(
         functools.partial(product_kernel, tiles, counts, places),
-        out_shape=[jax.ShapeDtypeStruct((members // ROW_BLOCKS, CTOK, lanes), jnp.bfloat16)] * ROW_BLOCKS
-        + [jax.ShapeDtypeStruct((MEMBERS if places else members, CTOK, TILE), jnp.bfloat16)],
+        out_shape=out,
         grid=(tiles,),
-        in_specs=[VMEM] * (len(counts) + len(earlier)) + [HBM],
-        out_specs=[VMEM] * (1 + ROW_BLOCKS),
-        scratch_shapes=[
-            pltpu.VMEM((members * (CTOK + STEPS), FEATURES), jnp.bfloat16),
-            pltpu.VMEM((TILE // 128, members * CTOK, 128), jnp.float32),
-            pltpu.VMEM((tiles, FEATURES, TILE), jnp.bfloat16),
-            pltpu.SemaphoreType.DMA((tiles,)),
-            pltpu.VMEM((members, CTOK, lanes), jnp.bfloat16),
-        ],
+        in_specs=in_specs,
+        out_specs=[VMEM] * len(out),
+        scratch_shapes=scratch,
         compiler_params=kernel_params(),
         cost_estimate=cost(2 * members * (CTOK + STEPS) * FEATURES * tiles * TILE, 12 * 10**6),
         name="block_product",
-    )(*messages, *earlier, in_hbm(blocks))
+    )(*operands)
 
 
 def sum_kernel(bias_ref, *refs):
@@ -441,41 +453,56 @@
     )(*args)
 
 
-def readout_kernel(head_ref, w_hbm, out_ref, w_ref, sem):
-    copy = pltpu.make_async_copy(w_hbm.at[0], w_ref, sem)
-    copy.start()
+def readout_kernel(head_ref, w_hbm, out_ref, w_ref, sems):
+    tiles = w_ref.shape[0]
+    copies = []
+    for i in range(tiles):
+        copies.append(
+            pltpu.make_async_copy(w_hbm.at[0, :, i * TILE : (i + 1) * TILE], w_ref.at[i], sems.at[i])
+        )
+        copies[-1].start()
     row = head_ref[pl.ds(lax.rem(lax.axis_index("tp"), COL_BLOCKS), 1), :]
     high = row.astype(jnp.bfloat16).astype(jnp.float32)
     middle = (row - high).astype(jnp.bfloat16).astype(jnp.float32)
     low = row - high - middle
     pieces = jnp.concatenate([high, middle, low, jnp.zeros((13, row.shape[1]), jnp.float32)], axis=0)
-    copy.wait()
-    prod = lax.dot_general(
-        pieces.astype(jnp.bfloat16), w_ref[...], (((1,), (1,)), ((), ())), preferred_element_type=jnp.float32
-    )
-    out_ref[...] = prod[0:1] + prod[1:2] + prod[2:3]
+    pieces = pieces.astype(jnp.bfloat16)
+    total = jnp.zeros((1, FEATURES), jnp.float32)
+    for i, copy in enumerate(copies):
+        copy.wait()
+        prod = lax.dot_general(
+            pieces[:, i * TILE : (i + 1) * TILE],
+            w_ref[i],
+            (((1,), (1,)), ((), ())),
+            preferred_element_type=jnp.float32,
+        )
+        total = total + (prod[0:1] + prod[1:2] + prod[2:3])
+    out_ref[...] = total
 
 
 def readout(value_head, blocks):
+    tiles = blocks.shape[2] // TILE
     return pl.pallas_call(
         readout_kernel,
-        out_shape=jax.ShapeDtypeStruct((1, FEATURES), jnp.float32),
-        in_specs=[whole(value_head.shape), HBM],
-        out_specs=whole((1, FEATURES)),
-        scratch_shapes=[pltpu.VMEM((FEATURES, D // COL_BLOCKS), jnp.bfloat16), pltpu.SemaphoreType.DMA],
+        out_shape=(
+            jax.ShapeDtypeStruct((1, FEATURES), jnp.float32),
+            jax.ShapeDtypeStruct((tiles, FEATURES, TILE), jnp.bfloat16),
+        ),
+        in_specs=[VMEM, HBM],
+        out_specs=(VMEM, VMEM),
+        scratch_shapes=[pltpu.SemaphoreType.DMA((tiles,))],
         compiler_params=kernel_params(),
         cost_estimate=cost(2 * 10**8, 5 * 10**6),
         name="readout",
     )(value_head, in_hbm(blocks))
 
 
-def out_kernel(tiles, x_ref, read_ref, w_hbm, *refs):
-    out_ref, rows_ref, wide_ref, read8_ref, w_ref, sems = refs[-6:]
+def out_kernel(tiles, x_ref, read_ref, w_ref, *refs):
+    out_ref, rows_ref, wide_ref, read8_ref = refs[-4:]
     n = pl.program_id(0)
     members = x_ref.shape[0]
     lines = members * STEPS
     halves = TILE // 128
-    tile = weight_tile(n, tiles, w_hbm, w_ref, sems)
 
     @pl.when(n == 0)
     def _():
@@ -489,7 +516,6 @@
                 lane = j * TILE + k * 128
                 rows_ref[:, lane : lane + 128] = wide_ref[k, pl.ds(j, lines, stride=8), :].astype(jnp.bfloat16)
 
-    tile.wait()
     prod = jnp.dot(rows_ref[...], w_ref[n], preferred_element_type=jnp.float32)
     for k in range(halves):
         wide_ref[k, pl.ds(n, lines, stride=4), :] = prod[:, k * 128 : (k + 1) * 128]
@@ -501,26 +527,24 @@
             out_ref[:, :8, k * 128 : (k + 1) * 128] = packed
 
 
-def out_product(rows, read, blocks, after):
+def out_product(rows, read, weight, after):
     members = rows.shape[0]
-    tiles = blocks.shape[2] // TILE
+    tiles = weight.shape[0]
     return pl.pallas_call(
         functools.partial(out_kernel, tiles),
         out_shape=jax.ShapeDtypeStruct((members, 16, TILE), jnp.float32),
         grid=(tiles,),
-        in_specs=[whole(rows.shape), whole(read.shape), HBM] + [UNREAD] * len(after),
-        out_specs=whole((members, 16, TILE)),
+        in_specs=[VMEM] * 3 + [UNREAD] * len(after),
+        out_specs=VMEM,
         scratch_shapes=[
             pltpu.VMEM((members * STEPS, FEATURES), jnp.bfloat16),
             pltpu.VMEM((TILE // 128, members * 16, 128), jnp.float32),
             pltpu.VMEM((8, TILE), jnp.float32),
-            pltpu.VMEM((tiles, FEATURES, TILE), jnp.bfloat16),
-            pltpu.SemaphoreType.DMA((tiles,)),
         ],
         compiler_params=kernel_params(),
         cost_estimate=cost(3 * 10**8, 5 * 10**6),
         name="out_product",
-    )(rows, read, in_hbm(blocks), *after)
+    )(rows, read, weight, *after)
 
 
 def finish_kernel(parts_ref, main_ref, cont_ref, head_ref, mixed_ref, out_ref, score_ref, wide_ref):
@@ -603,9 +627,9 @@
     after, before = from_side(near, 0, 1), from_side(near, 0, 3)
     over_after, over_before = from_side(over, 0, 1), from_side(over, 0, 3)
     far = [from_side(before, 0, 3), from_side(over_after, 0, 1)]
-    *first, main = block_product([near, over, after, before], blocks)
+    *first, main, weight = block_product([near, over, after, before], blocks)
     first = [first[0]] + [from_along(first[k], -k) for k in range(1, ROW_BLOCKS)]
-    *second, main = block_product([over_after, over_before] + far, blocks, (main,), HOMES)
+    *second, main = block_product([over_after, over_before] + far, weight, main, HOMES)
     main, first = lax.optimization_barrier((main, first))
     second = [second[0]] + [from_along(second[k], -k) for k in range(1, ROW_BLOCKS)]
     received = []
@@ -626,12 +650,12 @@
     step = jnp.arange(CTOK, dtype=jnp.int32) % STEPS
     main_tables = rope_tables(prefix_len + step[:8])
     cont_tables = rope_tables(prefix_len + boundary + step)
-    read = readout(value_head.reshape(COL_BLOCKS, D // COL_BLOCKS), w_out)
+    read, out_weight = readout(value_head.reshape(COL_BLOCKS, D // COL_BLOCKS), w_out)
     parts, main_parts, before = project(norm_rows(main, cont, rms_gain[None, :]), w_qkv, bias)
     mixed, main_kv = attend_main(prefix_len, bias, *main_tables, cache, main_parts, before + [read])
     mixed = exchange(mixed)
     cont_mixed = attend_cont(prefix_len, boundary, bias, *cont_tables, cache, main_kv, *parts)
-    parts = exchange(out_product(mixed, read, w_out, parts[4:6]))
+    parts = exchange(out_product(mixed, read, out_weight, parts[4:6]))
     main_out, score = finish(parts, main, cont, head, cont_mixed)
     return main_out[None], score[0, :1]
 

time: 113 us -> 113 us (level)
  local copies, waits for them, and re-layouts: 1.18 us -> 4.71 us
  Pallas kernels: 25.5 us -> 22.2 us
  waiting for transfers between devices: 21.3 us -> 19.9 us
  starting transfers between devices: 49.9 us -> 51.1 us
    unnamed x12 -> x14, local copies, waits for them, and re-layouts: 0.65 us -> 4.18 us
    all_to_all x3, waiting for transfers between devices: 3.18 us -> 1.8 us  [exchange(): return lax.all_to_all(rows, 'tp', split_axis=0, concat_axis=0, tiled=True)]
    all_to_all x3, starting transfers between devices: 17.8 us -> 19 us  [exchange(): return lax.all_to_all(rows, 'tp', split_axis=0, concat_axis=0, tiled=True)]
    pallas_call x1, Pallas kernels: 3.38 us -> 2.23 us  [out_product(): pl.pallas_call(functools.partial(out_kernel, tiles), out_shape=jax.ShapeD...]
  transfers between devices with their start and end apart: 23 -> 23, of which waited for: 10 -> 10; matrix products, arithmetic and copies ran while one was open for 0% -> 0% of each run, Pallas kernels for 14% -> 12%
where the time goes in v17:
time: 113 us
  starting transfers between devices  51.1 us (45%)
  Pallas kernels  22.2 us (20%)
  waiting for transfers between devices  19.9 us (18%)
  blocking collectives  12.2 us (11%)
  local copies, waits for them, and re-layouts  4.71 us (4%)
  between operations  2.12 us (2%)
    ppermute x14, starting transfers between devices, from_side(): return lax.ppermute(rows, 'tp', route)  23.2 us
    all_to_all x3, starting transfers between devices, exchange(): return lax.all_to_all(rows, 'tp', split_axis=0, concat_axis=0, tiled=True)  19 us
    ppermute x14, waiting for transfers between devices, from_side(): return lax.ppermute(rows, 'tp', route)  18.1 us
    all_to_all x1, blocking collectives, project(): lax.all_to_all(rows, 'tp', split_axis=0, concat_axis=0, tiled=True, axis_...  12.2 us
    ppermute x6, starting transfers between devices, from_along(): return lax.ppermute(rows, 'tp', route)  8.86 us
    pallas_call x2, Pallas kernels, block_product(): pl.pallas_call(functools.partial(product_kernel, tiles, counts, places),...  7.69 us
    unnamed x14, local copies, waits for them, and re-layouts  4.18 us
    pallas_call x1, Pallas kernels, attend_main(): pl.pallas_call(attend_main_kernel, out_shape=(jax.ShapeDtypeStruct((32, 1...  3.7 us
  transfers between devices with their start and end apart: 23, of which 10 were waited for; matrix products, arithmetic and copies ran while one was open for 0% of the time, Pallas kernels for 12%

profile of v17, /device:TPU:0, one launch (start us, length us, event | category | flops | bytes accessed | tf_op | source)
XLA Modules:
  0.0 112.7 jit_solution(7681351350993464605)
XLA Ops:
  2.0 12.2 %all_to_all.20.refs_0_ = bf16[4,16,2304]{2,1,0:T(8,128)(2,1)S(1)} all-to-all(bf16[4,16,2304]{2,1,0:T(8,128)(2,1)S(1)} %norm_rows.1), channel_id=1, replica_groups={{0,8,16,24},{1,9,17,25},{2,10,18,26},{3,11,19,27},{4,12,20,28},{5,13,21..., dimensions={0} | all-to-all | bytes 589824 | tf_op jit(solution)/shard_map/all_to_all | solution.py:625
  17.3 1.7 %collective-permute-start.6 = (bf16[4,16,2304]{2,1,0:T(8,128)(2,1)S(1)}, bf16[4,16,2304]{2,1,0:T(8,128)(2,1)S(1)}, u32[]{:S(2)}, u32[]{:S(2)}) collective-permute-start(bf16[4,16,2304]{2,1,0:T(8,128)(2,1)S(1)} %all_to_all.20.refs_0_), channel_id=1, source_target_pairs={{1,0},{2,1},{3,2},{0,3},{5,4},{6,5},{7,6},{4,7},{9,8},{10,9},{11,1... | collective-permute-start | bytes 884744 | tf_op jit(solution)/shard_map/ppermute | solution.py:611
  19.1 2.4 %collective-permute-done.refs_1_ = bf16[4,16,2304]{2,1,0:T(8,128)(2,1)S(1)} collective-permute-done((bf16[4,16,2304]{2,1,0:T(8,128)(2,1)S(1)}, bf16[4,16,2304]{2,1,0:T(8,128)(2,1)S(1)}, u32[]{:S(2)}, u32[]{:S(2)}) %collective-permute-start) | collective-permute-done | bytes 294944 | tf_op jit(solution)/shard_map/ppermute | solution.py:611
  21.5 2.8 %collective-permute-start.1 = (bf16[4,16,2304]{2,1,0:T(8,128)(2,1)S(1)}, bf16[4,16,2304]{2,1,0:T(8,128)(2,1)S(1)}, u32[]{:S(2)}, u32[]{:S(2)}) collective-permute-start(bf16[4,16,2304]{2,1,0:T(8,128)(2,1)S(1)} %collective-permute-done.refs_1_), channel_id=1, source_target_pairs={{1,0},{2,1},{3,2},{0,3},{5,4},{6,5},{7,6},{4,7},{9,8},{10,9},{11,1... | collective-permute-start | bytes 884744 | tf_op jit(solution)/shard_map/ppermute | solution.py:611
  26.6 3.9 %block_product.2 = (bf16[4,16,2048]{2,1,0:T(8,128)(2,1)S(1)}, bf16[4,16,2048]{2,1,0:T(8,128)(2,1)S(1)}, bf16[4,16,2048]{2,1,0:T(8,128)(2,1)S(1)}, bf16[4,16,2048...) custom-call(bf16[4,16,2304]{2,1,0:T(8,128)(2,1)S(1)} %all_to_all.20.refs_0_, ...), custom_call_target="tpu_custom_call" | custom-call | flops 1509949440 | bytes 12000000 | tf_op jit(solution)/shard_map/block_product/pallas_call | solution.py:217
  31.2 2.1 %collective-permute-start.8 = (bf16[4,16,2048]{2,1,0:T(8,128)(2,1)S(1)}, bf16[4,16,2048]{2,1,0:T(8,128)(2,1)S(1)}, u32[]{:S(2)}, u32[]{:S(2)}) collective-permute-start(bf16[4,16,2048]{2,1,0:T(8,128)(2,1)S(1)} %get-tuple-element.37), channel_id=1, source_target_pairs={{16,0},{17,1},{18,2},{19,3},{20,4},{21,5},{22,6},{23,7},{24,8},{25... | collective-permute-start | bytes 786440 | tf_op jit(solution)/shard_map/ppermute | solution.py:616
  37.5 4.7 %collective-permute-done.4.refs_2_ = bf16[4,16,2304]{2,1,0:T(8,128)(2,1)S(1)} collective-permute-done((bf16[4,16,2304]{2,1,0:T(8,128)(2,1)S(1)}, bf16[4,16,2304]{2,1,0:T(8,128)(2,1)S(1)}, u32[]{:S(2)}, u32[]{:S(2)}) %collective-permute-start.4) | collective-permute-done | bytes 294944 | tf_op jit(solution)/shard_map/ppermute | solution.py:611
  42.4 3.8 %block_product.3 = (bf16[4,16,2048]{2,1,0:T(8,128)(2,1)S(1)}, bf16[4,16,2048]{2,1,0:T(8,128)(2,1)}, bf16[4,16,2048]{2,1,0:T(8,128)(2,1)}, bf16[4,16,2048]{2,1,0:T(8,128)(2,1)S(1)}, bf16[32,16,256]{2,1,0:T(8,128)(2,1)}) custom-call(bf16[4,16,2304]{2,1,0:T(8,128)(2,1)S(1)} %collective-permute-done.1.refs_0_, ...), custom_call_target="tpu_custom_call" | custom-call | flops 1509949440 | bytes 12000000 | tf_op jit(solution)/shard_map/block_product/pallas_call | solution.py:217
  48.8 2.6 %collective-permute-start.12 = (bf16[4,16,2048]{2,1,0:T(8,128)(2,1)S(1)}, bf16[4,16,2048]{2,1,0:T(8,128)(2,1)S(1)}, u32[]{:S(2)}, u32[]{:S(2)}) collective-permute-start(bf16[4,16,2048]{2,1,0:T(8,128)(2,1)S(1)} %get-tuple-element.42), channel_id=1, source_target_pairs={{8,0},{9,1},{10,2},{11,3},{12,4},{13,5},{14,6},{15,7},{16,8},{17,9... | collective-permute-start | bytes 786440 | tf_op jit(solution)/shard_map/ppermute | solution.py:616
  51.7 6.5 %all-to-all-start.1 = ((bf16[32,16,256]{2,1,0:T(8,128)(2,1)}), bf16[32,16,256]{2,1,0:T(8,128)(2,1)S(1)}, u32[]{:S(2)}, u32[]{:S(2)}) async-start(bf16[32,16,256]{2,1,0:T(8,128)(2,1)} %get-tuple-element.39), calls=%async_computation.1 | async-start | bytes 524288 | tf_op jit(solution)/shard_map/all_to_all | solution.py:600
  58.3 1.9 %collective-permute-start.14 = (bf16[16,2048]{1,0:T(8,128)(2,1)S(1)}, bf16[16,2048]{1,0:T(8,128)(2,1)S(1)}, u32[]{:S(2)}, u32[]{:S(2)}) collective-permute-start(bf16[16,2048]{1,0:T(8,128)(2,1)S(1)} %get-tuple-element.48), channel_id=1, source_target_pairs={{3,0},{0,1},{1,2},{2,3},{7,4},{4,5},{5,6},{6,7},{11,8},{8,9},{9,10... | collective-permute-start | bytes 196616 | tf_op jit(solution)/shard_map/ppermute | solution.py:611
  61.7 2.8 %readout.1 = (f32[1,2048]{1,0:T(1,128)S(1)}, bf16[4,2048,256]{2,1,0:T(8,128)(2,1)S(1)}) custom-call(f32[8,1024]{1,0:T(8,128)S(1)} %reshape.34.head_ref, bf16[1,2048,1024]{2,1,0:T(8,128)(2,1)} %w_hbm.1), custom_call_target="tpu_custom_call" | custom-call | flops 200000000 | bytes 5000000 | tf_op jit(solution)/shard_map/readout/pallas_call | solution.py:485
  64.6 2.0 %copy-done.1 = bf16[4,2048,256]{2,1,0:T(8,128)(2,1)} copy-done((bf16[4,2048,256]{2,1,0:T(8,128)(2,1)}, bf16[4,2048,256]{2,1,0:T(8,128)(2,1)S(1)}, u32[]{:S(2)}) %copy-start.1) | copy-done | bytes 4194328
  67.5 3.7 %attend_main.1 = (bf16[32,16,256]{2,1,0:T(8,128)(2,1)}, f32[8,2048]{1,0:T(8,128)S(1)}) custom-call(s32[1]{0:T(128)} %copy.12.len_ref, f32[1,10240]{1,0:T(1,128)S(1)} %bitcast.16, f32[8,128]{1,0:T(8,128)S(1)} %get-tuple-element.68.cos_ref, f32[8,128]{1,0:T(8,128)S(1)} %get-tuple-element.69.sin_ref, bf16[256,2048]{1,0:T(8,128)(2,1)S(1)} %bitcast.11, ...), custom_call_target="tpu_custom_call" | custom-call | flops 200000000 | bytes 6000000 | tf_op jit(solution)/shard_map/attend_main/pallas_call | solution.py:395
  71.2 6.3 %all-to-all-start.2 = ((bf16[32,16,256]{2,1,0:T(8,128)(2,1)}), bf16[32,16,256]{2,1,0:T(8,128)(2,1)S(1)}, u32[]{:S(2)}, u32[]{:S(2)}) async-start(bf16[32,16,256]{2,1,0:T(8,128)(2,1)} %get-tuple-element.51), calls=%async_computation.2 | async-start | bytes 524288 | tf_op jit(solution)/shard_map/all_to_all | solution.py:600
  77.7 2.8 %collective-permute-start.16 = (bf16[16,2048]{1,0:T(8,128)(2,1)S(1)}, bf16[16,2048]{1,0:T(8,128)(2,1)S(1)}, u32[]{:S(2)}, u32[]{:S(2)}) collective-permute-start(bf16[16,2048]{1,0:T(8,128)(2,1)S(1)} %get-tuple-element.54), channel_id=1, source_target_pairs={{7,0},{4,1},{5,2},{6,3},{3,4},{0,5},{1,6},{2,7},{15,8},{12,9},{13,... | collective-permute-start | bytes 196616 | tf_op jit(solution)/shard_map/ppermute | solution.py:611
  81.9 3.4 %collective-permute-done.16.refs_0_.refs_4_ = bf16[16,2048]{1,0:T(8,128)(2,1)S(1)} collective-permute-done((bf16[16,2048]{1,0:T(8,128)(2,1)S(1)}, bf16[16,2048]{1,0:T(8,128)(2,1)S(1)}, u32[]{:S(2)}, u32[]{:S(2)}) %collective-permute-start.16) | collective-permute-done | bytes 65568 | tf_op jit(solution)/shard_map/ppermute | solution.py:611
  86.7 2.2 %copy-done.2 = bf16[4,2048,256]{2,1,0:T(8,128)(2,1)S(1)} copy-done((bf16[4,2048,256]{2,1,0:T(8,128)(2,1)S(1)}, bf16[4,2048,256]{2,1,0:T(8,128)(2,1)}, u32[]{:S(2)}) %copy-start.2) | copy-done | bytes 4194328
  88.9 2.2 %out_product.1 = f32[32,16,256]{2,1,0:T(8,128)} custom-call(bf16[32,16,256]{2,1,0:T(8,128)(2,1)S(1)} %all-to-all-done.2.x_ref, f32[1,2048]{1,0:T(1,128)S(1)} %get-tuple-element.50.refs_6_.read_ref, bf16[4,2048,256]{2,1,0:T(8,128)(2,1)S(1)} %copy-done.2, bf16[16,2048]{1,0:T(8,128)(2,1)S(1)} %collective-permute-done.16.refs_0_.refs_4_, ...), custom_call_target="tpu_custom_call" | custom-call | flops 300000000 | bytes 5000000 | tf_op jit(solution)/shard_map/out_product/pallas_call | solution.py:533
  91.2 6.2 %all-to-all-start.3 = ((f32[32,16,256]{2,1,0:T(8,128)}), f32[32,16,256]{2,1,0:T(8,128)S(1)}, u32[]{:S(2)}, u32[]{:S(2)}) async-start(f32[32,16,256]{2,1,0:T(8,128)} %out_product.1), calls=%async_computation.3 | async-start | bytes 1048576 | tf_op jit(solution)/shard_map/all_to_all | solution.py:600
  98.1 3.4 %collective-permute-start.18 = (bf16[16,2048]{1,0:T(8,128)(2,1)S(1)}, bf16[16,2048]{1,0:T(8,128)(2,1)S(1)}, u32[]{:S(2)}, u32[]{:S(2)}) collective-permute-start(bf16[16,2048]{1,0:T(8,128)(2,1)S(1)} %get-tuple-element.58), channel_id=1, source_target_pairs={{2,0},{3,1},{0,2},{1,3},{6,4},{7,5},{4,6},{5,7},{10,8},{11,9},{8,1... | collective-permute-start | bytes 196616 | tf_op jit(solution)/shard_map/ppermute | solution.py:611
  103.0 2.7 %collective-permute-done.18.refs_6_ = bf16[16,2048]{1,0:T(8,128)(2,1)S(1)} collective-permute-done((bf16[16,2048]{1,0:T(8,128)(2,1)S(1)}, bf16[16,2048]{1,0:T(8,128)(2,1)S(1)}, u32[]{:S(2)}, u32[]{:S(2)}) %collective-permute-start.18) | collective-permute-done | bytes 65568 | tf_op jit(solution)/shard_map/ppermute | solution.py:611
  105.8 2.4 %collective-permute-done.19.refs_7_ = bf16[16,2048]{1,0:T(8,128)(2,1)S(1)} collective-permute-done((bf16[16,2048]{1,0:T(8,128)(2,1)S(1)}, bf16[16,2048]{1,0:T(8,128)(2,1)S(1)}, u32[]{:S(2)}, u32[]{:S(2)}) %collective-permute-start.19) | collective-permute-done | bytes 65568 | tf_op jit(solution)/shard_map/ppermute | solution.py:611
  108.2 3.0 %attend_cont.1.mixed_ref = bf16[16,8192]{1,0:T(8,128)(2,1)S(1)} custom-call(s32[1]{0:T(128)} %copy.12.len_ref, s32[1]{0:T(128)S(6)} %copy.13.bound_ref, f32[1,10240]{1,0:T(1,128)S(1)} %bitcast.18, f32[16,128]{1,0:T(8,128)S(1)} %get-tuple-element.70.cos_ref, f32[16,128]{1,0:T(8,128)S(1)} %get-tuple-element.71.sin_ref, bf16[256,2048]{1,0:T(8,128)(2,1)S(1)} %bitcast.12, ...), custom_call_target="tpu_custom_call" | custom-call | flops 400000000 | bytes 8000000 | tf_op jit(solution)/shard_map/attend_cont/pallas_call | solution.py:441
  (57 shorter events, 22.8 us)
Async XLA Ops:
  14.2 7.3 %collective-permute-start = (bf16[4,16,2304]{2,1,0:T(8,128)(2,1)S(1)}, bf16[4,16,2304]{2,1,0:T(8,128)(2,1)S(1)}, u32[]{:S(2)}, u32[]{:S(2)}) collective-permute-start(bf16[4,16,2304]{2,1,0:T(8,128)(2,1)S(1)} %all_to_all.20.refs_0_), channel_id=1, source_target_pairs={{4,0},{5,1},{6,2},{7,3},{0,4},{1,5},{2,6},{3,7},{12,8},{13,9},{14,... | collective-permute-start | bytes 884744 | tf_op jit(solution)/shard_map/ppermute | solution.py:611
  15.8 9.1 %collective-permute-start.3 = (bf16[4,16,2304]{2,1,0:T(8,128)(2,1)S(1)}, bf16[4,16,2304]{2,1,0:T(8,128)(2,1)S(1)}, u32[]{:S(2)}, u32[]{:S(2)}) collective-permute-start(bf16[4,16,2304]{2,1,0:T(8,128)(2,1)S(1)} %all_to_all.20.refs_0_), channel_id=1, source_target_pairs={{3,0},{0,1},{1,2},{2,3},{7,4},{4,5},{5,6},{6,7},{11,8},{8,9},{9,10... | collective-permute-start | bytes 884744 | tf_op jit(solution)/shard_map/ppermute | solution.py:611
  17.3 9.3 %collective-permute-start.6 = (bf16[4,16,2304]{2,1,0:T(8,128)(2,1)S(1)}, bf16[4,16,2304]{2,1,0:T(8,128)(2,1)S(1)}, u32[]{:S(2)}, u32[]{:S(2)}) collective-permute-start(bf16[4,16,2304]{2,1,0:T(8,128)(2,1)S(1)} %all_to_all.20.refs_0_), channel_id=1, source_target_pairs={{1,0},{2,1},{3,2},{0,3},{5,4},{6,5},{7,6},{4,7},{9,8},{10,9},{11,1... | collective-permute-start | bytes 884744 | tf_op jit(solution)/shard_map/ppermute | solution.py:611
  21.5 12.7 %collective-permute-start.1 = (bf16[4,16,2304]{2,1,0:T(8,128)(2,1)S(1)}, bf16[4,16,2304]{2,1,0:T(8,128)(2,1)S(1)}, u32[]{:S(2)}, u32[]{:S(2)}) collective-permute-start(bf16[4,16,2304]{2,1,0:T(8,128)(2,1)S(1)} %collective-permute-done.refs_1_), channel_id=1, source_target_pairs={{1,0},{2,1},{3,2},{0,3},{5,4},{6,5},{7,6},{4,7},{9,8},{10,9},{11,1... | collective-permute-start | bytes 884744 | tf_op jit(solution)/shard_map/ppermute | solution.py:611
  24.3 11.4 %collective-permute-start.2 = (bf16[4,16,2304]{2,1,0:T(8,128)(2,1)S(1)}, bf16[4,16,2304]{2,1,0:T(8,128)(2,1)S(1)}, u32[]{:S(2)}, u32[]{:S(2)}) collective-permute-start(bf16[4,16,2304]{2,1,0:T(8,128)(2,1)S(1)} %collective-permute-done.refs_1_), channel_id=1, source_target_pairs={{3,0},{0,1},{1,2},{2,3},{7,4},{4,5},{5,6},{6,7},{11,8},{8,9},{9,10... | collective-permute-start | bytes 884744 | tf_op jit(solution)/shard_map/ppermute | solution.py:611
  30.5 18.2 %collective-permute-start.7 = (bf16[4,16,2048]{2,1,0:T(8,128)(2,1)S(1)}, bf16[4,16,2048]{2,1,0:T(8,128)(2,1)S(1)}, u32[]{:S(2)}, u32[]{:S(2)}) collective-permute-start(bf16[4,16,2048]{2,1,0:T(8,128)(2,1)S(1)} %get-tuple-element.36), channel_id=1, source_target_pairs={{24,0},{25,1},{26,2},{27,3},{28,4},{29,5},{30,6},{31,7},{0,8},{1,9... | collective-permute-start | bytes 786440 | tf_op jit(solution)/shard_map/ppermute | solution.py:616
  31.2 20.2 %collective-permute-start.8 = (bf16[4,16,2048]{2,1,0:T(8,128)(2,1)S(1)}, bf16[4,16,2048]{2,1,0:T(8,128)(2,1)S(1)}, u32[]{:S(2)}, u32[]{:S(2)}) collective-permute-start(bf16[4,16,2048]{2,1,0:T(8,128)(2,1)S(1)} %get-tuple-element.37), channel_id=1, source_target_pairs={{16,0},{17,1},{18,2},{19,3},{20,4},{21,5},{22,6},{23,7},{24,8},{25... | collective-permute-start | bytes 786440 | tf_op jit(solution)/shard_map/ppermute | solution.py:616
  33.2 18.2 %collective-permute-start.9 = (bf16[4,16,2048]{2,1,0:T(8,128)(2,1)S(1)}, bf16[4,16,2048]{2,1,0:T(8,128)(2,1)S(1)}, u32[]{:S(2)}, u32[]{:S(2)}) collective-permute-start(bf16[4,16,2048]{2,1,0:T(8,128)(2,1)S(1)} %get-tuple-element.38), channel_id=1, source_target_pairs={{8,0},{9,1},{10,2},{11,3},{12,4},{13,5},{14,6},{15,7},{16,8},{17,9... | collective-permute-start | bytes 786440 | tf_op jit(solution)/shard_map/ppermute | solution.py:616
  34.2 7.9 %collective-permute-start.4 = (bf16[4,16,2304]{2,1,0:T(8,128)(2,1)S(1)}, bf16[4,16,2304]{2,1,0:T(8,128)(2,1)S(1)}, u32[]{:S(2)}, u32[]{:S(2)}) collective-permute-start(bf16[4,16,2304]{2,1,0:T(8,128)(2,1)S(1)} %collective-permute-done.3.refs_3_), channel_id=1, source_target_pairs={{3,0},{0,1},{1,2},{2,3},{7,4},{4,5},{5,6},{6,7},{11,8},{8,9},{9,10... | collective-permute-start | bytes 884744 | tf_op jit(solution)/shard_map/ppermute | solution.py:611
  35.7 6.7 %collective-permute-start.5 = (bf16[4,16,2304]{2,1,0:T(8,128)(2,1)S(1)}, bf16[4,16,2304]{2,1,0:T(8,128)(2,1)S(1)}, u32[]{:S(2)}, u32[]{:S(2)}) collective-permute-start(bf16[4,16,2304]{2,1,0:T(8,128)(2,1)S(1)} %collective-permute-done.1.refs_0_), channel_id=1, source_target_pairs={{1,0},{2,1},{3,2},{0,3},{5,4},{6,5},{7,6},{4,7},{9,8},{10,9},{11,1... | collective-permute-start | bytes 884744 | tf_op jit(solution)/shard_map/ppermute | solution.py:611
  46.2 21.2 %collective-permute-start.10 = (bf16[4,16,2048]{2,1,0:T(8,128)(2,1)}, bf16[4,16,2048]{2,1,0:T(8,128)(2,1)S(1)}, u32[]{:S(2)}, u32[]{:S(2)}) collective-permute-start(bf16[4,16,2048]{2,1,0:T(8,128)(2,1)} %get-tuple-element.40), channel_id=1, source_target_pairs={{24,0},{25,1},{26,2},{27,3},{28,4},{29,5},{30,6},{31,7},{0,8},{1,9... | collective-permute-start | bytes 786440 | tf_op jit(solution)/shard_map/ppermute | solution.py:616
  47.2 20.2 %collective-permute-start.11 = (bf16[4,16,2048]{2,1,0:T(8,128)(2,1)}, bf16[4,16,2048]{2,1,0:T(8,128)(2,1)S(1)}, u32[]{:S(2)}, u32[]{:S(2)}) collective-permute-start(bf16[4,16,2048]{2,1,0:T(8,128)(2,1)} %get-tuple-element.41), channel_id=1, source_target_pairs={{16,0},{17,1},{18,2},{19,3},{20,4},{21,5},{22,6},{23,7},{24,8},{25... | collective-permute-start | bytes 786440 | tf_op jit(solution)/shard_map/ppermute | solution.py:616
  48.8 18.7 %collective-permute-start.12 = (bf16[4,16,2048]{2,1,0:T(8,128)(2,1)S(1)}, bf16[4,16,2048]{2,1,0:T(8,128)(2,1)S(1)}, u32[]{:S(2)}, u32[]{:S(2)}) collective-permute-start(bf16[4,16,2048]{2,1,0:T(8,128)(2,1)S(1)} %get-tuple-element.42), channel_id=1, source_target_pairs={{8,0},{9,1},{10,2},{11,3},{12,4},{13,5},{14,6},{15,7},{16,8},{17,9... | collective-permute-start | bytes 786440 | tf_op jit(solution)/shard_map/ppermute | solution.py:616
  51.6 8.6 %collective-permute-start.13 = (bf16[16,2048]{1,0:T(8,128)(2,1)S(1)}, bf16[16,2048]{1,0:T(8,128)(2,1)S(1)}, u32[]{:S(2)}, u32[]{:S(2)}) collective-permute-start(bf16[16,2048]{1,0:T(8,128)(2,1)S(1)} %get-tuple-element.47), channel_id=1, source_target_pairs={{4,0},{5,1},{6,2},{7,3},{0,4},{1,5},{2,6},{3,7},{12,8},{13,9},{14,... | collective-permute-start | bytes 196616 | tf_op jit(solution)/shard_map/ppermute | solution.py:611
  51.7 15.7 %all-to-all-start.1 = ((bf16[32,16,256]{2,1,0:T(8,128)(2,1)}), bf16[32,16,256]{2,1,0:T(8,128)(2,1)S(1)}, u32[]{:S(2)}, u32[]{:S(2)}) async-start(bf16[32,16,256]{2,1,0:T(8,128)(2,1)} %get-tuple-element.39), calls=%async_computation.1 | async-start | bytes 524288 | tf_op jit(solution)/shard_map/all_to_all | solution.py:600
  58.3 8.2 %collective-permute-start.14 = (bf16[16,2048]{1,0:T(8,128)(2,1)S(1)}, bf16[16,2048]{1,0:T(8,128)(2,1)S(1)}, u32[]{:S(2)}, u32[]{:S(2)}) collective-permute-start(bf16[16,2048]{1,0:T(8,128)(2,1)S(1)} %get-tuple-element.48), channel_id=1, source_target_pairs={{3,0},{0,1},{1,2},{2,3},{7,4},{4,5},{5,6},{6,7},{11,8},{8,9},{9,10... | collective-permute-start | bytes 196616 | tf_op jit(solution)/shard_map/ppermute | solution.py:611
  60.2 6.4 %collective-permute-start.15 = (bf16[16,2048]{1,0:T(8,128)(2,1)S(1)}, bf16[16,2048]{1,0:T(8,128)(2,1)S(1)}, u32[]{:S(2)}, u32[]{:S(2)}) collective-permute-start(bf16[16,2048]{1,0:T(8,128)(2,1)S(1)} %get-tuple-element.49), channel_id=1, source_target_pairs={{1,0},{2,1},{3,2},{0,3},{5,4},{6,5},{7,6},{4,7},{9,8},{10,9},{11,1... | collective-permute-start | bytes 196616 | tf_op jit(solution)/shard_map/ppermute | solution.py:611
  71.2 40.1 %copy-start.5 = (bf16[1,2,8192]{2,1,0:T(2,128)(2,1)S(1)}, bf16[1,2,8192]{2,1,0:T(2,128)(2,1)}, u32[]{:S(2)}) copy-start(bf16[1,2,8192]{2,1,0:T(2,128)(2,1)} %param.10) | copy-start | bytes 98308
  71.2 15.6 %all-to-all-start.2 = ((bf16[32,16,256]{2,1,0:T(8,128)(2,1)}), bf16[32,16,256]{2,1,0:T(8,128)(2,1)S(1)}, u32[]{:S(2)}, u32[]{:S(2)}) async-start(bf16[32,16,256]{2,1,0:T(8,128)(2,1)} %get-tuple-element.51), calls=%async_computation.2 | async-start | bytes 524288 | tf_op jit(solution)/shard_map/all_to_all | solution.py:600
  77.7 7.7 %collective-permute-start.16 = (bf16[16,2048]{1,0:T(8,128)(2,1)S(1)}, bf16[16,2048]{1,0:T(8,128)(2,1)S(1)}, u32[]{:S(2)}, u32[]{:S(2)}) collective-permute-start(bf16[16,2048]{1,0:T(8,128)(2,1)S(1)} %get-tuple-element.54), channel_id=1, source_target_pairs={{7,0},{4,1},{5,2},{6,3},{3,4},{0,5},{1,6},{2,7},{15,8},{12,9},{13,... | collective-permute-start | bytes 196616 | tf_op jit(solution)/shard_map/ppermute | solution.py:611
  80.5 5.4 %collective-permute-start.17 = (bf16[16,2048]{1,0:T(8,128)(2,1)S(1)}, bf16[16,2048]{1,0:T(8,128)(2,1)S(1)}, u32[]{:S(2)}, u32[]{:S(2)}) collective-permute-start(bf16[16,2048]{1,0:T(8,128)(2,1)S(1)} %get-tuple-element.55), channel_id=1, source_target_pairs={{5,0},{6,1},{7,2},{4,3},{1,4},{2,5},{3,6},{0,7},{13,8},{14,9},{15,... | collective-permute-start | bytes 196616 | tf_op jit(solution)/shard_map/ppermute | solution.py:611
  91.2 20.1 %all-to-all-start.3 = ((f32[32,16,256]{2,1,0:T(8,128)}), f32[32,16,256]{2,1,0:T(8,128)S(1)}, u32[]{:S(2)}, u32[]{:S(2)}) async-start(f32[32,16,256]{2,1,0:T(8,128)} %out_product.1), calls=%async_computation.3 | async-start | bytes 1048576 | tf_op jit(solution)/shard_map/all_to_all | solution.py:600
  98.1 7.7 %collective-permute-start.18 = (bf16[16,2048]{1,0:T(8,128)(2,1)S(1)}, bf16[16,2048]{1,0:T(8,128)(2,1)S(1)}, u32[]{:S(2)}, u32[]{:S(2)}) collective-permute-start(bf16[16,2048]{1,0:T(8,128)(2,1)S(1)} %get-tuple-element.58), channel_id=1, source_target_pairs={{2,0},{3,1},{0,2},{1,3},{6,4},{7,5},{4,6},{5,7},{10,8},{11,9},{8,1... | collective-permute-start | bytes 196616 | tf_op jit(solution)/shard_map/ppermute | solution.py:611
  101.5 6.7 %collective-permute-start.19 = (bf16[16,2048]{1,0:T(8,128)(2,1)S(1)}, bf16[16,2048]{1,0:T(8,128)(2,1)S(1)}, u32[]{:S(2)}, u32[]{:S(2)}) collective-permute-start(bf16[16,2048]{1,0:T(8,128)(2,1)S(1)} %get-tuple-element.59), channel_id=1, source_target_pairs={{6,0},{7,1},{4,2},{5,3},{2,4},{3,5},{0,6},{1,7},{14,8},{15,9},{12,... | collective-permute-start | bytes 196616 | tf_op jit(solution)/shard_map/ppermute | solution.py:611
  (6 other events, 126.9 us)

commit v18 on v15

--- a/solution.py
+++ b/solution.py
@@ -25,7 +25,7 @@
 EPS = 1e-06
 MASKED_SCORE = -1e30
 
-VMEM_LIMIT = 32 * 1024 * 1024
+VMEM_LIMIT = 28 * 1024 * 1024
 VMEM = pl.BlockSpec(memory_space=pltpu.VMEM)
 SMEM = pl.BlockSpec(memory_space=pltpu.SMEM)
 HBM = pl.BlockSpec(memory_space=pltpu.HBM)
@@ -123,16 +123,19 @@
 def product_kernel(tiles, counts, places, *refs):
     x_refs, refs = refs[: len(counts)], refs[len(counts) :]
     if places:
-        earlier_ref, refs = refs[0], refs[1:]
-    w_hbm, *out_refs = refs[: 1 + ROW_BLOCKS]
-    main_ref, rows_ref, wide_ref, w_ref, sems, part_ref = refs[1 + ROW_BLOCKS :]
+        earlier_ref, w_ref, *out_refs = refs[: 2 + ROW_BLOCKS]
+        main_ref, rows_ref, wide_ref, part_ref = refs[2 + ROW_BLOCKS :]
+    else:
+        w_hbm, *out_refs = refs[: 1 + ROW_BLOCKS]
+        main_ref, w_ref, rows_ref, wide_ref, part_ref, sems = refs[1 + ROW_BLOCKS :]
     n = pl.program_id(0)
     members = sum(counts)
     count = members * CTOK
     lines = members * STEPS
     halves = TILE // 128
     width = tiles * TILE
-    tile = weight_tile(n, tiles, w_hbm, w_ref, sems)
+    if not places:
+        tile = weight_tile(n, tiles, w_hbm, w_ref, sems)
 
     @pl.when(n == 0)
     def _():
@@ -149,7 +152,8 @@
                 lane = j * TILE + k * 128
                 rows_ref[count:, lane : lane + 128] = wide_ref[k, pl.ds(j, lines, stride=8), :].astype(jnp.bfloat16)
 
-    tile.wait()
+    if not places:
+        tile.wait()
     prod = jnp.dot(rows_ref[...], w_ref[n], preferred_element_type=jnp.float32)
     high = prod.astype(jnp.bfloat16)
     part_ref[:, :, pl.ds(pl.multiple_of(n * TILE, TILE), TILE)] = high[:count].reshape(members, CTOK, TILE)
@@ -190,29 +194,37 @@
                 out_ref[g] = part_ref[g * ROW_BLOCKS + to]
 
 
-def block_product(messages, blocks, earlier=(), places=()):
-    tiles = blocks.shape[2] // TILE
+def block_product(messages, weight, earlier=None, places=()):
+    tiles = QKV // COL_BLOCKS // TILE
     lanes = tiles * TILE + REST
     counts = tuple(rows.shape[0] for rows in messages)
     members = sum(counts)
+    out = [jax.ShapeDtypeStruct((members // ROW_BLOCKS, CTOK, lanes), jnp.bfloat16)] * ROW_BLOCKS
+    out.append(jax.ShapeDtypeStruct((MEMBERS if places else members, CTOK, TILE), jnp.bfloat16))
+    scratch = [
+        pltpu.VMEM((members * (CTOK + STEPS), FEATURES), jnp.bfloat16),
+        pltpu.VMEM((TILE // 128, members * CTOK, 128), jnp.float32),
+        pltpu.VMEM((members, CTOK, lanes), jnp.bfloat16),
+    ]
+    if places:
+        operands = list(messages) + [earlier, weight]
+        in_specs = [VMEM] * len(operands)
+    else:
+        operands = list(messages) + [in_hbm(weight)]
+        in_specs = [VMEM] * len(messages) + [HBM]
+        out.append(jax.ShapeDtypeStruct((tiles, FEATURES, TILE), jnp.bfloat16))
+        scratch.append(pltpu.SemaphoreType.DMA((tiles,)))
     return pl.pallas_call(
         functools.partial(product_kernel, tiles, counts, places),
-        out_shape=[jax.ShapeDtypeStruct((members // ROW_BLOCKS, CTOK, lanes), jnp.bfloat16)] * ROW_BLOCKS
-        + [jax.ShapeDtypeStruct((MEMBERS if places else members, CTOK, TILE), jnp.bfloat16)],
+        out_shape=out,
         grid=(tiles,),
-        in_specs=[VMEM] * (len(counts) + len(earlier)) + [HBM],
-        out_specs=[VMEM] * (1 + ROW_BLOCKS),
-        scratch_shapes=[
-            pltpu.VMEM((members * (CTOK + STEPS), FEATURES), jnp.bfloat16),
-            pltpu.VMEM((TILE // 128, members * CTOK, 128), jnp.float32),
-            pltpu.VMEM((tiles, FEATURES, TILE), jnp.bfloat16),
-            pltpu.SemaphoreType.DMA((tiles,)),
-            pltpu.VMEM((members, CTOK, lanes), jnp.bfloat16),
-        ],
+        in_specs=in_specs,
+        out_specs=[VMEM] * len(out),
+        scratch_shapes=scratch,
         compiler_params=kernel_params(),
         cost_estimate=cost(2 * members * (CTOK + STEPS) * FEATURES * tiles * TILE, 12 * 10**6),
         name="block_product",
-    )(*messages, *earlier, in_hbm(blocks))
+    )(*operands)
 
 
 def sum_kernel(bias_ref, *refs):
@@ -603,9 +615,9 @@
     after, before = from_side(near, 0, 1), from_side(near, 0, 3)
     over_after, over_before = from_side(over, 0, 1), from_side(over, 0, 3)
     far = [from_side(before, 0, 3), from_side(over_after, 0, 1)]
-    *first, main = block_product([near, over, after, before], blocks)
+    *first, main, weight = block_product([near, over, after, before], blocks)
     first = [first[0]] + [from_along(first[k], -k) for k in range(1, ROW_BLOCKS)]
-    *second, main = block_product([over_after, over_before] + far, blocks, (main,), HOMES)
+    *second, main = block_product([over_after, over_before] + far, weight, main, HOMES)
     main, first = lax.optimization_barrier((main, first))
     second = [second[0]] + [from_along(second[k], -k) for k in range(1, ROW_BLOCKS)]
     received = []
@@ -631,7 +643,7 @@
     mixed, main_kv = attend_main(prefix_len, bias, *main_tables, cache, main_parts, before + [read])
     mixed = exchange(mixed)
     cont_mixed = attend_cont(prefix_len, boundary, bias, *cont_tables, cache, main_kv, *parts)
-    parts = exchange(out_product(mixed, read, w_out, parts[4:6]))
+    parts = exchange(out_product(mixed, read, w_out, parts[4:7]))
     main_out, score = finish(parts, main, cont, head, cont_mixed)
     return main_out[None], score[0, :1]
 

time: 113 us -> 112 us (level)
  starting transfers between devices: 49.9 us -> 52.5 us
  waiting for transfers between devices: 21.3 us -> 19.3 us
  Pallas kernels: 25.5 us -> 24.3 us
    ppermute x14, starting transfers between devices: 23.2 us -> 24.7 us  [from_side(): return lax.ppermute(rows, 'tp', route)]
    pallas_call x2, Pallas kernels: 8.76 us -> 7.53 us  [block_product(): pl.pallas_call(functools.partial(product_kernel, tiles, counts, places),...]
    ppermute x14, waiting for transfers between devices: 18.1 us -> 16.9 us  [from_side(): return lax.ppermute(rows, 'tp', route)]
  transfers between devices with their start and end apart: 23 -> 23, of which waited for: 10 -> 9; matrix products, arithmetic and copies ran while one was open for 0% -> 0% of each run, Pallas kernels for 14% -> 13%
where the time goes in v18:
time: 112 us
  starting transfers between devices  52.5 us (47%)
  Pallas kernels  24.3 us (22%)
  waiting for transfers between devices  19.3 us (17%)
  blocking collectives  12.2 us (11%)
  between operations  2.12 us (2%)
  local copies, waits for them, and re-layouts  1.18 us (1%)
    ppermute x14, starting transfers between devices, from_side(): return lax.ppermute(rows, 'tp', route)  24.7 us
    all_to_all x3, starting transfers between devices, exchange(): return lax.all_to_all(rows, 'tp', split_axis=0, concat_axis=0, tiled=True)  18.9 us
    ppermute x14, waiting for transfers between devices, from_side(): return lax.ppermute(rows, 'tp', route)  16.9 us
    all_to_all x1, blocking collectives, project(): lax.all_to_all(rows, 'tp', split_axis=0, concat_axis=0, tiled=True, axis_...  12.2 us
    ppermute x6, starting transfers between devices, from_along(): return lax.ppermute(rows, 'tp', route)  8.86 us
    pallas_call x2, Pallas kernels, block_product(): pl.pallas_call(functools.partial(product_kernel, tiles, counts, places),...  7.53 us
    pallas_call x1, Pallas kernels, attend_main(): pl.pallas_call(attend_main_kernel, out_shape=(jax.ShapeDtypeStruct((32, 1...  3.71 us
    pallas_call x1, Pallas kernels, readout(): pl.pallas_call(readout_kernel, out_shape=jax.ShapeDtypeStruct((1, FEATURE...  3.41 us
  transfers between devices with their start and end apart: 23, of which 9 were waited for; matrix products, arithmetic and copies ran while one was open for 0% of the time, Pallas kernels for 13%

profile of v18, /device:TPU:0, one launch (start us, length us, event | category | flops | bytes accessed | tf_op | source)
XLA Modules:
  0.0 111.9 jit_solution(2570990214381779650)
XLA Ops:
  2.0 12.2 %all_to_all.20.refs_0_ = bf16[4,16,2304]{2,1,0:T(8,128)(2,1)S(1)} all-to-all(bf16[4,16,2304]{2,1,0:T(8,128)(2,1)S(1)} %norm_rows.1), channel_id=1, replica_groups={{0,8,16,24},{1,9,17,25},{2,10,18,26},{3,11,19,27},{4,12,20,28},{5,13,21..., dimensions={0} | all-to-all | bytes 589824 | tf_op jit(solution)/shard_map/all_to_all | solution.py:613
  17.3 1.7 %collective-permute-start.6 = (bf16[4,16,2304]{2,1,0:T(8,128)(2,1)S(1)}, bf16[4,16,2304]{2,1,0:T(8,128)(2,1)S(1)}, u32[]{:S(2)}, u32[]{:S(2)}) collective-permute-start(bf16[4,16,2304]{2,1,0:T(8,128)(2,1)S(1)} %all_to_all.20.refs_0_), channel_id=1, source_target_pairs={{1,0},{2,1},{3,2},{0,3},{5,4},{6,5},{7,6},{4,7},{9,8},{10,9},{11,1... | collective-permute-start | bytes 884744 | tf_op jit(solution)/shard_map/ppermute | solution.py:599
  19.1 2.4 %collective-permute-done.refs_1_ = bf16[4,16,2304]{2,1,0:T(8,128)(2,1)S(1)} collective-permute-done((bf16[4,16,2304]{2,1,0:T(8,128)(2,1)S(1)}, bf16[4,16,2304]{2,1,0:T(8,128)(2,1)S(1)}, u32[]{:S(2)}, u32[]{:S(2)}) %collective-permute-start) | collective-permute-done | bytes 294944 | tf_op jit(solution)/shard_map/ppermute | solution.py:599
  21.5 2.8 %collective-permute-start.1 = (bf16[4,16,2304]{2,1,0:T(8,128)(2,1)S(1)}, bf16[4,16,2304]{2,1,0:T(8,128)(2,1)S(1)}, u32[]{:S(2)}, u32[]{:S(2)}) collective-permute-start(bf16[4,16,2304]{2,1,0:T(8,128)(2,1)S(1)} %collective-permute-done.refs_1_), channel_id=1, source_target_pairs={{1,0},{2,1},{3,2},{0,3},{5,4},{6,5},{7,6},{4,7},{9,8},{10,9},{11,1... | collective-permute-start | bytes 884744 | tf_op jit(solution)/shard_map/ppermute | solution.py:599
  26.6 3.9 %block_product.2 = (bf16[4,16,2048]{2,1,0:T(8,128)(2,1)S(1)}, bf16[4,16,2048]{2,1,0:T(8,128)(2,1)S(1)}, bf16[4,16,2048]{2,1,0:T(8,128)(2,1)S(1)}, bf16[4,16,2048...) custom-call(bf16[4,16,2304]{2,1,0:T(8,128)(2,1)S(1)} %all_to_all.20.refs_0_, ...), custom_call_target="tpu_custom_call" | custom-call | flops 1509949440 | bytes 12000000 | tf_op jit(solution)/shard_map/block_product/pallas_call | solution.py:217
  31.2 2.1 %collective-permute-start.8 = (bf16[4,16,2048]{2,1,0:T(8,128)(2,1)S(1)}, bf16[4,16,2048]{2,1,0:T(8,128)(2,1)S(1)}, u32[]{:S(2)}, u32[]{:S(2)}) collective-permute-start(bf16[4,16,2048]{2,1,0:T(8,128)(2,1)S(1)} %get-tuple-element.35), channel_id=1, source_target_pairs={{16,0},{17,1},{18,2},{19,3},{20,4},{21,5},{22,6},{23,7},{24,8},{25... | collective-permute-start | bytes 786440 | tf_op jit(solution)/shard_map/ppermute | solution.py:604
  35.7 1.7 %collective-permute-start.5 = (bf16[4,16,2304]{2,1,0:T(8,128)(2,1)S(1)}, bf16[4,16,2304]{2,1,0:T(8,128)(2,1)S(1)}, u32[]{:S(2)}, u32[]{:S(2)}) collective-permute-start(bf16[4,16,2304]{2,1,0:T(8,128)(2,1)S(1)} %collective-permute-done.1.refs_0_), channel_id=1, source_target_pairs={{1,0},{2,1},{3,2},{0,3},{5,4},{6,5},{7,6},{4,7},{9,8},{10,9},{11,1... | collective-permute-start | bytes 884744 | tf_op jit(solution)/shard_map/ppermute | solution.py:599
  37.5 4.7 %collective-permute-done.4.refs_2_ = bf16[4,16,2304]{2,1,0:T(8,128)(2,1)S(1)} collective-permute-done((bf16[4,16,2304]{2,1,0:T(8,128)(2,1)S(1)}, bf16[4,16,2304]{2,1,0:T(8,128)(2,1)S(1)}, u32[]{:S(2)}, u32[]{:S(2)}) %collective-permute-start.4) | collective-permute-done | bytes 294944 | tf_op jit(solution)/shard_map/ppermute | solution.py:599
  42.4 3.6 %block_product.3 = (bf16[4,16,2048]{2,1,0:T(8,128)(2,1)S(1)}, bf16[4,16,2048]{2,1,0:T(8,128)(2,1)}, bf16[4,16,2048]{2,1,0:T(8,128)(2,1)S(1)}, bf16[4,16,2048]{2,1,0:T(8,128)(2,1)S(1)}, bf16[32,16,256]{2,1,0:T(8,128)(2,1)}) custom-call(bf16[4,16,2304]{2,1,0:T(8,128)(2,1)S(1)} %collective-permute-done.1.refs_0_, ...), custom_call_target="tpu_custom_call" | custom-call | flops 1509949440 | bytes 12000000 | tf_op jit(solution)/shard_map/block_product/pallas_call | solution.py:217
  48.6 2.6 %collective-permute-start.12 = (bf16[4,16,2048]{2,1,0:T(8,128)(2,1)S(1)}, bf16[4,16,2048]{2,1,0:T(8,128)(2,1)S(1)}, u32[]{:S(2)}, u32[]{:S(2)}) collective-permute-start(bf16[4,16,2048]{2,1,0:T(8,128)(2,1)S(1)} %get-tuple-element.40), channel_id=1, source_target_pairs={{8,0},{9,1},{10,2},{11,3},{12,4},{13,5},{14,6},{15,7},{16,8},{17,9... | collective-permute-start | bytes 786440 | tf_op jit(solution)/shard_map/ppermute | solution.py:604
  52.6 6.5 %all-to-all-start.1 = ((bf16[32,16,256]{2,1,0:T(8,128)(2,1)}), bf16[32,16,256]{2,1,0:T(8,128)(2,1)S(1)}, u32[]{:S(2)}, u32[]{:S(2)}) async-start(bf16[32,16,256]{2,1,0:T(8,128)(2,1)} %get-tuple-element.37), calls=%async_computation.1 | async-start | bytes 524288 | tf_op jit(solution)/shard_map/all_to_all | solution.py:588
  59.2 1.9 %collective-permute-start.14 = (bf16[16,2048]{1,0:T(8,128)(2,1)}, bf16[16,2048]{1,0:T(8,128)(2,1)S(1)}, u32[]{:S(2)}, u32[]{:S(2)}) collective-permute-start(bf16[16,2048]{1,0:T(8,128)(2,1)} %get-tuple-element.46), channel_id=1, source_target_pairs={{3,0},{0,1},{1,2},{2,3},{7,4},{4,5},{5,6},{6,7},{11,8},{8,9},{9,10... | collective-permute-start | bytes 196616 | tf_op jit(solution)/shard_map/ppermute | solution.py:599
  62.6 3.4 %readout.1.refs_6_.read_ref = f32[1,2048]{1,0:T(1,128)S(1)} custom-call(f32[8,1024]{1,0:T(8,128)S(1)} %reshape.34.head_ref, bf16[1,2048,1024]{2,1,0:T(8,128)(2,1)} %w_hbm.3), custom_call_target="tpu_custom_call" | custom-call | flops 200000000 | bytes 5000000 | tf_op jit(solution)/shard_map/readout/pallas_call | solution.py:472
  66.0 2.3 %all-to-all-done.1.parts_ref = bf16[32,16,256]{2,1,0:T(8,128)(2,1)S(1)} async-done(((bf16[32,16,256]{2,1,0:T(8,128)(2,1)}), bf16[32,16,256]{2,1,0:T(8,128)(2,1)S(1)}, u32[]{:S(2)}, u32[]{:S(2)}) %all-to-all-start.1) | async-done | bytes 262176 | tf_op jit(solution)/shard_map/all_to_all | solution.py:588
  68.3 3.7 %attend_main.1 = (bf16[32,16,256]{2,1,0:T(8,128)(2,1)}, f32[8,2048]{1,0:T(8,128)S(1)}) custom-call(s32[1]{0:T(128)} %copy.12.len_ref, f32[1,10240]{1,0:T(1,128)S(1)} %bitcast.16, f32[8,128]{1,0:T(8,128)S(1)} %get-tuple-element.64.cos_ref, f32[8,128]{1,0:T(8,128)S(1)} %get-tuple-element.65.sin_ref, bf16[256,2048]{1,0:T(8,128)(2,1)S(1)} %bitcast.11, ...), custom_call_target="tpu_custom_call" | custom-call | flops 200000000 | bytes 6000000 | tf_op jit(solution)/shard_map/attend_main/pallas_call | solution.py:395
  72.0 5.3 %all-to-all-start.2 = ((bf16[32,16,256]{2,1,0:T(8,128)(2,1)}), bf16[32,16,256]{2,1,0:T(8,128)(2,1)S(1)}, u32[]{:S(2)}, u32[]{:S(2)}) async-start(bf16[32,16,256]{2,1,0:T(8,128)(2,1)} %get-tuple-element.48), calls=%async_computation.2 | async-start | bytes 524288 | tf_op jit(solution)/shard_map/all_to_all | solution.py:588
  77.6 2.8 %collective-permute-start.16 = (bf16[16,2048]{1,0:T(8,128)(2,1)S(1)}, bf16[16,2048]{1,0:T(8,128)(2,1)S(1)}, u32[]{:S(2)}, u32[]{:S(2)}) collective-permute-start(bf16[16,2048]{1,0:T(8,128)(2,1)S(1)} %get-tuple-element.50), channel_id=1, source_target_pairs={{7,0},{4,1},{5,2},{6,3},{3,4},{0,5},{1,6},{2,7},{15,8},{12,9},{13,... | collective-permute-start | bytes 196616 | tf_op jit(solution)/shard_map/ppermute | solution.py:599
  81.8 2.1 %collective-permute-start.18 = (bf16[16,2048]{1,0:T(8,128)(2,1)S(1)}, bf16[16,2048]{1,0:T(8,128)(2,1)S(1)}, u32[]{:S(2)}, u32[]{:S(2)}) collective-permute-start(bf16[16,2048]{1,0:T(8,128)(2,1)S(1)} %get-tuple-element.52), channel_id=1, source_target_pairs={{2,0},{3,1},{0,2},{1,3},{6,4},{7,5},{4,6},{5,7},{10,8},{11,9},{8,1... | collective-permute-start | bytes 196616 | tf_op jit(solution)/shard_map/ppermute | solution.py:599
  85.7 1.8 %collective-permute-done.18.refs_2_.refs_6_ = bf16[16,2048]{1,0:T(8,128)(2,1)S(1)} collective-permute-done((bf16[16,2048]{1,0:T(8,128)(2,1)S(1)}, bf16[16,2048]{1,0:T(8,128)(2,1)S(1)}, u32[]{:S(2)}, u32[]{:S(2)}) %collective-permute-start.18) | collective-permute-done | bytes 65568 | tf_op jit(solution)/shard_map/ppermute | solution.py:599
  87.6 3.4 %out_product.1 = f32[32,16,256]{2,1,0:T(8,128)} custom-call(bf16[32,16,256]{2,1,0:T(8,128)(2,1)S(1)} %all-to-all-done.2.x_ref, f32[1,2048]{1,0:T(1,128)S(1)} %readout.1.refs_6_.read_ref, bf16[1,2048,1024]{2,1,0:T(8,128)(2,1)} %w_hbm.3, bf16[16,2048]{1,0:T(8,128)(2,1)S(1)} %collective-permute-done.16.refs_0_.refs_4_, ...), custom_call_target="tpu_custom_call" | custom-call | flops 300000000 | bytes 5000000 | tf_op jit(solution)/shard_map/out_product/pallas_call | solution.py:519
  90.9 7.1 %all-to-all-start.3 = ((f32[32,16,256]{2,1,0:T(8,128)}), f32[32,16,256]{2,1,0:T(8,128)S(1)}, u32[]{:S(2)}, u32[]{:S(2)}) async-start(f32[32,16,256]{2,1,0:T(8,128)} %out_product.1), calls=%async_computation.3 | async-start | bytes 1048576 | tf_op jit(solution)/shard_map/all_to_all | solution.py:588
  98.8 4.3 %collective-permute-start.19 = (bf16[16,2048]{1,0:T(8,128)(2,1)S(1)}, bf16[16,2048]{1,0:T(8,128)(2,1)S(1)}, u32[]{:S(2)}, u32[]{:S(2)}) collective-permute-start(bf16[16,2048]{1,0:T(8,128)(2,1)S(1)} %get-tuple-element.55), channel_id=1, source_target_pairs={{6,0},{7,1},{4,2},{5,3},{2,4},{3,5},{0,6},{1,7},{14,8},{15,9},{12,... | collective-permute-start | bytes 196616 | tf_op jit(solution)/shard_map/ppermute | solution.py:599
  103.2 4.2 %collective-permute-done.19.refs_7_ = bf16[16,2048]{1,0:T(8,128)(2,1)S(1)} collective-permute-done((bf16[16,2048]{1,0:T(8,128)(2,1)S(1)}, bf16[16,2048]{1,0:T(8,128)(2,1)S(1)}, u32[]{:S(2)}, u32[]{:S(2)}) %collective-permute-start.19) | collective-permute-done | bytes 65568 | tf_op jit(solution)/shard_map/ppermute | solution.py:599
  107.4 3.0 %attend_cont.1.mixed_ref = bf16[16,8192]{1,0:T(8,128)(2,1)S(1)} custom-call(s32[1]{0:T(128)} %copy.12.len_ref, s32[1]{0:T(128)S(6)} %copy.13.bound_ref, f32[1,10240]{1,0:T(1,128)S(1)} %bitcast.18, f32[16,128]{1,0:T(8,128)S(1)} %get-tuple-element.66.cos_ref, f32[16,128]{1,0:T(8,128)S(1)} %get-tuple-element.67.sin_ref, bf16[256,2048]{1,0:T(8,128)(2,1)S(1)} %bitcast.12, ...), custom_call_target="tpu_custom_call" | custom-call | flops 400000000 | bytes 8000000 | tf_op jit(solution)/shard_map/attend_cont/pallas_call | solution.py:441
  (55 shorter events, 20.2 us)
Async XLA Ops:
  14.2 7.3 %collective-permute-start = (bf16[4,16,2304]{2,1,0:T(8,128)(2,1)S(1)}, bf16[4,16,2304]{2,1,0:T(8,128)(2,1)S(1)}, u32[]{:S(2)}, u32[]{:S(2)}) collective-permute-start(bf16[4,16,2304]{2,1,0:T(8,128)(2,1)S(1)} %all_to_all.20.refs_0_), channel_id=1, source_target_pairs={{4,0},{5,1},{6,2},{7,3},{0,4},{1,5},{2,6},{3,7},{12,8},{13,9},{14,... | collective-permute-start | bytes 884744 | tf_op jit(solution)/shard_map/ppermute | solution.py:599
  15.8 9.1 %collective-permute-start.3 = (bf16[4,16,2304]{2,1,0:T(8,128)(2,1)S(1)}, bf16[4,16,2304]{2,1,0:T(8,128)(2,1)S(1)}, u32[]{:S(2)}, u32[]{:S(2)}) collective-permute-start(bf16[4,16,2304]{2,1,0:T(8,128)(2,1)S(1)} %all_to_all.20.refs_0_), channel_id=1, source_target_pairs={{3,0},{0,1},{1,2},{2,3},{7,4},{4,5},{5,6},{6,7},{11,8},{8,9},{9,10... | collective-permute-start | bytes 884744 | tf_op jit(solution)/shard_map/ppermute | solution.py:599
  17.3 9.3 %collective-permute-start.6 = (bf16[4,16,2304]{2,1,0:T(8,128)(2,1)S(1)}, bf16[4,16,2304]{2,1,0:T(8,128)(2,1)S(1)}, u32[]{:S(2)}, u32[]{:S(2)}) collective-permute-start(bf16[4,16,2304]{2,1,0:T(8,128)(2,1)S(1)} %all_to_all.20.refs_0_), channel_id=1, source_target_pairs={{1,0},{2,1},{3,2},{0,3},{5,4},{6,5},{7,6},{4,7},{9,8},{10,9},{11,1... | collective-permute-start | bytes 884744 | tf_op jit(solution)/shard_map/ppermute | solution.py:599
  21.5 12.7 %collective-permute-start.1 = (bf16[4,16,2304]{2,1,0:T(8,128)(2,1)S(1)}, bf16[4,16,2304]{2,1,0:T(8,128)(2,1)S(1)}, u32[]{:S(2)}, u32[]{:S(2)}) collective-permute-start(bf16[4,16,2304]{2,1,0:T(8,128)(2,1)S(1)} %collective-permute-done.refs_1_), channel_id=1, source_target_pairs={{1,0},{2,1},{3,2},{0,3},{5,4},{6,5},{7,6},{4,7},{9,8},{10,9},{11,1... | collective-permute-start | bytes 884744 | tf_op jit(solution)/shard_map/ppermute | solution.py:599
  24.3 11.4 %collective-permute-start.2 = (bf16[4,16,2304]{2,1,0:T(8,128)(2,1)S(1)}, bf16[4,16,2304]{2,1,0:T(8,128)(2,1)S(1)}, u32[]{:S(2)}, u32[]{:S(2)}) collective-permute-start(bf16[4,16,2304]{2,1,0:T(8,128)(2,1)S(1)} %collective-permute-done.refs_1_), channel_id=1, source_target_pairs={{3,0},{0,1},{1,2},{2,3},{7,4},{4,5},{5,6},{6,7},{11,8},{8,9},{9,10... | collective-permute-start | bytes 884744 | tf_op jit(solution)/shard_map/ppermute | solution.py:599
  30.5 18.1 %collective-permute-start.7 = (bf16[4,16,2048]{2,1,0:T(8,128)(2,1)S(1)}, bf16[4,16,2048]{2,1,0:T(8,128)(2,1)S(1)}, u32[]{:S(2)}, u32[]{:S(2)}) collective-permute-start(bf16[4,16,2048]{2,1,0:T(8,128)(2,1)S(1)} %get-tuple-element.34), channel_id=1, source_target_pairs={{24,0},{25,1},{26,2},{27,3},{28,4},{29,5},{30,6},{31,7},{0,8},{1,9... | collective-permute-start | bytes 786440 | tf_op jit(solution)/shard_map/ppermute | solution.py:604
  31.2 20.1 %collective-permute-start.8 = (bf16[4,16,2048]{2,1,0:T(8,128)(2,1)S(1)}, bf16[4,16,2048]{2,1,0:T(8,128)(2,1)S(1)}, u32[]{:S(2)}, u32[]{:S(2)}) collective-permute-start(bf16[4,16,2048]{2,1,0:T(8,128)(2,1)S(1)} %get-tuple-element.35), channel_id=1, source_target_pairs={{16,0},{17,1},{18,2},{19,3},{20,4},{21,5},{22,6},{23,7},{24,8},{25... | collective-permute-start | bytes 786440 | tf_op jit(solution)/shard_map/ppermute | solution.py:604
  33.2 18.0 %collective-permute-start.9 = (bf16[4,16,2048]{2,1,0:T(8,128)(2,1)S(1)}, bf16[4,16,2048]{2,1,0:T(8,128)(2,1)S(1)}, u32[]{:S(2)}, u32[]{:S(2)}) collective-permute-start(bf16[4,16,2048]{2,1,0:T(8,128)(2,1)S(1)} %get-tuple-element.36), channel_id=1, source_target_pairs={{8,0},{9,1},{10,2},{11,3},{12,4},{13,5},{14,6},{15,7},{16,8},{17,9... | collective-permute-start | bytes 786440 | tf_op jit(solution)/shard_map/ppermute | solution.py:604
  34.2 7.9 %collective-permute-start.4 = (bf16[4,16,2304]{2,1,0:T(8,128)(2,1)S(1)}, bf16[4,16,2304]{2,1,0:T(8,128)(2,1)S(1)}, u32[]{:S(2)}, u32[]{:S(2)}) collective-permute-start(bf16[4,16,2304]{2,1,0:T(8,128)(2,1)S(1)} %collective-permute-done.3.refs_3_), channel_id=1, source_target_pairs={{3,0},{0,1},{1,2},{2,3},{7,4},{4,5},{5,6},{6,7},{11,8},{8,9},{9,10... | collective-permute-start | bytes 884744 | tf_op jit(solution)/shard_map/ppermute | solution.py:599
  35.7 6.7 %collective-permute-start.5 = (bf16[4,16,2304]{2,1,0:T(8,128)(2,1)S(1)}, bf16[4,16,2304]{2,1,0:T(8,128)(2,1)S(1)}, u32[]{:S(2)}, u32[]{:S(2)}) collective-permute-start(bf16[4,16,2304]{2,1,0:T(8,128)(2,1)S(1)} %collective-permute-done.1.refs_0_), channel_id=1, source_target_pairs={{1,0},{2,1},{3,2},{0,3},{5,4},{6,5},{7,6},{4,7},{9,8},{10,9},{11,1... | collective-permute-start | bytes 884744 | tf_op jit(solution)/shard_map/ppermute | solution.py:599
  46.1 22.3 %collective-permute-start.10 = (bf16[4,16,2048]{2,1,0:T(8,128)(2,1)}, bf16[4,16,2048]{2,1,0:T(8,128)(2,1)S(1)}, u32[]{:S(2)}, u32[]{:S(2)}) collective-permute-start(bf16[4,16,2048]{2,1,0:T(8,128)(2,1)} %get-tuple-element.38), channel_id=1, source_target_pairs={{24,0},{25,1},{26,2},{27,3},{28,4},{29,5},{30,6},{31,7},{0,8},{1,9... | collective-permute-start | bytes 786440 | tf_op jit(solution)/shard_map/ppermute | solution.py:604
  47.1 21.2 %collective-permute-start.11 = (bf16[4,16,2048]{2,1,0:T(8,128)(2,1)S(1)}, bf16[4,16,2048]{2,1,0:T(8,128)(2,1)S(1)}, u32[]{:S(2)}, u32[]{:S(2)}) collective-permute-start(bf16[4,16,2048]{2,1,0:T(8,128)(2,1)S(1)} %get-tuple-element.39), channel_id=1, source_target_pairs={{16,0},{17,1},{18,2},{19,3},{20,4},{21,5},{22,6},{23,7},{24,8},{25... | collective-permute-start | bytes 786440 | tf_op jit(solution)/shard_map/ppermute | solution.py:604
  48.6 19.7 %collective-permute-start.12 = (bf16[4,16,2048]{2,1,0:T(8,128)(2,1)S(1)}, bf16[4,16,2048]{2,1,0:T(8,128)(2,1)S(1)}, u32[]{:S(2)}, u32[]{:S(2)}) collective-permute-start(bf16[4,16,2048]{2,1,0:T(8,128)(2,1)S(1)} %get-tuple-element.40), channel_id=1, source_target_pairs={{8,0},{9,1},{10,2},{11,3},{12,4},{13,5},{14,6},{15,7},{16,8},{17,9... | collective-permute-start | bytes 786440 | tf_op jit(solution)/shard_map/ppermute | solution.py:604
  52.5 8.5 %collective-permute-start.13 = (bf16[16,2048]{1,0:T(8,128)(2,1)S(1)}, bf16[16,2048]{1,0:T(8,128)(2,1)S(1)}, u32[]{:S(2)}, u32[]{:S(2)}) collective-permute-start(bf16[16,2048]{1,0:T(8,128)(2,1)S(1)} %get-tuple-element.45), channel_id=1, source_target_pairs={{4,0},{5,1},{6,2},{7,3},{0,4},{1,5},{2,6},{3,7},{12,8},{13,9},{14,... | collective-permute-start | bytes 196616 | tf_op jit(solution)/shard_map/ppermute | solution.py:599
  52.6 15.8 %all-to-all-start.1 = ((bf16[32,16,256]{2,1,0:T(8,128)(2,1)}), bf16[32,16,256]{2,1,0:T(8,128)(2,1)S(1)}, u32[]{:S(2)}, u32[]{:S(2)}) async-start(bf16[32,16,256]{2,1,0:T(8,128)(2,1)} %get-tuple-element.37), calls=%async_computation.1 | async-start | bytes 524288 | tf_op jit(solution)/shard_map/all_to_all | solution.py:588
  59.2 6.8 %collective-permute-start.14 = (bf16[16,2048]{1,0:T(8,128)(2,1)}, bf16[16,2048]{1,0:T(8,128)(2,1)S(1)}, u32[]{:S(2)}, u32[]{:S(2)}) collective-permute-start(bf16[16,2048]{1,0:T(8,128)(2,1)} %get-tuple-element.46), channel_id=1, source_target_pairs={{3,0},{0,1},{1,2},{2,3},{7,4},{4,5},{5,6},{6,7},{11,8},{8,9},{9,10... | collective-permute-start | bytes 196616 | tf_op jit(solution)/shard_map/ppermute | solution.py:599
  61.0 5.0 %collective-permute-start.15 = (bf16[16,2048]{1,0:T(8,128)(2,1)}, bf16[16,2048]{1,0:T(8,128)(2,1)S(1)}, u32[]{:S(2)}, u32[]{:S(2)}) collective-permute-start(bf16[16,2048]{1,0:T(8,128)(2,1)} %copy-done.5), channel_id=1, source_target_pairs={{1,0},{2,1},{3,2},{0,3},{5,4},{6,5},{7,6},{4,7},{9,8},{10,9},{11,1... | collective-permute-start | bytes 196616 | tf_op jit(solution)/shard_map/ppermute | solution.py:599
  72.0 38.4 %copy-start.3 = (bf16[1,2,8192]{2,1,0:T(2,128)(2,1)S(1)}, bf16[1,2,8192]{2,1,0:T(2,128)(2,1)}, u32[]{:S(2)}) copy-start(bf16[1,2,8192]{2,1,0:T(2,128)(2,1)} %param.10) | copy-start | bytes 98308
  72.0 15.5 %all-to-all-start.2 = ((bf16[32,16,256]{2,1,0:T(8,128)(2,1)}), bf16[32,16,256]{2,1,0:T(8,128)(2,1)S(1)}, u32[]{:S(2)}, u32[]{:S(2)}) async-start(bf16[32,16,256]{2,1,0:T(8,128)(2,1)} %get-tuple-element.48), calls=%async_computation.2 | async-start | bytes 524288 | tf_op jit(solution)/shard_map/all_to_all | solution.py:588
  77.6 7.7 %collective-permute-start.16 = (bf16[16,2048]{1,0:T(8,128)(2,1)S(1)}, bf16[16,2048]{1,0:T(8,128)(2,1)S(1)}, u32[]{:S(2)}, u32[]{:S(2)}) collective-permute-start(bf16[16,2048]{1,0:T(8,128)(2,1)S(1)} %get-tuple-element.50), channel_id=1, source_target_pairs={{7,0},{4,1},{5,2},{6,3},{3,4},{0,5},{1,6},{2,7},{15,8},{12,9},{13,... | collective-permute-start | bytes 196616 | tf_op jit(solution)/shard_map/ppermute | solution.py:599
  80.3 5.4 %collective-permute-start.17 = (bf16[16,2048]{1,0:T(8,128)(2,1)S(1)}, bf16[16,2048]{1,0:T(8,128)(2,1)S(1)}, u32[]{:S(2)}, u32[]{:S(2)}) collective-permute-start(bf16[16,2048]{1,0:T(8,128)(2,1)S(1)} %get-tuple-element.51), channel_id=1, source_target_pairs={{5,0},{6,1},{7,2},{4,3},{1,4},{2,5},{3,6},{0,7},{13,8},{14,9},{15,... | collective-permute-start | bytes 196616 | tf_op jit(solution)/shard_map/ppermute | solution.py:599
  81.8 5.8 %collective-permute-start.18 = (bf16[16,2048]{1,0:T(8,128)(2,1)S(1)}, bf16[16,2048]{1,0:T(8,128)(2,1)S(1)}, u32[]{:S(2)}, u32[]{:S(2)}) collective-permute-start(bf16[16,2048]{1,0:T(8,128)(2,1)S(1)} %get-tuple-element.52), channel_id=1, source_target_pairs={{2,0},{3,1},{0,2},{1,3},{6,4},{7,5},{4,6},{5,7},{10,8},{11,9},{8,1... | collective-permute-start | bytes 196616 | tf_op jit(solution)/shard_map/ppermute | solution.py:599
  90.9 19.5 %all-to-all-start.3 = ((f32[32,16,256]{2,1,0:T(8,128)}), f32[32,16,256]{2,1,0:T(8,128)S(1)}, u32[]{:S(2)}, u32[]{:S(2)}) async-start(f32[32,16,256]{2,1,0:T(8,128)} %out_product.1), calls=%async_computation.3 | async-start | bytes 1048576 | tf_op jit(solution)/shard_map/all_to_all | solution.py:588
  98.8 8.6 %collective-permute-start.19 = (bf16[16,2048]{1,0:T(8,128)(2,1)S(1)}, bf16[16,2048]{1,0:T(8,128)(2,1)S(1)}, u32[]{:S(2)}, u32[]{:S(2)}) collective-permute-start(bf16[16,2048]{1,0:T(8,128)(2,1)S(1)} %get-tuple-element.55), channel_id=1, source_target_pairs={{6,0},{7,1},{4,2},{5,3},{2,4},{3,5},{0,6},{1,7},{14,8},{15,9},{12,... | collective-permute-start | bytes 196616 | tf_op jit(solution)/shard_map/ppermute | solution.py:599
  (5 other events, 123.3 us)

commit v19 on v18

--- a/solution.py
+++ b/solution.py
@@ -176,7 +176,7 @@
         done = earlier_ref.shape[0] // ROW_BLOCKS if places else 0
         for k in range(halves):
             lanes = slice(k * 128, (k + 1) * 128)
-            packed = wide_ref[k].astype(jnp.bfloat16).reshape(members, CTOK, 128)
+            packed = wide_ref[k, :count, :].astype(jnp.bfloat16).reshape(members, CTOK, 128)
             if not places:
                 main_ref[:, :, lanes] = packed
             for i, (dy, dx) in enumerate(places):
@@ -203,7 +203,7 @@
     out.append(jax.ShapeDtypeStruct((MEMBERS if places else members, CTOK, TILE), jnp.bfloat16))
     scratch = [
         pltpu.VMEM((members * (CTOK + STEPS), FEATURES), jnp.bfloat16),
-        pltpu.VMEM((TILE // 128, members * CTOK, 128), jnp.float32),
+        pltpu.VMEM((TILE // 128, members * CTOK + 8, 128), jnp.float32),
         pltpu.VMEM((members, CTOK, lanes), jnp.bfloat16),
     ]
     if places:
@@ -496,7 +496,7 @@
         out_ref[:, 8:, :] = jnp.broadcast_to(read8_ref[...][None], (members, 8, TILE))
         packed = x_ref[...].reshape(members * 16, TILE).astype(jnp.float32)
         for k in range(halves):
-            wide_ref[k] = packed[:, k * 128 : (k + 1) * 128]
+            wide_ref[k, : members * 16, :] = packed[:, k * 128 : (k + 1) * 128]
             for j in range(FEATURES // TILE):
                 lane = j * TILE + k * 128
                 rows_ref[:, lane : lane + 128] = wide_ref[k, pl.ds(j, lines, stride=8), :].astype(jnp.bfloat16)
@@ -524,7 +524,7 @@
         out_specs=whole((members, 16, TILE)),
         scratch_shapes=[
             pltpu.VMEM((members * STEPS, FEATURES), jnp.bfloat16),
-            pltpu.VMEM((TILE // 128, members * 16, 128), jnp.float32),
+            pltpu.VMEM((TILE // 128, members * 16 + 8, 128), jnp.float32),
             pltpu.VMEM((8, TILE), jnp.float32),
             pltpu.VMEM((tiles, FEATURES, TILE), jnp.bfloat16),
             pltpu.SemaphoreType.DMA((tiles,)),
@@ -643,7 +643,7 @@
     mixed, main_kv = attend_main(prefix_len, bias, *main_tables, cache, main_parts, before + [read])
     mixed = exchange(mixed)
     cont_mixed = attend_cont(prefix_len, boundary, bias, *cont_tables, cache, main_kv, *parts)
-    parts = exchange(out_product(mixed, read, w_out, parts[4:7]))
+    parts = exchange(out_product(mixed, read, w_out, parts[4:6]))
     main_out, score = finish(parts, main, cont, head, cont_mixed)
     return main_out[None], score[0, :1]
 

time: 112 us -> 112 us (level)
  starting transfers between devices: 52.5 us -> 49.9 us
  waiting for transfers between devices: 19.3 us -> 21.3 us
    ppermute x14, starting transfers between devices: 24.7 us -> 23.2 us  [from_side(): return lax.ppermute(rows, 'tp', route)]
    ppermute x14, waiting for transfers between devices: 16.9 us -> 18.1 us  [from_side(): return lax.ppermute(rows, 'tp', route)]
  transfers between devices with their start and end apart: 23 -> 23, of which waited for: 9 -> 10; matrix products, arithmetic and copies ran while one was open for 0% -> 0% of each run, Pallas kernels for 13% -> 13%
where the time goes in v19:
time: 112 us; the launch traced here: 111 us
  starting transfers between devices  49.9 us (45%)
  Pallas kernels  24.3 us (22%)
  waiting for transfers between devices  21.3 us (19%)
  blocking collectives  12.2 us (11%)
  between operations  2.12 us (2%)
  local copies, waits for them, and re-layouts  1.18 us (1%)
    ppermute x14, starting transfers between devices, from_side(): return lax.ppermute(rows, 'tp', route)  23.2 us
    ppermute x14, waiting for transfers between devices, from_side(): return lax.ppermute(rows, 'tp', route)  18.1 us
    all_to_all x3, starting transfers between devices, exchange(): return lax.all_to_all(rows, 'tp', split_axis=0, concat_axis=0, tiled=True)  17.8 us
    all_to_all x1, blocking collectives, project(): lax.all_to_all(rows, 'tp', split_axis=0, concat_axis=0, tiled=True, axis_...  12.2 us
    ppermute x6, starting transfers between devices, from_along(): return lax.ppermute(rows, 'tp', route)  8.86 us
    pallas_call x2, Pallas kernels, block_product(): pl.pallas_call(functools.partial(product_kernel, tiles, counts, places),...  7.53 us
    pallas_call x1, Pallas kernels, attend_main(): pl.pallas_call(attend_main_kernel, out_shape=(jax.ShapeDtypeStruct((32, 1...  3.71 us
    pallas_call x1, Pallas kernels, readout(): pl.pallas_call(readout_kernel, out_shape=jax.ShapeDtypeStruct((1, FEATURE...  3.41 us
  transfers between devices with their start and end apart: 23, of which 10 were waited for; matrix products, arithmetic and copies ran while one was open for 0% of the time, Pallas kernels for 13%

profile of v19, /device:TPU:0, one launch (start us, length us, event | category | flops | bytes accessed | tf_op | source)
XLA Modules:
  0.0 111.3 jit_solution(13202147038316072291)
XLA Ops:
  2.0 12.2 %all_to_all.20.refs_0_ = bf16[4,16,2304]{2,1,0:T(8,128)(2,1)S(1)} all-to-all(bf16[4,16,2304]{2,1,0:T(8,128)(2,1)S(1)} %norm_rows.1), channel_id=1, replica_groups={{0,8,16,24},{1,9,17,25},{2,10,18,26},{3,11,19,27},{4,12,20,28},{5,13,21..., dimensions={0} | all-to-all | bytes 589824 | tf_op jit(solution)/shard_map/all_to_all | solution.py:613
  17.3 1.7 %collective-permute-start.6 = (bf16[4,16,2304]{2,1,0:T(8,128)(2,1)S(1)}, bf16[4,16,2304]{2,1,0:T(8,128)(2,1)S(1)}, u32[]{:S(2)}, u32[]{:S(2)}) collective-permute-start(bf16[4,16,2304]{2,1,0:T(8,128)(2,1)S(1)} %all_to_all.20.refs_0_), channel_id=1, source_target_pairs={{1,0},{2,1},{3,2},{0,3},{5,4},{6,5},{7,6},{4,7},{9,8},{10,9},{11,1... | collective-permute-start | bytes 884744 | tf_op jit(solution)/shard_map/ppermute | solution.py:599
  19.1 2.4 %collective-permute-done.refs_1_ = bf16[4,16,2304]{2,1,0:T(8,128)(2,1)S(1)} collective-permute-done((bf16[4,16,2304]{2,1,0:T(8,128)(2,1)S(1)}, bf16[4,16,2304]{2,1,0:T(8,128)(2,1)S(1)}, u32[]{:S(2)}, u32[]{:S(2)}) %collective-permute-start) | collective-permute-done | bytes 294944 | tf_op jit(solution)/shard_map/ppermute | solution.py:599
  21.5 2.8 %collective-permute-start.1 = (bf16[4,16,2304]{2,1,0:T(8,128)(2,1)S(1)}, bf16[4,16,2304]{2,1,0:T(8,128)(2,1)S(1)}, u32[]{:S(2)}, u32[]{:S(2)}) collective-permute-start(bf16[4,16,2304]{2,1,0:T(8,128)(2,1)S(1)} %collective-permute-done.refs_1_), channel_id=1, source_target_pairs={{1,0},{2,1},{3,2},{0,3},{5,4},{6,5},{7,6},{4,7},{9,8},{10,9},{11,1... | collective-permute-start | bytes 884744 | tf_op jit(solution)/shard_map/ppermute | solution.py:599
  26.6 3.9 %block_product.2 = (bf16[4,16,2048]{2,1,0:T(8,128)(2,1)S(1)}, bf16[4,16,2048]{2,1,0:T(8,128)(2,1)S(1)}, bf16[4,16,2048]{2,1,0:T(8,128)(2,1)S(1)}, bf16[4,16,2048...) custom-call(bf16[4,16,2304]{2,1,0:T(8,128)(2,1)S(1)} %all_to_all.20.refs_0_, ...), custom_call_target="tpu_custom_call" | custom-call | flops 1509949440 | bytes 12000000 | tf_op jit(solution)/shard_map/block_product/pallas_call | solution.py:217
  31.2 2.1 %collective-permute-start.8 = (bf16[4,16,2048]{2,1,0:T(8,128)(2,1)S(1)}, bf16[4,16,2048]{2,1,0:T(8,128)(2,1)S(1)}, u32[]{:S(2)}, u32[]{:S(2)}) collective-permute-start(bf16[4,16,2048]{2,1,0:T(8,128)(2,1)S(1)} %get-tuple-element.35), channel_id=1, source_target_pairs={{16,0},{17,1},{18,2},{19,3},{20,4},{21,5},{22,6},{23,7},{24,8},{25... | collective-permute-start | bytes 786440 | tf_op jit(solution)/shard_map/ppermute | solution.py:604
  35.7 1.7 %collective-permute-start.5 = (bf16[4,16,2304]{2,1,0:T(8,128)(2,1)S(1)}, bf16[4,16,2304]{2,1,0:T(8,128)(2,1)S(1)}, u32[]{:S(2)}, u32[]{:S(2)}) collective-permute-start(bf16[4,16,2304]{2,1,0:T(8,128)(2,1)S(1)} %collective-permute-done.1.refs_0_), channel_id=1, source_target_pairs={{1,0},{2,1},{3,2},{0,3},{5,4},{6,5},{7,6},{4,7},{9,8},{10,9},{11,1... | collective-permute-start | bytes 884744 | tf_op jit(solution)/shard_map/ppermute | solution.py:599
  37.5 4.7 %collective-permute-done.4.refs_2_ = bf16[4,16,2304]{2,1,0:T(8,128)(2,1)S(1)} collective-permute-done((bf16[4,16,2304]{2,1,0:T(8,128)(2,1)S(1)}, bf16[4,16,2304]{2,1,0:T(8,128)(2,1)S(1)}, u32[]{:S(2)}, u32[]{:S(2)}) %collective-permute-start.4) | collective-permute-done | bytes 294944 | tf_op jit(solution)/shard_map/ppermute | solution.py:599
  42.4 3.6 %block_product.3 = (bf16[4,16,2048]{2,1,0:T(8,128)(2,1)S(1)}, bf16[4,16,2048]{2,1,0:T(8,128)(2,1)}, bf16[4,16,2048]{2,1,0:T(8,128)(2,1)S(1)}, bf16[4,16,2048]{2,1,0:T(8,128)(2,1)S(1)}, bf16[32,16,256]{2,1,0:T(8,128)(2,1)}) custom-call(bf16[4,16,2304]{2,1,0:T(8,128)(2,1)S(1)} %collective-permute-done.1.refs_0_, ...), custom_call_target="tpu_custom_call" | custom-call | flops 1509949440 | bytes 12000000 | tf_op jit(solution)/shard_map/block_product/pallas_call | solution.py:217
  48.6 2.6 %collective-permute-start.12 = (bf16[4,16,2048]{2,1,0:T(8,128)(2,1)S(1)}, bf16[4,16,2048]{2,1,0:T(8,128)(2,1)S(1)}, u32[]{:S(2)}, u32[]{:S(2)}) collective-permute-start(bf16[4,16,2048]{2,1,0:T(8,128)(2,1)S(1)} %get-tuple-element.40), channel_id=1, source_target_pairs={{8,0},{9,1},{10,2},{11,3},{12,4},{13,5},{14,6},{15,7},{16,8},{17,9... | collective-permute-start | bytes 786440 | tf_op jit(solution)/shard_map/ppermute | solution.py:604
  52.6 6.5 %all-to-all-start.1 = ((bf16[32,16,256]{2,1,0:T(8,128)(2,1)}), bf16[32,16,256]{2,1,0:T(8,128)(2,1)S(1)}, u32[]{:S(2)}, u32[]{:S(2)}) async-start(bf16[32,16,256]{2,1,0:T(8,128)(2,1)} %get-tuple-element.37), calls=%async_computation.1 | async-start | bytes 524288 | tf_op jit(solution)/shard_map/all_to_all | solution.py:588
  59.2 1.9 %collective-permute-start.14 = (bf16[16,2048]{1,0:T(8,128)(2,1)}, bf16[16,2048]{1,0:T(8,128)(2,1)S(1)}, u32[]{:S(2)}, u32[]{:S(2)}) collective-permute-start(bf16[16,2048]{1,0:T(8,128)(2,1)} %get-tuple-element.46), channel_id=1, source_target_pairs={{3,0},{0,1},{1,2},{2,3},{7,4},{4,5},{5,6},{6,7},{11,8},{8,9},{9,10... | collective-permute-start | bytes 196616 | tf_op jit(solution)/shard_map/ppermute | solution.py:599
  62.6 3.4 %readout.1.refs_6_.read_ref = f32[1,2048]{1,0:T(1,128)S(1)} custom-call(f32[8,1024]{1,0:T(8,128)S(1)} %reshape.34.head_ref, bf16[1,2048,1024]{2,1,0:T(8,128)(2,1)} %w_hbm.3), custom_call_target="tpu_custom_call" | custom-call | flops 200000000 | bytes 5000000 | tf_op jit(solution)/shard_map/readout/pallas_call | solution.py:472
  66.0 2.3 %all-to-all-done.1.parts_ref = bf16[32,16,256]{2,1,0:T(8,128)(2,1)S(1)} async-done(((bf16[32,16,256]{2,1,0:T(8,128)(2,1)}), bf16[32,16,256]{2,1,0:T(8,128)(2,1)S(1)}, u32[]{:S(2)}, u32[]{:S(2)}) %all-to-all-start.1) | async-done | bytes 262176 | tf_op jit(solution)/shard_map/all_to_all | solution.py:588
  68.3 3.7 %attend_main.1 = (bf16[32,16,256]{2,1,0:T(8,128)(2,1)}, f32[8,2048]{1,0:T(8,128)S(1)}) custom-call(s32[1]{0:T(128)} %copy.12.len_ref, f32[1,10240]{1,0:T(1,128)S(1)} %bitcast.16, f32[8,128]{1,0:T(8,128)S(1)} %get-tuple-element.64.cos_ref, f32[8,128]{1,0:T(8,128)S(1)} %get-tuple-element.65.sin_ref, bf16[256,2048]{1,0:T(8,128)(2,1)S(1)} %bitcast.11, ...), custom_call_target="tpu_custom_call" | custom-call | flops 200000000 | bytes 6000000 | tf_op jit(solution)/shard_map/attend_main/pallas_call | solution.py:395
  72.0 5.3 %all-to-all-start.2 = ((bf16[32,16,256]{2,1,0:T(8,128)(2,1)}), bf16[32,16,256]{2,1,0:T(8,128)(2,1)S(1)}, u32[]{:S(2)}, u32[]{:S(2)}) async-start(bf16[32,16,256]{2,1,0:T(8,128)(2,1)} %get-tuple-element.48), calls=%async_computation.2 | async-start | bytes 524288 | tf_op jit(solution)/shard_map/all_to_all | solution.py:588
  77.6 2.8 %collective-permute-start.16 = (bf16[16,2048]{1,0:T(8,128)(2,1)S(1)}, bf16[16,2048]{1,0:T(8,128)(2,1)S(1)}, u32[]{:S(2)}, u32[]{:S(2)}) collective-permute-start(bf16[16,2048]{1,0:T(8,128)(2,1)S(1)} %get-tuple-element.50), channel_id=1, source_target_pairs={{7,0},{4,1},{5,2},{6,3},{3,4},{0,5},{1,6},{2,7},{15,8},{12,9},{13,... | collective-permute-start | bytes 196616 | tf_op jit(solution)/shard_map/ppermute | solution.py:599
  81.8 3.4 %collective-permute-done.16.refs_0_.refs_4_ = bf16[16,2048]{1,0:T(8,128)(2,1)S(1)} collective-permute-done((bf16[16,2048]{1,0:T(8,128)(2,1)S(1)}, bf16[16,2048]{1,0:T(8,128)(2,1)S(1)}, u32[]{:S(2)}, u32[]{:S(2)}) %collective-permute-start.16) | collective-permute-done | bytes 65568 | tf_op jit(solution)/shard_map/ppermute | solution.py:599
  86.6 3.4 %out_product.1 = f32[32,16,256]{2,1,0:T(8,128)} custom-call(bf16[32,16,256]{2,1,0:T(8,128)(2,1)S(1)} %all-to-all-done.2.x_ref, f32[1,2048]{1,0:T(1,128)S(1)} %readout.1.refs_6_.read_ref, bf16[1,2048,1024]{2,1,0:T(8,128)(2,1)} %w_hbm.3, bf16[16,2048]{1,0:T(8,128)(2,1)S(1)} %collective-permute-done.16.refs_0_.refs_4_, ...), custom_call_target="tpu_custom_call" | custom-call | flops 300000000 | bytes 5000000 | tf_op jit(solution)/shard_map/out_product/pallas_call | solution.py:519
  90.0 6.0 %all-to-all-start.3 = ((f32[32,16,256]{2,1,0:T(8,128)}), f32[32,16,256]{2,1,0:T(8,128)S(1)}, u32[]{:S(2)}, u32[]{:S(2)}) async-start(f32[32,16,256]{2,1,0:T(8,128)} %out_product.1), calls=%async_computation.3 | async-start | bytes 1048576 | tf_op jit(solution)/shard_map/all_to_all | solution.py:588
  96.8 3.4 %collective-permute-start.18 = (bf16[16,2048]{1,0:T(8,128)(2,1)S(1)}, bf16[16,2048]{1,0:T(8,128)(2,1)S(1)}, u32[]{:S(2)}, u32[]{:S(2)}) collective-permute-start(bf16[16,2048]{1,0:T(8,128)(2,1)S(1)} %get-tuple-element.54), channel_id=1, source_target_pairs={{2,0},{3,1},{0,2},{1,3},{6,4},{7,5},{4,6},{5,7},{10,8},{11,9},{8,1... | collective-permute-start | bytes 196616 | tf_op jit(solution)/shard_map/ppermute | solution.py:599
  101.7 2.7 %collective-permute-done.18.refs_6_ = bf16[16,2048]{1,0:T(8,128)(2,1)S(1)} collective-permute-done((bf16[16,2048]{1,0:T(8,128)(2,1)S(1)}, bf16[16,2048]{1,0:T(8,128)(2,1)S(1)}, u32[]{:S(2)}, u32[]{:S(2)}) %collective-permute-start.18) | collective-permute-done | bytes 65568 | tf_op jit(solution)/shard_map/ppermute | solution.py:599
  104.4 2.4 %collective-permute-done.19.refs_7_ = bf16[16,2048]{1,0:T(8,128)(2,1)S(1)} collective-permute-done((bf16[16,2048]{1,0:T(8,128)(2,1)S(1)}, bf16[16,2048]{1,0:T(8,128)(2,1)S(1)}, u32[]{:S(2)}, u32[]{:S(2)}) %collective-permute-start.19) | collective-permute-done | bytes 65568 | tf_op jit(solution)/shard_map/ppermute | solution.py:599
  106.8 3.0 %attend_cont.1.mixed_ref = bf16[16,8192]{1,0:T(8,128)(2,1)S(1)} custom-call(s32[1]{0:T(128)} %copy.12.len_ref, s32[1]{0:T(128)S(6)} %copy.13.bound_ref, f32[1,10240]{1,0:T(1,128)S(1)} %bitcast.18, f32[16,128]{1,0:T(8,128)S(1)} %get-tuple-element.66.cos_ref, f32[16,128]{1,0:T(8,128)S(1)} %get-tuple-element.67.sin_ref, bf16[256,2048]{1,0:T(8,128)(2,1)S(1)} %bitcast.12, ...), custom_call_target="tpu_custom_call" | custom-call | flops 400000000 | bytes 8000000 | tf_op jit(solution)/shard_map/attend_cont/pallas_call | solution.py:441
  (55 shorter events, 21.2 us)
Async XLA Ops:
  14.2 7.3 %collective-permute-start = (bf16[4,16,2304]{2,1,0:T(8,128)(2,1)S(1)}, bf16[4,16,2304]{2,1,0:T(8,128)(2,1)S(1)}, u32[]{:S(2)}, u32[]{:S(2)}) collective-permute-start(bf16[4,16,2304]{2,1,0:T(8,128)(2,1)S(1)} %all_to_all.20.refs_0_), channel_id=1, source_target_pairs={{4,0},{5,1},{6,2},{7,3},{0,4},{1,5},{2,6},{3,7},{12,8},{13,9},{14,... | collective-permute-start | bytes 884744 | tf_op jit(solution)/shard_map/ppermute | solution.py:599
  15.8 9.1 %collective-permute-start.3 = (bf16[4,16,2304]{2,1,0:T(8,128)(2,1)S(1)}, bf16[4,16,2304]{2,1,0:T(8,128)(2,1)S(1)}, u32[]{:S(2)}, u32[]{:S(2)}) collective-permute-start(bf16[4,16,2304]{2,1,0:T(8,128)(2,1)S(1)} %all_to_all.20.refs_0_), channel_id=1, source_target_pairs={{3,0},{0,1},{1,2},{2,3},{7,4},{4,5},{5,6},{6,7},{11,8},{8,9},{9,10... | collective-permute-start | bytes 884744 | tf_op jit(solution)/shard_map/ppermute | solution.py:599
  17.3 9.3 %collective-permute-start.6 = (bf16[4,16,2304]{2,1,0:T(8,128)(2,1)S(1)}, bf16[4,16,2304]{2,1,0:T(8,128)(2,1)S(1)}, u32[]{:S(2)}, u32[]{:S(2)}) collective-permute-start(bf16[4,16,2304]{2,1,0:T(8,128)(2,1)S(1)} %all_to_all.20.refs_0_), channel_id=1, source_target_pairs={{1,0},{2,1},{3,2},{0,3},{5,4},{6,5},{7,6},{4,7},{9,8},{10,9},{11,1... | collective-permute-start | bytes 884744 | tf_op jit(solution)/shard_map/ppermute | solution.py:599
  21.5 12.7 %collective-permute-start.1 = (bf16[4,16,2304]{2,1,0:T(8,128)(2,1)S(1)}, bf16[4,16,2304]{2,1,0:T(8,128)(2,1)S(1)}, u32[]{:S(2)}, u32[]{:S(2)}) collective-permute-start(bf16[4,16,2304]{2,1,0:T(8,128)(2,1)S(1)} %collective-permute-done.refs_1_), channel_id=1, source_target_pairs={{1,0},{2,1},{3,2},{0,3},{5,4},{6,5},{7,6},{4,7},{9,8},{10,9},{11,1... | collective-permute-start | bytes 884744 | tf_op jit(solution)/shard_map/ppermute | solution.py:599
  24.3 11.4 %collective-permute-start.2 = (bf16[4,16,2304]{2,1,0:T(8,128)(2,1)S(1)}, bf16[4,16,2304]{2,1,0:T(8,128)(2,1)S(1)}, u32[]{:S(2)}, u32[]{:S(2)}) collective-permute-start(bf16[4,16,2304]{2,1,0:T(8,128)(2,1)S(1)} %collective-permute-done.refs_1_), channel_id=1, source_target_pairs={{3,0},{0,1},{1,2},{2,3},{7,4},{4,5},{5,6},{6,7},{11,8},{8,9},{9,10... | collective-permute-start | bytes 884744 | tf_op jit(solution)/shard_map/ppermute | solution.py:599
  30.5 18.1 %collective-permute-start.7 = (bf16[4,16,2048]{2,1,0:T(8,128)(2,1)S(1)}, bf16[4,16,2048]{2,1,0:T(8,128)(2,1)S(1)}, u32[]{:S(2)}, u32[]{:S(2)}) collective-permute-start(bf16[4,16,2048]{2,1,0:T(8,128)(2,1)S(1)} %get-tuple-element.34), channel_id=1, source_target_pairs={{24,0},{25,1},{26,2},{27,3},{28,4},{29,5},{30,6},{31,7},{0,8},{1,9... | collective-permute-start | bytes 786440 | tf_op jit(solution)/shard_map/ppermute | solution.py:604
  31.2 20.1 %collective-permute-start.8 = (bf16[4,16,2048]{2,1,0:T(8,128)(2,1)S(1)}, bf16[4,16,2048]{2,1,0:T(8,128)(2,1)S(1)}, u32[]{:S(2)}, u32[]{:S(2)}) collective-permute-start(bf16[4,16,2048]{2,1,0:T(8,128)(2,1)S(1)} %get-tuple-element.35), channel_id=1, source_target_pairs={{16,0},{17,1},{18,2},{19,3},{20,4},{21,5},{22,6},{23,7},{24,8},{25... | collective-permute-start | bytes 786440 | tf_op jit(solution)/shard_map/ppermute | solution.py:604
  33.2 18.0 %collective-permute-start.9 = (bf16[4,16,2048]{2,1,0:T(8,128)(2,1)S(1)}, bf16[4,16,2048]{2,1,0:T(8,128)(2,1)S(1)}, u32[]{:S(2)}, u32[]{:S(2)}) collective-permute-start(bf16[4,16,2048]{2,1,0:T(8,128)(2,1)S(1)} %get-tuple-element.36), channel_id=1, source_target_pairs={{8,0},{9,1},{10,2},{11,3},{12,4},{13,5},{14,6},{15,7},{16,8},{17,9... | collective-permute-start | bytes 786440 | tf_op jit(solution)/shard_map/ppermute | solution.py:604
  34.2 7.9 %collective-permute-start.4 = (bf16[4,16,2304]{2,1,0:T(8,128)(2,1)S(1)}, bf16[4,16,2304]{2,1,0:T(8,128)(2,1)S(1)}, u32[]{:S(2)}, u32[]{:S(2)}) collective-permute-start(bf16[4,16,2304]{2,1,0:T(8,128)(2,1)S(1)} %collective-permute-done.3.refs_3_), channel_id=1, source_target_pairs={{3,0},{0,1},{1,2},{2,3},{7,4},{4,5},{5,6},{6,7},{11,8},{8,9},{9,10... | collective-permute-start | bytes 884744 | tf_op jit(solution)/shard_map/ppermute | solution.py:599
  35.7 6.7 %collective-permute-start.5 = (bf16[4,16,2304]{2,1,0:T(8,128)(2,1)S(1)}, bf16[4,16,2304]{2,1,0:T(8,128)(2,1)S(1)}, u32[]{:S(2)}, u32[]{:S(2)}) collective-permute-start(bf16[4,16,2304]{2,1,0:T(8,128)(2,1)S(1)} %collective-permute-done.1.refs_0_), channel_id=1, source_target_pairs={{1,0},{2,1},{3,2},{0,3},{5,4},{6,5},{7,6},{4,7},{9,8},{10,9},{11,1... | collective-permute-start | bytes 884744 | tf_op jit(solution)/shard_map/ppermute | solution.py:599
  46.1 22.3 %collective-permute-start.10 = (bf16[4,16,2048]{2,1,0:T(8,128)(2,1)}, bf16[4,16,2048]{2,1,0:T(8,128)(2,1)S(1)}, u32[]{:S(2)}, u32[]{:S(2)}) collective-permute-start(bf16[4,16,2048]{2,1,0:T(8,128)(2,1)} %get-tuple-element.38), channel_id=1, source_target_pairs={{24,0},{25,1},{26,2},{27,3},{28,4},{29,5},{30,6},{31,7},{0,8},{1,9... | collective-permute-start | bytes 786440 | tf_op jit(solution)/shard_map/ppermute | solution.py:604
  47.1 21.2 %collective-permute-start.11 = (bf16[4,16,2048]{2,1,0:T(8,128)(2,1)S(1)}, bf16[4,16,2048]{2,1,0:T(8,128)(2,1)S(1)}, u32[]{:S(2)}, u32[]{:S(2)}) collective-permute-start(bf16[4,16,2048]{2,1,0:T(8,128)(2,1)S(1)} %get-tuple-element.39), channel_id=1, source_target_pairs={{16,0},{17,1},{18,2},{19,3},{20,4},{21,5},{22,6},{23,7},{24,8},{25... | collective-permute-start | bytes 786440 | tf_op jit(solution)/shard_map/ppermute | solution.py:604
  48.6 19.7 %collective-permute-start.12 = (bf16[4,16,2048]{2,1,0:T(8,128)(2,1)S(1)}, bf16[4,16,2048]{2,1,0:T(8,128)(2,1)S(1)}, u32[]{:S(2)}, u32[]{:S(2)}) collective-permute-start(bf16[4,16,2048]{2,1,0:T(8,128)(2,1)S(1)} %get-tuple-element.40), channel_id=1, source_target_pairs={{8,0},{9,1},{10,2},{11,3},{12,4},{13,5},{14,6},{15,7},{16,8},{17,9... | collective-permute-start | bytes 786440 | tf_op jit(solution)/shard_map/ppermute | solution.py:604
  52.5 8.5 %collective-permute-start.13 = (bf16[16,2048]{1,0:T(8,128)(2,1)S(1)}, bf16[16,2048]{1,0:T(8,128)(2,1)S(1)}, u32[]{:S(2)}, u32[]{:S(2)}) collective-permute-start(bf16[16,2048]{1,0:T(8,128)(2,1)S(1)} %get-tuple-element.45), channel_id=1, source_target_pairs={{4,0},{5,1},{6,2},{7,3},{0,4},{1,5},{2,6},{3,7},{12,8},{13,9},{14,... | collective-permute-start | bytes 196616 | tf_op jit(solution)/shard_map/ppermute | solution.py:599
  52.6 15.8 %all-to-all-start.1 = ((bf16[32,16,256]{2,1,0:T(8,128)(2,1)}), bf16[32,16,256]{2,1,0:T(8,128)(2,1)S(1)}, u32[]{:S(2)}, u32[]{:S(2)}) async-start(bf16[32,16,256]{2,1,0:T(8,128)(2,1)} %get-tuple-element.37), calls=%async_computation.1 | async-start | bytes 524288 | tf_op jit(solution)/shard_map/all_to_all | solution.py:588
  59.2 6.8 %collective-permute-start.14 = (bf16[16,2048]{1,0:T(8,128)(2,1)}, bf16[16,2048]{1,0:T(8,128)(2,1)S(1)}, u32[]{:S(2)}, u32[]{:S(2)}) collective-permute-start(bf16[16,2048]{1,0:T(8,128)(2,1)} %get-tuple-element.46), channel_id=1, source_target_pairs={{3,0},{0,1},{1,2},{2,3},{7,4},{4,5},{5,6},{6,7},{11,8},{8,9},{9,10... | collective-permute-start | bytes 196616 | tf_op jit(solution)/shard_map/ppermute | solution.py:599
  61.0 5.0 %collective-permute-start.15 = (bf16[16,2048]{1,0:T(8,128)(2,1)}, bf16[16,2048]{1,0:T(8,128)(2,1)S(1)}, u32[]{:S(2)}, u32[]{:S(2)}) collective-permute-start(bf16[16,2048]{1,0:T(8,128)(2,1)} %copy-done.5), channel_id=1, source_target_pairs={{1,0},{2,1},{3,2},{0,3},{5,4},{6,5},{7,6},{4,7},{9,8},{10,9},{11,1... | collective-permute-start | bytes 196616 | tf_op jit(solution)/shard_map/ppermute | solution.py:599
  72.0 37.8 %copy-start.3 = (bf16[1,2,8192]{2,1,0:T(2,128)(2,1)S(1)}, bf16[1,2,8192]{2,1,0:T(2,128)(2,1)}, u32[]{:S(2)}) copy-start(bf16[1,2,8192]{2,1,0:T(2,128)(2,1)} %param.10) | copy-start | bytes 98308
  72.0 14.6 %all-to-all-start.2 = ((bf16[32,16,256]{2,1,0:T(8,128)(2,1)}), bf16[32,16,256]{2,1,0:T(8,128)(2,1)S(1)}, u32[]{:S(2)}, u32[]{:S(2)}) async-start(bf16[32,16,256]{2,1,0:T(8,128)(2,1)} %get-tuple-element.48), calls=%async_computation.2 | async-start | bytes 524288 | tf_op jit(solution)/shard_map/all_to_all | solution.py:588
  77.6 7.7 %collective-permute-start.16 = (bf16[16,2048]{1,0:T(8,128)(2,1)S(1)}, bf16[16,2048]{1,0:T(8,128)(2,1)S(1)}, u32[]{:S(2)}, u32[]{:S(2)}) collective-permute-start(bf16[16,2048]{1,0:T(8,128)(2,1)S(1)} %get-tuple-element.50), channel_id=1, source_target_pairs={{7,0},{4,1},{5,2},{6,3},{3,4},{0,5},{1,6},{2,7},{15,8},{12,9},{13,... | collective-permute-start | bytes 196616 | tf_op jit(solution)/shard_map/ppermute | solution.py:599
  80.3 5.4 %collective-permute-start.17 = (bf16[16,2048]{1,0:T(8,128)(2,1)S(1)}, bf16[16,2048]{1,0:T(8,128)(2,1)S(1)}, u32[]{:S(2)}, u32[]{:S(2)}) collective-permute-start(bf16[16,2048]{1,0:T(8,128)(2,1)S(1)} %get-tuple-element.51), channel_id=1, source_target_pairs={{5,0},{6,1},{7,2},{4,3},{1,4},{2,5},{3,6},{0,7},{13,8},{14,9},{15,... | collective-permute-start | bytes 196616 | tf_op jit(solution)/shard_map/ppermute | solution.py:599
  90.0 19.9 %all-to-all-start.3 = ((f32[32,16,256]{2,1,0:T(8,128)}), f32[32,16,256]{2,1,0:T(8,128)S(1)}, u32[]{:S(2)}, u32[]{:S(2)}) async-start(f32[32,16,256]{2,1,0:T(8,128)} %out_product.1), calls=%async_computation.3 | async-start | bytes 1048576 | tf_op jit(solution)/shard_map/all_to_all | solution.py:588
  96.8 7.7 %collective-permute-start.18 = (bf16[16,2048]{1,0:T(8,128)(2,1)S(1)}, bf16[16,2048]{1,0:T(8,128)(2,1)S(1)}, u32[]{:S(2)}, u32[]{:S(2)}) collective-permute-start(bf16[16,2048]{1,0:T(8,128)(2,1)S(1)} %get-tuple-element.54), channel_id=1, source_target_pairs={{2,0},{3,1},{0,2},{1,3},{6,4},{7,5},{4,6},{5,7},{10,8},{11,9},{8,1... | collective-permute-start | bytes 196616 | tf_op jit(solution)/shard_map/ppermute | solution.py:599
  100.1 6.7 %collective-permute-start.19 = (bf16[16,2048]{1,0:T(8,128)(2,1)S(1)}, bf16[16,2048]{1,0:T(8,128)(2,1)S(1)}, u32[]{:S(2)}, u32[]{:S(2)}) collective-permute-start(bf16[16,2048]{1,0:T(8,128)(2,1)S(1)} %get-tuple-element.55), channel_id=1, source_target_pairs={{6,0},{7,1},{4,2},{5,3},{2,4},{3,5},{0,6},{1,7},{14,8},{15,9},{12,... | collective-permute-start | bytes 196616 | tf_op jit(solution)/shard_map/ppermute | solution.py:599
  (5 other events, 122.7 us)

commit v20 on v19

--- a/solution.py
+++ b/solution.py
@@ -556,7 +556,7 @@
             for c in range(CONTS):
                 direct = direct + cont_ref[c, :, lanes].astype(jnp.float32) * head_ref[:, lanes]
     total = jnp.sum(score, axis=0, keepdims=True) + jnp.sum(direct, axis=0, keepdims=True)
-    score_ref[...] = jnp.broadcast_to(jnp.sum(total, axis=1, keepdims=True) / CONTS, (8, 128))
+    score_ref[0] = jnp.sum(total) / CONTS
 
 
 def finish(parts, main, cont, head, mixed):
@@ -564,10 +564,10 @@
         finish_kernel,
         out_shape=(
             jax.ShapeDtypeStruct((STEPS, D), jnp.bfloat16),
-            jax.ShapeDtypeStruct((8, 128), jnp.float32),
+            jax.ShapeDtypeStruct((1,), jnp.float32),
         ),
         in_specs=[whole(parts.shape), whole(main.shape), whole(cont.shape), whole(head.shape), whole(mixed.shape)],
-        out_specs=(whole((STEPS, D)), whole((8, 128))),
+        out_specs=(whole((STEPS, D)), SMEM),
         scratch_shapes=[pltpu.VMEM((8, D), jnp.float32)],
         compiler_params=kernel_params(),
         cost_estimate=cost(10**6, 2 * 10**6),
@@ -643,9 +643,9 @@
     mixed, main_kv = attend_main(prefix_len, bias, *main_tables, cache, main_parts, before + [read])
     mixed = exchange(mixed)
     cont_mixed = attend_cont(prefix_len, boundary, bias, *cont_tables, cache, main_kv, *parts)
-    parts = exchange(out_product(mixed, read, w_out, parts[4:6]))
+    parts = exchange(out_product(mixed, read, w_out, parts[6:]))
     main_out, score = finish(parts, main, cont, head, cont_mixed)
-    return main_out[None], score[0, :1]
+    return main_out[None], score
 
 
 def solution(mesh):

time: 112 us -> 112 us (level)
  transfers between devices with their start and end apart: 23 -> 23, of which waited for: 10 -> 8; matrix products, arithmetic and copies ran while one was open for 0% -> 0% of each run, Pallas kernels for 13% -> 13%
where the time goes in v20:
time: 112 us; the launch traced here: 111 us
  starting transfers between devices  50 us (45%)
  Pallas kernels  24.3 us (22%)
  waiting for transfers between devices  21.2 us (19%)
  blocking collectives  12.2 us (11%)
  between operations  2.28 us (2%)
    ppermute x14, starting transfers between devices, from_side(): return lax.ppermute(rows, 'tp', route)  23.2 us
    ppermute x14, waiting for transfers between devices, from_side(): return lax.ppermute(rows, 'tp', route)  18.9 us
    all_to_all x3, starting transfers between devices, exchange(): return lax.all_to_all(rows, 'tp', split_axis=0, concat_axis=0, tiled=True)  18 us
    all_to_all x1, blocking collectives, project(): lax.all_to_all(rows, 'tp', split_axis=0, concat_axis=0, tiled=True, axis_...  12.2 us
    ppermute x6, starting transfers between devices, from_along(): return lax.ppermute(rows, 'tp', route)  8.86 us
    pallas_call x2, Pallas kernels, block_product(): pl.pallas_call(functools.partial(product_kernel, tiles, counts, places),...  7.53 us
    pallas_call x1, Pallas kernels, attend_main(): pl.pallas_call(attend_main_kernel, out_shape=(jax.ShapeDtypeStruct((32, 1...  3.71 us
    pallas_call x1, Pallas kernels, readout(): pl.pallas_call(readout_kernel, out_shape=jax.ShapeDtypeStruct((1, FEATURE...  3.41 us
  transfers between devices with their start and end apart: 23, of which 8 were waited for; matrix products, arithmetic and copies ran while one was open for 0% of the time, Pallas kernels for 13%

profile of v20, /device:TPU:0, one launch (start us, length us, event | category | flops | bytes accessed | tf_op | source)
XLA Modules:
  0.0 111.1 jit_solution(10807844011498774037)
XLA Ops:
  2.0 12.2 %all_to_all.20.refs_0_ = bf16[4,16,2304]{2,1,0:T(8,128)(2,1)S(1)} all-to-all(bf16[4,16,2304]{2,1,0:T(8,128)(2,1)S(1)} %norm_rows.1), channel_id=1, replica_groups={{0,8,16,24},{1,9,17,25},{2,10,18,26},{3,11,19,27},{4,12,20,28},{5,13,21..., dimensions={0} | all-to-all | bytes 589824 | tf_op jit(solution)/shard_map/all_to_all | solution.py:613
  17.3 1.7 %collective-permute-start.6 = (bf16[4,16,2304]{2,1,0:T(8,128)(2,1)S(1)}, bf16[4,16,2304]{2,1,0:T(8,128)(2,1)S(1)}, u32[]{:S(2)}, u32[]{:S(2)}) collective-permute-start(bf16[4,16,2304]{2,1,0:T(8,128)(2,1)S(1)} %all_to_all.20.refs_0_), channel_id=1, source_target_pairs={{1,0},{2,1},{3,2},{0,3},{5,4},{6,5},{7,6},{4,7},{9,8},{10,9},{11,1... | collective-permute-start | bytes 884744 | tf_op jit(solution)/shard_map/ppermute | solution.py:599
  19.1 2.4 %collective-permute-done.refs_1_ = bf16[4,16,2304]{2,1,0:T(8,128)(2,1)S(1)} collective-permute-done((bf16[4,16,2304]{2,1,0:T(8,128)(2,1)S(1)}, bf16[4,16,2304]{2,1,0:T(8,128)(2,1)S(1)}, u32[]{:S(2)}, u32[]{:S(2)}) %collective-permute-start) | collective-permute-done | bytes 294944 | tf_op jit(solution)/shard_map/ppermute | solution.py:599
  21.5 2.8 %collective-permute-start.1 = (bf16[4,16,2304]{2,1,0:T(8,128)(2,1)S(1)}, bf16[4,16,2304]{2,1,0:T(8,128)(2,1)S(1)}, u32[]{:S(2)}, u32[]{:S(2)}) collective-permute-start(bf16[4,16,2304]{2,1,0:T(8,128)(2,1)S(1)} %collective-permute-done.refs_1_), channel_id=1, source_target_pairs={{1,0},{2,1},{3,2},{0,3},{5,4},{6,5},{7,6},{4,7},{9,8},{10,9},{11,1... | collective-permute-start | bytes 884744 | tf_op jit(solution)/shard_map/ppermute | solution.py:599
  26.6 3.9 %block_product.2 = (bf16[4,16,2048]{2,1,0:T(8,128)(2,1)S(1)}, bf16[4,16,2048]{2,1,0:T(8,128)(2,1)S(1)}, bf16[4,16,2048]{2,1,0:T(8,128)(2,1)S(1)}, bf16[4,16,2048...) custom-call(bf16[4,16,2304]{2,1,0:T(8,128)(2,1)S(1)} %all_to_all.20.refs_0_, ...), custom_call_target="tpu_custom_call" | custom-call | flops 1509949440 | bytes 12000000 | tf_op jit(solution)/shard_map/block_product/pallas_call | solution.py:217
  31.2 2.1 %collective-permute-start.8 = (bf16[4,16,2048]{2,1,0:T(8,128)(2,1)S(1)}, bf16[4,16,2048]{2,1,0:T(8,128)(2,1)S(1)}, u32[]{:S(2)}, u32[]{:S(2)}) collective-permute-start(bf16[4,16,2048]{2,1,0:T(8,128)(2,1)S(1)} %get-tuple-element.35), channel_id=1, source_target_pairs={{16,0},{17,1},{18,2},{19,3},{20,4},{21,5},{22,6},{23,7},{24,8},{25... | collective-permute-start | bytes 786440 | tf_op jit(solution)/shard_map/ppermute | solution.py:604
  35.7 1.7 %collective-permute-start.5 = (bf16[4,16,2304]{2,1,0:T(8,128)(2,1)S(1)}, bf16[4,16,2304]{2,1,0:T(8,128)(2,1)S(1)}, u32[]{:S(2)}, u32[]{:S(2)}) collective-permute-start(bf16[4,16,2304]{2,1,0:T(8,128)(2,1)S(1)} %collective-permute-done.1.refs_0_), channel_id=1, source_target_pairs={{1,0},{2,1},{3,2},{0,3},{5,4},{6,5},{7,6},{4,7},{9,8},{10,9},{11,1... | collective-permute-start | bytes 884744 | tf_op jit(solution)/shard_map/ppermute | solution.py:599
  37.5 4.7 %collective-permute-done.4.refs_2_ = bf16[4,16,2304]{2,1,0:T(8,128)(2,1)S(1)} collective-permute-done((bf16[4,16,2304]{2,1,0:T(8,128)(2,1)S(1)}, bf16[4,16,2304]{2,1,0:T(8,128)(2,1)S(1)}, u32[]{:S(2)}, u32[]{:S(2)}) %collective-permute-start.4) | collective-permute-done | bytes 294944 | tf_op jit(solution)/shard_map/ppermute | solution.py:599
  42.4 3.6 %block_product.3 = (bf16[4,16,2048]{2,1,0:T(8,128)(2,1)S(1)}, bf16[4,16,2048]{2,1,0:T(8,128)(2,1)}, bf16[4,16,2048]{2,1,0:T(8,128)(2,1)S(1)}, bf16[4,16,2048]{2,1,0:T(8,128)(2,1)S(1)}, bf16[32,16,256]{2,1,0:T(8,128)(2,1)}) custom-call(bf16[4,16,2304]{2,1,0:T(8,128)(2,1)S(1)} %collective-permute-done.1.refs_0_, ...), custom_call_target="tpu_custom_call" | custom-call | flops 1509949440 | bytes 12000000 | tf_op jit(solution)/shard_map/block_product/pallas_call | solution.py:217
  48.6 2.6 %collective-permute-start.12 = (bf16[4,16,2048]{2,1,0:T(8,128)(2,1)S(1)}, bf16[4,16,2048]{2,1,0:T(8,128)(2,1)S(1)}, u32[]{:S(2)}, u32[]{:S(2)}) collective-permute-start(bf16[4,16,2048]{2,1,0:T(8,128)(2,1)S(1)} %get-tuple-element.40), channel_id=1, source_target_pairs={{8,0},{9,1},{10,2},{11,3},{12,4},{13,5},{14,6},{15,7},{16,8},{17,9... | collective-permute-start | bytes 786440 | tf_op jit(solution)/shard_map/ppermute | solution.py:604
  52.6 6.5 %all-to-all-start.1 = ((bf16[32,16,256]{2,1,0:T(8,128)(2,1)}), bf16[32,16,256]{2,1,0:T(8,128)(2,1)S(1)}, u32[]{:S(2)}, u32[]{:S(2)}) async-start(bf16[32,16,256]{2,1,0:T(8,128)(2,1)} %get-tuple-element.37), calls=%async_computation.1 | async-start | bytes 524288 | tf_op jit(solution)/shard_map/all_to_all | solution.py:588
  59.2 1.9 %collective-permute-start.14 = (bf16[16,2048]{1,0:T(8,128)(2,1)}, bf16[16,2048]{1,0:T(8,128)(2,1)S(1)}, u32[]{:S(2)}, u32[]{:S(2)}) collective-permute-start(bf16[16,2048]{1,0:T(8,128)(2,1)} %get-tuple-element.46), channel_id=1, source_target_pairs={{3,0},{0,1},{1,2},{2,3},{7,4},{4,5},{5,6},{6,7},{11,8},{8,9},{9,10... | collective-permute-start | bytes 196616 | tf_op jit(solution)/shard_map/ppermute | solution.py:599
  62.6 3.4 %readout.1.refs_6_.read_ref = f32[1,2048]{1,0:T(1,128)S(1)} custom-call(f32[8,1024]{1,0:T(8,128)S(1)} %reshape.34.head_ref, bf16[1,2048,1024]{2,1,0:T(8,128)(2,1)} %w_hbm.3), custom_call_target="tpu_custom_call" | custom-call | flops 200000000 | bytes 5000000 | tf_op jit(solution)/shard_map/readout/pallas_call | solution.py:472
  66.0 2.3 %all-to-all-done.1.parts_ref = bf16[32,16,256]{2,1,0:T(8,128)(2,1)S(1)} async-done(((bf16[32,16,256]{2,1,0:T(8,128)(2,1)}), bf16[32,16,256]{2,1,0:T(8,128)(2,1)S(1)}, u32[]{:S(2)}, u32[]{:S(2)}) %all-to-all-start.1) | async-done | bytes 262176 | tf_op jit(solution)/shard_map/all_to_all | solution.py:588
  68.3 3.7 %attend_main.1 = (bf16[32,16,256]{2,1,0:T(8,128)(2,1)}, f32[8,2048]{1,0:T(8,128)S(1)}) custom-call(s32[1]{0:T(128)} %copy.12.len_ref, f32[1,10240]{1,0:T(1,128)S(1)} %bitcast.15, f32[8,128]{1,0:T(8,128)S(1)} %get-tuple-element.64.cos_ref, f32[8,128]{1,0:T(8,128)S(1)} %get-tuple-element.65.sin_ref, bf16[256,2048]{1,0:T(8,128)(2,1)S(1)} %bitcast.10, ...), custom_call_target="tpu_custom_call" | custom-call | flops 200000000 | bytes 6000000 | tf_op jit(solution)/shard_map/attend_main/pallas_call | solution.py:395
  72.0 5.3 %all-to-all-start.2 = ((bf16[32,16,256]{2,1,0:T(8,128)(2,1)}), bf16[32,16,256]{2,1,0:T(8,128)(2,1)S(1)}, u32[]{:S(2)}, u32[]{:S(2)}) async-start(bf16[32,16,256]{2,1,0:T(8,128)(2,1)} %get-tuple-element.48), calls=%async_computation.2 | async-start | bytes 524288 | tf_op jit(solution)/shard_map/all_to_all | solution.py:588
  77.6 3.4 %collective-permute-start.16 = (bf16[16,2048]{1,0:T(8,128)(2,1)S(1)}, bf16[16,2048]{1,0:T(8,128)(2,1)S(1)}, u32[]{:S(2)}, u32[]{:S(2)}) collective-permute-start(bf16[16,2048]{1,0:T(8,128)(2,1)S(1)} %get-tuple-element.50), channel_id=1, source_target_pairs={{2,0},{3,1},{0,2},{1,3},{6,4},{7,5},{4,6},{5,7},{10,8},{11,9},{8,1... | collective-permute-start | bytes 196616 | tf_op jit(solution)/shard_map/ppermute | solution.py:599
  82.4 2.0 %collective-permute-done.16.refs_0_.refs_6_ = bf16[16,2048]{1,0:T(8,128)(2,1)S(1)} collective-permute-done((bf16[16,2048]{1,0:T(8,128)(2,1)S(1)}, bf16[16,2048]{1,0:T(8,128)(2,1)S(1)}, u32[]{:S(2)}, u32[]{:S(2)}) %collective-permute-start.16) | collective-permute-done | bytes 65568 | tf_op jit(solution)/shard_map/ppermute | solution.py:599
  84.4 3.2 %collective-permute-done.17.refs_1_.refs_7_ = bf16[16,2048]{1,0:T(8,128)(2,1)S(1)} collective-permute-done((bf16[16,2048]{1,0:T(8,128)(2,1)S(1)}, bf16[16,2048]{1,0:T(8,128)(2,1)S(1)}, u32[]{:S(2)}, u32[]{:S(2)}) %collective-permute-start.17) | collective-permute-done | bytes 65568 | tf_op jit(solution)/shard_map/ppermute | solution.py:599
  87.6 3.4 %out_product.1 = f32[32,16,256]{2,1,0:T(8,128)} custom-call(bf16[32,16,256]{2,1,0:T(8,128)(2,1)S(1)} %all-to-all-done.2.x_ref, f32[1,2048]{1,0:T(1,128)S(1)} %readout.1.refs_6_.read_ref, bf16[1,2048,1024]{2,1,0:T(8,128)(2,1)} %w_hbm.3, bf16[16,2048]{1,0:T(8,128)(2,1)S(1)} %collective-permute-done.16.refs_0_.refs_6_, ...), custom_call_target="tpu_custom_call" | custom-call | flops 300000000 | bytes 5000000 | tf_op jit(solution)/shard_map/out_product/pallas_call | solution.py:519
  91.0 6.2 %all-to-all-start.3 = ((f32[32,16,256]{2,1,0:T(8,128)}), f32[32,16,256]{2,1,0:T(8,128)S(1)}, u32[]{:S(2)}, u32[]{:S(2)}) async-start(f32[32,16,256]{2,1,0:T(8,128)} %out_product.1), calls=%async_computation.3 | async-start | bytes 1048576 | tf_op jit(solution)/shard_map/all_to_all | solution.py:588
  98.0 2.8 %collective-permute-start.18 = (bf16[16,2048]{1,0:T(8,128)(2,1)S(1)}, bf16[16,2048]{1,0:T(8,128)(2,1)S(1)}, u32[]{:S(2)}, u32[]{:S(2)}) collective-permute-start(bf16[16,2048]{1,0:T(8,128)(2,1)S(1)} %get-tuple-element.54), channel_id=1, source_target_pairs={{7,0},{4,1},{5,2},{6,3},{3,4},{0,5},{1,6},{2,7},{15,8},{12,9},{13,... | collective-permute-start | bytes 196616 | tf_op jit(solution)/shard_map/ppermute | solution.py:599
  102.2 4.6 %collective-permute-done.18.refs_4_ = bf16[16,2048]{1,0:T(8,128)(2,1)S(1)} collective-permute-done((bf16[16,2048]{1,0:T(8,128)(2,1)S(1)}, bf16[16,2048]{1,0:T(8,128)(2,1)S(1)}, u32[]{:S(2)}, u32[]{:S(2)}) %collective-permute-start.18) | collective-permute-done | bytes 65568 | tf_op jit(solution)/shard_map/ppermute | solution.py:599
  106.9 3.0 %attend_cont.1.mixed_ref = bf16[16,8192]{1,0:T(8,128)(2,1)S(1)} custom-call(s32[1]{0:T(128)} %copy.12.len_ref, s32[1]{0:T(128)S(6)} %copy.13.bound_ref, f32[1,10240]{1,0:T(1,128)S(1)} %bitcast.17, f32[16,128]{1,0:T(8,128)S(1)} %get-tuple-element.66.cos_ref, f32[16,128]{1,0:T(8,128)S(1)} %get-tuple-element.67.sin_ref, bf16[256,2048]{1,0:T(8,128)(2,1)S(1)} %bitcast.11, ...), custom_call_target="tpu_custom_call" | custom-call | flops 400000000 | bytes 8000000 | tf_op jit(solution)/shard_map/attend_cont/pallas_call | solution.py:441
  (54 shorter events, 19.4 us)
Async XLA Ops:
  14.2 7.3 %collective-permute-start = (bf16[4,16,2304]{2,1,0:T(8,128)(2,1)S(1)}, bf16[4,16,2304]{2,1,0:T(8,128)(2,1)S(1)}, u32[]{:S(2)}, u32[]{:S(2)}) collective-permute-start(bf16[4,16,2304]{2,1,0:T(8,128)(2,1)S(1)} %all_to_all.20.refs_0_), channel_id=1, source_target_pairs={{4,0},{5,1},{6,2},{7,3},{0,4},{1,5},{2,6},{3,7},{12,8},{13,9},{14,... | collective-permute-start | bytes 884744 | tf_op jit(solution)/shard_map/ppermute | solution.py:599
  15.8 9.1 %collective-permute-start.3 = (bf16[4,16,2304]{2,1,0:T(8,128)(2,1)S(1)}, bf16[4,16,2304]{2,1,0:T(8,128)(2,1)S(1)}, u32[]{:S(2)}, u32[]{:S(2)}) collective-permute-start(bf16[4,16,2304]{2,1,0:T(8,128)(2,1)S(1)} %all_to_all.20.refs_0_), channel_id=1, source_target_pairs={{3,0},{0,1},{1,2},{2,3},{7,4},{4,5},{5,6},{6,7},{11,8},{8,9},{9,10... | collective-permute-start | bytes 884744 | tf_op jit(solution)/shard_map/ppermute | solution.py:599
  17.3 9.3 %collective-permute-start.6 = (bf16[4,16,2304]{2,1,0:T(8,128)(2,1)S(1)}, bf16[4,16,2304]{2,1,0:T(8,128)(2,1)S(1)}, u32[]{:S(2)}, u32[]{:S(2)}) collective-permute-start(bf16[4,16,2304]{2,1,0:T(8,128)(2,1)S(1)} %all_to_all.20.refs_0_), channel_id=1, source_target_pairs={{1,0},{2,1},{3,2},{0,3},{5,4},{6,5},{7,6},{4,7},{9,8},{10,9},{11,1... | collective-permute-start | bytes 884744 | tf_op jit(solution)/shard_map/ppermute | solution.py:599
  21.5 12.7 %collective-permute-start.1 = (bf16[4,16,2304]{2,1,0:T(8,128)(2,1)S(1)}, bf16[4,16,2304]{2,1,0:T(8,128)(2,1)S(1)}, u32[]{:S(2)}, u32[]{:S(2)}) collective-permute-start(bf16[4,16,2304]{2,1,0:T(8,128)(2,1)S(1)} %collective-permute-done.refs_1_), channel_id=1, source_target_pairs={{1,0},{2,1},{3,2},{0,3},{5,4},{6,5},{7,6},{4,7},{9,8},{10,9},{11,1... | collective-permute-start | bytes 884744 | tf_op jit(solution)/shard_map/ppermute | solution.py:599
  24.3 11.4 %collective-permute-start.2 = (bf16[4,16,2304]{2,1,0:T(8,128)(2,1)S(1)}, bf16[4,16,2304]{2,1,0:T(8,128)(2,1)S(1)}, u32[]{:S(2)}, u32[]{:S(2)}) collective-permute-start(bf16[4,16,2304]{2,1,0:T(8,128)(2,1)S(1)} %collective-permute-done.refs_1_), channel_id=1, source_target_pairs={{3,0},{0,1},{1,2},{2,3},{7,4},{4,5},{5,6},{6,7},{11,8},{8,9},{9,10... | collective-permute-start | bytes 884744 | tf_op jit(solution)/shard_map/ppermute | solution.py:599
  30.5 18.1 %collective-permute-start.7 = (bf16[4,16,2048]{2,1,0:T(8,128)(2,1)S(1)}, bf16[4,16,2048]{2,1,0:T(8,128)(2,1)S(1)}, u32[]{:S(2)}, u32[]{:S(2)}) collective-permute-start(bf16[4,16,2048]{2,1,0:T(8,128)(2,1)S(1)} %get-tuple-element.34), channel_id=1, source_target_pairs={{24,0},{25,1},{26,2},{27,3},{28,4},{29,5},{30,6},{31,7},{0,8},{1,9... | collective-permute-start | bytes 786440 | tf_op jit(solution)/shard_map/ppermute | solution.py:604
  31.2 20.1 %collective-permute-start.8 = (bf16[4,16,2048]{2,1,0:T(8,128)(2,1)S(1)}, bf16[4,16,2048]{2,1,0:T(8,128)(2,1)S(1)}, u32[]{:S(2)}, u32[]{:S(2)}) collective-permute-start(bf16[4,16,2048]{2,1,0:T(8,128)(2,1)S(1)} %get-tuple-element.35), channel_id=1, source_target_pairs={{16,0},{17,1},{18,2},{19,3},{20,4},{21,5},{22,6},{23,7},{24,8},{25... | collective-permute-start | bytes 786440 | tf_op jit(solution)/shard_map/ppermute | solution.py:604
  33.2 18.0 %collective-permute-start.9 = (bf16[4,16,2048]{2,1,0:T(8,128)(2,1)S(1)}, bf16[4,16,2048]{2,1,0:T(8,128)(2,1)S(1)}, u32[]{:S(2)}, u32[]{:S(2)}) collective-permute-start(bf16[4,16,2048]{2,1,0:T(8,128)(2,1)S(1)} %get-tuple-element.36), channel_id=1, source_target_pairs={{8,0},{9,1},{10,2},{11,3},{12,4},{13,5},{14,6},{15,7},{16,8},{17,9... | collective-permute-start | bytes 786440 | tf_op jit(solution)/shard_map/ppermute | solution.py:604
  34.2 7.9 %collective-permute-start.4 = (bf16[4,16,2304]{2,1,0:T(8,128)(2,1)S(1)}, bf16[4,16,2304]{2,1,0:T(8,128)(2,1)S(1)}, u32[]{:S(2)}, u32[]{:S(2)}) collective-permute-start(bf16[4,16,2304]{2,1,0:T(8,128)(2,1)S(1)} %collective-permute-done.3.refs_3_), channel_id=1, source_target_pairs={{3,0},{0,1},{1,2},{2,3},{7,4},{4,5},{5,6},{6,7},{11,8},{8,9},{9,10... | collective-permute-start | bytes 884744 | tf_op jit(solution)/shard_map/ppermute | solution.py:599
  35.7 6.7 %collective-permute-start.5 = (bf16[4,16,2304]{2,1,0:T(8,128)(2,1)S(1)}, bf16[4,16,2304]{2,1,0:T(8,128)(2,1)S(1)}, u32[]{:S(2)}, u32[]{:S(2)}) collective-permute-start(bf16[4,16,2304]{2,1,0:T(8,128)(2,1)S(1)} %collective-permute-done.1.refs_0_), channel_id=1, source_target_pairs={{1,0},{2,1},{3,2},{0,3},{5,4},{6,5},{7,6},{4,7},{9,8},{10,9},{11,1... | collective-permute-start | bytes 884744 | tf_op jit(solution)/shard_map/ppermute | solution.py:599
  46.1 22.3 %collective-permute-start.10 = (bf16[4,16,2048]{2,1,0:T(8,128)(2,1)}, bf16[4,16,2048]{2,1,0:T(8,128)(2,1)S(1)}, u32[]{:S(2)}, u32[]{:S(2)}) collective-permute-start(bf16[4,16,2048]{2,1,0:T(8,128)(2,1)} %get-tuple-element.38), channel_id=1, source_target_pairs={{24,0},{25,1},{26,2},{27,3},{28,4},{29,5},{30,6},{31,7},{0,8},{1,9... | collective-permute-start | bytes 786440 | tf_op jit(solution)/shard_map/ppermute | solution.py:604
  47.1 21.2 %collective-permute-start.11 = (bf16[4,16,2048]{2,1,0:T(8,128)(2,1)S(1)}, bf16[4,16,2048]{2,1,0:T(8,128)(2,1)S(1)}, u32[]{:S(2)}, u32[]{:S(2)}) collective-permute-start(bf16[4,16,2048]{2,1,0:T(8,128)(2,1)S(1)} %get-tuple-element.39), channel_id=1, source_target_pairs={{16,0},{17,1},{18,2},{19,3},{20,4},{21,5},{22,6},{23,7},{24,8},{25... | collective-permute-start | bytes 786440 | tf_op jit(solution)/shard_map/ppermute | solution.py:604
  48.6 19.7 %collective-permute-start.12 = (bf16[4,16,2048]{2,1,0:T(8,128)(2,1)S(1)}, bf16[4,16,2048]{2,1,0:T(8,128)(2,1)S(1)}, u32[]{:S(2)}, u32[]{:S(2)}) collective-permute-start(bf16[4,16,2048]{2,1,0:T(8,128)(2,1)S(1)} %get-tuple-element.40), channel_id=1, source_target_pairs={{8,0},{9,1},{10,2},{11,3},{12,4},{13,5},{14,6},{15,7},{16,8},{17,9... | collective-permute-start | bytes 786440 | tf_op jit(solution)/shard_map/ppermute | solution.py:604
  52.5 8.5 %collective-permute-start.13 = (bf16[16,2048]{1,0:T(8,128)(2,1)S(1)}, bf16[16,2048]{1,0:T(8,128)(2,1)S(1)}, u32[]{:S(2)}, u32[]{:S(2)}) collective-permute-start(bf16[16,2048]{1,0:T(8,128)(2,1)S(1)} %get-tuple-element.45), channel_id=1, source_target_pairs={{4,0},{5,1},{6,2},{7,3},{0,4},{1,5},{2,6},{3,7},{12,8},{13,9},{14,... | collective-permute-start | bytes 196616 | tf_op jit(solution)/shard_map/ppermute | solution.py:599
  52.6 15.8 %all-to-all-start.1 = ((bf16[32,16,256]{2,1,0:T(8,128)(2,1)}), bf16[32,16,256]{2,1,0:T(8,128)(2,1)S(1)}, u32[]{:S(2)}, u32[]{:S(2)}) async-start(bf16[32,16,256]{2,1,0:T(8,128)(2,1)} %get-tuple-element.37), calls=%async_computation.1 | async-start | bytes 524288 | tf_op jit(solution)/shard_map/all_to_all | solution.py:588
  59.2 6.8 %collective-permute-start.14 = (bf16[16,2048]{1,0:T(8,128)(2,1)}, bf16[16,2048]{1,0:T(8,128)(2,1)S(1)}, u32[]{:S(2)}, u32[]{:S(2)}) collective-permute-start(bf16[16,2048]{1,0:T(8,128)(2,1)} %get-tuple-element.46), channel_id=1, source_target_pairs={{3,0},{0,1},{1,2},{2,3},{7,4},{4,5},{5,6},{6,7},{11,8},{8,9},{9,10... | collective-permute-start | bytes 196616 | tf_op jit(solution)/shard_map/ppermute | solution.py:599
  61.0 5.0 %collective-permute-start.15 = (bf16[16,2048]{1,0:T(8,128)(2,1)}, bf16[16,2048]{1,0:T(8,128)(2,1)S(1)}, u32[]{:S(2)}, u32[]{:S(2)}) collective-permute-start(bf16[16,2048]{1,0:T(8,128)(2,1)} %copy-done.5), channel_id=1, source_target_pairs={{1,0},{2,1},{3,2},{0,3},{5,4},{6,5},{7,6},{4,7},{9,8},{10,9},{11,1... | collective-permute-start | bytes 196616 | tf_op jit(solution)/shard_map/ppermute | solution.py:599
  72.0 37.9 %copy-start.3 = (bf16[1,2,8192]{2,1,0:T(2,128)(2,1)S(1)}, bf16[1,2,8192]{2,1,0:T(2,128)(2,1)}, u32[]{:S(2)}) copy-start(bf16[1,2,8192]{2,1,0:T(2,128)(2,1)} %param.10) | copy-start | bytes 98308
  72.0 15.6 %all-to-all-start.2 = ((bf16[32,16,256]{2,1,0:T(8,128)(2,1)}), bf16[32,16,256]{2,1,0:T(8,128)(2,1)S(1)}, u32[]{:S(2)}, u32[]{:S(2)}) async-start(bf16[32,16,256]{2,1,0:T(8,128)(2,1)} %get-tuple-element.48), calls=%async_computation.2 | async-start | bytes 524288 | tf_op jit(solution)/shard_map/all_to_all | solution.py:588
  77.6 6.8 %collective-permute-start.16 = (bf16[16,2048]{1,0:T(8,128)(2,1)S(1)}, bf16[16,2048]{1,0:T(8,128)(2,1)S(1)}, u32[]{:S(2)}, u32[]{:S(2)}) collective-permute-start(bf16[16,2048]{1,0:T(8,128)(2,1)S(1)} %get-tuple-element.50), channel_id=1, source_target_pairs={{2,0},{3,1},{0,2},{1,3},{6,4},{7,5},{4,6},{5,7},{10,8},{11,9},{8,1... | collective-permute-start | bytes 196616 | tf_op jit(solution)/shard_map/ppermute | solution.py:599
  80.9 6.7 %collective-permute-start.17 = (bf16[16,2048]{1,0:T(8,128)(2,1)S(1)}, bf16[16,2048]{1,0:T(8,128)(2,1)S(1)}, u32[]{:S(2)}, u32[]{:S(2)}) collective-permute-start(bf16[16,2048]{1,0:T(8,128)(2,1)S(1)} %get-tuple-element.51), channel_id=1, source_target_pairs={{6,0},{7,1},{4,2},{5,3},{2,4},{3,5},{0,6},{1,7},{14,8},{15,9},{12,... | collective-permute-start | bytes 196616 | tf_op jit(solution)/shard_map/ppermute | solution.py:599
  91.0 18.9 %all-to-all-start.3 = ((f32[32,16,256]{2,1,0:T(8,128)}), f32[32,16,256]{2,1,0:T(8,128)S(1)}, u32[]{:S(2)}, u32[]{:S(2)}) async-start(f32[32,16,256]{2,1,0:T(8,128)} %out_product.1), calls=%async_computation.3 | async-start | bytes 1048576 | tf_op jit(solution)/shard_map/all_to_all | solution.py:588
  98.0 8.9 %collective-permute-start.18 = (bf16[16,2048]{1,0:T(8,128)(2,1)S(1)}, bf16[16,2048]{1,0:T(8,128)(2,1)S(1)}, u32[]{:S(2)}, u32[]{:S(2)}) collective-permute-start(bf16[16,2048]{1,0:T(8,128)(2,1)S(1)} %get-tuple-element.54), channel_id=1, source_target_pairs={{7,0},{4,1},{5,2},{6,3},{3,4},{0,5},{1,6},{2,7},{15,8},{12,9},{13,... | collective-permute-start | bytes 196616 | tf_op jit(solution)/shard_map/ppermute | solution.py:599
  100.7 6.2 %collective-permute-start.19 = (bf16[16,2048]{1,0:T(8,128)(2,1)S(1)}, bf16[16,2048]{1,0:T(8,128)(2,1)S(1)}, u32[]{:S(2)}, u32[]{:S(2)}) collective-permute-start(bf16[16,2048]{1,0:T(8,128)(2,1)S(1)} %get-tuple-element.55), channel_id=1, source_target_pairs={{5,0},{6,1},{7,2},{4,3},{1,4},{2,5},{3,6},{0,7},{13,8},{14,9},{15,... | collective-permute-start | bytes 196616 | tf_op jit(solution)/shard_map/ppermute | solution.py:599
  (5 other events, 122.8 us)

commit v21 on v20

--- a/solution.py
+++ b/solution.py
@@ -399,7 +399,7 @@
             jax.ShapeDtypeStruct((8, 2 * KV_WIDTH), jnp.float32),
         ),
         in_specs=[SMEM] + [VMEM] * 5 + [UNREAD] * len(after),
-        out_specs=(whole((32, 16, TILE)), whole((8, 2 * KV_WIDTH))),
+        out_specs=(VMEM, VMEM),
         scratch_shapes=[
             pltpu.VMEM((8, QKV), jnp.float32),
             pltpu.VMEM((ROW_BLOCKS, 16, TILE), jnp.float32),
@@ -442,7 +442,7 @@
         attend_cont_kernel,
         out_shape=jax.ShapeDtypeStruct((CTOK, D), jnp.bfloat16),
         in_specs=[SMEM, SMEM] + [VMEM] * 4 + [whole((8, 2 * KV_WIDTH))] + [VMEM] * COL_BLOCKS,
-        out_specs=whole((CTOK, D)),
+        out_specs=VMEM,
         scratch_shapes=[
             pltpu.VMEM((CTOK, QKV), jnp.float32),
             pltpu.VMEM((COL_BLOCKS,) + args[-1].shape, jnp.bfloat16),
@@ -520,8 +520,8 @@
         functools.partial(out_kernel, tiles),
         out_shape=jax.ShapeDtypeStruct((members, 16, TILE), jnp.float32),
         grid=(tiles,),
-        in_specs=[whole(rows.shape), whole(read.shape), HBM] + [UNREAD] * len(after),
-        out_specs=whole((members, 16, TILE)),
+        in_specs=[VMEM, VMEM, HBM] + [UNREAD] * len(after),
+        out_specs=VMEM,
         scratch_shapes=[
             pltpu.VMEM((members * STEPS, FEATURES), jnp.bfloat16),
             pltpu.VMEM((TILE // 128, members * 16 + 8, 128), jnp.float32),
@@ -566,7 +566,7 @@
             jax.ShapeDtypeStruct((STEPS, D), jnp.bfloat16),
             jax.ShapeDtypeStruct((1,), jnp.float32),
         ),
-        in_specs=[whole(parts.shape), whole(main.shape), whole(cont.shape), whole(head.shape), whole(mixed.shape)],
+        in_specs=[VMEM] * 5,
         out_specs=(whole((STEPS, D)), SMEM),
         scratch_shapes=[pltpu.VMEM((8, D), jnp.float32)],
         compiler_params=kernel_params(),

time: 112 us -> 112 us (level)
  no operation moved by 1% of the time
where the time goes in v21:
time: 112 us; the launch traced here: 111 us
  starting transfers between devices  50 us (45%)
  Pallas kernels  24.3 us (22%)
  waiting for transfers between devices  21.2 us (19%)
  blocking collectives  12.2 us (11%)
  between operations  2.28 us (2%)
    ppermute x14, starting transfers between devices, from_side(): return lax.ppermute(rows, 'tp', route)  23.2 us
    ppermute x14, waiting for transfers between devices, from_side(): return lax.ppermute(rows, 'tp', route)  18.9 us
    all_to_all x3, starting transfers between devices, exchange(): return lax.all_to_all(rows, 'tp', split_axis=0, concat_axis=0, tiled=True)  18 us
    all_to_all x1, blocking collectives, project(): lax.all_to_all(rows, 'tp', split_axis=0, concat_axis=0, tiled=True, axis_...  12.2 us
    ppermute x6, starting transfers between devices, from_along(): return lax.ppermute(rows, 'tp', route)  8.86 us
    pallas_call x2, Pallas kernels, block_product(): pl.pallas_call(functools.partial(product_kernel, tiles, counts, places),...  7.53 us
    pallas_call x1, Pallas kernels, attend_main(): pl.pallas_call(attend_main_kernel, out_shape=(jax.ShapeDtypeStruct((32, 1...  3.71 us
    pallas_call x1, Pallas kernels, readout(): pl.pallas_call(readout_kernel, out_shape=jax.ShapeDtypeStruct((1, FEATURE...  3.41 us
  transfers between devices with their start and end apart: 23, of which 8 were waited for; matrix products, arithmetic and copies ran while one was open for 0% of the time, Pallas kernels for 13%

profile of v21, /device:TPU:0, one launch (start us, length us, event | category | flops | bytes accessed | tf_op | source)
XLA Modules:
  0.0 111.1 jit_solution(10807844011498774037)
XLA Ops:
  2.0 12.2 %all_to_all.20.refs_0_ = bf16[4,16,2304]{2,1,0:T(8,128)(2,1)S(1)} all-to-all(bf16[4,16,2304]{2,1,0:T(8,128)(2,1)S(1)} %norm_rows.1), channel_id=1, replica_groups={{0,8,16,24},{1,9,17,25},{2,10,18,26},{3,11,19,27},{4,12,20,28},{5,13,21..., dimensions={0} | all-to-all | bytes 589824 | tf_op jit(solution)/shard_map/all_to_all | solution.py:613
  17.3 1.7 %collective-permute-start.6 = (bf16[4,16,2304]{2,1,0:T(8,128)(2,1)S(1)}, bf16[4,16,2304]{2,1,0:T(8,128)(2,1)S(1)}, u32[]{:S(2)}, u32[]{:S(2)}) collective-permute-start(bf16[4,16,2304]{2,1,0:T(8,128)(2,1)S(1)} %all_to_all.20.refs_0_), channel_id=1, source_target_pairs={{1,0},{2,1},{3,2},{0,3},{5,4},{6,5},{7,6},{4,7},{9,8},{10,9},{11,1... | collective-permute-start | bytes 884744 | tf_op jit(solution)/shard_map/ppermute | solution.py:599
  19.1 2.4 %collective-permute-done.refs_1_ = bf16[4,16,2304]{2,1,0:T(8,128)(2,1)S(1)} collective-permute-done((bf16[4,16,2304]{2,1,0:T(8,128)(2,1)S(1)}, bf16[4,16,2304]{2,1,0:T(8,128)(2,1)S(1)}, u32[]{:S(2)}, u32[]{:S(2)}) %collective-permute-start) | collective-permute-done | bytes 294944 | tf_op jit(solution)/shard_map/ppermute | solution.py:599
  21.5 2.8 %collective-permute-start.1 = (bf16[4,16,2304]{2,1,0:T(8,128)(2,1)S(1)}, bf16[4,16,2304]{2,1,0:T(8,128)(2,1)S(1)}, u32[]{:S(2)}, u32[]{:S(2)}) collective-permute-start(bf16[4,16,2304]{2,1,0:T(8,128)(2,1)S(1)} %collective-permute-done.refs_1_), channel_id=1, source_target_pairs={{1,0},{2,1},{3,2},{0,3},{5,4},{6,5},{7,6},{4,7},{9,8},{10,9},{11,1... | collective-permute-start | bytes 884744 | tf_op jit(solution)/shard_map/ppermute | solution.py:599
  26.6 3.9 %block_product.2 = (bf16[4,16,2048]{2,1,0:T(8,128)(2,1)S(1)}, bf16[4,16,2048]{2,1,0:T(8,128)(2,1)S(1)}, bf16[4,16,2048]{2,1,0:T(8,128)(2,1)S(1)}, bf16[4,16,2048...) custom-call(bf16[4,16,2304]{2,1,0:T(8,128)(2,1)S(1)} %all_to_all.20.refs_0_, ...), custom_call_target="tpu_custom_call" | custom-call | flops 1509949440 | bytes 12000000 | tf_op jit(solution)/shard_map/block_product/pallas_call | solution.py:217
  31.2 2.1 %collective-permute-start.8 = (bf16[4,16,2048]{2,1,0:T(8,128)(2,1)S(1)}, bf16[4,16,2048]{2,1,0:T(8,128)(2,1)S(1)}, u32[]{:S(2)}, u32[]{:S(2)}) collective-permute-start(bf16[4,16,2048]{2,1,0:T(8,128)(2,1)S(1)} %get-tuple-element.35), channel_id=1, source_target_pairs={{16,0},{17,1},{18,2},{19,3},{20,4},{21,5},{22,6},{23,7},{24,8},{25... | collective-permute-start | bytes 786440 | tf_op jit(solution)/shard_map/ppermute | solution.py:604
  35.7 1.7 %collective-permute-start.5 = (bf16[4,16,2304]{2,1,0:T(8,128)(2,1)S(1)}, bf16[4,16,2304]{2,1,0:T(8,128)(2,1)S(1)}, u32[]{:S(2)}, u32[]{:S(2)}) collective-permute-start(bf16[4,16,2304]{2,1,0:T(8,128)(2,1)S(1)} %collective-permute-done.1.refs_0_), channel_id=1, source_target_pairs={{1,0},{2,1},{3,2},{0,3},{5,4},{6,5},{7,6},{4,7},{9,8},{10,9},{11,1... | collective-permute-start | bytes 884744 | tf_op jit(solution)/shard_map/ppermute | solution.py:599
  37.5 4.7 %collective-permute-done.4.refs_2_ = bf16[4,16,2304]{2,1,0:T(8,128)(2,1)S(1)} collective-permute-done((bf16[4,16,2304]{2,1,0:T(8,128)(2,1)S(1)}, bf16[4,16,2304]{2,1,0:T(8,128)(2,1)S(1)}, u32[]{:S(2)}, u32[]{:S(2)}) %collective-permute-start.4) | collective-permute-done | bytes 294944 | tf_op jit(solution)/shard_map/ppermute | solution.py:599
  42.4 3.6 %block_product.3 = (bf16[4,16,2048]{2,1,0:T(8,128)(2,1)S(1)}, bf16[4,16,2048]{2,1,0:T(8,128)(2,1)}, bf16[4,16,2048]{2,1,0:T(8,128)(2,1)S(1)}, bf16[4,16,2048]{2,1,0:T(8,128)(2,1)S(1)}, bf16[32,16,256]{2,1,0:T(8,128)(2,1)}) custom-call(bf16[4,16,2304]{2,1,0:T(8,128)(2,1)S(1)} %collective-permute-done.1.refs_0_, ...), custom_call_target="tpu_custom_call" | custom-call | flops 1509949440 | bytes 12000000 | tf_op jit(solution)/shard_map/block_product/pallas_call | solution.py:217
  48.6 2.6 %collective-permute-start.12 = (bf16[4,16,2048]{2,1,0:T(8,128)(2,1)S(1)}, bf16[4,16,2048]{2,1,0:T(8,128)(2,1)S(1)}, u32[]{:S(2)}, u32[]{:S(2)}) collective-permute-start(bf16[4,16,2048]{2,1,0:T(8,128)(2,1)S(1)} %get-tuple-element.40), channel_id=1, source_target_pairs={{8,0},{9,1},{10,2},{11,3},{12,4},{13,5},{14,6},{15,7},{16,8},{17,9... | collective-permute-start | bytes 786440 | tf_op jit(solution)/shard_map/ppermute | solution.py:604
  52.6 6.5 %all-to-all-start.1 = ((bf16[32,16,256]{2,1,0:T(8,128)(2,1)}), bf16[32,16,256]{2,1,0:T(8,128)(2,1)S(1)}, u32[]{:S(2)}, u32[]{:S(2)}) async-start(bf16[32,16,256]{2,1,0:T(8,128)(2,1)} %get-tuple-element.37), calls=%async_computation.1 | async-start | bytes 524288 | tf_op jit(solution)/shard_map/all_to_all | solution.py:588
  59.2 1.9 %collective-permute-start.14 = (bf16[16,2048]{1,0:T(8,128)(2,1)}, bf16[16,2048]{1,0:T(8,128)(2,1)S(1)}, u32[]{:S(2)}, u32[]{:S(2)}) collective-permute-start(bf16[16,2048]{1,0:T(8,128)(2,1)} %get-tuple-element.46), channel_id=1, source_target_pairs={{3,0},{0,1},{1,2},{2,3},{7,4},{4,5},{5,6},{6,7},{11,8},{8,9},{9,10... | collective-permute-start | bytes 196616 | tf_op jit(solution)/shard_map/ppermute | solution.py:599
  62.6 3.4 %readout.1.refs_6_.read_ref = f32[1,2048]{1,0:T(1,128)S(1)} custom-call(f32[8,1024]{1,0:T(8,128)S(1)} %reshape.34.head_ref, bf16[1,2048,1024]{2,1,0:T(8,128)(2,1)} %w_hbm.3), custom_call_target="tpu_custom_call" | custom-call | flops 200000000 | bytes 5000000 | tf_op jit(solution)/shard_map/readout/pallas_call | solution.py:472
  66.0 2.3 %all-to-all-done.1.parts_ref = bf16[32,16,256]{2,1,0:T(8,128)(2,1)S(1)} async-done(((bf16[32,16,256]{2,1,0:T(8,128)(2,1)}), bf16[32,16,256]{2,1,0:T(8,128)(2,1)S(1)}, u32[]{:S(2)}, u32[]{:S(2)}) %all-to-all-start.1) | async-done | bytes 262176 | tf_op jit(solution)/shard_map/all_to_all | solution.py:588
  68.3 3.7 %attend_main.1 = (bf16[32,16,256]{2,1,0:T(8,128)(2,1)}, f32[8,2048]{1,0:T(8,128)S(1)}) custom-call(s32[1]{0:T(128)} %copy.12.len_ref, f32[1,10240]{1,0:T(1,128)S(1)} %bitcast.15, f32[8,128]{1,0:T(8,128)S(1)} %get-tuple-element.64.cos_ref, f32[8,128]{1,0:T(8,128)S(1)} %get-tuple-element.65.sin_ref, bf16[256,2048]{1,0:T(8,128)(2,1)S(1)} %bitcast.10, ...), custom_call_target="tpu_custom_call" | custom-call | flops 200000000 | bytes 6000000 | tf_op jit(solution)/shard_map/attend_main/pallas_call | solution.py:395
  72.0 5.3 %all-to-all-start.2 = ((bf16[32,16,256]{2,1,0:T(8,128)(2,1)}), bf16[32,16,256]{2,1,0:T(8,128)(2,1)S(1)}, u32[]{:S(2)}, u32[]{:S(2)}) async-start(bf16[32,16,256]{2,1,0:T(8,128)(2,1)} %get-tuple-element.48), calls=%async_computation.2 | async-start | bytes 524288 | tf_op jit(solution)/shard_map/all_to_all | solution.py:588
  77.6 3.4 %collective-permute-start.16 = (bf16[16,2048]{1,0:T(8,128)(2,1)S(1)}, bf16[16,2048]{1,0:T(8,128)(2,1)S(1)}, u32[]{:S(2)}, u32[]{:S(2)}) collective-permute-start(bf16[16,2048]{1,0:T(8,128)(2,1)S(1)} %get-tuple-element.50), channel_id=1, source_target_pairs={{2,0},{3,1},{0,2},{1,3},{6,4},{7,5},{4,6},{5,7},{10,8},{11,9},{8,1... | collective-permute-start | bytes 196616 | tf_op jit(solution)/shard_map/ppermute | solution.py:599
  82.4 2.0 %collective-permute-done.16.refs_0_.refs_6_ = bf16[16,2048]{1,0:T(8,128)(2,1)S(1)} collective-permute-done((bf16[16,2048]{1,0:T(8,128)(2,1)S(1)}, bf16[16,2048]{1,0:T(8,128)(2,1)S(1)}, u32[]{:S(2)}, u32[]{:S(2)}) %collective-permute-start.16) | collective-permute-done | bytes 65568 | tf_op jit(solution)/shard_map/ppermute | solution.py:599
  84.4 3.2 %collective-permute-done.17.refs_1_.refs_7_ = bf16[16,2048]{1,0:T(8,128)(2,1)S(1)} collective-permute-done((bf16[16,2048]{1,0:T(8,128)(2,1)S(1)}, bf16[16,2048]{1,0:T(8,128)(2,1)S(1)}, u32[]{:S(2)}, u32[]{:S(2)}) %collective-permute-start.17) | collective-permute-done | bytes 65568 | tf_op jit(solution)/shard_map/ppermute | solution.py:599
  87.6 3.4 %out_product.1 = f32[32,16,256]{2,1,0:T(8,128)} custom-call(bf16[32,16,256]{2,1,0:T(8,128)(2,1)S(1)} %all-to-all-done.2.x_ref, f32[1,2048]{1,0:T(1,128)S(1)} %readout.1.refs_6_.read_ref, bf16[1,2048,1024]{2,1,0:T(8,128)(2,1)} %w_hbm.3, bf16[16,2048]{1,0:T(8,128)(2,1)S(1)} %collective-permute-done.16.refs_0_.refs_6_, ...), custom_call_target="tpu_custom_call" | custom-call | flops 300000000 | bytes 5000000 | tf_op jit(solution)/shard_map/out_product/pallas_call | solution.py:519
  91.0 6.2 %all-to-all-start.3 = ((f32[32,16,256]{2,1,0:T(8,128)}), f32[32,16,256]{2,1,0:T(8,128)S(1)}, u32[]{:S(2)}, u32[]{:S(2)}) async-start(f32[32,16,256]{2,1,0:T(8,128)} %out_product.1), calls=%async_computation.3 | async-start | bytes 1048576 | tf_op jit(solution)/shard_map/all_to_all | solution.py:588
  98.0 2.8 %collective-permute-start.18 = (bf16[16,2048]{1,0:T(8,128)(2,1)S(1)}, bf16[16,2048]{1,0:T(8,128)(2,1)S(1)}, u32[]{:S(2)}, u32[]{:S(2)}) collective-permute-start(bf16[16,2048]{1,0:T(8,128)(2,1)S(1)} %get-tuple-element.54), channel_id=1, source_target_pairs={{7,0},{4,1},{5,2},{6,3},{3,4},{0,5},{1,6},{2,7},{15,8},{12,9},{13,... | collective-permute-start | bytes 196616 | tf_op jit(solution)/shard_map/ppermute | solution.py:599
  102.2 4.6 %collective-permute-done.18.refs_4_ = bf16[16,2048]{1,0:T(8,128)(2,1)S(1)} collective-permute-done((bf16[16,2048]{1,0:T(8,128)(2,1)S(1)}, bf16[16,2048]{1,0:T(8,128)(2,1)S(1)}, u32[]{:S(2)}, u32[]{:S(2)}) %collective-permute-start.18) | collective-permute-done | bytes 65568 | tf_op jit(solution)/shard_map/ppermute | solution.py:599
  106.9 3.0 %attend_cont.1.mixed_ref = bf16[16,8192]{1,0:T(8,128)(2,1)S(1)} custom-call(s32[1]{0:T(128)} %copy.12.len_ref, s32[1]{0:T(128)S(6)} %copy.13.bound_ref, f32[1,10240]{1,0:T(1,128)S(1)} %bitcast.17, f32[16,128]{1,0:T(8,128)S(1)} %get-tuple-element.66.cos_ref, f32[16,128]{1,0:T(8,128)S(1)} %get-tuple-element.67.sin_ref, bf16[256,2048]{1,0:T(8,128)(2,1)S(1)} %bitcast.11, ...), custom_call_target="tpu_custom_call" | custom-call | flops 400000000 | bytes 8000000 | tf_op jit(solution)/shard_map/attend_cont/pallas_call | solution.py:441
  (54 shorter events, 19.4 us)
Async XLA Ops:
  14.2 7.3 %collective-permute-start = (bf16[4,16,2304]{2,1,0:T(8,128)(2,1)S(1)}, bf16[4,16,2304]{2,1,0:T(8,128)(2,1)S(1)}, u32[]{:S(2)}, u32[]{:S(2)}) collective-permute-start(bf16[4,16,2304]{2,1,0:T(8,128)(2,1)S(1)} %all_to_all.20.refs_0_), channel_id=1, source_target_pairs={{4,0},{5,1},{6,2},{7,3},{0,4},{1,5},{2,6},{3,7},{12,8},{13,9},{14,... | collective-permute-start | bytes 884744 | tf_op jit(solution)/shard_map/ppermute | solution.py:599
  15.8 9.1 %collective-permute-start.3 = (bf16[4,16,2304]{2,1,0:T(8,128)(2,1)S(1)}, bf16[4,16,2304]{2,1,0:T(8,128)(2,1)S(1)}, u32[]{:S(2)}, u32[]{:S(2)}) collective-permute-start(bf16[4,16,2304]{2,1,0:T(8,128)(2,1)S(1)} %all_to_all.20.refs_0_), channel_id=1, source_target_pairs={{3,0},{0,1},{1,2},{2,3},{7,4},{4,5},{5,6},{6,7},{11,8},{8,9},{9,10... | collective-permute-start | bytes 884744 | tf_op jit(solution)/shard_map/ppermute | solution.py:599
  17.3 9.3 %collective-permute-start.6 = (bf16[4,16,2304]{2,1,0:T(8,128)(2,1)S(1)}, bf16[4,16,2304]{2,1,0:T(8,128)(2,1)S(1)}, u32[]{:S(2)}, u32[]{:S(2)}) collective-permute-start(bf16[4,16,2304]{2,1,0:T(8,128)(2,1)S(1)} %all_to_all.20.refs_0_), channel_id=1, source_target_pairs={{1,0},{2,1},{3,2},{0,3},{5,4},{6,5},{7,6},{4,7},{9,8},{10,9},{11,1... | collective-permute-start | bytes 884744 | tf_op jit(solution)/shard_map/ppermute | solution.py:599
  21.5 12.7 %collective-permute-start.1 = (bf16[4,16,2304]{2,1,0:T(8,128)(2,1)S(1)}, bf16[4,16,2304]{2,1,0:T(8,128)(2,1)S(1)}, u32[]{:S(2)}, u32[]{:S(2)}) collective-permute-start(bf16[4,16,2304]{2,1,0:T(8,128)(2,1)S(1)} %collective-permute-done.refs_1_), channel_id=1, source_target_pairs={{1,0},{2,1},{3,2},{0,3},{5,4},{6,5},{7,6},{4,7},{9,8},{10,9},{11,1... | collective-permute-start | bytes 884744 | tf_op jit(solution)/shard_map/ppermute | solution.py:599
  24.3 11.4 %collective-permute-start.2 = (bf16[4,16,2304]{2,1,0:T(8,128)(2,1)S(1)}, bf16[4,16,2304]{2,1,0:T(8,128)(2,1)S(1)}, u32[]{:S(2)}, u32[]{:S(2)}) collective-permute-start(bf16[4,16,2304]{2,1,0:T(8,128)(2,1)S(1)} %collective-permute-done.refs_1_), channel_id=1, source_target_pairs={{3,0},{0,1},{1,2},{2,3},{7,4},{4,5},{5,6},{6,7},{11,8},{8,9},{9,10... | collective-permute-start | bytes 884744 | tf_op jit(solution)/shard_map/ppermute | solution.py:599
  30.5 18.1 %collective-permute-start.7 = (bf16[4,16,2048]{2,1,0:T(8,128)(2,1)S(1)}, bf16[4,16,2048]{2,1,0:T(8,128)(2,1)S(1)}, u32[]{:S(2)}, u32[]{:S(2)}) collective-permute-start(bf16[4,16,2048]{2,1,0:T(8,128)(2,1)S(1)} %get-tuple-element.34), channel_id=1, source_target_pairs={{24,0},{25,1},{26,2},{27,3},{28,4},{29,5},{30,6},{31,7},{0,8},{1,9... | collective-permute-start | bytes 786440 | tf_op jit(solution)/shard_map/ppermute | solution.py:604
  31.2 20.1 %collective-permute-start.8 = (bf16[4,16,2048]{2,1,0:T(8,128)(2,1)S(1)}, bf16[4,16,2048]{2,1,0:T(8,128)(2,1)S(1)}, u32[]{:S(2)}, u32[]{:S(2)}) collective-permute-start(bf16[4,16,2048]{2,1,0:T(8,128)(2,1)S(1)} %get-tuple-element.35), channel_id=1, source_target_pairs={{16,0},{17,1},{18,2},{19,3},{20,4},{21,5},{22,6},{23,7},{24,8},{25... | collective-permute-start | bytes 786440 | tf_op jit(solution)/shard_map/ppermute | solution.py:604
  33.2 18.0 %collective-permute-start.9 = (bf16[4,16,2048]{2,1,0:T(8,128)(2,1)S(1)}, bf16[4,16,2048]{2,1,0:T(8,128)(2,1)S(1)}, u32[]{:S(2)}, u32[]{:S(2)}) collective-permute-start(bf16[4,16,2048]{2,1,0:T(8,128)(2,1)S(1)} %get-tuple-element.36), channel_id=1, source_target_pairs={{8,0},{9,1},{10,2},{11,3},{12,4},{13,5},{14,6},{15,7},{16,8},{17,9... | collective-permute-start | bytes 786440 | tf_op jit(solution)/shard_map/ppermute | solution.py:604
  34.2 7.9 %collective-permute-start.4 = (bf16[4,16,2304]{2,1,0:T(8,128)(2,1)S(1)}, bf16[4,16,2304]{2,1,0:T(8,128)(2,1)S(1)}, u32[]{:S(2)}, u32[]{:S(2)}) collective-permute-start(bf16[4,16,2304]{2,1,0:T(8,128)(2,1)S(1)} %collective-permute-done.3.refs_3_), channel_id=1, source_target_pairs={{3,0},{0,1},{1,2},{2,3},{7,4},{4,5},{5,6},{6,7},{11,8},{8,9},{9,10... | collective-permute-start | bytes 884744 | tf_op jit(solution)/shard_map/ppermute | solution.py:599
  35.7 6.7 %collective-permute-start.5 = (bf16[4,16,2304]{2,1,0:T(8,128)(2,1)S(1)}, bf16[4,16,2304]{2,1,0:T(8,128)(2,1)S(1)}, u32[]{:S(2)}, u32[]{:S(2)}) collective-permute-start(bf16[4,16,2304]{2,1,0:T(8,128)(2,1)S(1)} %collective-permute-done.1.refs_0_), channel_id=1, source_target_pairs={{1,0},{2,1},{3,2},{0,3},{5,4},{6,5},{7,6},{4,7},{9,8},{10,9},{11,1... | collective-permute-start | bytes 884744 | tf_op jit(solution)/shard_map/ppermute | solution.py:599
  46.1 22.3 %collective-permute-start.10 = (bf16[4,16,2048]{2,1,0:T(8,128)(2,1)}, bf16[4,16,2048]{2,1,0:T(8,128)(2,1)S(1)}, u32[]{:S(2)}, u32[]{:S(2)}) collective-permute-start(bf16[4,16,2048]{2,1,0:T(8,128)(2,1)} %get-tuple-element.38), channel_id=1, source_target_pairs={{24,0},{25,1},{26,2},{27,3},{28,4},{29,5},{30,6},{31,7},{0,8},{1,9... | collective-permute-start | bytes 786440 | tf_op jit(solution)/shard_map/ppermute | solution.py:604
  47.1 21.2 %collective-permute-start.11 = (bf16[4,16,2048]{2,1,0:T(8,128)(2,1)S(1)}, bf16[4,16,2048]{2,1,0:T(8,128)(2,1)S(1)}, u32[]{:S(2)}, u32[]{:S(2)}) collective-permute-start(bf16[4,16,2048]{2,1,0:T(8,128)(2,1)S(1)} %get-tuple-element.39), channel_id=1, source_target_pairs={{16,0},{17,1},{18,2},{19,3},{20,4},{21,5},{22,6},{23,7},{24,8},{25... | collective-permute-start | bytes 786440 | tf_op jit(solution)/shard_map/ppermute | solution.py:604
  48.6 19.7 %collective-permute-start.12 = (bf16[4,16,2048]{2,1,0:T(8,128)(2,1)S(1)}, bf16[4,16,2048]{2,1,0:T(8,128)(2,1)S(1)}, u32[]{:S(2)}, u32[]{:S(2)}) collective-permute-start(bf16[4,16,2048]{2,1,0:T(8,128)(2,1)S(1)} %get-tuple-element.40), channel_id=1, source_target_pairs={{8,0},{9,1},{10,2},{11,3},{12,4},{13,5},{14,6},{15,7},{16,8},{17,9... | collective-permute-start | bytes 786440 | tf_op jit(solution)/shard_map/ppermute | solution.py:604
  52.5 8.5 %collective-permute-start.13 = (bf16[16,2048]{1,0:T(8,128)(2,1)S(1)}, bf16[16,2048]{1,0:T(8,128)(2,1)S(1)}, u32[]{:S(2)}, u32[]{:S(2)}) collective-permute-start(bf16[16,2048]{1,0:T(8,128)(2,1)S(1)} %get-tuple-element.45), channel_id=1, source_target_pairs={{4,0},{5,1},{6,2},{7,3},{0,4},{1,5},{2,6},{3,7},{12,8},{13,9},{14,... | collective-permute-start | bytes 196616 | tf_op jit(solution)/shard_map/ppermute | solution.py:599
  52.6 15.8 %all-to-all-start.1 = ((bf16[32,16,256]{2,1,0:T(8,128)(2,1)}), bf16[32,16,256]{2,1,0:T(8,128)(2,1)S(1)}, u32[]{:S(2)}, u32[]{:S(2)}) async-start(bf16[32,16,256]{2,1,0:T(8,128)(2,1)} %get-tuple-element.37), calls=%async_computation.1 | async-start | bytes 524288 | tf_op jit(solution)/shard_map/all_to_all | solution.py:588
  59.2 6.8 %collective-permute-start.14 = (bf16[16,2048]{1,0:T(8,128)(2,1)}, bf16[16,2048]{1,0:T(8,128)(2,1)S(1)}, u32[]{:S(2)}, u32[]{:S(2)}) collective-permute-start(bf16[16,2048]{1,0:T(8,128)(2,1)} %get-tuple-element.46), channel_id=1, source_target_pairs={{3,0},{0,1},{1,2},{2,3},{7,4},{4,5},{5,6},{6,7},{11,8},{8,9},{9,10... | collective-permute-start | bytes 196616 | tf_op jit(solution)/shard_map/ppermute | solution.py:599
  61.0 5.0 %collective-permute-start.15 = (bf16[16,2048]{1,0:T(8,128)(2,1)}, bf16[16,2048]{1,0:T(8,128)(2,1)S(1)}, u32[]{:S(2)}, u32[]{:S(2)}) collective-permute-start(bf16[16,2048]{1,0:T(8,128)(2,1)} %copy-done.5), channel_id=1, source_target_pairs={{1,0},{2,1},{3,2},{0,3},{5,4},{6,5},{7,6},{4,7},{9,8},{10,9},{11,1... | collective-permute-start | bytes 196616 | tf_op jit(solution)/shard_map/ppermute | solution.py:599
  72.0 37.9 %copy-start.3 = (bf16[1,2,8192]{2,1,0:T(2,128)(2,1)S(1)}, bf16[1,2,8192]{2,1,0:T(2,128)(2,1)}, u32[]{:S(2)}) copy-start(bf16[1,2,8192]{2,1,0:T(2,128)(2,1)} %param.10) | copy-start | bytes 98308
  72.0 15.6 %all-to-all-start.2 = ((bf16[32,16,256]{2,1,0:T(8,128)(2,1)}), bf16[32,16,256]{2,1,0:T(8,128)(2,1)S(1)}, u32[]{:S(2)}, u32[]{:S(2)}) async-start(bf16[32,16,256]{2,1,0:T(8,128)(2,1)} %get-tuple-element.48), calls=%async_computation.2 | async-start | bytes 524288 | tf_op jit(solution)/shard_map/all_to_all | solution.py:588
  77.6 6.8 %collective-permute-start.16 = (bf16[16,2048]{1,0:T(8,128)(2,1)S(1)}, bf16[16,2048]{1,0:T(8,128)(2,1)S(1)}, u32[]{:S(2)}, u32[]{:S(2)}) collective-permute-start(bf16[16,2048]{1,0:T(8,128)(2,1)S(1)} %get-tuple-element.50), channel_id=1, source_target_pairs={{2,0},{3,1},{0,2},{1,3},{6,4},{7,5},{4,6},{5,7},{10,8},{11,9},{8,1... | collective-permute-start | bytes 196616 | tf_op jit(solution)/shard_map/ppermute | solution.py:599
  80.9 6.7 %collective-permute-start.17 = (bf16[16,2048]{1,0:T(8,128)(2,1)S(1)}, bf16[16,2048]{1,0:T(8,128)(2,1)S(1)}, u32[]{:S(2)}, u32[]{:S(2)}) collective-permute-start(bf16[16,2048]{1,0:T(8,128)(2,1)S(1)} %get-tuple-element.51), channel_id=1, source_target_pairs={{6,0},{7,1},{4,2},{5,3},{2,4},{3,5},{0,6},{1,7},{14,8},{15,9},{12,... | collective-permute-start | bytes 196616 | tf_op jit(solution)/shard_map/ppermute | solution.py:599
  91.0 18.9 %all-to-all-start.3 = ((f32[32,16,256]{2,1,0:T(8,128)}), f32[32,16,256]{2,1,0:T(8,128)S(1)}, u32[]{:S(2)}, u32[]{:S(2)}) async-start(f32[32,16,256]{2,1,0:T(8,128)} %out_product.1), calls=%async_computation.3 | async-start | bytes 1048576 | tf_op jit(solution)/shard_map/all_to_all | solution.py:588
  98.0 8.9 %collective-permute-start.18 = (bf16[16,2048]{1,0:T(8,128)(2,1)S(1)}, bf16[16,2048]{1,0:T(8,128)(2,1)S(1)}, u32[]{:S(2)}, u32[]{:S(2)}) collective-permute-start(bf16[16,2048]{1,0:T(8,128)(2,1)S(1)} %get-tuple-element.54), channel_id=1, source_target_pairs={{7,0},{4,1},{5,2},{6,3},{3,4},{0,5},{1,6},{2,7},{15,8},{12,9},{13,... | collective-permute-start | bytes 196616 | tf_op jit(solution)/shard_map/ppermute | solution.py:599
  100.7 6.2 %collective-permute-start.19 = (bf16[16,2048]{1,0:T(8,128)(2,1)S(1)}, bf16[16,2048]{1,0:T(8,128)(2,1)S(1)}, u32[]{:S(2)}, u32[]{:S(2)}) collective-permute-start(bf16[16,2048]{1,0:T(8,128)(2,1)S(1)} %get-tuple-element.55), channel_id=1, source_target_pairs={{5,0},{6,1},{7,2},{4,3},{1,4},{2,5},{3,6},{0,7},{13,8},{14,9},{15,... | collective-permute-start | bytes 196616 | tf_op jit(solution)/shard_map/ppermute | solution.py:599
  (5 other events, 122.8 us)

commit v22 on v20

--- a/solution.py
+++ b/solution.py
@@ -604,8 +604,8 @@
     return lax.ppermute(rows, "tp", route)
 
 
-FIRST_HOMES = ((0, 0), (1, 0), (0, 1), (0, 3))
-SECOND_HOMES = ((1, 1), (1, 3), (0, 2), (1, 2))
+FIRST_HOMES = ((0, 0), (1, 0), (0, 1), (0, 3), (1, 1))
+SECOND_HOMES = ((1, 3), (0, 2), (1, 2))
 HOMES = FIRST_HOMES + SECOND_HOMES
 
 
@@ -615,16 +615,16 @@
     after, before = from_side(near, 0, 1), from_side(near, 0, 3)
     over_after, over_before = from_side(over, 0, 1), from_side(over, 0, 3)
     far = [from_side(before, 0, 3), from_side(over_after, 0, 1)]
-    *first, main, weight = block_product([near, over, after, before], blocks)
+    *first, main, weight = block_product([near, over, after, before, over_after], blocks)
     first = [first[0]] + [from_along(first[k], -k) for k in range(1, ROW_BLOCKS)]
-    *second, main = block_product([over_after, over_before] + far, weight, main, HOMES)
+    *second, main = block_product([over_before] + far, weight, main, HOMES)
     main, first = lax.optimization_barrier((main, first))
     second = [second[0]] + [from_along(second[k], -k) for k in range(1, ROW_BLOCKS)]
     received = []
     for homes, parts in ((FIRST_HOMES, first), (SECOND_HOMES, second)):
         for (dy, dx), summed in zip(homes, sum_parts(bias, parts)):
             received.append(from_side(summed, -dy, -dx) if dy or dx else summed)
-    return received, exchange(main), second[1:] + received[1:4]
+    return received, exchange(main), second[1:] + received[1:5]
 
 
 def on_device(

time: 112 us -> 125 us (1.12)
  waiting for transfers between devices: 21.2 us -> 31.5 us
  starting transfers between devices: 50 us -> 53.6 us
    ppermute x6, waiting for transfers between devices: 0.02 us -> 6.72 us  [from_along(): return lax.ppermute(rows, 'tp', route)]
    ppermute x14, waiting for transfers between devices: 18.9 us -> 24.7 us  [from_side(): return lax.ppermute(rows, 'tp', route)]
    ppermute x14, starting transfers between devices: 23.2 us -> 26.5 us  [from_side(): return lax.ppermute(rows, 'tp', route)]
    all_to_all x3, starting transfers between devices: 18 us -> 20.8 us  [exchange(): return lax.all_to_all(rows, 'tp', split_axis=0, concat_axis=0, tiled=True)]
    ppermute x6, starting transfers between devices: 8.86 us -> 6.22 us  [from_along(): return lax.ppermute(rows, 'tp', route)]
    all_to_all x3, waiting for transfers between devices: 2.3 us -> 0.01 us  [exchange(): return lax.all_to_all(rows, 'tp', split_axis=0, concat_axis=0, tiled=True)]
  transfers between devices with their start and end apart: 23 -> 23, of which waited for: 8 -> 9; matrix products, arithmetic and copies ran while one was open for 0% -> 0% of each run, Pallas kernels for 13% -> 12%
where the time goes in v22:
time: 125 us; the launch traced here: 124 us
  starting transfers between devices  53.6 us (43%)
  waiting for transfers between devices  31.5 us (25%)
  Pallas kernels  24.3 us (19%)
  blocking collectives  12.2 us (10%)
  between operations  2.3 us (2%)
    ppermute x14, starting transfers between devices, from_side(): return lax.ppermute(rows, 'tp', route)  26.5 us
    ppermute x14, waiting for transfers between devices, from_side(): return lax.ppermute(rows, 'tp', route)  24.7 us
    all_to_all x3, starting transfers between devices, exchange(): return lax.all_to_all(rows, 'tp', split_axis=0, concat_axis=0, tiled=True)  20.8 us
    all_to_all x1, blocking collectives, project(): lax.all_to_all(rows, 'tp', split_axis=0, concat_axis=0, tiled=True, axis_...  12.2 us
    pallas_call x2, Pallas kernels, block_product(): pl.pallas_call(functools.partial(product_kernel, tiles, counts, places),...  7.55 us
    ppermute x6, waiting for transfers between devices, from_along(): return lax.ppermute(rows, 'tp', route)  6.72 us
    ppermute x6, starting transfers between devices, from_along(): return lax.ppermute(rows, 'tp', route)  6.22 us
    pallas_call x1, Pallas kernels, attend_main(): pl.pallas_call(attend_main_kernel, out_shape=(jax.ShapeDtypeStruct((32, 1...  3.7 us
  transfers between devices with their start and end apart: 23, of which 9 were waited for; matrix products, arithmetic and copies ran while one was open for 0% of the time, Pallas kernels for 12%

profile of v22, /device:TPU:0, one launch (start us, length us, event | category | flops | bytes accessed | tf_op | source)
XLA Modules:
  0.0 124.3 jit_solution(17292686070229249567)
XLA Ops:
  2.0 12.2 %all_to_all.20.refs_0_ = bf16[4,16,2304]{2,1,0:T(8,128)(2,1)S(1)} all-to-all(bf16[4,16,2304]{2,1,0:T(8,128)(2,1)S(1)} %norm_rows.1), channel_id=1, replica_groups={{0,8,16,24},{1,9,17,25},{2,10,18,26},{3,11,19,27},{4,12,20,28},{5,13,21..., dimensions={0} | all-to-all | bytes 589824 | tf_op jit(solution)/shard_map/all_to_all | solution.py:613
  17.3 4.2 %collective-permute-done.refs_1_ = bf16[4,16,2304]{2,1,0:T(8,128)(2,1)S(1)} collective-permute-done((bf16[4,16,2304]{2,1,0:T(8,128)(2,1)S(1)}, bf16[4,16,2304]{2,1,0:T(8,128)(2,1)S(1)}, u32[]{:S(2)}, u32[]{:S(2)}) %collective-permute-start) | collective-permute-done | bytes 294944 | tf_op jit(solution)/shard_map/ppermute | solution.py:599
  21.5 2.8 %collective-permute-start.4 = (bf16[4,16,2304]{2,1,0:T(8,128)(2,1)S(1)}, bf16[4,16,2304]{2,1,0:T(8,128)(2,1)S(1)}, u32[]{:S(2)}, u32[]{:S(2)}) collective-permute-start(bf16[4,16,2304]{2,1,0:T(8,128)(2,1)S(1)} %collective-permute-done.refs_1_), channel_id=1, source_target_pairs={{1,0},{2,1},{3,2},{0,3},{5,4},{6,5},{7,6},{4,7},{9,8},{10,9},{11,1... | collective-permute-start | bytes 884744 | tf_op jit(solution)/shard_map/ppermute | solution.py:599
  27.1 4.7 %collective-permute-done.4.refs_4_ = bf16[4,16,2304]{2,1,0:T(8,128)(2,1)S(1)} collective-permute-done((bf16[4,16,2304]{2,1,0:T(8,128)(2,1)S(1)}, bf16[4,16,2304]{2,1,0:T(8,128)(2,1)S(1)}, u32[]{:S(2)}, u32[]{:S(2)}) %collective-permute-start.4) | collective-permute-done | bytes 294944 | tf_op jit(solution)/shard_map/ppermute | solution.py:599
  31.7 3.7 %collective-permute-start.5 = (bf16[4,16,2304]{2,1,0:T(8,128)(2,1)S(1)}, bf16[4,16,2304]{2,1,0:T(8,128)(2,1)S(1)}, u32[]{:S(2)}, u32[]{:S(2)}) collective-permute-start(bf16[4,16,2304]{2,1,0:T(8,128)(2,1)S(1)} %collective-permute-done.4.refs_4_), channel_id=1, source_target_pairs={{1,0},{2,1},{3,2},{0,3},{5,4},{6,5},{7,6},{4,7},{9,8},{10,9},{11,1... | collective-permute-start | bytes 884744 | tf_op jit(solution)/shard_map/ppermute | solution.py:599
  35.4 2.2 %collective-permute-done.6.refs_2_ = bf16[4,16,2304]{2,1,0:T(8,128)(2,1)S(1)} collective-permute-done((bf16[4,16,2304]{2,1,0:T(8,128)(2,1)S(1)}, bf16[4,16,2304]{2,1,0:T(8,128)(2,1)S(1)}, u32[]{:S(2)}, u32[]{:S(2)}) %collective-permute-start.6) | collective-permute-done | bytes 294944 | tf_op jit(solution)/shard_map/ppermute | solution.py:599
  37.6 4.4 %block_product.2 = (bf16[5,16,2048]{2,1,0:T(8,128)(2,1)S(1)}, bf16[5,16,2048]{2,1,0:T(8,128)(2,1)S(1)}, bf16[5,16,2048]{2,1,0:T(8,128)(2,1)S(1)}, bf16[5,16,2048...) custom-call(bf16[4,16,2304]{2,1,0:T(8,128)(2,1)S(1)} %all_to_all.20.refs_0_, ...), custom_call_target="tpu_custom_call" | custom-call | flops 1887436800 | bytes 12000000 | tf_op jit(solution)/shard_map/block_product/pallas_call | solution.py:217
  42.6 2.1 %collective-permute-start.8 = (bf16[5,16,2048]{2,1,0:T(8,128)(2,1)S(1)}, bf16[5,16,2048]{2,1,0:T(8,128)(2,1)S(1)}, u32[]{:S(2)}, u32[]{:S(2)}) collective-permute-start(bf16[5,16,2048]{2,1,0:T(8,128)(2,1)S(1)} %get-tuple-element.35), channel_id=1, source_target_pairs={{16,0},{17,1},{18,2},{19,3},{20,4},{21,5},{22,6},{23,7},{24,8},{25... | collective-permute-start | bytes 983048 | tf_op jit(solution)/shard_map/ppermute | solution.py:604
  46.2 3.2 %block_product.3 = (bf16[3,16,2048]{2,1,0:T(8,128)(2,1)S(1)}, bf16[3,16,2048]{2,1,0:T(8,128)(2,1)S(1)}, bf16[3,16,2048]{2,1,0:T(8,128)(2,1)S(1)}, bf16[3,16,2048]{2,1,0:T(8,128)(2,1)S(1)}, bf16[32,16,256]{2,1,0:T(8,128)(2,1)}) custom-call(bf16[4,16,2304]{2,1,0:T(8,128)(2,1)S(1)} %collective-permute-done.1.refs_0_, ...), custom_call_target="tpu_custom_call" | custom-call | flops 1132462080 | bytes 12000000 | tf_op jit(solution)/shard_map/block_product/pallas_call | solution.py:217
  51.4 6.1 %collective-permute-done.7.refs_1_ = bf16[5,16,2048]{2,1,0:T(8,128)(2,1)S(1)} collective-permute-done((bf16[5,16,2048]{2,1,0:T(8,128)(2,1)S(1)}, bf16[5,16,2048]{2,1,0:T(8,128)(2,1)S(1)}, u32[]{:S(2)}, u32[]{:S(2)}) %collective-permute-start.7) | collective-permute-done | bytes 327712 | tf_op jit(solution)/shard_map/ppermute | solution.py:604
  61.6 10.5 %all-to-all-start.1 = ((bf16[32,16,256]{2,1,0:T(8,128)(2,1)}), bf16[32,16,256]{2,1,0:T(8,128)(2,1)S(1)}, u32[]{:S(2)}, u32[]{:S(2)}) async-start(bf16[32,16,256]{2,1,0:T(8,128)(2,1)} %get-tuple-element.37), calls=%async_computation.1 | async-start | bytes 524288 | tf_op jit(solution)/shard_map/all_to_all | solution.py:588
  72.2 3.1 %collective-permute-start.15 = (bf16[16,2048]{1,0:T(8,128)(2,1)}, bf16[16,2048]{1,0:T(8,128)(2,1)S(1)}, u32[]{:S(2)}, u32[]{:S(2)}) collective-permute-start(bf16[16,2048]{1,0:T(8,128)(2,1)} %get-tuple-element.47), channel_id=1, source_target_pairs={{1,0},{2,1},{3,2},{0,3},{5,4},{6,5},{7,6},{4,7},{9,8},{10,9},{11,1... | collective-permute-start | bytes 196616 | tf_op jit(solution)/shard_map/ppermute | solution.py:599
  75.6 3.4 %readout.1.refs_7_.read_ref = f32[1,2048]{1,0:T(1,128)S(1)} custom-call(f32[8,1024]{1,0:T(8,128)S(1)} %reshape.34.head_ref, bf16[1,2048,1024]{2,1,0:T(8,128)(2,1)} %w_hbm.3), custom_call_target="tpu_custom_call" | custom-call | flops 200000000 | bytes 5000000 | tf_op jit(solution)/shard_map/readout/pallas_call | solution.py:472
  79.1 3.6 %collective-permute-done.16.refs_6_.refs_4_ = bf16[16,2048]{1,0:T(8,128)(2,1)S(1)} collective-permute-done((bf16[16,2048]{1,0:T(8,128)(2,1)S(1)}, bf16[16,2048]{1,0:T(8,128)(2,1)S(1)}, u32[]{:S(2)}, u32[]{:S(2)}) %collective-permute-start.16) | collective-permute-done | bytes 65568 | tf_op jit(solution)/shard_map/ppermute | solution.py:599
  82.7 3.7 %attend_main.1 = (bf16[32,16,256]{2,1,0:T(8,128)(2,1)}, f32[8,2048]{1,0:T(8,128)S(1)}) custom-call(s32[1]{0:T(128)} %copy.12.len_ref, f32[1,10240]{1,0:T(1,128)S(1)} %bitcast.15, f32[8,128]{1,0:T(8,128)S(1)} %get-tuple-element.64.cos_ref, f32[8,128]{1,0:T(8,128)S(1)} %get-tuple-element.65.sin_ref, bf16[256,2048]{1,0:T(8,128)(2,1)S(1)} %bitcast.10, ...), custom_call_target="tpu_custom_call" | custom-call | flops 200000000 | bytes 6000000 | tf_op jit(solution)/shard_map/attend_main/pallas_call | solution.py:395
  86.4 5.0 %all-to-all-start.2 = ((bf16[32,16,256]{2,1,0:T(8,128)(2,1)}), bf16[32,16,256]{2,1,0:T(8,128)(2,1)S(1)}, u32[]{:S(2)}, u32[]{:S(2)}) async-start(bf16[32,16,256]{2,1,0:T(8,128)(2,1)} %get-tuple-element.49), calls=%async_computation.2 | async-start | bytes 524288 | tf_op jit(solution)/shard_map/all_to_all | solution.py:588
  91.5 3.4 %collective-permute-start.17 = (bf16[16,2048]{1,0:T(8,128)(2,1)S(1)}, bf16[16,2048]{1,0:T(8,128)(2,1)S(1)}, u32[]{:S(2)}, u32[]{:S(2)}) collective-permute-start(bf16[16,2048]{1,0:T(8,128)(2,1)S(1)} %get-tuple-element.51), channel_id=1, source_target_pairs={{2,0},{3,1},{0,2},{1,3},{6,4},{7,5},{4,6},{5,7},{10,8},{11,9},{8,1... | collective-permute-start | bytes 196616 | tf_op jit(solution)/shard_map/ppermute | solution.py:599
  96.4 3.9 %collective-permute-done.17.refs_0_.refs_6_ = bf16[16,2048]{1,0:T(8,128)(2,1)S(1)} collective-permute-done((bf16[16,2048]{1,0:T(8,128)(2,1)S(1)}, bf16[16,2048]{1,0:T(8,128)(2,1)S(1)}, u32[]{:S(2)}, u32[]{:S(2)}) %collective-permute-start.17) | collective-permute-done | bytes 65568 | tf_op jit(solution)/shard_map/ppermute | solution.py:599
  100.3 2.8 %collective-permute-done.18.refs_1_.refs_7_ = bf16[16,2048]{1,0:T(8,128)(2,1)S(1)} collective-permute-done((bf16[16,2048]{1,0:T(8,128)(2,1)S(1)}, bf16[16,2048]{1,0:T(8,128)(2,1)S(1)}, u32[]{:S(2)}, u32[]{:S(2)}) %collective-permute-start.18) | collective-permute-done | bytes 65568 | tf_op jit(solution)/shard_map/ppermute | solution.py:599
  103.1 3.4 %out_product.1 = f32[32,16,256]{2,1,0:T(8,128)} custom-call(bf16[32,16,256]{2,1,0:T(8,128)(2,1)S(1)} %all-to-all-done.2.x_ref, f32[1,2048]{1,0:T(1,128)S(1)} %readout.1.refs_7_.read_ref, bf16[1,2048,1024]{2,1,0:T(8,128)(2,1)} %w_hbm.3, bf16[16,2048]{1,0:T(8,128)(2,1)S(1)} %collective-permute-done.17.refs_0_.refs_6_, ...), custom_call_target="tpu_custom_call" | custom-call | flops 300000000 | bytes 5000000 | tf_op jit(solution)/shard_map/out_product/pallas_call | solution.py:519
  106.5 5.4 %all-to-all-start.3 = ((f32[32,16,256]{2,1,0:T(8,128)}), f32[32,16,256]{2,1,0:T(8,128)S(1)}, u32[]{:S(2)}, u32[]{:S(2)}) async-start(f32[32,16,256]{2,1,0:T(8,128)} %out_product.1), calls=%async_computation.3 | async-start | bytes 1048576 | tf_op jit(solution)/shard_map/all_to_all | solution.py:588
  112.7 4.0 %collective-permute-start.19 = (bf16[16,2048]{1,0:T(8,128)(2,1)S(1)}, bf16[16,2048]{1,0:T(8,128)(2,1)S(1)}, u32[]{:S(2)}, u32[]{:S(2)}) collective-permute-start(bf16[16,2048]{1,0:T(8,128)(2,1)S(1)} %get-tuple-element.55), channel_id=1, source_target_pairs={{5,0},{6,1},{7,2},{4,3},{1,4},{2,5},{3,6},{0,7},{13,8},{14,9},{15,... | collective-permute-start | bytes 196616 | tf_op jit(solution)/shard_map/ppermute | solution.py:599
  116.7 3.4 %collective-permute-done.19.refs_5_ = bf16[16,2048]{1,0:T(8,128)(2,1)S(1)} collective-permute-done((bf16[16,2048]{1,0:T(8,128)(2,1)S(1)}, bf16[16,2048]{1,0:T(8,128)(2,1)S(1)}, u32[]{:S(2)}, u32[]{:S(2)}) %collective-permute-start.19) | collective-permute-done | bytes 65568 | tf_op jit(solution)/shard_map/ppermute | solution.py:599
  120.1 3.0 %attend_cont.1.mixed_ref = bf16[16,8192]{1,0:T(8,128)(2,1)S(1)} custom-call(s32[1]{0:T(128)} %copy.12.len_ref, s32[1]{0:T(128)S(6)} %copy.13.bound_ref, f32[1,10240]{1,0:T(1,128)S(1)} %bitcast.17, f32[16,128]{1,0:T(8,128)S(1)} %get-tuple-element.66.cos_ref, f32[16,128]{1,0:T(8,128)S(1)} %get-tuple-element.67.sin_ref, bf16[256,2048]{1,0:T(8,128)(2,1)S(1)} %bitcast.11, ...), custom_call_target="tpu_custom_call" | custom-call | flops 400000000 | bytes 8000000 | tf_op jit(solution)/shard_map/attend_cont/pallas_call | solution.py:441
  (52 shorter events, 18.2 us)
Async XLA Ops:
  14.2 7.3 %collective-permute-start = (bf16[4,16,2304]{2,1,0:T(8,128)(2,1)S(1)}, bf16[4,16,2304]{2,1,0:T(8,128)(2,1)S(1)}, u32[]{:S(2)}, u32[]{:S(2)}) collective-permute-start(bf16[4,16,2304]{2,1,0:T(8,128)(2,1)S(1)} %all_to_all.20.refs_0_), channel_id=1, source_target_pairs={{4,0},{5,1},{6,2},{7,3},{0,4},{1,5},{2,6},{3,7},{12,8},{13,9},{14,... | collective-permute-start | bytes 884744 | tf_op jit(solution)/shard_map/ppermute | solution.py:599
  15.8 11.2 %collective-permute-start.2 = (bf16[4,16,2304]{2,1,0:T(8,128)(2,1)S(1)}, bf16[4,16,2304]{2,1,0:T(8,128)(2,1)S(1)}, u32[]{:S(2)}, u32[]{:S(2)}) collective-permute-start(bf16[4,16,2304]{2,1,0:T(8,128)(2,1)S(1)} %all_to_all.20.refs_0_), channel_id=1, source_target_pairs={{3,0},{0,1},{1,2},{2,3},{7,4},{4,5},{5,6},{6,7},{11,8},{8,9},{9,10... | collective-permute-start | bytes 884744 | tf_op jit(solution)/shard_map/ppermute | solution.py:599
  21.5 10.2 %collective-permute-start.4 = (bf16[4,16,2304]{2,1,0:T(8,128)(2,1)S(1)}, bf16[4,16,2304]{2,1,0:T(8,128)(2,1)S(1)}, u32[]{:S(2)}, u32[]{:S(2)}) collective-permute-start(bf16[4,16,2304]{2,1,0:T(8,128)(2,1)S(1)} %collective-permute-done.refs_1_), channel_id=1, source_target_pairs={{1,0},{2,1},{3,2},{0,3},{5,4},{6,5},{7,6},{4,7},{9,8},{10,9},{11,1... | collective-permute-start | bytes 884744 | tf_op jit(solution)/shard_map/ppermute | solution.py:599
  24.3 13.3 %collective-permute-start.6 = (bf16[4,16,2304]{2,1,0:T(8,128)(2,1)S(1)}, bf16[4,16,2304]{2,1,0:T(8,128)(2,1)S(1)}, u32[]{:S(2)}, u32[]{:S(2)}) collective-permute-start(bf16[4,16,2304]{2,1,0:T(8,128)(2,1)S(1)} %all_to_all.20.refs_0_), channel_id=1, source_target_pairs={{1,0},{2,1},{3,2},{0,3},{5,4},{6,5},{7,6},{4,7},{9,8},{10,9},{11,1... | collective-permute-start | bytes 884744 | tf_op jit(solution)/shard_map/ppermute | solution.py:599
  25.1 19.6 %collective-permute-start.1 = (bf16[4,16,2304]{2,1,0:T(8,128)(2,1)S(1)}, bf16[4,16,2304]{2,1,0:T(8,128)(2,1)S(1)}, u32[]{:S(2)}, u32[]{:S(2)}) collective-permute-start(bf16[4,16,2304]{2,1,0:T(8,128)(2,1)S(1)} %collective-permute-done.refs_1_), channel_id=1, source_target_pairs={{3,0},{0,1},{1,2},{2,3},{7,4},{4,5},{5,6},{6,7},{11,8},{8,9},{9,10... | collective-permute-start | bytes 884744 | tf_op jit(solution)/shard_map/ppermute | solution.py:599
  27.0 19.2 %collective-permute-start.3 = (bf16[4,16,2304]{2,1,0:T(8,128)(2,1)S(1)}, bf16[4,16,2304]{2,1,0:T(8,128)(2,1)S(1)}, u32[]{:S(2)}, u32[]{:S(2)}) collective-permute-start(bf16[4,16,2304]{2,1,0:T(8,128)(2,1)S(1)} %collective-permute-done.2.refs_3_), channel_id=1, source_target_pairs={{3,0},{0,1},{1,2},{2,3},{7,4},{4,5},{5,6},{6,7},{11,8},{8,9},{9,10... | collective-permute-start | bytes 884744 | tf_op jit(solution)/shard_map/ppermute | solution.py:599
  31.7 14.5 %collective-permute-start.5 = (bf16[4,16,2304]{2,1,0:T(8,128)(2,1)S(1)}, bf16[4,16,2304]{2,1,0:T(8,128)(2,1)S(1)}, u32[]{:S(2)}, u32[]{:S(2)}) collective-permute-start(bf16[4,16,2304]{2,1,0:T(8,128)(2,1)S(1)} %collective-permute-done.4.refs_4_), channel_id=1, source_target_pairs={{1,0},{2,1},{3,2},{0,3},{5,4},{6,5},{7,6},{4,7},{9,8},{10,9},{11,1... | collective-permute-start | bytes 884744 | tf_op jit(solution)/shard_map/ppermute | solution.py:599
  42.0 15.5 %collective-permute-start.7 = (bf16[5,16,2048]{2,1,0:T(8,128)(2,1)S(1)}, bf16[5,16,2048]{2,1,0:T(8,128)(2,1)S(1)}, u32[]{:S(2)}, u32[]{:S(2)}) collective-permute-start(bf16[5,16,2048]{2,1,0:T(8,128)(2,1)S(1)} %get-tuple-element.34), channel_id=1, source_target_pairs={{24,0},{25,1},{26,2},{27,3},{28,4},{29,5},{30,6},{31,7},{0,8},{1,9... | collective-permute-start | bytes 983048 | tf_op jit(solution)/shard_map/ppermute | solution.py:604
  42.6 14.8 %collective-permute-start.8 = (bf16[5,16,2048]{2,1,0:T(8,128)(2,1)S(1)}, bf16[5,16,2048]{2,1,0:T(8,128)(2,1)S(1)}, u32[]{:S(2)}, u32[]{:S(2)}) collective-permute-start(bf16[5,16,2048]{2,1,0:T(8,128)(2,1)S(1)} %get-tuple-element.35), channel_id=1, source_target_pairs={{16,0},{17,1},{18,2},{19,3},{20,4},{21,5},{22,6},{23,7},{24,8},{25... | collective-permute-start | bytes 983048 | tf_op jit(solution)/shard_map/ppermute | solution.py:604
  44.7 13.4 %collective-permute-start.9 = (bf16[5,16,2048]{2,1,0:T(8,128)(2,1)S(1)}, bf16[5,16,2048]{2,1,0:T(8,128)(2,1)S(1)}, u32[]{:S(2)}, u32[]{:S(2)}) collective-permute-start(bf16[5,16,2048]{2,1,0:T(8,128)(2,1)S(1)} %get-tuple-element.36), channel_id=1, source_target_pairs={{8,0},{9,1},{10,2},{11,3},{12,4},{13,5},{14,6},{15,7},{16,8},{17,9... | collective-permute-start | bytes 983048 | tf_op jit(solution)/shard_map/ppermute | solution.py:604
  49.4 33.2 %collective-permute-start.10 = (bf16[3,16,2048]{2,1,0:T(8,128)(2,1)S(1)}, bf16[3,16,2048]{2,1,0:T(8,128)(2,1)S(1)}, u32[]{:S(2)}, u32[]{:S(2)}) collective-permute-start(bf16[3,16,2048]{2,1,0:T(8,128)(2,1)S(1)} %get-tuple-element.38), channel_id=1, source_target_pairs={{24,0},{25,1},{26,2},{27,3},{28,4},{29,5},{30,6},{31,7},{0,8},{1,9... | collective-permute-start | bytes 589832 | tf_op jit(solution)/shard_map/ppermute | solution.py:604
  49.9 32.7 %collective-permute-start.11 = (bf16[3,16,2048]{2,1,0:T(8,128)(2,1)S(1)}, bf16[3,16,2048]{2,1,0:T(8,128)(2,1)S(1)}, u32[]{:S(2)}, u32[]{:S(2)}) collective-permute-start(bf16[3,16,2048]{2,1,0:T(8,128)(2,1)S(1)} %get-tuple-element.39), channel_id=1, source_target_pairs={{16,0},{17,1},{18,2},{19,3},{20,4},{21,5},{22,6},{23,7},{24,8},{25... | collective-permute-start | bytes 589832 | tf_op jit(solution)/shard_map/ppermute | solution.py:604
  57.5 25.2 %collective-permute-start.12 = (bf16[3,16,2048]{2,1,0:T(8,128)(2,1)S(1)}, bf16[3,16,2048]{2,1,0:T(8,128)(2,1)S(1)}, u32[]{:S(2)}, u32[]{:S(2)}) collective-permute-start(bf16[3,16,2048]{2,1,0:T(8,128)(2,1)S(1)} %get-tuple-element.40), channel_id=1, source_target_pairs={{8,0},{9,1},{10,2},{11,3},{12,4},{13,5},{14,6},{15,7},{16,8},{17,9... | collective-permute-start | bytes 589832 | tf_op jit(solution)/shard_map/ppermute | solution.py:604
  58.8 13.4 %collective-permute-start.13 = (bf16[16,2048]{1,0:T(8,128)(2,1)S(1)}, bf16[16,2048]{1,0:T(8,128)(2,1)S(1)}, u32[]{:S(2)}, u32[]{:S(2)}) collective-permute-start(bf16[16,2048]{1,0:T(8,128)(2,1)S(1)} %get-tuple-element.45), channel_id=1, source_target_pairs={{4,0},{5,1},{6,2},{7,3},{0,4},{1,5},{2,6},{3,7},{12,8},{13,9},{14,... | collective-permute-start | bytes 196616 | tf_op jit(solution)/shard_map/ppermute | solution.py:599
  60.4 14.9 %collective-permute-start.14 = (bf16[16,2048]{1,0:T(8,128)(2,1)S(1)}, bf16[16,2048]{1,0:T(8,128)(2,1)S(1)}, u32[]{:S(2)}, u32[]{:S(2)}) collective-permute-start(bf16[16,2048]{1,0:T(8,128)(2,1)S(1)} %get-tuple-element.46), channel_id=1, source_target_pairs={{3,0},{0,1},{1,2},{2,3},{7,4},{4,5},{5,6},{6,7},{11,8},{8,9},{9,10... | collective-permute-start | bytes 196616 | tf_op jit(solution)/shard_map/ppermute | solution.py:599
  61.6 21.1 %all-to-all-start.1 = ((bf16[32,16,256]{2,1,0:T(8,128)(2,1)}), bf16[32,16,256]{2,1,0:T(8,128)(2,1)S(1)}, u32[]{:S(2)}, u32[]{:S(2)}) async-start(bf16[32,16,256]{2,1,0:T(8,128)(2,1)} %get-tuple-element.37), calls=%async_computation.1 | async-start | bytes 524288 | tf_op jit(solution)/shard_map/all_to_all | solution.py:588
  72.2 6.8 %collective-permute-start.15 = (bf16[16,2048]{1,0:T(8,128)(2,1)}, bf16[16,2048]{1,0:T(8,128)(2,1)S(1)}, u32[]{:S(2)}, u32[]{:S(2)}) collective-permute-start(bf16[16,2048]{1,0:T(8,128)(2,1)} %get-tuple-element.47), channel_id=1, source_target_pairs={{1,0},{2,1},{3,2},{0,3},{5,4},{6,5},{7,6},{4,7},{9,8},{10,9},{11,1... | collective-permute-start | bytes 196616 | tf_op jit(solution)/shard_map/ppermute | solution.py:599
  75.3 7.4 %collective-permute-start.16 = (bf16[16,2048]{1,0:T(8,128)(2,1)S(1)}, bf16[16,2048]{1,0:T(8,128)(2,1)S(1)}, u32[]{:S(2)}, u32[]{:S(2)}) collective-permute-start(bf16[16,2048]{1,0:T(8,128)(2,1)S(1)} %get-tuple-element.48), channel_id=1, source_target_pairs={{7,0},{4,1},{5,2},{6,3},{3,4},{0,5},{1,6},{2,7},{15,8},{12,9},{13,... | collective-permute-start | bytes 196616 | tf_op jit(solution)/shard_map/ppermute | solution.py:599
  86.4 36.8 %copy-start.3 = (bf16[1,2,8192]{2,1,0:T(2,128)(2,1)S(1)}, bf16[1,2,8192]{2,1,0:T(2,128)(2,1)}, u32[]{:S(2)}) copy-start(bf16[1,2,8192]{2,1,0:T(2,128)(2,1)} %param.10) | copy-start | bytes 98308
  86.4 16.7 %all-to-all-start.2 = ((bf16[32,16,256]{2,1,0:T(8,128)(2,1)}), bf16[32,16,256]{2,1,0:T(8,128)(2,1)S(1)}, u32[]{:S(2)}, u32[]{:S(2)}) async-start(bf16[32,16,256]{2,1,0:T(8,128)(2,1)} %get-tuple-element.49), calls=%async_computation.2 | async-start | bytes 524288 | tf_op jit(solution)/shard_map/all_to_all | solution.py:588
  91.5 8.8 %collective-permute-start.17 = (bf16[16,2048]{1,0:T(8,128)(2,1)S(1)}, bf16[16,2048]{1,0:T(8,128)(2,1)S(1)}, u32[]{:S(2)}, u32[]{:S(2)}) collective-permute-start(bf16[16,2048]{1,0:T(8,128)(2,1)S(1)} %get-tuple-element.51), channel_id=1, source_target_pairs={{2,0},{3,1},{0,2},{1,3},{6,4},{7,5},{4,6},{5,7},{10,8},{11,9},{8,1... | collective-permute-start | bytes 196616 | tf_op jit(solution)/shard_map/ppermute | solution.py:599
  94.9 8.2 %collective-permute-start.18 = (bf16[16,2048]{1,0:T(8,128)(2,1)S(1)}, bf16[16,2048]{1,0:T(8,128)(2,1)S(1)}, u32[]{:S(2)}, u32[]{:S(2)}) collective-permute-start(bf16[16,2048]{1,0:T(8,128)(2,1)S(1)} %get-tuple-element.52), channel_id=1, source_target_pairs={{6,0},{7,1},{4,2},{5,3},{2,4},{3,5},{0,6},{1,7},{14,8},{15,9},{12,... | collective-permute-start | bytes 196616 | tf_op jit(solution)/shard_map/ppermute | solution.py:599
  106.5 16.7 %all-to-all-start.3 = ((f32[32,16,256]{2,1,0:T(8,128)}), f32[32,16,256]{2,1,0:T(8,128)S(1)}, u32[]{:S(2)}, u32[]{:S(2)}) async-start(f32[32,16,256]{2,1,0:T(8,128)} %out_product.1), calls=%async_computation.3 | async-start | bytes 1048576 | tf_op jit(solution)/shard_map/all_to_all | solution.py:588
  112.7 7.4 %collective-permute-start.19 = (bf16[16,2048]{1,0:T(8,128)(2,1)S(1)}, bf16[16,2048]{1,0:T(8,128)(2,1)S(1)}, u32[]{:S(2)}, u32[]{:S(2)}) collective-permute-start(bf16[16,2048]{1,0:T(8,128)(2,1)S(1)} %get-tuple-element.55), channel_id=1, source_target_pairs={{5,0},{6,1},{7,2},{4,3},{1,4},{2,5},{3,6},{0,7},{13,8},{14,9},{15,... | collective-permute-start | bytes 196616 | tf_op jit(solution)/shard_map/ppermute | solution.py:599
  (4 other events, 138.0 us)
